TPU v7x, 32 devices: a whole 2x2x4 slice. The times are simulated.
32 devices in a mesh: group: 2 (over x), expert: 16 (over z, y, core).
Axes of the slice: x: 2, y: 2, z: 4, core: 2. Of those that a mesh axis runs over, the one named last changes fastest.
Arguments:
- q_abs: bfloat16 [4, 256, 36864], P(None, ('group', 'expert')), parts along dimension 1, may hold values from -24 to 24
- new_lat: bfloat16 [4, 256, 576], P(None, ('group', 'expert')), parts along dimension 1, may hold values from -24 to 24
- latent_cache: bfloat16 [256, 32, 576], P('group', 'expert'), parts along dimension 0, may hold values from -24 to 24
- lengths: int32 [256], P('group'), parts along dimension 0, may hold values from 1 to 32, 2048 in all
- owner: int32 [256], P('group'), parts along dimension 0, may hold values from 0 to 127, each once
- resid: bfloat16 [4, 256, 3584], P(None, ('group', 'expert')), parts along dimension 1, may hold values from -6 to 6
- routes: int32 [4, 256, 8], P(None, ('group', 'expert')), parts along dimension 1, may hold values from 0 to 15, all different within a row; in each aligned block of 8 rows (0 to 7, 8 to 15, ..., all dimensions but the last counted through in order) at most 6 rows name the same one
- w_out: bfloat16 [512, 3584], replicated, may hold values from -0.03125 to 0.03125
- norm_gain: bfloat16 [3584], replicated, may hold values from 0.5 to 1.5
- w_router: bfloat16 [3584, 16], replicated, may hold values from -0.09375 to 0.09375
- w_gate: bfloat16 [16, 3584, 1024], P('expert'), may hold values from -0.09375 to 0.09375
- w_up: bfloat16 [16, 3584, 1024], P('expert'), may hold values from -0.09375 to 0.09375
- w_down: bfloat16 [16, 1024, 3584], P('expert'), may hold values from -0.1875 to 0.1875
Outputs:
- mixed: bfloat16 [4, 256, 3584], P(None, ('group', 'expert')), parts along dimension 1
There are 2 independent parts, one for each index of `group`. A program takes and returns all parts, laid end to end along the dimension named above; an argument that names none is the same for every part. Nothing has to cross between parts.
Inputs may be any that keep to these rules, and one draw needn't show every extreme that they name: `routes`: each row names 8 different experts; within the rows of one device at one step no expert is named by more than 6 rows, a bound that some block reaches. `owner`: each request is served by exactly one decode row. `lengths`: some request has all 32 positions.
All inputs are finite; a program needn't handle non-finite values.
Results may differ from a plain program's by a relative error of at most 0.012.
Values may be sent and summed in bfloat16 or wider, within the bound.
No kernel may reach another device: no remote copies, remote signals or barrier semaphores. Data moves between devices by JAX's collectives and lax.ppermute only.
A program may use at most 128 MiB of HBM per device.

v0:
```python
import jax
import jax.numpy as jnp
from jax import lax
from jax.sharding import PartitionSpec as P

CAP = 6


qk_scale = 192.0 ** (-0.5)


def local(
    q_abs,
    new_lat,
    latent_cache,
    lengths,
    owner,
    resid,
    routes,
    w_out,
    norm_gain,
    w_router,
    w_gate,
    w_up,
    w_down,
):
    devices = lax.axis_size("expert")
    device_index = lax.axis_index("expert")
    step_count, row_count, model_width = resid.shape
    kv_width = new_lat.shape[2]
    head_count = q_abs.shape[2] // kv_width
    latent = w_out.shape[0]
    topk_count = routes.shape[2]
    experts_all = w_router.shape[1]
    sharers = devices // experts_all
    slot_count = CAP
    ordered = jnp.take(latent_cache, owner, axis=0)
    owned_cache = lax.all_to_all(ordered, "expert", split_axis=0, concat_axis=1, tiled=True)
    context = owned_cache.shape[1]
    row_lengths = lax.dynamic_slice_in_dim(
        jnp.take(lengths, owner), device_index * row_count, row_count
    )
    queries = q_abs.reshape(step_count, row_count, head_count, kv_width)
    cache_scores = (
        jnp.einsum("srhk,rpk->srhp", queries, owned_cache, preferred_element_type=jnp.float32)
        * qk_scale
    )
    visible = jnp.arange(context)[None, :] < row_lengths[:, None]
    cache_scores = jnp.where(visible[None, :, None, :], cache_scores, -1e30)
    fresh_scores = (
        jnp.einsum("srhk,trk->srht", queries, new_lat, preferred_element_type=jnp.float32)
        * qk_scale
    )
    causal = jnp.arange(step_count)[:, None] >= jnp.arange(step_count)[None, :]
    fresh_scores = jnp.where(causal[:, None, None, :], fresh_scores, -1e30)
    scores = jnp.concatenate([cache_scores, fresh_scores], axis=-1)
    weights = jax.nn.softmax(scores, axis=-1).astype(jnp.bfloat16)
    pooled = jnp.einsum(
        "srhp,rpl->srl",
        weights[..., :context],
        owned_cache[..., :latent],
        preferred_element_type=jnp.float32,
    )
    pooled = pooled + jnp.einsum(
        "srht,trl->srl",
        weights[..., context:],
        new_lat[..., :latent],
        preferred_element_type=jnp.float32,
    )
    pooled = pooled.astype(jnp.bfloat16)
    hidden_state = resid.astype(jnp.float32) + jnp.einsum(
        "srl,ld->srd", pooled, w_out, preferred_element_type=jnp.float32
    )
    normed = (
        hidden_state
        * lax.rsqrt(jnp.mean(hidden_state * hidden_state, axis=-1, keepdims=True) + 1e-06)
        * norm_gain.astype(jnp.float32)
    )
    normed = normed.astype(jnp.bfloat16)
    affinity = jax.nn.sigmoid(
        jnp.einsum("srd,de->sre", normed, w_router, preferred_element_type=jnp.float32)
    )
    picked = jnp.take_along_axis(affinity, routes, axis=2)
    gate_weights = 2.5 * picked / jnp.sum(picked, axis=2, keepdims=True)
    routed_mask = jnp.any(routes[..., None] == jnp.arange(experts_all, dtype=jnp.int32), axis=2)
    routed_int = routed_mask.astype(jnp.int32)
    slot_rank = jnp.cumsum(routed_int, axis=1) - routed_int
    all_rows, all_routes = (
        lax.all_gather(normed, "expert", axis=1, tiled=True),
        lax.all_gather(routes, "expert", axis=1, tiled=True),
    )
    my_expert = device_index // sharers
    local_hits = jnp.any(all_routes == my_expert, axis=2).astype(jnp.int32)
    local_hits = local_hits.reshape(step_count, devices, row_count)
    local_rank = jnp.cumsum(local_hits, axis=2) - local_hits
    selector = (local_hits[..., None] == 1) & (
        local_rank[..., None] == jnp.arange(slot_count, dtype=jnp.int32)
    )
    received = jnp.einsum(
        "snjc,snjd->sncd",
        selector.astype(jnp.bfloat16),
        all_rows.reshape(step_count, devices, row_count, model_width),
        preferred_element_type=jnp.float32,
    )
    received = received.astype(jnp.bfloat16).reshape(
        1, step_count, devices * slot_count, model_width
    )
    gate_part = jnp.einsum("lsmd,ldf->lsmf", received, w_gate, preferred_element_type=jnp.float32)
    up_part = jnp.einsum("lsmd,ldf->lsmf", received, w_up, preferred_element_type=jnp.float32)
    activated = (jax.nn.silu(gate_part) * up_part).astype(jnp.bfloat16)
    expert_part = jnp.einsum(
        "lsmf,lfd->lsmd", activated, w_down, preferred_element_type=jnp.float32
    ).astype(jnp.bfloat16)
    returned = lax.all_to_all(expert_part, "expert", split_axis=2, concat_axis=0, tiled=True)
    summed = jnp.sum(
        returned.reshape(experts_all, sharers, step_count, slot_count, model_width).astype(
            jnp.float32
        ),
        axis=1,
    )
    pair_rank = jnp.take_along_axis(slot_rank, routes, axis=2)
    flat_index = (
        routes * (step_count * slot_count)
        + jnp.arange(step_count, dtype=jnp.int32)[:, None, None] * slot_count
        + pair_rank
    )
    taken = jnp.take(summed.reshape(-1, model_width), flat_index.reshape(-1), axis=0)
    taken = taken.reshape(step_count, row_count, topk_count, model_width)
    routed_sum = jnp.sum(taken * gate_weights[..., None], axis=2)
    return (hidden_state + routed_sum).astype(jnp.bfloat16)


def solution(mesh):
    return jax.shard_map(
        local,
        mesh=mesh,
        in_specs=(
            P(None, ("group", "expert"), None),
            P(None, ("group", "expert"), None),
            P("group", "expert", None),
            P("group"),
            P("group"),
            P(None, ("group", "expert"), None),
            P(None, ("group", "expert"), None),
            P(),
            P(),
            P(),
            P("expert", None, None),
            P("expert", None, None),
            P("expert", None, None),
        ),
        out_specs=P(None, ("group", "expert"), None),
        check_vma=False,
    )
```

profile of v0, /device:TPU:13, one launch (start us, length us, event | category | flops | bytes accessed | tf_op | source)
XLA Modules:
  0.0 203.0 jit_solution(7829697955891295489)
XLA Ops:
  6.5 0.7 compare_select_fusion.3
  7.2 1.6 gather_fusion.1
  8.8 0.7 broadcast_select_fusion.3
  9.5 1.4 copy.42
  10.9 1.3 gather_fusion
  12.2 1.1 broadcast_select_fusion
  13.3 6.6 %all-to-all-start = ((bf16[128,2,576]{2,1,0:T(2,128)(2,1)}), bf16[128,2,576]{2,1,0:T(2,128)(2,1)S(1)}, u32[]{:S(2)}, u32[]{:S(2)}) async-start(bf16[128,2,576]{2,1,0:T(2,128)(2,1)} %broadcast_select_fusion), calls=%async_computation | async-start | bytes 655360 | tf_op jit(solution)/shard_map/all_to_all | solution.py:38
  19.9 0.7 convert_element_type.77
  20.6 0.8 slice.15
  21.4 4.5 %reshape.191 = bf16[4,8,64,576]{3,2,1,0:T(8,128)(2,1)S(1)} reshape(bf16[4,8,36864]{2,1,0:T(8,128)(2,1)} %param.13) | data formatting | bytes 4718592 | tf_op jit(solution)/shard_map/reshape | solution.py:43
  26.1 1.4 fusion.67
  27.5 1.8 all-to-all-done
  29.3 0.3 copy.44
  29.6 1.0 reshape.250
  30.6 0.2 all_to_all.23
  30.9 2.6 %fusion.66 = (f32[4,8,64]{2,0,1:T(4,128)S(1)}, f32[4,8,64,32]{2,3,0,1:T(8,128)S(1)}) fusion(bf16[4,8,64,576]{3,2,1,0:T(8,128)(2,1)S(1)} %reshape.191, bf16[8,32,576,1]{2,1,0,3:T(8,128)(2,1)} %reshape.250, pred[8,32]{1,0:T(8,128)(4,1)S(1)} %iota_compare_fusion.2), kind=kOutput, calls=%fused_computation.90 | convolution fusion | flops 75692032 | bytes 2924800 | tf_op jit(solution)/shard_map/srhk,rpk->srhp/dot_general | solution.py:45
  33.5 0.2 fusion.48
  33.7 0.2 divide_convert_fusion
  33.9 0.1 convert_reduce_fusion.1
  34.0 0.2 convert_reduce_fusion
  34.3 0.1 convolution_bitcast_fusion.1
  34.4 0.2 fusion.43
  34.6 0.8 multiply_reduce_fusion.1
  35.4 0.8 multiply_convert_fusion.1
  36.2 17.4 %all_gather.6 = s32[4,128,8]{2,1,0:T(8,128)S(1)} all-gather(s32[4,8,8]{2,1,0:T(8,128)S(1)} %copy-done.2), channel_id=1, replica_groups=mesh['group'=2,'expert'=16] {'expert'}, dimensions={1}, use_global_device_ids=true | all-gather | bytes 17408 | tf_op jit(solution)/shard_map/all_gather | solution.py:90
  53.7 0.1 compare_reduce_fusion
  53.8 0.1 reshape.201
  53.9 0.7 reduce_window_sum.23
  54.6 29.4 %all-gather.2.cloned.1.call-done = bf16[4,128,3584]{2,1,0:T(8,128)(2,1)} async-done(((bf16[4,8,3584]{2,1,0:T(8,128)(2,1)}), bf16[4,128,3584]{2,1,0:T(8,128)(2,1)}) %all-gather.2.cloned.1.call-update) | async-done | bytes 3670032 | tf_op jit(solution)/shard_map/all_gather | solution.py:89
  84.0 3.1 %convolution_convert_fusion = bf16[4,16,6,3584]{3,2,1,0:T(8,128)(2,1)S(1)} fusion(bf16[4,128,3584]{2,1,0:T(8,128)(2,1)} %all-gather.2.cloned.1.call-done, s32[4,16,8]{2,1,0:T(8,128)S(1)} %sub.23, pred[4,16,8]{2,1,0:T(8,128)(4,1)S(1)} %broadcast_compare_fusion), kind=kOutput, calls=%fused_computation.11 | convolution fusion | flops 23402496 | bytes 6425088 | tf_op jit(solution)/shard_map/snjc,snjd->sncd/dot_general | solution.py:99
  87.1 2.1 %copy.50 = bf16[4,16,6,3584]{3,0,2,1:T(4,128)(2,1)S(1)} copy(bf16[4,16,6,3584]{3,2,1,0:T(8,128)(2,1)S(1)} %convolution_convert_fusion) | data formatting | bytes 5505024 | tf_op jit(solution)/shard_map/convert_element_type | solution.py:105
  89.3 5.4 %fusion.4 = f32[4,96,1024]{2,1,0:T(8,128)S(1)} fusion(bf16[1,3584,1024]{2,1,0:T(8,128)(2,1)} %param.23, bf16[4,96,3584]{2,0,1:T(4,128)(2,1)S(1)} %bitcast.77), kind=kOutput, calls=%fused_computation.9 | convolution fusion | flops 2818572288 | bytes 11665408 | tf_op jit(solution)/shard_map/lsmd,ldf->lsmf/dot_general | solution.py:108
  94.7 3.2 %multiply_convert_fusion = bf16[4,96,1024]{2,1,0:T(8,128)(2,1)S(1)} fusion(f32[4,96,1024]{2,1,0:T(8,128)S(1)} %fusion.4, bf16[1,3584,1024]{2,1,0:T(8,128)(2,1)S(1)} %bitcast.83, bf16[4,96,3584]{2,0,1:T(4,128)(2,1)S(1)} %bitcast.78), kind=kOutput, calls=%fused_computation.25 | convolution fusion | flops 2820931584 | bytes 12451840 | tf_op jit(solution)/shard_map/lsmd,ldf->lsmf/dot_general | solution.py:109
  98.0 3.2 %fusion.9 = bf16[1,4,96,3584]{3,2,1,0:T(8,128)(2,1)S(1)} fusion(bf16[4,96,1024]{2,1,0:T(8,128)(2,1)S(1)} %multiply_convert_fusion, bf16[1,1024,3584]{2,1,0:T(8,128)(2,1)S(1)} %bitcast.85), kind=kOutput, calls=%fused_computation.14 | convolution fusion | flops 2819948544 | bytes 10878976 | tf_op jit(solution)/shard_map/lsmf,lfd->lsmd/dot_general | solution.py:111
  101.2 3.7 %copy.53 = bf16[1,4,96,3584]{3,1,0,2:T(4,128)(2,1)} copy(bf16[1,4,96,3584]{3,2,1,0:T(8,128)(2,1)S(1)} %fusion.9) | data formatting | bytes 5505024 | tf_op jit(solution)/shard_map/convert_element_type | solution.py:113
  104.9 4.4 %all-to-all-start.1 = ((bf16[1,4,96,3584]{3,1,0,2:T(4,128)(2,1)}), bf16[1,4,96,3584]{3,1,0,2:T(4,128)(2,1)S(1)}, u32[]{:S(2)}, u32[]{:S(2)}) async-start(bf16[1,4,96,3584]{3,1,0,2:T(4,128)(2,1)} %copy.53), calls=%async_computation.1 | async-start | bytes 5505024 | tf_op jit(solution)/shard_map/all_to_all | solution.py:114
  109.3 0.1 fusion.54
  109.6 1.9 gather_fusion.3
  111.8 1.1 fusion.46
  113.0 1.9 gather_fusion.4
  114.9 0.3 multiply_divide_fusion
  115.3 55.5 %all-to-all-done.1 = bf16[1,4,96,3584]{3,1,0,2:T(4,128)(2,1)S(1)} async-done(((bf16[1,4,96,3584]{3,1,0,2:T(4,128)(2,1)}), bf16[1,4,96,3584]{3,1,0,2:T(4,128)(2,1)S(1)}, u32[]{:S(2)}, u32[]{:S(2)}) %all-to-all-start.1) | async-done | bytes 2752544 | tf_op jit(solution)/shard_map/all_to_all | solution.py:114
  170.8 1.5 convert_bitcast_fusion
  172.3 4.7 %copy.54 = f32[16,1,4,6,3584]{4,3,2,0,1:T(8,128)} copy(f32[16,1,4,6,3584]{4,2,3,0,1:T(4,128)S(1)} %convert_bitcast_fusion) | data formatting | bytes 11010048 | tf_op jit(solution)/shard_map/reshape | solution.py:127
  177.0 7.2 %reshape.203 = f32[384,3584]{1,0:T(8,128)} reshape(f32[16,1,4,6,3584]{4,3,2,0,1:T(8,128)} %copy.54) | data formatting | bytes 11010048 | tf_op jit(solution)/shard_map/reshape | solution.py:127
  184.2 7.7 %gather_fusion.2 = f32[256,3584]{1,0:T(8,128)} fusion(f32[384,3584]{1,0:T(8,128)} %reshape.203, s32[1024]{0:T(1024)S(1)} %pad_clamp_fusion), kind=kCustom, calls=%fused_computation.2 | custom fusion | bytes 7341056 | tf_op jit(solution)/shard_map/jit(_take)/gather | solution.py:127
  191.9 3.5 %multiply_reduce_fusion = f32[4,8,3584]{2,1,0:T(8,128)S(1)} fusion(f32[4,8,8]{2,1,0:T(8,128)S(1)} %multiply_divide_fusion, pred[4,8,8]{2,1,0:T(8,128)(4,1)S(1)} %get-tuple-element.5, f32[256,3584]{1,0:T(8,128)} %gather_fusion.2), kind=kLoop, calls=%fused_computation.18 | loop fusion | flops 2637824 | bytes 4130048 | tf_op jit(solution)/shard_map/reduce_sum | solution.py:129
  195.5 0.7 add_convert_fusion
  (44 shorter events, 0.8 us)
Async XLA Ops:
  6.5 105.3 %copy-start = (bf16[3584,16]{0,1:T(8,128)(2,1)S(1)}, bf16[3584,16]{0,1:T(8,128)(2,1)}, u32[]{:S(2)}) copy-start(bf16[3584,16]{0,1:T(8,128)(2,1)} %param.22) | copy-start | bytes 344068
  10.9 15.2 %copy-start.4 = (bf16[4,8,576]{2,1,0:T(8,128)(2,1)S(1)}, bf16[4,8,576]{2,1,0:T(8,128)(2,1)}, u32[]{:S(2)}) copy-start(bf16[4,8,576]{2,1,0:T(8,128)(2,1)} %param.14) | copy-start | bytes 110596
  13.3 15.9 %all-to-all-start = ((bf16[128,2,576]{2,1,0:T(2,128)(2,1)}), bf16[128,2,576]{2,1,0:T(2,128)(2,1)S(1)}, u32[]{:S(2)}, u32[]{:S(2)}) async-start(bf16[128,2,576]{2,1,0:T(2,128)(2,1)} %broadcast_select_fusion), calls=%async_computation | async-start | bytes 655360 | tf_op jit(solution)/shard_map/all_to_all | solution.py:38
  19.9 64.1 %all-gather.2.cloned.1.call-start = ((), (), s32[]{:S(2)}) async-start(), calls=%async_computation.2 | async-start | bytes 3899392 | tf_op jit(solution)/shard_map/all_gather | solution.py:89
  30.8 3.7 %copy-start.1 = (bf16[512,3584]{1,0:T(8,128)(2,1)S(1)}, bf16[512,3584]{1,0:T(8,128)(2,1)}, u32[]{:S(2)}) copy-start(bf16[512,3584]{1,0:T(8,128)(2,1)} %param.20) | copy-start | bytes 11010052
  30.9 3.7 %copy-start.3 = (bf16[4,8,3584]{2,1,0:T(8,128)(2,1)S(1)}, bf16[4,8,3584]{2,1,0:T(8,128)(2,1)}, u32[]{:S(2)}) copy-start(bf16[4,8,3584]{2,1,0:T(8,128)(2,1)} %param.18) | copy-start | bytes 688132
  33.7 2.5 %copy-start.2 = (s32[4,8,8]{2,1,0:T(8,128)S(1)}, s32[4,8,8]{2,1,0:T(8,128)}, u32[]{:S(2)}) copy-start(s32[4,8,8]{2,1,0:T(8,128)} %param.19) | copy-start | bytes 3076
  87.1 7.6 %slice-start = ((s8[7340032]{0:T(1024)(128)(4,1)}), s8[4194304]{0:T(1024)(128)(4,1)S(1)}, s32[]{:S(2)}) async-start(s8[7340032]{0:T(1024)(128)(4,1)} %bitcast.82), calls=%async_computation.3 | async-start | bytes 8388608
  89.3 5.4 %slice-start.1 = ((s8[7340032]{0:T(1024)(128)(4,1)}), s8[3145728]{0:T(1024)(128)(4,1)S(1)}, s32[]{:S(2)}) async-start(s8[7340032]{0:T(1024)(128)(4,1)} %bitcast.82), calls=%async_computation.4 | async-start | bytes 6291456
  89.3 8.7 %slice-start.2 = ((s8[7340032]{0:T(1024)(128)(4,1)}), s8[4194304]{0:T(1024)(128)(4,1)S(1)}, s32[]{:S(2)}) async-start(s8[7340032]{0:T(1024)(128)(4,1)} %bitcast.84), calls=%async_computation.5 | async-start | bytes 8388608
  94.7 3.2 %slice-start.3 = ((s8[7340032]{0:T(1024)(128)(4,1)}), s8[3145728]{0:T(1024)(128)(4,1)S(1)}, s32[]{:S(2)}) async-start(s8[7340032]{0:T(1024)(128)(4,1)} %bitcast.84), calls=%async_computation.6 | async-start | bytes 6291456
  104.9 65.9 %all-to-all-start.1 = ((bf16[1,4,96,3584]{3,1,0,2:T(4,128)(2,1)}), bf16[1,4,96,3584]{3,1,0,2:T(4,128)(2,1)S(1)}, u32[]{:S(2)}, u32[]{:S(2)}) async-start(bf16[1,4,96,3584]{3,1,0,2:T(4,128)(2,1)} %copy.53), calls=%async_computation.1 | async-start | bytes 5505024 | tf_op jit(solution)/shard_map/all_to_all | solution.py:114
Sparse Core Ops, SparseCore 0:
  36.3 47.5 all-gather.1
where the time goes:
time: 204 us; the launch traced here: 203 us
  waiting for transfers between devices  86.7 us (42%)
  local copies, waits for them, and re-layouts  40.9 us (20%)
  matrix products  21.2 us (10%)
  blocking collectives  17.4 us (9%)
  between operations  13.8 us (7%)
  other arithmetic  12 us (6%)
  starting transfers between devices  11 us (5%)
    all_to_all x1, waiting for transfers between devices, local(): lax.all_to_all(expert_part, 'expert', split_axis=2, concat_axis=0, tiled=...  55.5 us
    all_gather x1, waiting for transfers between devices, local(): lax.all_gather(normed, 'expert', axis=1, tiled=True)  29.4 us
    all_gather x1, blocking collectives, local(): lax.all_gather(routes, 'expert', axis=1, tiled=True)  17.4 us
    reshape x2, local copies, waits for them, and re-layouts, local(): summed.reshape(-1, model_width)  11.9 us
    gather x1, local copies, waits for them, and re-layouts, local(): jnp.take(summed.reshape(-1, model_width), flat_index.reshape(-1), axis=0)  7.72 us
    all_to_all x1, starting transfers between devices, local(): lax.all_to_all(ordered, 'expert', split_axis=0, concat_axis=1, tiled=True)  6.55 us
    dot_general x1, matrix products, local(): jnp.einsum('lsmd,ldf->lsmf', received, w_gate, preferred_element_type=jnp...  5.39 us
    reshape x1, local copies, waits for them, and re-layouts, local(): queries = q_abs.reshape(step_count, row_count, head_count, kv_width)  4.54 us
  transfers between devices with their start and end apart: 3, of which 3 were waited for; matrix products, arithmetic and copies ran while one was open for 7% of the time, Pallas kernels for 0%

commit v1 on v0

v1 whole, which is shorter than its diff:
```python
import jax
import jax.numpy as jnp
from jax import lax
from jax.experimental import pallas as pl
from jax.experimental.pallas import tpu as pltpu
from jax.sharding import PartitionSpec as P

qk_scale = 192.0 ** (-0.5)
LANES = 128


def ring_of(chips):
    return list(range(0, chips, 2)) + list(range(chips - 1, 0, -2))


def shift_perm(chips, by):
    ring = ring_of(chips)
    return [
        (2 * ring[p] + core, 2 * ring[(p + by) % chips] + core)
        for p in range(chips)
        for core in range(2)
    ]


def sibling_perm(chips):
    return [(d, d ^ 1) for d in range(2 * chips)]


def distances(chips):
    half = chips // 2
    order = [0]
    for t in range(1, half):
        order += [t, -t]
    return order + [half]


def tile_of(size, most):
    return max(t for t in range(LANES, min(size, most) + 1, LANES) if size % t == 0)


def expert_kernel(chips, rows, gate_steps, *refs):
    blocks = 2 * chips
    resid = refs[:blocks]
    (pooled_own, pooled_sib, w_out, gain, w_router, lane_pick, w_gate, w_up, w_down) = refs[
        blocks : blocks + 9
    ]
    hidden = refs[blocks + 9]
    outs = refs[blocks + 10 : blocks + 10 + blocks]
    x, act, ssq, scale, weight = refs[blocks + 10 + blocks :]
    step = pl.program_id(0)
    width = x.shape[1]
    latent = w_out.shape[0]
    side = chips * rows
    gate_tile = w_gate.shape[2]
    chunk = min(256, side)
    chunks = 2 * side // chunk

    @pl.when(step == 0)
    def _():
        ssq[...] = jnp.zeros_like(ssq)
        cols_tile = tile_of(width, 512)

        def columns(j, carry):
            cols = pl.ds(pl.multiple_of(j * cols_tile, cols_tile), cols_tile)
            w = w_out[:, cols]
            g = gain[:, cols].astype(jnp.float32)
            for s, pooled in enumerate((pooled_own, pooled_sib)):
                proj = jnp.dot(pooled[:, :latent], w, preferred_element_type=jnp.float32)
                for b in range(chips):
                    at = pl.ds((s * chips + b) * rows, rows)
                    h = proj[b * rows : (b + 1) * rows] + resid[s * chips + b][:, cols].astype(
                        jnp.float32
                    )
                    if s == 0 and b == 0:
                        hidden[:, cols] = h
                    x[at, cols] = (h * g).astype(jnp.bfloat16)
                    sq = h * h
                    part = sq[:, :LANES]
                    for k in range(1, cols_tile // LANES):
                        part = part + sq[:, k * LANES : (k + 1) * LANES]
                    ssq[at, :] += part
            return carry

        lax.fori_loop(0, width // cols_tile, columns, 0)
        for s, pooled in enumerate((pooled_own, pooled_sib)):
            at = pl.ds(s * side, side)
            mean = jnp.sum(ssq[at, :], axis=1, keepdims=True) * (1.0 / width)
            r = lax.rsqrt(mean + 1e-06)
            logits = jnp.dot(x[at, :], w_router[...], preferred_element_type=jnp.float32) * r
            affinity = jax.nn.sigmoid(logits) * pooled[:, latent:].astype(jnp.float32)
            total = jnp.sum(affinity, axis=1, keepdims=True)
            mine = jnp.sum(affinity * lane_pick[...], axis=1, keepdims=True)
            scale[at, :] = jnp.broadcast_to(r, (side, LANES))
            weight[at, :] = jnp.broadcast_to(2.5 * mine / total, (side, LANES))

    @pl.when((step > 0) & (step <= gate_steps))
    def _():
        cols = pl.ds(pl.multiple_of((step - 1) * gate_tile, gate_tile), gate_tile)

        def body(i, carry):
            at = pl.ds(pl.multiple_of(i * chunk, chunk), chunk)
            xs = x[at, :]
            r = scale[at, :1]
            a = jnp.dot(xs, w_gate[0], preferred_element_type=jnp.float32) * r
            b = jnp.dot(xs, w_up[0], preferred_element_type=jnp.float32) * r
            act[at, cols] = (jax.nn.silu(a) * b * weight[at, :1]).astype(jnp.bfloat16)
            return carry

        lax.fori_loop(0, chunks, body, 0)

    @pl.when(step > gate_steps)
    def _():
        per = chunk // rows
        for i in range(chunks):
            y = jnp.dot(
                act[i * chunk : (i + 1) * chunk, :], w_down[0], preferred_element_type=jnp.float32
            )
            for b in range(per):
                outs[i * per + b][...] = y[b * rows : (b + 1) * rows].astype(jnp.bfloat16)


def experts(resid_blocks, pooled_own, pooled_sib, w_out, gain, w_router, lane_pick, wg, wu, wd):
    blocks = len(resid_blocks)
    chips = blocks // 2
    rows, width = resid_blocks[0].shape
    hidden_units = wg.shape[2]
    gate_tile = tile_of(hidden_units, 256)
    gate_steps = hidden_units // gate_tile
    down_tile = tile_of(width, 1024)
    down_steps = width // down_tile
    total = blocks * rows

    def whole(a):
        return pl.BlockSpec(a.shape, lambda i: (0,) * a.ndim, pipeline_mode=pl.Buffered(1))

    def gate_at(i):
        return (0, 0, jnp.clip(i - 1, 0, gate_steps - 1))

    def down_at(i):
        return (0, 0, jnp.clip(i - 1 - gate_steps, 0, down_steps - 1))

    def out_at(i):
        return (0, jnp.clip(i - 1 - gate_steps, 0, down_steps - 1))

    fixed = list(resid_blocks) + [pooled_own, pooled_sib, w_out, gain, w_router, lane_pick]
    results = pl.pallas_call(
        lambda *refs: expert_kernel(chips, rows, gate_steps, *refs),
        grid=(1 + gate_steps + down_steps,),
        in_specs=[whole(a) for a in fixed]
        + [
            pl.BlockSpec((1, width, gate_tile), gate_at),
            pl.BlockSpec((1, width, gate_tile), gate_at),
            pl.BlockSpec((1, hidden_units, down_tile), down_at),
        ],
        out_shape=[jax.ShapeDtypeStruct((rows, width), jnp.float32)]
        + [jax.ShapeDtypeStruct((rows, width), jnp.bfloat16)] * blocks,
        out_specs=[pl.BlockSpec((rows, width), lambda i: (0, 0))]
        + [pl.BlockSpec((rows, down_tile), out_at)] * blocks,
        scratch_shapes=[
            pltpu.VMEM((total, width), jnp.bfloat16),
            pltpu.VMEM((total, hidden_units), jnp.bfloat16),
            pltpu.VMEM((total, LANES), jnp.float32),
            pltpu.VMEM((total, LANES), jnp.float32),
            pltpu.VMEM((total, LANES), jnp.float32),
        ],
        compiler_params=pltpu.CompilerParams(
            dimension_semantics=("arbitrary",), vmem_limit_bytes=56 * 1024 * 1024
        ),
        cost_estimate=pl.CostEstimate(
            flops=2 * total * width * (3 * hidden_units + w_out.shape[0]),
            bytes_accessed=3 * width * hidden_units * 2 + 2 * total * width * 2,
            transcendentals=total * hidden_units,
        ),
        name="experts",
    )(*fixed, wg, wu, wd)
    return results[0], results[1 : 1 + chips], results[1 + chips :]


def attention(q_abs, new_lat, owned_cache, row_lengths, latent):
    step_count, row_count, kv_width = new_lat.shape
    head_count = q_abs.shape[2] // kv_width
    context = owned_cache.shape[1]
    queries = q_abs.reshape(step_count, row_count, head_count, kv_width)
    cache_scores = (
        jnp.einsum("srhk,rpk->srhp", queries, owned_cache, preferred_element_type=jnp.float32)
        * qk_scale
    )
    visible = jnp.arange(context)[None, :] < row_lengths[:, None]
    cache_scores = jnp.where(visible[None, :, None, :], cache_scores, -1e30)
    fresh_scores = (
        jnp.einsum("srhk,trk->srht", queries, new_lat, preferred_element_type=jnp.float32)
        * qk_scale
    )
    causal = jnp.arange(step_count)[:, None] >= jnp.arange(step_count)[None, :]
    fresh_scores = jnp.where(causal[:, None, None, :], fresh_scores, -1e30)
    scores = jnp.concatenate([cache_scores, fresh_scores], axis=-1)
    weights = jax.nn.softmax(scores, axis=-1).astype(jnp.bfloat16)
    pooled = jnp.einsum(
        "srhp,rpl->srl",
        weights[..., :context],
        owned_cache[..., :latent],
        preferred_element_type=jnp.float32,
    )
    pooled = pooled + jnp.einsum(
        "srht,trl->srl",
        weights[..., context:],
        new_lat[..., :latent],
        preferred_element_type=jnp.float32,
    )
    return pooled.astype(jnp.bfloat16)


def local(
    q_abs,
    new_lat,
    latent_cache,
    lengths,
    owner,
    resid,
    routes,
    w_out,
    norm_gain,
    w_router,
    w_gate,
    w_up,
    w_down,
):
    devices = lax.axis_size("expert")
    device_index = lax.axis_index("expert")
    step_count, row_count, width = resid.shape
    rows = step_count * row_count
    experts_all = w_router.shape[1]
    sharers = devices // experts_all
    chips = devices // 2
    half = chips // 2
    cut = rows // 2
    order = distances(chips)
    sibling = sibling_perm(chips)

    def send(a, perm):
        return lax.ppermute(a, "expert", perm)

    to_right, to_left = shift_perm(chips, 1), shift_perm(chips, -1)

    ordered = latent_cache.at[owner].get(mode="promise_in_bounds", unique_indices=True)
    owned_cache = lax.all_to_all(ordered, "expert", split_axis=0, concat_axis=1, tiled=True)

    mine = resid.reshape(rows, width)
    held = {0: mine}
    for t in range(1, half):
        held[-t] = send(held[-t + 1], to_right)
        held[t] = send(held[t - 1], to_left)
    held[half] = jnp.concatenate(
        [send(held[1 - half][:cut], to_right), send(held[half - 1][cut:], to_left)], axis=0
    )
    resid_own = [held[d] for d in order]
    resid_sib = [send(a, sibling) for a in resid_own]

    row_lengths = lax.dynamic_slice_in_dim(
        lengths.at[owner].get(mode="promise_in_bounds"), device_index * row_count, row_count
    )
    pooled = attention(q_abs, new_lat, owned_cache, row_lengths, w_out.shape[0])

    routed = jnp.any(routes[..., None] == jnp.arange(LANES, dtype=jnp.int32), axis=2)
    packet = jnp.concatenate([pooled, routed.astype(jnp.bfloat16)], axis=2).reshape(rows, -1)
    packets = [packet if d == 0 else send(packet, shift_perm(chips, -d)) for d in order]
    pooled_own = jnp.concatenate(packets, axis=0)
    pooled_sib = send(pooled_own, sibling)

    lane_pick = (jnp.arange(LANES) == device_index // sharers).astype(jnp.float32)[None, :]
    hidden, to_own, to_sib = experts(
        resid_own + resid_sib,
        pooled_own,
        pooled_sib,
        w_out,
        norm_gain[None, :],
        jnp.pad(w_router, ((0, 0), (0, LANES - experts_all))),
        lane_pick,
        w_gate,
        w_up,
        w_down,
    )

    f32 = jnp.float32
    own = dict(zip(order, to_own))
    got = {d: send(a, sibling) for d, a in reversed(list(zip(order, to_sib)))}

    def part(d, lo=0, hi=rows):
        return own[d][lo:hi].astype(f32) + got[d][lo:hi].astype(f32)

    right = send(part(half, 0, cut).astype(jnp.bfloat16), to_right).astype(f32)
    left = send(part(half, cut, rows).astype(jnp.bfloat16), to_left).astype(f32)
    right = jnp.concatenate([right, jnp.zeros((rows - cut, width), f32)], axis=0)
    left = jnp.concatenate([jnp.zeros((cut, width), f32), left], axis=0)
    for t in range(half - 1, 0, -1):
        right = send((part(t) + right).astype(jnp.bfloat16), to_right).astype(f32)
        left = send((part(-t) + left).astype(jnp.bfloat16), to_left).astype(f32)
    mixed = hidden + part(0) + right + left
    return mixed.astype(jnp.bfloat16).reshape(step_count, row_count, width)


def solution(mesh):
    return jax.shard_map(
        local,
        mesh=mesh,
        in_specs=(
            P(None, ("group", "expert"), None),
            P(None, ("group", "expert"), None),
            P("group", "expert", None),
            P("group"),
            P("group"),
            P(None, ("group", "expert"), None),
            P(None, ("group", "expert"), None),
            P(),
            P(),
            P(),
            P("expert", None, None),
            P("expert", None, None),
            P("expert", None, None),
        ),
        out_specs=P(None, ("group", "expert"), None),
        check_vma=False,
    )
```

time: 204 us -> 153 us (0.75)
  the two profiles are of different devices: /device:TPU:13 before, /device:TPU:0 now
where the time goes in v1:
time: 153 us; the launch traced here: 152 us
  waiting for transfers between devices  57.6 us (38%)
  starting transfers between devices  39.1 us (26%)
  Pallas kernels  26.7 us (17%)
  local copies, waits for them, and re-layouts  16.6 us (11%)
  other arithmetic  7.36 us (5%)
  matrix products  4.17 us (3%)
    ppermute x40, waiting for transfers between devices, send(): return lax.ppermute(a, 'expert', perm)  57.6 us
    ppermute x40, starting transfers between devices, send(): return lax.ppermute(a, 'expert', perm)  32.8 us
    pallas_call x1, Pallas kernels, experts(): pl.pallas_call(lambda *refs: expert_kernel(chips, rows, gate_steps, *refs...  26.7 us
    all_to_all x1, starting transfers between devices, local(): lax.all_to_all(ordered, 'expert', split_axis=0, concat_axis=1, tiled=True)  6.35 us
    reshape x1, local copies, waits for them, and re-layouts, attention(): queries = q_abs.reshape(step_count, row_count, head_count, kv_width)  4.55 us
    unnamed x52, local copies, waits for them, and re-layouts  3.58 us
  transfers between devices with their start and end apart: 41, of which 16 were waited for; matrix products, arithmetic and copies ran while one was open for 17% of the time, Pallas kernels for 0%

profile of v1, /device:TPU:0, one launch (start us, length us, event | category | flops | bytes accessed | tf_op | source)
XLA Modules:
  0.0 151.9 jit_solution(1395906452697731006)
XLA Ops:
  0.5 2.6 %collective-permute-start.1 = (bf16[32,3584]{1,0:T(8,128)(2,1)}, bf16[32,3584]{1,0:T(8,128)(2,1)}, u32[]{:S(2)}, u32[]{:S(2)}) collective-permute-start(bf16[32,3584]{1,0:T(8,128)(2,1)} %bitcast.45), channel_id=1, source_target_pairs={{0,4},{1,5},{4,8},{5,9},{8,12},{9,13},{12,14},{13,15},{14,10},{15,... | collective-permute-start | bytes 688136 | tf_op jit(solution)/shard_map/ppermute | solution.py:241
  3.1 0.7 compare_select_fusion
  3.8 1.4 copy.30
  5.2 2.0 %gather_fusion = bf16[128,2,576]{2,1,0:T(2,128)(2,1)} fusion(bf16[128,2,576]{2,1,0:T(2,128)(2,1)S(1)} %copy.30, s32[1024]{0:T(1024)S(1)} %pad_clamp_fusion), kind=kCustom, calls=%fused_computation | custom fusion | bytes 590336 | tf_op jit(solution)/shard_map/gather | solution.py:245
  7.2 6.4 %all-to-all-start = ((bf16[128,2,576]{2,1,0:T(2,128)(2,1)}), bf16[128,2,576]{2,1,0:T(2,128)(2,1)S(1)}, u32[]{:S(2)}, u32[]{:S(2)}) async-start(bf16[128,2,576]{2,1,0:T(2,128)(2,1)} %gather_fusion), calls=%async_computation | async-start | bytes 655360 | tf_op jit(solution)/shard_map/all_to_all | solution.py:246
  13.6 4.5 %reshape.59 = bf16[4,8,64,576]{3,2,1,0:T(8,128)(2,1)S(1)} reshape(bf16[4,8,36864]{2,1,0:T(8,128)(2,1)} %param.13) | data formatting | bytes 4718592 | tf_op jit(solution)/shard_map/reshape | solution.py:183
  18.1 1.4 fusion.33
  19.5 1.2 gather_fusion.1
  20.9 1.9 %collective-permute-start.3 = (bf16[32,3584]{1,0:T(8,128)(2,1)}, bf16[32,3584]{1,0:T(8,128)(2,1)}, u32[]{:S(2)}, u32[]{:S(2)}) collective-permute-start(bf16[32,3584]{1,0:T(8,128)(2,1)} %collective-permute-done.1.refs_2_), channel_id=1, source_target_pairs={{0,4},{1,5},{4,8},{5,9},{8,12},{9,13},{12,14},{13,15},{14,10},{15,... | collective-permute-start | bytes 688136 | tf_op jit(solution)/shard_map/ppermute | solution.py:241
  23.2 6.4 %collective-permute-done.3.refs_4_ = bf16[32,3584]{1,0:T(8,128)(2,1)} collective-permute-done((bf16[32,3584]{1,0:T(8,128)(2,1)}, bf16[32,3584]{1,0:T(8,128)(2,1)}, u32[]{:S(2)}, u32[]{:S(2)}) %collective-permute-start.3) | collective-permute-done | bytes 229408 | tf_op jit(solution)/shard_map/ppermute | solution.py:241
  29.5 1.3 collective-permute-start.5
  30.8 0.8 collective-permute-start.4
  32.0 1.0 reshape.80
  33.2 2.5 %fusion.32 = (f32[4,8,64]{2,0,1:T(4,128)S(1)}, f32[4,8,64,32]{2,3,0,1:T(8,128)S(1)}) fusion(bf16[4,8,64,576]{3,2,1,0:T(8,128)(2,1)S(1)} %reshape.59, bf16[8,32,576,1]{2,1,0,3:T(8,128)(2,1)} %reshape.80, pred[8,32]{1,0:T(8,128)(4,1)S(1)} %iota_compare_fusion.1), kind=kOutput, calls=%fused_computation.57 | convolution fusion | flops 75692032 | bytes 2924800 | tf_op jit(solution)/shard_map/srhk,rpk->srhp/dot_general | solution.py:185
  36.8 1.3 collective-permute-start.16
  38.2 2.7 %collective-permute-done.16 = bf16[32,640]{1,0:T(8,128)(2,1)S(1)} collective-permute-done((bf16[32,640]{1,0:T(8,128)(2,1)S(1)}, bf16[32,640]{1,0:T(8,128)(2,1)S(1)}, u32[]{:S(2)}, u32[]{:S(2)}) %collective-permute-start.16) | collective-permute-done | bytes 40992 | tf_op jit(solution)/shard_map/ppermute | solution.py:241
  40.9 1.3 collective-permute-start.17
  42.2 2.7 %collective-permute-done.17 = bf16[32,640]{1,0:T(8,128)(2,1)S(1)} collective-permute-done((bf16[32,640]{1,0:T(8,128)(2,1)S(1)}, bf16[32,640]{1,0:T(8,128)(2,1)S(1)}, u32[]{:S(2)}, u32[]{:S(2)}) %collective-permute-start.17) | collective-permute-done | bytes 40992 | tf_op jit(solution)/shard_map/ppermute | solution.py:241
  44.9 2.2 %collective-permute-start.18 = (bf16[32,640]{1,0:T(8,128)(2,1)S(1)}, bf16[32,640]{1,0:T(8,128)(2,1)S(1)}, u32[]{:S(2)}, u32[]{:S(2)}) collective-permute-start(bf16[32,640]{1,0:T(8,128)(2,1)S(1)} %bitcast.38), channel_id=1, source_target_pairs={{0,6},{1,7},{4,2},{5,3},{8,0},{9,1},{12,4},{13,5},{14,8},{15,9},{1... | collective-permute-start | bytes 122888 | tf_op jit(solution)/shard_map/ppermute | solution.py:241
  47.1 2.8 %collective-permute-done.18 = bf16[32,640]{1,0:T(8,128)(2,1)S(1)} collective-permute-done((bf16[32,640]{1,0:T(8,128)(2,1)S(1)}, bf16[32,640]{1,0:T(8,128)(2,1)S(1)}, u32[]{:S(2)}, u32[]{:S(2)}) %collective-permute-start.18) | collective-permute-done | bytes 40992 | tf_op jit(solution)/shard_map/ppermute | solution.py:241
  49.9 2.1 %collective-permute-start.19 = (bf16[32,640]{1,0:T(8,128)(2,1)S(1)}, bf16[32,640]{1,0:T(8,128)(2,1)S(1)}, u32[]{:S(2)}, u32[]{:S(2)}) collective-permute-start(bf16[32,640]{1,0:T(8,128)(2,1)S(1)} %bitcast.39), channel_id=1, source_target_pairs={{0,8},{1,9},{4,12},{5,13},{8,14},{9,15},{12,10},{13,11},{14,6},{15... | collective-permute-start | bytes 122888 | tf_op jit(solution)/shard_map/ppermute | solution.py:241
  52.0 2.8 %collective-permute-done.19 = bf16[32,640]{1,0:T(8,128)(2,1)S(1)} collective-permute-done((bf16[32,640]{1,0:T(8,128)(2,1)S(1)}, bf16[32,640]{1,0:T(8,128)(2,1)S(1)}, u32[]{:S(2)}, u32[]{:S(2)}) %collective-permute-start.19) | collective-permute-done | bytes 40992 | tf_op jit(solution)/shard_map/ppermute | solution.py:241
  54.8 3.1 %collective-permute-start.20 = (bf16[32,640]{1,0:T(8,128)(2,1)S(1)}, bf16[32,640]{1,0:T(8,128)(2,1)S(1)}, u32[]{:S(2)}, u32[]{:S(2)}) collective-permute-start(bf16[32,640]{1,0:T(8,128)(2,1)S(1)} %bitcast.40), channel_id=1, source_target_pairs={{0,10},{1,11},{4,6},{5,7},{8,2},{9,3},{12,0},{13,1},{14,4},{15,5},... | collective-permute-start | bytes 122888 | tf_op jit(solution)/shard_map/ppermute | solution.py:241
  57.9 2.7 %collective-permute-done.20 = bf16[32,640]{1,0:T(8,128)(2,1)S(1)} collective-permute-done((bf16[32,640]{1,0:T(8,128)(2,1)S(1)}, bf16[32,640]{1,0:T(8,128)(2,1)S(1)}, u32[]{:S(2)}, u32[]{:S(2)}) %collective-permute-start.20) | collective-permute-done | bytes 40992 | tf_op jit(solution)/shard_map/ppermute | solution.py:241
  60.6 3.6 %collective-permute-start.21 = (bf16[32,640]{1,0:T(8,128)(2,1)S(1)}, bf16[32,640]{1,0:T(8,128)(2,1)S(1)}, u32[]{:S(2)}, u32[]{:S(2)}) collective-permute-start(bf16[32,640]{1,0:T(8,128)(2,1)S(1)} %bitcast.41), channel_id=1, source_target_pairs={{0,12},{1,13},{4,14},{5,15},{8,10},{9,11},{12,6},{13,7},{14,2},{15... | collective-permute-start | bytes 122888 | tf_op jit(solution)/shard_map/ppermute | solution.py:241
  64.3 1.6 %collective-permute-start.22 = (bf16[32,640]{1,0:T(8,128)(2,1)S(1)}, bf16[32,640]{1,0:T(8,128)(2,1)S(1)}, u32[]{:S(2)}, u32[]{:S(2)}) collective-permute-start(bf16[32,640]{1,0:T(8,128)(2,1)S(1)} %bitcast.42), channel_id=1, source_target_pairs={{0,14},{1,15},{4,10},{5,11},{8,6},{9,7},{12,2},{13,3},{14,0},{15,1... | collective-permute-start | bytes 122888 | tf_op jit(solution)/shard_map/ppermute | solution.py:241
  65.8 0.9 slice.44
  66.7 1.0 collective-permute-start.6
  67.7 3.4 %collective-permute-done.22 = bf16[32,640]{1,0:T(8,128)(2,1)S(1)} collective-permute-done((bf16[32,640]{1,0:T(8,128)(2,1)S(1)}, bf16[32,640]{1,0:T(8,128)(2,1)S(1)}, u32[]{:S(2)}, u32[]{:S(2)}) %collective-permute-start.22) | collective-permute-done | bytes 40992 | tf_op jit(solution)/shard_map/ppermute | solution.py:241
  71.7 0.9 slice.45
  73.1 4.9 %collective-permute-done.7 = bf16[16,3584]{1,0:T(8,128)(2,1)S(1)} collective-permute-done((bf16[16,3584]{1,0:T(8,128)(2,1)S(1)}, bf16[16,3584]{1,0:T(8,128)(2,1)S(1)}, u32[]{:S(2)}, u32[]{:S(2)}) %collective-permute-start.7) | collective-permute-done | bytes 114720 | tf_op jit(solution)/shard_map/ppermute | solution.py:241
  80.2 1.1 pad.8.refs_20_
  82.9 0.7 copy-done.20
  83.6 26.7 %experts.1 = (f32[32,3584]{1,0:T(8,128)}, bf16[32,3584]{1,0:T(8,128)(2,1)}, bf16[32,3584]{1,0:T(8,128)(2,1)}, bf16[32,3584]{1,0:T(8,128)(2,1)}, bf16[32,3584]{1,...) custom-call(bf16[32,3584]{1,0:T(8,128)(2,1)} %bitcast.47, ...), custom_call_target="tpu_custom_call" | custom-call | flops 13153337344 | bytes 29360128 | tf_op jit(solution)/shard_map/experts/pallas_call | solution.py:146
  110.9 1.2 collective-permute-done.28
  112.1 1.0 add_convert_fusion.8
  114.3 4.3 %collective-permute-done.29 = bf16[16,3584]{1,0:T(8,128)(2,1)S(1)} collective-permute-done((bf16[16,3584]{1,0:T(8,128)(2,1)S(1)}, bf16[16,3584]{1,0:T(8,128)(2,1)S(1)}, u32[]{:S(2)}, u32[]{:S(2)}) %collective-permute-start.29) | collective-permute-done | bytes 114720 | tf_op jit(solution)/shard_map/ppermute | solution.py:241
  118.9 1.1 add_convert_fusion.6
  120.0 3.3 %collective-permute-done.36 = bf16[16,3584]{1,0:T(8,128)(2,1)S(1)} collective-permute-done((bf16[16,3584]{1,0:T(8,128)(2,1)S(1)}, bf16[16,3584]{1,0:T(8,128)(2,1)S(1)}, u32[]{:S(2)}, u32[]{:S(2)}) %collective-permute-start.36) | collective-permute-done | bytes 114720 | tf_op jit(solution)/shard_map/ppermute | solution.py:241
  123.7 1.0 add_convert_fusion.3
  124.8 4.6 %collective-permute-done.30 = bf16[32,3584]{1,0:T(8,128)(2,1)S(1)} collective-permute-done((bf16[32,3584]{1,0:T(8,128)(2,1)S(1)}, bf16[32,3584]{1,0:T(8,128)(2,1)S(1)}, u32[]{:S(2)}, u32[]{:S(2)}) %collective-permute-start.30) | collective-permute-done | bytes 229408 | tf_op jit(solution)/shard_map/ppermute | solution.py:241
  129.7 1.0 add_convert_fusion.5
  130.7 1.8 %collective-permute-start.31 = (bf16[32,3584]{1,0:T(8,128)(2,1)S(1)}, bf16[32,3584]{1,0:T(8,128)(2,1)S(1)}, u32[]{:S(2)}, u32[]{:S(2)}) collective-permute-start(bf16[32,3584]{1,0:T(8,128)(2,1)S(1)} %add_convert_fusion.5), channel_id=1, source_target_pairs={{0,4},{1,5},{4,8},{5,9},{8,12},{9,13},{12,14},{13,15},{14,10},{15,... | collective-permute-start | bytes 688136 | tf_op jit(solution)/shard_map/ppermute | solution.py:241
  132.5 4.0 %collective-permute-done.37 = bf16[32,3584]{1,0:T(8,128)(2,1)S(1)} collective-permute-done((bf16[32,3584]{1,0:T(8,128)(2,1)S(1)}, bf16[32,3584]{1,0:T(8,128)(2,1)S(1)}, u32[]{:S(2)}, u32[]{:S(2)}) %collective-permute-start.37) | collective-permute-done | bytes 229408 | tf_op jit(solution)/shard_map/ppermute | solution.py:241
  137.4 2.4 %collective-permute-start.32 = (bf16[32,3584]{1,0:T(8,128)(2,1)S(1)}, bf16[32,3584]{1,0:T(8,128)(2,1)S(1)}, u32[]{:S(2)}, u32[]{:S(2)}) collective-permute-start(bf16[32,3584]{1,0:T(8,128)(2,1)S(1)} %add_convert_fusion.4), channel_id=1, source_target_pairs={{0,4},{1,5},{4,8},{5,9},{8,12},{9,13},{12,14},{13,15},{14,10},{15,... | collective-permute-start | bytes 688136 | tf_op jit(solution)/shard_map/ppermute | solution.py:241
  139.8 5.2 %collective-permute-done.38 = bf16[32,3584]{1,0:T(8,128)(2,1)S(1)} collective-permute-done((bf16[32,3584]{1,0:T(8,128)(2,1)S(1)}, bf16[32,3584]{1,0:T(8,128)(2,1)S(1)}, u32[]{:S(2)}, u32[]{:S(2)}) %collective-permute-start.38) | collective-permute-done | bytes 229408 | tf_op jit(solution)/shard_map/ppermute | solution.py:241
  145.1 6.0 %collective-permute-done.39 = bf16[32,3584]{1,0:T(8,128)(2,1)S(1)} collective-permute-done((bf16[32,3584]{1,0:T(8,128)(2,1)S(1)}, bf16[32,3584]{1,0:T(8,128)(2,1)S(1)}, u32[]{:S(2)}, u32[]{:S(2)}) %collective-permute-start.39) | collective-permute-done | bytes 229408 | tf_op jit(solution)/shard_map/ppermute | solution.py:241
  151.1 0.8 fusion.28
  (128 shorter events, 11.2 us)
Async XLA Ops:
  0.0 78.0 %collective-permute-start.8 = (bf16[32,3584]{1,0:T(8,128)(2,1)}, bf16[32,3584]{1,0:T(8,128)(2,1)}, u32[]{:S(2)}, u32[]{:S(2)}) collective-permute-start(bf16[32,3584]{1,0:T(8,128)(2,1)} %bitcast.44), channel_id=1, source_target_pairs={{0,1},{1,0},{2,3},{3,2},{4,5},{5,4},{6,7},{7,6},{8,9},{9,8},{10,11... | collective-permute-start | bytes 688136 | tf_op jit(solution)/shard_map/ppermute | solution.py:241
  0.5 20.5 %collective-permute-start.1 = (bf16[32,3584]{1,0:T(8,128)(2,1)}, bf16[32,3584]{1,0:T(8,128)(2,1)}, u32[]{:S(2)}, u32[]{:S(2)}) collective-permute-start(bf16[32,3584]{1,0:T(8,128)(2,1)} %bitcast.45), channel_id=1, source_target_pairs={{0,4},{1,5},{4,8},{5,9},{8,12},{9,13},{12,14},{13,15},{14,10},{15,... | collective-permute-start | bytes 688136 | tf_op jit(solution)/shard_map/ppermute | solution.py:241
  3.1 19.8 %collective-permute-start = (bf16[32,3584]{1,0:T(8,128)(2,1)}, bf16[32,3584]{1,0:T(8,128)(2,1)S(1)}, u32[]{:S(2)}, u32[]{:S(2)}) collective-permute-start(bf16[32,3584]{1,0:T(8,128)(2,1)} %bitcast.46), channel_id=1, source_target_pairs={{0,2},{1,3},{4,0},{5,1},{8,4},{9,5},{12,8},{13,9},{14,12},{15,13},... | collective-permute-start | bytes 688136 | tf_op jit(solution)/shard_map/ppermute | solution.py:241
  7.2 24.4 %all-to-all-start = ((bf16[128,2,576]{2,1,0:T(2,128)(2,1)}), bf16[128,2,576]{2,1,0:T(2,128)(2,1)S(1)}, u32[]{:S(2)}, u32[]{:S(2)}) async-start(bf16[128,2,576]{2,1,0:T(2,128)(2,1)} %gather_fusion), calls=%async_computation | async-start | bytes 655360 | tf_op jit(solution)/shard_map/all_to_all | solution.py:246
  20.9 8.6 %collective-permute-start.3 = (bf16[32,3584]{1,0:T(8,128)(2,1)}, bf16[32,3584]{1,0:T(8,128)(2,1)}, u32[]{:S(2)}, u32[]{:S(2)}) collective-permute-start(bf16[32,3584]{1,0:T(8,128)(2,1)} %collective-permute-done.1.refs_2_), channel_id=1, source_target_pairs={{0,4},{1,5},{4,8},{5,9},{8,12},{9,13},{12,14},{13,15},{14,10},{15,... | collective-permute-start | bytes 688136 | tf_op jit(solution)/shard_map/ppermute | solution.py:241
  22.8 8.0 %collective-permute-start.2 = (bf16[32,3584]{1,0:T(8,128)(2,1)S(1)}, bf16[32,3584]{1,0:T(8,128)(2,1)}, u32[]{:S(2)}, u32[]{:S(2)}) collective-permute-start(bf16[32,3584]{1,0:T(8,128)(2,1)S(1)} %collective-permute-done.refs_1_), channel_id=1, source_target_pairs={{0,2},{1,3},{4,0},{5,1},{8,4},{9,5},{12,8},{13,9},{14,12},{15,13},... | collective-permute-start | bytes 688136 | tf_op jit(solution)/shard_map/ppermute | solution.py:241
  23.1 55.5 %collective-permute-start.10 = (bf16[32,3584]{1,0:T(8,128)(2,1)}, bf16[32,3584]{1,0:T(8,128)(2,1)}, u32[]{:S(2)}, u32[]{:S(2)}) collective-permute-start(bf16[32,3584]{1,0:T(8,128)(2,1)} %collective-permute-done.1.refs_2_), channel_id=1, source_target_pairs={{0,1},{1,0},{2,3},{3,2},{4,5},{5,4},{6,7},{7,6},{8,9},{9,8},{10,11... | collective-permute-start | bytes 688136 | tf_op jit(solution)/shard_map/ppermute | solution.py:241
  29.5 34.7 %collective-permute-start.5 = (bf16[32,3584]{1,0:T(8,128)(2,1)}, bf16[32,3584]{1,0:T(8,128)(2,1)}, u32[]{:S(2)}, u32[]{:S(2)}) collective-permute-start(bf16[32,3584]{1,0:T(8,128)(2,1)} %collective-permute-done.3.refs_4_), channel_id=1, source_target_pairs={{0,4},{1,5},{4,8},{5,9},{8,12},{9,13},{12,14},{13,15},{14,10},{15,... | collective-permute-start | bytes 688136 | tf_op jit(solution)/shard_map/ppermute | solution.py:241
  30.8 40.3 %collective-permute-start.4 = (bf16[32,3584]{1,0:T(8,128)(2,1)}, bf16[32,3584]{1,0:T(8,128)(2,1)}, u32[]{:S(2)}, u32[]{:S(2)}) collective-permute-start(bf16[32,3584]{1,0:T(8,128)(2,1)} %collective-permute-done.2.refs_3_), channel_id=1, source_target_pairs={{0,2},{1,3},{4,0},{5,1},{8,4},{9,5},{12,8},{13,9},{14,12},{15,13},... | collective-permute-start | bytes 688136 | tf_op jit(solution)/shard_map/ppermute | solution.py:241
  35.7 35.4 %copy-start.14 = (bf16[32,3584]{1,0:T(8,128)(2,1)S(1)}, bf16[32,3584]{1,0:T(8,128)(2,1)}, u32[]{:S(2)}) copy-start(bf16[32,3584]{1,0:T(8,128)(2,1)} %copy-done.13) | copy-start | bytes 688132
  35.7 43.5 %copy-start.10 = (bf16[3584]{0:T(1024)(128)(2,1)S(1)}, bf16[3584]{0:T(1024)(128)(2,1)}, u32[]{:S(2)}) copy-start(bf16[3584]{0:T(1024)(128)(2,1)} %param.21) | copy-start | bytes 21508
  35.7 44.1 %copy-start.6 = (bf16[3584,16]{0,1:T(8,128)(2,1)S(1)}, bf16[3584,16]{0,1:T(8,128)(2,1)}, u32[]{:S(2)}) copy-start(bf16[3584,16]{0,1:T(8,128)(2,1)} %param.22) | copy-start | bytes 344068
  36.8 4.1 %collective-permute-start.16 = (bf16[32,640]{1,0:T(8,128)(2,1)S(1)}, bf16[32,640]{1,0:T(8,128)(2,1)S(1)}, u32[]{:S(2)}, u32[]{:S(2)}) collective-permute-start(bf16[32,640]{1,0:T(8,128)(2,1)S(1)} %bitcast.36), channel_id=1, source_target_pairs={{0,2},{1,3},{4,0},{5,1},{8,4},{9,5},{12,8},{13,9},{14,12},{15,13},... | collective-permute-start | bytes 122888 | tf_op jit(solution)/shard_map/ppermute | solution.py:241
  40.9 4.0 %collective-permute-start.17 = (bf16[32,640]{1,0:T(8,128)(2,1)S(1)}, bf16[32,640]{1,0:T(8,128)(2,1)S(1)}, u32[]{:S(2)}, u32[]{:S(2)}) collective-permute-start(bf16[32,640]{1,0:T(8,128)(2,1)S(1)} %bitcast.37), channel_id=1, source_target_pairs={{0,4},{1,5},{4,8},{5,9},{8,12},{9,13},{12,14},{13,15},{14,10},{15,... | collective-permute-start | bytes 122888 | tf_op jit(solution)/shard_map/ppermute | solution.py:241
  44.9 5.0 %collective-permute-start.18 = (bf16[32,640]{1,0:T(8,128)(2,1)S(1)}, bf16[32,640]{1,0:T(8,128)(2,1)S(1)}, u32[]{:S(2)}, u32[]{:S(2)}) collective-permute-start(bf16[32,640]{1,0:T(8,128)(2,1)S(1)} %bitcast.38), channel_id=1, source_target_pairs={{0,6},{1,7},{4,2},{5,3},{8,0},{9,1},{12,4},{13,5},{14,8},{15,9},{1... | collective-permute-start | bytes 122888 | tf_op jit(solution)/shard_map/ppermute | solution.py:241
  49.9 4.9 %collective-permute-start.19 = (bf16[32,640]{1,0:T(8,128)(2,1)S(1)}, bf16[32,640]{1,0:T(8,128)(2,1)S(1)}, u32[]{:S(2)}, u32[]{:S(2)}) collective-permute-start(bf16[32,640]{1,0:T(8,128)(2,1)S(1)} %bitcast.39), channel_id=1, source_target_pairs={{0,8},{1,9},{4,12},{5,13},{8,14},{9,15},{12,10},{13,11},{14,6},{15... | collective-permute-start | bytes 122888 | tf_op jit(solution)/shard_map/ppermute | solution.py:241
  54.8 5.8 %collective-permute-start.20 = (bf16[32,640]{1,0:T(8,128)(2,1)S(1)}, bf16[32,640]{1,0:T(8,128)(2,1)S(1)}, u32[]{:S(2)}, u32[]{:S(2)}) collective-permute-start(bf16[32,640]{1,0:T(8,128)(2,1)S(1)} %bitcast.40), channel_id=1, source_target_pairs={{0,10},{1,11},{4,6},{5,7},{8,2},{9,3},{12,0},{13,1},{14,4},{15,5},... | collective-permute-start | bytes 122888 | tf_op jit(solution)/shard_map/ppermute | solution.py:241
  60.6 6.1 %collective-permute-start.21 = (bf16[32,640]{1,0:T(8,128)(2,1)S(1)}, bf16[32,640]{1,0:T(8,128)(2,1)S(1)}, u32[]{:S(2)}, u32[]{:S(2)}) collective-permute-start(bf16[32,640]{1,0:T(8,128)(2,1)S(1)} %bitcast.41), channel_id=1, source_target_pairs={{0,12},{1,13},{4,14},{5,15},{8,10},{9,11},{12,6},{13,7},{14,2},{15... | collective-permute-start | bytes 122888 | tf_op jit(solution)/shard_map/ppermute | solution.py:241
  64.3 6.9 %collective-permute-start.22 = (bf16[32,640]{1,0:T(8,128)(2,1)S(1)}, bf16[32,640]{1,0:T(8,128)(2,1)S(1)}, u32[]{:S(2)}, u32[]{:S(2)}) collective-permute-start(bf16[32,640]{1,0:T(8,128)(2,1)S(1)} %bitcast.42), channel_id=1, source_target_pairs={{0,14},{1,15},{4,10},{5,11},{8,6},{9,7},{12,2},{13,3},{14,0},{15,1... | collective-permute-start | bytes 122888 | tf_op jit(solution)/shard_map/ppermute | solution.py:241
  66.7 5.9 %collective-permute-start.6 = (bf16[16,3584]{1,0:T(8,128)(2,1)S(1)}, bf16[16,3584]{1,0:T(8,128)(2,1)S(1)}, u32[]{:S(2)}, u32[]{:S(2)}) collective-permute-start(bf16[16,3584]{1,0:T(8,128)(2,1)S(1)} %slice.44), channel_id=1, source_target_pairs={{0,4},{1,5},{4,8},{5,9},{8,12},{9,13},{12,14},{13,15},{14,10},{15,... | collective-permute-start | bytes 344072 | tf_op jit(solution)/shard_map/ppermute | solution.py:241
  71.1 7.6 %collective-permute-start.9 = (bf16[32,3584]{1,0:T(8,128)(2,1)S(1)}, bf16[32,3584]{1,0:T(8,128)(2,1)S(1)}, u32[]{:S(2)}, u32[]{:S(2)}) collective-permute-start(bf16[32,3584]{1,0:T(8,128)(2,1)S(1)} %copy-done.14), channel_id=1, source_target_pairs={{0,1},{1,0},{2,3},{3,2},{4,5},{5,4},{6,7},{7,6},{8,9},{9,8},{10,11... | collective-permute-start | bytes 688136 | tf_op jit(solution)/shard_map/ppermute | solution.py:241
  71.2 7.9 %collective-permute-start.12 = (bf16[32,3584]{1,0:T(8,128)(2,1)}, bf16[32,3584]{1,0:T(8,128)(2,1)S(1)}, u32[]{:S(2)}, u32[]{:S(2)}) collective-permute-start(bf16[32,3584]{1,0:T(8,128)(2,1)} %collective-permute-done.3.refs_4_), channel_id=1, source_target_pairs={{0,1},{1,0},{2,3},{3,2},{4,5},{5,4},{6,7},{7,6},{8,9},{9,8},{10,11... | collective-permute-start | bytes 688136 | tf_op jit(solution)/shard_map/ppermute | solution.py:241
  72.6 5.3 %collective-permute-start.7 = (bf16[16,3584]{1,0:T(8,128)(2,1)S(1)}, bf16[16,3584]{1,0:T(8,128)(2,1)S(1)}, u32[]{:S(2)}, u32[]{:S(2)}) collective-permute-start(bf16[16,3584]{1,0:T(8,128)(2,1)S(1)} %slice.45), channel_id=1, source_target_pairs={{0,2},{1,3},{4,0},{5,1},{8,4},{9,5},{12,8},{13,9},{14,12},{15,13},... | collective-permute-start | bytes 344072 | tf_op jit(solution)/shard_map/ppermute | solution.py:241
  78.0 4.0 %collective-permute-start.23 = (bf16[256,640]{1,0:T(8,128)(2,1)S(1)}, bf16[256,640]{1,0:T(8,128)(2,1)S(1)}, u32[]{:S(2)}, u32[]{:S(2)}) collective-permute-start(bf16[256,640]{1,0:T(8,128)(2,1)S(1)} %constant_dynamic-update-slice_fusion.2.refs_16_), channel_id=1, source_target_pairs={{0,1},{1,0},{2,3},{3,2},{4,5},{5,4},{6,7},{7,6},{8,9},{9,8},{10,11... | collective-permute-start | bytes 983048 | tf_op jit(solution)/shard_map/ppermute | solution.py:241
  78.0 3.9 %collective-permute-start.11 = (bf16[32,3584]{1,0:T(8,128)(2,1)}, bf16[32,3584]{1,0:T(8,128)(2,1)S(1)}, u32[]{:S(2)}, u32[]{:S(2)}) collective-permute-start(bf16[32,3584]{1,0:T(8,128)(2,1)} %collective-permute-done.2.refs_3_), channel_id=1, source_target_pairs={{0,1},{1,0},{2,3},{3,2},{4,5},{5,4},{6,7},{7,6},{8,9},{9,8},{10,11... | collective-permute-start | bytes 688136 | tf_op jit(solution)/shard_map/ppermute | solution.py:241
  78.6 3.3 %collective-permute-start.14 = (bf16[32,3584]{1,0:T(8,128)(2,1)}, bf16[32,3584]{1,0:T(8,128)(2,1)S(1)}, u32[]{:S(2)}, u32[]{:S(2)}) collective-permute-start(bf16[32,3584]{1,0:T(8,128)(2,1)} %collective-permute-done.5.refs_6_), channel_id=1, source_target_pairs={{0,1},{1,0},{2,3},{3,2},{4,5},{5,4},{6,7},{7,6},{8,9},{9,8},{10,11... | collective-permute-start | bytes 688136 | tf_op jit(solution)/shard_map/ppermute | solution.py:241
  78.7 3.2 %collective-permute-start.13 = (bf16[32,3584]{1,0:T(8,128)(2,1)}, bf16[32,3584]{1,0:T(8,128)(2,1)S(1)}, u32[]{:S(2)}, u32[]{:S(2)}) collective-permute-start(bf16[32,3584]{1,0:T(8,128)(2,1)} %collective-permute-done.4.refs_5_), channel_id=1, source_target_pairs={{0,1},{1,0},{2,3},{3,2},{4,5},{5,4},{6,7},{7,6},{8,9},{9,8},{10,11... | collective-permute-start | bytes 688136 | tf_op jit(solution)/shard_map/ppermute | solution.py:241
  79.1 2.9 %collective-permute-start.15 = (bf16[32,3584]{1,0:T(8,128)(2,1)S(1)}, bf16[32,3584]{1,0:T(8,128)(2,1)S(1)}, u32[]{:S(2)}, u32[]{:S(2)}) collective-permute-start(bf16[32,3584]{1,0:T(8,128)(2,1)S(1)} %constant_dynamic-update-slice_fusion.refs_7_), channel_id=1, source_target_pairs={{0,1},{1,0},{2,3},{3,2},{4,5},{5,4},{6,7},{7,6},{8,9},{9,8},{10,11... | collective-permute-start | bytes 688136 | tf_op jit(solution)/shard_map/ppermute | solution.py:241
  110.3 27.0 %copy-start.4 = (bf16[32,3584]{1,0:T(8,128)(2,1)S(1)}, bf16[32,3584]{1,0:T(8,128)(2,1)}, u32[]{:S(2)}) copy-start(bf16[32,3584]{1,0:T(8,128)(2,1)} %get-tuple-element.25) | copy-start | bytes 688132
  110.3 34.7 %copy-start.3 = (bf16[32,3584]{1,0:T(8,128)(2,1)S(1)}, bf16[32,3584]{1,0:T(8,128)(2,1)}, u32[]{:S(2)}) copy-start(bf16[32,3584]{1,0:T(8,128)(2,1)} %get-tuple-element.33) | copy-start | bytes 688132
  110.3 1.8 %collective-permute-start.28 = (bf16[32,3584]{1,0:T(8,128)(2,1)}, bf16[32,3584]{1,0:T(8,128)(2,1)S(1)}, u32[]{:S(2)}, u32[]{:S(2)}) collective-permute-start(bf16[32,3584]{1,0:T(8,128)(2,1)} %get-tuple-element.32), channel_id=1, source_target_pairs={{0,1},{1,0},{2,3},{3,2},{4,5},{5,4},{6,7},{7,6},{8,9},{9,8},{10,11... | collective-permute-start | bytes 688136 | tf_op jit(solution)/shard_map/ppermute | solution.py:241
  110.8 3.4 %collective-permute-start.27 = (bf16[32,3584]{1,0:T(8,128)(2,1)}, bf16[32,3584]{1,0:T(8,128)(2,1)S(1)}, u32[]{:S(2)}, u32[]{:S(2)}) collective-permute-start(bf16[32,3584]{1,0:T(8,128)(2,1)} %get-tuple-element.30), channel_id=1, source_target_pairs={{0,1},{1,0},{2,3},{3,2},{4,5},{5,4},{6,7},{7,6},{8,9},{9,8},{10,11... | collective-permute-start | bytes 688136 | tf_op jit(solution)/shard_map/ppermute | solution.py:241
  113.1 5.5 %collective-permute-start.29 = (bf16[16,3584]{1,0:T(8,128)(2,1)S(1)}, bf16[16,3584]{1,0:T(8,128)(2,1)S(1)}, u32[]{:S(2)}, u32[]{:S(2)}) collective-permute-start(bf16[16,3584]{1,0:T(8,128)(2,1)S(1)} %get-tuple-element.39), channel_id=1, source_target_pairs={{0,4},{1,5},{4,8},{5,9},{8,12},{9,13},{12,14},{13,15},{14,10},{15,... | collective-permute-start | bytes 344072 | tf_op jit(solution)/shard_map/ppermute | solution.py:241
  113.2 31.9 %collective-permute-start.24 = (bf16[32,3584]{1,0:T(8,128)(2,1)}, bf16[32,3584]{1,0:T(8,128)(2,1)S(1)}, u32[]{:S(2)}, u32[]{:S(2)}) collective-permute-start(bf16[32,3584]{1,0:T(8,128)(2,1)} %get-tuple-element.24), channel_id=1, source_target_pairs={{0,1},{1,0},{2,3},{3,2},{4,5},{5,4},{6,7},{7,6},{8,9},{9,8},{10,11... | collective-permute-start | bytes 688136 | tf_op jit(solution)/shard_map/ppermute | solution.py:241
  113.6 23.2 %collective-permute-start.25 = (bf16[32,3584]{1,0:T(8,128)(2,1)}, bf16[32,3584]{1,0:T(8,128)(2,1)S(1)}, u32[]{:S(2)}, u32[]{:S(2)}) collective-permute-start(bf16[32,3584]{1,0:T(8,128)(2,1)} %get-tuple-element.26), channel_id=1, source_target_pairs={{0,1},{1,0},{2,3},{3,2},{4,5},{5,4},{6,7},{7,6},{8,9},{9,8},{10,11... | collective-permute-start | bytes 688136 | tf_op jit(solution)/shard_map/ppermute | solution.py:241
  113.7 11.0 %collective-permute-start.26 = (bf16[32,3584]{1,0:T(8,128)(2,1)}, bf16[32,3584]{1,0:T(8,128)(2,1)S(1)}, u32[]{:S(2)}, u32[]{:S(2)}) collective-permute-start(bf16[32,3584]{1,0:T(8,128)(2,1)} %get-tuple-element.28), channel_id=1, source_target_pairs={{0,1},{1,0},{2,3},{3,2},{4,5},{5,4},{6,7},{7,6},{8,9},{9,8},{10,11... | collective-permute-start | bytes 688136 | tf_op jit(solution)/shard_map/ppermute | solution.py:241
  114.1 5.8 %collective-permute-start.35 = (bf16[32,3584]{1,0:T(8,128)(2,1)}, bf16[32,3584]{1,0:T(8,128)(2,1)S(1)}, u32[]{:S(2)}, u32[]{:S(2)}) collective-permute-start(bf16[32,3584]{1,0:T(8,128)(2,1)} %get-tuple-element.38), channel_id=1, source_target_pairs={{0,1},{1,0},{2,3},{3,2},{4,5},{5,4},{6,7},{7,6},{8,9},{9,8},{10,11... | collective-permute-start | bytes 688136 | tf_op jit(solution)/shard_map/ppermute | solution.py:241
  118.6 4.8 %collective-permute-start.36 = (bf16[16,3584]{1,0:T(8,128)(2,1)S(1)}, bf16[16,3584]{1,0:T(8,128)(2,1)S(1)}, u32[]{:S(2)}, u32[]{:S(2)}) collective-permute-start(bf16[16,3584]{1,0:T(8,128)(2,1)S(1)} %get-tuple-element.40), channel_id=1, source_target_pairs={{0,2},{1,3},{4,0},{5,1},{8,4},{9,5},{12,8},{13,9},{14,12},{15,13},... | collective-permute-start | bytes 344072 | tf_op jit(solution)/shard_map/ppermute | solution.py:241
  118.9 32.3 %copy-start.1 = (f32[32,3584]{1,0:T(8,128)S(1)}, f32[32,3584]{1,0:T(8,128)}, u32[]{:S(2)}) copy-start(f32[32,3584]{1,0:T(8,128)} %get-tuple-element.22) | copy-start | bytes 1376260
  118.9 32.3 %copy-start.2 = (bf16[32,3584]{1,0:T(8,128)(2,1)S(1)}, bf16[32,3584]{1,0:T(8,128)(2,1)}, u32[]{:S(2)}) copy-start(bf16[32,3584]{1,0:T(8,128)(2,1)} %get-tuple-element.23) | copy-start | bytes 688132
  120.0 19.8 %collective-permute-start.33 = (bf16[32,3584]{1,0:T(8,128)(2,1)}, bf16[32,3584]{1,0:T(8,128)(2,1)S(1)}, u32[]{:S(2)}, u32[]{:S(2)}) collective-permute-start(bf16[32,3584]{1,0:T(8,128)(2,1)} %get-tuple-element.34), channel_id=1, source_target_pairs={{0,1},{1,0},{2,3},{3,2},{4,5},{5,4},{6,7},{7,6},{8,9},{9,8},{10,11... | collective-permute-start | bytes 688136 | tf_op jit(solution)/shard_map/ppermute | solution.py:241
  123.4 6.0 %collective-permute-start.30 = (bf16[32,3584]{1,0:T(8,128)(2,1)S(1)}, bf16[32,3584]{1,0:T(8,128)(2,1)S(1)}, u32[]{:S(2)}, u32[]{:S(2)}) collective-permute-start(bf16[32,3584]{1,0:T(8,128)(2,1)S(1)} %add_convert_fusion.6), channel_id=1, source_target_pairs={{0,4},{1,5},{4,8},{5,9},{8,12},{9,13},{12,14},{13,15},{14,10},{15,... | collective-permute-start | bytes 688136 | tf_op jit(solution)/shard_map/ppermute | solution.py:241
  124.8 6.0 %collective-permute-start.34 = (bf16[32,3584]{1,0:T(8,128)(2,1)}, bf16[32,3584]{1,0:T(8,128)(2,1)S(1)}, u32[]{:S(2)}, u32[]{:S(2)}) collective-permute-start(bf16[32,3584]{1,0:T(8,128)(2,1)} %get-tuple-element.36), channel_id=1, source_target_pairs={{0,1},{1,0},{2,3},{3,2},{4,5},{5,4},{6,7},{7,6},{8,9},{9,8},{10,11... | collective-permute-start | bytes 688136 | tf_op jit(solution)/shard_map/ppermute | solution.py:241
  129.4 7.1 %collective-permute-start.37 = (bf16[32,3584]{1,0:T(8,128)(2,1)S(1)}, bf16[32,3584]{1,0:T(8,128)(2,1)S(1)}, u32[]{:S(2)}, u32[]{:S(2)}) collective-permute-start(bf16[32,3584]{1,0:T(8,128)(2,1)S(1)} %add_convert_fusion.3), channel_id=1, source_target_pairs={{0,2},{1,3},{4,0},{5,1},{8,4},{9,5},{12,8},{13,9},{14,12},{15,13},... | collective-permute-start | bytes 688136 | tf_op jit(solution)/shard_map/ppermute | solution.py:241
  130.7 6.5 %collective-permute-start.31 = (bf16[32,3584]{1,0:T(8,128)(2,1)S(1)}, bf16[32,3584]{1,0:T(8,128)(2,1)S(1)}, u32[]{:S(2)}, u32[]{:S(2)}) collective-permute-start(bf16[32,3584]{1,0:T(8,128)(2,1)S(1)} %add_convert_fusion.5), channel_id=1, source_target_pairs={{0,4},{1,5},{4,8},{5,9},{8,12},{9,13},{12,14},{13,15},{14,10},{15,... | collective-permute-start | bytes 688136 | tf_op jit(solution)/shard_map/ppermute | solution.py:241
  136.6 8.3 %collective-permute-start.38 = (bf16[32,3584]{1,0:T(8,128)(2,1)S(1)}, bf16[32,3584]{1,0:T(8,128)(2,1)S(1)}, u32[]{:S(2)}, u32[]{:S(2)}) collective-permute-start(bf16[32,3584]{1,0:T(8,128)(2,1)S(1)} %add_convert_fusion.2), channel_id=1, source_target_pairs={{0,2},{1,3},{4,0},{5,1},{8,4},{9,5},{12,8},{13,9},{14,12},{15,13},... | collective-permute-start | bytes 688136 | tf_op jit(solution)/shard_map/ppermute | solution.py:241
  137.4 7.8 %collective-permute-start.32 = (bf16[32,3584]{1,0:T(8,128)(2,1)S(1)}, bf16[32,3584]{1,0:T(8,128)(2,1)S(1)}, u32[]{:S(2)}, u32[]{:S(2)}) collective-permute-start(bf16[32,3584]{1,0:T(8,128)(2,1)S(1)} %add_convert_fusion.4), channel_id=1, source_target_pairs={{0,4},{1,5},{4,8},{5,9},{8,12},{9,13},{12,14},{13,15},{14,10},{15,... | collective-permute-start | bytes 688136 | tf_op jit(solution)/shard_map/ppermute | solution.py:241
  145.0 6.1 %collective-permute-start.39 = (bf16[32,3584]{1,0:T(8,128)(2,1)S(1)}, bf16[32,3584]{1,0:T(8,128)(2,1)S(1)}, u32[]{:S(2)}, u32[]{:S(2)}) collective-permute-start(bf16[32,3584]{1,0:T(8,128)(2,1)S(1)} %add_convert_fusion.1), channel_id=1, source_target_pairs={{0,2},{1,3},{4,0},{5,1},{8,4},{9,5},{12,8},{13,9},{14,12},{15,13},... | collective-permute-start | bytes 688136 | tf_op jit(solution)/shard_map/ppermute | solution.py:241
  (14 other events, 89.0 us)

commit v2 on v1

v2 whole, which is shorter than its diff:
```python
import jax
import jax.numpy as jnp
from jax import lax
from jax.experimental import pallas as pl
from jax.experimental.pallas import tpu as pltpu
from jax.sharding import PartitionSpec as P

qk_scale = 192.0 ** (-0.5)
LANES = 128


def ring_of(chips):
    return list(range(0, chips, 2)) + list(range(chips - 1, 0, -2))


def shift_perm(chips, by):
    ring = ring_of(chips)
    return [
        (2 * ring[p] + core, 2 * ring[(p + by) % chips] + core)
        for p in range(chips)
        for core in range(2)
    ]


def sibling_perm(chips):
    return [(d, d ^ 1) for d in range(2 * chips)]


def distances(chips):
    half = chips // 2
    order = [0]
    for t in range(1, half):
        order += [t, -t]
    return order + [half]


def tile_of(size, most):
    return max(t for t in range(LANES, min(size, most) + 1, LANES) if size % t == 0)


def norm_kernel(blocks, rows, latent, width, *refs):
    pick = refs[0]
    pooled = refs[1 : 1 + blocks]
    resid = refs[1 + blocks : 1 + 2 * blocks]
    w_out, gain, w_router, x, scale, weight, hidden, joined, ssq, logits = refs[1 + 2 * blocks :]
    step = pl.program_id(0)
    cols = w_out.shape[1]
    total = blocks * rows
    experts_all = w_router.shape[0]
    chunk = min(512, total)

    @pl.when(step == 0)
    def _():
        for b in range(blocks):
            joined[b * rows : (b + 1) * rows, :] = pooled[b][...]
        ssq[...] = jnp.zeros_like(ssq)
        logits[...] = jnp.zeros_like(logits)

    g = gain[...].astype(jnp.float32)
    for c in range(0, total, chunk):
        proj = jnp.dot(
            joined[c : c + chunk, :latent], w_out[...], preferred_element_type=jnp.float32
        )
        for b in range(c // rows, (c + chunk) // rows):
            at = slice(b * rows, (b + 1) * rows)
            h = proj[b * rows - c : (b + 1) * rows - c] + resid[b][...].astype(jnp.float32)
            if b == 0:
                hidden[...] = h
            x[at, :] = (h * g).astype(jnp.bfloat16)
            sq = h * h
            part = sq[:, :LANES]
            for k in range(1, cols // LANES):
                part = part + sq[:, k * LANES : (k + 1) * LANES]
            ssq[at, :] += part
        logits[c : c + chunk, :] += lax.dot_general(
            x[c : c + chunk, :],
            w_router[...],
            (((1,), (1,)), ((), ())),
            preferred_element_type=jnp.float32,
        )

    @pl.when(step == pl.num_programs(0) - 1)
    def _():
        mean = jnp.sum(ssq[...], axis=1, keepdims=True) * (1.0 / width)
        r = lax.rsqrt(mean + 1e-06)
        mask = joined[:, latent : latent + experts_all].astype(jnp.float32)
        affinity = jax.nn.sigmoid(logits[...] * r) * mask
        lane = lax.broadcasted_iota(jnp.int32, affinity.shape, 1)
        mine = jnp.sum(jnp.where(lane == pick[0], affinity, 0.0), axis=1, keepdims=True)
        gate = 2.5 * mine / jnp.sum(affinity, axis=1, keepdims=True)
        scale[...] = jnp.broadcast_to(r, (total, LANES))
        weight[...] = jnp.broadcast_to(gate, (total, LANES))


def mib(amount):
    return (int(amount) // (1 << 20) + 1) << 20


def normalize(pick, packets, resid_blocks, w_out, gain, w_router_t):
    blocks = len(packets)
    rows, width = resid_blocks[0].shape
    latent = w_out.shape[0]
    total = blocks * rows
    cols = tile_of(width, 512)
    packed = packets[0].shape[1]
    experts_all = w_router_t.shape[0]

    def whole(a):
        return pl.BlockSpec(a.shape, lambda i: (0, 0), pipeline_mode=pl.Buffered(1))

    def tiles(height):
        return pl.BlockSpec((height, cols), lambda i: (0, i))

    need = total * (cols * 24 + packed * 4 + 6 * LANES * 4) + 4 * latent * cols
    return pl.pallas_call(
        lambda *refs: norm_kernel(blocks, rows, latent, width, *refs),
        grid=(width // cols,),
        in_specs=[pl.BlockSpec(memory_space=pltpu.SMEM)]
        + [whole(a) for a in packets]
        + [tiles(rows)] * blocks
        + [tiles(latent), tiles(1), tiles(experts_all)],
        out_shape=[
            jax.ShapeDtypeStruct((total, width), jnp.bfloat16),
            jax.ShapeDtypeStruct((total, LANES), jnp.float32),
            jax.ShapeDtypeStruct((total, LANES), jnp.float32),
            jax.ShapeDtypeStruct((rows, width), jnp.float32),
        ],
        out_specs=[
            tiles(total),
            pl.BlockSpec((total, LANES), lambda i: (0, 0)),
            pl.BlockSpec((total, LANES), lambda i: (0, 0)),
            tiles(rows),
        ],
        scratch_shapes=[
            pltpu.VMEM((total, packed), jnp.bfloat16),
            pltpu.VMEM((total, LANES), jnp.float32),
            pltpu.VMEM((total, experts_all), jnp.float32),
        ],
        compiler_params=pltpu.CompilerParams(
            dimension_semantics=("arbitrary",), vmem_limit_bytes=mib(need) + (4 << 20)
        ),
        cost_estimate=pl.CostEstimate(
            flops=2 * total * width * latent,
            bytes_accessed=2 * total * width * 2 + latent * width * 2,
            transcendentals=total,
        ),
        name="normalize",
    )(pick, *packets, *resid_blocks, w_out, gain, w_router_t)


def expert_kernel(rows, gate_steps, x, scale, weight, w_gate, w_up, w_down, *refs):
    outs, act = refs[:-1], refs[-1]
    step = pl.program_id(0)
    total = x.shape[0]
    gate_tile = w_gate.shape[2]
    chunk = min(512, total)
    chunks = total // chunk

    @pl.when(step < gate_steps)
    def _():
        cols = pl.ds(pl.multiple_of(step * gate_tile, gate_tile), gate_tile)
        for i in range(chunks):
            at = pl.ds(i * chunk, chunk)
            xs = x[at, :]
            r = scale[at, :1]
            a = jnp.dot(xs, w_gate[0], preferred_element_type=jnp.float32) * r
            b = jnp.dot(xs, w_up[0], preferred_element_type=jnp.float32) * r
            act[at, cols] = (jax.nn.silu(a) * b * weight[at, :1]).astype(jnp.bfloat16)

    @pl.when(step >= gate_steps)
    def _():
        per = chunk // rows
        for i in range(chunks):
            y = jnp.dot(
                act[i * chunk : (i + 1) * chunk, :], w_down[0], preferred_element_type=jnp.float32
            )
            for b in range(per):
                outs[i * per + b][...] = y[b * rows : (b + 1) * rows].astype(jnp.bfloat16)


def experts(rows, x, scale, weight, wg, wu, wd):
    total, width = x.shape
    blocks = total // rows
    hidden_units = wg.shape[2]
    gate_tile = tile_of(hidden_units, 256)
    gate_steps = hidden_units // gate_tile
    down_tile = tile_of(width, 512)
    down_steps = width // down_tile

    def whole(a):
        return pl.BlockSpec(a.shape, lambda i: (0, 0), pipeline_mode=pl.Buffered(1))

    def gate_at(i):
        return (0, 0, jnp.clip(i, 0, gate_steps - 1))

    def down_at(i):
        return (0, 0, jnp.clip(i - gate_steps, 0, down_steps - 1))

    def out_at(i):
        return (0, jnp.clip(i - gate_steps, 0, down_steps - 1))

    need = (
        total * (2 * width + 2 * hidden_units + 8 * down_tile + 2 * LANES * 4)
        + 8 * width * gate_tile
        + 4 * hidden_units * down_tile
        + min(512, total) * gate_tile * 16
    )
    return pl.pallas_call(
        lambda *refs: expert_kernel(rows, gate_steps, *refs),
        grid=(gate_steps + down_steps,),
        in_specs=[whole(x), whole(scale), whole(weight)]
        + [
            pl.BlockSpec((1, width, gate_tile), gate_at),
            pl.BlockSpec((1, width, gate_tile), gate_at),
            pl.BlockSpec((1, hidden_units, down_tile), down_at),
        ],
        out_shape=[jax.ShapeDtypeStruct((rows, width), jnp.bfloat16)] * blocks,
        out_specs=[pl.BlockSpec((rows, down_tile), out_at)] * blocks,
        scratch_shapes=[pltpu.VMEM((total, hidden_units), jnp.bfloat16)],
        compiler_params=pltpu.CompilerParams(
            dimension_semantics=("arbitrary",), vmem_limit_bytes=mib(need) + (6 << 20)
        ),
        cost_estimate=pl.CostEstimate(
            flops=2 * total * width * 3 * hidden_units,
            bytes_accessed=3 * width * hidden_units * 2 + 2 * total * width * 2,
            transcendentals=total * hidden_units,
        ),
        name="experts",
    )(x, scale, weight, wg, wu, wd)


def attention(q_abs, new_lat, owned_cache, row_lengths, latent):
    step_count, row_count, kv_width = new_lat.shape
    head_count = q_abs.shape[2] // kv_width
    context = owned_cache.shape[1]
    queries = q_abs.reshape(step_count, row_count, head_count, kv_width)
    cache_scores = (
        jnp.einsum("srhk,rpk->srhp", queries, owned_cache, preferred_element_type=jnp.float32)
        * qk_scale
    )
    visible = jnp.arange(context)[None, :] < row_lengths[:, None]
    cache_scores = jnp.where(visible[None, :, None, :], cache_scores, -1e30)
    fresh_scores = (
        jnp.einsum("srhk,trk->srht", queries, new_lat, preferred_element_type=jnp.float32)
        * qk_scale
    )
    causal = jnp.arange(step_count)[:, None] >= jnp.arange(step_count)[None, :]
    fresh_scores = jnp.where(causal[:, None, None, :], fresh_scores, -1e30)
    scores = jnp.concatenate([cache_scores, fresh_scores], axis=-1)
    weights = jax.nn.softmax(scores, axis=-1).astype(jnp.bfloat16)
    pooled = jnp.einsum(
        "srhp,rpl->srl",
        weights[..., :context],
        owned_cache[..., :latent],
        preferred_element_type=jnp.float32,
    )
    pooled = pooled + jnp.einsum(
        "srht,trl->srl",
        weights[..., context:],
        new_lat[..., :latent],
        preferred_element_type=jnp.float32,
    )
    return pooled.astype(jnp.bfloat16)


def local(
    q_abs,
    new_lat,
    latent_cache,
    lengths,
    owner,
    resid,
    routes,
    w_out,
    norm_gain,
    w_router,
    w_gate,
    w_up,
    w_down,
):
    devices = lax.axis_size("expert")
    device_index = lax.axis_index("expert")
    step_count, row_count, width = resid.shape
    rows = step_count * row_count
    experts_all = w_router.shape[1]
    sharers = devices // experts_all
    chips = devices // 2
    half = chips // 2
    cut = rows // 2
    order = distances(chips)
    sibling = sibling_perm(chips)

    def send(a, perm):
        return lax.ppermute(a, "expert", perm)

    to_right, to_left = shift_perm(chips, 1), shift_perm(chips, -1)

    wanted = (owner[:, None] == jnp.arange(owner.shape[0], dtype=jnp.int32)).astype(jnp.bfloat16)
    ordered = jnp.einsum(
        "jr,rpk->jpk", wanted, latent_cache, preferred_element_type=jnp.float32
    ).astype(jnp.bfloat16)
    owned_cache = lax.all_to_all(ordered, "expert", split_axis=0, concat_axis=1, tiled=True)

    mine = resid.reshape(rows, width)
    held = {0: mine}
    for t in range(1, half):
        held[-t] = send(held[-t + 1], to_right)
        held[t] = send(held[t - 1], to_left)
    held[half] = jnp.concatenate(
        [send(held[1 - half][:cut], to_right), send(held[half - 1][cut:], to_left)], axis=0
    )
    resid_own = [held[d] for d in order]
    resid_sib = [send(a, sibling) for a in resid_own]

    row_owner = lax.dynamic_slice_in_dim(owner, device_index * row_count, row_count)
    row_lengths = jnp.sum(
        jnp.where(
            row_owner[:, None] == jnp.arange(owner.shape[0], dtype=jnp.int32), lengths[None, :], 0
        ),
        axis=1,
    )
    routed = jnp.any(routes[..., None] == jnp.arange(LANES, dtype=jnp.int32), axis=2)
    routed = routed.astype(jnp.bfloat16)
    gain = norm_gain[None, :]
    pick = (device_index // sharers).astype(jnp.int32)[None]
    owned_cache, row_lengths, routed, gain, pick = lax.optimization_barrier(
        (owned_cache, row_lengths, routed, gain, pick)
    )
    pooled = attention(q_abs, new_lat, owned_cache, row_lengths, w_out.shape[0])

    packet = jnp.concatenate([pooled, routed], axis=2).reshape(rows, -1)
    packets = {0: packet}
    for t in range(1, half):
        packets[-t], packets[t] = lax.optimization_barrier(
            (send(packets[1 - t], to_right), send(packets[t - 1], to_left))
        )
    packets[half] = send(packets[1 - half], to_right)
    packets_own = [packets[d] for d in order]
    packets_sib = [send(a, sibling) for a in packets_own]

    x, scale, weight, hidden = normalize(
        pick, packets_own + packets_sib, resid_own + resid_sib, w_out, gain, w_router.T
    )
    outs = experts(rows, x, scale, weight, w_gate, w_up, w_down)
    own = dict(zip(order, outs[:chips]))
    to_sib = dict(zip(order, outs[chips:]))

    f32 = jnp.float32
    got = {d: send(to_sib[d], sibling) for d in reversed(order)}

    def part(d, lo=0, hi=rows):
        return own[d][lo:hi].astype(f32) + got[d][lo:hi].astype(f32)

    def both(right, left):
        right, left = lax.optimization_barrier(
            (
                send(right.astype(jnp.bfloat16), to_right),
                send(left.astype(jnp.bfloat16), to_left),
            )
        )
        return right.astype(f32), left.astype(f32)

    right, left = both(part(half, 0, cut), part(half, cut, rows))
    right = jnp.concatenate([right, jnp.zeros((rows - cut, width), f32)], axis=0)
    left = jnp.concatenate([jnp.zeros((cut, width), f32), left], axis=0)
    for t in range(half - 1, 0, -1):
        right, left = both(part(t) + right, part(-t) + left)
    mixed = hidden + part(0) + right + left
    return mixed.astype(jnp.bfloat16).reshape(step_count, row_count, width)


def solution(mesh):
    return jax.shard_map(
        local,
        mesh=mesh,
        in_specs=(
            P(None, ("group", "expert"), None),
            P(None, ("group", "expert"), None),
            P("group", "expert", None),
            P("group"),
            P("group"),
            P(None, ("group", "expert"), None),
            P(None, ("group", "expert"), None),
            P(),
            P(),
            P(),
            P("expert", None, None),
            P("expert", None, None),
            P("expert", None, None),
        ),
        out_specs=P(None, ("group", "expert"), None),
        check_vma=False,
    )
```

time: 153 us -> 133 us (0.87)
  waiting for transfers between devices: 57.6 us -> 41.5 us
  other arithmetic: 7.36 us -> 3.21 us
  Pallas kernels: 26.7 us -> 23.7 us
  matrix products: 4.17 us -> 6.03 us
    ppermute x40 -> x47, waiting for transfers between devices: 57.6 us -> 41.5 us  [send(): return lax.ppermute(a, 'expert', perm)]
    unnamed x52 -> x23, local copies, waits for them, and re-layouts: 3.58 us -> 9.36 us
    convert_element_type x9 -> x8, other arithmetic: 4.94 us -> 0.56 us  [the longest x4 0.31 us: both(): left.astype(jnp.bfloat16)]
    gather x2 -> x0, local copies, waits for them, and re-layouts: 3.19 us -> none  [the longest x1 1.96 us: local(): latent_cache.at[owner].get(mode='promise_in_bounds', unique_indices=True)]
    pallas_call x1 -> x2, Pallas kernels: 26.7 us -> 23.7 us  [the longest x1 17.1 us: experts(): pl.pallas_call(lambda *refs: expert_kernel(rows, gate_steps, *refs), grid...]
    ppermute x40 -> x47, starting transfers between devices: 32.8 us -> 33.3 us  [send(): return lax.ppermute(a, 'expert', perm)]
  transfers between devices with their start and end apart: 41 -> 48, of which waited for: 16 -> 19; matrix products, arithmetic and copies ran while one was open for 17% -> 12% of each run, Pallas kernels for 0% -> 0%
where the time goes in v2:
time: 133 us; the launch traced here: 132 us
  waiting for transfers between devices  41.5 us (31%)
  starting transfers between devices  39.7 us (30%)
  Pallas kernels  23.7 us (18%)
  local copies, waits for them, and re-layouts  17.6 us (13%)
  matrix products  6.03 us (5%)
  other arithmetic  3.21 us (2%)
    ppermute x47, waiting for transfers between devices, send(): return lax.ppermute(a, 'expert', perm)  41.5 us
    ppermute x47, starting transfers between devices, send(): return lax.ppermute(a, 'expert', perm)  33.3 us
    pallas_call x1, Pallas kernels, experts(): pl.pallas_call(lambda *refs: expert_kernel(rows, gate_steps, *refs), grid...  17.1 us
    unnamed x23, local copies, waits for them, and re-layouts  9.36 us
    pallas_call x1, Pallas kernels, normalize(): pl.pallas_call(lambda *refs: norm_kernel(blocks, rows, latent, width, *re...  6.59 us
    all_to_all x1, starting transfers between devices, local(): lax.all_to_all(ordered, 'expert', split_axis=0, concat_axis=1, tiled=True)  6.43 us
    reshape x1, local copies, waits for them, and re-layouts, attention(): queries = q_abs.reshape(step_count, row_count, head_count, kv_width)  4.55 us
    dot_general x1, matrix products, attention(): jnp.einsum('srhk,rpk->srhp', queries, owned_cache, preferred_element_type...  3.41 us
  transfers between devices with their start and end apart: 48, of which 19 were waited for; matrix products, arithmetic and copies ran while one was open for 12% of the time, Pallas kernels for 0%

profile of v2, /device:TPU:0, one launch (start us, length us, event | category | flops | bytes accessed | tf_op | source)
XLA Modules:
  0.0 132.1 jit_solution(4561776264767567881)
XLA Ops:
  0.0 3.0 %collective-permute-start.16 = (bf16[32,3584]{1,0:T(8,128)(2,1)}, bf16[32,3584]{1,0:T(8,128)(2,1)S(1)}, u32[]{:S(2)}, u32[]{:S(2)}) collective-permute-start(bf16[32,3584]{1,0:T(8,128)(2,1)} %bitcast.41), channel_id=1, source_target_pairs={{0,4},{1,5},{4,8},{5,9},{8,12},{9,13},{12,14},{13,15},{14,10},{15,... | collective-permute-start | bytes 688136 | tf_op jit(solution)/shard_map/ppermute | solution.py:294
  3.0 1.0 convolution_convert_fusion
  4.0 1.3 copy.35
  5.3 6.4 %all-to-all-start = ((bf16[128,2,576]{2,1,0:T(2,128)(2,1)}), bf16[128,2,576]{2,1,0:T(2,128)(2,1)}, u32[]{:S(2)}, u32[]{:S(2)}) async-start(bf16[128,2,576]{2,1,0:T(2,128)(2,1)} %copy.35), calls=%async_computation | async-start | bytes 655360 | tf_op jit(solution)/shard_map/all_to_all | solution.py:302
  12.5 0.8 fusion.29
  13.3 4.5 %reshape.51 = bf16[4,8,64,576]{3,2,1,0:T(8,128)(2,1)S(1)} reshape(bf16[4,8,36864]{2,1,0:T(8,128)(2,1)} %param.13) | data formatting | bytes 4718592 | tf_op jit(solution)/shard_map/reshape | solution.py:236
  17.9 1.4 %fusion.36 = (f32[4,8,64]{2,0,1:T(4,128)S(1)}, f32[4,8,64,4]{2,3,0,1:T(4,128)S(1)}) fusion(bf16[4,8,64,576]{3,2,1,0:T(8,128)(2,1)S(1)} %reshape.51, bf16[4,8,576,1]{2,1,0,3:T(8,128)(2,1)S(1)} %bitcast.51, pred[4,4]{1,0:T(4,128)(4,1)S(1)} %iota_compare_fusion.4), kind=kOutput, calls=%fused_computation.51 | convolution fusion | flops 9459712 | bytes 2437136 | tf_op jit(solution)/shard_map/srhk,trk->srht/dot_general | solution.py:244
  19.4 1.9 %collective-permute-start.18 = (bf16[32,3584]{1,0:T(8,128)(2,1)S(1)}, bf16[32,3584]{1,0:T(8,128)(2,1)S(1)}, u32[]{:S(2)}, u32[]{:S(2)}) collective-permute-start(bf16[32,3584]{1,0:T(8,128)(2,1)S(1)} %collective-permute-done.16.refs_19_), channel_id=1, source_target_pairs={{0,4},{1,5},{4,8},{5,9},{8,12},{9,13},{12,14},{13,15},{14,10},{15,... | collective-permute-start | bytes 688136 | tf_op jit(solution)/shard_map/ppermute | solution.py:294
  21.7 5.9 %collective-permute-done.18.refs_21_ = bf16[32,3584]{1,0:T(8,128)(2,1)S(1)} collective-permute-done((bf16[32,3584]{1,0:T(8,128)(2,1)S(1)}, bf16[32,3584]{1,0:T(8,128)(2,1)S(1)}, u32[]{:S(2)}, u32[]{:S(2)}) %collective-permute-start.18) | collective-permute-done | bytes 229408 | tf_op jit(solution)/shard_map/ppermute | solution.py:294
  27.6 1.3 collective-permute-start.20
  28.9 1.0 copy.78
  30.6 3.4 %fusion.35 = (f32[4,8,64]{2,0,1:T(4,128)S(1)}, f32[4,8,64,32]{2,3,0,1:T(8,128)S(1)}) fusion(bf16[4,8,64,576]{3,2,1,0:T(8,128)(2,1)} %copy-done.7, bf16[8,32,576]{2,1,0:T(8,128)(2,1)S(1)} %all_to_all.16, pred[8,32]{1,0:T(8,128)(4,1)S(1)} %iota_compare_fusion.2), kind=kOutput, calls=%fused_computation.50 | convolution fusion | flops 75692032 | bytes 2924800 | tf_op jit(solution)/shard_map/srhk,rpk->srhp/dot_general | solution.py:238
  35.1 0.8 collective-permute-start.1
  35.9 1.3 collective-permute-start
  37.2 2.0 %collective-permute-done.1.refs_2_ = bf16[32,640]{1,0:T(8,128)(2,1)S(1)} collective-permute-done((bf16[32,640]{1,0:T(8,128)(2,1)S(1)}, bf16[32,640]{1,0:T(8,128)(2,1)S(1)}, u32[]{:S(2)}, u32[]{:S(2)}) %collective-permute-start.1) | collective-permute-done | bytes 40992 | tf_op jit(solution)/shard_map/ppermute | solution.py:294
  39.9 1.3 collective-permute-start.3
  41.2 1.5 %collective-permute-start.19 = (bf16[32,3584]{1,0:T(8,128)(2,1)S(1)}, bf16[32,3584]{1,0:T(8,128)(2,1)S(1)}, u32[]{:S(2)}, u32[]{:S(2)}) collective-permute-start(bf16[32,3584]{1,0:T(8,128)(2,1)S(1)} %collective-permute-done.17.refs_20_), channel_id=1, source_target_pairs={{0,2},{1,3},{4,0},{5,1},{8,4},{9,5},{12,8},{13,9},{14,12},{15,13},... | collective-permute-start | bytes 688136 | tf_op jit(solution)/shard_map/ppermute | solution.py:294
  43.2 0.8 collective-permute-done.3.refs_4_
  44.0 1.2 collective-permute-start.2
  45.3 2.8 %collective-permute-done.2.refs_5_ = bf16[32,640]{1,0:T(8,128)(2,1)S(1)} collective-permute-done((bf16[32,640]{1,0:T(8,128)(2,1)S(1)}, bf16[32,640]{1,0:T(8,128)(2,1)S(1)}, u32[]{:S(2)}, u32[]{:S(2)}) %collective-permute-start.2) | collective-permute-done | bytes 40992 | tf_op jit(solution)/shard_map/ppermute | solution.py:294
  48.0 1.2 collective-permute-start.21
  50.4 2.5 %collective-permute-done.21 = bf16[16,3584]{1,0:T(8,128)(2,1)S(1)} collective-permute-done((bf16[16,3584]{1,0:T(8,128)(2,1)S(1)}, bf16[16,3584]{1,0:T(8,128)(2,1)S(1)}, u32[]{:S(2)}, u32[]{:S(2)}) %collective-permute-start.21) | collective-permute-done | bytes 114720 | tf_op jit(solution)/shard_map/ppermute | solution.py:294
  52.8 1.5 %collective-permute-start.22 = (bf16[16,3584]{1,0:T(8,128)(2,1)S(1)}, bf16[16,3584]{1,0:T(8,128)(2,1)S(1)}, u32[]{:S(2)}, u32[]{:S(2)}) collective-permute-start(bf16[16,3584]{1,0:T(8,128)(2,1)S(1)} %slice.43), channel_id=1, source_target_pairs={{0,2},{1,3},{4,0},{5,1},{8,4},{9,5},{12,8},{13,9},{14,12},{15,13},... | collective-permute-start | bytes 344072 | tf_op jit(solution)/shard_map/ppermute | solution.py:294
  54.9 1.5 %collective-permute-start.5 = (bf16[32,640]{1,0:T(8,128)(2,1)S(1)}, bf16[32,640]{1,0:T(8,128)(2,1)S(1)}, u32[]{:S(2)}, u32[]{:S(2)}) collective-permute-start(bf16[32,640]{1,0:T(8,128)(2,1)S(1)} %collective-permute-done.3.refs_4_), channel_id=1, source_target_pairs={{0,2},{1,3},{4,0},{5,1},{8,4},{9,5},{12,8},{13,9},{14,12},{15,13},... | collective-permute-start | bytes 122888 | tf_op jit(solution)/shard_map/ppermute | solution.py:294
  56.4 1.3 collective-permute-done.22
  57.6 1.6 %collective-permute-start.4 = (bf16[32,640]{1,0:T(8,128)(2,1)S(1)}, bf16[32,640]{1,0:T(8,128)(2,1)S(1)}, u32[]{:S(2)}, u32[]{:S(2)}) collective-permute-start(bf16[32,640]{1,0:T(8,128)(2,1)S(1)} %collective-permute-done.2.refs_5_), channel_id=1, source_target_pairs={{0,4},{1,5},{4,8},{5,9},{8,12},{9,13},{12,14},{13,15},{14,10},{15,... | collective-permute-start | bytes 122888 | tf_op jit(solution)/shard_map/ppermute | solution.py:294
  59.9 1.8 %collective-permute-done.4.refs_7_ = bf16[32,640]{1,0:T(8,128)(2,1)S(1)} collective-permute-done((bf16[32,640]{1,0:T(8,128)(2,1)S(1)}, bf16[32,640]{1,0:T(8,128)(2,1)S(1)}, u32[]{:S(2)}, u32[]{:S(2)}) %collective-permute-start.4) | collective-permute-done | bytes 40992 | tf_op jit(solution)/shard_map/ppermute | solution.py:294
  62.2 1.6 %collective-permute-start.6 = (bf16[32,640]{1,0:T(8,128)(2,1)S(1)}, bf16[32,640]{1,0:T(8,128)(2,1)S(1)}, u32[]{:S(2)}, u32[]{:S(2)}) collective-permute-start(bf16[32,640]{1,0:T(8,128)(2,1)S(1)} %collective-permute-done.4.refs_7_), channel_id=1, source_target_pairs={{0,4},{1,5},{4,8},{5,9},{8,12},{9,13},{12,14},{13,15},{14,10},{15,... | collective-permute-start | bytes 122888 | tf_op jit(solution)/shard_map/ppermute | solution.py:294
  63.8 2.4 %collective-permute-done.6.refs_8_ = bf16[32,640]{1,0:T(8,128)(2,1)S(1)} collective-permute-done((bf16[32,640]{1,0:T(8,128)(2,1)S(1)}, bf16[32,640]{1,0:T(8,128)(2,1)S(1)}, u32[]{:S(2)}, u32[]{:S(2)}) %collective-permute-start.6) | collective-permute-done | bytes 40992 | tf_op jit(solution)/shard_map/ppermute | solution.py:294
  66.2 1.2 collective-permute-done.14.refs_16_
  67.4 6.6 %normalize.1 = (bf16[512,3584]{1,0:T(8,128)(2,1)S(1)}, f32[512,128]{1,0:T(8,128)S(1)}, f32[512,128]{1,0:T(8,128)S(1)}, f32[32,3584]{1,0:T(8,128)S(1)}) custom-call(s32[1]{0:T(128)} %bitcast.3.refs_0_, bf16[32,640]{1,0:T(8,128)(2,1)S(1)} %bitcast.48, bf16[32,640]{1,0:T(8,128)(2,1)S(1)} %collective-permute-done.1.refs_2_, ...), custom_call_target="tpu_custom_call" | custom-call | flops 1879048192 | bytes 11010048 | tf_op jit(solution)/shard_map/normalize/pallas_call | solution.py:115
  74.0 3.1 %copy-done.4 = bf16[1,3584,1024]{2,1,0:T(8,128)(2,1)S(1)} copy-done((bf16[1,3584,1024]{2,1,0:T(8,128)(2,1)S(1)}, bf16[1,3584,1024]{2,1,0:T(8,128)(2,1)}, u32[]{:S(2)}) %copy-start.4) | copy-done | bytes 7340056
  77.1 3.1 %copy-done.5 = bf16[1,3584,1024]{2,1,0:T(8,128)(2,1)S(1)} copy-done((bf16[1,3584,1024]{2,1,0:T(8,128)(2,1)S(1)}, bf16[1,3584,1024]{2,1,0:T(8,128)(2,1)}, u32[]{:S(2)}) %copy-start.5) | copy-done | bytes 7340056
  80.2 3.1 %copy-done.6 = bf16[1,1024,3584]{2,1,0:T(8,128)(2,1)S(1)} copy-done((bf16[1,1024,3584]{2,1,0:T(8,128)(2,1)S(1)}, bf16[1,1024,3584]{2,1,0:T(8,128)(2,1)}, u32[]{:S(2)}) %copy-start.6) | copy-done | bytes 7340056
  83.3 17.1 %experts.1 = (bf16[32,3584]{1,0:T(8,128)(2,1)S(1)}, bf16[32,3584]{1,0:T(8,128)(2,1)S(1)}, bf16[32,3584]{1,0:T(8,128)(2,1)S(1)}, bf16[32,3584]{1,0:T(8,128)(2,1)S...) custom-call(bf16[512,3584]{1,0:T(8,128)(2,1)S(1)} %get-tuple-element, ...), custom_call_target="tpu_custom_call" | custom-call | flops 11274289152 | bytes 29360128 | tf_op jit(solution)/shard_map/experts/pallas_call | solution.py:208
  101.0 1.0 collective-permute-done.35
  102.0 1.5 %collective-permute-start.37 = (bf16[16,3584]{1,0:T(8,128)(2,1)S(1)}, bf16[16,3584]{1,0:T(8,128)(2,1)S(1)}, u32[]{:S(2)}, u32[]{:S(2)}) collective-permute-start(bf16[16,3584]{1,0:T(8,128)(2,1)S(1)} %get-tuple-element.83), channel_id=1, source_target_pairs={{0,2},{1,3},{4,0},{5,1},{8,4},{9,5},{12,8},{13,9},{14,12},{15,13},... | collective-permute-start | bytes 344072 | tf_op jit(solution)/shard_map/ppermute | solution.py:294
  104.1 3.2 %collective-permute-done.37 = bf16[16,3584]{1,0:T(8,128)(2,1)S(1)} collective-permute-done((bf16[16,3584]{1,0:T(8,128)(2,1)S(1)}, bf16[16,3584]{1,0:T(8,128)(2,1)S(1)}, u32[]{:S(2)}, u32[]{:S(2)}) %collective-permute-start.37) | collective-permute-done | bytes 114720 | tf_op jit(solution)/shard_map/ppermute | solution.py:294
  107.3 1.2 collective-permute-done.36
  109.2 1.5 %collective-permute-start.40 = (bf16[32,3584]{1,0:T(8,128)(2,1)S(1)}, bf16[32,3584]{1,0:T(8,128)(2,1)S(1)}, u32[]{:S(2)}, u32[]{:S(2)}) collective-permute-start(bf16[32,3584]{1,0:T(8,128)(2,1)S(1)} %add_convert_fusion.5), channel_id=1, source_target_pairs={{0,2},{1,3},{4,0},{5,1},{8,4},{9,5},{12,8},{13,9},{14,12},{15,13},... | collective-permute-start | bytes 688136 | tf_op jit(solution)/shard_map/ppermute | solution.py:294
  111.3 3.8 %collective-permute-done.38 = bf16[32,3584]{1,0:T(8,128)(2,1)S(1)} collective-permute-done((bf16[32,3584]{1,0:T(8,128)(2,1)S(1)}, bf16[32,3584]{1,0:T(8,128)(2,1)S(1)}, u32[]{:S(2)}, u32[]{:S(2)}) %collective-permute-start.38) | collective-permute-done | bytes 229408 | tf_op jit(solution)/shard_map/ppermute | solution.py:294
  115.8 1.5 %collective-permute-start.41 = (bf16[32,3584]{1,0:T(8,128)(2,1)S(1)}, bf16[32,3584]{1,0:T(8,128)(2,1)S(1)}, u32[]{:S(2)}, u32[]{:S(2)}) collective-permute-start(bf16[32,3584]{1,0:T(8,128)(2,1)S(1)} %add_convert_fusion.4), channel_id=1, source_target_pairs={{0,4},{1,5},{4,8},{5,9},{8,12},{9,13},{12,14},{13,15},{14,10},{15,... | collective-permute-start | bytes 688136 | tf_op jit(solution)/shard_map/ppermute | solution.py:294
  118.6 3.3 %collective-permute-done.41 = bf16[32,3584]{1,0:T(8,128)(2,1)S(1)} collective-permute-done((bf16[32,3584]{1,0:T(8,128)(2,1)S(1)}, bf16[32,3584]{1,0:T(8,128)(2,1)S(1)}, u32[]{:S(2)}, u32[]{:S(2)}) %collective-permute-start.41) | collective-permute-done | bytes 229408 | tf_op jit(solution)/shard_map/ppermute | solution.py:294
  121.9 1.6 %collective-permute-done.43 = bf16[32,3584]{1,0:T(8,128)(2,1)S(1)} collective-permute-done((bf16[32,3584]{1,0:T(8,128)(2,1)S(1)}, bf16[32,3584]{1,0:T(8,128)(2,1)S(1)}, u32[]{:S(2)}, u32[]{:S(2)}) %collective-permute-start.43) | collective-permute-done | bytes 229408 | tf_op jit(solution)/shard_map/ppermute | solution.py:294
  123.6 1.5 %collective-permute-start.44 = (bf16[32,3584]{1,0:T(8,128)(2,1)S(1)}, bf16[32,3584]{1,0:T(8,128)(2,1)S(1)}, u32[]{:S(2)}, u32[]{:S(2)}) collective-permute-start(bf16[32,3584]{1,0:T(8,128)(2,1)S(1)} %add_convert_fusion.2), channel_id=1, source_target_pairs={{0,4},{1,5},{4,8},{5,9},{8,12},{9,13},{12,14},{13,15},{14,10},{15,... | collective-permute-start | bytes 688136 | tf_op jit(solution)/shard_map/ppermute | solution.py:294
  125.8 3.8 %collective-permute-done.44 = bf16[32,3584]{1,0:T(8,128)(2,1)S(1)} collective-permute-done((bf16[32,3584]{1,0:T(8,128)(2,1)S(1)}, bf16[32,3584]{1,0:T(8,128)(2,1)S(1)}, u32[]{:S(2)}, u32[]{:S(2)}) %collective-permute-start.44) | collective-permute-done | bytes 229408 | tf_op jit(solution)/shard_map/ppermute | solution.py:294
  129.6 1.6 %collective-permute-done.46 = bf16[32,3584]{1,0:T(8,128)(2,1)S(1)} collective-permute-done((bf16[32,3584]{1,0:T(8,128)(2,1)S(1)}, bf16[32,3584]{1,0:T(8,128)(2,1)S(1)}, u32[]{:S(2)}, u32[]{:S(2)}) %collective-permute-start.46) | collective-permute-done | bytes 229408 | tf_op jit(solution)/shard_map/ppermute | solution.py:294
  131.3 0.8 fusion.28
  (109 shorter events, 12.3 us)
Async XLA Ops:
  0.0 19.4 %collective-permute-start.16 = (bf16[32,3584]{1,0:T(8,128)(2,1)}, bf16[32,3584]{1,0:T(8,128)(2,1)S(1)}, u32[]{:S(2)}, u32[]{:S(2)}) collective-permute-start(bf16[32,3584]{1,0:T(8,128)(2,1)} %bitcast.41), channel_id=1, source_target_pairs={{0,4},{1,5},{4,8},{5,9},{8,12},{9,13},{12,14},{13,15},{14,10},{15,... | collective-permute-start | bytes 688136 | tf_op jit(solution)/shard_map/ppermute | solution.py:294
  3.0 18.5 %collective-permute-start.15 = (bf16[32,3584]{1,0:T(8,128)(2,1)}, bf16[32,3584]{1,0:T(8,128)(2,1)S(1)}, u32[]{:S(2)}, u32[]{:S(2)}) collective-permute-start(bf16[32,3584]{1,0:T(8,128)(2,1)} %bitcast.42), channel_id=1, source_target_pairs={{0,2},{1,3},{4,0},{5,1},{8,4},{9,5},{12,8},{13,9},{14,12},{15,13},... | collective-permute-start | bytes 688136 | tf_op jit(solution)/shard_map/ppermute | solution.py:294
  5.3 23.6 %all-to-all-start = ((bf16[128,2,576]{2,1,0:T(2,128)(2,1)}), bf16[128,2,576]{2,1,0:T(2,128)(2,1)}, u32[]{:S(2)}, u32[]{:S(2)}) async-start(bf16[128,2,576]{2,1,0:T(2,128)(2,1)} %copy.35), calls=%async_computation | async-start | bytes 655360 | tf_op jit(solution)/shard_map/all_to_all | solution.py:302
  19.4 8.2 %collective-permute-start.18 = (bf16[32,3584]{1,0:T(8,128)(2,1)S(1)}, bf16[32,3584]{1,0:T(8,128)(2,1)S(1)}, u32[]{:S(2)}, u32[]{:S(2)}) collective-permute-start(bf16[32,3584]{1,0:T(8,128)(2,1)S(1)} %collective-permute-done.16.refs_19_), channel_id=1, source_target_pairs={{0,4},{1,5},{4,8},{5,9},{8,12},{9,13},{12,14},{13,15},{14,10},{15,... | collective-permute-start | bytes 688136 | tf_op jit(solution)/shard_map/ppermute | solution.py:294
  21.5 19.7 %collective-permute-start.17 = (bf16[32,3584]{1,0:T(8,128)(2,1)S(1)}, bf16[32,3584]{1,0:T(8,128)(2,1)S(1)}, u32[]{:S(2)}, u32[]{:S(2)}) collective-permute-start(bf16[32,3584]{1,0:T(8,128)(2,1)S(1)} %collective-permute-done.15.refs_18_), channel_id=1, source_target_pairs={{0,2},{1,3},{4,0},{5,1},{8,4},{9,5},{12,8},{13,9},{14,12},{15,13},... | collective-permute-start | bytes 688136 | tf_op jit(solution)/shard_map/ppermute | solution.py:294
  27.6 16.4 %collective-permute-start.20 = (bf16[32,3584]{1,0:T(8,128)(2,1)S(1)}, bf16[32,3584]{1,0:T(8,128)(2,1)S(1)}, u32[]{:S(2)}, u32[]{:S(2)}) collective-permute-start(bf16[32,3584]{1,0:T(8,128)(2,1)S(1)} %collective-permute-done.18.refs_21_), channel_id=1, source_target_pairs={{0,4},{1,5},{4,8},{5,9},{8,12},{9,13},{12,14},{13,15},{14,10},{15,... | collective-permute-start | bytes 688136 | tf_op jit(solution)/shard_map/ppermute | solution.py:294
  35.1 4.1 %collective-permute-start.1 = (bf16[32,640]{1,0:T(8,128)(2,1)S(1)}, bf16[32,640]{1,0:T(8,128)(2,1)S(1)}, u32[]{:S(2)}, u32[]{:S(2)}) collective-permute-start(bf16[32,640]{1,0:T(8,128)(2,1)S(1)} %bitcast.45), channel_id=1, source_target_pairs={{0,2},{1,3},{4,0},{5,1},{8,4},{9,5},{12,8},{13,9},{14,12},{15,13},... | collective-permute-start | bytes 122888 | tf_op jit(solution)/shard_map/ppermute | solution.py:294
  35.9 4.0 %collective-permute-start = (bf16[32,640]{1,0:T(8,128)(2,1)S(1)}, bf16[32,640]{1,0:T(8,128)(2,1)S(1)}, u32[]{:S(2)}, u32[]{:S(2)}) collective-permute-start(bf16[32,640]{1,0:T(8,128)(2,1)S(1)} %bitcast.46), channel_id=1, source_target_pairs={{0,4},{1,5},{4,8},{5,9},{8,12},{9,13},{12,14},{13,15},{14,10},{15,... | collective-permute-start | bytes 122888 | tf_op jit(solution)/shard_map/ppermute | solution.py:294
  39.9 4.1 %collective-permute-start.3 = (bf16[32,640]{1,0:T(8,128)(2,1)S(1)}, bf16[32,640]{1,0:T(8,128)(2,1)S(1)}, u32[]{:S(2)}, u32[]{:S(2)}) collective-permute-start(bf16[32,640]{1,0:T(8,128)(2,1)S(1)} %collective-permute-done.1.refs_2_), channel_id=1, source_target_pairs={{0,2},{1,3},{4,0},{5,1},{8,4},{9,5},{12,8},{13,9},{14,12},{15,13},... | collective-permute-start | bytes 122888 | tf_op jit(solution)/shard_map/ppermute | solution.py:294
  41.2 8.1 %collective-permute-start.19 = (bf16[32,3584]{1,0:T(8,128)(2,1)S(1)}, bf16[32,3584]{1,0:T(8,128)(2,1)S(1)}, u32[]{:S(2)}, u32[]{:S(2)}) collective-permute-start(bf16[32,3584]{1,0:T(8,128)(2,1)S(1)} %collective-permute-done.17.refs_20_), channel_id=1, source_target_pairs={{0,2},{1,3},{4,0},{5,1},{8,4},{9,5},{12,8},{13,9},{14,12},{15,13},... | collective-permute-start | bytes 688136 | tf_op jit(solution)/shard_map/ppermute | solution.py:294
  42.7 6.6 %collective-permute-start.23 = (bf16[32,3584]{1,0:T(8,128)(2,1)S(1)}, bf16[32,3584]{1,0:T(8,128)(2,1)S(1)}, u32[]{:S(2)}, u32[]{:S(2)}) collective-permute-start(bf16[32,3584]{1,0:T(8,128)(2,1)S(1)} %bitcast.43), channel_id=1, source_target_pairs={{0,1},{1,0},{2,3},{3,2},{4,5},{5,4},{6,7},{7,6},{8,9},{9,8},{10,11... | collective-permute-start | bytes 688136 | tf_op jit(solution)/shard_map/ppermute | solution.py:294
  42.7 7.2 %collective-permute-start.25 = (bf16[32,3584]{1,0:T(8,128)(2,1)S(1)}, bf16[32,3584]{1,0:T(8,128)(2,1)S(1)}, u32[]{:S(2)}, u32[]{:S(2)}) collective-permute-start(bf16[32,3584]{1,0:T(8,128)(2,1)S(1)} %collective-permute-done.16.refs_19_), channel_id=1, source_target_pairs={{0,1},{1,0},{2,3},{3,2},{4,5},{5,4},{6,7},{7,6},{8,9},{9,8},{10,11... | collective-permute-start | bytes 688136 | tf_op jit(solution)/shard_map/ppermute | solution.py:294
  44.0 5.9 %collective-permute-start.24 = (bf16[32,3584]{1,0:T(8,128)(2,1)S(1)}, bf16[32,3584]{1,0:T(8,128)(2,1)S(1)}, u32[]{:S(2)}, u32[]{:S(2)}) collective-permute-start(bf16[32,3584]{1,0:T(8,128)(2,1)S(1)} %collective-permute-done.15.refs_18_), channel_id=1, source_target_pairs={{0,1},{1,0},{2,3},{3,2},{4,5},{5,4},{6,7},{7,6},{8,9},{9,8},{10,11... | collective-permute-start | bytes 688136 | tf_op jit(solution)/shard_map/ppermute | solution.py:294
  44.0 4.0 %collective-permute-start.2 = (bf16[32,640]{1,0:T(8,128)(2,1)S(1)}, bf16[32,640]{1,0:T(8,128)(2,1)S(1)}, u32[]{:S(2)}, u32[]{:S(2)}) collective-permute-start(bf16[32,640]{1,0:T(8,128)(2,1)S(1)} %collective-permute-done.refs_3_), channel_id=1, source_target_pairs={{0,4},{1,5},{4,8},{5,9},{8,12},{9,13},{12,14},{13,15},{14,10},{15,... | collective-permute-start | bytes 122888 | tf_op jit(solution)/shard_map/ppermute | solution.py:294
  48.0 4.8 %collective-permute-start.21 = (bf16[16,3584]{1,0:T(8,128)(2,1)S(1)}, bf16[16,3584]{1,0:T(8,128)(2,1)S(1)}, u32[]{:S(2)}, u32[]{:S(2)}) collective-permute-start(bf16[16,3584]{1,0:T(8,128)(2,1)S(1)} %slice.42), channel_id=1, source_target_pairs={{0,4},{1,5},{4,8},{5,9},{8,12},{9,13},{12,14},{13,15},{14,10},{15,... | collective-permute-start | bytes 344072 | tf_op jit(solution)/shard_map/ppermute | solution.py:294
  49.3 5.0 %collective-permute-start.7 = (bf16[32,640]{1,0:T(8,128)(2,1)S(1)}, bf16[32,640]{1,0:T(8,128)(2,1)S(1)}, u32[]{:S(2)}, u32[]{:S(2)}) collective-permute-start(bf16[32,640]{1,0:T(8,128)(2,1)S(1)} %bitcast.47), channel_id=1, source_target_pairs={{0,1},{1,0},{2,3},{3,2},{4,5},{5,4},{6,7},{7,6},{8,9},{9,8},{10,11... | collective-permute-start | bytes 122888 | tf_op jit(solution)/shard_map/ppermute | solution.py:294
  49.3 5.1 %collective-permute-start.8 = (bf16[32,640]{1,0:T(8,128)(2,1)S(1)}, bf16[32,640]{1,0:T(8,128)(2,1)S(1)}, u32[]{:S(2)}, u32[]{:S(2)}) collective-permute-start(bf16[32,640]{1,0:T(8,128)(2,1)S(1)} %collective-permute-done.1.refs_2_), channel_id=1, source_target_pairs={{0,1},{1,0},{2,3},{3,2},{4,5},{5,4},{6,7},{7,6},{8,9},{9,8},{10,11... | collective-permute-start | bytes 122888 | tf_op jit(solution)/shard_map/ppermute | solution.py:294
  49.9 5.0 %collective-permute-start.9 = (bf16[32,640]{1,0:T(8,128)(2,1)S(1)}, bf16[32,640]{1,0:T(8,128)(2,1)S(1)}, u32[]{:S(2)}, u32[]{:S(2)}) collective-permute-start(bf16[32,640]{1,0:T(8,128)(2,1)S(1)} %collective-permute-done.refs_3_), channel_id=1, source_target_pairs={{0,1},{1,0},{2,3},{3,2},{4,5},{5,4},{6,7},{7,6},{8,9},{9,8},{10,11... | collective-permute-start | bytes 122888 | tf_op jit(solution)/shard_map/ppermute | solution.py:294
  49.9 6.4 %collective-permute-start.10 = (bf16[32,640]{1,0:T(8,128)(2,1)S(1)}, bf16[32,640]{1,0:T(8,128)(2,1)S(1)}, u32[]{:S(2)}, u32[]{:S(2)}) collective-permute-start(bf16[32,640]{1,0:T(8,128)(2,1)S(1)} %collective-permute-done.3.refs_4_), channel_id=1, source_target_pairs={{0,1},{1,0},{2,3},{3,2},{4,5},{5,4},{6,7},{7,6},{8,9},{9,8},{10,11... | collective-permute-start | bytes 122888 | tf_op jit(solution)/shard_map/ppermute | solution.py:294
  52.8 4.8 %collective-permute-start.22 = (bf16[16,3584]{1,0:T(8,128)(2,1)S(1)}, bf16[16,3584]{1,0:T(8,128)(2,1)S(1)}, u32[]{:S(2)}, u32[]{:S(2)}) collective-permute-start(bf16[16,3584]{1,0:T(8,128)(2,1)S(1)} %slice.43), channel_id=1, source_target_pairs={{0,2},{1,3},{4,0},{5,1},{8,4},{9,5},{12,8},{13,9},{14,12},{15,13},... | collective-permute-start | bytes 344072 | tf_op jit(solution)/shard_map/ppermute | solution.py:294
  54.3 7.3 %collective-permute-start.27 = (bf16[32,3584]{1,0:T(8,128)(2,1)S(1)}, bf16[32,3584]{1,0:T(8,128)(2,1)S(1)}, u32[]{:S(2)}, u32[]{:S(2)}) collective-permute-start(bf16[32,3584]{1,0:T(8,128)(2,1)S(1)} %collective-permute-done.18.refs_21_), channel_id=1, source_target_pairs={{0,1},{1,0},{2,3},{3,2},{4,5},{5,4},{6,7},{7,6},{8,9},{9,8},{10,11... | collective-permute-start | bytes 688136 | tf_op jit(solution)/shard_map/ppermute | solution.py:294
  54.4 7.8 %collective-permute-start.26 = (bf16[32,3584]{1,0:T(8,128)(2,1)S(1)}, bf16[32,3584]{1,0:T(8,128)(2,1)S(1)}, u32[]{:S(2)}, u32[]{:S(2)}) collective-permute-start(bf16[32,3584]{1,0:T(8,128)(2,1)S(1)} %collective-permute-done.17.refs_20_), channel_id=1, source_target_pairs={{0,1},{1,0},{2,3},{3,2},{4,5},{5,4},{6,7},{7,6},{8,9},{9,8},{10,11... | collective-permute-start | bytes 688136 | tf_op jit(solution)/shard_map/ppermute | solution.py:294
  54.9 4.4 %collective-permute-start.5 = (bf16[32,640]{1,0:T(8,128)(2,1)S(1)}, bf16[32,640]{1,0:T(8,128)(2,1)S(1)}, u32[]{:S(2)}, u32[]{:S(2)}) collective-permute-start(bf16[32,640]{1,0:T(8,128)(2,1)S(1)} %collective-permute-done.3.refs_4_), channel_id=1, source_target_pairs={{0,2},{1,3},{4,0},{5,1},{8,4},{9,5},{12,8},{13,9},{14,12},{15,13},... | collective-permute-start | bytes 122888 | tf_op jit(solution)/shard_map/ppermute | solution.py:294
  56.4 3.0 %collective-permute-start.11 = (bf16[32,640]{1,0:T(8,128)(2,1)S(1)}, bf16[32,640]{1,0:T(8,128)(2,1)S(1)}, u32[]{:S(2)}, u32[]{:S(2)}) collective-permute-start(bf16[32,640]{1,0:T(8,128)(2,1)S(1)} %collective-permute-done.2.refs_5_), channel_id=1, source_target_pairs={{0,1},{1,0},{2,3},{3,2},{4,5},{5,4},{6,7},{7,6},{8,9},{9,8},{10,11... | collective-permute-start | bytes 122888 | tf_op jit(solution)/shard_map/ppermute | solution.py:294
  57.6 4.0 %collective-permute-start.4 = (bf16[32,640]{1,0:T(8,128)(2,1)S(1)}, bf16[32,640]{1,0:T(8,128)(2,1)S(1)}, u32[]{:S(2)}, u32[]{:S(2)}) collective-permute-start(bf16[32,640]{1,0:T(8,128)(2,1)S(1)} %collective-permute-done.2.refs_5_), channel_id=1, source_target_pairs={{0,4},{1,5},{4,8},{5,9},{8,12},{9,13},{12,14},{13,15},{14,10},{15,... | collective-permute-start | bytes 122888 | tf_op jit(solution)/shard_map/ppermute | solution.py:294
  59.3 8.1 %collective-permute-start.29 = (bf16[32,3584]{1,0:T(8,128)(2,1)S(1)}, bf16[32,3584]{1,0:T(8,128)(2,1)S(1)}, u32[]{:S(2)}, u32[]{:S(2)}) collective-permute-start(bf16[32,3584]{1,0:T(8,128)(2,1)S(1)} %collective-permute-done.20.refs_23_), channel_id=1, source_target_pairs={{0,1},{1,0},{2,3},{3,2},{4,5},{5,4},{6,7},{7,6},{8,9},{9,8},{10,11... | collective-permute-start | bytes 688136 | tf_op jit(solution)/shard_map/ppermute | solution.py:294
  59.4 8.0 %collective-permute-start.28 = (bf16[32,3584]{1,0:T(8,128)(2,1)S(1)}, bf16[32,3584]{1,0:T(8,128)(2,1)S(1)}, u32[]{:S(2)}, u32[]{:S(2)}) collective-permute-start(bf16[32,3584]{1,0:T(8,128)(2,1)S(1)} %collective-permute-done.19.refs_22_), channel_id=1, source_target_pairs={{0,1},{1,0},{2,3},{3,2},{4,5},{5,4},{6,7},{7,6},{8,9},{9,8},{10,11... | collective-permute-start | bytes 688136 | tf_op jit(solution)/shard_map/ppermute | solution.py:294
  61.6 5.8 %collective-permute-start.30 = (bf16[32,3584]{1,0:T(8,128)(2,1)S(1)}, bf16[32,3584]{1,0:T(8,128)(2,1)S(1)}, u32[]{:S(2)}, u32[]{:S(2)}) collective-permute-start(bf16[32,3584]{1,0:T(8,128)(2,1)S(1)} %constant_dynamic-update-slice_fusion.refs_24_), channel_id=1, source_target_pairs={{0,1},{1,0},{2,3},{3,2},{4,5},{5,4},{6,7},{7,6},{8,9},{9,8},{10,11... | collective-permute-start | bytes 688136 | tf_op jit(solution)/shard_map/ppermute | solution.py:294
  61.6 2.2 %collective-permute-start.12 = (bf16[32,640]{1,0:T(8,128)(2,1)S(1)}, bf16[32,640]{1,0:T(8,128)(2,1)S(1)}, u32[]{:S(2)}, u32[]{:S(2)}) collective-permute-start(bf16[32,640]{1,0:T(8,128)(2,1)S(1)} %collective-permute-done.5.refs_6_), channel_id=1, source_target_pairs={{0,1},{1,0},{2,3},{3,2},{4,5},{5,4},{6,7},{7,6},{8,9},{9,8},{10,11... | collective-permute-start | bytes 122888 | tf_op jit(solution)/shard_map/ppermute | solution.py:294
  62.2 4.0 %collective-permute-start.6 = (bf16[32,640]{1,0:T(8,128)(2,1)S(1)}, bf16[32,640]{1,0:T(8,128)(2,1)S(1)}, u32[]{:S(2)}, u32[]{:S(2)}) collective-permute-start(bf16[32,640]{1,0:T(8,128)(2,1)S(1)} %collective-permute-done.4.refs_7_), channel_id=1, source_target_pairs={{0,4},{1,5},{4,8},{5,9},{8,12},{9,13},{12,14},{13,15},{14,10},{15,... | collective-permute-start | bytes 122888 | tf_op jit(solution)/shard_map/ppermute | solution.py:294
  63.8 2.4 %collective-permute-start.13 = (bf16[32,640]{1,0:T(8,128)(2,1)S(1)}, bf16[32,640]{1,0:T(8,128)(2,1)S(1)}, u32[]{:S(2)}, u32[]{:S(2)}) collective-permute-start(bf16[32,640]{1,0:T(8,128)(2,1)S(1)} %collective-permute-done.4.refs_7_), channel_id=1, source_target_pairs={{0,1},{1,0},{2,3},{3,2},{4,5},{5,4},{6,7},{7,6},{8,9},{9,8},{10,11... | collective-permute-start | bytes 122888 | tf_op jit(solution)/shard_map/ppermute | solution.py:294
  66.2 1.2 collective-permute-start.14
  100.4 1.6 %collective-permute-start.35 = (bf16[32,3584]{1,0:T(8,128)(2,1)S(1)}, bf16[32,3584]{1,0:T(8,128)(2,1)S(1)}, u32[]{:S(2)}, u32[]{:S(2)}) collective-permute-start(bf16[32,3584]{1,0:T(8,128)(2,1)S(1)} %get-tuple-element.68), channel_id=1, source_target_pairs={{0,1},{1,0},{2,3},{3,2},{4,5},{5,4},{6,7},{7,6},{8,9},{9,8},{10,11... | collective-permute-start | bytes 688136 | tf_op jit(solution)/shard_map/ppermute | solution.py:294
  100.6 7.8 %collective-permute-start.34 = (bf16[32,3584]{1,0:T(8,128)(2,1)S(1)}, bf16[32,3584]{1,0:T(8,128)(2,1)S(1)}, u32[]{:S(2)}, u32[]{:S(2)}) collective-permute-start(bf16[32,3584]{1,0:T(8,128)(2,1)S(1)} %get-tuple-element.66), channel_id=1, source_target_pairs={{0,1},{1,0},{2,3},{3,2},{4,5},{5,4},{6,7},{7,6},{8,9},{9,8},{10,11... | collective-permute-start | bytes 688136 | tf_op jit(solution)/shard_map/ppermute | solution.py:294
  102.0 5.3 %collective-permute-start.37 = (bf16[16,3584]{1,0:T(8,128)(2,1)S(1)}, bf16[16,3584]{1,0:T(8,128)(2,1)S(1)}, u32[]{:S(2)}, u32[]{:S(2)}) collective-permute-start(bf16[16,3584]{1,0:T(8,128)(2,1)S(1)} %get-tuple-element.83), channel_id=1, source_target_pairs={{0,2},{1,3},{4,0},{5,1},{8,4},{9,5},{12,8},{13,9},{14,12},{15,13},... | collective-permute-start | bytes 344072 | tf_op jit(solution)/shard_map/ppermute | solution.py:294
  103.5 4.9 %collective-permute-start.36 = (bf16[16,3584]{1,0:T(8,128)(2,1)S(1)}, bf16[16,3584]{1,0:T(8,128)(2,1)S(1)}, u32[]{:S(2)}, u32[]{:S(2)}) collective-permute-start(bf16[16,3584]{1,0:T(8,128)(2,1)S(1)} %get-tuple-element.84), channel_id=1, source_target_pairs={{0,4},{1,5},{4,8},{5,9},{8,12},{9,13},{12,14},{13,15},{14,10},{15,... | collective-permute-start | bytes 344072 | tf_op jit(solution)/shard_map/ppermute | solution.py:294
  104.1 5.1 %collective-permute-start.39 = (bf16[32,3584]{1,0:T(8,128)(2,1)S(1)}, bf16[32,3584]{1,0:T(8,128)(2,1)S(1)}, u32[]{:S(2)}, u32[]{:S(2)}) collective-permute-start(bf16[32,3584]{1,0:T(8,128)(2,1)S(1)} %get-tuple-element.71), channel_id=1, source_target_pairs={{0,1},{1,0},{2,3},{3,2},{4,5},{5,4},{6,7},{7,6},{8,9},{9,8},{10,11... | collective-permute-start | bytes 688136 | tf_op jit(solution)/shard_map/ppermute | solution.py:294
  108.5 6.6 %collective-permute-start.38 = (bf16[32,3584]{1,0:T(8,128)(2,1)S(1)}, bf16[32,3584]{1,0:T(8,128)(2,1)S(1)}, u32[]{:S(2)}, u32[]{:S(2)}) collective-permute-start(bf16[32,3584]{1,0:T(8,128)(2,1)S(1)} %add_convert_fusion.6), channel_id=1, source_target_pairs={{0,4},{1,5},{4,8},{5,9},{8,12},{9,13},{12,14},{13,15},{14,10},{15,... | collective-permute-start | bytes 688136 | tf_op jit(solution)/shard_map/ppermute | solution.py:294
  109.2 6.5 %collective-permute-start.40 = (bf16[32,3584]{1,0:T(8,128)(2,1)S(1)}, bf16[32,3584]{1,0:T(8,128)(2,1)S(1)}, u32[]{:S(2)}, u32[]{:S(2)}) collective-permute-start(bf16[32,3584]{1,0:T(8,128)(2,1)S(1)} %add_convert_fusion.5), channel_id=1, source_target_pairs={{0,2},{1,3},{4,0},{5,1},{8,4},{9,5},{12,8},{13,9},{14,12},{15,13},... | collective-permute-start | bytes 688136 | tf_op jit(solution)/shard_map/ppermute | solution.py:294
  110.7 5.0 %collective-permute-start.33 = (bf16[32,3584]{1,0:T(8,128)(2,1)S(1)}, bf16[32,3584]{1,0:T(8,128)(2,1)S(1)}, u32[]{:S(2)}, u32[]{:S(2)}) collective-permute-start(bf16[32,3584]{1,0:T(8,128)(2,1)S(1)} %get-tuple-element.64), channel_id=1, source_target_pairs={{0,1},{1,0},{2,3},{3,2},{4,5},{5,4},{6,7},{7,6},{8,9},{9,8},{10,11... | collective-permute-start | bytes 688136 | tf_op jit(solution)/shard_map/ppermute | solution.py:294
  110.8 6.6 %collective-permute-start.42 = (bf16[32,3584]{1,0:T(8,128)(2,1)S(1)}, bf16[32,3584]{1,0:T(8,128)(2,1)S(1)}, u32[]{:S(2)}, u32[]{:S(2)}) collective-permute-start(bf16[32,3584]{1,0:T(8,128)(2,1)S(1)} %get-tuple-element.75), channel_id=1, source_target_pairs={{0,1},{1,0},{2,3},{3,2},{4,5},{5,4},{6,7},{7,6},{8,9},{9,8},{10,11... | collective-permute-start | bytes 688136 | tf_op jit(solution)/shard_map/ppermute | solution.py:294
  115.8 6.1 %collective-permute-start.41 = (bf16[32,3584]{1,0:T(8,128)(2,1)S(1)}, bf16[32,3584]{1,0:T(8,128)(2,1)S(1)}, u32[]{:S(2)}, u32[]{:S(2)}) collective-permute-start(bf16[32,3584]{1,0:T(8,128)(2,1)S(1)} %add_convert_fusion.4), channel_id=1, source_target_pairs={{0,4},{1,5},{4,8},{5,9},{8,12},{9,13},{12,14},{13,15},{14,10},{15,... | collective-permute-start | bytes 688136 | tf_op jit(solution)/shard_map/ppermute | solution.py:294
  117.4 6.1 %collective-permute-start.43 = (bf16[32,3584]{1,0:T(8,128)(2,1)S(1)}, bf16[32,3584]{1,0:T(8,128)(2,1)S(1)}, u32[]{:S(2)}, u32[]{:S(2)}) collective-permute-start(bf16[32,3584]{1,0:T(8,128)(2,1)S(1)} %add_convert_fusion.3), channel_id=1, source_target_pairs={{0,2},{1,3},{4,0},{5,1},{8,4},{9,5},{12,8},{13,9},{14,12},{15,13},... | collective-permute-start | bytes 688136 | tf_op jit(solution)/shard_map/ppermute | solution.py:294
  118.1 5.4 %collective-permute-start.32 = (bf16[32,3584]{1,0:T(8,128)(2,1)S(1)}, bf16[32,3584]{1,0:T(8,128)(2,1)S(1)}, u32[]{:S(2)}, u32[]{:S(2)}) collective-permute-start(bf16[32,3584]{1,0:T(8,128)(2,1)S(1)} %get-tuple-element.62), channel_id=1, source_target_pairs={{0,1},{1,0},{2,3},{3,2},{4,5},{5,4},{6,7},{7,6},{8,9},{9,8},{10,11... | collective-permute-start | bytes 688136 | tf_op jit(solution)/shard_map/ppermute | solution.py:294
  118.1 7.0 %collective-permute-start.45 = (bf16[32,3584]{1,0:T(8,128)(2,1)S(1)}, bf16[32,3584]{1,0:T(8,128)(2,1)S(1)}, u32[]{:S(2)}, u32[]{:S(2)}) collective-permute-start(bf16[32,3584]{1,0:T(8,128)(2,1)S(1)} %get-tuple-element.79), channel_id=1, source_target_pairs={{0,1},{1,0},{2,3},{3,2},{4,5},{5,4},{6,7},{7,6},{8,9},{9,8},{10,11... | collective-permute-start | bytes 688136 | tf_op jit(solution)/shard_map/ppermute | solution.py:294
  123.6 6.1 %collective-permute-start.44 = (bf16[32,3584]{1,0:T(8,128)(2,1)S(1)}, bf16[32,3584]{1,0:T(8,128)(2,1)S(1)}, u32[]{:S(2)}, u32[]{:S(2)}) collective-permute-start(bf16[32,3584]{1,0:T(8,128)(2,1)S(1)} %add_convert_fusion.2), channel_id=1, source_target_pairs={{0,4},{1,5},{4,8},{5,9},{8,12},{9,13},{12,14},{13,15},{14,10},{15,... | collective-permute-start | bytes 688136 | tf_op jit(solution)/shard_map/ppermute | solution.py:294
  125.2 6.1 %collective-permute-start.46 = (bf16[32,3584]{1,0:T(8,128)(2,1)S(1)}, bf16[32,3584]{1,0:T(8,128)(2,1)S(1)}, u32[]{:S(2)}, u32[]{:S(2)}) collective-permute-start(bf16[32,3584]{1,0:T(8,128)(2,1)S(1)} %add_convert_fusion.1), channel_id=1, source_target_pairs={{0,2},{1,3},{4,0},{5,1},{8,4},{9,5},{12,8},{13,9},{14,12},{15,13},... | collective-permute-start | bytes 688136 | tf_op jit(solution)/shard_map/ppermute | solution.py:294
  125.8 5.5 %collective-permute-start.31 = (bf16[32,3584]{1,0:T(8,128)(2,1)S(1)}, bf16[32,3584]{1,0:T(8,128)(2,1)S(1)}, u32[]{:S(2)}, u32[]{:S(2)}) collective-permute-start(bf16[32,3584]{1,0:T(8,128)(2,1)S(1)} %get-tuple-element.60), channel_id=1, source_target_pairs={{0,1},{1,0},{2,3},{3,2},{4,5},{5,4},{6,7},{7,6},{8,9},{9,8},{10,11... | collective-permute-start | bytes 688136 | tf_op jit(solution)/shard_map/ppermute | solution.py:294
  (11 other events, 109.1 us)

commit v3 on v2

v3 whole, which is shorter than its diff:
```python
import jax
import jax.numpy as jnp
from jax import lax
from jax.experimental import pallas as pl
from jax.experimental.pallas import tpu as pltpu
from jax.sharding import PartitionSpec as P

qk_scale = 192.0 ** (-0.5)
LANES = 128


def ring_of(chips):
    return list(range(0, chips, 2)) + list(range(chips - 1, 0, -2))


def shift_perm(chips, by):
    ring = ring_of(chips)
    return [
        (2 * ring[p] + core, 2 * ring[(p + by) % chips] + core)
        for p in range(chips)
        for core in range(2)
    ]


def sibling_perm(chips):
    return [(d, d ^ 1) for d in range(2 * chips)]


def distances(chips):
    half = chips // 2
    far = [half, half - 1, 1 - half]
    return far, [d for d in range(half - 1) for d in ((d, -d) if d else (0,))]


def tile_of(size, most):
    return max(t for t in range(LANES, min(size, most) + 1, LANES) if size % t == 0)


def scoped(need):
    return max(52 << 20, (int(need) // (1 << 20) + 5) << 20)


def expert_rows(xs, r, gate, w_g, w_u):
    a = jnp.dot(xs, w_g, preferred_element_type=jnp.float32) * r
    b = jnp.dot(xs, w_u, preferred_element_type=jnp.float32) * r
    return (jax.nn.silu(a) * b * gate).astype(jnp.bfloat16)


def front_kernel(far, blocks, rows, latent, width, *refs):
    pick = refs[0]
    pooled = refs[1 : 1 + blocks]
    resid = refs[1 + blocks : 1 + 2 * blocks]
    w_out, gain, w_router, w_gate, w_up, w_down = refs[1 + 2 * blocks : 7 + 2 * blocks]
    x, scale, weight, hidden = refs[7 + 2 * blocks : 11 + 2 * blocks]
    outs = refs[11 + 2 * blocks : 11 + 2 * blocks + far]
    joined, ssq, logits, x_far, act, wg, wu, wd, sems = refs[11 + 2 * blocks + far :]
    step = pl.program_id(0)
    cols = w_out.shape[1]
    tiles = width // cols
    total = blocks * rows
    far_rows = far * rows
    experts_all = w_router.shape[0]
    units = wg.shape[1]
    chunk = min(512, total)

    copies = []
    for k in range(2):
        part = slice(k * units // 2, (k + 1) * units // 2)
        copies.append(pltpu.make_async_copy(w_gate.at[0, :, part], wg.at[:, part], sems.at[2 * k]))
        copies.append(pltpu.make_async_copy(w_up.at[0, :, part], wu.at[:, part], sems.at[2 * k + 1]))
    for k in range(2):
        part = slice(k * width // 2, (k + 1) * width // 2)
        copies.append(pltpu.make_async_copy(w_down.at[0, :, part], wd.at[:, part], sems.at[4 + k]))
    for j, copy in enumerate(copies):
        pl.when(step == min(j, tiles - 1))(copy.start)

    @pl.when(step == 0)
    def _():
        for b in range(blocks):
            joined[b * rows : (b + 1) * rows, :] = pooled[b][...]
        ssq[...] = jnp.zeros_like(ssq)
        logits[...] = jnp.zeros_like(logits)

    @pl.when(step < tiles)
    def _():
        g = gain[...].astype(jnp.float32)
        here = pl.ds(pl.multiple_of(step * cols, cols), cols)
        for c in range(0, total, chunk):
            end = min(c + chunk, total)
            proj = jnp.dot(joined[c:end, :latent], w_out[...], preferred_element_type=jnp.float32)
            for b in range(c // rows, end // rows):
                at = slice(b * rows, (b + 1) * rows)
                h = proj[b * rows - c : (b + 1) * rows - c] + resid[b][...].astype(jnp.float32)
                if b == far:
                    hidden[...] = h
                scaled = (h * g).astype(jnp.bfloat16)
                if b < far:
                    x_far[at, here] = scaled
                else:
                    x[(b - far) * rows : (b - far + 1) * rows, :] = scaled
                sq = h * h
                part = sq[:, :LANES]
                for k in range(1, cols // LANES):
                    part = part + sq[:, k * LANES : (k + 1) * LANES]
                ssq[at, :] += part
        nt = (((1,), (1,)), ((), ()))
        logits[:far_rows, :] += lax.dot_general(
            x_far[:, here], w_router[...], nt, preferred_element_type=jnp.float32
        )
        logits[far_rows:, :] += lax.dot_general(
            x[...], w_router[...], nt, preferred_element_type=jnp.float32
        )

    @pl.when(step == tiles)
    def _():
        mean = jnp.sum(ssq[...], axis=1, keepdims=True) * (1.0 / width)
        r = lax.rsqrt(mean + 1e-06)
        mask = joined[:, latent : latent + experts_all].astype(jnp.float32)
        affinity = jax.nn.sigmoid(logits[...] * r) * mask
        lane = lax.broadcasted_iota(jnp.int32, affinity.shape, 1)
        mine = jnp.sum(jnp.where(lane == pick[0], affinity, 0.0), axis=1, keepdims=True)
        gate = 2.5 * mine / jnp.sum(affinity, axis=1, keepdims=True)
        scale[...] = jnp.broadcast_to(r[far_rows:], (total - far_rows, LANES))
        weight[...] = jnp.broadcast_to(gate[far_rows:], (total - far_rows, LANES))
        for k in range(2):
            part = slice(k * units // 2, (k + 1) * units // 2)
            copies[2 * k].wait()
            copies[2 * k + 1].wait()
            act[:, part] = expert_rows(
                x_far[...], r[:far_rows], gate[:far_rows], wg[:, part], wu[:, part]
            )
        down = tile_of(width // 2, 1024)
        for k in range(2):
            copies[4 + k].wait()
            for c in range(k * width // 2, (k + 1) * width // 2, down):
                y = jnp.dot(act[...], wd[:, c : c + down], preferred_element_type=jnp.float32)
                for b in range(far):
                    outs[b][:, c : c + down] = y[b * rows : (b + 1) * rows].astype(jnp.bfloat16)


def front(far, pick, packets, resid_blocks, w_out, gain, w_router_t, wg, wu, wd):
    blocks = len(packets)
    rows, width = resid_blocks[0].shape
    latent = w_out.shape[0]
    total = blocks * rows
    rest = total - far * rows
    cols = tile_of(width, 512)
    tile_count = width // cols
    packed = packets[0].shape[1]
    experts_all = w_router_t.shape[0]
    units = wg.shape[2]

    def whole(shape):
        return pl.BlockSpec(shape, lambda i: (0, 0), pipeline_mode=pl.Buffered(1))

    def tiles(height):
        return pl.BlockSpec((height, cols), lambda i: (0, jnp.minimum(i, tile_count - 1)))

    in_hbm = pl.BlockSpec(memory_space=pltpu.HBM)
    need = (
        total * (cols * 24 + packed * 4 + 8 * LANES * 4)
        + 4 * latent * cols
        + far * rows * (width * 8 + units * 16)
        + 6 * width * units
    )
    results = pl.pallas_call(
        lambda *refs: front_kernel(far, blocks, rows, latent, width, *refs),
        grid=(tile_count + 1,),
        in_specs=[pl.BlockSpec(memory_space=pltpu.SMEM)]
        + [whole(a.shape) for a in packets]
        + [tiles(rows)] * blocks
        + [tiles(latent), tiles(1), tiles(experts_all)]
        + [in_hbm] * 3,
        out_shape=[
            jax.ShapeDtypeStruct((rest, width), jnp.bfloat16),
            jax.ShapeDtypeStruct((rest, LANES), jnp.float32),
            jax.ShapeDtypeStruct((rest, LANES), jnp.float32),
            jax.ShapeDtypeStruct((rows, width), jnp.float32),
        ]
        + [jax.ShapeDtypeStruct((rows, width), jnp.bfloat16)] * far,
        out_specs=[tiles(rest), whole((rest, LANES)), whole((rest, LANES)), tiles(rows)]
        + [whole((rows, width))] * far,
        scratch_shapes=[
            pltpu.VMEM((total, packed), jnp.bfloat16),
            pltpu.VMEM((total, LANES), jnp.float32),
            pltpu.VMEM((total, experts_all), jnp.float32),
            pltpu.VMEM((far * rows, width), jnp.bfloat16),
            pltpu.VMEM((far * rows, units), jnp.bfloat16),
            pltpu.VMEM((width, units), jnp.bfloat16),
            pltpu.VMEM((width, units), jnp.bfloat16),
            pltpu.VMEM((units, width), jnp.bfloat16),
            pltpu.SemaphoreType.DMA((6,)),
        ],
        compiler_params=pltpu.CompilerParams(
            dimension_semantics=("arbitrary",), vmem_limit_bytes=scoped(need)
        ),
        cost_estimate=pl.CostEstimate(
            flops=2 * total * width * latent + 6 * far * rows * width * units,
            bytes_accessed=2 * total * width * 2 + latent * width * 2 + 6 * width * units,
            transcendentals=total,
        ),
        name="front",
    )(pick, *packets, *resid_blocks, w_out, gain, w_router_t, wg, wu, wd)
    return results[:4], results[4:]


def gate_up_kernel(tile, x, scale, weight, w_gate, w_up, act, wg, wu, sems):
    total = x.shape[0]
    copies = []
    for k in range(wg.shape[1] // tile):
        part = slice(k * tile, (k + 1) * tile)
        copies.append(pltpu.make_async_copy(w_gate.at[0, :, part], wg.at[:, part], sems.at[2 * k]))
        copies.append(pltpu.make_async_copy(w_up.at[0, :, part], wu.at[:, part], sems.at[2 * k + 1]))
    for copy in copies:
        copy.start()
    for k in range(wg.shape[1] // tile):
        part = slice(k * tile, (k + 1) * tile)
        copies[2 * k].wait()
        copies[2 * k + 1].wait()
        for c in range(0, total, 512):
            at = slice(c, min(c + 512, total))
            act[at, part] = expert_rows(
                x[at, :], scale[at, :1], weight[at, :1], wg[:, part], wu[:, part]
            )


def gate_up(x, scale, weight, wg, wu):
    total, width = x.shape
    units = wg.shape[2]
    tile = tile_of(units, 256)
    in_hbm, in_vmem = pl.BlockSpec(memory_space=pltpu.HBM), pl.BlockSpec(memory_space=pltpu.VMEM)
    need = total * (2 * width + 4 * units + 8 * LANES) + 4 * width * units + 512 * tile * 16
    return pl.pallas_call(
        lambda *refs: gate_up_kernel(tile, *refs),
        in_specs=[in_vmem] * 3 + [in_hbm] * 2,
        out_specs=in_vmem,
        out_shape=jax.ShapeDtypeStruct((total, units), jnp.bfloat16),
        scratch_shapes=[
            pltpu.VMEM((width, units), jnp.bfloat16),
            pltpu.VMEM((width, units), jnp.bfloat16),
            pltpu.SemaphoreType.DMA((2 * (units // tile),)),
        ],
        compiler_params=pltpu.CompilerParams(vmem_limit_bytes=scoped(need)),
        cost_estimate=pl.CostEstimate(
            flops=4 * total * width * units,
            bytes_accessed=4 * width * units + 2 * total * width,
            transcendentals=total * units,
        ),
        name="gate_up",
    )(x, scale, weight, wg, wu)


def down_kernel(rows, tile, act, w_down, *refs):
    outs, wd, sems = refs[:-2], refs[-2], refs[-1]
    total = act.shape[0]
    copies = []
    for k in range(wd.shape[1] // tile):
        part = slice(k * tile, (k + 1) * tile)
        copies.append(pltpu.make_async_copy(w_down.at[0, :, part], wd.at[:, part], sems.at[k]))
    for copy in copies:
        copy.start()
    for k in range(wd.shape[1] // tile):
        part = slice(k * tile, (k + 1) * tile)
        copies[k].wait()
        for c in range(0, total, 512):
            end = min(c + 512, total)
            y = jnp.dot(act[c:end, :], wd[:, part], preferred_element_type=jnp.float32)
            for b in range(c // rows, end // rows):
                outs[b][:, part] = y[b * rows - c : (b + 1) * rows - c].astype(jnp.bfloat16)


def down(rows, act, wd):
    total, units = act.shape
    width = wd.shape[2]
    tile = tile_of(width, 512)
    blocks = total // rows
    in_hbm, in_vmem = pl.BlockSpec(memory_space=pltpu.HBM), pl.BlockSpec(memory_space=pltpu.VMEM)
    need = total * (2 * width + 2 * units) + 2 * width * units + 512 * tile * 8
    return pl.pallas_call(
        lambda *refs: down_kernel(rows, tile, *refs),
        in_specs=[in_vmem, in_hbm],
        out_specs=[in_vmem] * blocks,
        out_shape=[jax.ShapeDtypeStruct((rows, width), jnp.bfloat16)] * blocks,
        scratch_shapes=[
            pltpu.VMEM((units, width), jnp.bfloat16),
            pltpu.SemaphoreType.DMA((width // tile,)),
        ],
        compiler_params=pltpu.CompilerParams(vmem_limit_bytes=scoped(need)),
        cost_estimate=pl.CostEstimate(
            flops=2 * total * width * units,
            bytes_accessed=2 * width * units + 2 * total * width,
            transcendentals=0,
        ),
        name="down",
    )(act, wd)


def attention(q_abs, new_lat, owned_cache, row_lengths, latent):
    step_count, row_count, kv_width = new_lat.shape
    head_count = q_abs.shape[2] // kv_width
    context = owned_cache.shape[1]
    queries = q_abs.reshape(step_count, row_count, head_count, kv_width)
    cache_scores = (
        jnp.einsum("srhk,rpk->srhp", queries, owned_cache, preferred_element_type=jnp.float32)
        * qk_scale
    )
    visible = jnp.arange(context)[None, :] < row_lengths[:, None]
    cache_scores = jnp.where(visible[None, :, None, :], cache_scores, -1e30)
    fresh_scores = (
        jnp.einsum("srhk,trk->srht", queries, new_lat, preferred_element_type=jnp.float32)
        * qk_scale
    )
    causal = jnp.arange(step_count)[:, None] >= jnp.arange(step_count)[None, :]
    fresh_scores = jnp.where(causal[:, None, None, :], fresh_scores, -1e30)
    scores = jnp.concatenate([cache_scores, fresh_scores], axis=-1)
    weights = jax.nn.softmax(scores, axis=-1).astype(jnp.bfloat16)
    pooled = jnp.einsum(
        "srhp,rpl->srl",
        weights[..., :context],
        owned_cache[..., :latent],
        preferred_element_type=jnp.float32,
    )
    pooled = pooled + jnp.einsum(
        "srht,trl->srl",
        weights[..., context:],
        new_lat[..., :latent],
        preferred_element_type=jnp.float32,
    )
    return pooled.astype(jnp.bfloat16)


def local(
    q_abs,
    new_lat,
    latent_cache,
    lengths,
    owner,
    resid,
    routes,
    w_out,
    norm_gain,
    w_router,
    w_gate,
    w_up,
    w_down,
):
    devices = lax.axis_size("expert")
    device_index = lax.axis_index("expert")
    step_count, row_count, width = resid.shape
    rows = step_count * row_count
    experts_all = w_router.shape[1]
    sharers = devices // experts_all
    chips = devices // 2
    half = chips // 2
    cut = rows // 2
    far, near = distances(chips)
    hold = lax.optimization_barrier
    sibling = sibling_perm(chips)

    def send(a, perm):
        return lax.ppermute(a, "expert", perm)

    to_right, to_left = shift_perm(chips, 1), shift_perm(chips, -1)

    def around(to_the_right, to_the_left):
        return send(to_the_right, to_right), send(to_the_left, to_left)

    wanted = (owner[:, None] == jnp.arange(owner.shape[0], dtype=jnp.int32)).astype(jnp.bfloat16)
    ordered = jnp.einsum(
        "jr,rpk->jpk", wanted, latent_cache, preferred_element_type=jnp.float32
    ).astype(jnp.bfloat16)
    row_owner = lax.dynamic_slice_in_dim(owner, device_index * row_count, row_count)
    row_lengths = jnp.sum(
        jnp.where(
            row_owner[:, None] == jnp.arange(owner.shape[0], dtype=jnp.int32), lengths[None, :], 0
        ),
        axis=1,
    )
    routed = jnp.any(routes[..., None] == jnp.arange(LANES, dtype=jnp.int32), axis=2)
    routed = routed.astype(jnp.bfloat16)
    gain = norm_gain[None, :]
    pick = (device_index // sharers).astype(jnp.int32)[None]

    mine = resid.reshape(rows, width)
    held, sib = {0: mine}, {}
    held[-1], held[1] = around(mine, mine)
    ordered, held[-1], held[1] = hold((ordered, held[-1], held[1]))
    owned_cache = lax.all_to_all(ordered, "expert", split_axis=0, concat_axis=1, tiled=True)
    held[-2], held[2] = around(held[-1], held[1])
    sib[0] = send(mine, sibling)
    queries, held[-2], held[2], sib[0] = hold((q_abs, held[-2], held[2], sib[0]))
    for t in range(3, half):
        held[-t], held[t] = around(held[1 - t], held[t - 1])
    sib[-1], sib[1] = send(held[-1], sibling), send(held[1], sibling)
    owned_cache, row_lengths, routed, gain, pick, held[1 - half], held[half - 1], sib[-1], sib[1] = hold(
        (owned_cache, row_lengths, routed, gain, pick, held[1 - half], held[half - 1], sib[-1], sib[1])
    )
    last = around(held[1 - half][:cut], held[half - 1][cut:])
    for t in range(2, half):
        sib[-t], sib[t] = send(held[-t], sibling), send(held[t], sibling)
    pooled = attention(queries, new_lat, owned_cache, row_lengths, w_out.shape[0])
    packet = jnp.concatenate([pooled, routed], axis=2).reshape(rows, -1)
    packet, last, sib = hold((packet, last, sib))
    held[half] = jnp.concatenate(last, axis=0)
    sib[half] = send(held[half], sibling)

    packets, packets_sib = {0: packet}, {}
    for t in range(1, half):
        packets[-t], packets[t] = around(packets[1 - t], packets[t - 1])
        for d in {1 - t, t - 1}:
            packets_sib[d] = send(packets[d], sibling)
        packets, packets_sib, sib[half] = hold((packets, packets_sib, sib[half]))
    packets[half] = send(packets[1 - half], to_right)
    for d in (1 - half, half - 1, half):
        packets_sib[d] = send(packets[d], sibling)

    def laid(own, other):
        return [own[d] for d in far] + [other[d] for d in far] + (
            [own[d] for d in near] + [other[d] for d in near]
        )

    (x, scale, weight, hidden), outs = front(
        2 * len(far),
        pick,
        laid(packets, packets_sib),
        laid(held, sib),
        w_out,
        gain,
        w_router.T,
        w_gate,
        w_up,
        w_down,
    )

    f32 = jnp.float32
    own, got = {}, {}

    def swap(dists, results):
        for d, a, b in zip(dists, results[: len(dists)], results[len(dists) :]):
            own[d], got[d] = a, send(b, sibling)

    def part(d, lo=0, hi=rows):
        return own[d][lo:hi].astype(f32) + got[d][lo:hi].astype(f32)

    def both(right, left):
        return around(right.astype(jnp.bfloat16), left.astype(jnp.bfloat16))

    swap(far, outs)
    x, got = hold((x, got))
    right, left = both(part(half, 0, cut), part(half, cut, rows))
    act = gate_up(x, scale, weight, w_gate, w_up)
    act, right, left = hold((act, right, left))
    right = jnp.concatenate([right.astype(f32), jnp.zeros((rows - cut, width), f32)], axis=0)
    left = jnp.concatenate([jnp.zeros((cut, width), f32), left.astype(f32)], axis=0)
    right, left = both(part(half - 1) + right, part(1 - half) + left)
    outs = down(rows, act, w_down)
    outs, right, left = hold((outs, right, left))
    swap(near, outs)
    for t in range(half - 2, 0, -1):
        right, left = hold(both(part(t) + right.astype(f32), part(-t) + left.astype(f32)))
    mixed = hidden + part(0) + right.astype(f32) + left.astype(f32)
    return mixed.astype(jnp.bfloat16).reshape(step_count, row_count, width)


def solution(mesh):
    return jax.shard_map(
        local,
        mesh=mesh,
        in_specs=(
            P(None, ("group", "expert"), None),
            P(None, ("group", "expert"), None),
            P("group", "expert", None),
            P("group"),
            P("group"),
            P(None, ("group", "expert"), None),
            P(None, ("group", "expert"), None),
            P(),
            P(),
            P(),
            P("expert", None, None),
            P("expert", None, None),
            P("expert", None, None),
        ),
        out_specs=P(None, ("group", "expert"), None),
        check_vma=False,
    )
```

time: 133 us -> 138 us (1.038)
  Pallas kernels: 23.7 us -> 33.6 us
  local copies, waits for them, and re-layouts: 17.6 us -> 11.8 us
  starting transfers between devices: 39.7 us -> 36.8 us
  other arithmetic: 3.21 us -> 6.1 us
    pallas_call x2 -> x3, Pallas kernels: 23.7 us -> 33.6 us  [the longest x1 17.7 us: front(): pl.pallas_call(lambda *refs: front_kernel(far, blocks, rows, latent, widt...]
    unnamed x23 -> x31, local copies, waits for them, and re-layouts: 9.36 us -> 0.91 us
    ppermute x47, starting transfers between devices: 33.3 us -> 31.8 us  [send(): return lax.ppermute(a, 'expert', perm)]
    all_to_all x1, starting transfers between devices: 6.43 us -> 4.98 us  [local(): lax.all_to_all(ordered, 'expert', split_axis=0, concat_axis=1, tiled=True)]
  transfers between devices with their start and end apart: 48 -> 48, of which waited for: 19 -> 22; matrix products, arithmetic and copies ran while one was open for 12% -> 16% of each run, Pallas kernels for 0% -> 12%
where the time goes in v3:
time: 138 us; the launch traced here: 137 us
  waiting for transfers between devices  41.8 us (30%)
  starting transfers between devices  36.8 us (27%)
  Pallas kernels  33.6 us (24%)
  local copies, waits for them, and re-layouts  11.8 us (9%)
  matrix products  6.52 us (5%)
  other arithmetic  6.1 us (4%)
    ppermute x47, waiting for transfers between devices, send(): return lax.ppermute(a, 'expert', perm)  41.8 us
    ppermute x47, starting transfers between devices, send(): return lax.ppermute(a, 'expert', perm)  31.8 us
    pallas_call x1, Pallas kernels, front(): pl.pallas_call(lambda *refs: front_kernel(far, blocks, rows, latent, widt...  17.7 us
    pallas_call x1, Pallas kernels, gate_up(): pl.pallas_call(lambda *refs: gate_up_kernel(tile, *refs), in_specs=[in_vm...  9.26 us
    pallas_call x1, Pallas kernels, down(): pl.pallas_call(lambda *refs: down_kernel(rows, tile, *refs), in_specs=[in...  6.66 us
    all_to_all x1, starting transfers between devices, local(): lax.all_to_all(ordered, 'expert', split_axis=0, concat_axis=1, tiled=True)  4.98 us
    reshape x1, local copies, waits for them, and re-layouts, attention(): queries = q_abs.reshape(step_count, row_count, head_count, kv_width)  4.54 us
  transfers between devices with their start and end apart: 48, of which 22 were waited for; matrix products, arithmetic and copies ran while one was open for 16% of the time, Pallas kernels for 12%

profile of v3, /device:TPU:0, one launch (start us, length us, event | category | flops | bytes accessed | tf_op | source)
XLA Modules:
  0.0 136.9 jit_solution(2669195307864191604)
XLA Ops:
  0.5 2.6 %collective-permute-start.1 = (bf16[32,3584]{1,0:T(8,128)(2,1)}, bf16[32,3584]{1,0:T(8,128)(2,1)}, u32[]{:S(2)}, u32[]{:S(2)}) collective-permute-start(bf16[32,3584]{1,0:T(8,128)(2,1)} %bitcast.46), channel_id=1, source_target_pairs={{0,2},{1,3},{4,0},{5,1},{8,4},{9,5},{12,8},{13,9},{14,12},{15,13},... | collective-permute-start | bytes 688136 | tf_op jit(solution)/shard_map/ppermute | solution.py:361
  3.2 0.8 fusion.29
  4.0 0.7 dynamic_slice.3
  4.8 1.4 select_reduce_fusion
  6.1 1.0 convolution_convert_fusion
  7.1 2.5 %collective-permute-done.1.refs_24_ = bf16[32,3584]{1,0:T(8,128)(2,1)} collective-permute-done((bf16[32,3584]{1,0:T(8,128)(2,1)}, bf16[32,3584]{1,0:T(8,128)(2,1)}, u32[]{:S(2)}, u32[]{:S(2)}) %collective-permute-start.1) | collective-permute-done | bytes 229408 | tf_op jit(solution)/shard_map/ppermute | solution.py:361
  9.6 1.4 %collective-permute-done.refs_25_ = bf16[32,3584]{1,0:T(8,128)(2,1)} collective-permute-done((bf16[32,3584]{1,0:T(8,128)(2,1)}, bf16[32,3584]{1,0:T(8,128)(2,1)}, u32[]{:S(2)}, u32[]{:S(2)}) %collective-permute-start) | collective-permute-done | bytes 229408 | tf_op jit(solution)/shard_map/ppermute | solution.py:361
  11.0 1.3 copy.35
  12.3 5.0 %all-to-all-start = ((bf16[128,2,576]{2,1,0:T(2,128)(2,1)}), bf16[128,2,576]{2,1,0:T(2,128)(2,1)S(1)}, u32[]{:S(2)}, u32[]{:S(2)}) async-start(bf16[128,2,576]{2,1,0:T(2,128)(2,1)} %copy.35), calls=%async_computation | async-start | bytes 655360 | tf_op jit(solution)/shard_map/all_to_all | solution.py:388
  17.3 1.9 %collective-permute-start.2 = (bf16[32,3584]{1,0:T(8,128)(2,1)}, bf16[32,3584]{1,0:T(8,128)(2,1)}, u32[]{:S(2)}, u32[]{:S(2)}) collective-permute-start(bf16[32,3584]{1,0:T(8,128)(2,1)} %collective-permute-done.refs_25_), channel_id=1, source_target_pairs={{0,4},{1,5},{4,8},{5,9},{8,12},{9,13},{12,14},{13,15},{14,10},{15,... | collective-permute-start | bytes 688136 | tf_op jit(solution)/shard_map/ppermute | solution.py:361
  19.9 0.7 broadcast_in_dim.59.refs_34_
  20.6 1.4 %slice.33 = bf16[4,8,512]{2,1,0:T(8,128)(2,1)} slice(bf16[4,8,576]{2,1,0:T(8,128)(2,1)} %param.14), slice={[0:4], [0:8], [0:512]} | slice | bytes 65536 | tf_op jit(solution)/shard_map/slice | solution.py:326
  23.1 5.8 %collective-permute-done.2.refs_27_ = bf16[32,3584]{1,0:T(8,128)(2,1)} collective-permute-done((bf16[32,3584]{1,0:T(8,128)(2,1)}, bf16[32,3584]{1,0:T(8,128)(2,1)}, u32[]{:S(2)}, u32[]{:S(2)}) %collective-permute-start.2) | collective-permute-done | bytes 229408 | tf_op jit(solution)/shard_map/ppermute | solution.py:361
  28.9 1.8 %collective-permute-done.3.refs_26_ = bf16[32,3584]{1,0:T(8,128)(2,1)} collective-permute-done((bf16[32,3584]{1,0:T(8,128)(2,1)}, bf16[32,3584]{1,0:T(8,128)(2,1)}, u32[]{:S(2)}, u32[]{:S(2)}) %collective-permute-start.3) | collective-permute-done | bytes 229408 | tf_op jit(solution)/shard_map/ppermute | solution.py:361
  30.7 3.2 %collective-permute-start.5 = (bf16[32,3584]{1,0:T(8,128)(2,1)}, bf16[32,3584]{1,0:T(8,128)(2,1)S(1)}, u32[]{:S(2)}, u32[]{:S(2)}) collective-permute-start(bf16[32,3584]{1,0:T(8,128)(2,1)} %collective-permute-done.2.refs_27_), channel_id=1, source_target_pairs={{0,4},{1,5},{4,8},{5,9},{8,12},{9,13},{12,14},{13,15},{14,10},{15,... | collective-permute-start | bytes 688136 | tf_op jit(solution)/shard_map/ppermute | solution.py:361
  33.9 4.5 %reshape.52 = bf16[4,8,64,576]{3,2,1,0:T(8,128)(2,1)S(1)} reshape(bf16[4,8,36864]{2,1,0:T(8,128)(2,1)} %param.13) | data formatting | bytes 4718592 | tf_op jit(solution)/shard_map/reshape | solution.py:302
  38.5 2.7 %fusion.36 = (f32[4,8,64]{2,0,1:T(4,128)}, f32[4,8,64,4]{2,3,0,1:T(4,128)S(1)}) fusion(bf16[4,8,576,1]{2,1,0,3:T(8,128)(2,1)} %bitcast.49, bf16[4,8,64,576]{3,2,1,0:T(8,128)(2,1)S(1)} %reshape.52, pred[4,4]{1,0:T(4,128)(4,1)} %iota_compare_fusion.4), kind=kOutput, calls=%fused_computation.51 | convolution fusion | flops 9459712 | bytes 2437136 | tf_op jit(solution)/shard_map/srhk,trk->srht/dot_general | solution.py:310
  41.6 1.0 all_to_all.16
  43.2 0.9 slice.35
  45.0 2.5 %fusion.35 = (f32[4,8,64]{2,0,1:T(4,128)S(1)}, f32[4,8,64,32]{2,3,0,1:T(8,128)S(1)}) fusion(bf16[4,8,64,576]{3,2,1,0:T(8,128)(2,1)S(1)} %reshape.52, bf16[8,32,576]{2,1,0:T(8,128)(2,1)} %all_to_all.16, pred[8,32]{1,0:T(8,128)(4,1)S(1)} %iota_compare_fusion.2), kind=kOutput, calls=%fused_computation.50 | convolution fusion | flops 75692032 | bytes 2924800 | tf_op jit(solution)/shard_map/srhk,rpk->srhp/dot_general | solution.py:304
  48.3 1.5 %collective-permute-start.10 = (bf16[16,3584]{1,0:T(8,128)(2,1)S(1)}, bf16[16,3584]{1,0:T(8,128)(2,1)S(1)}, u32[]{:S(2)}, u32[]{:S(2)}) collective-permute-start(bf16[16,3584]{1,0:T(8,128)(2,1)S(1)} %slice.35), channel_id=1, source_target_pairs={{0,2},{1,3},{4,0},{5,1},{8,4},{9,5},{12,8},{13,9},{14,12},{15,13},... | collective-permute-start | bytes 344072 | tf_op jit(solution)/shard_map/ppermute | solution.py:361
  50.8 3.2 %collective-permute-done.10 = bf16[16,3584]{1,0:T(8,128)(2,1)S(1)} collective-permute-done((bf16[16,3584]{1,0:T(8,128)(2,1)S(1)}, bf16[16,3584]{1,0:T(8,128)(2,1)S(1)}, u32[]{:S(2)}, u32[]{:S(2)}) %collective-permute-start.10) | collective-permute-done | bytes 114720 | tf_op jit(solution)/shard_map/ppermute | solution.py:361
  54.0 1.4 %collective-permute-done.9 = bf16[16,3584]{1,0:T(8,128)(2,1)S(1)} collective-permute-done((bf16[16,3584]{1,0:T(8,128)(2,1)S(1)}, bf16[16,3584]{1,0:T(8,128)(2,1)S(1)}, u32[]{:S(2)}, u32[]{:S(2)}) %collective-permute-start.9) | collective-permute-done | bytes 114720 | tf_op jit(solution)/shard_map/ppermute | solution.py:361
  56.0 1.7 %collective-permute-start.16 = (bf16[32,640]{1,0:T(8,128)(2,1)S(1)}, bf16[32,640]{1,0:T(8,128)(2,1)S(1)}, u32[]{:S(2)}, u32[]{:S(2)}) collective-permute-start(bf16[32,640]{1,0:T(8,128)(2,1)S(1)} %bitcast.40), channel_id=1, source_target_pairs={{0,2},{1,3},{4,0},{5,1},{8,4},{9,5},{12,8},{13,9},{14,12},{15,13},... | collective-permute-start | bytes 122888 | tf_op jit(solution)/shard_map/ppermute | solution.py:361
  58.0 2.0 %collective-permute-done.16.refs_8_ = bf16[32,640]{1,0:T(8,128)(2,1)S(1)} collective-permute-done((bf16[32,640]{1,0:T(8,128)(2,1)S(1)}, bf16[32,640]{1,0:T(8,128)(2,1)S(1)}, u32[]{:S(2)}, u32[]{:S(2)}) %collective-permute-start.16) | collective-permute-done | bytes 40992 | tf_op jit(solution)/shard_map/ppermute | solution.py:361
  60.0 1.7 %collective-permute-done.15.refs_9_ = bf16[32,640]{1,0:T(8,128)(2,1)S(1)} collective-permute-done((bf16[32,640]{1,0:T(8,128)(2,1)S(1)}, bf16[32,640]{1,0:T(8,128)(2,1)S(1)}, u32[]{:S(2)}, u32[]{:S(2)}) %collective-permute-start.15) | collective-permute-done | bytes 40992 | tf_op jit(solution)/shard_map/ppermute | solution.py:361
  62.3 1.7 %collective-permute-start.20 = (bf16[32,640]{1,0:T(8,128)(2,1)S(1)}, bf16[32,640]{1,0:T(8,128)(2,1)S(1)}, u32[]{:S(2)}, u32[]{:S(2)}) collective-permute-start(bf16[32,640]{1,0:T(8,128)(2,1)S(1)} %collective-permute-done.16.refs_8_), channel_id=1, source_target_pairs={{0,2},{1,3},{4,0},{5,1},{8,4},{9,5},{12,8},{13,9},{14,12},{15,13},... | collective-permute-start | bytes 122888 | tf_op jit(solution)/shard_map/ppermute | solution.py:361
  64.0 1.8 %collective-permute-done.19.refs_11_ = bf16[32,640]{1,0:T(8,128)(2,1)S(1)} collective-permute-done((bf16[32,640]{1,0:T(8,128)(2,1)S(1)}, bf16[32,640]{1,0:T(8,128)(2,1)S(1)}, u32[]{:S(2)}, u32[]{:S(2)}) %collective-permute-start.19) | collective-permute-done | bytes 40992 | tf_op jit(solution)/shard_map/ppermute | solution.py:361
  67.1 1.5 %collective-permute-start.24 = (bf16[32,640]{1,0:T(8,128)(2,1)S(1)}, bf16[32,640]{1,0:T(8,128)(2,1)S(1)}, u32[]{:S(2)}, u32[]{:S(2)}) collective-permute-start(bf16[32,640]{1,0:T(8,128)(2,1)S(1)} %collective-permute-done.20.refs_10_), channel_id=1, source_target_pairs={{0,2},{1,3},{4,0},{5,1},{8,4},{9,5},{12,8},{13,9},{14,12},{15,13},... | collective-permute-start | bytes 122888 | tf_op jit(solution)/shard_map/ppermute | solution.py:361
  68.5 1.7 %collective-permute-done.23.refs_3_ = bf16[32,640]{1,0:T(8,128)(2,1)S(1)} collective-permute-done((bf16[32,640]{1,0:T(8,128)(2,1)S(1)}, bf16[32,640]{1,0:T(8,128)(2,1)S(1)}, u32[]{:S(2)}, u32[]{:S(2)}) %collective-permute-start.23) | collective-permute-done | bytes 40992 | tf_op jit(solution)/shard_map/ppermute | solution.py:361
  70.3 0.8 collective-permute-done.24.refs_2_
  71.1 1.7 %collective-permute-start.27 = (bf16[32,640]{1,0:T(8,128)(2,1)S(1)}, bf16[32,640]{1,0:T(8,128)(2,1)S(1)}, u32[]{:S(2)}, u32[]{:S(2)}) collective-permute-start(bf16[32,640]{1,0:T(8,128)(2,1)S(1)} %collective-permute-done.23.refs_3_), channel_id=1, source_target_pairs={{0,4},{1,5},{4,8},{5,9},{8,12},{9,13},{12,14},{13,15},{14,10},{15,... | collective-permute-start | bytes 122888 | tf_op jit(solution)/shard_map/ppermute | solution.py:361
  73.3 1.8 %collective-permute-done.27.refs_1_ = bf16[32,640]{1,0:T(8,128)(2,1)S(1)} collective-permute-done((bf16[32,640]{1,0:T(8,128)(2,1)S(1)}, bf16[32,640]{1,0:T(8,128)(2,1)S(1)}, u32[]{:S(2)}, u32[]{:S(2)}) %collective-permute-start.27) | collective-permute-done | bytes 40992 | tf_op jit(solution)/shard_map/ppermute | solution.py:361
  75.1 1.2 collective-permute-done.28.refs_4_
  76.4 17.7 %front.1 = (bf16[320,3584]{1,0:T(8,128)(2,1)}, f32[320,128]{1,0:T(8,128)S(1)}, f32[320,128]{1,0:T(8,128)S(1)}, f32[32,3584]{1,0:T(8,128)}, bf16[32,3584]{1,0:T(8...) custom-call(s32[1]{0:T(128)} %bitcast.4.refs_0_, ...), custom_call_target="tpu_custom_call" | custom-call | flops 6106906624 | bytes 33030144 | tf_op jit(solution)/shard_map/front/pallas_call | solution.py:166
  94.8 1.0 collective-permute-done.31
  96.5 1.5 %collective-permute-start.35 = (bf16[16,3584]{1,0:T(8,128)(2,1)S(1)}, bf16[16,3584]{1,0:T(8,128)(2,1)S(1)}, u32[]{:S(2)}, u32[]{:S(2)}) collective-permute-start(bf16[16,3584]{1,0:T(8,128)(2,1)S(1)} %get-tuple-element.197), channel_id=1, source_target_pairs={{0,2},{1,3},{4,0},{5,1},{8,4},{9,5},{12,8},{13,9},{14,12},{15,13},... | collective-permute-start | bytes 344072 | tf_op jit(solution)/shard_map/ppermute | solution.py:361
  98.6 9.3 %gate_up.1.refs_0_ = bf16[320,1024]{1,0:T(8,128)(2,1)S(1)} custom-call(bf16[320,3584]{1,0:T(8,128)(2,1)} %get-tuple-element.159.refs_0_, f32[320,128]{1,0:T(8,128)S(1)} %get-tuple-element.160.refs_1_, f32[320,128]{1,0:T(8,128)S(1)} %get-tuple-element.161.refs_2_, bf16[1,3584,1024]{2,1,0:T(8,128)(2,1)} %refs_3_.1, bf16[1,3584,1024]{2,1,0:T(8,128)(2,1)} %refs_4_.1), custom_call_target="tpu_custom_call" | custom-call | flops 4697620480 | bytes 16973824 | tf_op jit(solution)/shard_map/gate_up/pallas_call | solution.py:233
  107.9 0.8 copy-done.1
  108.8 1.8 %collective-permute-start.36 = (bf16[32,3584]{1,0:T(8,128)(2,1)S(1)}, bf16[32,3584]{1,0:T(8,128)(2,1)S(1)}, u32[]{:S(2)}, u32[]{:S(2)}) collective-permute-start(bf16[32,3584]{1,0:T(8,128)(2,1)S(1)} %add_convert_fusion.6), channel_id=1, source_target_pairs={{0,4},{1,5},{4,8},{5,9},{8,12},{9,13},{12,14},{13,15},{14,10},{15,... | collective-permute-start | bytes 688136 | tf_op jit(solution)/shard_map/ppermute | solution.py:361
  111.2 6.7 %down.1 = (bf16[32,3584]{1,0:T(8,128)(2,1)S(1)}, bf16[32,3584]{1,0:T(8,128)(2,1)S(1)}, bf16[32,3584]{1,0:T(8,128)(2,1)S(1)}, bf16[32,3584]{1,0:T(8,128)(2,1)S(1)...) custom-call(bf16[320,1024]{1,0:T(8,128)(2,1)} %copy-done.1, ...), custom_call_target="tpu_custom_call" | custom-call | flops 2348810240 | bytes 9633792 | tf_op jit(solution)/shard_map/down/pallas_call | solution.py:279
  118.5 1.2 collective-permute-done.40
  119.8 1.8 %collective-permute-start.41 = (bf16[32,3584]{1,0:T(8,128)(2,1)S(1)}, bf16[32,3584]{1,0:T(8,128)(2,1)S(1)}, u32[]{:S(2)}, u32[]{:S(2)}) collective-permute-start(bf16[32,3584]{1,0:T(8,128)(2,1)S(1)} %add_convert_fusion.4), channel_id=1, source_target_pairs={{0,4},{1,5},{4,8},{5,9},{8,12},{9,13},{12,14},{13,15},{14,10},{15,... | collective-permute-start | bytes 688136 | tf_op jit(solution)/shard_map/ppermute | solution.py:361
  122.5 5.0 %collective-permute-done.41 = bf16[32,3584]{1,0:T(8,128)(2,1)S(1)} collective-permute-done((bf16[32,3584]{1,0:T(8,128)(2,1)S(1)}, bf16[32,3584]{1,0:T(8,128)(2,1)S(1)}, u32[]{:S(2)}, u32[]{:S(2)}) %collective-permute-start.41) | collective-permute-done | bytes 229408 | tf_op jit(solution)/shard_map/ppermute | solution.py:361
  127.5 1.6 %collective-permute-done.43 = bf16[32,3584]{1,0:T(8,128)(2,1)S(1)} collective-permute-done((bf16[32,3584]{1,0:T(8,128)(2,1)S(1)}, bf16[32,3584]{1,0:T(8,128)(2,1)S(1)}, u32[]{:S(2)}, u32[]{:S(2)}) %collective-permute-start.43) | collective-permute-done | bytes 229408 | tf_op jit(solution)/shard_map/ppermute | solution.py:361
  129.8 1.5 %collective-permute-start.46 = (bf16[32,3584]{1,0:T(8,128)(2,1)S(1)}, bf16[32,3584]{1,0:T(8,128)(2,1)S(1)}, u32[]{:S(2)}, u32[]{:S(2)}) collective-permute-start(bf16[32,3584]{1,0:T(8,128)(2,1)S(1)} %add_convert_fusion.1), channel_id=1, source_target_pairs={{0,2},{1,3},{4,0},{5,1},{8,4},{9,5},{12,8},{13,9},{14,12},{15,13},... | collective-permute-start | bytes 688136 | tf_op jit(solution)/shard_map/ppermute | solution.py:361
  131.4 4.3 %collective-permute-done.44 = bf16[32,3584]{1,0:T(8,128)(2,1)S(1)} collective-permute-done((bf16[32,3584]{1,0:T(8,128)(2,1)S(1)}, bf16[32,3584]{1,0:T(8,128)(2,1)S(1)}, u32[]{:S(2)}, u32[]{:S(2)}) %collective-permute-start.44) | collective-permute-done | bytes 229408 | tf_op jit(solution)/shard_map/ppermute | solution.py:361
  136.1 0.8 fusion.28
  (118 shorter events, 14.7 us)
Async XLA Ops:
  0.0 23.1 %collective-permute-start.4 = (bf16[32,3584]{1,0:T(8,128)(2,1)}, bf16[32,3584]{1,0:T(8,128)(2,1)S(1)}, u32[]{:S(2)}, u32[]{:S(2)}) collective-permute-start(bf16[32,3584]{1,0:T(8,128)(2,1)} %bitcast.45), channel_id=1, source_target_pairs={{0,1},{1,0},{2,3},{3,2},{4,5},{5,4},{6,7},{7,6},{8,9},{9,8},{10,11... | collective-permute-start | bytes 688136 | tf_op jit(solution)/shard_map/ppermute | solution.py:361
  0.5 9.2 %collective-permute-start.1 = (bf16[32,3584]{1,0:T(8,128)(2,1)}, bf16[32,3584]{1,0:T(8,128)(2,1)}, u32[]{:S(2)}, u32[]{:S(2)}) collective-permute-start(bf16[32,3584]{1,0:T(8,128)(2,1)} %bitcast.46), channel_id=1, source_target_pairs={{0,2},{1,3},{4,0},{5,1},{8,4},{9,5},{12,8},{13,9},{14,12},{15,13},... | collective-permute-start | bytes 688136 | tf_op jit(solution)/shard_map/ppermute | solution.py:361
  3.0 8.0 %collective-permute-start = (bf16[32,3584]{1,0:T(8,128)(2,1)}, bf16[32,3584]{1,0:T(8,128)(2,1)}, u32[]{:S(2)}, u32[]{:S(2)}) collective-permute-start(bf16[32,3584]{1,0:T(8,128)(2,1)} %bitcast.47), channel_id=1, source_target_pairs={{0,4},{1,5},{4,8},{5,9},{8,12},{9,13},{12,14},{13,15},{14,10},{15,... | collective-permute-start | bytes 688136 | tf_op jit(solution)/shard_map/ppermute | solution.py:361
  12.3 28.9 %all-to-all-start = ((bf16[128,2,576]{2,1,0:T(2,128)(2,1)}), bf16[128,2,576]{2,1,0:T(2,128)(2,1)S(1)}, u32[]{:S(2)}, u32[]{:S(2)}) async-start(bf16[128,2,576]{2,1,0:T(2,128)(2,1)} %copy.35), calls=%async_computation | async-start | bytes 655360 | tf_op jit(solution)/shard_map/all_to_all | solution.py:388
  17.3 11.6 %collective-permute-start.2 = (bf16[32,3584]{1,0:T(8,128)(2,1)}, bf16[32,3584]{1,0:T(8,128)(2,1)}, u32[]{:S(2)}, u32[]{:S(2)}) collective-permute-start(bf16[32,3584]{1,0:T(8,128)(2,1)} %collective-permute-done.refs_25_), channel_id=1, source_target_pairs={{0,4},{1,5},{4,8},{5,9},{8,12},{9,13},{12,14},{13,15},{14,10},{15,... | collective-permute-start | bytes 688136 | tf_op jit(solution)/shard_map/ppermute | solution.py:361
  19.2 11.5 %collective-permute-start.3 = (bf16[32,3584]{1,0:T(8,128)(2,1)}, bf16[32,3584]{1,0:T(8,128)(2,1)}, u32[]{:S(2)}, u32[]{:S(2)}) collective-permute-start(bf16[32,3584]{1,0:T(8,128)(2,1)} %collective-permute-done.1.refs_24_), channel_id=1, source_target_pairs={{0,2},{1,3},{4,0},{5,1},{8,4},{9,5},{12,8},{13,9},{14,12},{15,13},... | collective-permute-start | bytes 688136 | tf_op jit(solution)/shard_map/ppermute | solution.py:361
  22.6 20.0 %collective-permute-start.7 = (bf16[32,3584]{1,0:T(8,128)(2,1)}, bf16[32,3584]{1,0:T(8,128)(2,1)}, u32[]{:S(2)}, u32[]{:S(2)}) collective-permute-start(bf16[32,3584]{1,0:T(8,128)(2,1)} %collective-permute-done.refs_25_), channel_id=1, source_target_pairs={{0,1},{1,0},{2,3},{3,2},{4,5},{5,4},{6,7},{7,6},{8,9},{9,8},{10,11... | collective-permute-start | bytes 688136 | tf_op jit(solution)/shard_map/ppermute | solution.py:361
  22.6 20.2 %collective-permute-start.8 = (bf16[32,3584]{1,0:T(8,128)(2,1)}, bf16[32,3584]{1,0:T(8,128)(2,1)}, u32[]{:S(2)}, u32[]{:S(2)}) collective-permute-start(bf16[32,3584]{1,0:T(8,128)(2,1)} %collective-permute-done.1.refs_24_), channel_id=1, source_target_pairs={{0,1},{1,0},{2,3},{3,2},{4,5},{5,4},{6,7},{7,6},{8,9},{9,8},{10,11... | collective-permute-start | bytes 688136 | tf_op jit(solution)/shard_map/ppermute | solution.py:361
  30.7 19.3 %collective-permute-start.12 = (bf16[32,3584]{1,0:T(8,128)(2,1)}, bf16[32,3584]{1,0:T(8,128)(2,1)}, u32[]{:S(2)}, u32[]{:S(2)}) collective-permute-start(bf16[32,3584]{1,0:T(8,128)(2,1)} %collective-permute-done.2.refs_27_), channel_id=1, source_target_pairs={{0,1},{1,0},{2,3},{3,2},{4,5},{5,4},{6,7},{7,6},{8,9},{9,8},{10,11... | collective-permute-start | bytes 688136 | tf_op jit(solution)/shard_map/ppermute | solution.py:361
  30.7 12.1 %collective-permute-start.5 = (bf16[32,3584]{1,0:T(8,128)(2,1)}, bf16[32,3584]{1,0:T(8,128)(2,1)S(1)}, u32[]{:S(2)}, u32[]{:S(2)}) collective-permute-start(bf16[32,3584]{1,0:T(8,128)(2,1)} %collective-permute-done.2.refs_27_), channel_id=1, source_target_pairs={{0,4},{1,5},{4,8},{5,9},{8,12},{9,13},{12,14},{13,15},{14,10},{15,... | collective-permute-start | bytes 688136 | tf_op jit(solution)/shard_map/ppermute | solution.py:361
  33.9 8.9 %collective-permute-start.6 = (bf16[32,3584]{1,0:T(8,128)(2,1)}, bf16[32,3584]{1,0:T(8,128)(2,1)}, u32[]{:S(2)}, u32[]{:S(2)}) collective-permute-start(bf16[32,3584]{1,0:T(8,128)(2,1)} %collective-permute-done.3.refs_26_), channel_id=1, source_target_pairs={{0,2},{1,3},{4,0},{5,1},{8,4},{9,5},{12,8},{13,9},{14,12},{15,13},... | collective-permute-start | bytes 688136 | tf_op jit(solution)/shard_map/ppermute | solution.py:361
  42.6 8.2 %collective-permute-start.13 = (bf16[32,3584]{1,0:T(8,128)(2,1)}, bf16[32,3584]{1,0:T(8,128)(2,1)S(1)}, u32[]{:S(2)}, u32[]{:S(2)}) collective-permute-start(bf16[32,3584]{1,0:T(8,128)(2,1)} %collective-permute-done.3.refs_26_), channel_id=1, source_target_pairs={{0,1},{1,0},{2,3},{3,2},{4,5},{5,4},{6,7},{7,6},{8,9},{9,8},{10,11... | collective-permute-start | bytes 688136 | tf_op jit(solution)/shard_map/ppermute | solution.py:361
  42.8 12.6 %collective-permute-start.11 = (bf16[32,3584]{1,0:T(8,128)(2,1)S(1)}, bf16[32,3584]{1,0:T(8,128)(2,1)S(1)}, u32[]{:S(2)}, u32[]{:S(2)}) collective-permute-start(bf16[32,3584]{1,0:T(8,128)(2,1)S(1)} %collective-permute-done.5.refs_19_), channel_id=1, source_target_pairs={{0,1},{1,0},{2,3},{3,2},{4,5},{5,4},{6,7},{7,6},{8,9},{9,8},{10,11... | collective-permute-start | bytes 688136 | tf_op jit(solution)/shard_map/ppermute | solution.py:361
  44.1 11.3 %collective-permute-start.14 = (bf16[32,3584]{1,0:T(8,128)(2,1)}, bf16[32,3584]{1,0:T(8,128)(2,1)S(1)}, u32[]{:S(2)}, u32[]{:S(2)}) collective-permute-start(bf16[32,3584]{1,0:T(8,128)(2,1)} %collective-permute-done.6.refs_18_), channel_id=1, source_target_pairs={{0,1},{1,0},{2,3},{3,2},{4,5},{5,4},{6,7},{7,6},{8,9},{9,8},{10,11... | collective-permute-start | bytes 688136 | tf_op jit(solution)/shard_map/ppermute | solution.py:361
  48.3 5.7 %collective-permute-start.10 = (bf16[16,3584]{1,0:T(8,128)(2,1)S(1)}, bf16[16,3584]{1,0:T(8,128)(2,1)S(1)}, u32[]{:S(2)}, u32[]{:S(2)}) collective-permute-start(bf16[16,3584]{1,0:T(8,128)(2,1)S(1)} %slice.35), channel_id=1, source_target_pairs={{0,2},{1,3},{4,0},{5,1},{8,4},{9,5},{12,8},{13,9},{14,12},{15,13},... | collective-permute-start | bytes 344072 | tf_op jit(solution)/shard_map/ppermute | solution.py:361
  50.0 5.4 %collective-permute-start.9 = (bf16[16,3584]{1,0:T(8,128)(2,1)S(1)}, bf16[16,3584]{1,0:T(8,128)(2,1)S(1)}, u32[]{:S(2)}, u32[]{:S(2)}) collective-permute-start(bf16[16,3584]{1,0:T(8,128)(2,1)S(1)} %slice.34), channel_id=1, source_target_pairs={{0,4},{1,5},{4,8},{5,9},{8,12},{9,13},{12,14},{13,15},{14,10},{15,... | collective-permute-start | bytes 344072 | tf_op jit(solution)/shard_map/ppermute | solution.py:361
  55.4 6.3 %collective-permute-start.18 = (bf16[32,3584]{1,0:T(8,128)(2,1)S(1)}, bf16[32,3584]{1,0:T(8,128)(2,1)S(1)}, u32[]{:S(2)}, u32[]{:S(2)}) collective-permute-start(bf16[32,3584]{1,0:T(8,128)(2,1)S(1)} %constant_dynamic-update-slice_fusion.refs_17_), channel_id=1, source_target_pairs={{0,1},{1,0},{2,3},{3,2},{4,5},{5,4},{6,7},{7,6},{8,9},{9,8},{10,11... | collective-permute-start | bytes 688136 | tf_op jit(solution)/shard_map/ppermute | solution.py:361
  55.5 2.5 %collective-permute-start.17 = (bf16[32,640]{1,0:T(8,128)(2,1)S(1)}, bf16[32,640]{1,0:T(8,128)(2,1)S(1)}, u32[]{:S(2)}, u32[]{:S(2)}) collective-permute-start(bf16[32,640]{1,0:T(8,128)(2,1)S(1)} %bitcast.39), channel_id=1, source_target_pairs={{0,1},{1,0},{2,3},{3,2},{4,5},{5,4},{6,7},{7,6},{8,9},{9,8},{10,11... | collective-permute-start | bytes 122888 | tf_op jit(solution)/shard_map/ppermute | solution.py:361
  56.0 4.0 %collective-permute-start.16 = (bf16[32,640]{1,0:T(8,128)(2,1)S(1)}, bf16[32,640]{1,0:T(8,128)(2,1)S(1)}, u32[]{:S(2)}, u32[]{:S(2)}) collective-permute-start(bf16[32,640]{1,0:T(8,128)(2,1)S(1)} %bitcast.40), channel_id=1, source_target_pairs={{0,2},{1,3},{4,0},{5,1},{8,4},{9,5},{12,8},{13,9},{14,12},{15,13},... | collective-permute-start | bytes 122888 | tf_op jit(solution)/shard_map/ppermute | solution.py:361
  57.8 4.0 %collective-permute-start.15 = (bf16[32,640]{1,0:T(8,128)(2,1)S(1)}, bf16[32,640]{1,0:T(8,128)(2,1)S(1)}, u32[]{:S(2)}, u32[]{:S(2)}) collective-permute-start(bf16[32,640]{1,0:T(8,128)(2,1)S(1)} %bitcast.41), channel_id=1, source_target_pairs={{0,4},{1,5},{4,8},{5,9},{8,12},{9,13},{12,14},{13,15},{14,10},{15,... | collective-permute-start | bytes 122888 | tf_op jit(solution)/shard_map/ppermute | solution.py:361
  61.8 2.3 %collective-permute-start.21 = (bf16[32,640]{1,0:T(8,128)(2,1)S(1)}, bf16[32,640]{1,0:T(8,128)(2,1)S(1)}, u32[]{:S(2)}, u32[]{:S(2)}) collective-permute-start(bf16[32,640]{1,0:T(8,128)(2,1)S(1)} %collective-permute-done.15.refs_9_), channel_id=1, source_target_pairs={{0,1},{1,0},{2,3},{3,2},{4,5},{5,4},{6,7},{7,6},{8,9},{9,8},{10,11... | collective-permute-start | bytes 122888 | tf_op jit(solution)/shard_map/ppermute | solution.py:361
  61.8 4.1 %collective-permute-start.19 = (bf16[32,640]{1,0:T(8,128)(2,1)S(1)}, bf16[32,640]{1,0:T(8,128)(2,1)S(1)}, u32[]{:S(2)}, u32[]{:S(2)}) collective-permute-start(bf16[32,640]{1,0:T(8,128)(2,1)S(1)} %collective-permute-done.15.refs_9_), channel_id=1, source_target_pairs={{0,4},{1,5},{4,8},{5,9},{8,12},{9,13},{12,14},{13,15},{14,10},{15,... | collective-permute-start | bytes 122888 | tf_op jit(solution)/shard_map/ppermute | solution.py:361
  62.1 3.7 %collective-permute-start.22 = (bf16[32,640]{1,0:T(8,128)(2,1)S(1)}, bf16[32,640]{1,0:T(8,128)(2,1)S(1)}, u32[]{:S(2)}, u32[]{:S(2)}) collective-permute-start(bf16[32,640]{1,0:T(8,128)(2,1)S(1)} %collective-permute-done.16.refs_8_), channel_id=1, source_target_pairs={{0,1},{1,0},{2,3},{3,2},{4,5},{5,4},{6,7},{7,6},{8,9},{9,8},{10,11... | collective-permute-start | bytes 122888 | tf_op jit(solution)/shard_map/ppermute | solution.py:361
  62.3 4.0 %collective-permute-start.20 = (bf16[32,640]{1,0:T(8,128)(2,1)S(1)}, bf16[32,640]{1,0:T(8,128)(2,1)S(1)}, u32[]{:S(2)}, u32[]{:S(2)}) collective-permute-start(bf16[32,640]{1,0:T(8,128)(2,1)S(1)} %collective-permute-done.16.refs_8_), channel_id=1, source_target_pairs={{0,2},{1,3},{4,0},{5,1},{8,4},{9,5},{12,8},{13,9},{14,12},{15,13},... | collective-permute-start | bytes 122888 | tf_op jit(solution)/shard_map/ppermute | solution.py:361
  66.3 2.3 %collective-permute-start.25 = (bf16[32,640]{1,0:T(8,128)(2,1)S(1)}, bf16[32,640]{1,0:T(8,128)(2,1)S(1)}, u32[]{:S(2)}, u32[]{:S(2)}) collective-permute-start(bf16[32,640]{1,0:T(8,128)(2,1)S(1)} %collective-permute-done.19.refs_11_), channel_id=1, source_target_pairs={{0,1},{1,0},{2,3},{3,2},{4,5},{5,4},{6,7},{7,6},{8,9},{9,8},{10,11... | collective-permute-start | bytes 122888 | tf_op jit(solution)/shard_map/ppermute | solution.py:361
  66.3 4.0 %collective-permute-start.23 = (bf16[32,640]{1,0:T(8,128)(2,1)S(1)}, bf16[32,640]{1,0:T(8,128)(2,1)S(1)}, u32[]{:S(2)}, u32[]{:S(2)}) collective-permute-start(bf16[32,640]{1,0:T(8,128)(2,1)S(1)} %collective-permute-done.19.refs_11_), channel_id=1, source_target_pairs={{0,4},{1,5},{4,8},{5,9},{8,12},{9,13},{12,14},{13,15},{14,10},{15,... | collective-permute-start | bytes 122888 | tf_op jit(solution)/shard_map/ppermute | solution.py:361
  66.9 3.4 %collective-permute-start.26 = (bf16[32,640]{1,0:T(8,128)(2,1)S(1)}, bf16[32,640]{1,0:T(8,128)(2,1)S(1)}, u32[]{:S(2)}, u32[]{:S(2)}) collective-permute-start(bf16[32,640]{1,0:T(8,128)(2,1)S(1)} %collective-permute-done.20.refs_10_), channel_id=1, source_target_pairs={{0,1},{1,0},{2,3},{3,2},{4,5},{5,4},{6,7},{7,6},{8,9},{9,8},{10,11... | collective-permute-start | bytes 122888 | tf_op jit(solution)/shard_map/ppermute | solution.py:361
  67.1 4.0 %collective-permute-start.24 = (bf16[32,640]{1,0:T(8,128)(2,1)S(1)}, bf16[32,640]{1,0:T(8,128)(2,1)S(1)}, u32[]{:S(2)}, u32[]{:S(2)}) collective-permute-start(bf16[32,640]{1,0:T(8,128)(2,1)S(1)} %collective-permute-done.20.refs_10_), channel_id=1, source_target_pairs={{0,2},{1,3},{4,0},{5,1},{8,4},{9,5},{12,8},{13,9},{14,12},{15,13},... | collective-permute-start | bytes 122888 | tf_op jit(solution)/shard_map/ppermute | solution.py:361
  71.1 4.0 %collective-permute-start.27 = (bf16[32,640]{1,0:T(8,128)(2,1)S(1)}, bf16[32,640]{1,0:T(8,128)(2,1)S(1)}, u32[]{:S(2)}, u32[]{:S(2)}) collective-permute-start(bf16[32,640]{1,0:T(8,128)(2,1)S(1)} %collective-permute-done.23.refs_3_), channel_id=1, source_target_pairs={{0,4},{1,5},{4,8},{5,9},{8,12},{9,13},{12,14},{13,15},{14,10},{15,... | collective-permute-start | bytes 122888 | tf_op jit(solution)/shard_map/ppermute | solution.py:361
  72.8 2.3 %collective-permute-start.30 = (bf16[32,640]{1,0:T(8,128)(2,1)S(1)}, bf16[32,640]{1,0:T(8,128)(2,1)S(1)}, u32[]{:S(2)}, u32[]{:S(2)}) collective-permute-start(bf16[32,640]{1,0:T(8,128)(2,1)S(1)} %collective-permute-done.23.refs_3_), channel_id=1, source_target_pairs={{0,1},{1,0},{2,3},{3,2},{4,5},{5,4},{6,7},{7,6},{8,9},{9,8},{10,11... | collective-permute-start | bytes 122888 | tf_op jit(solution)/shard_map/ppermute | solution.py:361
  72.8 2.3 %collective-permute-start.29 = (bf16[32,640]{1,0:T(8,128)(2,1)S(1)}, bf16[32,640]{1,0:T(8,128)(2,1)S(1)}, u32[]{:S(2)}, u32[]{:S(2)}) collective-permute-start(bf16[32,640]{1,0:T(8,128)(2,1)S(1)} %collective-permute-done.24.refs_2_), channel_id=1, source_target_pairs={{0,1},{1,0},{2,3},{3,2},{4,5},{5,4},{6,7},{7,6},{8,9},{9,8},{10,11... | collective-permute-start | bytes 122888 | tf_op jit(solution)/shard_map/ppermute | solution.py:361
  75.1 1.2 collective-permute-start.28
  94.0 1.8 %collective-permute-start.31 = (bf16[32,3584]{1,0:T(8,128)(2,1)}, bf16[32,3584]{1,0:T(8,128)(2,1)S(1)}, u32[]{:S(2)}, u32[]{:S(2)}) collective-permute-start(bf16[32,3584]{1,0:T(8,128)(2,1)} %get-tuple-element.156), channel_id=1, source_target_pairs={{0,1},{1,0},{2,3},{3,2},{4,5},{5,4},{6,7},{7,6},{8,9},{9,8},{10,11... | collective-permute-start | bytes 688136 | tf_op jit(solution)/shard_map/ppermute | solution.py:361
  94.2 1.9 %collective-permute-start.32 = (bf16[32,3584]{1,0:T(8,128)(2,1)}, bf16[32,3584]{1,0:T(8,128)(2,1)S(1)}, u32[]{:S(2)}, u32[]{:S(2)}) collective-permute-start(bf16[32,3584]{1,0:T(8,128)(2,1)} %get-tuple-element.157), channel_id=1, source_target_pairs={{0,1},{1,0},{2,3},{3,2},{4,5},{5,4},{6,7},{7,6},{8,9},{9,8},{10,11... | collective-permute-start | bytes 688136 | tf_op jit(solution)/shard_map/ppermute | solution.py:361
  94.6 1.8 %collective-permute-start.33 = (bf16[32,3584]{1,0:T(8,128)(2,1)}, bf16[32,3584]{1,0:T(8,128)(2,1)S(1)}, u32[]{:S(2)}, u32[]{:S(2)}) collective-permute-start(bf16[32,3584]{1,0:T(8,128)(2,1)} %get-tuple-element.158), channel_id=1, source_target_pairs={{0,1},{1,0},{2,3},{3,2},{4,5},{5,4},{6,7},{7,6},{8,9},{9,8},{10,11... | collective-permute-start | bytes 688136 | tf_op jit(solution)/shard_map/ppermute | solution.py:361
  96.5 12.2 %collective-permute-start.35 = (bf16[16,3584]{1,0:T(8,128)(2,1)S(1)}, bf16[16,3584]{1,0:T(8,128)(2,1)S(1)}, u32[]{:S(2)}, u32[]{:S(2)}) collective-permute-start(bf16[16,3584]{1,0:T(8,128)(2,1)S(1)} %get-tuple-element.197), channel_id=1, source_target_pairs={{0,2},{1,3},{4,0},{5,1},{8,4},{9,5},{12,8},{13,9},{14,12},{15,13},... | collective-permute-start | bytes 344072 | tf_op jit(solution)/shard_map/ppermute | solution.py:361
  98.0 10.7 %collective-permute-start.34 = (bf16[16,3584]{1,0:T(8,128)(2,1)S(1)}, bf16[16,3584]{1,0:T(8,128)(2,1)S(1)}, u32[]{:S(2)}, u32[]{:S(2)}) collective-permute-start(bf16[16,3584]{1,0:T(8,128)(2,1)S(1)} %get-tuple-element.198), channel_id=1, source_target_pairs={{0,4},{1,5},{4,8},{5,9},{8,12},{9,13},{12,14},{13,15},{14,10},{15,... | collective-permute-start | bytes 344072 | tf_op jit(solution)/shard_map/ppermute | solution.py:361
  108.8 9.1 %collective-permute-start.36 = (bf16[32,3584]{1,0:T(8,128)(2,1)S(1)}, bf16[32,3584]{1,0:T(8,128)(2,1)S(1)}, u32[]{:S(2)}, u32[]{:S(2)}) collective-permute-start(bf16[32,3584]{1,0:T(8,128)(2,1)S(1)} %add_convert_fusion.6), channel_id=1, source_target_pairs={{0,4},{1,5},{4,8},{5,9},{8,12},{9,13},{12,14},{13,15},{14,10},{15,... | collective-permute-start | bytes 688136 | tf_op jit(solution)/shard_map/ppermute | solution.py:361
  110.6 7.3 %collective-permute-start.37 = (bf16[32,3584]{1,0:T(8,128)(2,1)S(1)}, bf16[32,3584]{1,0:T(8,128)(2,1)S(1)}, u32[]{:S(2)}, u32[]{:S(2)}) collective-permute-start(bf16[32,3584]{1,0:T(8,128)(2,1)S(1)} %add_convert_fusion.5), channel_id=1, source_target_pairs={{0,2},{1,3},{4,0},{5,1},{8,4},{9,5},{12,8},{13,9},{14,12},{15,13},... | collective-permute-start | bytes 688136 | tf_op jit(solution)/shard_map/ppermute | solution.py:361
  117.9 1.8 %collective-permute-start.40 = (bf16[32,3584]{1,0:T(8,128)(2,1)}, bf16[32,3584]{1,0:T(8,128)(2,1)S(1)}, u32[]{:S(2)}, u32[]{:S(2)}) collective-permute-start(bf16[32,3584]{1,0:T(8,128)(2,1)} %get-tuple-element.186), channel_id=1, source_target_pairs={{0,1},{1,0},{2,3},{3,2},{4,5},{5,4},{6,7},{7,6},{8,9},{9,8},{10,11... | collective-permute-start | bytes 688136 | tf_op jit(solution)/shard_map/ppermute | solution.py:361
  118.0 3.6 %collective-permute-start.42 = (bf16[32,3584]{1,0:T(8,128)(2,1)}, bf16[32,3584]{1,0:T(8,128)(2,1)S(1)}, u32[]{:S(2)}, u32[]{:S(2)}) collective-permute-start(bf16[32,3584]{1,0:T(8,128)(2,1)} %get-tuple-element.189), channel_id=1, source_target_pairs={{0,1},{1,0},{2,3},{3,2},{4,5},{5,4},{6,7},{7,6},{8,9},{9,8},{10,11... | collective-permute-start | bytes 688136 | tf_op jit(solution)/shard_map/ppermute | solution.py:361
  119.8 7.7 %collective-permute-start.41 = (bf16[32,3584]{1,0:T(8,128)(2,1)S(1)}, bf16[32,3584]{1,0:T(8,128)(2,1)S(1)}, u32[]{:S(2)}, u32[]{:S(2)}) collective-permute-start(bf16[32,3584]{1,0:T(8,128)(2,1)S(1)} %add_convert_fusion.4), channel_id=1, source_target_pairs={{0,4},{1,5},{4,8},{5,9},{8,12},{9,13},{12,14},{13,15},{14,10},{15,... | collective-permute-start | bytes 688136 | tf_op jit(solution)/shard_map/ppermute | solution.py:361
  121.6 7.4 %collective-permute-start.43 = (bf16[32,3584]{1,0:T(8,128)(2,1)S(1)}, bf16[32,3584]{1,0:T(8,128)(2,1)S(1)}, u32[]{:S(2)}, u32[]{:S(2)}) collective-permute-start(bf16[32,3584]{1,0:T(8,128)(2,1)S(1)} %add_convert_fusion.3), channel_id=1, source_target_pairs={{0,2},{1,3},{4,0},{5,1},{8,4},{9,5},{12,8},{13,9},{14,12},{15,13},... | collective-permute-start | bytes 688136 | tf_op jit(solution)/shard_map/ppermute | solution.py:361
  122.0 7.1 %collective-permute-start.39 = (bf16[32,3584]{1,0:T(8,128)(2,1)S(1)}, bf16[32,3584]{1,0:T(8,128)(2,1)S(1)}, u32[]{:S(2)}, u32[]{:S(2)}) collective-permute-start(bf16[32,3584]{1,0:T(8,128)(2,1)S(1)} %get-tuple-element.184), channel_id=1, source_target_pairs={{0,1},{1,0},{2,3},{3,2},{4,5},{5,4},{6,7},{7,6},{8,9},{9,8},{10,11... | collective-permute-start | bytes 688136 | tf_op jit(solution)/shard_map/ppermute | solution.py:361
  122.0 7.7 %collective-permute-start.45 = (bf16[32,3584]{1,0:T(8,128)(2,1)S(1)}, bf16[32,3584]{1,0:T(8,128)(2,1)S(1)}, u32[]{:S(2)}, u32[]{:S(2)}) collective-permute-start(bf16[32,3584]{1,0:T(8,128)(2,1)S(1)} %get-tuple-element.193), channel_id=1, source_target_pairs={{0,1},{1,0},{2,3},{3,2},{4,5},{5,4},{6,7},{7,6},{8,9},{9,8},{10,11... | collective-permute-start | bytes 688136 | tf_op jit(solution)/shard_map/ppermute | solution.py:361
  129.1 6.5 %collective-permute-start.44 = (bf16[32,3584]{1,0:T(8,128)(2,1)S(1)}, bf16[32,3584]{1,0:T(8,128)(2,1)S(1)}, u32[]{:S(2)}, u32[]{:S(2)}) collective-permute-start(bf16[32,3584]{1,0:T(8,128)(2,1)S(1)} %add_convert_fusion.2), channel_id=1, source_target_pairs={{0,4},{1,5},{4,8},{5,9},{8,12},{9,13},{12,14},{13,15},{14,10},{15,... | collective-permute-start | bytes 688136 | tf_op jit(solution)/shard_map/ppermute | solution.py:361
  129.8 6.3 %collective-permute-start.46 = (bf16[32,3584]{1,0:T(8,128)(2,1)S(1)}, bf16[32,3584]{1,0:T(8,128)(2,1)S(1)}, u32[]{:S(2)}, u32[]{:S(2)}) collective-permute-start(bf16[32,3584]{1,0:T(8,128)(2,1)S(1)} %add_convert_fusion.1), channel_id=1, source_target_pairs={{0,2},{1,3},{4,0},{5,1},{8,4},{9,5},{12,8},{13,9},{14,12},{15,13},... | collective-permute-start | bytes 688136 | tf_op jit(solution)/shard_map/ppermute | solution.py:361
  131.4 4.7 %collective-permute-start.38 = (bf16[32,3584]{1,0:T(8,128)(2,1)S(1)}, bf16[32,3584]{1,0:T(8,128)(2,1)S(1)}, u32[]{:S(2)}, u32[]{:S(2)}) collective-permute-start(bf16[32,3584]{1,0:T(8,128)(2,1)S(1)} %get-tuple-element.182), channel_id=1, source_target_pairs={{0,1},{1,0},{2,3},{3,2},{4,5},{5,4},{6,7},{7,6},{8,9},{9,8},{10,11... | collective-permute-start | bytes 688136 | tf_op jit(solution)/shard_map/ppermute | solution.py:361
  (15 other events, 196.6 us)

commit v4 on v3

--- a/solution.py
+++ b/solution.py
@@ -32,6 +32,39 @@
     return far, [d for d in range(half - 1) for d in ((d, -d) if d else (0,))]
 
 
+def gather_steps(chips):
+    high = 4 if chips % 4 == 0 else 2
+    return high, chips // high
+
+
+def step_perm(chips, by_high, by_low):
+    high, low = gather_steps(chips)
+    return [
+        (
+            2 * (h * low + l) + core,
+            2 * ((h - by_high) % high * low + (l - by_low) % low) + core,
+        )
+        for h in range(high)
+        for l in range(low)
+        for core in range(2)
+    ]
+
+
+def gathered_place(chips, parts):
+    high, low = gather_steps(chips)
+    ring = ring_of(chips)
+    table = [[] for _ in range(chips)]
+    for p, chip in enumerate(ring):
+        for part in parts:
+            for side in (0, chips):
+                for d in part:
+                    other = ring[(p + d) % chips]
+                    by_high = (other // low - chip // low) % high
+                    by_low = (other % low - chip % low) % low
+                    table[chip].append(side + by_low * high + by_high)
+    return table
+
+
 def tile_of(size, most):
     return max(t for t in range(LANES, min(size, most) + 1, LANES) if size % t == 0)
 
@@ -40,44 +73,63 @@
     return max(52 << 20, (int(need) // (1 << 20) + 5) << 20)
 
 
-def expert_rows(xs, r, gate, w_g, w_u):
-    a = jnp.dot(xs, w_g, preferred_element_type=jnp.float32) * r
-    b = jnp.dot(xs, w_u, preferred_element_type=jnp.float32) * r
-    return (jax.nn.silu(a) * b * gate).astype(jnp.bfloat16)
-
-
-def front_kernel(far, blocks, rows, latent, width, *refs):
-    pick = refs[0]
-    pooled = refs[1 : 1 + blocks]
-    resid = refs[1 + blocks : 1 + 2 * blocks]
-    w_out, gain, w_router, w_gate, w_up, w_down = refs[1 + 2 * blocks : 7 + 2 * blocks]
-    x, scale, weight, hidden = refs[7 + 2 * blocks : 11 + 2 * blocks]
-    outs = refs[11 + 2 * blocks : 11 + 2 * blocks + far]
-    joined, ssq, logits, x_far, act, wg, wu, wd, sems = refs[11 + 2 * blocks + far :]
+def expert_rows(xs, r, gate, w_gu):
+    both = jnp.dot(xs, w_gu, preferred_element_type=jnp.float32) * r
+    half = both.shape[1] // 2
+    return (jax.nn.silu(both[:, :half]) * both[:, half:] * gate).astype(jnp.bfloat16)
+
+
+def stream_gate_up(tile, w_gate, w_up, wgu, sems):
+    copies = []
+    for k in range(w_gate.shape[2] // tile):
+        part, at = slice(k * tile, (k + 1) * tile), 2 * k * tile
+        copies.append(
+            pltpu.make_async_copy(w_gate.at[0, :, part], wgu.at[:, at : at + tile], sems.at[2 * k])
+        )
+        copies.append(
+            pltpu.make_async_copy(
+                w_up.at[0, :, part], wgu.at[:, at + tile : at + 2 * tile], sems.at[2 * k + 1]
+            )
+        )
+    return copies
+
+
+def front_kernel(far, blocks, rows, latent, width, tile, down_tile, *refs):
+    scalars = refs[0]
+    pooled = refs[1:5]
+    resid = refs[5 : 5 + blocks]
+    w_out, gain, w_router, w_gate, w_up, w_down = refs[5 + blocks : 11 + blocks]
+    x, scale, weight, hidden = refs[11 + blocks : 15 + blocks]
+    outs = refs[15 + blocks : 15 + blocks + far]
+    raw, joined, ssq, logits, x_far, act, wgu, wd, sems = refs[15 + blocks + far :]
     step = pl.program_id(0)
     cols = w_out.shape[1]
     tiles = width // cols
     total = blocks * rows
     far_rows = far * rows
     experts_all = w_router.shape[0]
-    units = wg.shape[1]
+    units = act.shape[1]
     chunk = min(512, total)
 
-    copies = []
-    for k in range(2):
-        part = slice(k * units // 2, (k + 1) * units // 2)
-        copies.append(pltpu.make_async_copy(w_gate.at[0, :, part], wg.at[:, part], sems.at[2 * k]))
-        copies.append(pltpu.make_async_copy(w_up.at[0, :, part], wu.at[:, part], sems.at[2 * k + 1]))
-    for k in range(2):
-        part = slice(k * width // 2, (k + 1) * width // 2)
-        copies.append(pltpu.make_async_copy(w_down.at[0, :, part], wd.at[:, part], sems.at[4 + k]))
+    copies = stream_gate_up(tile, w_gate, w_up, wgu, sems)
+    gate_copies = len(copies)
+    for k in range(width // down_tile):
+        part = slice(k * down_tile, (k + 1) * down_tile)
+        copies.append(
+            pltpu.make_async_copy(w_down.at[0, :, part], wd.at[:, part], sems.at[gate_copies + k])
+        )
     for j, copy in enumerate(copies):
-        pl.when(step == min(j, tiles - 1))(copy.start)
+        pl.when(step == min(j // 2, tiles - 1))(copy.start)
 
     @pl.when(step == 0)
     def _():
+        start = 0
+        for piece in pooled:
+            raw[start : start + piece.shape[0], :] = piece[...]
+            start += piece.shape[0]
         for b in range(blocks):
-            joined[b * rows : (b + 1) * rows, :] = pooled[b][...]
+            place = pl.ds(pl.multiple_of(scalars[1 + b] * rows, rows), rows)
+            joined[b * rows : (b + 1) * rows, :] = raw[place, :]
         ssq[...] = jnp.zeros_like(ssq)
         logits[...] = jnp.zeros_like(logits)
 
@@ -118,37 +170,37 @@
         mask = joined[:, latent : latent + experts_all].astype(jnp.float32)
         affinity = jax.nn.sigmoid(logits[...] * r) * mask
         lane = lax.broadcasted_iota(jnp.int32, affinity.shape, 1)
-        mine = jnp.sum(jnp.where(lane == pick[0], affinity, 0.0), axis=1, keepdims=True)
+        mine = jnp.sum(jnp.where(lane == scalars[0], affinity, 0.0), axis=1, keepdims=True)
         gate = 2.5 * mine / jnp.sum(affinity, axis=1, keepdims=True)
         scale[...] = jnp.broadcast_to(r[far_rows:], (total - far_rows, LANES))
         weight[...] = jnp.broadcast_to(gate[far_rows:], (total - far_rows, LANES))
-        for k in range(2):
-            part = slice(k * units // 2, (k + 1) * units // 2)
+        for k in range(units // tile):
             copies[2 * k].wait()
             copies[2 * k + 1].wait()
-            act[:, part] = expert_rows(
-                x_far[...], r[:far_rows], gate[:far_rows], wg[:, part], wu[:, part]
+            act[:, k * tile : (k + 1) * tile] = expert_rows(
+                x_far[...], r[:far_rows], gate[:far_rows], wgu[:, 2 * k * tile : 2 * (k + 1) * tile]
             )
-        down = tile_of(width // 2, 1024)
-        for k in range(2):
-            copies[4 + k].wait()
-            for c in range(k * width // 2, (k + 1) * width // 2, down):
-                y = jnp.dot(act[...], wd[:, c : c + down], preferred_element_type=jnp.float32)
-                for b in range(far):
-                    outs[b][:, c : c + down] = y[b * rows : (b + 1) * rows].astype(jnp.bfloat16)
-
-
-def front(far, pick, packets, resid_blocks, w_out, gain, w_router_t, wg, wu, wd):
-    blocks = len(packets)
+        for k in range(width // down_tile):
+            copies[gate_copies + k].wait()
+            part = slice(k * down_tile, (k + 1) * down_tile)
+            y = jnp.dot(act[...], wd[:, part], preferred_element_type=jnp.float32)
+            for b in range(far):
+                outs[b][:, part] = y[b * rows : (b + 1) * rows].astype(jnp.bfloat16)
+
+
+def front(far, scalars, pooled, resid_blocks, w_out, gain, w_router_t, wg, wu, wd):
+    blocks = len(resid_blocks)
     rows, width = resid_blocks[0].shape
     latent = w_out.shape[0]
     total = blocks * rows
     rest = total - far * rows
     cols = tile_of(width, 512)
     tile_count = width // cols
-    packed = packets[0].shape[1]
+    packed = pooled[0].shape[1]
     experts_all = w_router_t.shape[0]
     units = wg.shape[2]
+    tile = tile_of(units, 256)
+    down_tile = tile_of(width, 512)
 
     def whole(shape):
         return pl.BlockSpec(shape, lambda i: (0, 0), pipeline_mode=pl.Buffered(1))
@@ -158,16 +210,16 @@
 
     in_hbm = pl.BlockSpec(memory_space=pltpu.HBM)
     need = (
-        total * (cols * 24 + packed * 4 + 8 * LANES * 4)
+        total * (cols * 24 + packed * 6 + 8 * LANES * 4)
         + 4 * latent * cols
         + far * rows * (width * 8 + units * 16)
         + 6 * width * units
     )
     results = pl.pallas_call(
-        lambda *refs: front_kernel(far, blocks, rows, latent, width, *refs),
+        lambda *refs: front_kernel(far, blocks, rows, latent, width, tile, down_tile, *refs),
         grid=(tile_count + 1,),
         in_specs=[pl.BlockSpec(memory_space=pltpu.SMEM)]
-        + [whole(a.shape) for a in packets]
+        + [whole(a.shape) for a in pooled]
         + [tiles(rows)] * blocks
         + [tiles(latent), tiles(1), tiles(experts_all)]
         + [in_hbm] * 3,
@@ -182,14 +234,14 @@
         + [whole((rows, width))] * far,
         scratch_shapes=[
             pltpu.VMEM((total, packed), jnp.bfloat16),
+            pltpu.VMEM((total, packed), jnp.bfloat16),
             pltpu.VMEM((total, LANES), jnp.float32),
             pltpu.VMEM((total, experts_all), jnp.float32),
             pltpu.VMEM((far * rows, width), jnp.bfloat16),
             pltpu.VMEM((far * rows, units), jnp.bfloat16),
-            pltpu.VMEM((width, units), jnp.bfloat16),
-            pltpu.VMEM((width, units), jnp.bfloat16),
+            pltpu.VMEM((width, 2 * units), jnp.bfloat16),
             pltpu.VMEM((units, width), jnp.bfloat16),
-            pltpu.SemaphoreType.DMA((6,)),
+            pltpu.SemaphoreType.DMA((2 * (units // tile) + width // down_tile,)),
         ],
         compiler_params=pltpu.CompilerParams(
             dimension_semantics=("arbitrary",), vmem_limit_bytes=scoped(need)
@@ -200,27 +252,22 @@
             transcendentals=total,
         ),
         name="front",
-    )(pick, *packets, *resid_blocks, w_out, gain, w_router_t, wg, wu, wd)
+    )(scalars, *pooled, *resid_blocks, w_out, gain, w_router_t, wg, wu, wd)
     return results[:4], results[4:]
 
 
-def gate_up_kernel(tile, x, scale, weight, w_gate, w_up, act, wg, wu, sems):
+def gate_up_kernel(tile, x, scale, weight, w_gate, w_up, act, wgu, sems):
     total = x.shape[0]
-    copies = []
-    for k in range(wg.shape[1] // tile):
-        part = slice(k * tile, (k + 1) * tile)
-        copies.append(pltpu.make_async_copy(w_gate.at[0, :, part], wg.at[:, part], sems.at[2 * k]))
-        copies.append(pltpu.make_async_copy(w_up.at[0, :, part], wu.at[:, part], sems.at[2 * k + 1]))
+    copies = stream_gate_up(tile, w_gate, w_up, wgu, sems)
     for copy in copies:
         copy.start()
-    for k in range(wg.shape[1] // tile):
-        part = slice(k * tile, (k + 1) * tile)
+    for k in range(w_gate.shape[2] // tile):
         copies[2 * k].wait()
         copies[2 * k + 1].wait()
         for c in range(0, total, 512):
             at = slice(c, min(c + 512, total))
-            act[at, part] = expert_rows(
-                x[at, :], scale[at, :1], weight[at, :1], wg[:, part], wu[:, part]
+            act[at, k * tile : (k + 1) * tile] = expert_rows(
+                x[at, :], scale[at, :1], weight[at, :1], wgu[:, 2 * k * tile : 2 * (k + 1) * tile]
             )
 
 
@@ -236,8 +283,7 @@
         out_specs=in_vmem,
         out_shape=jax.ShapeDtypeStruct((total, units), jnp.bfloat16),
         scratch_shapes=[
-            pltpu.VMEM((width, units), jnp.bfloat16),
-            pltpu.VMEM((width, units), jnp.bfloat16),
+            pltpu.VMEM((width, 2 * units), jnp.bfloat16),
             pltpu.SemaphoreType.DMA((2 * (units // tile),)),
         ],
         compiler_params=pltpu.CompilerParams(vmem_limit_bytes=scoped(need)),
@@ -295,11 +341,9 @@
     )(act, wd)
 
 
-def attention(q_abs, new_lat, owned_cache, row_lengths, latent):
+def attention(queries, new_lat, owned_cache, row_lengths, latent):
     step_count, row_count, kv_width = new_lat.shape
-    head_count = q_abs.shape[2] // kv_width
     context = owned_cache.shape[1]
-    queries = q_abs.reshape(step_count, row_count, head_count, kv_width)
     cache_scores = (
         jnp.einsum("srhk,rpk->srhp", queries, owned_cache, preferred_element_type=jnp.float32)
         * qk_scale
@@ -369,6 +413,16 @@
     ordered = jnp.einsum(
         "jr,rpk->jpk", wanted, latent_cache, preferred_element_type=jnp.float32
     ).astype(jnp.bfloat16)
+    owned_cache = lax.all_to_all(ordered, "expert", split_axis=0, concat_axis=1, tiled=True)
+
+    mine = resid.reshape(rows, width)
+    held, sib = {0: mine}, {}
+    held[-1], held[1] = around(mine, mine)
+    owner, lengths, routes, norm_gain, new_lat, held[-1], held[1] = hold(
+        (owner, lengths, routes, norm_gain, new_lat, held[-1], held[1])
+    )
+    held[-2], held[2] = around(held[-1], held[1])
+    sib[0] = send(mine, sibling)
     row_owner = lax.dynamic_slice_in_dim(owner, device_index * row_count, row_count)
     row_lengths = jnp.sum(
         jnp.where(
@@ -379,40 +433,38 @@
     routed = jnp.any(routes[..., None] == jnp.arange(LANES, dtype=jnp.int32), axis=2)
     routed = routed.astype(jnp.bfloat16)
     gain = norm_gain[None, :]
-    pick = (device_index // sharers).astype(jnp.int32)[None]
-
-    mine = resid.reshape(rows, width)
-    held, sib = {0: mine}, {}
-    held[-1], held[1] = around(mine, mine)
-    ordered, held[-1], held[1] = hold((ordered, held[-1], held[1]))
-    owned_cache = lax.all_to_all(ordered, "expert", split_axis=0, concat_axis=1, tiled=True)
-    held[-2], held[2] = around(held[-1], held[1])
-    sib[0] = send(mine, sibling)
-    queries, held[-2], held[2], sib[0] = hold((q_abs, held[-2], held[2], sib[0]))
+    scalars = jnp.array(
+        [
+            [device // sharers] + places
+            for chip, places in enumerate(gathered_place(chips, (far, near)))
+            for device in (2 * chip, 2 * chip + 1)
+        ],
+        jnp.int32,
+    )[device_index]
+    queries = q_abs.reshape(step_count, row_count, -1, new_lat.shape[2])
+    queries, row_lengths, routed, gain, scalars, held[-2], held[2], sib[0] = hold(
+        (queries, row_lengths, routed, gain, scalars, held[-2], held[2], sib[0])
+    )
     for t in range(3, half):
         held[-t], held[t] = around(held[1 - t], held[t - 1])
     sib[-1], sib[1] = send(held[-1], sibling), send(held[1], sibling)
-    owned_cache, row_lengths, routed, gain, pick, held[1 - half], held[half - 1], sib[-1], sib[1] = hold(
-        (owned_cache, row_lengths, routed, gain, pick, held[1 - half], held[half - 1], sib[-1], sib[1])
-    )
+    pooled = attention(queries, new_lat, owned_cache, row_lengths, w_out.shape[0])
+    packet = jnp.concatenate([pooled, routed], axis=2).reshape(rows, -1)
+    packet, held, sib = hold((packet, held, sib))
+
     last = around(held[1 - half][:cut], held[half - 1][cut:])
     for t in range(2, half):
         sib[-t], sib[t] = send(held[-t], sibling), send(held[t], sibling)
-    pooled = attention(queries, new_lat, owned_cache, row_lengths, w_out.shape[0])
-    packet = jnp.concatenate([pooled, routed], axis=2).reshape(rows, -1)
-    packet, last, sib = hold((packet, last, sib))
+    high, low = gather_steps(chips)
+    along = hold([send(packet, step_perm(chips, i, 0)) for i in range(1, high)])
+    along = jnp.concatenate([packet] + along, axis=0)
+    across = [send(along, step_perm(chips, 0, i)) for i in range(1, low)]
+    along_sib = send(along, sibling)
+    across, last, sib = hold((across, last, sib))
     held[half] = jnp.concatenate(last, axis=0)
     sib[half] = send(held[half], sibling)
-
-    packets, packets_sib = {0: packet}, {}
-    for t in range(1, half):
-        packets[-t], packets[t] = around(packets[1 - t], packets[t - 1])
-        for d in {1 - t, t - 1}:
-            packets_sib[d] = send(packets[d], sibling)
-        packets, packets_sib, sib[half] = hold((packets, packets_sib, sib[half]))
-    packets[half] = send(packets[1 - half], to_right)
-    for d in (1 - half, half - 1, half):
-        packets_sib[d] = send(packets[d], sibling)
+    across = across[0] if low == 2 else jnp.concatenate(across, axis=0)
+    packets = [along, across, along_sib, send(across, sibling)]
 
     def laid(own, other):
         return [own[d] for d in far] + [other[d] for d in far] + (
@@ -421,8 +473,8 @@
 
     (x, scale, weight, hidden), outs = front(
         2 * len(far),
-        pick,
-        laid(packets, packets_sib),
+        scalars,
+        packets,
         laid(held, sib),
         w_out,
         gain,

time: 138 us -> 121 us (0.88)
  waiting for transfers between devices: 41.8 us -> 30.5 us
  starting transfers between devices: 36.8 us -> 33.7 us
  other arithmetic: 6.1 us -> 3.33 us
    ppermute x47 -> x38, waiting for transfers between devices: 41.8 us -> 30.5 us  [send(): return lax.ppermute(a, 'expert', perm)]
    ppermute x47 -> x38, starting transfers between devices: 31.8 us -> 27.4 us  [send(): return lax.ppermute(a, 'expert', perm)]
  transfers between devices with their start and end apart: 48 -> 39, of which waited for: 22 -> 15; matrix products, arithmetic and copies ran while one was open for 16% -> 15% of each run, Pallas kernels for 12% -> 13%
where the time goes in v4:
time: 121 us
  Pallas kernels  34.3 us (28%)
  starting transfers between devices  33.7 us (28%)
  waiting for transfers between devices  30.5 us (25%)
  local copies, waits for them, and re-layouts  12.1 us (10%)
  matrix products  6.38 us (5%)
  other arithmetic  3.33 us (3%)
    ppermute x38, waiting for transfers between devices, send(): return lax.ppermute(a, 'expert', perm)  30.5 us
    ppermute x38, starting transfers between devices, send(): return lax.ppermute(a, 'expert', perm)  27.4 us
    pallas_call x1, Pallas kernels, front(): pl.pallas_call(lambda *refs: front_kernel(far, blocks, rows, latent, widt...  18.4 us
    pallas_call x1, Pallas kernels, gate_up(): pl.pallas_call(lambda *refs: gate_up_kernel(tile, *refs), in_specs=[in_vm...  9.23 us
    pallas_call x1, Pallas kernels, down(): pl.pallas_call(lambda *refs: down_kernel(rows, tile, *refs), in_specs=[in...  6.68 us
    all_to_all x1, starting transfers between devices, local(): lax.all_to_all(ordered, 'expert', split_axis=0, concat_axis=1, tiled=True)  6.29 us
    reshape x1, local copies, waits for them, and re-layouts, local(): queries = q_abs.reshape(step_count, row_count, -1, new_lat.shape[2])  4.56 us
    dot_general x1, matrix products, attention(): jnp.einsum('srhk,trk->srht', queries, new_lat, preferred_element_type=jnp...  2.56 us
  transfers between devices with their start and end apart: 39, of which 15 were waited for; matrix products, arithmetic and copies ran while one was open for 15% of the time, Pallas kernels for 13%

profile of v4, /device:TPU:0, one launch (start us, length us, event | category | flops | bytes accessed | tf_op | source)
XLA Modules:
  0.0 120.9 jit_solution(17434178484973782114)
XLA Ops:
  0.5 2.6 %collective-permute-start.1 = (bf16[32,3584]{1,0:T(8,128)(2,1)}, bf16[32,3584]{1,0:T(8,128)(2,1)}, u32[]{:S(2)}, u32[]{:S(2)}) collective-permute-start(bf16[32,3584]{1,0:T(8,128)(2,1)} %bitcast.37), channel_id=1, source_target_pairs={{0,2},{1,3},{4,0},{5,1},{8,4},{9,5},{12,8},{13,9},{14,12},{15,13},... | collective-permute-start | bytes 688136 | tf_op jit(solution)/shard_map/ppermute | solution.py:405
  3.2 1.0 convolution_convert_fusion
  4.2 1.3 %copy.37 = bf16[128,2,576]{2,1,0:T(2,128)(2,1)} copy(bf16[128,2,576]{0,2,1:T(8,128)(2,1)S(1)} %convolution_convert_fusion) | data formatting | bytes 589824 | tf_op jit(solution)/shard_map/convert_element_type | solution.py:415
  5.4 6.3 %all-to-all-start = ((bf16[128,2,576]{2,1,0:T(2,128)(2,1)}), bf16[128,2,576]{2,1,0:T(2,128)(2,1)S(1)}, u32[]{:S(2)}, u32[]{:S(2)}) async-start(bf16[128,2,576]{2,1,0:T(2,128)(2,1)} %copy.37), calls=%async_computation | async-start | bytes 655360 | tf_op jit(solution)/shard_map/all_to_all | solution.py:416
  11.8 4.6 %reshape.51 = bf16[4,8,64,576]{3,2,1,0:T(8,128)(2,1)S(1)} reshape(bf16[4,8,36864]{2,1,0:T(8,128)(2,1)} %param.14) | data formatting | bytes 4718592 | tf_op jit(solution)/shard_map/reshape | solution.py:444
  16.4 0.7 dynamic-slice_bitcast_fusion.refs_0_
  17.6 1.7 %collective-permute-start.2 = (bf16[32,3584]{1,0:T(8,128)(2,1)}, bf16[32,3584]{1,0:T(8,128)(2,1)}, u32[]{:S(2)}, u32[]{:S(2)}) collective-permute-start(bf16[32,3584]{1,0:T(8,128)(2,1)} %collective-permute-done.refs_13_), channel_id=1, source_target_pairs={{0,4},{1,5},{4,8},{5,9},{8,12},{9,13},{12,14},{13,15},{14,10},{15,... | collective-permute-start | bytes 688136 | tf_op jit(solution)/shard_map/ppermute | solution.py:405
  20.0 0.6 copy.43
  20.7 5.7 %collective-permute-done.2.refs_15_ = bf16[32,3584]{1,0:T(8,128)(2,1)} collective-permute-done((bf16[32,3584]{1,0:T(8,128)(2,1)}, bf16[32,3584]{1,0:T(8,128)(2,1)}, u32[]{:S(2)}, u32[]{:S(2)}) %collective-permute-start.2) | collective-permute-done | bytes 229408 | tf_op jit(solution)/shard_map/ppermute | solution.py:405
  26.3 1.2 %collective-permute-done.3.refs_14_ = bf16[32,3584]{1,0:T(8,128)(2,1)} collective-permute-done((bf16[32,3584]{1,0:T(8,128)(2,1)}, bf16[32,3584]{1,0:T(8,128)(2,1)}, u32[]{:S(2)}, u32[]{:S(2)}) %collective-permute-start.3) | collective-permute-done | bytes 229408 | tf_op jit(solution)/shard_map/ppermute | solution.py:405
  27.6 1.5 %collective-permute-start.5 = (bf16[32,3584]{1,0:T(8,128)(2,1)}, bf16[32,3584]{1,0:T(8,128)(2,1)S(1)}, u32[]{:S(2)}, u32[]{:S(2)}) collective-permute-start(bf16[32,3584]{1,0:T(8,128)(2,1)} %collective-permute-done.2.refs_15_), channel_id=1, source_target_pairs={{0,4},{1,5},{4,8},{5,9},{8,12},{9,13},{12,14},{13,15},{14,10},{15,... | collective-permute-start | bytes 688136 | tf_op jit(solution)/shard_map/ppermute | solution.py:405
  29.0 0.6 collective-permute-start.6
  29.7 2.6 %fusion.37 = (f32[4,8,64]{2,0,1:T(4,128)}, f32[4,8,64,4]{2,3,0,1:T(4,128)}) fusion(bf16[4,8,64,576]{3,2,1,0:T(8,128)(2,1)S(1)} %reshape.51, bf16[4,8,576,1]{2,1,0,3:T(8,128)(2,1)S(1)} %bitcast.44, pred[4,4]{1,0:T(4,128)(4,1)S(1)} %iota_compare_fusion.4), kind=kOutput, calls=%fused_computation.56 | convolution fusion | flops 9459712 | bytes 2437136 | tf_op jit(solution)/shard_map/srhk,trk->srht/dot_general | solution.py:354
  32.6 1.0 reshape.56
  33.6 1.0 all_to_all.16
  34.6 2.6 %fusion.36 = (f32[4,8,64]{2,0,1:T(4,128)S(1)}, f32[4,8,64,32]{2,3,0,1:T(8,128)S(1)}) fusion(bf16[4,8,64,576]{3,2,1,0:T(8,128)(2,1)S(1)} %reshape.51, bf16[8,32,576,1]{2,1,0,3:T(8,128)(2,1)} %reshape.56, pred[8,32]{1,0:T(8,128)(4,1)S(1)} %iota_compare_fusion.2), kind=kOutput, calls=%fused_computation.55 | convolution fusion | flops 75692032 | bytes 2924800 | tf_op jit(solution)/shard_map/srhk,rpk->srhp/dot_general | solution.py:348
  37.2 1.0 fusion.25
  39.2 1.5 %collective-permute-start.11 = (bf16[32,640]{1,0:T(8,128)(2,1)S(1)}, bf16[32,640]{1,0:T(8,128)(2,1)S(1)}, u32[]{:S(2)}, u32[]{:S(2)}) collective-permute-start(bf16[32,640]{1,0:T(8,128)(2,1)S(1)} %bitcast.40), channel_id=1, source_target_pairs={{0,4},{1,5},{2,6},{3,7},{4,8},{5,9},{6,10},{7,11},{8,12},{9,13},{1... | collective-permute-start | bytes 122888 | tf_op jit(solution)/shard_map/ppermute | solution.py:405
  40.7 2.4 %collective-permute-start.10 = (bf16[32,640]{1,0:T(8,128)(2,1)S(1)}, bf16[32,640]{1,0:T(8,128)(2,1)S(1)}, u32[]{:S(2)}, u32[]{:S(2)}) collective-permute-start(bf16[32,640]{1,0:T(8,128)(2,1)S(1)} %bitcast.41), channel_id=1, source_target_pairs={{0,8},{1,9},{2,10},{3,11},{4,12},{5,13},{6,14},{7,15},{8,0},{9,1},... | collective-permute-start | bytes 122888 | tf_op jit(solution)/shard_map/ppermute | solution.py:405
  43.1 1.5 %collective-permute-start.9 = (bf16[32,640]{1,0:T(8,128)(2,1)S(1)}, bf16[32,640]{1,0:T(8,128)(2,1)S(1)}, u32[]{:S(2)}, u32[]{:S(2)}) collective-permute-start(bf16[32,640]{1,0:T(8,128)(2,1)S(1)} %bitcast.42), channel_id=1, source_target_pairs={{0,12},{1,13},{2,14},{3,15},{4,0},{5,1},{6,2},{7,3},{8,4},{9,5},{1... | collective-permute-start | bytes 122888 | tf_op jit(solution)/shard_map/ppermute | solution.py:405
  44.6 0.9 slice.35
  46.0 0.6 collective-permute-start.14
  46.6 1.5 %collective-permute-start.13 = (bf16[16,3584]{1,0:T(8,128)(2,1)S(1)}, bf16[16,3584]{1,0:T(8,128)(2,1)S(1)}, u32[]{:S(2)}, u32[]{:S(2)}) collective-permute-start(bf16[16,3584]{1,0:T(8,128)(2,1)S(1)} %slice.34), channel_id=1, source_target_pairs={{0,4},{1,5},{4,8},{5,9},{8,12},{9,13},{12,14},{13,15},{14,10},{15,... | collective-permute-start | bytes 344072 | tf_op jit(solution)/shard_map/ppermute | solution.py:405
  48.1 3.1 %collective-permute-done.14 = bf16[16,3584]{1,0:T(8,128)(2,1)S(1)} collective-permute-done((bf16[16,3584]{1,0:T(8,128)(2,1)S(1)}, bf16[16,3584]{1,0:T(8,128)(2,1)S(1)}, u32[]{:S(2)}, u32[]{:S(2)}) %collective-permute-start.14) | collective-permute-done | bytes 114720 | tf_op jit(solution)/shard_map/ppermute | solution.py:405
  51.4 0.6 collective-permute-start.12
  52.0 5.8 %collective-permute-done.12.refs_2_ = bf16[128,640]{1,0:T(8,128)(2,1)S(1)} collective-permute-done((bf16[128,640]{1,0:T(8,128)(2,1)S(1)}, bf16[128,640]{1,0:T(8,128)(2,1)S(1)}, u32[]{:S(2)}, u32[]{:S(2)}) %collective-permute-start.12) | collective-permute-done | bytes 163872 | tf_op jit(solution)/shard_map/ppermute | solution.py:405
  58.0 0.5 collective-permute-start.19
  58.6 1.1 collective-permute-done.19.refs_3_
  60.0 0.7 copy-done.12
  60.7 18.4 %front.1 = (bf16[320,3584]{1,0:T(8,128)(2,1)}, f32[320,128]{1,0:T(8,128)S(1)}, f32[320,128]{1,0:T(8,128)S(1)}, f32[32,3584]{1,0:T(8,128)}, bf16[32,3584]{1,0:T(8...) custom-call(s32[17]{0:T(128)S(1)} %dynamic-slice_bitcast_fusion.refs, ...), custom_call_target="tpu_custom_call" | custom-call | flops 6106906624 | bytes 33030144 | tf_op jit(solution)/shard_map/front/pallas_call | solution.py:218
  79.9 1.0 collective-permute-done.22
  81.6 0.6 collective-permute-start.26
  82.2 1.5 %collective-permute-start.25 = (bf16[16,3584]{1,0:T(8,128)(2,1)S(1)}, bf16[16,3584]{1,0:T(8,128)(2,1)S(1)}, u32[]{:S(2)}, u32[]{:S(2)}) collective-permute-start(bf16[16,3584]{1,0:T(8,128)(2,1)S(1)} %get-tuple-element.170), channel_id=1, source_target_pairs={{0,4},{1,5},{4,8},{5,9},{8,12},{9,13},{12,14},{13,15},{14,10},{15,... | collective-permute-start | bytes 344072 | tf_op jit(solution)/shard_map/ppermute | solution.py:405
  83.7 9.2 %gate_up.1.refs_0_ = bf16[320,1024]{1,0:T(8,128)(2,1)S(1)} custom-call(bf16[320,3584]{1,0:T(8,128)(2,1)} %get-tuple-element.131.refs_0_, f32[320,128]{1,0:T(8,128)S(1)} %get-tuple-element.132.refs_1_, f32[320,128]{1,0:T(8,128)S(1)} %get-tuple-element.133.refs_2_, bf16[1,3584,1024]{2,1,0:T(8,128)(2,1)} %refs_3_.1, bf16[1,3584,1024]{2,1,0:T(8,128)(2,1)} %refs_4_.1), custom_call_target="tpu_custom_call" | custom-call | flops 4697620480 | bytes 16973824 | tf_op jit(solution)/shard_map/gate_up/pallas_call | solution.py:280
  92.9 0.8 copy-done.1
  93.8 0.6 collective-permute-start.27
  94.5 1.7 %collective-permute-start.28 = (bf16[32,3584]{1,0:T(8,128)(2,1)S(1)}, bf16[32,3584]{1,0:T(8,128)(2,1)S(1)}, u32[]{:S(2)}, u32[]{:S(2)}) collective-permute-start(bf16[32,3584]{1,0:T(8,128)(2,1)S(1)} %add_convert_fusion.5), channel_id=1, source_target_pairs={{0,2},{1,3},{4,0},{5,1},{8,4},{9,5},{12,8},{13,9},{14,12},{15,13},... | collective-permute-start | bytes 688136 | tf_op jit(solution)/shard_map/ppermute | solution.py:405
  96.3 6.7 %down.1 = (bf16[32,3584]{1,0:T(8,128)(2,1)S(1)}, bf16[32,3584]{1,0:T(8,128)(2,1)S(1)}, bf16[32,3584]{1,0:T(8,128)(2,1)S(1)}, bf16[32,3584]{1,0:T(8,128)(2,1)S(1)...) custom-call(bf16[320,1024]{1,0:T(8,128)(2,1)} %copy-done.1, ...), custom_call_target="tpu_custom_call" | custom-call | flops 2348810240 | bytes 9633792 | tf_op jit(solution)/shard_map/down/pallas_call | solution.py:325
  103.1 0.5 collective-permute-start.33
  103.6 1.2 collective-permute-done.31
  104.8 0.6 collective-permute-start.32
  105.5 1.5 %collective-permute-start.34 = (bf16[32,3584]{1,0:T(8,128)(2,1)S(1)}, bf16[32,3584]{1,0:T(8,128)(2,1)S(1)}, u32[]{:S(2)}, u32[]{:S(2)}) collective-permute-start(bf16[32,3584]{1,0:T(8,128)(2,1)S(1)} %add_convert_fusion.3), channel_id=1, source_target_pairs={{0,2},{1,3},{4,0},{5,1},{8,4},{9,5},{12,8},{13,9},{14,12},{15,13},... | collective-permute-start | bytes 688136 | tf_op jit(solution)/shard_map/ppermute | solution.py:405
  107.1 0.5 collective-permute-start.36
  107.6 5.0 %collective-permute-done.32 = bf16[32,3584]{1,0:T(8,128)(2,1)S(1)} collective-permute-done((bf16[32,3584]{1,0:T(8,128)(2,1)S(1)}, bf16[32,3584]{1,0:T(8,128)(2,1)S(1)}, u32[]{:S(2)}, u32[]{:S(2)}) %collective-permute-start.32) | collective-permute-done | bytes 229408 | tf_op jit(solution)/shard_map/ppermute | solution.py:405
  113.1 0.6 collective-permute-start.35
  113.8 1.5 %collective-permute-start.37 = (bf16[32,3584]{1,0:T(8,128)(2,1)S(1)}, bf16[32,3584]{1,0:T(8,128)(2,1)S(1)}, u32[]{:S(2)}, u32[]{:S(2)}) collective-permute-start(bf16[32,3584]{1,0:T(8,128)(2,1)S(1)} %add_convert_fusion.1), channel_id=1, source_target_pairs={{0,2},{1,3},{4,0},{5,1},{8,4},{9,5},{12,8},{13,9},{14,12},{15,13},... | collective-permute-start | bytes 688136 | tf_op jit(solution)/shard_map/ppermute | solution.py:405
  115.3 4.3 %collective-permute-done.35 = bf16[32,3584]{1,0:T(8,128)(2,1)S(1)} collective-permute-done((bf16[32,3584]{1,0:T(8,128)(2,1)S(1)}, bf16[32,3584]{1,0:T(8,128)(2,1)S(1)}, u32[]{:S(2)}, u32[]{:S(2)}) %collective-permute-start.35) | collective-permute-done | bytes 229408 | tf_op jit(solution)/shard_map/ppermute | solution.py:405
  120.0 0.8 fusion.29
  (116 shorter events, 7.4 us)
Async XLA Ops:
  0.0 20.7 %collective-permute-start.4 = (bf16[32,3584]{1,0:T(8,128)(2,1)}, bf16[32,3584]{1,0:T(8,128)(2,1)}, u32[]{:S(2)}, u32[]{:S(2)}) collective-permute-start(bf16[32,3584]{1,0:T(8,128)(2,1)} %bitcast.36), channel_id=1, source_target_pairs={{0,1},{1,0},{2,3},{3,2},{4,5},{5,4},{6,7},{7,6},{8,9},{9,8},{10,11... | collective-permute-start | bytes 688136 | tf_op jit(solution)/shard_map/ppermute | solution.py:405
  0.5 16.6 %collective-permute-start.1 = (bf16[32,3584]{1,0:T(8,128)(2,1)}, bf16[32,3584]{1,0:T(8,128)(2,1)}, u32[]{:S(2)}, u32[]{:S(2)}) collective-permute-start(bf16[32,3584]{1,0:T(8,128)(2,1)} %bitcast.37), channel_id=1, source_target_pairs={{0,2},{1,3},{4,0},{5,1},{8,4},{9,5},{12,8},{13,9},{14,12},{15,13},... | collective-permute-start | bytes 688136 | tf_op jit(solution)/shard_map/ppermute | solution.py:405
  3.0 14.1 %collective-permute-start = (bf16[32,3584]{1,0:T(8,128)(2,1)}, bf16[32,3584]{1,0:T(8,128)(2,1)}, u32[]{:S(2)}, u32[]{:S(2)}) collective-permute-start(bf16[32,3584]{1,0:T(8,128)(2,1)} %bitcast.38), channel_id=1, source_target_pairs={{0,4},{1,5},{4,8},{5,9},{8,12},{9,13},{12,14},{13,15},{14,10},{15,... | collective-permute-start | bytes 688136 | tf_op jit(solution)/shard_map/ppermute | solution.py:405
  5.4 26.8 %all-to-all-start = ((bf16[128,2,576]{2,1,0:T(2,128)(2,1)}), bf16[128,2,576]{2,1,0:T(2,128)(2,1)S(1)}, u32[]{:S(2)}, u32[]{:S(2)}) async-start(bf16[128,2,576]{2,1,0:T(2,128)(2,1)} %copy.37), calls=%async_computation | async-start | bytes 655360 | tf_op jit(solution)/shard_map/all_to_all | solution.py:416
  11.7 7.9 %copy-start.16 = (s32[4,8,8]{2,1,0:T(8,128)S(1)}, s32[4,8,8]{2,1,0:T(8,128)}, u32[]{:S(2)}) copy-start(s32[4,8,8]{2,1,0:T(8,128)} %param.20) | copy-start | bytes 3076
  11.8 8.0 %copy-start.18 = (s32[128]{0:T(128)S(1)}, s32[128]{0:T(128)}, u32[]{:S(2)}) copy-start(s32[128]{0:T(128)} %param.18) | copy-start | bytes 1540
  11.8 8.1 %copy-start.19 = (s32[128]{0:T(128)S(1)}, s32[128]{0:T(128)}, u32[]{:S(2)}) copy-start(s32[128]{0:T(128)} %param.17) | copy-start | bytes 1540
  11.8 8.2 %copy-start.17 = (bf16[3584]{0:T(1024)(128)(2,1)S(1)}, bf16[3584]{0:T(1024)(128)(2,1)}, u32[]{:S(2)}) copy-start(bf16[3584]{0:T(1024)(128)(2,1)} %param.22) | copy-start | bytes 21508
  11.8 8.2 %copy-start.13 = (bf16[4,8,576]{2,1,0:T(8,128)(2,1)S(1)}, bf16[4,8,576]{2,1,0:T(8,128)(2,1)}, u32[]{:S(2)}) copy-start(bf16[4,8,576]{2,1,0:T(8,128)(2,1)} %param.15) | copy-start | bytes 110596
  17.1 22.0 %collective-permute-start.7 = (bf16[32,3584]{1,0:T(8,128)(2,1)}, bf16[32,3584]{1,0:T(8,128)(2,1)}, u32[]{:S(2)}, u32[]{:S(2)}) collective-permute-start(bf16[32,3584]{1,0:T(8,128)(2,1)} %collective-permute-done.refs_13_), channel_id=1, source_target_pairs={{0,1},{1,0},{2,3},{3,2},{4,5},{5,4},{6,7},{7,6},{8,9},{9,8},{10,11... | collective-permute-start | bytes 688136 | tf_op jit(solution)/shard_map/ppermute | solution.py:405
  17.6 8.8 %collective-permute-start.2 = (bf16[32,3584]{1,0:T(8,128)(2,1)}, bf16[32,3584]{1,0:T(8,128)(2,1)}, u32[]{:S(2)}, u32[]{:S(2)}) collective-permute-start(bf16[32,3584]{1,0:T(8,128)(2,1)} %collective-permute-done.refs_13_), channel_id=1, source_target_pairs={{0,4},{1,5},{4,8},{5,9},{8,12},{9,13},{12,14},{13,15},{14,10},{15,... | collective-permute-start | bytes 688136 | tf_op jit(solution)/shard_map/ppermute | solution.py:405
  19.2 19.9 %collective-permute-start.8 = (bf16[32,3584]{1,0:T(8,128)(2,1)}, bf16[32,3584]{1,0:T(8,128)(2,1)}, u32[]{:S(2)}, u32[]{:S(2)}) collective-permute-start(bf16[32,3584]{1,0:T(8,128)(2,1)} %collective-permute-done.1.refs_12_), channel_id=1, source_target_pairs={{0,1},{1,0},{2,3},{3,2},{4,5},{5,4},{6,7},{7,6},{8,9},{9,8},{10,11... | collective-permute-start | bytes 688136 | tf_op jit(solution)/shard_map/ppermute | solution.py:405
  19.3 8.3 %collective-permute-start.3 = (bf16[32,3584]{1,0:T(8,128)(2,1)}, bf16[32,3584]{1,0:T(8,128)(2,1)}, u32[]{:S(2)}, u32[]{:S(2)}) collective-permute-start(bf16[32,3584]{1,0:T(8,128)(2,1)} %collective-permute-done.1.refs_12_), channel_id=1, source_target_pairs={{0,2},{1,3},{4,0},{5,1},{8,4},{9,5},{12,8},{13,9},{14,12},{15,13},... | collective-permute-start | bytes 688136 | tf_op jit(solution)/shard_map/ppermute | solution.py:405
  27.6 11.6 %collective-permute-start.5 = (bf16[32,3584]{1,0:T(8,128)(2,1)}, bf16[32,3584]{1,0:T(8,128)(2,1)S(1)}, u32[]{:S(2)}, u32[]{:S(2)}) collective-permute-start(bf16[32,3584]{1,0:T(8,128)(2,1)} %collective-permute-done.2.refs_15_), channel_id=1, source_target_pairs={{0,4},{1,5},{4,8},{5,9},{8,12},{9,13},{12,14},{13,15},{14,10},{15,... | collective-permute-start | bytes 688136 | tf_op jit(solution)/shard_map/ppermute | solution.py:405
  29.0 10.1 %collective-permute-start.6 = (bf16[32,3584]{1,0:T(8,128)(2,1)}, bf16[32,3584]{1,0:T(8,128)(2,1)}, u32[]{:S(2)}, u32[]{:S(2)}) collective-permute-start(bf16[32,3584]{1,0:T(8,128)(2,1)} %collective-permute-done.3.refs_14_), channel_id=1, source_target_pairs={{0,2},{1,3},{4,0},{5,1},{8,4},{9,5},{12,8},{13,9},{14,12},{15,13},... | collective-permute-start | bytes 688136 | tf_op jit(solution)/shard_map/ppermute | solution.py:405
  32.6 4.5 %copy-start.15 = (f32[4,8,64]{2,0,1:T(4,128)S(1)}, f32[4,8,64]{2,0,1:T(4,128)}, u32[]{:S(2)}) copy-start(f32[4,8,64]{2,0,1:T(4,128)} %get-tuple-element.173) | copy-start | bytes 24580
  37.2 23.5 %copy-start.2 = (bf16[3584,16]{0,1:T(8,128)(2,1)S(1)}, bf16[3584,16]{0,1:T(8,128)(2,1)}, u32[]{:S(2)}) copy-start(bf16[3584,16]{0,1:T(8,128)(2,1)} %param.23) | copy-start | bytes 344068
  39.2 20.8 %copy-start.3 = (bf16[32,3584]{1,0:T(8,128)(2,1)}, bf16[32,3584]{1,0:T(8,128)(2,1)S(1)}, u32[]{:S(2)}) copy-start(bf16[32,3584]{1,0:T(8,128)(2,1)S(1)} %collective-permute-done.5.refs_7_) | copy-start | bytes 688132
  39.2 6.8 %collective-permute-start.11 = (bf16[32,640]{1,0:T(8,128)(2,1)S(1)}, bf16[32,640]{1,0:T(8,128)(2,1)S(1)}, u32[]{:S(2)}, u32[]{:S(2)}) collective-permute-start(bf16[32,640]{1,0:T(8,128)(2,1)S(1)} %bitcast.40), channel_id=1, source_target_pairs={{0,4},{1,5},{2,6},{3,7},{4,8},{5,9},{6,10},{7,11},{8,12},{9,13},{1... | collective-permute-start | bytes 122888 | tf_op jit(solution)/shard_map/ppermute | solution.py:405
  40.7 5.9 %collective-permute-start.10 = (bf16[32,640]{1,0:T(8,128)(2,1)S(1)}, bf16[32,640]{1,0:T(8,128)(2,1)S(1)}, u32[]{:S(2)}, u32[]{:S(2)}) collective-permute-start(bf16[32,640]{1,0:T(8,128)(2,1)S(1)} %bitcast.41), channel_id=1, source_target_pairs={{0,8},{1,9},{2,10},{3,11},{4,12},{5,13},{6,14},{7,15},{8,0},{9,1},... | collective-permute-start | bytes 122888 | tf_op jit(solution)/shard_map/ppermute | solution.py:405
  43.1 5.0 %collective-permute-start.9 = (bf16[32,640]{1,0:T(8,128)(2,1)S(1)}, bf16[32,640]{1,0:T(8,128)(2,1)S(1)}, u32[]{:S(2)}, u32[]{:S(2)}) collective-permute-start(bf16[32,640]{1,0:T(8,128)(2,1)S(1)} %bitcast.42), channel_id=1, source_target_pairs={{0,12},{1,13},{2,14},{3,15},{4,0},{5,1},{6,2},{7,3},{8,4},{9,5},{1... | collective-permute-start | bytes 122888 | tf_op jit(solution)/shard_map/ppermute | solution.py:405
  44.5 13.3 %collective-permute-start.15 = (bf16[32,3584]{1,0:T(8,128)(2,1)S(1)}, bf16[32,3584]{1,0:T(8,128)(2,1)S(1)}, u32[]{:S(2)}, u32[]{:S(2)}) collective-permute-start(bf16[32,3584]{1,0:T(8,128)(2,1)S(1)} %collective-permute-done.5.refs_7_), channel_id=1, source_target_pairs={{0,1},{1,0},{2,3},{3,2},{4,5},{5,4},{6,7},{7,6},{8,9},{9,8},{10,11... | collective-permute-start | bytes 688136 | tf_op jit(solution)/shard_map/ppermute | solution.py:405
  45.5 12.4 %collective-permute-start.18 = (bf16[32,3584]{1,0:T(8,128)(2,1)}, bf16[32,3584]{1,0:T(8,128)(2,1)S(1)}, u32[]{:S(2)}, u32[]{:S(2)}) collective-permute-start(bf16[32,3584]{1,0:T(8,128)(2,1)} %collective-permute-done.6.refs_6_), channel_id=1, source_target_pairs={{0,1},{1,0},{2,3},{3,2},{4,5},{5,4},{6,7},{7,6},{8,9},{9,8},{10,11... | collective-permute-start | bytes 688136 | tf_op jit(solution)/shard_map/ppermute | solution.py:405
  46.0 5.1 %collective-permute-start.14 = (bf16[16,3584]{1,0:T(8,128)(2,1)S(1)}, bf16[16,3584]{1,0:T(8,128)(2,1)S(1)}, u32[]{:S(2)}, u32[]{:S(2)}) collective-permute-start(bf16[16,3584]{1,0:T(8,128)(2,1)S(1)} %slice.35), channel_id=1, source_target_pairs={{0,2},{1,3},{4,0},{5,1},{8,4},{9,5},{12,8},{13,9},{14,12},{15,13},... | collective-permute-start | bytes 344072 | tf_op jit(solution)/shard_map/ppermute | solution.py:405
  46.6 4.8 %collective-permute-start.13 = (bf16[16,3584]{1,0:T(8,128)(2,1)S(1)}, bf16[16,3584]{1,0:T(8,128)(2,1)S(1)}, u32[]{:S(2)}, u32[]{:S(2)}) collective-permute-start(bf16[16,3584]{1,0:T(8,128)(2,1)S(1)} %slice.34), channel_id=1, source_target_pairs={{0,4},{1,5},{4,8},{5,9},{8,12},{9,13},{12,14},{13,15},{14,10},{15,... | collective-permute-start | bytes 344072 | tf_op jit(solution)/shard_map/ppermute | solution.py:405
  48.1 9.8 %collective-permute-start.16 = (bf16[32,3584]{1,0:T(8,128)(2,1)}, bf16[32,3584]{1,0:T(8,128)(2,1)S(1)}, u32[]{:S(2)}, u32[]{:S(2)}) collective-permute-start(bf16[32,3584]{1,0:T(8,128)(2,1)} %collective-permute-done.2.refs_15_), channel_id=1, source_target_pairs={{0,1},{1,0},{2,3},{3,2},{4,5},{5,4},{6,7},{7,6},{8,9},{9,8},{10,11... | collective-permute-start | bytes 688136 | tf_op jit(solution)/shard_map/ppermute | solution.py:405
  51.2 6.7 %collective-permute-start.17 = (bf16[32,3584]{1,0:T(8,128)(2,1)}, bf16[32,3584]{1,0:T(8,128)(2,1)S(1)}, u32[]{:S(2)}, u32[]{:S(2)}) collective-permute-start(bf16[32,3584]{1,0:T(8,128)(2,1)} %collective-permute-done.3.refs_14_), channel_id=1, source_target_pairs={{0,1},{1,0},{2,3},{3,2},{4,5},{5,4},{6,7},{7,6},{8,9},{9,8},{10,11... | collective-permute-start | bytes 688136 | tf_op jit(solution)/shard_map/ppermute | solution.py:405
  51.4 6.4 %collective-permute-start.12 = (bf16[128,640]{1,0:T(8,128)(2,1)S(1)}, bf16[128,640]{1,0:T(8,128)(2,1)S(1)}, u32[]{:S(2)}, u32[]{:S(2)}) collective-permute-start(bf16[128,640]{1,0:T(8,128)(2,1)S(1)} %constant_dynamic-update-slice_fusion.refs_1_), channel_id=1, source_target_pairs={{0,2},{1,3},{2,0},{3,1},{4,6},{5,7},{6,4},{7,5},{8,10},{9,11},{10,... | collective-permute-start | bytes 491528 | tf_op jit(solution)/shard_map/ppermute | solution.py:405
  58.0 2.0 %collective-permute-start.21 = (bf16[32,3584]{1,0:T(8,128)(2,1)S(1)}, bf16[32,3584]{1,0:T(8,128)(2,1)S(1)}, u32[]{:S(2)}, u32[]{:S(2)}) collective-permute-start(bf16[32,3584]{1,0:T(8,128)(2,1)S(1)} %constant_dynamic-update-slice_fusion.4.refs_5_), channel_id=1, source_target_pairs={{0,1},{1,0},{2,3},{3,2},{4,5},{5,4},{6,7},{7,6},{8,9},{9,8},{10,11... | collective-permute-start | bytes 688136 | tf_op jit(solution)/shard_map/ppermute | solution.py:405
  58.0 1.7 %collective-permute-start.19 = (bf16[128,640]{1,0:T(8,128)(2,1)S(1)}, bf16[128,640]{1,0:T(8,128)(2,1)S(1)}, u32[]{:S(2)}, u32[]{:S(2)}) collective-permute-start(bf16[128,640]{1,0:T(8,128)(2,1)S(1)} %constant_dynamic-update-slice_fusion.refs_1_), channel_id=1, source_target_pairs={{0,1},{1,0},{2,3},{3,2},{4,5},{5,4},{6,7},{7,6},{8,9},{9,8},{10,11... | collective-permute-start | bytes 491528 | tf_op jit(solution)/shard_map/ppermute | solution.py:405
  58.5 1.4 %collective-permute-start.20 = (bf16[128,640]{1,0:T(8,128)(2,1)S(1)}, bf16[128,640]{1,0:T(8,128)(2,1)S(1)}, u32[]{:S(2)}, u32[]{:S(2)}) collective-permute-start(bf16[128,640]{1,0:T(8,128)(2,1)S(1)} %collective-permute-done.12.refs_2_), channel_id=1, source_target_pairs={{0,1},{1,0},{2,3},{3,2},{4,5},{5,4},{6,7},{7,6},{8,9},{9,8},{10,11... | collective-permute-start | bytes 491528 | tf_op jit(solution)/shard_map/ppermute | solution.py:405
  79.1 1.8 %collective-permute-start.22 = (bf16[32,3584]{1,0:T(8,128)(2,1)}, bf16[32,3584]{1,0:T(8,128)(2,1)S(1)}, u32[]{:S(2)}, u32[]{:S(2)}) collective-permute-start(bf16[32,3584]{1,0:T(8,128)(2,1)} %get-tuple-element.128), channel_id=1, source_target_pairs={{0,1},{1,0},{2,3},{3,2},{4,5},{5,4},{6,7},{7,6},{8,9},{9,8},{10,11... | collective-permute-start | bytes 688136 | tf_op jit(solution)/shard_map/ppermute | solution.py:405
  79.3 1.9 %collective-permute-start.23 = (bf16[32,3584]{1,0:T(8,128)(2,1)}, bf16[32,3584]{1,0:T(8,128)(2,1)S(1)}, u32[]{:S(2)}, u32[]{:S(2)}) collective-permute-start(bf16[32,3584]{1,0:T(8,128)(2,1)} %get-tuple-element.129), channel_id=1, source_target_pairs={{0,1},{1,0},{2,3},{3,2},{4,5},{5,4},{6,7},{7,6},{8,9},{9,8},{10,11... | collective-permute-start | bytes 688136 | tf_op jit(solution)/shard_map/ppermute | solution.py:405
  79.7 1.8 %collective-permute-start.24 = (bf16[32,3584]{1,0:T(8,128)(2,1)}, bf16[32,3584]{1,0:T(8,128)(2,1)S(1)}, u32[]{:S(2)}, u32[]{:S(2)}) collective-permute-start(bf16[32,3584]{1,0:T(8,128)(2,1)} %get-tuple-element.130), channel_id=1, source_target_pairs={{0,1},{1,0},{2,3},{3,2},{4,5},{5,4},{6,7},{7,6},{8,9},{9,8},{10,11... | collective-permute-start | bytes 688136 | tf_op jit(solution)/shard_map/ppermute | solution.py:405
  81.6 12.2 %collective-permute-start.26 = (bf16[16,3584]{1,0:T(8,128)(2,1)S(1)}, bf16[16,3584]{1,0:T(8,128)(2,1)S(1)}, u32[]{:S(2)}, u32[]{:S(2)}) collective-permute-start(bf16[16,3584]{1,0:T(8,128)(2,1)S(1)} %get-tuple-element.169), channel_id=1, source_target_pairs={{0,2},{1,3},{4,0},{5,1},{8,4},{9,5},{12,8},{13,9},{14,12},{15,13},... | collective-permute-start | bytes 344072 | tf_op jit(solution)/shard_map/ppermute | solution.py:405
  82.2 11.6 %collective-permute-start.25 = (bf16[16,3584]{1,0:T(8,128)(2,1)S(1)}, bf16[16,3584]{1,0:T(8,128)(2,1)S(1)}, u32[]{:S(2)}, u32[]{:S(2)}) collective-permute-start(bf16[16,3584]{1,0:T(8,128)(2,1)S(1)} %get-tuple-element.170), channel_id=1, source_target_pairs={{0,4},{1,5},{4,8},{5,9},{8,12},{9,13},{12,14},{13,15},{14,10},{15,... | collective-permute-start | bytes 344072 | tf_op jit(solution)/shard_map/ppermute | solution.py:405
  93.8 9.1 %collective-permute-start.27 = (bf16[32,3584]{1,0:T(8,128)(2,1)S(1)}, bf16[32,3584]{1,0:T(8,128)(2,1)S(1)}, u32[]{:S(2)}, u32[]{:S(2)}) collective-permute-start(bf16[32,3584]{1,0:T(8,128)(2,1)S(1)} %add_convert_fusion.6), channel_id=1, source_target_pairs={{0,4},{1,5},{4,8},{5,9},{8,12},{9,13},{12,14},{13,15},{14,10},{15,... | collective-permute-start | bytes 688136 | tf_op jit(solution)/shard_map/ppermute | solution.py:405
  94.5 8.4 %collective-permute-start.28 = (bf16[32,3584]{1,0:T(8,128)(2,1)S(1)}, bf16[32,3584]{1,0:T(8,128)(2,1)S(1)}, u32[]{:S(2)}, u32[]{:S(2)}) collective-permute-start(bf16[32,3584]{1,0:T(8,128)(2,1)S(1)} %add_convert_fusion.5), channel_id=1, source_target_pairs={{0,2},{1,3},{4,0},{5,1},{8,4},{9,5},{12,8},{13,9},{14,12},{15,13},... | collective-permute-start | bytes 688136 | tf_op jit(solution)/shard_map/ppermute | solution.py:405
  102.9 17.1 %copy-start.5 = (f32[32,3584]{1,0:T(8,128)S(1)}, f32[32,3584]{1,0:T(8,128)}, u32[]{:S(2)}) copy-start(f32[32,3584]{1,0:T(8,128)} %get-tuple-element.126) | copy-start | bytes 1376260
  103.0 1.8 %collective-permute-start.31 = (bf16[32,3584]{1,0:T(8,128)(2,1)}, bf16[32,3584]{1,0:T(8,128)(2,1)S(1)}, u32[]{:S(2)}, u32[]{:S(2)}) collective-permute-start(bf16[32,3584]{1,0:T(8,128)(2,1)} %get-tuple-element.158), channel_id=1, source_target_pairs={{0,1},{1,0},{2,3},{3,2},{4,5},{5,4},{6,7},{7,6},{8,9},{9,8},{10,11... | collective-permute-start | bytes 688136 | tf_op jit(solution)/shard_map/ppermute | solution.py:405
  103.1 2.4 %collective-permute-start.33 = (bf16[32,3584]{1,0:T(8,128)(2,1)}, bf16[32,3584]{1,0:T(8,128)(2,1)S(1)}, u32[]{:S(2)}, u32[]{:S(2)}) collective-permute-start(bf16[32,3584]{1,0:T(8,128)(2,1)} %get-tuple-element.161), channel_id=1, source_target_pairs={{0,1},{1,0},{2,3},{3,2},{4,5},{5,4},{6,7},{7,6},{8,9},{9,8},{10,11... | collective-permute-start | bytes 688136 | tf_op jit(solution)/shard_map/ppermute | solution.py:405
  104.8 7.7 %collective-permute-start.32 = (bf16[32,3584]{1,0:T(8,128)(2,1)S(1)}, bf16[32,3584]{1,0:T(8,128)(2,1)S(1)}, u32[]{:S(2)}, u32[]{:S(2)}) collective-permute-start(bf16[32,3584]{1,0:T(8,128)(2,1)S(1)} %add_convert_fusion.4), channel_id=1, source_target_pairs={{0,4},{1,5},{4,8},{5,9},{8,12},{9,13},{12,14},{13,15},{14,10},{15,... | collective-permute-start | bytes 688136 | tf_op jit(solution)/shard_map/ppermute | solution.py:405
  105.5 7.4 %collective-permute-start.34 = (bf16[32,3584]{1,0:T(8,128)(2,1)S(1)}, bf16[32,3584]{1,0:T(8,128)(2,1)S(1)}, u32[]{:S(2)}, u32[]{:S(2)}) collective-permute-start(bf16[32,3584]{1,0:T(8,128)(2,1)S(1)} %add_convert_fusion.3), channel_id=1, source_target_pairs={{0,2},{1,3},{4,0},{5,1},{8,4},{9,5},{12,8},{13,9},{14,12},{15,13},... | collective-permute-start | bytes 688136 | tf_op jit(solution)/shard_map/ppermute | solution.py:405
  107.1 5.9 %collective-permute-start.30 = (bf16[32,3584]{1,0:T(8,128)(2,1)S(1)}, bf16[32,3584]{1,0:T(8,128)(2,1)S(1)}, u32[]{:S(2)}, u32[]{:S(2)}) collective-permute-start(bf16[32,3584]{1,0:T(8,128)(2,1)S(1)} %get-tuple-element.156), channel_id=1, source_target_pairs={{0,1},{1,0},{2,3},{3,2},{4,5},{5,4},{6,7},{7,6},{8,9},{9,8},{10,11... | collective-permute-start | bytes 688136 | tf_op jit(solution)/shard_map/ppermute | solution.py:405
  107.1 6.6 %collective-permute-start.36 = (bf16[32,3584]{1,0:T(8,128)(2,1)S(1)}, bf16[32,3584]{1,0:T(8,128)(2,1)S(1)}, u32[]{:S(2)}, u32[]{:S(2)}) collective-permute-start(bf16[32,3584]{1,0:T(8,128)(2,1)S(1)} %get-tuple-element.165), channel_id=1, source_target_pairs={{0,1},{1,0},{2,3},{3,2},{4,5},{5,4},{6,7},{7,6},{8,9},{9,8},{10,11... | collective-permute-start | bytes 688136 | tf_op jit(solution)/shard_map/ppermute | solution.py:405
  113.1 6.5 %collective-permute-start.35 = (bf16[32,3584]{1,0:T(8,128)(2,1)S(1)}, bf16[32,3584]{1,0:T(8,128)(2,1)S(1)}, u32[]{:S(2)}, u32[]{:S(2)}) collective-permute-start(bf16[32,3584]{1,0:T(8,128)(2,1)S(1)} %add_convert_fusion.2), channel_id=1, source_target_pairs={{0,4},{1,5},{4,8},{5,9},{8,12},{9,13},{12,14},{13,15},{14,10},{15,... | collective-permute-start | bytes 688136 | tf_op jit(solution)/shard_map/ppermute | solution.py:405
  113.8 6.3 %collective-permute-start.37 = (bf16[32,3584]{1,0:T(8,128)(2,1)S(1)}, bf16[32,3584]{1,0:T(8,128)(2,1)S(1)}, u32[]{:S(2)}, u32[]{:S(2)}) collective-permute-start(bf16[32,3584]{1,0:T(8,128)(2,1)S(1)} %add_convert_fusion.1), channel_id=1, source_target_pairs={{0,2},{1,3},{4,0},{5,1},{8,4},{9,5},{12,8},{13,9},{14,12},{15,13},... | collective-permute-start | bytes 688136 | tf_op jit(solution)/shard_map/ppermute | solution.py:405
  115.3 4.8 %collective-permute-start.29 = (bf16[32,3584]{1,0:T(8,128)(2,1)S(1)}, bf16[32,3584]{1,0:T(8,128)(2,1)S(1)}, u32[]{:S(2)}, u32[]{:S(2)}) collective-permute-start(bf16[32,3584]{1,0:T(8,128)(2,1)S(1)} %get-tuple-element.154), channel_id=1, source_target_pairs={{0,1},{1,0},{2,3},{3,2},{4,5},{5,4},{6,7},{7,6},{8,9},{9,8},{10,11... | collective-permute-start | bytes 688136 | tf_op jit(solution)/shard_map/ppermute | solution.py:405
  (11 other events, 27.5 us)

commit v5 on v4

v5 whole, which is shorter than its diff:
```python
import jax
import jax.numpy as jnp
from jax import lax
from jax.experimental import pallas as pl
from jax.experimental.pallas import tpu as pltpu
from jax.sharding import PartitionSpec as P

qk_scale = 192.0 ** (-0.5)
LANES = 128


def ring_of(chips):
    return list(range(0, chips, 2)) + list(range(chips - 1, 0, -2))


def shift_perm(chips, by):
    ring = ring_of(chips)
    return [
        (2 * ring[p] + core, 2 * ring[(p + by) % chips] + core)
        for p in range(chips)
        for core in range(2)
    ]


def sibling_perm(chips):
    return [(d, d ^ 1) for d in range(2 * chips)]


def distances(chips):
    half = chips // 2
    return [0] + [d for t in range(1, half) for d in (t, -t)] + [half]


def gather_steps(chips):
    high = 4 if chips % 4 == 0 else 2
    return high, chips // high


def step_perm(chips, by_high, by_low):
    high, low = gather_steps(chips)
    return [
        (
            2 * (h * low + l) + core,
            2 * ((h - by_high) % high * low + (l - by_low) % low) + core,
        )
        for h in range(high)
        for l in range(low)
        for core in range(2)
    ]


def gathered_place(chips):
    high, low = gather_steps(chips)
    ring = ring_of(chips)
    table = [[] for _ in range(chips)]
    for p, chip in enumerate(ring):
        for side in (0, chips):
            for d in distances(chips):
                other = ring[(p + d) % chips]
                by_high = (other // low - chip // low) % high
                by_low = (other % low - chip % low) % low
                table[chip].append(side + by_low * high + by_high)
    return table


def tile_of(size, most):
    return max(t for t in range(LANES, min(size, most) + 1, LANES) if size % t == 0)


def scoped(need):
    return max(52 << 20, (int(need) // (1 << 20) + 5) << 20)


def expert_kernel(blocks, rows, latent, width, gate_tile, *refs):
    scalars = refs[0]
    pooled = refs[1:5]
    resid = refs[5 : 5 + blocks]
    w_out, gain, w_router, w_gate, w_up, w_down = refs[5 + blocks : 11 + blocks]
    hidden = refs[11 + blocks]
    outs = refs[12 + blocks : 12 + 2 * blocks]
    raw, joined, ssq, logits, scale, weight, x, act, wg, wu, wd, sems = refs[12 + 2 * blocks :]
    step = pl.program_id(0)
    cols = w_out.shape[1]
    tiles = width // cols
    total = blocks * rows
    experts_all = w_router.shape[0]
    units = act.shape[1]
    chunk = min(512, total)
    gate_steps = units // gate_tile

    def rows_of(source, target, pieces, first):
        height = source.shape[1] // pieces
        return [
            pltpu.make_async_copy(
                source.at[0, k * height : (k + 1) * height, :],
                target.at[k * height : (k + 1) * height, :],
                sems.at[first + k],
            )
            for k in range(pieces)
        ]

    gates, ups, downs = rows_of(w_gate, wg, 4, 0), rows_of(w_up, wu, 4, 4), rows_of(w_down, wd, 4, 8)
    queue = [c for pair in zip(gates, ups) for c in pair] + downs
    for j, copy in enumerate(queue):
        pl.when(step == min(j // 2, tiles - 1))(copy.start)

    @pl.when(step == 0)
    def _():
        start = 0
        for piece in pooled:
            raw[start : start + piece.shape[0], :] = piece[...]
            start += piece.shape[0]
        for b in range(blocks):
            place = pl.ds(pl.multiple_of(scalars[1 + b] * rows, rows), rows)
            joined[b * rows : (b + 1) * rows, :] = raw[place, :]
        ssq[...] = jnp.zeros_like(ssq)
        logits[...] = jnp.zeros_like(logits)

    @pl.when(step < tiles)
    def _():
        g = gain[...].astype(jnp.float32)
        here = pl.ds(pl.multiple_of(step * cols, cols), cols)
        for c in range(0, total, chunk):
            end = min(c + chunk, total)
            proj = jnp.dot(joined[c:end, :latent], w_out[...], preferred_element_type=jnp.float32)
            for b in range(c // rows, end // rows):
                at = slice(b * rows, (b + 1) * rows)
                h = proj[b * rows - c : (b + 1) * rows - c] + resid[b][...].astype(jnp.float32)
                if b == 0:
                    hidden[...] = h
                x[at, here] = (h * g).astype(jnp.bfloat16)
                sq = h * h
                part = sq[:, :LANES]
                for k in range(1, cols // LANES):
                    part = part + sq[:, k * LANES : (k + 1) * LANES]
                ssq[at, :] += part
            logits[c:end, :] += lax.dot_general(
                x[c:end, here],
                w_router[...],
                (((1,), (1,)), ((), ())),
                preferred_element_type=jnp.float32,
            )

    @pl.when(step == tiles)
    def _():
        mean = jnp.sum(ssq[...], axis=1, keepdims=True) * (1.0 / width)
        r = lax.rsqrt(mean + 1e-06)
        mask = joined[:, latent : latent + experts_all].astype(jnp.float32)
        affinity = jax.nn.sigmoid(logits[...] * r) * mask
        lane = lax.broadcasted_iota(jnp.int32, affinity.shape, 1)
        mine = jnp.sum(jnp.where(lane == scalars[0], affinity, 0.0), axis=1, keepdims=True)
        gate = 2.5 * mine / jnp.sum(affinity, axis=1, keepdims=True)
        scale[...] = jnp.broadcast_to(r, scale.shape)
        weight[...] = jnp.broadcast_to(gate, weight.shape)
        for copy in gates + ups:
            copy.wait()

    @pl.when((step >= tiles) & (step < tiles + gate_steps))
    def _():
        part = pl.ds(pl.multiple_of((step - tiles) * gate_tile, gate_tile), gate_tile)
        for c in range(0, total, chunk):
            at = slice(c, min(c + chunk, total))
            r = scale[at, :1]
            a = jnp.dot(x[at, :], wg[:, part], preferred_element_type=jnp.float32) * r
            b = jnp.dot(x[at, :], wu[:, part], preferred_element_type=jnp.float32) * r
            act[at, part] = (jax.nn.silu(a) * b * weight[at, :1]).astype(jnp.bfloat16)

    @pl.when(step == tiles + gate_steps)
    def _():
        for copy in downs:
            copy.wait()

    @pl.when(step >= tiles + gate_steps)
    def _():
        here = pl.ds(pl.multiple_of((step - tiles - gate_steps) * cols, cols), cols)
        for c in range(0, total, chunk):
            end = min(c + chunk, total)
            y = jnp.dot(act[c:end, :], wd[:, here], preferred_element_type=jnp.float32)
            for b in range(c // rows, end // rows):
                outs[b][...] = y[b * rows - c : (b + 1) * rows - c].astype(jnp.bfloat16)


def experts(scalars, pooled, resid_blocks, w_out, gain, w_router_t, wg, wu, wd):
    blocks = len(resid_blocks)
    rows, width = resid_blocks[0].shape
    latent = w_out.shape[0]
    total = blocks * rows
    cols = tile_of(width, 512)
    tile_count = width // cols
    packed = pooled[0].shape[1]
    experts_all = w_router_t.shape[0]
    units = wg.shape[2]
    gate_tile = tile_of(units, 512)
    gate_steps = units // gate_tile

    def whole(shape):
        return pl.BlockSpec(shape, lambda i: (0, 0), pipeline_mode=pl.Buffered(1))

    def tiles(height):
        return pl.BlockSpec((height, cols), lambda i: (0, jnp.minimum(i, tile_count - 1)))

    out_tiles = pl.BlockSpec(
        (rows, cols), lambda i: (0, jnp.clip(i - tile_count - gate_steps, 0, tile_count - 1))
    )
    in_hbm = pl.BlockSpec(memory_space=pltpu.HBM)
    need = total * (2 * width + 2 * units + cols * 20 + packed * 6 + 8 * LANES * 4)
    need = need + 4 * latent * cols + 6 * width * units
    results = pl.pallas_call(
        lambda *refs: expert_kernel(blocks, rows, latent, width, gate_tile, *refs),
        grid=(2 * tile_count + gate_steps,),
        in_specs=[pl.BlockSpec(memory_space=pltpu.SMEM)]
        + [whole(a.shape) for a in pooled]
        + [tiles(rows)] * blocks
        + [tiles(latent), tiles(1), tiles(experts_all)]
        + [in_hbm] * 3,
        out_shape=[jax.ShapeDtypeStruct((rows, width), jnp.float32)]
        + [jax.ShapeDtypeStruct((rows, width), jnp.bfloat16)] * blocks,
        out_specs=[tiles(rows)] + [out_tiles] * blocks,
        scratch_shapes=[
            pltpu.VMEM((total, packed), jnp.bfloat16),
            pltpu.VMEM((total, packed), jnp.bfloat16),
            pltpu.VMEM((total, LANES), jnp.float32),
            pltpu.VMEM((total, experts_all), jnp.float32),
            pltpu.VMEM((total, LANES), jnp.float32),
            pltpu.VMEM((total, LANES), jnp.float32),
            pltpu.VMEM((total, width), jnp.bfloat16),
            pltpu.VMEM((total, units), jnp.bfloat16),
            pltpu.VMEM((width, units), jnp.bfloat16),
            pltpu.VMEM((width, units), jnp.bfloat16),
            pltpu.VMEM((units, width), jnp.bfloat16),
            pltpu.SemaphoreType.DMA((12,)),
        ],
        compiler_params=pltpu.CompilerParams(
            dimension_semantics=("arbitrary",), vmem_limit_bytes=scoped(need)
        ),
        cost_estimate=pl.CostEstimate(
            flops=2 * total * width * (latent + 3 * units),
            bytes_accessed=2 * total * width * 2 + latent * width * 2 + 6 * width * units,
            transcendentals=total * units,
        ),
        name="experts",
    )(scalars, *pooled, *resid_blocks, w_out, gain, w_router_t, wg, wu, wd)
    return results[0], results[1 : 1 + blocks // 2], results[1 + blocks // 2 :]


def attention(queries, new_lat, owned_cache, row_lengths, latent):
    step_count, row_count, kv_width = new_lat.shape
    context = owned_cache.shape[1]
    cache_scores = (
        jnp.einsum("srhk,rpk->srhp", queries, owned_cache, preferred_element_type=jnp.float32)
        * qk_scale
    )
    visible = jnp.arange(context)[None, :] < row_lengths[:, None]
    cache_scores = jnp.where(visible[None, :, None, :], cache_scores, -1e30)
    fresh_scores = (
        jnp.einsum("srhk,trk->srht", queries, new_lat, preferred_element_type=jnp.float32)
        * qk_scale
    )
    causal = jnp.arange(step_count)[:, None] >= jnp.arange(step_count)[None, :]
    fresh_scores = jnp.where(causal[:, None, None, :], fresh_scores, -1e30)
    scores = jnp.concatenate([cache_scores, fresh_scores], axis=-1)
    weights = jax.nn.softmax(scores, axis=-1).astype(jnp.bfloat16)
    pooled = jnp.einsum(
        "srhp,rpl->srl",
        weights[..., :context],
        owned_cache[..., :latent],
        preferred_element_type=jnp.float32,
    )
    pooled = pooled + jnp.einsum(
        "srht,trl->srl",
        weights[..., context:],
        new_lat[..., :latent],
        preferred_element_type=jnp.float32,
    )
    return pooled.astype(jnp.bfloat16)


def local(
    q_abs,
    new_lat,
    latent_cache,
    lengths,
    owner,
    resid,
    routes,
    w_out,
    norm_gain,
    w_router,
    w_gate,
    w_up,
    w_down,
):
    devices = lax.axis_size("expert")
    device_index = lax.axis_index("expert")
    step_count, row_count, width = resid.shape
    rows = step_count * row_count
    experts_all = w_router.shape[1]
    sharers = devices // experts_all
    chips = devices // 2
    half = chips // 2
    cut = rows // 2
    order = distances(chips)
    hold = lax.optimization_barrier
    sibling = sibling_perm(chips)

    def send(a, perm):
        return lax.ppermute(a, "expert", perm)

    to_right, to_left = shift_perm(chips, 1), shift_perm(chips, -1)

    def around(to_the_right, to_the_left):
        return send(to_the_right, to_right), send(to_the_left, to_left)

    wanted = (owner[:, None] == jnp.arange(owner.shape[0], dtype=jnp.int32)).astype(jnp.bfloat16)
    ordered = jnp.einsum(
        "jr,rpk->jpk", wanted, latent_cache, preferred_element_type=jnp.float32
    ).astype(jnp.bfloat16)
    owned_cache = lax.all_to_all(ordered, "expert", split_axis=0, concat_axis=1, tiled=True)

    mine = resid.reshape(rows, width)
    held, sib = {0: mine}, {}
    held[-1], held[1] = around(mine, mine)
    owner, lengths, routes, norm_gain, new_lat, held[-1], held[1] = hold(
        (owner, lengths, routes, norm_gain, new_lat, held[-1], held[1])
    )
    held[-2], held[2] = around(held[-1], held[1])
    sib[0] = send(mine, sibling)
    row_owner = lax.dynamic_slice_in_dim(owner, device_index * row_count, row_count)
    row_lengths = jnp.sum(
        jnp.where(
            row_owner[:, None] == jnp.arange(owner.shape[0], dtype=jnp.int32), lengths[None, :], 0
        ),
        axis=1,
    )
    routed = jnp.any(routes[..., None] == jnp.arange(LANES, dtype=jnp.int32), axis=2)
    routed = routed.astype(jnp.bfloat16)
    gain = norm_gain[None, :]
    scalars = jnp.array(
        [
            [device // sharers] + places
            for chip, places in enumerate(gathered_place(chips))
            for device in (2 * chip, 2 * chip + 1)
        ],
        jnp.int32,
    )[device_index]
    queries = q_abs.reshape(step_count, row_count, -1, new_lat.shape[2])
    owned_cache, queries, row_lengths, routed, gain, scalars, held[-2], held[2], sib[0] = hold(
        (owned_cache, queries, row_lengths, routed, gain, scalars, held[-2], held[2], sib[0])
    )
    for t in range(3, half):
        held[-t], held[t] = around(held[1 - t], held[t - 1])
    sib[-1], sib[1] = send(held[-1], sibling), send(held[1], sibling)
    pooled = attention(queries, new_lat, owned_cache, row_lengths, w_out.shape[0])
    packet = jnp.concatenate([pooled, routed], axis=2).reshape(rows, -1)
    packet, held, sib = hold((packet, held, sib))

    last = around(held[1 - half][:cut], held[half - 1][cut:])
    for t in range(2, half):
        sib[-t], sib[t] = send(held[-t], sibling), send(held[t], sibling)
    high, low = gather_steps(chips)
    along, last = hold(([send(packet, step_perm(chips, i, 0)) for i in range(1, high)], last))
    along = jnp.concatenate([packet] + along, axis=0)
    across = [send(along, step_perm(chips, 0, i)) for i in range(1, low)]
    held[half] = jnp.concatenate(last, axis=0)
    sib[half] = send(held[half], sibling)
    across, sib = hold((across, sib))
    across = across[0] if low == 2 else jnp.concatenate(across, axis=0)

    hidden, to_own, to_sib = experts(
        scalars,
        [along, across, send(along, sibling), send(across, sibling)],
        [held[d] for d in order] + [sib[d] for d in order],
        w_out,
        gain,
        w_router.T,
        w_gate,
        w_up,
        w_down,
    )

    f32 = jnp.float32
    own = dict(zip(order, to_own))
    got = {d: send(a, sibling) for d, a in reversed(list(zip(order, to_sib)))}
    halves = (slice(0, cut), slice(cut, rows))

    parts = {}
    for d in reversed(order):
        sums = [own[d][h].astype(f32) + got[d][h].astype(f32) for h in halves]
        parts[d] = hold(sums) if d else sums

    right, left = {}, {}
    for t, which in [(half, 0)] + [(t, w) for t in range(half - 1, 0, -1) for w in (1, 0)]:
        other = 1 - which
        to_r, to_l = parts[t][which], parts[-t if t < half else t][other]
        if which in right:
            to_r, to_l = to_r + right[which].astype(f32), to_l + left[other].astype(f32)
        right[which], left[other] = hold(around(to_r.astype(jnp.bfloat16), to_l.astype(jnp.bfloat16)))
    mixed = [
        hidden[halves[w]] + parts[0][w] + right[w].astype(f32) + left[w].astype(f32) for w in range(2)
    ]
    mixed = jnp.concatenate(mixed, axis=0)
    return mixed.astype(jnp.bfloat16).reshape(step_count, row_count, width)


def solution(mesh):
    return jax.shard_map(
        local,
        mesh=mesh,
        in_specs=(
            P(None, ("group", "expert"), None),
            P(None, ("group", "expert"), None),
            P("group", "expert", None),
            P("group"),
            P("group"),
            P(None, ("group", "expert"), None),
            P(None, ("group", "expert"), None),
            P(),
            P(),
            P(),
            P("expert", None, None),
            P("expert", None, None),
            P("expert", None, None),
        ),
        out_specs=P(None, ("group", "expert"), None),
        check_vma=False,
    )
```

time: 121 us -> 121 us (level)
  waiting for transfers between devices: 30.5 us -> 39.9 us
  Pallas kernels: 34.3 us -> 26.5 us
  starting transfers between devices: 33.7 us -> 38.1 us
  local copies, waits for them, and re-layouts: 12.1 us -> 8.16 us
  matrix products: 6.38 us -> 4.16 us
    pallas_call x3 -> x1, Pallas kernels: 34.3 us -> 26.5 us  [experts(): pl.pallas_call(lambda *refs: expert_kernel(blocks, rows, latent, width, g...]
    ppermute x38 -> x44, waiting for transfers between devices: 30.5 us -> 37.1 us  [send(): return lax.ppermute(a, 'expert', perm)]
    ppermute x38 -> x44, starting transfers between devices: 27.4 us -> 31.8 us  [send(): return lax.ppermute(a, 'expert', perm)]
    all_to_all x1, waiting for transfers between devices: 0.01 us -> 2.8 us  [local(): lax.all_to_all(ordered, 'expert', split_axis=0, concat_axis=1, tiled=True)]
    unnamed x44 -> x42, local copies, waits for them, and re-layouts: 1.6 us -> 0.13 us
    add x0 -> x9, other arithmetic: none -> 1.32 us  [local(): sums = [own[d][h].astype(f32) + got[d][h].astype(f32) for h in halves]]
  transfers between devices with their start and end apart: 39 -> 45, of which waited for: 15 -> 24; matrix products, arithmetic and copies ran while one was open for 15% -> 12% of each run, Pallas kernels for 13% -> 0%
where the time goes in v5:
time: 121 us
  waiting for transfers between devices  39.9 us (33%)
  starting transfers between devices  38.1 us (31%)
  Pallas kernels  26.5 us (22%)
  local copies, waits for them, and re-layouts  8.16 us (7%)
  matrix products  4.16 us (3%)
  other arithmetic  3.52 us (3%)
    ppermute x44, waiting for transfers between devices, send(): return lax.ppermute(a, 'expert', perm)  37.1 us
    ppermute x44, starting transfers between devices, send(): return lax.ppermute(a, 'expert', perm)  31.8 us
    pallas_call x1, Pallas kernels, experts(): pl.pallas_call(lambda *refs: expert_kernel(blocks, rows, latent, width, g...  26.5 us
    all_to_all x1, starting transfers between devices, local(): lax.all_to_all(ordered, 'expert', split_axis=0, concat_axis=1, tiled=True)  6.3 us
    reshape x1, local copies, waits for them, and re-layouts, local(): queries = q_abs.reshape(step_count, row_count, -1, new_lat.shape[2])  4.56 us
    all_to_all x1, waiting for transfers between devices, local(): lax.all_to_all(ordered, 'expert', split_axis=0, concat_axis=1, tiled=True)  2.8 us
  transfers between devices with their start and end apart: 45, of which 24 were waited for; matrix products, arithmetic and copies ran while one was open for 12% of the time, Pallas kernels for 0%

profile of v5, /device:TPU:0, one launch (start us, length us, event | category | flops | bytes accessed | tf_op | source)
XLA Modules:
  0.0 120.9 jit_solution(12965039539565218306)
XLA Ops:
  0.5 2.6 %collective-permute-start.1 = (bf16[32,3584]{1,0:T(8,128)(2,1)}, bf16[32,3584]{1,0:T(8,128)(2,1)}, u32[]{:S(2)}, u32[]{:S(2)}) collective-permute-start(bf16[32,3584]{1,0:T(8,128)(2,1)} %bitcast.44), channel_id=1, source_target_pairs={{0,2},{1,3},{4,0},{5,1},{8,4},{9,5},{12,8},{13,9},{14,12},{15,13},... | collective-permute-start | bytes 688136 | tf_op jit(solution)/shard_map/ppermute | solution.py:307
  3.2 1.0 convolution_convert_fusion
  4.2 1.3 %copy.36 = bf16[128,2,576]{2,1,0:T(2,128)(2,1)} copy(bf16[128,2,576]{0,2,1:T(8,128)(2,1)S(1)} %convolution_convert_fusion) | data formatting | bytes 589824 | tf_op jit(solution)/shard_map/convert_element_type | solution.py:317
  5.4 6.3 %all-to-all-start = ((bf16[128,2,576]{2,1,0:T(2,128)(2,1)}), bf16[128,2,576]{2,1,0:T(2,128)(2,1)S(1)}, u32[]{:S(2)}, u32[]{:S(2)}) async-start(bf16[128,2,576]{2,1,0:T(2,128)(2,1)} %copy.36), calls=%async_computation | async-start | bytes 655360 | tf_op jit(solution)/shard_map/all_to_all | solution.py:318
  11.8 4.6 %reshape.51 = bf16[4,8,64,576]{3,2,1,0:T(8,128)(2,1)S(1)} reshape(bf16[4,8,36864]{2,1,0:T(8,128)(2,1)} %param.14) | data formatting | bytes 4718592 | tf_op jit(solution)/shard_map/reshape | solution.py:346
  16.4 0.7 dynamic-slice_bitcast_fusion.refs_0_
  17.6 1.7 %collective-permute-start.2 = (bf16[32,3584]{1,0:T(8,128)(2,1)}, bf16[32,3584]{1,0:T(8,128)(2,1)}, u32[]{:S(2)}, u32[]{:S(2)}) collective-permute-start(bf16[32,3584]{1,0:T(8,128)(2,1)} %collective-permute-done.refs_7_), channel_id=1, source_target_pairs={{0,4},{1,5},{4,8},{5,9},{8,12},{9,13},{12,14},{13,15},{14,10},{15,... | collective-permute-start | bytes 688136 | tf_op jit(solution)/shard_map/ppermute | solution.py:307
  20.1 2.8 %all-to-all-done = bf16[128,2,576]{2,1,0:T(2,128)(2,1)S(1)} async-done(((bf16[128,2,576]{2,1,0:T(2,128)(2,1)}), bf16[128,2,576]{2,1,0:T(2,128)(2,1)S(1)}, u32[]{:S(2)}, u32[]{:S(2)}) %all-to-all-start) | async-done | bytes 294944 | tf_op jit(solution)/shard_map/all_to_all | solution.py:318
  23.3 1.0 all_to_all.16
  24.2 2.1 %collective-permute-done.2.refs_9_ = bf16[32,3584]{1,0:T(8,128)(2,1)} collective-permute-done((bf16[32,3584]{1,0:T(8,128)(2,1)}, bf16[32,3584]{1,0:T(8,128)(2,1)}, u32[]{:S(2)}, u32[]{:S(2)}) %collective-permute-start.2) | collective-permute-done | bytes 229408 | tf_op jit(solution)/shard_map/ppermute | solution.py:307
  26.3 1.2 %collective-permute-done.3.refs_8_ = bf16[32,3584]{1,0:T(8,128)(2,1)} collective-permute-done((bf16[32,3584]{1,0:T(8,128)(2,1)}, bf16[32,3584]{1,0:T(8,128)(2,1)}, u32[]{:S(2)}, u32[]{:S(2)}) %collective-permute-start.3) | collective-permute-done | bytes 229408 | tf_op jit(solution)/shard_map/ppermute | solution.py:307
  27.7 1.4 %fusion.36 = (f32[4,8,64]{2,0,1:T(4,128)S(1)}, f32[4,8,64,4]{2,3,0,1:T(4,128)S(1)}) fusion(bf16[4,8,64,576]{3,2,1,0:T(8,128)(2,1)S(1)} %reshape.51, bf16[4,8,576,1]{2,1,0,3:T(8,128)(2,1)S(1)} %bitcast.42, pred[4,4]{1,0:T(4,128)(4,1)S(1)} %iota_compare_fusion.4), kind=kOutput, calls=%fused_computation.73 | convolution fusion | flops 9459712 | bytes 2437136 | tf_op jit(solution)/shard_map/srhk,trk->srht/dot_general | solution.py:256
  29.0 1.5 %fusion.35 = (f32[4,8,64]{2,0,1:T(4,128)S(1)}, f32[4,8,64,32]{2,3,0,1:T(8,128)S(1)}) fusion(bf16[4,8,64,576]{3,2,1,0:T(8,128)(2,1)S(1)} %reshape.51, bf16[8,32,576]{2,1,0:T(8,128)(2,1)S(1)} %copy-done.3, pred[8,32]{1,0:T(8,128)(4,1)S(1)} %iota_compare_fusion.2), kind=kOutput, calls=%fused_computation.72 | convolution fusion | flops 75692032 | bytes 2924800 | tf_op jit(solution)/shard_map/srhk,rpk->srhp/dot_general | solution.py:250
  31.3 1.5 %collective-permute-start.5 = (bf16[32,3584]{1,0:T(8,128)(2,1)}, bf16[32,3584]{1,0:T(8,128)(2,1)S(1)}, u32[]{:S(2)}, u32[]{:S(2)}) collective-permute-start(bf16[32,3584]{1,0:T(8,128)(2,1)} %collective-permute-done.2.refs_9_), channel_id=1, source_target_pairs={{0,4},{1,5},{4,8},{5,9},{8,12},{9,13},{12,14},{13,15},{14,10},{15,... | collective-permute-start | bytes 688136 | tf_op jit(solution)/shard_map/ppermute | solution.py:307
  33.8 5.0 %collective-permute-done.5.refs_11_ = bf16[32,3584]{1,0:T(8,128)(2,1)S(1)} collective-permute-done((bf16[32,3584]{1,0:T(8,128)(2,1)}, bf16[32,3584]{1,0:T(8,128)(2,1)S(1)}, u32[]{:S(2)}, u32[]{:S(2)}) %collective-permute-start.5) | collective-permute-done | bytes 229408 | tf_op jit(solution)/shard_map/ppermute | solution.py:307
  38.7 1.2 collective-permute-done.6.refs_10_
  39.9 0.6 collective-permute-start.13
  40.6 1.5 %collective-permute-start.12 = (bf16[16,3584]{1,0:T(8,128)(2,1)S(1)}, bf16[16,3584]{1,0:T(8,128)(2,1)S(1)}, u32[]{:S(2)}, u32[]{:S(2)}) collective-permute-start(bf16[16,3584]{1,0:T(8,128)(2,1)S(1)} %slice.124), channel_id=1, source_target_pairs={{0,4},{1,5},{4,8},{5,9},{8,12},{9,13},{12,14},{13,15},{14,10},{15,... | collective-permute-start | bytes 344072 | tf_op jit(solution)/shard_map/ppermute | solution.py:307
  42.1 1.5 %collective-permute-start.11 = (bf16[32,640]{1,0:T(8,128)(2,1)S(1)}, bf16[32,640]{1,0:T(8,128)(2,1)S(1)}, u32[]{:S(2)}, u32[]{:S(2)}) collective-permute-start(bf16[32,640]{1,0:T(8,128)(2,1)S(1)} %bitcast.38), channel_id=1, source_target_pairs={{0,4},{1,5},{2,6},{3,7},{4,8},{5,9},{6,10},{7,11},{8,12},{9,13},{1... | collective-permute-start | bytes 122888 | tf_op jit(solution)/shard_map/ppermute | solution.py:307
  43.5 1.5 %collective-permute-start.10 = (bf16[32,640]{1,0:T(8,128)(2,1)S(1)}, bf16[32,640]{1,0:T(8,128)(2,1)S(1)}, u32[]{:S(2)}, u32[]{:S(2)}) collective-permute-start(bf16[32,640]{1,0:T(8,128)(2,1)S(1)} %bitcast.39), channel_id=1, source_target_pairs={{0,8},{1,9},{2,10},{3,11},{4,12},{5,13},{6,14},{7,15},{8,0},{9,1},... | collective-permute-start | bytes 122888 | tf_op jit(solution)/shard_map/ppermute | solution.py:307
  45.0 2.4 %collective-permute-start.9 = (bf16[32,640]{1,0:T(8,128)(2,1)S(1)}, bf16[32,640]{1,0:T(8,128)(2,1)S(1)}, u32[]{:S(2)}, u32[]{:S(2)}) collective-permute-start(bf16[32,640]{1,0:T(8,128)(2,1)S(1)} %bitcast.40), channel_id=1, source_target_pairs={{0,12},{1,13},{2,14},{3,15},{4,0},{5,1},{6,2},{7,3},{8,4},{9,5},{1... | collective-permute-start | bytes 122888 | tf_op jit(solution)/shard_map/ppermute | solution.py:307
  48.4 0.6 collective-permute-done.9
  49.7 1.0 collective-permute-done.16.refs_17_
  50.7 0.7 collective-permute-start.14
  51.5 5.5 %collective-permute-done.14.refs_2_ = bf16[128,640]{1,0:T(8,128)(2,1)S(1)} collective-permute-done((bf16[128,640]{1,0:T(8,128)(2,1)S(1)}, bf16[128,640]{1,0:T(8,128)(2,1)S(1)}, u32[]{:S(2)}, u32[]{:S(2)}) %collective-permute-start.14) | collective-permute-done | bytes 163872 | tf_op jit(solution)/shard_map/ppermute | solution.py:307
  57.0 1.4 %collective-permute-done.21.refs_4_ = bf16[128,640]{1,0:T(8,128)(2,1)S(1)} collective-permute-done((bf16[128,640]{1,0:T(8,128)(2,1)S(1)}, bf16[128,640]{1,0:T(8,128)(2,1)S(1)}, u32[]{:S(2)}, u32[]{:S(2)}) %collective-permute-start.21) | collective-permute-done | bytes 163872 | tf_op jit(solution)/shard_map/ppermute | solution.py:307
  58.5 26.5 %experts.1 = (f32[32,3584]{1,0:T(8,128)}, bf16[32,3584]{1,0:T(8,128)(2,1)S(1)}, bf16[32,3584]{1,0:T(8,128)(2,1)S(1)}, bf16[32,3584]{1,0:T(8,128)(2,1)S(1)}, bf16...) custom-call(s32[17]{0:T(128)S(1)} %dynamic-slice_bitcast_fusion.refs, ...), custom_call_target="tpu_custom_call" | custom-call | flops 13153337344 | bytes 33030144 | tf_op jit(solution)/shard_map/experts/pallas_call | solution.py:208
  88.3 1.0 convert_add_fusion.6
  89.3 1.5 %collective-permute-start.27 = (bf16[16,3584]{1,0:T(8,128)(2,1)S(1)}, bf16[16,3584]{1,0:T(8,128)(2,1)S(1)}, u32[]{:S(2)}, u32[]{:S(2)}) collective-permute-start(bf16[16,3584]{1,0:T(8,128)(2,1)S(1)} %get-tuple-element.146), channel_id=1, source_target_pairs={{0,4},{1,5},{4,8},{5,9},{8,12},{9,13},{12,14},{13,15},{14,10},{15,... | collective-permute-start | bytes 344072 | tf_op jit(solution)/shard_map/ppermute | solution.py:307
  90.9 0.6 collective-permute-start.38
  91.5 1.5 %collective-permute-start.28 = (bf16[16,3584]{1,0:T(8,128)(2,1)S(1)}, bf16[16,3584]{1,0:T(8,128)(2,1)S(1)}, u32[]{:S(2)}, u32[]{:S(2)}) collective-permute-start(bf16[16,3584]{1,0:T(8,128)(2,1)S(1)} %get-tuple-element.147), channel_id=1, source_target_pairs={{0,2},{1,3},{4,0},{5,1},{8,4},{9,5},{12,8},{13,9},{14,12},{15,13},... | collective-permute-start | bytes 344072 | tf_op jit(solution)/shard_map/ppermute | solution.py:307
  93.1 0.7 collective-permute-start.39
  93.8 1.5 %collective-permute-done.27 = bf16[16,3584]{1,0:T(8,128)(2,1)S(1)} collective-permute-done((bf16[16,3584]{1,0:T(8,128)(2,1)S(1)}, bf16[16,3584]{1,0:T(8,128)(2,1)S(1)}, u32[]{:S(2)}, u32[]{:S(2)}) %collective-permute-start.27) | collective-permute-done | bytes 114720 | tf_op jit(solution)/shard_map/ppermute | solution.py:307
  95.3 3.5 %collective-permute-done.28 = bf16[16,3584]{1,0:T(8,128)(2,1)S(1)} collective-permute-done((bf16[16,3584]{1,0:T(8,128)(2,1)S(1)}, bf16[16,3584]{1,0:T(8,128)(2,1)S(1)}, u32[]{:S(2)}, u32[]{:S(2)}) %collective-permute-start.28) | collective-permute-done | bytes 114720 | tf_op jit(solution)/shard_map/ppermute | solution.py:307
  98.8 2.1 %collective-permute-start.29 = (bf16[16,3584]{1,0:T(8,128)(2,1)S(1)}, bf16[16,3584]{1,0:T(8,128)(2,1)S(1)}, u32[]{:S(2)}, u32[]{:S(2)}) collective-permute-start(bf16[16,3584]{1,0:T(8,128)(2,1)S(1)} %add_convert_fusion.11), channel_id=1, source_target_pairs={{0,4},{1,5},{4,8},{5,9},{8,12},{9,13},{12,14},{13,15},{14,10},{15,... | collective-permute-start | bytes 344072 | tf_op jit(solution)/shard_map/ppermute | solution.py:307
  101.0 2.0 %collective-permute-start.40 = (bf16[16,3584]{1,0:T(8,128)(2,1)S(1)}, bf16[16,3584]{1,0:T(8,128)(2,1)S(1)}, u32[]{:S(2)}, u32[]{:S(2)}) collective-permute-start(bf16[16,3584]{1,0:T(8,128)(2,1)S(1)} %add_convert_fusion.5), channel_id=1, source_target_pairs={{0,4},{1,5},{4,8},{5,9},{8,12},{9,13},{12,14},{13,15},{14,10},{15,... | collective-permute-start | bytes 344072 | tf_op jit(solution)/shard_map/ppermute | solution.py:307
  103.2 1.4 %collective-permute-done.29 = bf16[16,3584]{1,0:T(8,128)(2,1)S(1)} collective-permute-done((bf16[16,3584]{1,0:T(8,128)(2,1)S(1)}, bf16[16,3584]{1,0:T(8,128)(2,1)S(1)}, u32[]{:S(2)}, u32[]{:S(2)}) %collective-permute-start.29) | collective-permute-done | bytes 114720 | tf_op jit(solution)/shard_map/ppermute | solution.py:307
  104.6 1.2 %collective-permute-done.31 = bf16[16,3584]{1,0:T(8,128)(2,1)S(1)} collective-permute-done((bf16[16,3584]{1,0:T(8,128)(2,1)S(1)}, bf16[16,3584]{1,0:T(8,128)(2,1)S(1)}, u32[]{:S(2)}, u32[]{:S(2)}) %collective-permute-start.31) | collective-permute-done | bytes 114720 | tf_op jit(solution)/shard_map/ppermute | solution.py:307
  105.9 0.7 collective-permute-start.32
  107.1 0.9 collective-permute-done.41
  108.0 0.6 collective-permute-start.42
  108.6 1.5 %collective-permute-start.34 = (bf16[16,3584]{1,0:T(8,128)(2,1)S(1)}, bf16[16,3584]{1,0:T(8,128)(2,1)S(1)}, u32[]{:S(2)}, u32[]{:S(2)}) collective-permute-start(bf16[16,3584]{1,0:T(8,128)(2,1)S(1)} %add_convert_fusion.8), channel_id=1, source_target_pairs={{0,2},{1,3},{4,0},{5,1},{8,4},{9,5},{12,8},{13,9},{14,12},{15,13},... | collective-permute-start | bytes 344072 | tf_op jit(solution)/shard_map/ppermute | solution.py:307
  110.7 3.3 %collective-permute-done.34 = bf16[16,3584]{1,0:T(8,128)(2,1)S(1)} collective-permute-done((bf16[16,3584]{1,0:T(8,128)(2,1)S(1)}, bf16[16,3584]{1,0:T(8,128)(2,1)S(1)}, u32[]{:S(2)}, u32[]{:S(2)}) %collective-permute-start.34) | collective-permute-done | bytes 114720 | tf_op jit(solution)/shard_map/ppermute | solution.py:307
  114.1 1.0 collective-permute-start.35
  115.2 1.1 collective-permute-start.37
  116.3 2.7 %collective-permute-done.35 = bf16[16,3584]{1,0:T(8,128)(2,1)S(1)} collective-permute-done((bf16[16,3584]{1,0:T(8,128)(2,1)S(1)}, bf16[16,3584]{1,0:T(8,128)(2,1)S(1)}, u32[]{:S(2)}, u32[]{:S(2)}) %collective-permute-start.35) | collective-permute-done | bytes 114720 | tf_op jit(solution)/shard_map/ppermute | solution.py:307
  118.9 1.1 collective-permute-done.37
  120.2 0.7 maximum_bitcast_fusion
  (136 shorter events, 10.8 us)
Async XLA Ops:
  0.0 24.2 %collective-permute-start.4 = (bf16[32,3584]{1,0:T(8,128)(2,1)}, bf16[32,3584]{1,0:T(8,128)(2,1)}, u32[]{:S(2)}, u32[]{:S(2)}) collective-permute-start(bf16[32,3584]{1,0:T(8,128)(2,1)} %bitcast.43), channel_id=1, source_target_pairs={{0,1},{1,0},{2,3},{3,2},{4,5},{5,4},{6,7},{7,6},{8,9},{9,8},{10,11... | collective-permute-start | bytes 688136 | tf_op jit(solution)/shard_map/ppermute | solution.py:307
  0.5 16.6 %collective-permute-start.1 = (bf16[32,3584]{1,0:T(8,128)(2,1)}, bf16[32,3584]{1,0:T(8,128)(2,1)}, u32[]{:S(2)}, u32[]{:S(2)}) collective-permute-start(bf16[32,3584]{1,0:T(8,128)(2,1)} %bitcast.44), channel_id=1, source_target_pairs={{0,2},{1,3},{4,0},{5,1},{8,4},{9,5},{12,8},{13,9},{14,12},{15,13},... | collective-permute-start | bytes 688136 | tf_op jit(solution)/shard_map/ppermute | solution.py:307
  3.0 14.1 %collective-permute-start = (bf16[32,3584]{1,0:T(8,128)(2,1)}, bf16[32,3584]{1,0:T(8,128)(2,1)}, u32[]{:S(2)}, u32[]{:S(2)}) collective-permute-start(bf16[32,3584]{1,0:T(8,128)(2,1)} %bitcast.45), channel_id=1, source_target_pairs={{0,4},{1,5},{4,8},{5,9},{8,12},{9,13},{12,14},{13,15},{14,10},{15,... | collective-permute-start | bytes 688136 | tf_op jit(solution)/shard_map/ppermute | solution.py:307
  5.4 17.4 %all-to-all-start = ((bf16[128,2,576]{2,1,0:T(2,128)(2,1)}), bf16[128,2,576]{2,1,0:T(2,128)(2,1)S(1)}, u32[]{:S(2)}, u32[]{:S(2)}) async-start(bf16[128,2,576]{2,1,0:T(2,128)(2,1)} %copy.36), calls=%async_computation | async-start | bytes 655360 | tf_op jit(solution)/shard_map/all_to_all | solution.py:318
  17.1 16.6 %collective-permute-start.7 = (bf16[32,3584]{1,0:T(8,128)(2,1)}, bf16[32,3584]{1,0:T(8,128)(2,1)}, u32[]{:S(2)}, u32[]{:S(2)}) collective-permute-start(bf16[32,3584]{1,0:T(8,128)(2,1)} %collective-permute-done.refs_7_), channel_id=1, source_target_pairs={{0,1},{1,0},{2,3},{3,2},{4,5},{5,4},{6,7},{7,6},{8,9},{9,8},{10,11... | collective-permute-start | bytes 688136 | tf_op jit(solution)/shard_map/ppermute | solution.py:307
  17.6 8.8 %collective-permute-start.2 = (bf16[32,3584]{1,0:T(8,128)(2,1)}, bf16[32,3584]{1,0:T(8,128)(2,1)}, u32[]{:S(2)}, u32[]{:S(2)}) collective-permute-start(bf16[32,3584]{1,0:T(8,128)(2,1)} %collective-permute-done.refs_7_), channel_id=1, source_target_pairs={{0,4},{1,5},{4,8},{5,9},{8,12},{9,13},{12,14},{13,15},{14,10},{15,... | collective-permute-start | bytes 688136 | tf_op jit(solution)/shard_map/ppermute | solution.py:307
  19.2 14.5 %collective-permute-start.8 = (bf16[32,3584]{1,0:T(8,128)(2,1)}, bf16[32,3584]{1,0:T(8,128)(2,1)}, u32[]{:S(2)}, u32[]{:S(2)}) collective-permute-start(bf16[32,3584]{1,0:T(8,128)(2,1)} %collective-permute-done.1.refs_6_), channel_id=1, source_target_pairs={{0,1},{1,0},{2,3},{3,2},{4,5},{5,4},{6,7},{7,6},{8,9},{9,8},{10,11... | collective-permute-start | bytes 688136 | tf_op jit(solution)/shard_map/ppermute | solution.py:307
  19.3 8.3 %collective-permute-start.3 = (bf16[32,3584]{1,0:T(8,128)(2,1)}, bf16[32,3584]{1,0:T(8,128)(2,1)}, u32[]{:S(2)}, u32[]{:S(2)}) collective-permute-start(bf16[32,3584]{1,0:T(8,128)(2,1)} %collective-permute-done.1.refs_6_), channel_id=1, source_target_pairs={{0,2},{1,3},{4,0},{5,1},{8,4},{9,5},{12,8},{13,9},{14,12},{15,13},... | collective-permute-start | bytes 688136 | tf_op jit(solution)/shard_map/ppermute | solution.py:307
  30.6 27.9 %copy-start.1 = (bf16[3584,16]{0,1:T(8,128)(2,1)S(1)}, bf16[3584,16]{0,1:T(8,128)(2,1)}, u32[]{:S(2)}) copy-start(bf16[3584,16]{0,1:T(8,128)(2,1)} %param.23) | copy-start | bytes 344068
  31.3 7.4 %collective-permute-start.5 = (bf16[32,3584]{1,0:T(8,128)(2,1)}, bf16[32,3584]{1,0:T(8,128)(2,1)S(1)}, u32[]{:S(2)}, u32[]{:S(2)}) collective-permute-start(bf16[32,3584]{1,0:T(8,128)(2,1)} %collective-permute-done.2.refs_9_), channel_id=1, source_target_pairs={{0,4},{1,5},{4,8},{5,9},{8,12},{9,13},{12,14},{13,15},{14,10},{15,... | collective-permute-start | bytes 688136 | tf_op jit(solution)/shard_map/ppermute | solution.py:307
  32.8 7.1 %collective-permute-start.6 = (bf16[32,3584]{1,0:T(8,128)(2,1)}, bf16[32,3584]{1,0:T(8,128)(2,1)S(1)}, u32[]{:S(2)}, u32[]{:S(2)}) collective-permute-start(bf16[32,3584]{1,0:T(8,128)(2,1)} %collective-permute-done.3.refs_8_), channel_id=1, source_target_pairs={{0,2},{1,3},{4,0},{5,1},{8,4},{9,5},{12,8},{13,9},{14,12},{15,13},... | collective-permute-start | bytes 688136 | tf_op jit(solution)/shard_map/ppermute | solution.py:307
  38.7 19.7 %copy-start.6 = (bf16[32,3584]{1,0:T(8,128)(2,1)}, bf16[32,3584]{1,0:T(8,128)(2,1)S(1)}, u32[]{:S(2)}) copy-start(bf16[32,3584]{1,0:T(8,128)(2,1)S(1)} %collective-permute-done.5.refs_11_) | copy-start | bytes 688132
  39.9 9.1 %collective-permute-start.13 = (bf16[16,3584]{1,0:T(8,128)(2,1)S(1)}, bf16[16,3584]{1,0:T(8,128)(2,1)S(1)}, u32[]{:S(2)}, u32[]{:S(2)}) collective-permute-start(bf16[16,3584]{1,0:T(8,128)(2,1)S(1)} %slice.125), channel_id=1, source_target_pairs={{0,2},{1,3},{4,0},{5,1},{8,4},{9,5},{12,8},{13,9},{14,12},{15,13},... | collective-permute-start | bytes 344072 | tf_op jit(solution)/shard_map/ppermute | solution.py:307
  40.6 9.0 %collective-permute-start.12 = (bf16[16,3584]{1,0:T(8,128)(2,1)S(1)}, bf16[16,3584]{1,0:T(8,128)(2,1)S(1)}, u32[]{:S(2)}, u32[]{:S(2)}) collective-permute-start(bf16[16,3584]{1,0:T(8,128)(2,1)S(1)} %slice.124), channel_id=1, source_target_pairs={{0,4},{1,5},{4,8},{5,9},{8,12},{9,13},{12,14},{13,15},{14,10},{15,... | collective-permute-start | bytes 344072 | tf_op jit(solution)/shard_map/ppermute | solution.py:307
  42.1 5.8 %collective-permute-start.11 = (bf16[32,640]{1,0:T(8,128)(2,1)S(1)}, bf16[32,640]{1,0:T(8,128)(2,1)S(1)}, u32[]{:S(2)}, u32[]{:S(2)}) collective-permute-start(bf16[32,640]{1,0:T(8,128)(2,1)S(1)} %bitcast.38), channel_id=1, source_target_pairs={{0,4},{1,5},{2,6},{3,7},{4,8},{5,9},{6,10},{7,11},{8,12},{9,13},{1... | collective-permute-start | bytes 122888 | tf_op jit(solution)/shard_map/ppermute | solution.py:307
  43.5 4.9 %collective-permute-start.10 = (bf16[32,640]{1,0:T(8,128)(2,1)S(1)}, bf16[32,640]{1,0:T(8,128)(2,1)S(1)}, u32[]{:S(2)}, u32[]{:S(2)}) collective-permute-start(bf16[32,640]{1,0:T(8,128)(2,1)S(1)} %bitcast.39), channel_id=1, source_target_pairs={{0,8},{1,9},{2,10},{3,11},{4,12},{5,13},{6,14},{7,15},{8,0},{9,1},... | collective-permute-start | bytes 122888 | tf_op jit(solution)/shard_map/ppermute | solution.py:307
  45.0 4.0 %collective-permute-start.9 = (bf16[32,640]{1,0:T(8,128)(2,1)S(1)}, bf16[32,640]{1,0:T(8,128)(2,1)S(1)}, u32[]{:S(2)}, u32[]{:S(2)}) collective-permute-start(bf16[32,640]{1,0:T(8,128)(2,1)S(1)} %bitcast.40), channel_id=1, source_target_pairs={{0,12},{1,13},{2,14},{3,15},{4,0},{5,1},{6,2},{7,3},{8,4},{9,5},{1... | collective-permute-start | bytes 122888 | tf_op jit(solution)/shard_map/ppermute | solution.py:307
  47.9 3.6 %collective-permute-start.15 = (bf16[32,3584]{1,0:T(8,128)(2,1)S(1)}, bf16[32,3584]{1,0:T(8,128)(2,1)S(1)}, u32[]{:S(2)}, u32[]{:S(2)}) collective-permute-start(bf16[32,3584]{1,0:T(8,128)(2,1)S(1)} %collective-permute-done.5.refs_11_), channel_id=1, source_target_pairs={{0,1},{1,0},{2,3},{3,2},{4,5},{5,4},{6,7},{7,6},{8,9},{9,8},{10,11... | collective-permute-start | bytes 688136 | tf_op jit(solution)/shard_map/ppermute | solution.py:307
  48.4 3.0 %collective-permute-start.18 = (bf16[32,3584]{1,0:T(8,128)(2,1)S(1)}, bf16[32,3584]{1,0:T(8,128)(2,1)S(1)}, u32[]{:S(2)}, u32[]{:S(2)}) collective-permute-start(bf16[32,3584]{1,0:T(8,128)(2,1)S(1)} %collective-permute-done.6.refs_10_), channel_id=1, source_target_pairs={{0,1},{1,0},{2,3},{3,2},{4,5},{5,4},{6,7},{7,6},{8,9},{9,8},{10,11... | collective-permute-start | bytes 688136 | tf_op jit(solution)/shard_map/ppermute | solution.py:307
  49.0 1.7 %collective-permute-start.16 = (bf16[32,3584]{1,0:T(8,128)(2,1)}, bf16[32,3584]{1,0:T(8,128)(2,1)S(1)}, u32[]{:S(2)}, u32[]{:S(2)}) collective-permute-start(bf16[32,3584]{1,0:T(8,128)(2,1)} %collective-permute-done.2.refs_9_), channel_id=1, source_target_pairs={{0,1},{1,0},{2,3},{3,2},{4,5},{5,4},{6,7},{7,6},{8,9},{9,8},{10,11... | collective-permute-start | bytes 688136 | tf_op jit(solution)/shard_map/ppermute | solution.py:307
  49.0 2.4 %collective-permute-start.17 = (bf16[32,3584]{1,0:T(8,128)(2,1)}, bf16[32,3584]{1,0:T(8,128)(2,1)S(1)}, u32[]{:S(2)}, u32[]{:S(2)}) collective-permute-start(bf16[32,3584]{1,0:T(8,128)(2,1)} %collective-permute-done.3.refs_8_), channel_id=1, source_target_pairs={{0,1},{1,0},{2,3},{3,2},{4,5},{5,4},{6,7},{7,6},{8,9},{9,8},{10,11... | collective-permute-start | bytes 688136 | tf_op jit(solution)/shard_map/ppermute | solution.py:307
  49.6 7.4 %collective-permute-start.19 = (bf16[32,3584]{1,0:T(8,128)(2,1)S(1)}, bf16[32,3584]{1,0:T(8,128)(2,1)S(1)}, u32[]{:S(2)}, u32[]{:S(2)}) collective-permute-start(bf16[32,3584]{1,0:T(8,128)(2,1)S(1)} %constant_dynamic-update-slice_fusion.4.refs_12_), channel_id=1, source_target_pairs={{0,1},{1,0},{2,3},{3,2},{4,5},{5,4},{6,7},{7,6},{8,9},{9,8},{10,11... | collective-permute-start | bytes 688136 | tf_op jit(solution)/shard_map/ppermute | solution.py:307
  50.7 6.2 %collective-permute-start.14 = (bf16[128,640]{1,0:T(8,128)(2,1)S(1)}, bf16[128,640]{1,0:T(8,128)(2,1)S(1)}, u32[]{:S(2)}, u32[]{:S(2)}) collective-permute-start(bf16[128,640]{1,0:T(8,128)(2,1)S(1)} %constant_dynamic-update-slice_fusion.refs_1_), channel_id=1, source_target_pairs={{0,2},{1,3},{2,0},{3,1},{4,6},{5,7},{6,4},{7,5},{8,10},{9,11},{10,... | collective-permute-start | bytes 491528 | tf_op jit(solution)/shard_map/ppermute | solution.py:307
  51.5 5.5 %collective-permute-start.20 = (bf16[128,640]{1,0:T(8,128)(2,1)S(1)}, bf16[128,640]{1,0:T(8,128)(2,1)S(1)}, u32[]{:S(2)}, u32[]{:S(2)}) collective-permute-start(bf16[128,640]{1,0:T(8,128)(2,1)S(1)} %constant_dynamic-update-slice_fusion.refs_1_), channel_id=1, source_target_pairs={{0,1},{1,0},{2,3},{3,2},{4,5},{5,4},{6,7},{7,6},{8,9},{9,8},{10,11... | collective-permute-start | bytes 491528 | tf_op jit(solution)/shard_map/ppermute | solution.py:307
  57.0 1.4 %collective-permute-start.21 = (bf16[128,640]{1,0:T(8,128)(2,1)S(1)}, bf16[128,640]{1,0:T(8,128)(2,1)S(1)}, u32[]{:S(2)}, u32[]{:S(2)}) collective-permute-start(bf16[128,640]{1,0:T(8,128)(2,1)S(1)} %collective-permute-done.14.refs_2_), channel_id=1, source_target_pairs={{0,1},{1,0},{2,3},{3,2},{4,5},{5,4},{6,7},{7,6},{8,9},{9,8},{10,11... | collective-permute-start | bytes 491528 | tf_op jit(solution)/shard_map/ppermute | solution.py:307
  85.0 1.8 %collective-permute-start.23 = (bf16[32,3584]{1,0:T(8,128)(2,1)}, bf16[32,3584]{1,0:T(8,128)(2,1)S(1)}, u32[]{:S(2)}, u32[]{:S(2)}) collective-permute-start(bf16[32,3584]{1,0:T(8,128)(2,1)} %get-tuple-element.136), channel_id=1, source_target_pairs={{0,1},{1,0},{2,3},{3,2},{4,5},{5,4},{6,7},{7,6},{8,9},{9,8},{10,11... | collective-permute-start | bytes 688136 | tf_op jit(solution)/shard_map/ppermute | solution.py:307
  85.2 34.8 %collective-permute-start.22 = (bf16[32,3584]{1,0:T(8,128)(2,1)}, bf16[32,3584]{1,0:T(8,128)(2,1)S(1)}, u32[]{:S(2)}, u32[]{:S(2)}) collective-permute-start(bf16[32,3584]{1,0:T(8,128)(2,1)} %get-tuple-element.134), channel_id=1, source_target_pairs={{0,1},{1,0},{2,3},{3,2},{4,5},{5,4},{6,7},{7,6},{8,9},{9,8},{10,11... | collective-permute-start | bytes 688136 | tf_op jit(solution)/shard_map/ppermute | solution.py:307
  85.6 1.8 %collective-permute-start.24 = (bf16[32,3584]{1,0:T(8,128)(2,1)}, bf16[32,3584]{1,0:T(8,128)(2,1)S(1)}, u32[]{:S(2)}, u32[]{:S(2)}) collective-permute-start(bf16[32,3584]{1,0:T(8,128)(2,1)} %get-tuple-element.139), channel_id=1, source_target_pairs={{0,1},{1,0},{2,3},{3,2},{4,5},{5,4},{6,7},{7,6},{8,9},{9,8},{10,11... | collective-permute-start | bytes 688136 | tf_op jit(solution)/shard_map/ppermute | solution.py:307
  85.7 3.6 %collective-permute-start.25 = (bf16[32,3584]{1,0:T(8,128)(2,1)}, bf16[32,3584]{1,0:T(8,128)(2,1)S(1)}, u32[]{:S(2)}, u32[]{:S(2)}) collective-permute-start(bf16[32,3584]{1,0:T(8,128)(2,1)} %get-tuple-element.142), channel_id=1, source_target_pairs={{0,1},{1,0},{2,3},{3,2},{4,5},{5,4},{6,7},{7,6},{8,9},{9,8},{10,11... | collective-permute-start | bytes 688136 | tf_op jit(solution)/shard_map/ppermute | solution.py:307
  86.1 2.0 %collective-permute-start.26 = (bf16[32,3584]{1,0:T(8,128)(2,1)}, bf16[32,3584]{1,0:T(8,128)(2,1)S(1)}, u32[]{:S(2)}, u32[]{:S(2)}) collective-permute-start(bf16[32,3584]{1,0:T(8,128)(2,1)} %get-tuple-element.145), channel_id=1, source_target_pairs={{0,1},{1,0},{2,3},{3,2},{4,5},{5,4},{6,7},{7,6},{8,9},{9,8},{10,11... | collective-permute-start | bytes 688136 | tf_op jit(solution)/shard_map/ppermute | solution.py:307
  86.8 4.0 %collective-permute-start.30 = (bf16[32,3584]{1,0:T(8,128)(2,1)}, bf16[32,3584]{1,0:T(8,128)(2,1)S(1)}, u32[]{:S(2)}, u32[]{:S(2)}) collective-permute-start(bf16[32,3584]{1,0:T(8,128)(2,1)} %get-tuple-element.150), channel_id=1, source_target_pairs={{0,1},{1,0},{2,3},{3,2},{4,5},{5,4},{6,7},{7,6},{8,9},{9,8},{10,11... | collective-permute-start | bytes 688136 | tf_op jit(solution)/shard_map/ppermute | solution.py:307
  87.4 5.6 %collective-permute-start.33 = (bf16[32,3584]{1,0:T(8,128)(2,1)}, bf16[32,3584]{1,0:T(8,128)(2,1)S(1)}, u32[]{:S(2)}, u32[]{:S(2)}) collective-permute-start(bf16[32,3584]{1,0:T(8,128)(2,1)} %get-tuple-element.155), channel_id=1, source_target_pairs={{0,1},{1,0},{2,3},{3,2},{4,5},{5,4},{6,7},{7,6},{8,9},{9,8},{10,11... | collective-permute-start | bytes 688136 | tf_op jit(solution)/shard_map/ppermute | solution.py:307
  88.1 3.4 %collective-permute-start.36 = (bf16[32,3584]{1,0:T(8,128)(2,1)}, bf16[32,3584]{1,0:T(8,128)(2,1)S(1)}, u32[]{:S(2)}, u32[]{:S(2)}) collective-permute-start(bf16[32,3584]{1,0:T(8,128)(2,1)} %get-tuple-element.160), channel_id=1, source_target_pairs={{0,1},{1,0},{2,3},{3,2},{4,5},{5,4},{6,7},{7,6},{8,9},{9,8},{10,11... | collective-permute-start | bytes 688136 | tf_op jit(solution)/shard_map/ppermute | solution.py:307
  89.3 6.0 %collective-permute-start.27 = (bf16[16,3584]{1,0:T(8,128)(2,1)S(1)}, bf16[16,3584]{1,0:T(8,128)(2,1)S(1)}, u32[]{:S(2)}, u32[]{:S(2)}) collective-permute-start(bf16[16,3584]{1,0:T(8,128)(2,1)S(1)} %get-tuple-element.146), channel_id=1, source_target_pairs={{0,4},{1,5},{4,8},{5,9},{8,12},{9,13},{12,14},{13,15},{14,10},{15,... | collective-permute-start | bytes 344072 | tf_op jit(solution)/shard_map/ppermute | solution.py:307
  90.9 10.1 %collective-permute-start.38 = (bf16[16,3584]{1,0:T(8,128)(2,1)S(1)}, bf16[16,3584]{1,0:T(8,128)(2,1)S(1)}, u32[]{:S(2)}, u32[]{:S(2)}) collective-permute-start(bf16[16,3584]{1,0:T(8,128)(2,1)S(1)} %convert_add_fusion.8), channel_id=1, source_target_pairs={{0,4},{1,5},{4,8},{5,9},{8,12},{9,13},{12,14},{13,15},{14,10},{15,... | collective-permute-start | bytes 344072 | tf_op jit(solution)/shard_map/ppermute | solution.py:307
  91.5 7.3 %collective-permute-start.28 = (bf16[16,3584]{1,0:T(8,128)(2,1)S(1)}, bf16[16,3584]{1,0:T(8,128)(2,1)S(1)}, u32[]{:S(2)}, u32[]{:S(2)}) collective-permute-start(bf16[16,3584]{1,0:T(8,128)(2,1)S(1)} %get-tuple-element.147), channel_id=1, source_target_pairs={{0,2},{1,3},{4,0},{5,1},{8,4},{9,5},{12,8},{13,9},{14,12},{15,13},... | collective-permute-start | bytes 344072 | tf_op jit(solution)/shard_map/ppermute | solution.py:307
  93.1 7.9 %collective-permute-start.39 = (bf16[16,3584]{1,0:T(8,128)(2,1)S(1)}, bf16[16,3584]{1,0:T(8,128)(2,1)S(1)}, u32[]{:S(2)}, u32[]{:S(2)}) collective-permute-start(bf16[16,3584]{1,0:T(8,128)(2,1)S(1)} %convert_add_fusion.5), channel_id=1, source_target_pairs={{0,2},{1,3},{4,0},{5,1},{8,4},{9,5},{12,8},{13,9},{14,12},{15,13},... | collective-permute-start | bytes 344072 | tf_op jit(solution)/shard_map/ppermute | solution.py:307
  93.8 26.3 %copy-start.2 = (f32[32,3584]{1,0:T(8,128)S(1)}, f32[32,3584]{1,0:T(8,128)}, u32[]{:S(2)}) copy-start(f32[32,3584]{1,0:T(8,128)} %get-tuple-element.132) | copy-start | bytes 1376260
  98.8 5.9 %collective-permute-start.29 = (bf16[16,3584]{1,0:T(8,128)(2,1)S(1)}, bf16[16,3584]{1,0:T(8,128)(2,1)S(1)}, u32[]{:S(2)}, u32[]{:S(2)}) collective-permute-start(bf16[16,3584]{1,0:T(8,128)(2,1)S(1)} %add_convert_fusion.11), channel_id=1, source_target_pairs={{0,4},{1,5},{4,8},{5,9},{8,12},{9,13},{12,14},{13,15},{14,10},{15,... | collective-permute-start | bytes 344072 | tf_op jit(solution)/shard_map/ppermute | solution.py:307
  100.9 4.9 %collective-permute-start.31 = (bf16[16,3584]{1,0:T(8,128)(2,1)S(1)}, bf16[16,3584]{1,0:T(8,128)(2,1)S(1)}, u32[]{:S(2)}, u32[]{:S(2)}) collective-permute-start(bf16[16,3584]{1,0:T(8,128)(2,1)S(1)} %add_convert_fusion.10), channel_id=1, source_target_pairs={{0,2},{1,3},{4,0},{5,1},{8,4},{9,5},{12,8},{13,9},{14,12},{15,13},... | collective-permute-start | bytes 344072 | tf_op jit(solution)/shard_map/ppermute | solution.py:307
  101.0 6.1 %collective-permute-start.40 = (bf16[16,3584]{1,0:T(8,128)(2,1)S(1)}, bf16[16,3584]{1,0:T(8,128)(2,1)S(1)}, u32[]{:S(2)}, u32[]{:S(2)}) collective-permute-start(bf16[16,3584]{1,0:T(8,128)(2,1)S(1)} %add_convert_fusion.5), channel_id=1, source_target_pairs={{0,4},{1,5},{4,8},{5,9},{8,12},{9,13},{12,14},{13,15},{14,10},{15,... | collective-permute-start | bytes 344072 | tf_op jit(solution)/shard_map/ppermute | solution.py:307
  103.1 4.8 %collective-permute-start.41 = (bf16[16,3584]{1,0:T(8,128)(2,1)S(1)}, bf16[16,3584]{1,0:T(8,128)(2,1)S(1)}, u32[]{:S(2)}, u32[]{:S(2)}) collective-permute-start(bf16[16,3584]{1,0:T(8,128)(2,1)S(1)} %add_convert_fusion.4), channel_id=1, source_target_pairs={{0,2},{1,3},{4,0},{5,1},{8,4},{9,5},{12,8},{13,9},{14,12},{15,13},... | collective-permute-start | bytes 344072 | tf_op jit(solution)/shard_map/ppermute | solution.py:307
  105.9 4.8 %collective-permute-start.32 = (bf16[16,3584]{1,0:T(8,128)(2,1)S(1)}, bf16[16,3584]{1,0:T(8,128)(2,1)S(1)}, u32[]{:S(2)}, u32[]{:S(2)}) collective-permute-start(bf16[16,3584]{1,0:T(8,128)(2,1)S(1)} %add_convert_fusion.9), channel_id=1, source_target_pairs={{0,4},{1,5},{4,8},{5,9},{8,12},{9,13},{12,14},{13,15},{14,10},{15,... | collective-permute-start | bytes 344072 | tf_op jit(solution)/shard_map/ppermute | solution.py:307
  108.0 8.3 %collective-permute-start.42 = (bf16[16,3584]{1,0:T(8,128)(2,1)S(1)}, bf16[16,3584]{1,0:T(8,128)(2,1)S(1)}, u32[]{:S(2)}, u32[]{:S(2)}) collective-permute-start(bf16[16,3584]{1,0:T(8,128)(2,1)S(1)} %add_convert_fusion.3), channel_id=1, source_target_pairs={{0,4},{1,5},{4,8},{5,9},{8,12},{9,13},{12,14},{13,15},{14,10},{15,... | collective-permute-start | bytes 344072 | tf_op jit(solution)/shard_map/ppermute | solution.py:307
  108.6 5.4 %collective-permute-start.34 = (bf16[16,3584]{1,0:T(8,128)(2,1)S(1)}, bf16[16,3584]{1,0:T(8,128)(2,1)S(1)}, u32[]{:S(2)}, u32[]{:S(2)}) collective-permute-start(bf16[16,3584]{1,0:T(8,128)(2,1)S(1)} %add_convert_fusion.8), channel_id=1, source_target_pairs={{0,2},{1,3},{4,0},{5,1},{8,4},{9,5},{12,8},{13,9},{14,12},{15,13},... | collective-permute-start | bytes 344072 | tf_op jit(solution)/shard_map/ppermute | solution.py:307
  110.2 6.1 %collective-permute-start.43 = (bf16[16,3584]{1,0:T(8,128)(2,1)S(1)}, bf16[16,3584]{1,0:T(8,128)(2,1)S(1)}, u32[]{:S(2)}, u32[]{:S(2)}) collective-permute-start(bf16[16,3584]{1,0:T(8,128)(2,1)S(1)} %add_convert_fusion.2), channel_id=1, source_target_pairs={{0,2},{1,3},{4,0},{5,1},{8,4},{9,5},{12,8},{13,9},{14,12},{15,13},... | collective-permute-start | bytes 344072 | tf_op jit(solution)/shard_map/ppermute | solution.py:307
  114.1 4.8 %collective-permute-start.35 = (bf16[16,3584]{1,0:T(8,128)(2,1)S(1)}, bf16[16,3584]{1,0:T(8,128)(2,1)S(1)}, u32[]{:S(2)}, u32[]{:S(2)}) collective-permute-start(bf16[16,3584]{1,0:T(8,128)(2,1)S(1)} %add_convert_fusion.7), channel_id=1, source_target_pairs={{0,4},{1,5},{4,8},{5,9},{8,12},{9,13},{12,14},{13,15},{14,10},{15,... | collective-permute-start | bytes 344072 | tf_op jit(solution)/shard_map/ppermute | solution.py:307
  115.2 4.8 %collective-permute-start.37 = (bf16[16,3584]{1,0:T(8,128)(2,1)S(1)}, bf16[16,3584]{1,0:T(8,128)(2,1)S(1)}, u32[]{:S(2)}, u32[]{:S(2)}) collective-permute-start(bf16[16,3584]{1,0:T(8,128)(2,1)S(1)} %add_convert_fusion.6), channel_id=1, source_target_pairs={{0,2},{1,3},{4,0},{5,1},{8,4},{9,5},{12,8},{13,9},{14,12},{15,13},... | collective-permute-start | bytes 344072 | tf_op jit(solution)/shard_map/ppermute | solution.py:307
  (16 other events, 117.1 us)

commit v6 on v5

v6 whole, which is shorter than its diff:
```python
import jax
import jax.numpy as jnp
from jax import lax
from jax.experimental import pallas as pl
from jax.experimental.pallas import tpu as pltpu
from jax.sharding import PartitionSpec as P

qk_scale = 192.0 ** (-0.5)
LANES = 128


def ring_of(chips):
    return list(range(0, chips, 2)) + list(range(chips - 1, 0, -2))


def shift_perm(chips, by):
    ring = ring_of(chips)
    return [
        (2 * ring[p] + core, 2 * ring[(p + by) % chips] + core)
        for p in range(chips)
        for core in range(2)
    ]


def sibling_perm(chips):
    return [(d, d ^ 1) for d in range(2 * chips)]


def distances(chips):
    half = chips // 2
    far = [half, half - 1, 1 - half]
    return far, [0] + [d for t in range(1, half - 1) for d in (t, -t)]


def gather_steps(chips):
    high = 4 if chips % 4 == 0 else 2
    return high, chips // high


def step_perm(chips, by_high, by_low):
    high, low = gather_steps(chips)
    return [
        (
            2 * (h * low + l) + core,
            2 * ((h - by_high) % high * low + (l - by_low) % low) + core,
        )
        for h in range(high)
        for l in range(low)
        for core in range(2)
    ]


def gathered_place(chips):
    high, low = gather_steps(chips)
    ring = ring_of(chips)
    table = [[] for _ in range(chips)]
    for p, chip in enumerate(ring):
        for part in distances(chips):
            for side in (0, chips):
                for d in part:
                    other = ring[(p + d) % chips]
                    by_high = (other // low - chip // low) % high
                    by_low = (other % low - chip % low) % low
                    table[chip].append(side + by_low * high + by_high)
    return table


def tile_of(size, most):
    return max(t for t in range(LANES, min(size, most) + 1, LANES) if size % t == 0)


def norm_kernel(far, blocks, rows, latent, width, *refs):
    scalars = refs[0]
    pooled = refs[1:5]
    resid = refs[5 : 5 + blocks]
    w_out, gain, w_router, x_far, x_near = refs[5 + blocks : 10 + blocks]
    scale, weight, hidden, raw, joined, ssq, logits = refs[10 + blocks :]
    step = pl.program_id(0)
    cols = w_out.shape[1]
    total = blocks * rows
    far_rows = far * rows
    experts_all = w_router.shape[0]
    chunk = min(512, total)

    @pl.when(step == 0)
    def _():
        start = 0
        for piece in pooled:
            raw[start : start + piece.shape[0], :] = piece[...]
            start += piece.shape[0]
        for b in range(blocks):
            place = pl.ds(pl.multiple_of(scalars[1 + b] * rows, rows), rows)
            joined[b * rows : (b + 1) * rows, :] = raw[place, :]
        ssq[...] = jnp.zeros_like(ssq)
        logits[...] = jnp.zeros_like(logits)

    g = gain[...].astype(jnp.float32)
    for c in range(0, total, chunk):
        end = min(c + chunk, total)
        proj = jnp.dot(joined[c:end, :latent], w_out[...], preferred_element_type=jnp.float32)
        for b in range(c // rows, end // rows):
            at = slice(b * rows, (b + 1) * rows)
            h = proj[b * rows - c : (b + 1) * rows - c] + resid[b][...].astype(jnp.float32)
            if b == far:
                hidden[...] = h
            scaled = (h * g).astype(jnp.bfloat16)
            if b < far:
                x_far[at, :] = scaled
            else:
                x_near[(b - far) * rows : (b - far + 1) * rows, :] = scaled
            sq = h * h
            part = sq[:, :LANES]
            for k in range(1, cols // LANES):
                part = part + sq[:, k * LANES : (k + 1) * LANES]
            ssq[at, :] += part
    nt = (((1,), (1,)), ((), ()))
    for x, at in ((x_far, slice(0, far_rows)), (x_near, slice(far_rows, total))):
        logits[at, :] += lax.dot_general(
            x[...], w_router[...], nt, preferred_element_type=jnp.float32
        )

    @pl.when(step == pl.num_programs(0) - 1)
    def _():
        mean = jnp.sum(ssq[...], axis=1, keepdims=True) * (1.0 / width)
        r = lax.rsqrt(mean + 1e-06)
        mask = joined[:, latent : latent + experts_all].astype(jnp.float32)
        affinity = jax.nn.sigmoid(logits[...] * r) * mask
        lane = lax.broadcasted_iota(jnp.int32, affinity.shape, 1)
        mine = jnp.sum(jnp.where(lane == scalars[0], affinity, 0.0), axis=1, keepdims=True)
        gate = 2.5 * mine / jnp.sum(affinity, axis=1, keepdims=True)
        scale[...] = jnp.broadcast_to(r, scale.shape)
        weight[...] = jnp.broadcast_to(gate, weight.shape)


def normalize(far, scalars, pooled, resid_blocks, w_out, gain, w_router_t):
    blocks = len(resid_blocks)
    rows, width = resid_blocks[0].shape
    latent = w_out.shape[0]
    total = blocks * rows
    cols = tile_of(width, 512)
    packed = pooled[0].shape[1]
    experts_all = w_router_t.shape[0]

    def whole(shape):
        return pl.BlockSpec(shape, lambda i: (0, 0), pipeline_mode=pl.Buffered(1))

    def tiles(height):
        return pl.BlockSpec((height, cols), lambda i: (0, i))

    need = total * (cols * 24 + packed * 6 + 8 * LANES * 4) + 4 * latent * cols
    return pl.pallas_call(
        lambda *refs: norm_kernel(far, blocks, rows, latent, width, *refs),
        grid=(width // cols,),
        in_specs=[pl.BlockSpec(memory_space=pltpu.SMEM)]
        + [whole(a.shape) for a in pooled]
        + [tiles(rows)] * blocks
        + [tiles(latent), tiles(1), tiles(experts_all)],
        out_shape=[
            jax.ShapeDtypeStruct((far * rows, width), jnp.bfloat16),
            jax.ShapeDtypeStruct((total - far * rows, width), jnp.bfloat16),
            jax.ShapeDtypeStruct((total, LANES), jnp.float32),
            jax.ShapeDtypeStruct((total, LANES), jnp.float32),
            jax.ShapeDtypeStruct((rows, width), jnp.float32),
        ],
        out_specs=[tiles(far * rows), tiles(total - far * rows)]
        + [whole((total, LANES)), whole((total, LANES)), tiles(rows)],
        scratch_shapes=[
            pltpu.VMEM((total, packed), jnp.bfloat16),
            pltpu.VMEM((total, packed), jnp.bfloat16),
            pltpu.VMEM((total, LANES), jnp.float32),
            pltpu.VMEM((total, experts_all), jnp.float32),
        ],
        compiler_params=pltpu.CompilerParams(
            dimension_semantics=("arbitrary",), vmem_limit_bytes=(int(need) // (1 << 20) + 6) << 20
        ),
        cost_estimate=pl.CostEstimate(
            flops=2 * total * width * latent,
            bytes_accessed=2 * total * width * 2 + latent * width * 2,
            transcendentals=total,
        ),
        name="normalize",
    )(scalars, *pooled, *resid_blocks, w_out, gain, w_router_t)


def attention(queries, new_lat, owned_cache, row_lengths, latent):
    step_count, row_count, kv_width = new_lat.shape
    context = owned_cache.shape[1]
    cache_scores = (
        jnp.einsum("srhk,rpk->srhp", queries, owned_cache, preferred_element_type=jnp.float32)
        * qk_scale
    )
    visible = jnp.arange(context)[None, :] < row_lengths[:, None]
    cache_scores = jnp.where(visible[None, :, None, :], cache_scores, -1e30)
    fresh_scores = (
        jnp.einsum("srhk,trk->srht", queries, new_lat, preferred_element_type=jnp.float32)
        * qk_scale
    )
    causal = jnp.arange(step_count)[:, None] >= jnp.arange(step_count)[None, :]
    fresh_scores = jnp.where(causal[:, None, None, :], fresh_scores, -1e30)
    scores = jnp.concatenate([cache_scores, fresh_scores], axis=-1)
    weights = jax.nn.softmax(scores, axis=-1).astype(jnp.bfloat16)
    pooled = jnp.einsum(
        "srhp,rpl->srl",
        weights[..., :context],
        owned_cache[..., :latent],
        preferred_element_type=jnp.float32,
    )
    pooled = pooled + jnp.einsum(
        "srht,trl->srl",
        weights[..., context:],
        new_lat[..., :latent],
        preferred_element_type=jnp.float32,
    )
    return pooled.astype(jnp.bfloat16)


def local(
    q_abs,
    new_lat,
    latent_cache,
    lengths,
    owner,
    resid,
    routes,
    w_out,
    norm_gain,
    w_router,
    w_gate,
    w_up,
    w_down,
):
    devices = lax.axis_size("expert")
    device_index = lax.axis_index("expert")
    step_count, row_count, width = resid.shape
    rows = step_count * row_count
    experts_all = w_router.shape[1]
    sharers = devices // experts_all
    chips = devices // 2
    half = chips // 2
    cut = rows // 2
    far, near = distances(chips)
    hold = lax.optimization_barrier
    sibling = sibling_perm(chips)

    def send(a, perm):
        return lax.ppermute(a, "expert", perm)

    to_right, to_left = shift_perm(chips, 1), shift_perm(chips, -1)

    def around(to_the_right, to_the_left):
        return send(to_the_right, to_right), send(to_the_left, to_left)

    wanted = (owner[:, None] == jnp.arange(owner.shape[0], dtype=jnp.int32)).astype(jnp.bfloat16)
    ordered = jnp.einsum(
        "jr,rpk->jpk", wanted, latent_cache, preferred_element_type=jnp.float32
    ).astype(jnp.bfloat16)
    owned_cache = lax.all_to_all(ordered, "expert", split_axis=0, concat_axis=1, tiled=True)

    mine = resid.reshape(rows, width)
    held, sib = {0: mine}, {}
    held[-1], held[1] = around(mine, mine)
    owner, lengths, routes, norm_gain, new_lat, held[-1], held[1] = hold(
        (owner, lengths, routes, norm_gain, new_lat, held[-1], held[1])
    )
    held[-2], held[2] = around(held[-1], held[1])
    sib[0] = send(mine, sibling)
    row_owner = lax.dynamic_slice_in_dim(owner, device_index * row_count, row_count)
    row_lengths = jnp.sum(
        jnp.where(
            row_owner[:, None] == jnp.arange(owner.shape[0], dtype=jnp.int32), lengths[None, :], 0
        ),
        axis=1,
    )
    routed = jnp.any(routes[..., None] == jnp.arange(LANES, dtype=jnp.int32), axis=2)
    routed = routed.astype(jnp.bfloat16)
    gain = norm_gain[None, :]
    scalars = jnp.array(
        [
            [device // sharers] + places
            for chip, places in enumerate(gathered_place(chips))
            for device in (2 * chip, 2 * chip + 1)
        ],
        jnp.int32,
    )[device_index]
    queries = q_abs.reshape(step_count, row_count, -1, new_lat.shape[2])
    owned_cache, queries, row_lengths, routed, gain, scalars = hold(
        (owned_cache, queries, row_lengths, routed, gain, scalars)
    )
    pooled = attention(queries, new_lat, owned_cache, row_lengths, w_out.shape[0])
    packet = jnp.concatenate([pooled, routed], axis=2).reshape(rows, -1)
    packet, held[-2], held[2], sib[0] = hold((packet, held[-2], held[2], sib[0]))

    high, low = gather_steps(chips)
    along = [send(packet, step_perm(chips, i, 0)) for i in range(1, high)]
    for t in range(3, half):
        held[-t], held[t] = around(held[1 - t], held[t - 1])
    sib[-1], sib[1] = send(held[-1], sibling), send(held[1], sibling)
    along, held, sib = hold((along, held, sib))
    along = jnp.concatenate([packet] + along, axis=0)
    across = [send(along, step_perm(chips, 0, i)) for i in range(1, low)]
    last = around(held[1 - half][:cut], held[half - 1][cut:])
    for t in range(2, half):
        sib[-t], sib[t] = send(held[-t], sibling), send(held[t], sibling)
    along_sib = send(along, sibling)
    across, last, sib, along_sib = hold((across, last, sib, along_sib))
    held[half] = jnp.concatenate(last, axis=0)
    sib[half] = send(held[half], sibling)
    across = across[0] if low == 2 else jnp.concatenate(across, axis=0)

    f32 = jnp.float32
    x_far, x_near, scale, weight, hidden = normalize(
        2 * len(far),
        scalars,
        [along, across, along_sib, send(across, sibling)],
        [a[d] for part in (far, near) for a in (held, sib) for d in part],
        w_out,
        gain,
        w_router.T,
    )

    def product(a, w):
        return jnp.dot(a, w[0], preferred_element_type=f32)

    def activate(a, b, at):
        r, g = scale[at, :1], weight[at, :1]
        return (jax.nn.silu(a * r) * (b * r) * g).astype(jnp.bfloat16)

    cut_at = x_far.shape[0]
    sums = {}

    def swap(dists, y):
        return y, send(y[len(dists) * rows :], sibling)

    def add_up(dists, y, received):
        for i, d in enumerate(dists):
            at = slice(i * rows, (i + 1) * rows)
            sums[d] = y[at].astype(f32) + received[at].astype(f32)

    def both(right, left):
        return around(right.astype(jnp.bfloat16), left.astype(jnp.bfloat16))

    act = hold(activate(product(x_far, w_gate), product(x_far, w_up), slice(0, cut_at)))
    y, received = swap(far, product(act, w_down).astype(jnp.bfloat16))
    gated, y, received = hold((product(x_near, w_gate), y, received))
    add_up(far, y, received)
    right, left = both(sums[half][:cut], sums[half][cut:])
    act = activate(gated, product(x_near, w_up), slice(cut_at, None))
    act, right, left = hold((act, right, left))
    right = jnp.concatenate([right.astype(f32), jnp.zeros((rows - cut, width), f32)], axis=0)
    left = jnp.concatenate([jnp.zeros((cut, width), f32), left.astype(f32)], axis=0)
    right, left = both(sums[half - 1] + right, sums[1 - half] + left)
    y, received = swap(near, product(act, w_down).astype(jnp.bfloat16))
    y, received, right, left = hold((y, received, right, left))
    add_up(near, y, received)
    for t in range(half - 2, 0, -1):
        right, left = hold(both(sums[t] + right.astype(f32), sums[-t] + left.astype(f32)))
    mixed = hidden + sums[0] + right.astype(f32) + left.astype(f32)
    return mixed.astype(jnp.bfloat16).reshape(step_count, row_count, width)


def solution(mesh):
    return jax.shard_map(
        local,
        mesh=mesh,
        in_specs=(
            P(None, ("group", "expert"), None),
            P(None, ("group", "expert"), None),
            P("group", "expert", None),
            P("group"),
            P("group"),
            P(None, ("group", "expert"), None),
            P(None, ("group", "expert"), None),
            P(),
            P(),
            P(),
            P("expert", None, None),
            P("expert", None, None),
            P("expert", None, None),
        ),
        out_specs=P(None, ("group", "expert"), None),
        check_vma=False,
    )
```

time: 121 us -> 107 us (0.88)
  Pallas kernels: 26.5 us -> 7.23 us
  matrix products: 4.16 us -> 18.9 us
  starting transfers between devices: 38.1 us -> 31.3 us
  waiting for transfers between devices: 39.9 us -> 35.6 us
  local copies, waits for them, and re-layouts: 8.16 us -> 10.5 us
    pallas_call x1, Pallas kernels: 26.5 us -> 7.23 us  [normalize(): pl.pallas_call(lambda *refs: norm_kernel(far, blocks, rows, latent, width...]
    dot_general x0 -> x6, matrix products: none -> 12.9 us  [product(): return jnp.dot(a, w[0], preferred_element_type=f32)]
    ppermute x44 -> x32, starting transfers between devices: 31.8 us -> 25 us  [send(): return lax.ppermute(a, 'expert', perm)]
    ppermute x44 -> x32, waiting for transfers between devices: 37.1 us -> 33.9 us  [send(): return lax.ppermute(a, 'expert', perm)]
    dot_general x1, matrix products: 1.36 us -> 3.24 us  [attention(): jnp.einsum('srhk,trk->srht', queries, new_lat, preferred_element_type=jnp...]
    unnamed x42 -> x34, local copies, waits for them, and re-layouts: 0.13 us -> 1.66 us
    add x9 -> x0, other arithmetic: 1.32 us -> none  [local(): sums = [own[d][h].astype(f32) + got[d][h].astype(f32) for h in halves]]
  transfers between devices with their start and end apart: 45 -> 33, of which waited for: 24 -> 14; matrix products, arithmetic and copies ran while one was open for 12% -> 19% of each run, Pallas kernels for 0% -> 0%
where the time goes in v6:
time: 107 us
  waiting for transfers between devices  35.6 us (33%)
  starting transfers between devices  31.3 us (29%)
  matrix products  18.9 us (18%)
  local copies, waits for them, and re-layouts  10.5 us (10%)
  Pallas kernels  7.23 us (7%)
  other arithmetic  2.47 us (2%)
    ppermute x32, waiting for transfers between devices, send(): return lax.ppermute(a, 'expert', perm)  33.9 us
    ppermute x32, starting transfers between devices, send(): return lax.ppermute(a, 'expert', perm)  25 us
    dot_general x6, matrix products, product(): return jnp.dot(a, w[0], preferred_element_type=f32)  12.9 us
    pallas_call x1, Pallas kernels, normalize(): pl.pallas_call(lambda *refs: norm_kernel(far, blocks, rows, latent, width...  7.23 us
    all_to_all x1, starting transfers between devices, local(): lax.all_to_all(ordered, 'expert', split_axis=0, concat_axis=1, tiled=True)  6.29 us
    reshape x1, local copies, waits for them, and re-layouts, local(): queries = q_abs.reshape(step_count, row_count, -1, new_lat.shape[2])  5.66 us
    dot_general x1, matrix products, attention(): jnp.einsum('srhk,trk->srht', queries, new_lat, preferred_element_type=jnp...  3.24 us
  transfers between devices with their start and end apart: 33, of which 14 were waited for; matrix products, arithmetic and copies ran while one was open for 19% of the time, Pallas kernels for 0%

profile of v6, /device:TPU:0, one launch (start us, length us, event | category | flops | bytes accessed | tf_op | source)
XLA Modules:
  0.0 106.6 jit_solution(11640535832052366248)
XLA Ops:
  0.5 2.6 %collective-permute-start.1 = (bf16[32,3584]{1,0:T(8,128)(2,1)}, bf16[32,3584]{1,0:T(8,128)(2,1)S(1)}, u32[]{:S(2)}, u32[]{:S(2)}) collective-permute-start(bf16[32,3584]{1,0:T(8,128)(2,1)} %bitcast.72), channel_id=1, source_target_pairs={{0,2},{1,3},{4,0},{5,1},{8,4},{9,5},{12,8},{13,9},{14,12},{15,13},... | collective-permute-start | bytes 688136 | tf_op jit(solution)/shard_map/ppermute | solution.py:246
  3.2 1.0 convolution_convert_fusion
  4.2 1.3 %copy.36 = bf16[128,2,576]{2,1,0:T(2,128)(2,1)} copy(bf16[128,2,576]{0,2,1:T(8,128)(2,1)S(1)} %convolution_convert_fusion) | data formatting | bytes 589824 | tf_op jit(solution)/shard_map/convert_element_type | solution.py:256
  5.4 6.3 %all-to-all-start = ((bf16[128,2,576]{2,1,0:T(2,128)(2,1)}), bf16[128,2,576]{2,1,0:T(2,128)(2,1)S(1)}, u32[]{:S(2)}, u32[]{:S(2)}) async-start(bf16[128,2,576]{2,1,0:T(2,128)(2,1)} %copy.36), calls=%async_computation | async-start | bytes 655360 | tf_op jit(solution)/shard_map/all_to_all | solution.py:257
  11.8 5.7 %reshape.51 = bf16[4,8,64,576]{3,2,1,0:T(8,128)(2,1)} reshape(bf16[4,8,36864]{2,1,0:T(8,128)(2,1)} %param.14) | data formatting | bytes 4718592 | tf_op jit(solution)/shard_map/reshape | solution.py:285
  17.5 0.7 dynamic-slice_bitcast_fusion.refs_0_
  18.2 0.5 collective-permute-start.10
  18.6 1.7 %collective-permute-start.2 = (bf16[32,3584]{1,0:T(8,128)(2,1)S(1)}, bf16[32,3584]{1,0:T(8,128)(2,1)S(1)}, u32[]{:S(2)}, u32[]{:S(2)}) collective-permute-start(bf16[32,3584]{1,0:T(8,128)(2,1)S(1)} %collective-permute-done.refs_13_), channel_id=1, source_target_pairs={{0,4},{1,5},{4,8},{5,9},{8,12},{9,13},{12,14},{13,15},{14,10},{15,... | collective-permute-start | bytes 688136 | tf_op jit(solution)/shard_map/ppermute | solution.py:246
  21.1 1.7 %all-to-all-done = bf16[128,2,576]{2,1,0:T(2,128)(2,1)S(1)} async-done(((bf16[128,2,576]{2,1,0:T(2,128)(2,1)}), bf16[128,2,576]{2,1,0:T(2,128)(2,1)S(1)}, u32[]{:S(2)}, u32[]{:S(2)}) %all-to-all-start) | async-done | bytes 294944 | tf_op jit(solution)/shard_map/all_to_all | solution.py:257
  23.6 3.2 %fusion.69 = (f32[4,8,64]{2,0,1:T(4,128)S(1)}, f32[4,8,64,4]{2,3,0,1:T(4,128)S(1)}) fusion(bf16[4,8,64,576]{3,2,1,0:T(8,128)(2,1)} %reshape.51, bf16[4,8,576,1]{2,1,0,3:T(8,128)(2,1)S(1)} %bitcast.81, pred[4,4]{1,0:T(4,128)(4,1)S(1)} %iota_compare_fusion.4), kind=kOutput, calls=%fused_computation.79 | convolution fusion | flops 9459712 | bytes 2437136 | tf_op jit(solution)/shard_map/srhk,trk->srht/dot_general | solution.py:195
  26.9 1.5 %fusion.68 = (f32[4,8,64]{2,0,1:T(4,128)S(1)}, f32[4,8,64,32]{2,3,0,1:T(8,128)S(1)}) fusion(bf16[4,8,64,576]{3,2,1,0:T(8,128)(2,1)S(1)} %copy-done.4, bf16[8,32,576]{2,1,0:T(8,128)(2,1)S(1)} %all_to_all.16, pred[8,32]{1,0:T(8,128)(4,1)S(1)} %iota_compare_fusion.2), kind=kOutput, calls=%fused_computation.78 | convolution fusion | flops 75692032 | bytes 2924800 | tf_op jit(solution)/shard_map/srhk,rpk->srhp/dot_general | solution.py:189
  29.9 1.8 %collective-permute-start.9 = (bf16[32,3584]{1,0:T(8,128)(2,1)S(1)}, bf16[32,3584]{1,0:T(8,128)(2,1)S(1)}, u32[]{:S(2)}, u32[]{:S(2)}) collective-permute-start(bf16[32,3584]{1,0:T(8,128)(2,1)S(1)} %collective-permute-done.3.refs_14_), channel_id=1, source_target_pairs={{0,2},{1,3},{4,0},{5,1},{8,4},{9,5},{12,8},{13,9},{14,12},{15,13},... | collective-permute-start | bytes 688136 | tf_op jit(solution)/shard_map/ppermute | solution.py:246
  31.9 2.3 %collective-permute-start.6 = (bf16[32,640]{1,0:T(8,128)(2,1)S(1)}, bf16[32,640]{1,0:T(8,128)(2,1)S(1)}, u32[]{:S(2)}, u32[]{:S(2)}) collective-permute-start(bf16[32,640]{1,0:T(8,128)(2,1)S(1)} %bitcast.78), channel_id=1, source_target_pairs={{0,8},{1,9},{2,10},{3,11},{4,12},{5,13},{6,14},{7,15},{8,0},{9,1},... | collective-permute-start | bytes 122888 | tf_op jit(solution)/shard_map/ppermute | solution.py:246
  34.2 1.7 %collective-permute-start.5 = (bf16[32,640]{1,0:T(8,128)(2,1)S(1)}, bf16[32,640]{1,0:T(8,128)(2,1)S(1)}, u32[]{:S(2)}, u32[]{:S(2)}) collective-permute-start(bf16[32,640]{1,0:T(8,128)(2,1)S(1)} %bitcast.79), channel_id=1, source_target_pairs={{0,12},{1,13},{2,14},{3,15},{4,0},{5,1},{6,2},{7,3},{8,4},{9,5},{1... | collective-permute-start | bytes 122888 | tf_op jit(solution)/shard_map/ppermute | solution.py:246
  36.0 4.7 %collective-permute-done.7 = bf16[32,640]{1,0:T(8,128)(2,1)S(1)} collective-permute-done((bf16[32,640]{1,0:T(8,128)(2,1)S(1)}, bf16[32,640]{1,0:T(8,128)(2,1)S(1)}, u32[]{:S(2)}, u32[]{:S(2)}) %collective-permute-start.7) | collective-permute-done | bytes 40992 | tf_op jit(solution)/shard_map/ppermute | solution.py:246
  40.7 0.8 collective-permute-start.14
  41.5 1.3 %collective-permute-start.13 = (bf16[16,3584]{1,0:T(8,128)(2,1)S(1)}, bf16[16,3584]{1,0:T(8,128)(2,1)S(1)}, u32[]{:S(2)}, u32[]{:S(2)}) collective-permute-start(bf16[16,3584]{1,0:T(8,128)(2,1)S(1)} %slice.96), channel_id=1, source_target_pairs={{0,4},{1,5},{4,8},{5,9},{8,12},{9,13},{12,14},{13,15},{14,10},{15,... | collective-permute-start | bytes 344072 | tf_op jit(solution)/shard_map/ppermute | solution.py:246
  42.9 0.5 collective-permute-start.15
  43.5 2.1 %collective-permute-done.14 = bf16[16,3584]{1,0:T(8,128)(2,1)S(1)} collective-permute-done((bf16[16,3584]{1,0:T(8,128)(2,1)S(1)}, bf16[16,3584]{1,0:T(8,128)(2,1)S(1)}, u32[]{:S(2)}, u32[]{:S(2)}) %collective-permute-start.14) | collective-permute-done | bytes 114720 | tf_op jit(solution)/shard_map/ppermute | solution.py:246
  45.6 0.7 collective-permute-done.13
  46.3 1.0 collective-permute-start.12
  47.3 5.6 %collective-permute-done.12.refs_2_ = bf16[128,640]{1,0:T(8,128)(2,1)S(1)} collective-permute-done((bf16[128,640]{1,0:T(8,128)(2,1)S(1)}, bf16[128,640]{1,0:T(8,128)(2,1)S(1)}, u32[]{:S(2)}, u32[]{:S(2)}) %collective-permute-start.12) | collective-permute-done | bytes 163872 | tf_op jit(solution)/shard_map/ppermute | solution.py:246
  53.1 0.5 collective-permute-start.20
  53.6 1.2 %collective-permute-done.20.refs_4_ = bf16[128,640]{1,0:T(8,128)(2,1)S(1)} collective-permute-done((bf16[128,640]{1,0:T(8,128)(2,1)S(1)}, bf16[128,640]{1,0:T(8,128)(2,1)S(1)}, u32[]{:S(2)}, u32[]{:S(2)}) %collective-permute-start.20) | collective-permute-done | bytes 163872 | tf_op jit(solution)/shard_map/ppermute | solution.py:246
  54.8 7.2 %normalize.1 = (bf16[192,3584]{1,0:T(8,128)(2,1)S(1)}, bf16[320,3584]{1,0:T(8,128)(2,1)S(1)}, f32[512,128]{1,0:T(8,128)S(1)}, f32[512,128]{1,0:T(8,128)S(1)}, f32[32,3584]{1,0:T(8,128)S(1)}) custom-call(s32[17]{0:T(128)S(1)} %dynamic-slice_bitcast_fusion.refs_0_, bf16[128,640]{1,0:T(8,128)(2,1)S(1)} %constant_dynamic-update-slice_fusion.refs_1_, ...), custom_call_target="tpu_custom_call" | custom-call | flops 1879048192 | bytes 11010048 | tf_op jit(solution)/shard_map/normalize/pallas_call | solution.py:151
  62.4 1.7 %fusion.25 = f32[192,1024]{1,0:T(8,128)S(1)} fusion(bf16[192,3584]{1,0:T(8,128)(2,1)S(1)} %get-tuple-element.108, bf16[1,3584,1024]{2,1,0:T(8,128)(2,1)S(1)} %copy-done.9, f32[192]{0:T(256)S(1)} %get-tuple-element.140), kind=kOutput, calls=%fused_computation.20 | convolution fusion | flops 1409482752 | bytes 9503488 | tf_op jit(solution)/shard_map/dot_general | solution.py:322
  64.2 1.1 %slice-done.1 = s8[3145728]{0:T(1024)(128)(4,1)S(1)} async-done(((s8[7340032]{0:T(1024)(128)(4,1)}), s8[3145728]{0:T(1024)(128)(4,1)S(1)}, s32[]{:S(2)}) %slice-start.1) | async-done | bytes 3145752
  65.3 1.8 %multiply_convert_fusion.1 = bf16[192,1024]{1,0:T(8,128)(2,1)S(1)} fusion(f32[192,1024]{1,0:T(8,128)S(1)} %fusion.25, f32[192]{0:T(256)S(1)} %get-tuple-element.139, f32[192]{0:T(256)S(1)} %get-tuple-element.140, bf16[192,3584]{1,0:T(8,128)(2,1)S(1)} %get-tuple-element.108, bf16[1,3584,1024]{2,1,0:T(8,128)(2,1)S(1)} %bitcast.83), kind=kOutput, calls=%fused_computation.32 | convolution fusion | flops 1410859008 | bytes 9897472 | tf_op jit(solution)/shard_map/dot_general | solution.py:322
  67.5 1.6 %fusion.15 = bf16[192,3584]{1,0:T(8,128)(2,1)S(1)} fusion(bf16[192,1024]{1,0:T(8,128)(2,1)S(1)} %multiply_convert_fusion.1, bf16[1,1024,3584]{2,1,0:T(8,128)(2,1)S(1)} %bitcast.85), kind=kOutput, calls=%fused_computation.13 | convolution fusion | flops 1409974272 | bytes 9109504 | tf_op jit(solution)/shard_map/dot_general | solution.py:322
  69.4 2.5 %fusion.10 = f32[320,1024]{1,0:T(8,128)S(1)} fusion(bf16[320,3584]{1,0:T(8,128)(2,1)S(1)} %get-tuple-element.107, bf16[1,3584,1024]{2,1,0:T(8,128)(2,1)S(1)} %copy-done.9), kind=kOutput, calls=%fused_computation.10 | convolution fusion | flops 2348810240 | bytes 10944512 | tf_op jit(solution)/shard_map/dot_general | solution.py:322
  72.1 1.0 collective-permute-start.24
  73.1 1.0 collective-permute-start.23
  74.2 2.7 %multiply_convert_fusion = bf16[320,1024]{1,0:T(8,128)(2,1)S(1)} fusion(f32[320,1024]{1,0:T(8,128)S(1)} %fusion.10, f32[320]{0:T(512)S(1)} %get-tuple-element.137, f32[320]{0:T(512)S(1)} %get-tuple-element.138, bf16[320,3584]{1,0:T(8,128)(2,1)S(1)} %get-tuple-element.107, bf16[1,3584,1024]{2,1,0:T(8,128)(2,1)S(1)} %bitcast.83), kind=kOutput, calls=%fused_computation.19 | convolution fusion | flops 2351759360 | bytes 11602432 | tf_op jit(solution)/shard_map/dot_general | solution.py:322
  76.9 0.6 collective-permute-done.24
  77.5 0.7 collective-permute-done.23
  78.2 2.5 %fusion.12 = bf16[320,3584]{1,0:T(8,128)(2,1)S(1)} fusion(bf16[320,1024]{1,0:T(8,128)(2,1)S(1)} %multiply_convert_fusion, bf16[1,1024,3584]{2,1,0:T(8,128)(2,1)S(1)} %bitcast.85), kind=kOutput, calls=%fused_computation.12 | convolution fusion | flops 2349957120 | bytes 10289152 | tf_op jit(solution)/shard_map/dot_general | solution.py:322
  81.1 1.5 %collective-permute-start.27 = (bf16[32,3584]{1,0:T(8,128)(2,1)S(1)}, bf16[32,3584]{1,0:T(8,128)(2,1)S(1)}, u32[]{:S(2)}, u32[]{:S(2)}) collective-permute-start(bf16[32,3584]{1,0:T(8,128)(2,1)S(1)} %get-tuple-element.129), channel_id=1, source_target_pairs={{0,2},{1,3},{4,0},{5,1},{8,4},{9,5},{12,8},{13,9},{14,12},{15,13},... | collective-permute-start | bytes 688136 | tf_op jit(solution)/shard_map/ppermute | solution.py:246
  82.6 0.6 collective-permute-start.26
  83.1 6.0 %collective-permute-done.27 = bf16[32,3584]{1,0:T(8,128)(2,1)S(1)} collective-permute-done((bf16[32,3584]{1,0:T(8,128)(2,1)S(1)}, bf16[32,3584]{1,0:T(8,128)(2,1)S(1)}, u32[]{:S(2)}, u32[]{:S(2)}) %collective-permute-start.27) | collective-permute-done | bytes 229408 | tf_op jit(solution)/shard_map/ppermute | solution.py:246
  89.1 1.2 %collective-permute-done.26 = bf16[32,3584]{1,0:T(8,128)(2,1)S(1)} collective-permute-done((bf16[32,3584]{1,0:T(8,128)(2,1)S(1)}, bf16[32,3584]{1,0:T(8,128)(2,1)S(1)}, u32[]{:S(2)}, u32[]{:S(2)}) %collective-permute-start.26) | collective-permute-done | bytes 229408 | tf_op jit(solution)/shard_map/ppermute | solution.py:246
  90.5 1.8 %collective-permute-start.29 = (bf16[32,3584]{1,0:T(8,128)(2,1)S(1)}, bf16[32,3584]{1,0:T(8,128)(2,1)S(1)}, u32[]{:S(2)}, u32[]{:S(2)}) collective-permute-start(bf16[32,3584]{1,0:T(8,128)(2,1)S(1)} %get-tuple-element.127), channel_id=1, source_target_pairs={{0,2},{1,3},{4,0},{5,1},{8,4},{9,5},{12,8},{13,9},{14,12},{15,13},... | collective-permute-start | bytes 688136 | tf_op jit(solution)/shard_map/ppermute | solution.py:246
  92.6 4.9 %collective-permute-done.29 = bf16[32,3584]{1,0:T(8,128)(2,1)S(1)} collective-permute-done((bf16[32,3584]{1,0:T(8,128)(2,1)S(1)}, bf16[32,3584]{1,0:T(8,128)(2,1)S(1)}, u32[]{:S(2)}, u32[]{:S(2)}) %collective-permute-start.29) | collective-permute-done | bytes 229408 | tf_op jit(solution)/shard_map/ppermute | solution.py:246
  97.4 1.5 %collective-permute-done.28 = bf16[32,3584]{1,0:T(8,128)(2,1)S(1)} collective-permute-done((bf16[32,3584]{1,0:T(8,128)(2,1)S(1)}, bf16[32,3584]{1,0:T(8,128)(2,1)S(1)}, u32[]{:S(2)}, u32[]{:S(2)}) %collective-permute-start.28) | collective-permute-done | bytes 229408 | tf_op jit(solution)/shard_map/ppermute | solution.py:246
  99.1 0.7 collective-permute-start.31
  99.7 1.4 %collective-permute-start.30 = (bf16[32,3584]{1,0:T(8,128)(2,1)S(1)}, bf16[32,3584]{1,0:T(8,128)(2,1)S(1)}, u32[]{:S(2)}, u32[]{:S(2)}) collective-permute-start(bf16[32,3584]{1,0:T(8,128)(2,1)S(1)} %get-tuple-element.126), channel_id=1, source_target_pairs={{0,4},{1,5},{4,8},{5,9},{8,12},{9,13},{12,14},{13,15},{14,10},{15,... | collective-permute-start | bytes 688136 | tf_op jit(solution)/shard_map/ppermute | solution.py:246
  101.2 4.0 %collective-permute-done.31 = bf16[32,3584]{1,0:T(8,128)(2,1)S(1)} collective-permute-done((bf16[32,3584]{1,0:T(8,128)(2,1)S(1)}, bf16[32,3584]{1,0:T(8,128)(2,1)S(1)}, u32[]{:S(2)}, u32[]{:S(2)}) %collective-permute-start.31) | collective-permute-done | bytes 229408 | tf_op jit(solution)/shard_map/ppermute | solution.py:246
  105.2 0.6 collective-permute-done.30
  105.8 0.8 fusion.60
  (101 shorter events, 6.2 us)
Async XLA Ops:
  0.0 3.2 %copy-start = (bf16[128,2,576]{0,2,1:T(8,128)(2,1)S(1)}, bf16[128,2,576]{0,2,1:T(8,128)(2,1)}, u32[]{:S(2)}) copy-start(bf16[128,2,576]{0,2,1:T(8,128)(2,1)} %param.16) | copy-start | bytes 884740
  0.0 29.5 %collective-permute-start.4 = (bf16[32,3584]{1,0:T(8,128)(2,1)}, bf16[32,3584]{1,0:T(8,128)(2,1)S(1)}, u32[]{:S(2)}, u32[]{:S(2)}) collective-permute-start(bf16[32,3584]{1,0:T(8,128)(2,1)} %bitcast.71), channel_id=1, source_target_pairs={{0,1},{1,0},{2,3},{3,2},{4,5},{5,4},{6,7},{7,6},{8,9},{9,8},{10,11... | collective-permute-start | bytes 688136 | tf_op jit(solution)/shard_map/ppermute | solution.py:246
  0.5 17.7 %collective-permute-start.1 = (bf16[32,3584]{1,0:T(8,128)(2,1)}, bf16[32,3584]{1,0:T(8,128)(2,1)S(1)}, u32[]{:S(2)}, u32[]{:S(2)}) collective-permute-start(bf16[32,3584]{1,0:T(8,128)(2,1)} %bitcast.72), channel_id=1, source_target_pairs={{0,2},{1,3},{4,0},{5,1},{8,4},{9,5},{12,8},{13,9},{14,12},{15,13},... | collective-permute-start | bytes 688136 | tf_op jit(solution)/shard_map/ppermute | solution.py:246
  3.0 15.1 %collective-permute-start = (bf16[32,3584]{1,0:T(8,128)(2,1)}, bf16[32,3584]{1,0:T(8,128)(2,1)S(1)}, u32[]{:S(2)}, u32[]{:S(2)}) collective-permute-start(bf16[32,3584]{1,0:T(8,128)(2,1)} %bitcast.73), channel_id=1, source_target_pairs={{0,4},{1,5},{4,8},{5,9},{8,12},{9,13},{12,14},{13,15},{14,10},{15,... | collective-permute-start | bytes 688136 | tf_op jit(solution)/shard_map/ppermute | solution.py:246
  5.4 17.4 %all-to-all-start = ((bf16[128,2,576]{2,1,0:T(2,128)(2,1)}), bf16[128,2,576]{2,1,0:T(2,128)(2,1)S(1)}, u32[]{:S(2)}, u32[]{:S(2)}) async-start(bf16[128,2,576]{2,1,0:T(2,128)(2,1)} %copy.36), calls=%async_computation | async-start | bytes 655360 | tf_op jit(solution)/shard_map/all_to_all | solution.py:257
  11.8 8.9 %copy-start.7 = (bf16[3584]{0:T(1024)(128)(2,1)S(1)}, bf16[3584]{0:T(1024)(128)(2,1)}, u32[]{:S(2)}) copy-start(bf16[3584]{0:T(1024)(128)(2,1)} %param.22) | copy-start | bytes 21508
  11.8 8.9 %copy-start.5 = (bf16[4,8,576]{2,1,0:T(8,128)(2,1)S(1)}, bf16[4,8,576]{2,1,0:T(8,128)(2,1)}, u32[]{:S(2)}) copy-start(bf16[4,8,576]{2,1,0:T(8,128)(2,1)} %param.15) | copy-start | bytes 110596
  11.8 9.0 %copy-start.8 = (s32[128]{0:T(128)S(1)}, s32[128]{0:T(128)}, u32[]{:S(2)}) copy-start(s32[128]{0:T(128)} %param.18) | copy-start | bytes 1540
  11.8 9.0 %copy-start.10 = (s32[128]{0:T(128)S(1)}, s32[128]{0:T(128)}, u32[]{:S(2)}) copy-start(s32[128]{0:T(128)} %param.17) | copy-start | bytes 1540
  11.8 9.2 %copy-start.6 = (s32[4,8,8]{2,1,0:T(8,128)S(1)}, s32[4,8,8]{2,1,0:T(8,128)}, u32[]{:S(2)}) copy-start(s32[4,8,8]{2,1,0:T(8,128)} %param.20) | copy-start | bytes 3076
  18.2 13.7 %collective-permute-start.10 = (bf16[32,3584]{1,0:T(8,128)(2,1)S(1)}, bf16[32,3584]{1,0:T(8,128)(2,1)S(1)}, u32[]{:S(2)}, u32[]{:S(2)}) collective-permute-start(bf16[32,3584]{1,0:T(8,128)(2,1)S(1)} %collective-permute-done.refs_13_), channel_id=1, source_target_pairs={{0,1},{1,0},{2,3},{3,2},{4,5},{5,4},{6,7},{7,6},{8,9},{9,8},{10,11... | collective-permute-start | bytes 688136 | tf_op jit(solution)/shard_map/ppermute | solution.py:246
  18.6 10.9 %collective-permute-start.2 = (bf16[32,3584]{1,0:T(8,128)(2,1)S(1)}, bf16[32,3584]{1,0:T(8,128)(2,1)S(1)}, u32[]{:S(2)}, u32[]{:S(2)}) collective-permute-start(bf16[32,3584]{1,0:T(8,128)(2,1)S(1)} %collective-permute-done.refs_13_), channel_id=1, source_target_pairs={{0,4},{1,5},{4,8},{5,9},{8,12},{9,13},{12,14},{13,15},{14,10},{15,... | collective-permute-start | bytes 688136 | tf_op jit(solution)/shard_map/ppermute | solution.py:246
  20.3 13.9 %collective-permute-start.11 = (bf16[32,3584]{1,0:T(8,128)(2,1)S(1)}, bf16[32,3584]{1,0:T(8,128)(2,1)S(1)}, u32[]{:S(2)}, u32[]{:S(2)}) collective-permute-start(bf16[32,3584]{1,0:T(8,128)(2,1)S(1)} %collective-permute-done.1.refs_12_), channel_id=1, source_target_pairs={{0,1},{1,0},{2,3},{3,2},{4,5},{5,4},{6,7},{7,6},{8,9},{9,8},{10,11... | collective-permute-start | bytes 688136 | tf_op jit(solution)/shard_map/ppermute | solution.py:246
  20.4 9.1 %collective-permute-start.3 = (bf16[32,3584]{1,0:T(8,128)(2,1)S(1)}, bf16[32,3584]{1,0:T(8,128)(2,1)S(1)}, u32[]{:S(2)}, u32[]{:S(2)}) collective-permute-start(bf16[32,3584]{1,0:T(8,128)(2,1)S(1)} %collective-permute-done.1.refs_12_), channel_id=1, source_target_pairs={{0,2},{1,3},{4,0},{5,1},{8,4},{9,5},{12,8},{13,9},{14,12},{15,13},... | collective-permute-start | bytes 688136 | tf_op jit(solution)/shard_map/ppermute | solution.py:246
  23.5 3.3 %copy-start.4 = (bf16[4,8,64,576]{3,2,1,0:T(8,128)(2,1)S(1)}, bf16[4,8,64,576]{3,2,1,0:T(8,128)(2,1)}, u32[]{:S(2)}) copy-start(bf16[4,8,64,576]{3,2,1,0:T(8,128)(2,1)} %reshape.51) | copy-start | bytes 7077892
  26.9 27.9 %copy-start.2 = (bf16[4,8,3584]{2,1,0:T(8,128)(2,1)S(1)}, bf16[4,8,3584]{2,1,0:T(8,128)(2,1)}, u32[]{:S(2)}) copy-start(bf16[4,8,3584]{2,1,0:T(8,128)(2,1)} %param.19) | copy-start | bytes 688132
  28.4 26.4 %copy-start.1 = (bf16[512,3584]{1,0:T(8,128)(2,1)S(1)}, bf16[512,3584]{1,0:T(8,128)(2,1)}, u32[]{:S(2)}) copy-start(bf16[512,3584]{1,0:T(8,128)(2,1)} %refs_21_.1) | copy-start | bytes 11010052
  28.4 26.4 %copy-start.3 = (bf16[3584,16]{0,1:T(8,128)(2,1)S(1)}, bf16[3584,16]{0,1:T(8,128)(2,1)}, u32[]{:S(2)}) copy-start(bf16[3584,16]{0,1:T(8,128)(2,1)} %param.23) | copy-start | bytes 344068
  29.6 11.1 %collective-permute-start.8 = (bf16[32,3584]{1,0:T(8,128)(2,1)S(1)}, bf16[32,3584]{1,0:T(8,128)(2,1)S(1)}, u32[]{:S(2)}, u32[]{:S(2)}) collective-permute-start(bf16[32,3584]{1,0:T(8,128)(2,1)S(1)} %collective-permute-done.2.refs_15_), channel_id=1, source_target_pairs={{0,4},{1,5},{4,8},{5,9},{8,12},{9,13},{12,14},{13,15},{14,10},{15,... | collective-permute-start | bytes 688136 | tf_op jit(solution)/shard_map/ppermute | solution.py:246
  29.9 10.8 %collective-permute-start.9 = (bf16[32,3584]{1,0:T(8,128)(2,1)S(1)}, bf16[32,3584]{1,0:T(8,128)(2,1)S(1)}, u32[]{:S(2)}, u32[]{:S(2)}) collective-permute-start(bf16[32,3584]{1,0:T(8,128)(2,1)S(1)} %collective-permute-done.3.refs_14_), channel_id=1, source_target_pairs={{0,2},{1,3},{4,0},{5,1},{8,4},{9,5},{12,8},{13,9},{14,12},{15,13},... | collective-permute-start | bytes 688136 | tf_op jit(solution)/shard_map/ppermute | solution.py:246
  31.6 9.1 %collective-permute-start.7 = (bf16[32,640]{1,0:T(8,128)(2,1)S(1)}, bf16[32,640]{1,0:T(8,128)(2,1)S(1)}, u32[]{:S(2)}, u32[]{:S(2)}) collective-permute-start(bf16[32,640]{1,0:T(8,128)(2,1)S(1)} %bitcast.77), channel_id=1, source_target_pairs={{0,4},{1,5},{2,6},{3,7},{4,8},{5,9},{6,10},{7,11},{8,12},{9,13},{1... | collective-permute-start | bytes 122888 | tf_op jit(solution)/shard_map/ppermute | solution.py:246
  31.9 8.8 %collective-permute-start.6 = (bf16[32,640]{1,0:T(8,128)(2,1)S(1)}, bf16[32,640]{1,0:T(8,128)(2,1)S(1)}, u32[]{:S(2)}, u32[]{:S(2)}) collective-permute-start(bf16[32,640]{1,0:T(8,128)(2,1)S(1)} %bitcast.78), channel_id=1, source_target_pairs={{0,8},{1,9},{2,10},{3,11},{4,12},{5,13},{6,14},{7,15},{8,0},{9,1},... | collective-permute-start | bytes 122888 | tf_op jit(solution)/shard_map/ppermute | solution.py:246
  34.2 6.5 %collective-permute-start.5 = (bf16[32,640]{1,0:T(8,128)(2,1)S(1)}, bf16[32,640]{1,0:T(8,128)(2,1)S(1)}, u32[]{:S(2)}, u32[]{:S(2)}) collective-permute-start(bf16[32,640]{1,0:T(8,128)(2,1)S(1)} %bitcast.79), channel_id=1, source_target_pairs={{0,12},{1,13},{2,14},{3,15},{4,0},{5,1},{6,2},{7,3},{8,4},{9,5},{1... | collective-permute-start | bytes 122888 | tf_op jit(solution)/shard_map/ppermute | solution.py:246
  40.7 4.8 %collective-permute-start.14 = (bf16[16,3584]{1,0:T(8,128)(2,1)S(1)}, bf16[16,3584]{1,0:T(8,128)(2,1)S(1)}, u32[]{:S(2)}, u32[]{:S(2)}) collective-permute-start(bf16[16,3584]{1,0:T(8,128)(2,1)S(1)} %slice.97), channel_id=1, source_target_pairs={{0,2},{1,3},{4,0},{5,1},{8,4},{9,5},{12,8},{13,9},{14,12},{15,13},... | collective-permute-start | bytes 344072 | tf_op jit(solution)/shard_map/ppermute | solution.py:246
  41.5 4.8 %collective-permute-start.13 = (bf16[16,3584]{1,0:T(8,128)(2,1)S(1)}, bf16[16,3584]{1,0:T(8,128)(2,1)S(1)}, u32[]{:S(2)}, u32[]{:S(2)}) collective-permute-start(bf16[16,3584]{1,0:T(8,128)(2,1)S(1)} %slice.96), channel_id=1, source_target_pairs={{0,4},{1,5},{4,8},{5,9},{8,12},{9,13},{12,14},{13,15},{14,10},{15,... | collective-permute-start | bytes 344072 | tf_op jit(solution)/shard_map/ppermute | solution.py:246
  42.9 3.5 %collective-permute-start.19 = (bf16[128,640]{1,0:T(8,128)(2,1)S(1)}, bf16[128,640]{1,0:T(8,128)(2,1)S(1)}, u32[]{:S(2)}, u32[]{:S(2)}) collective-permute-start(bf16[128,640]{1,0:T(8,128)(2,1)S(1)} %constant_dynamic-update-slice_fusion.refs_1_), channel_id=1, source_target_pairs={{0,1},{1,0},{2,3},{3,2},{4,5},{5,4},{6,7},{7,6},{8,9},{9,8},{10,11... | collective-permute-start | bytes 491528 | tf_op jit(solution)/shard_map/ppermute | solution.py:246
  42.9 10.0 %collective-permute-start.15 = (bf16[32,3584]{1,0:T(8,128)(2,1)S(1)}, bf16[32,3584]{1,0:T(8,128)(2,1)S(1)}, u32[]{:S(2)}, u32[]{:S(2)}) collective-permute-start(bf16[32,3584]{1,0:T(8,128)(2,1)S(1)} %collective-permute-done.8.refs_7_), channel_id=1, source_target_pairs={{0,1},{1,0},{2,3},{3,2},{4,5},{5,4},{6,7},{7,6},{8,9},{9,8},{10,11... | collective-permute-start | bytes 688136 | tf_op jit(solution)/shard_map/ppermute | solution.py:246
  43.4 9.5 %collective-permute-start.16 = (bf16[32,3584]{1,0:T(8,128)(2,1)S(1)}, bf16[32,3584]{1,0:T(8,128)(2,1)S(1)}, u32[]{:S(2)}, u32[]{:S(2)}) collective-permute-start(bf16[32,3584]{1,0:T(8,128)(2,1)S(1)} %collective-permute-done.2.refs_15_), channel_id=1, source_target_pairs={{0,1},{1,0},{2,3},{3,2},{4,5},{5,4},{6,7},{7,6},{8,9},{9,8},{10,11... | collective-permute-start | bytes 688136 | tf_op jit(solution)/shard_map/ppermute | solution.py:246
  45.6 7.3 %collective-permute-start.17 = (bf16[32,3584]{1,0:T(8,128)(2,1)S(1)}, bf16[32,3584]{1,0:T(8,128)(2,1)S(1)}, u32[]{:S(2)}, u32[]{:S(2)}) collective-permute-start(bf16[32,3584]{1,0:T(8,128)(2,1)S(1)} %collective-permute-done.3.refs_14_), channel_id=1, source_target_pairs={{0,1},{1,0},{2,3},{3,2},{4,5},{5,4},{6,7},{7,6},{8,9},{9,8},{10,11... | collective-permute-start | bytes 688136 | tf_op jit(solution)/shard_map/ppermute | solution.py:246
  46.3 6.6 %collective-permute-start.18 = (bf16[32,3584]{1,0:T(8,128)(2,1)S(1)}, bf16[32,3584]{1,0:T(8,128)(2,1)S(1)}, u32[]{:S(2)}, u32[]{:S(2)}) collective-permute-start(bf16[32,3584]{1,0:T(8,128)(2,1)S(1)} %collective-permute-done.9.refs_6_), channel_id=1, source_target_pairs={{0,1},{1,0},{2,3},{3,2},{4,5},{5,4},{6,7},{7,6},{8,9},{9,8},{10,11... | collective-permute-start | bytes 688136 | tf_op jit(solution)/shard_map/ppermute | solution.py:246
  46.3 6.6 %collective-permute-start.12 = (bf16[128,640]{1,0:T(8,128)(2,1)S(1)}, bf16[128,640]{1,0:T(8,128)(2,1)S(1)}, u32[]{:S(2)}, u32[]{:S(2)}) collective-permute-start(bf16[128,640]{1,0:T(8,128)(2,1)S(1)} %constant_dynamic-update-slice_fusion.refs_1_), channel_id=1, source_target_pairs={{0,2},{1,3},{2,0},{3,1},{4,6},{5,7},{6,4},{7,5},{8,10},{9,11},{10,... | collective-permute-start | bytes 491528 | tf_op jit(solution)/shard_map/ppermute | solution.py:246
  53.0 1.8 %collective-permute-start.21 = (bf16[32,3584]{1,0:T(8,128)(2,1)S(1)}, bf16[32,3584]{1,0:T(8,128)(2,1)S(1)}, u32[]{:S(2)}, u32[]{:S(2)}) collective-permute-start(bf16[32,3584]{1,0:T(8,128)(2,1)S(1)} %constant_dynamic-update-slice_fusion.4.refs_5_), channel_id=1, source_target_pairs={{0,1},{1,0},{2,3},{3,2},{4,5},{5,4},{6,7},{7,6},{8,9},{9,8},{10,11... | collective-permute-start | bytes 688136 | tf_op jit(solution)/shard_map/ppermute | solution.py:246
  53.1 1.7 %collective-permute-start.20 = (bf16[128,640]{1,0:T(8,128)(2,1)S(1)}, bf16[128,640]{1,0:T(8,128)(2,1)S(1)}, u32[]{:S(2)}, u32[]{:S(2)}) collective-permute-start(bf16[128,640]{1,0:T(8,128)(2,1)S(1)} %collective-permute-done.12.refs_2_), channel_id=1, source_target_pairs={{0,1},{1,0},{2,3},{3,2},{4,5},{5,4},{6,7},{7,6},{8,9},{9,8},{10,11... | collective-permute-start | bytes 491528 | tf_op jit(solution)/shard_map/ppermute | solution.py:246
  54.8 7.6 %copy-start.9 = (bf16[1,3584,1024]{2,1,0:T(8,128)(2,1)S(1)}, bf16[1,3584,1024]{2,1,0:T(8,128)(2,1)}, u32[]{:S(2)}) copy-start(bf16[1,3584,1024]{2,1,0:T(8,128)(2,1)} %param.24) | copy-start | bytes 22020100
  62.1 2.2 %slice-start = ((s8[7340032]{0:T(1024)(128)(4,1)}), s8[4194304]{0:T(1024)(128)(4,1)S(1)}, s32[]{:S(2)}) async-start(s8[7340032]{0:T(1024)(128)(4,1)} %bitcast.82), calls=%async_computation.1 | async-start | bytes 8388608
  62.4 2.9 %slice-start.1 = ((s8[7340032]{0:T(1024)(128)(4,1)}), s8[3145728]{0:T(1024)(128)(4,1)S(1)}, s32[]{:S(2)}) async-start(s8[7340032]{0:T(1024)(128)(4,1)} %bitcast.82), calls=%async_computation.2 | async-start | bytes 6291456
  62.4 4.7 %slice-start.2 = ((s8[7340032]{0:T(1024)(128)(4,1)}), s8[4194304]{0:T(1024)(128)(4,1)S(1)}, s32[]{:S(2)}) async-start(s8[7340032]{0:T(1024)(128)(4,1)} %bitcast.84), calls=%async_computation.3 | async-start | bytes 8388608
  65.3 2.2 %slice-start.3 = ((s8[7340032]{0:T(1024)(128)(4,1)}), s8[3145728]{0:T(1024)(128)(4,1)S(1)}, s32[]{:S(2)}) async-start(s8[7340032]{0:T(1024)(128)(4,1)} %bitcast.84), calls=%async_computation.4 | async-start | bytes 6291456
  69.2 2.8 %collective-permute-start.22 = (bf16[96,3584]{1,0:T(8,128)(2,1)S(1)}, bf16[96,3584]{1,0:T(8,128)(2,1)S(1)}, u32[]{:S(2)}, u32[]{:S(2)}) collective-permute-start(bf16[96,3584]{1,0:T(8,128)(2,1)S(1)} %slice.125), channel_id=1, source_target_pairs={{0,1},{1,0},{2,3},{3,2},{4,5},{5,4},{6,7},{7,6},{8,9},{9,8},{10,11... | collective-permute-start | bytes 2064392 | tf_op jit(solution)/shard_map/ppermute | solution.py:246
  72.1 5.4 %collective-permute-start.24 = (bf16[16,3584]{1,0:T(8,128)(2,1)S(1)}, bf16[16,3584]{1,0:T(8,128)(2,1)S(1)}, u32[]{:S(2)}, u32[]{:S(2)}) collective-permute-start(bf16[16,3584]{1,0:T(8,128)(2,1)S(1)} %get-tuple-element.131), channel_id=1, source_target_pairs={{0,2},{1,3},{4,0},{5,1},{8,4},{9,5},{12,8},{13,9},{14,12},{15,13},... | collective-permute-start | bytes 344072 | tf_op jit(solution)/shard_map/ppermute | solution.py:246
  73.1 5.1 %collective-permute-start.23 = (bf16[16,3584]{1,0:T(8,128)(2,1)S(1)}, bf16[16,3584]{1,0:T(8,128)(2,1)S(1)}, u32[]{:S(2)}, u32[]{:S(2)}) collective-permute-start(bf16[16,3584]{1,0:T(8,128)(2,1)S(1)} %get-tuple-element.132), channel_id=1, source_target_pairs={{0,4},{1,5},{4,8},{5,9},{8,12},{9,13},{12,14},{13,15},{14,10},{15,... | collective-permute-start | bytes 344072 | tf_op jit(solution)/shard_map/ppermute | solution.py:246
  80.8 9.5 %collective-permute-start.25 = (bf16[160,3584]{1,0:T(8,128)(2,1)S(1)}, bf16[160,3584]{1,0:T(8,128)(2,1)S(1)}, u32[]{:S(2)}, u32[]{:S(2)}) collective-permute-start(bf16[160,3584]{1,0:T(8,128)(2,1)S(1)} %slice.128), channel_id=1, source_target_pairs={{0,1},{1,0},{2,3},{3,2},{4,5},{5,4},{6,7},{7,6},{8,9},{9,8},{10,11... | collective-permute-start | bytes 3440648 | tf_op jit(solution)/shard_map/ppermute | solution.py:246
  81.1 8.1 %collective-permute-start.27 = (bf16[32,3584]{1,0:T(8,128)(2,1)S(1)}, bf16[32,3584]{1,0:T(8,128)(2,1)S(1)}, u32[]{:S(2)}, u32[]{:S(2)}) collective-permute-start(bf16[32,3584]{1,0:T(8,128)(2,1)S(1)} %get-tuple-element.129), channel_id=1, source_target_pairs={{0,2},{1,3},{4,0},{5,1},{8,4},{9,5},{12,8},{13,9},{14,12},{15,13},... | collective-permute-start | bytes 688136 | tf_op jit(solution)/shard_map/ppermute | solution.py:246
  82.6 7.7 %collective-permute-start.26 = (bf16[32,3584]{1,0:T(8,128)(2,1)S(1)}, bf16[32,3584]{1,0:T(8,128)(2,1)S(1)}, u32[]{:S(2)}, u32[]{:S(2)}) collective-permute-start(bf16[32,3584]{1,0:T(8,128)(2,1)S(1)} %get-tuple-element.130), channel_id=1, source_target_pairs={{0,4},{1,5},{4,8},{5,9},{8,12},{9,13},{12,14},{13,15},{14,10},{15,... | collective-permute-start | bytes 688136 | tf_op jit(solution)/shard_map/ppermute | solution.py:246
  90.5 7.0 %collective-permute-start.29 = (bf16[32,3584]{1,0:T(8,128)(2,1)S(1)}, bf16[32,3584]{1,0:T(8,128)(2,1)S(1)}, u32[]{:S(2)}, u32[]{:S(2)}) collective-permute-start(bf16[32,3584]{1,0:T(8,128)(2,1)S(1)} %get-tuple-element.127), channel_id=1, source_target_pairs={{0,2},{1,3},{4,0},{5,1},{8,4},{9,5},{12,8},{13,9},{14,12},{15,13},... | collective-permute-start | bytes 688136 | tf_op jit(solution)/shard_map/ppermute | solution.py:246
  92.3 6.6 %collective-permute-start.28 = (bf16[32,3584]{1,0:T(8,128)(2,1)S(1)}, bf16[32,3584]{1,0:T(8,128)(2,1)S(1)}, u32[]{:S(2)}, u32[]{:S(2)}) collective-permute-start(bf16[32,3584]{1,0:T(8,128)(2,1)S(1)} %get-tuple-element.128), channel_id=1, source_target_pairs={{0,4},{1,5},{4,8},{5,9},{8,12},{9,13},{12,14},{13,15},{14,10},{15,... | collective-permute-start | bytes 688136 | tf_op jit(solution)/shard_map/ppermute | solution.py:246
  99.1 6.1 %collective-permute-start.31 = (bf16[32,3584]{1,0:T(8,128)(2,1)S(1)}, bf16[32,3584]{1,0:T(8,128)(2,1)S(1)}, u32[]{:S(2)}, u32[]{:S(2)}) collective-permute-start(bf16[32,3584]{1,0:T(8,128)(2,1)S(1)} %get-tuple-element.125), channel_id=1, source_target_pairs={{0,2},{1,3},{4,0},{5,1},{8,4},{9,5},{12,8},{13,9},{14,12},{15,13},... | collective-permute-start | bytes 688136 | tf_op jit(solution)/shard_map/ppermute | solution.py:246
  99.7 6.0 %collective-permute-start.30 = (bf16[32,3584]{1,0:T(8,128)(2,1)S(1)}, bf16[32,3584]{1,0:T(8,128)(2,1)S(1)}, u32[]{:S(2)}, u32[]{:S(2)}) collective-permute-start(bf16[32,3584]{1,0:T(8,128)(2,1)S(1)} %get-tuple-element.126), channel_id=1, source_target_pairs={{0,4},{1,5},{4,8},{5,9},{8,12},{9,13},{12,14},{13,15},{14,10},{15,... | collective-permute-start | bytes 688136 | tf_op jit(solution)/shard_map/ppermute | solution.py:246

commit v7 on v6

--- a/solution.py
+++ b/solution.py
@@ -69,16 +69,16 @@
     return max(t for t in range(LANES, min(size, most) + 1, LANES) if size % t == 0)
 
 
-def norm_kernel(far, blocks, rows, latent, width, *refs):
+def norm_kernel(first, blocks, rows, latent, width, with_hidden, *refs):
     scalars = refs[0]
     pooled = refs[1:5]
     resid = refs[5 : 5 + blocks]
-    w_out, gain, w_router, x_far, x_near = refs[5 + blocks : 10 + blocks]
-    scale, weight, hidden, raw, joined, ssq, logits = refs[10 + blocks :]
+    w_out, gain, w_router, x, scale, weight = refs[5 + blocks : 11 + blocks]
+    hidden = refs[11 + blocks] if with_hidden else None
+    raw, joined, ssq, logits = refs[-4:]
     step = pl.program_id(0)
     cols = w_out.shape[1]
     total = blocks * rows
-    far_rows = far * rows
     experts_all = w_router.shape[0]
     chunk = min(512, total)
 
@@ -89,7 +89,7 @@
             raw[start : start + piece.shape[0], :] = piece[...]
             start += piece.shape[0]
         for b in range(blocks):
-            place = pl.ds(pl.multiple_of(scalars[1 + b] * rows, rows), rows)
+            place = pl.ds(pl.multiple_of(scalars[first + b] * rows, rows), rows)
             joined[b * rows : (b + 1) * rows, :] = raw[place, :]
         ssq[...] = jnp.zeros_like(ssq)
         logits[...] = jnp.zeros_like(logits)
@@ -101,23 +101,17 @@
         for b in range(c // rows, end // rows):
             at = slice(b * rows, (b + 1) * rows)
             h = proj[b * rows - c : (b + 1) * rows - c] + resid[b][...].astype(jnp.float32)
-            if b == far:
+            if with_hidden and b == 0:
                 hidden[...] = h
-            scaled = (h * g).astype(jnp.bfloat16)
-            if b < far:
-                x_far[at, :] = scaled
-            else:
-                x_near[(b - far) * rows : (b - far + 1) * rows, :] = scaled
+            x[at, :] = (h * g).astype(jnp.bfloat16)
             sq = h * h
             part = sq[:, :LANES]
             for k in range(1, cols // LANES):
                 part = part + sq[:, k * LANES : (k + 1) * LANES]
             ssq[at, :] += part
-    nt = (((1,), (1,)), ((), ()))
-    for x, at in ((x_far, slice(0, far_rows)), (x_near, slice(far_rows, total))):
-        logits[at, :] += lax.dot_general(
-            x[...], w_router[...], nt, preferred_element_type=jnp.float32
-        )
+    logits[...] += lax.dot_general(
+        x[...], w_router[...], (((1,), (1,)), ((), ())), preferred_element_type=jnp.float32
+    )
 
     @pl.when(step == pl.num_programs(0) - 1)
     def _():
@@ -132,7 +126,7 @@
         weight[...] = jnp.broadcast_to(gate, weight.shape)
 
 
-def normalize(far, scalars, pooled, resid_blocks, w_out, gain, w_router_t):
+def normalize(first, with_hidden, scalars, pooled, w_out, gain, w_router_t, resid_blocks):
     blocks = len(resid_blocks)
     rows, width = resid_blocks[0].shape
     latent = w_out.shape[0]
@@ -147,25 +141,25 @@
     def tiles(height):
         return pl.BlockSpec((height, cols), lambda i: (0, i))
 
-    need = total * (cols * 24 + packed * 6 + 8 * LANES * 4) + 4 * latent * cols
+    gathered = sum(a.shape[0] for a in pooled)
+    need = total * (cols * 24 + packed * 2 + 8 * LANES * 4) + gathered * packed * 4 + 4 * latent * cols
     return pl.pallas_call(
-        lambda *refs: norm_kernel(far, blocks, rows, latent, width, *refs),
+        lambda *refs: norm_kernel(first, blocks, rows, latent, width, with_hidden, *refs),
         grid=(width // cols,),
         in_specs=[pl.BlockSpec(memory_space=pltpu.SMEM)]
         + [whole(a.shape) for a in pooled]
         + [tiles(rows)] * blocks
         + [tiles(latent), tiles(1), tiles(experts_all)],
         out_shape=[
-            jax.ShapeDtypeStruct((far * rows, width), jnp.bfloat16),
-            jax.ShapeDtypeStruct((total - far * rows, width), jnp.bfloat16),
+            jax.ShapeDtypeStruct((total, width), jnp.bfloat16),
             jax.ShapeDtypeStruct((total, LANES), jnp.float32),
             jax.ShapeDtypeStruct((total, LANES), jnp.float32),
-            jax.ShapeDtypeStruct((rows, width), jnp.float32),
-        ],
-        out_specs=[tiles(far * rows), tiles(total - far * rows)]
-        + [whole((total, LANES)), whole((total, LANES)), tiles(rows)],
+        ]
+        + [jax.ShapeDtypeStruct((rows, width), jnp.float32)] * with_hidden,
+        out_specs=[tiles(total), whole((total, LANES)), whole((total, LANES))]
+        + [tiles(rows)] * with_hidden,
         scratch_shapes=[
-            pltpu.VMEM((total, packed), jnp.bfloat16),
+            pltpu.VMEM((gathered, packed), jnp.bfloat16),
             pltpu.VMEM((total, packed), jnp.bfloat16),
             pltpu.VMEM((total, LANES), jnp.float32),
             pltpu.VMEM((total, experts_all), jnp.float32),
@@ -182,36 +176,93 @@
     )(scalars, *pooled, *resid_blocks, w_out, gain, w_router_t)
 
 
-def attention(queries, new_lat, owned_cache, row_lengths, latent):
-    step_count, row_count, kv_width = new_lat.shape
-    context = owned_cache.shape[1]
-    cache_scores = (
-        jnp.einsum("srhk,rpk->srhp", queries, owned_cache, preferred_element_type=jnp.float32)
-        * qk_scale
-    )
-    visible = jnp.arange(context)[None, :] < row_lengths[:, None]
-    cache_scores = jnp.where(visible[None, :, None, :], cache_scores, -1e30)
-    fresh_scores = (
-        jnp.einsum("srhk,trk->srht", queries, new_lat, preferred_element_type=jnp.float32)
-        * qk_scale
-    )
-    causal = jnp.arange(step_count)[:, None] >= jnp.arange(step_count)[None, :]
-    fresh_scores = jnp.where(causal[:, None, None, :], fresh_scores, -1e30)
-    scores = jnp.concatenate([cache_scores, fresh_scores], axis=-1)
-    weights = jax.nn.softmax(scores, axis=-1).astype(jnp.bfloat16)
-    pooled = jnp.einsum(
-        "srhp,rpl->srl",
-        weights[..., :context],
-        owned_cache[..., :latent],
-        preferred_element_type=jnp.float32,
-    )
-    pooled = pooled + jnp.einsum(
-        "srht,trl->srl",
-        weights[..., context:],
-        new_lat[..., :latent],
-        preferred_element_type=jnp.float32,
-    )
-    return pooled.astype(jnp.bfloat16)
+def attention_kernel(context, latent, q, cache, fresh, lengths, routes, packet, keys_a, keys_b, total):
+    step = pl.program_id(0)
+    rows, kv_width = q.shape[1], cache.shape[1]
+    wide = keys_a.shape[1]
+    pairs = q.shape[2] // (2 * kv_width)
+    keys = keys_a.shape[0]
+    cached = cache.shape[0]
+
+    @pl.when(step == 0)
+    def _():
+        keys_a[...] = jnp.zeros_like(keys_a)
+        keys_a[:cached, :kv_width] = cache[...]
+        keys_a[cached:, :kv_width] = fresh[...]
+        shifted = pltpu.roll(keys_a[...].astype(jnp.float32), wide - kv_width, 1)
+        keys_b[...] = shifted.astype(jnp.bfloat16)
+
+    row = lax.broadcasted_iota(jnp.int32, (rows, keys), 0)
+    key = lax.broadcasted_iota(jnp.int32, (rows, keys), 1)
+    place = key // rows
+    seen = (place < lengths[:, :1]) & (place < context)
+    seen = seen | ((place >= context) & (place <= context + step))
+    bias = jnp.where(seen & (key % rows == row), 0.0, -1e30)
+    summed = jnp.zeros((rows, keys), jnp.float32)
+    for held, first in ((keys_a, 0), (keys_b, 2 * kv_width - wide)):
+        heads = [
+            q[0, :, 2 * kv_width * i + first : 2 * kv_width * i + first + wide].astype(jnp.float32)
+            for i in range(pairs)
+        ]
+        scores = lax.dot_general(
+            jnp.concatenate(heads, axis=0).astype(jnp.bfloat16),
+            held[...],
+            (((1,), (1,)), ((), ())),
+            preferred_element_type=jnp.float32,
+        )
+        scores = (scores * qk_scale).reshape(pairs, rows, keys) + bias[None]
+        e = jnp.exp(scores - jnp.max(scores, axis=2, keepdims=True))
+        weights = e / jnp.sum(e, axis=2, keepdims=True)
+        summed = summed + jnp.sum(weights.astype(jnp.bfloat16).astype(jnp.float32), axis=0)
+    total[pl.ds(pl.multiple_of(step * rows, rows), rows), :] = summed
+
+    @pl.when(step == pl.num_programs(0) - 1)
+    def _():
+        high = total[...].astype(jnp.bfloat16)
+        low = (total[...] - high.astype(jnp.float32)).astype(jnp.bfloat16)
+        values = keys_a[:, :latent]
+        pooled = jnp.dot(high, values, preferred_element_type=jnp.float32)
+        pooled = pooled + jnp.dot(low, values, preferred_element_type=jnp.float32)
+        packet[:, :latent] = pooled.astype(jnp.bfloat16)
+        lane = lax.broadcasted_iota(jnp.int32, (packet.shape[0], LANES), 1)
+        routed = jnp.zeros(lane.shape, jnp.float32)
+        for k in range(routes.shape[1]):
+            routed = jnp.where(routes[:, k : k + 1] == lane, 1.0, routed)
+        packet[:, latent:] = routed.astype(jnp.bfloat16)
+
+
+def attention(q_abs, cache, fresh, lengths, routes, context, latent):
+    steps, rows, _ = q_abs.shape
+    kv_width = cache.shape[1]
+    keys = cache.shape[0] + fresh.shape[0]
+    wide = -(-kv_width // LANES) * LANES
+
+    def whole(a):
+        return pl.BlockSpec(a.shape, lambda i: (0, 0), pipeline_mode=pl.Buffered(1))
+
+    heads = q_abs.shape[2] // kv_width
+    return pl.pallas_call(
+        lambda *refs: attention_kernel(context, latent, *refs),
+        grid=(steps,),
+        in_specs=[pl.BlockSpec((1, rows, q_abs.shape[2]), lambda i: (i, 0, 0))]
+        + [whole(a) for a in (cache, fresh, lengths, routes)],
+        out_shape=jax.ShapeDtypeStruct((steps * rows, latent + LANES), jnp.bfloat16),
+        out_specs=pl.BlockSpec((steps * rows, latent + LANES), lambda i: (0, 0)),
+        scratch_shapes=[
+            pltpu.VMEM((keys, wide), jnp.bfloat16),
+            pltpu.VMEM((keys, wide), jnp.bfloat16),
+            pltpu.VMEM((steps * rows, keys), jnp.float32),
+        ],
+        compiler_params=pltpu.CompilerParams(
+            dimension_semantics=("arbitrary",), vmem_limit_bytes=24 << 20
+        ),
+        cost_estimate=pl.CostEstimate(
+            flops=2 * steps * rows * heads * wide * keys,
+            bytes_accessed=2 * q_abs.size,
+            transcendentals=steps * rows * heads * keys,
+        ),
+        name="attention",
+    )(q_abs, cache, fresh, lengths, routes)
 
 
 def local(
@@ -250,18 +301,18 @@
     def around(to_the_right, to_the_left):
         return send(to_the_right, to_right), send(to_the_left, to_left)
 
+    positions, kv_width = latent_cache.shape[1:]
     wanted = (owner[:, None] == jnp.arange(owner.shape[0], dtype=jnp.int32)).astype(jnp.bfloat16)
     ordered = jnp.einsum(
-        "jr,rpk->jpk", wanted, latent_cache, preferred_element_type=jnp.float32
+        "jr,rpk->pjk", wanted, latent_cache, preferred_element_type=jnp.float32
     ).astype(jnp.bfloat16)
-    owned_cache = lax.all_to_all(ordered, "expert", split_axis=0, concat_axis=1, tiled=True)
+    ordered = ordered.reshape(positions, devices, row_count, kv_width).swapaxes(0, 1)
+    owned = lax.all_to_all(ordered, "expert", split_axis=0, concat_axis=0, tiled=True)
 
     mine = resid.reshape(rows, width)
     held, sib = {0: mine}, {}
     held[-1], held[1] = around(mine, mine)
-    owner, lengths, routes, norm_gain, new_lat, held[-1], held[1] = hold(
-        (owner, lengths, routes, norm_gain, new_lat, held[-1], held[1])
-    )
+    owner, lengths, held[-1], held[1] = hold((owner, lengths, held[-1], held[1]))
     held[-2], held[2] = around(held[-1], held[1])
     sib[0] = send(mine, sibling)
     row_owner = lax.dynamic_slice_in_dim(owner, device_index * row_count, row_count)
@@ -270,9 +321,9 @@
             row_owner[:, None] == jnp.arange(owner.shape[0], dtype=jnp.int32), lengths[None, :], 0
         ),
         axis=1,
+        keepdims=True,
     )
-    routed = jnp.any(routes[..., None] == jnp.arange(LANES, dtype=jnp.int32), axis=2)
-    routed = routed.astype(jnp.bfloat16)
+    row_lengths = jnp.broadcast_to(row_lengths, (row_count, LANES))
     gain = norm_gain[None, :]
     scalars = jnp.array(
         [
@@ -282,50 +333,51 @@
         ],
         jnp.int32,
     )[device_index]
-    queries = q_abs.reshape(step_count, row_count, -1, new_lat.shape[2])
-    owned_cache, queries, row_lengths, routed, gain, scalars = hold(
-        (owned_cache, queries, row_lengths, routed, gain, scalars)
+    owned, row_lengths, gain, scalars, held[-2], held[2], sib[0] = hold(
+        (owned, row_lengths, gain, scalars, held[-2], held[2], sib[0])
     )
-    pooled = attention(queries, new_lat, owned_cache, row_lengths, w_out.shape[0])
-    packet = jnp.concatenate([pooled, routed], axis=2).reshape(rows, -1)
-    packet, held[-2], held[2], sib[0] = hold((packet, held[-2], held[2], sib[0]))
-
-    high, low = gather_steps(chips)
-    along = [send(packet, step_perm(chips, i, 0)) for i in range(1, high)]
     for t in range(3, half):
         held[-t], held[t] = around(held[1 - t], held[t - 1])
     sib[-1], sib[1] = send(held[-1], sibling), send(held[1], sibling)
-    along, held, sib = hold((along, held, sib))
+    packet = attention(
+        q_abs,
+        owned.reshape(-1, kv_width),
+        new_lat.reshape(rows, kv_width),
+        row_lengths,
+        routes.reshape(rows, -1),
+        devices * positions,
+        w_out.shape[0],
+    )
+    packet, held, sib = hold((packet, held, sib))
+
+    high, low = gather_steps(chips)
+    along = [send(packet, step_perm(chips, i, 0)) for i in range(1, high)]
+    last = around(held[1 - half][:cut], held[half - 1][cut:])
+    for t in range(2, half - 1):
+        sib[-t], sib[t] = send(held[-t], sibling), send(held[t], sibling)
+    along, last, sib = hold((along, last, sib))
     along = jnp.concatenate([packet] + along, axis=0)
     across = [send(along, step_perm(chips, 0, i)) for i in range(1, low)]
-    last = around(held[1 - half][:cut], held[half - 1][cut:])
-    for t in range(2, half):
-        sib[-t], sib[t] = send(held[-t], sibling), send(held[t], sibling)
-    along_sib = send(along, sibling)
-    across, last, sib, along_sib = hold((across, last, sib, along_sib))
     held[half] = jnp.concatenate(last, axis=0)
-    sib[half] = send(held[half], sibling)
+    for d in (1 - half, half - 1, half):
+        sib[d] = send(held[d], sibling)
+    across, sib = hold((across, sib))
     across = across[0] if low == 2 else jnp.concatenate(across, axis=0)
+    gathered = [along, across, send(along, sibling), send(across, sibling)]
 
     f32 = jnp.float32
-    x_far, x_near, scale, weight, hidden = normalize(
-        2 * len(far),
-        scalars,
-        [along, across, along_sib, send(across, sibling)],
-        [a[d] for part in (far, near) for a in (held, sib) for d in part],
-        w_out,
-        gain,
-        w_router.T,
-    )
+
+    def normed(first, dists, with_hidden, gathered):
+        blocks = [a[d] for a in (held, sib) for d in dists]
+        return normalize(first, with_hidden, scalars, gathered, w_out, gain, w_router.T, blocks)
 
     def product(a, w):
         return jnp.dot(a, w[0], preferred_element_type=f32)
 
-    def activate(a, b, at):
-        r, g = scale[at, :1], weight[at, :1]
+    def activate(a, b, scale, weight):
+        r, g = scale[:, :1], weight[:, :1]
         return (jax.nn.silu(a * r) * (b * r) * g).astype(jnp.bfloat16)
 
-    cut_at = x_far.shape[0]
     sums = {}
 
     def swap(dists, y):
@@ -339,12 +391,15 @@
     def both(right, left):
         return around(right.astype(jnp.bfloat16), left.astype(jnp.bfloat16))
 
-    act = hold(activate(product(x_far, w_gate), product(x_far, w_up), slice(0, cut_at)))
+    x, scale, weight = normed(1, far, False, gathered)
+    act = hold(activate(product(x, w_gate), product(x, w_up), scale, weight))
     y, received = swap(far, product(act, w_down).astype(jnp.bfloat16))
-    gated, y, received = hold((product(x_near, w_gate), y, received))
+    y, gathered = hold((y, gathered))
+    x, scale, weight, hidden = normed(1 + 2 * len(far), near, True, gathered)
+    x, y, received = hold((x, y, received))
     add_up(far, y, received)
     right, left = both(sums[half][:cut], sums[half][cut:])
-    act = activate(gated, product(x_near, w_up), slice(cut_at, None))
+    act = activate(product(x, w_gate), product(x, w_up), scale, weight)
     act, right, left = hold((act, right, left))
     right = jnp.concatenate([right.astype(f32), jnp.zeros((rows - cut, width), f32)], axis=0)
     left = jnp.concatenate([jnp.zeros((cut, width), f32), left.astype(f32)], axis=0)

time: 107 us -> 118 us (1.10)
  waiting for transfers between devices: 35.6 us -> 46.5 us
  Pallas kernels: 7.23 us -> 14.1 us
  local copies, waits for them, and re-layouts: 10.5 us -> 5.43 us
  starting transfers between devices: 31.3 us -> 33.3 us
  matrix products: 18.9 us -> 17 us
    ppermute x32, waiting for transfers between devices: 33.9 us -> 46.5 us  [send(): return lax.ppermute(a, 'expert', perm)]
    pallas_call x1 -> x3, Pallas kernels: 7.23 us -> 14.1 us  [the longest x2 10.5 us: normalize(): pl.pallas_call(lambda *refs: norm_kernel(first, blocks, rows, latent, wid...]
    reshape x1 -> x0, local copies, waits for them, and re-layouts: 5.66 us -> none  [local(): queries = q_abs.reshape(step_count, row_count, -1, new_lat.shape[2])]
    dot_general x5 -> x1, matrix products: 6.05 us -> 0.95 us  [local(): jnp.einsum('jr,rpk->pjk', wanted, latent_cache, preferred_element_type=jn...]
    dot_general x6, matrix products: 12.9 us -> 16 us  [product(): return jnp.dot(a, w[0], preferred_element_type=f32)]
    all_to_all x1, waiting for transfers between devices: 1.73 us -> 0.01 us  [local(): lax.all_to_all(ordered, 'expert', split_axis=0, concat_axis=0, tiled=True)]
    unnamed x34 -> x36, local copies, waits for them, and re-layouts: 1.66 us -> 3 us
    all_to_all x1, starting transfers between devices: 6.29 us -> 7.53 us  [local(): lax.all_to_all(ordered, 'expert', split_axis=0, concat_axis=0, tiled=True)]
  transfers between devices with their start and end apart: 33 -> 33, of which waited for: 14 -> 14; matrix products, arithmetic and copies ran while one was open for 19% -> 6% of each run, Pallas kernels for 0% -> 8%
where the time goes in v7:
time: 118 us
  waiting for transfers between devices  46.5 us (39%)
  starting transfers between devices  33.3 us (28%)
  matrix products  17 us (14%)
  Pallas kernels  14.1 us (12%)
  local copies, waits for them, and re-layouts  5.43 us (5%)
  other arithmetic  1.53 us (1%)
    ppermute x32, waiting for transfers between devices, send(): return lax.ppermute(a, 'expert', perm)  46.5 us
    ppermute x32, starting transfers between devices, send(): return lax.ppermute(a, 'expert', perm)  25.7 us
    dot_general x6, matrix products, product(): return jnp.dot(a, w[0], preferred_element_type=f32)  16 us
    pallas_call x2, Pallas kernels, normalize(): pl.pallas_call(lambda *refs: norm_kernel(first, blocks, rows, latent, wid...  10.5 us
    all_to_all x1, starting transfers between devices, local(): lax.all_to_all(ordered, 'expert', split_axis=0, concat_axis=0, tiled=True)  7.53 us
    pallas_call x1, Pallas kernels, attention(): pl.pallas_call(lambda *refs: attention_kernel(context, latent, *refs), gr...  3.65 us
    unnamed x36, local copies, waits for them, and re-layouts  3 us
  transfers between devices with their start and end apart: 33, of which 14 were waited for; matrix products, arithmetic and copies ran while one was open for 6% of the time, Pallas kernels for 8%

profile of v7, /device:TPU:0, one launch (start us, length us, event | category | flops | bytes accessed | tf_op | source)
XLA Modules:
  0.0 118.2 jit_solution(15310465731615503753)
XLA Ops:
  0.0 1.0 copy-done
  1.1 1.0 fusion.30
  2.3 0.8 copy.21
  3.0 7.5 %all-to-all-start = ((bf16[16,2,8,576]{3,2,1,0:T(8,128)(2,1)}), bf16[16,2,8,576]{3,2,1,0:T(8,128)(2,1)S(1)}, u32[]{:S(2)}, u32[]{:S(2)}) async-start(bf16[16,2,8,576]{3,2,1,0:T(8,128)(2,1)} %copy.21), calls=%async_computation | async-start | bytes 655360 | tf_op jit(solution)/shard_map/all_to_all | solution.py:310
  10.6 2.0 %collective-permute-start.1 = (bf16[32,3584]{1,0:T(8,128)(2,1)S(1)}, bf16[32,3584]{1,0:T(8,128)(2,1)S(1)}, u32[]{:S(2)}, u32[]{:S(2)}) collective-permute-start(bf16[32,3584]{1,0:T(8,128)(2,1)S(1)} %bitcast.58), channel_id=1, source_target_pairs={{0,2},{1,3},{4,0},{5,1},{8,4},{9,5},{12,8},{13,9},{14,12},{15,13},... | collective-permute-start | bytes 688136 | tf_op jit(solution)/shard_map/ppermute | solution.py:297
  12.6 11.2 %collective-permute-done.1.refs_6_ = bf16[32,3584]{1,0:T(8,128)(2,1)S(1)} collective-permute-done((bf16[32,3584]{1,0:T(8,128)(2,1)S(1)}, bf16[32,3584]{1,0:T(8,128)(2,1)S(1)}, u32[]{:S(2)}, u32[]{:S(2)}) %collective-permute-start.1) | collective-permute-done | bytes 229408 | tf_op jit(solution)/shard_map/ppermute | solution.py:297
  23.9 3.2 %collective-permute-start.2 = (bf16[32,3584]{1,0:T(8,128)(2,1)S(1)}, bf16[32,3584]{1,0:T(8,128)(2,1)S(1)}, u32[]{:S(2)}, u32[]{:S(2)}) collective-permute-start(bf16[32,3584]{1,0:T(8,128)(2,1)S(1)} %collective-permute-done.refs_7_), channel_id=1, source_target_pairs={{0,4},{1,5},{4,8},{5,9},{8,12},{9,13},{12,14},{13,15},{14,10},{15,... | collective-permute-start | bytes 688136 | tf_op jit(solution)/shard_map/ppermute | solution.py:297
  27.1 0.7 dynamic-slice_bitcast_fusion.refs_0_
  27.8 0.5 collective-permute-start.8
  28.6 3.2 %collective-permute-done.2.refs_9_ = bf16[32,3584]{1,0:T(8,128)(2,1)S(1)} collective-permute-done((bf16[32,3584]{1,0:T(8,128)(2,1)S(1)}, bf16[32,3584]{1,0:T(8,128)(2,1)S(1)}, u32[]{:S(2)}, u32[]{:S(2)}) %collective-permute-start.2) | collective-permute-done | bytes 229408 | tf_op jit(solution)/shard_map/ppermute | solution.py:297
  31.8 2.2 %collective-permute-done.3.refs_8_ = bf16[32,3584]{1,0:T(8,128)(2,1)S(1)} collective-permute-done((bf16[32,3584]{1,0:T(8,128)(2,1)S(1)}, bf16[32,3584]{1,0:T(8,128)(2,1)S(1)}, u32[]{:S(2)}, u32[]{:S(2)}) %collective-permute-start.3) | collective-permute-done | bytes 229408 | tf_op jit(solution)/shard_map/ppermute | solution.py:297
  34.0 0.6 collective-permute-start.5
  34.6 1.4 %collective-permute-start.6 = (bf16[32,3584]{1,0:T(8,128)(2,1)S(1)}, bf16[32,3584]{1,0:T(8,128)(2,1)S(1)}, u32[]{:S(2)}, u32[]{:S(2)}) collective-permute-start(bf16[32,3584]{1,0:T(8,128)(2,1)S(1)} %collective-permute-done.3.refs_8_), channel_id=1, source_target_pairs={{0,2},{1,3},{4,0},{5,1},{8,4},{9,5},{12,8},{13,9},{14,12},{15,13},... | collective-permute-start | bytes 688136 | tf_op jit(solution)/shard_map/ppermute | solution.py:297
  36.1 1.7 %copy-done.4 = bf16[4,8,36864]{2,1,0:T(8,128)(2,1)S(1)} copy-done((bf16[4,8,36864]{2,1,0:T(8,128)(2,1)S(1)}, bf16[4,8,36864]{2,1,0:T(8,128)(2,1)}, u32[]{:S(2)}) %copy-start.4) | copy-done | bytes 2359320
  37.7 3.7 %attention.1 = bf16[32,640]{1,0:T(8,128)(2,1)S(1)} custom-call(bf16[4,8,36864]{2,1,0:T(8,128)(2,1)S(1)} %copy-done.4, bf16[256,576]{1,0:T(8,128)(2,1)S(1)} %bitcast.57, bf16[32,576]{1,0:T(8,128)(2,1)S(1)} %bitcast.62, s32[8,128]{1,0:T(8,128)S(1)} %broadcast_in_dim.28.refs_3_, s32[32,8]{1,0:T(8,128)S(1)} %bitcast.63), custom_call_target="tpu_custom_call" | custom-call | flops 754974720 | bytes 2359296 | tf_op jit(solution)/shard_map/attention/pallas_call | solution.py:244
  41.5 0.5 collective-permute-start.15
  42.0 0.6 collective-permute-start.11
  42.6 1.6 %collective-permute-start.10 = (bf16[32,640]{1,0:T(8,128)(2,1)S(1)}, bf16[32,640]{1,0:T(8,128)(2,1)S(1)}, u32[]{:S(2)}, u32[]{:S(2)}) collective-permute-start(bf16[32,640]{1,0:T(8,128)(2,1)S(1)} %attention.1), channel_id=1, source_target_pairs={{0,8},{1,9},{2,10},{3,11},{4,12},{5,13},{6,14},{7,15},{8,0},{9,1},... | collective-permute-start | bytes 122888 | tf_op jit(solution)/shard_map/ppermute | solution.py:297
  44.2 1.5 %collective-permute-start.13 = (bf16[16,3584]{1,0:T(8,128)(2,1)S(1)}, bf16[16,3584]{1,0:T(8,128)(2,1)S(1)}, u32[]{:S(2)}, u32[]{:S(2)}) collective-permute-start(bf16[16,3584]{1,0:T(8,128)(2,1)S(1)} %slice.81), channel_id=1, source_target_pairs={{0,2},{1,3},{4,0},{5,1},{8,4},{9,5},{12,8},{13,9},{14,12},{15,13},... | collective-permute-start | bytes 344072 | tf_op jit(solution)/shard_map/ppermute | solution.py:297
  45.7 2.5 %collective-permute-done.11 = bf16[32,640]{1,0:T(8,128)(2,1)S(1)} collective-permute-done((bf16[32,640]{1,0:T(8,128)(2,1)S(1)}, bf16[32,640]{1,0:T(8,128)(2,1)S(1)}, u32[]{:S(2)}, u32[]{:S(2)}) %collective-permute-start.11) | collective-permute-done | bytes 40992 | tf_op jit(solution)/shard_map/ppermute | solution.py:297
  48.4 2.4 %collective-permute-start.9 = (bf16[32,640]{1,0:T(8,128)(2,1)S(1)}, bf16[32,640]{1,0:T(8,128)(2,1)S(1)}, u32[]{:S(2)}, u32[]{:S(2)}) collective-permute-start(bf16[32,640]{1,0:T(8,128)(2,1)S(1)} %attention.1), channel_id=1, source_target_pairs={{0,12},{1,13},{2,14},{3,15},{4,0},{5,1},{6,2},{7,3},{8,4},{9,5},{1... | collective-permute-start | bytes 122888 | tf_op jit(solution)/shard_map/ppermute | solution.py:297
  50.9 1.7 %collective-permute-done.9 = bf16[32,640]{1,0:T(8,128)(2,1)S(1)} collective-permute-done((bf16[32,640]{1,0:T(8,128)(2,1)S(1)}, bf16[32,640]{1,0:T(8,128)(2,1)S(1)}, u32[]{:S(2)}, u32[]{:S(2)}) %collective-permute-start.9) | collective-permute-done | bytes 40992 | tf_op jit(solution)/shard_map/ppermute | solution.py:297
  52.5 0.5 collective-permute-start.18
  53.2 1.8 %collective-permute-start.16 = (bf16[128,640]{1,0:T(8,128)(2,1)S(1)}, bf16[128,640]{1,0:T(8,128)(2,1)S(1)}, u32[]{:S(2)}, u32[]{:S(2)}) collective-permute-start(bf16[128,640]{1,0:T(8,128)(2,1)S(1)} %constant_dynamic-update-slice_fusion.refs_1_), channel_id=1, source_target_pairs={{0,2},{1,3},{2,0},{3,1},{4,6},{5,7},{6,4},{7,5},{8,10},{9,11},{10,... | collective-permute-start | bytes 491528 | tf_op jit(solution)/shard_map/ppermute | solution.py:297
  55.2 4.6 %collective-permute-done.16.refs_2_ = bf16[128,640]{1,0:T(8,128)(2,1)S(1)} collective-permute-done((bf16[128,640]{1,0:T(8,128)(2,1)S(1)}, bf16[128,640]{1,0:T(8,128)(2,1)S(1)}, u32[]{:S(2)}, u32[]{:S(2)}) %collective-permute-start.16) | collective-permute-done | bytes 163872 | tf_op jit(solution)/shard_map/ppermute | solution.py:297
  59.9 1.4 %collective-permute-done.21.refs_4_ = bf16[128,640]{1,0:T(8,128)(2,1)S(1)} collective-permute-done((bf16[128,640]{1,0:T(8,128)(2,1)S(1)}, bf16[128,640]{1,0:T(8,128)(2,1)S(1)}, u32[]{:S(2)}, u32[]{:S(2)}) %collective-permute-start.21) | collective-permute-done | bytes 163872 | tf_op jit(solution)/shard_map/ppermute | solution.py:297
  61.3 4.8 %normalize.2 = (bf16[192,3584]{1,0:T(8,128)(2,1)S(1)}, f32[192,128]{1,0:T(8,128)S(1)}, f32[192,128]{1,0:T(8,128)S(1)}) custom-call(s32[17]{0:T(128)S(1)} %dynamic-slice_bitcast_fusion.refs_0_, bf16[128,640]{1,0:T(8,128)(2,1)S(1)} %constant_dynamic-update-slice_fusion.refs_1_, bf16[128,640]{1,0:T(8,128)(2,1)S(1)} %collective-permute-done.16.refs_2_, ...), custom_call_target="tpu_custom_call" | custom-call | flops 704643072 | bytes 6422528 | tf_op jit(solution)/shard_map/normalize/pallas_call | solution.py:146
  66.2 4.9 %fusion.24 = f32[192,1024]{1,0:T(8,128)S(1)} fusion(bf16[192,3584]{1,0:T(8,128)(2,1)S(1)} %get-tuple-element.105, bf16[1,3584,1024]{2,1,0:T(8,128)(2,1)} %param.24, f32[192]{0:T(256)S(1)} %get-tuple-element.148), kind=kOutput, calls=%fused_computation.17 | convolution fusion | flops 1409482752 | bytes 9503488 | tf_op jit(solution)/shard_map/dot_general | solution.py:375
  71.2 1.7 %multiply_convert_fusion.1 = bf16[192,1024]{1,0:T(8,128)(2,1)S(1)} fusion(f32[192,1024]{1,0:T(8,128)S(1)} %fusion.24, f32[192]{0:T(256)S(1)} %get-tuple-element.147, f32[192]{0:T(256)S(1)} %get-tuple-element.148, bf16[192,3584]{1,0:T(8,128)(2,1)S(1)} %get-tuple-element.105, bf16[1,3584,1024]{2,1,0:T(8,128)(2,1)S(1)} %bitcast.68), kind=kOutput, calls=%fused_computation.21 | convolution fusion | flops 1410859008 | bytes 9897472 | tf_op jit(solution)/shard_map/dot_general | solution.py:375
  73.2 1.6 %fusion.15 = bf16[192,3584]{1,0:T(8,128)(2,1)S(1)} fusion(bf16[192,1024]{1,0:T(8,128)(2,1)S(1)} %multiply_convert_fusion.1, bf16[1,1024,3584]{2,1,0:T(8,128)(2,1)S(1)} %bitcast.70), kind=kOutput, calls=%fused_computation.13 | convolution fusion | flops 1409974272 | bytes 9109504 | tf_op jit(solution)/shard_map/dot_general | solution.py:375
  75.0 5.7 %normalize.3 = (bf16[320,3584]{1,0:T(8,128)(2,1)S(1)}, f32[320,128]{1,0:T(8,128)S(1)}, f32[320,128]{1,0:T(8,128)S(1)}, f32[32,3584]{1,0:T(8,128)S(1)}) custom-call(s32[17]{0:T(128)S(1)} %dynamic-slice_bitcast_fusion.refs_0_, bf16[128,640]{1,0:T(8,128)(2,1)S(1)} %constant_dynamic-update-slice_fusion.refs_1_, ...), custom_call_target="tpu_custom_call" | custom-call | flops 1174405120 | bytes 8257536 | tf_op jit(solution)/shard_map/normalize/pallas_call | solution.py:146
  81.1 1.8 %collective-permute-start.24 = (bf16[16,3584]{1,0:T(8,128)(2,1)S(1)}, bf16[16,3584]{1,0:T(8,128)(2,1)S(1)}, u32[]{:S(2)}, u32[]{:S(2)}) collective-permute-start(bf16[16,3584]{1,0:T(8,128)(2,1)S(1)} %get-tuple-element.145), channel_id=1, source_target_pairs={{0,2},{1,3},{4,0},{5,1},{8,4},{9,5},{12,8},{13,9},{14,12},{15,13},... | collective-permute-start | bytes 344072 | tf_op jit(solution)/shard_map/ppermute | solution.py:297
  82.9 0.3 collective-permute-start.23
  83.2 2.5 %fusion.18 = f32[320,1024]{1,0:T(8,128)S(1)} fusion(bf16[320,3584]{1,0:T(8,128)(2,1)S(1)} %get-tuple-element.123, bf16[1,3584,1024]{2,1,0:T(8,128)(2,1)S(1)} %bitcast.66, f32[320]{0:T(512)S(1)} %slice_reduce_fusion.1), kind=kOutput, calls=%fused_computation.14 | convolution fusion | flops 2349137920 | bytes 10945792 | tf_op jit(solution)/shard_map/dot_general | solution.py:375
  85.8 2.7 %multiply_convert_fusion = bf16[320,1024]{1,0:T(8,128)(2,1)S(1)} fusion(f32[320,1024]{1,0:T(8,128)S(1)} %fusion.18, f32[320]{0:T(512)S(1)} %slice_reduce_fusion, f32[320]{0:T(512)S(1)} %slice_reduce_fusion.1, bf16[320,3584]{1,0:T(8,128)(2,1)S(1)} %get-tuple-element.123, bf16[1,3584,1024]{2,1,0:T(8,128)(2,1)S(1)} %bitcast.68), kind=kOutput, calls=%fused_computation.16 | convolution fusion | flops 2351431680 | bytes 11602432 | tf_op jit(solution)/shard_map/dot_general | solution.py:375
  88.5 2.6 %fusion.12 = bf16[320,3584]{1,0:T(8,128)(2,1)S(1)} fusion(bf16[320,1024]{1,0:T(8,128)(2,1)S(1)} %multiply_convert_fusion, bf16[1,1024,3584]{2,1,0:T(8,128)(2,1)S(1)} %bitcast.70), kind=kOutput, calls=%fused_computation.12 | convolution fusion | flops 2349957120 | bytes 10289152 | tf_op jit(solution)/shard_map/dot_general | solution.py:375
  91.4 1.8 %collective-permute-start.27 = (bf16[32,3584]{1,0:T(8,128)(2,1)S(1)}, bf16[32,3584]{1,0:T(8,128)(2,1)S(1)}, u32[]{:S(2)}, u32[]{:S(2)}) collective-permute-start(bf16[32,3584]{1,0:T(8,128)(2,1)S(1)} %get-tuple-element.143), channel_id=1, source_target_pairs={{0,2},{1,3},{4,0},{5,1},{8,4},{9,5},{12,8},{13,9},{14,12},{15,13},... | collective-permute-start | bytes 688136 | tf_op jit(solution)/shard_map/ppermute | solution.py:297
  93.1 0.3 collective-permute-start.26
  93.4 6.0 %collective-permute-done.27 = bf16[32,3584]{1,0:T(8,128)(2,1)S(1)} collective-permute-done((bf16[32,3584]{1,0:T(8,128)(2,1)S(1)}, bf16[32,3584]{1,0:T(8,128)(2,1)S(1)}, u32[]{:S(2)}, u32[]{:S(2)}) %collective-permute-start.27) | collective-permute-done | bytes 229408 | tf_op jit(solution)/shard_map/ppermute | solution.py:297
  99.4 1.4 %collective-permute-done.26 = bf16[32,3584]{1,0:T(8,128)(2,1)S(1)} collective-permute-done((bf16[32,3584]{1,0:T(8,128)(2,1)S(1)}, bf16[32,3584]{1,0:T(8,128)(2,1)S(1)}, u32[]{:S(2)}, u32[]{:S(2)}) %collective-permute-start.26) | collective-permute-done | bytes 229408 | tf_op jit(solution)/shard_map/ppermute | solution.py:297
  101.0 1.2 %collective-permute-start.29 = (bf16[32,3584]{1,0:T(8,128)(2,1)S(1)}, bf16[32,3584]{1,0:T(8,128)(2,1)S(1)}, u32[]{:S(2)}, u32[]{:S(2)}) collective-permute-start(bf16[32,3584]{1,0:T(8,128)(2,1)S(1)} %get-tuple-element.141), channel_id=1, source_target_pairs={{0,2},{1,3},{4,0},{5,1},{8,4},{9,5},{12,8},{13,9},{14,12},{15,13},... | collective-permute-start | bytes 688136 | tf_op jit(solution)/shard_map/ppermute | solution.py:297
  102.2 0.8 collective-permute-start.28
  103.1 4.9 %collective-permute-done.29 = bf16[32,3584]{1,0:T(8,128)(2,1)S(1)} collective-permute-done((bf16[32,3584]{1,0:T(8,128)(2,1)S(1)}, bf16[32,3584]{1,0:T(8,128)(2,1)S(1)}, u32[]{:S(2)}, u32[]{:S(2)}) %collective-permute-start.29) | collective-permute-done | bytes 229408 | tf_op jit(solution)/shard_map/ppermute | solution.py:297
  108.0 1.4 %collective-permute-done.28 = bf16[32,3584]{1,0:T(8,128)(2,1)S(1)} collective-permute-done((bf16[32,3584]{1,0:T(8,128)(2,1)S(1)}, bf16[32,3584]{1,0:T(8,128)(2,1)S(1)}, u32[]{:S(2)}, u32[]{:S(2)}) %collective-permute-start.28) | collective-permute-done | bytes 229408 | tf_op jit(solution)/shard_map/ppermute | solution.py:297
  109.5 1.8 %collective-permute-start.31 = (bf16[32,3584]{1,0:T(8,128)(2,1)S(1)}, bf16[32,3584]{1,0:T(8,128)(2,1)S(1)}, u32[]{:S(2)}, u32[]{:S(2)}) collective-permute-start(bf16[32,3584]{1,0:T(8,128)(2,1)S(1)} %get-tuple-element.139), channel_id=1, source_target_pairs={{0,2},{1,3},{4,0},{5,1},{8,4},{9,5},{12,8},{13,9},{14,12},{15,13},... | collective-permute-start | bytes 688136 | tf_op jit(solution)/shard_map/ppermute | solution.py:297
  111.6 4.2 %collective-permute-done.31 = bf16[32,3584]{1,0:T(8,128)(2,1)S(1)} collective-permute-done((bf16[32,3584]{1,0:T(8,128)(2,1)S(1)}, bf16[32,3584]{1,0:T(8,128)(2,1)S(1)}, u32[]{:S(2)}, u32[]{:S(2)}) %collective-permute-start.31) | collective-permute-done | bytes 229408 | tf_op jit(solution)/shard_map/ppermute | solution.py:297
  115.8 1.6 %collective-permute-done.30 = bf16[32,3584]{1,0:T(8,128)(2,1)S(1)} collective-permute-done((bf16[32,3584]{1,0:T(8,128)(2,1)S(1)}, bf16[32,3584]{1,0:T(8,128)(2,1)S(1)}, u32[]{:S(2)}, u32[]{:S(2)}) %collective-permute-start.30) | collective-permute-done | bytes 229408 | tf_op jit(solution)/shard_map/ppermute | solution.py:297
  117.4 0.8 fusion.35
  (89 shorter events, 3.2 us)
Async XLA Ops:
  0.0 28.3 %copy-start.8 = (s32[128]{0:T(128)S(1)}, s32[128]{0:T(128)}, u32[]{:S(2)}) copy-start(s32[128]{0:T(128)} %param.18) | copy-start | bytes 1540
  0.0 10.5 %copy-start.3 = (bf16[4,8,3584]{2,1,0:T(8,128)(2,1)S(1)}, bf16[4,8,3584]{2,1,0:T(8,128)(2,1)}, u32[]{:S(2)}) copy-start(bf16[4,8,3584]{2,1,0:T(8,128)(2,1)} %param.19) | copy-start | bytes 688132
  0.0 28.4 %copy-start.9 = (s32[128]{0:T(128)S(1)}, s32[128]{0:T(128)}, u32[]{:S(2)}) copy-start(s32[128]{0:T(128)} %param.17) | copy-start | bytes 1540
  0.0 27.1 %copy-start.7 = (bf16[3584]{0:T(1024)(128)(2,1)S(1)}, bf16[3584]{0:T(1024)(128)(2,1)}, u32[]{:S(2)}) copy-start(bf16[3584]{0:T(1024)(128)(2,1)} %param.22) | copy-start | bytes 21508
  0.0 36.0 %copy-start.6 = (s32[4,8,8]{2,1,0:T(8,128)S(1)}, s32[4,8,8]{2,1,0:T(8,128)}, u32[]{:S(2)}) copy-start(s32[4,8,8]{2,1,0:T(8,128)} %param.20) | copy-start | bytes 3076
  0.0 36.0 %copy-start.5 = (bf16[4,8,576]{2,1,0:T(8,128)(2,1)S(1)}, bf16[4,8,576]{2,1,0:T(8,128)(2,1)}, u32[]{:S(2)}) copy-start(bf16[4,8,576]{2,1,0:T(8,128)(2,1)} %param.15) | copy-start | bytes 110596
  3.0 58.3 %copy-start.2 = (bf16[3584,16]{0,1:T(8,128)(2,1)S(1)}, bf16[3584,16]{0,1:T(8,128)(2,1)}, u32[]{:S(2)}) copy-start(bf16[3584,16]{0,1:T(8,128)(2,1)} %param.23) | copy-start | bytes 344068
  3.0 30.9 %all-to-all-start = ((bf16[16,2,8,576]{3,2,1,0:T(8,128)(2,1)}), bf16[16,2,8,576]{3,2,1,0:T(8,128)(2,1)S(1)}, u32[]{:S(2)}, u32[]{:S(2)}) async-start(bf16[16,2,8,576]{3,2,1,0:T(8,128)(2,1)} %copy.21), calls=%async_computation | async-start | bytes 655360 | tf_op jit(solution)/shard_map/all_to_all | solution.py:310
  10.6 13.3 %collective-permute-start.1 = (bf16[32,3584]{1,0:T(8,128)(2,1)S(1)}, bf16[32,3584]{1,0:T(8,128)(2,1)S(1)}, u32[]{:S(2)}, u32[]{:S(2)}) collective-permute-start(bf16[32,3584]{1,0:T(8,128)(2,1)S(1)} %bitcast.58), channel_id=1, source_target_pairs={{0,2},{1,3},{4,0},{5,1},{8,4},{9,5},{12,8},{13,9},{14,12},{15,13},... | collective-permute-start | bytes 688136 | tf_op jit(solution)/shard_map/ppermute | solution.py:297
  12.5 11.3 %collective-permute-start = (bf16[32,3584]{1,0:T(8,128)(2,1)S(1)}, bf16[32,3584]{1,0:T(8,128)(2,1)S(1)}, u32[]{:S(2)}, u32[]{:S(2)}) collective-permute-start(bf16[32,3584]{1,0:T(8,128)(2,1)S(1)} %bitcast.59), channel_id=1, source_target_pairs={{0,4},{1,5},{4,8},{5,9},{8,12},{9,13},{12,14},{13,15},{14,10},{15,... | collective-permute-start | bytes 688136 | tf_op jit(solution)/shard_map/ppermute | solution.py:297
  12.6 15.9 %collective-permute-start.4 = (bf16[32,3584]{1,0:T(8,128)(2,1)S(1)}, bf16[32,3584]{1,0:T(8,128)(2,1)S(1)}, u32[]{:S(2)}, u32[]{:S(2)}) collective-permute-start(bf16[32,3584]{1,0:T(8,128)(2,1)S(1)} %bitcast.60), channel_id=1, source_target_pairs={{0,1},{1,0},{2,3},{3,2},{4,5},{5,4},{6,7},{7,6},{8,9},{9,8},{10,11... | collective-permute-start | bytes 688136 | tf_op jit(solution)/shard_map/ppermute | solution.py:297
  23.9 7.9 %collective-permute-start.2 = (bf16[32,3584]{1,0:T(8,128)(2,1)S(1)}, bf16[32,3584]{1,0:T(8,128)(2,1)S(1)}, u32[]{:S(2)}, u32[]{:S(2)}) collective-permute-start(bf16[32,3584]{1,0:T(8,128)(2,1)S(1)} %collective-permute-done.refs_7_), channel_id=1, source_target_pairs={{0,4},{1,5},{4,8},{5,9},{8,12},{9,13},{12,14},{13,15},{14,10},{15,... | collective-permute-start | bytes 688136 | tf_op jit(solution)/shard_map/ppermute | solution.py:297
  27.1 6.9 %collective-permute-start.3 = (bf16[32,3584]{1,0:T(8,128)(2,1)S(1)}, bf16[32,3584]{1,0:T(8,128)(2,1)S(1)}, u32[]{:S(2)}, u32[]{:S(2)}) collective-permute-start(bf16[32,3584]{1,0:T(8,128)(2,1)S(1)} %collective-permute-done.1.refs_6_), channel_id=1, source_target_pairs={{0,2},{1,3},{4,0},{5,1},{8,4},{9,5},{12,8},{13,9},{14,12},{15,13},... | collective-permute-start | bytes 688136 | tf_op jit(solution)/shard_map/ppermute | solution.py:297
  27.8 13.6 %collective-permute-start.7 = (bf16[32,3584]{1,0:T(8,128)(2,1)S(1)}, bf16[32,3584]{1,0:T(8,128)(2,1)S(1)}, u32[]{:S(2)}, u32[]{:S(2)}) collective-permute-start(bf16[32,3584]{1,0:T(8,128)(2,1)S(1)} %collective-permute-done.refs_7_), channel_id=1, source_target_pairs={{0,1},{1,0},{2,3},{3,2},{4,5},{5,4},{6,7},{7,6},{8,9},{9,8},{10,11... | collective-permute-start | bytes 688136 | tf_op jit(solution)/shard_map/ppermute | solution.py:297
  27.8 13.6 %collective-permute-start.8 = (bf16[32,3584]{1,0:T(8,128)(2,1)S(1)}, bf16[32,3584]{1,0:T(8,128)(2,1)S(1)}, u32[]{:S(2)}, u32[]{:S(2)}) collective-permute-start(bf16[32,3584]{1,0:T(8,128)(2,1)S(1)} %collective-permute-done.1.refs_6_), channel_id=1, source_target_pairs={{0,1},{1,0},{2,3},{3,2},{4,5},{5,4},{6,7},{7,6},{8,9},{9,8},{10,11... | collective-permute-start | bytes 688136 | tf_op jit(solution)/shard_map/ppermute | solution.py:297
  34.0 27.3 %copy-start.1 = (bf16[512,3584]{1,0:T(8,128)(2,1)S(1)}, bf16[512,3584]{1,0:T(8,128)(2,1)}, u32[]{:S(2)}) copy-start(bf16[512,3584]{1,0:T(8,128)(2,1)} %refs_15_.1) | copy-start | bytes 11010052
  34.0 7.4 %collective-permute-start.5 = (bf16[32,3584]{1,0:T(8,128)(2,1)S(1)}, bf16[32,3584]{1,0:T(8,128)(2,1)S(1)}, u32[]{:S(2)}, u32[]{:S(2)}) collective-permute-start(bf16[32,3584]{1,0:T(8,128)(2,1)S(1)} %collective-permute-done.2.refs_9_), channel_id=1, source_target_pairs={{0,4},{1,5},{4,8},{5,9},{8,12},{9,13},{12,14},{13,15},{14,10},{15,... | collective-permute-start | bytes 688136 | tf_op jit(solution)/shard_map/ppermute | solution.py:297
  34.6 6.8 %collective-permute-start.6 = (bf16[32,3584]{1,0:T(8,128)(2,1)S(1)}, bf16[32,3584]{1,0:T(8,128)(2,1)S(1)}, u32[]{:S(2)}, u32[]{:S(2)}) collective-permute-start(bf16[32,3584]{1,0:T(8,128)(2,1)S(1)} %collective-permute-done.3.refs_8_), channel_id=1, source_target_pairs={{0,2},{1,3},{4,0},{5,1},{8,4},{9,5},{12,8},{13,9},{14,12},{15,13},... | collective-permute-start | bytes 688136 | tf_op jit(solution)/shard_map/ppermute | solution.py:297
  36.1 1.7 %copy-start.4 = (bf16[4,8,36864]{2,1,0:T(8,128)(2,1)S(1)}, bf16[4,8,36864]{2,1,0:T(8,128)(2,1)}, u32[]{:S(2)}) copy-start(bf16[4,8,36864]{2,1,0:T(8,128)(2,1)} %refs_0_.1) | copy-start | bytes 7077892
  41.4 11.6 %collective-permute-start.14 = (bf16[32,3584]{1,0:T(8,128)(2,1)S(1)}, bf16[32,3584]{1,0:T(8,128)(2,1)S(1)}, u32[]{:S(2)}, u32[]{:S(2)}) collective-permute-start(bf16[32,3584]{1,0:T(8,128)(2,1)S(1)} %collective-permute-done.2.refs_9_), channel_id=1, source_target_pairs={{0,1},{1,0},{2,3},{3,2},{4,5},{5,4},{6,7},{7,6},{8,9},{9,8},{10,11... | collective-permute-start | bytes 688136 | tf_op jit(solution)/shard_map/ppermute | solution.py:297
  41.5 11.6 %collective-permute-start.15 = (bf16[32,3584]{1,0:T(8,128)(2,1)S(1)}, bf16[32,3584]{1,0:T(8,128)(2,1)S(1)}, u32[]{:S(2)}, u32[]{:S(2)}) collective-permute-start(bf16[32,3584]{1,0:T(8,128)(2,1)S(1)} %collective-permute-done.3.refs_8_), channel_id=1, source_target_pairs={{0,1},{1,0},{2,3},{3,2},{4,5},{5,4},{6,7},{7,6},{8,9},{9,8},{10,11... | collective-permute-start | bytes 688136 | tf_op jit(solution)/shard_map/ppermute | solution.py:297
  42.0 6.2 %collective-permute-start.11 = (bf16[32,640]{1,0:T(8,128)(2,1)S(1)}, bf16[32,640]{1,0:T(8,128)(2,1)S(1)}, u32[]{:S(2)}, u32[]{:S(2)}) collective-permute-start(bf16[32,640]{1,0:T(8,128)(2,1)S(1)} %attention.1), channel_id=1, source_target_pairs={{0,4},{1,5},{2,6},{3,7},{4,8},{5,9},{6,10},{7,11},{8,12},{9,13},{1... | collective-permute-start | bytes 122888 | tf_op jit(solution)/shard_map/ppermute | solution.py:297
  42.6 5.8 %collective-permute-start.10 = (bf16[32,640]{1,0:T(8,128)(2,1)S(1)}, bf16[32,640]{1,0:T(8,128)(2,1)S(1)}, u32[]{:S(2)}, u32[]{:S(2)}) collective-permute-start(bf16[32,640]{1,0:T(8,128)(2,1)S(1)} %attention.1), channel_id=1, source_target_pairs={{0,8},{1,9},{2,10},{3,11},{4,12},{5,13},{6,14},{7,15},{8,0},{9,1},... | collective-permute-start | bytes 122888 | tf_op jit(solution)/shard_map/ppermute | solution.py:297
  44.2 8.3 %collective-permute-start.13 = (bf16[16,3584]{1,0:T(8,128)(2,1)S(1)}, bf16[16,3584]{1,0:T(8,128)(2,1)S(1)}, u32[]{:S(2)}, u32[]{:S(2)}) collective-permute-start(bf16[16,3584]{1,0:T(8,128)(2,1)S(1)} %slice.81), channel_id=1, source_target_pairs={{0,2},{1,3},{4,0},{5,1},{8,4},{9,5},{12,8},{13,9},{14,12},{15,13},... | collective-permute-start | bytes 344072 | tf_op jit(solution)/shard_map/ppermute | solution.py:297
  48.2 4.8 %collective-permute-start.12 = (bf16[16,3584]{1,0:T(8,128)(2,1)S(1)}, bf16[16,3584]{1,0:T(8,128)(2,1)S(1)}, u32[]{:S(2)}, u32[]{:S(2)}) collective-permute-start(bf16[16,3584]{1,0:T(8,128)(2,1)S(1)} %slice.80), channel_id=1, source_target_pairs={{0,4},{1,5},{4,8},{5,9},{8,12},{9,13},{12,14},{13,15},{14,10},{15,... | collective-permute-start | bytes 344072 | tf_op jit(solution)/shard_map/ppermute | solution.py:297
  48.4 4.1 %collective-permute-start.9 = (bf16[32,640]{1,0:T(8,128)(2,1)S(1)}, bf16[32,640]{1,0:T(8,128)(2,1)S(1)}, u32[]{:S(2)}, u32[]{:S(2)}) collective-permute-start(bf16[32,640]{1,0:T(8,128)(2,1)S(1)} %attention.1), channel_id=1, source_target_pairs={{0,12},{1,13},{2,14},{3,15},{4,0},{5,1},{6,2},{7,3},{8,4},{9,5},{1... | collective-permute-start | bytes 122888 | tf_op jit(solution)/shard_map/ppermute | solution.py:297
  52.5 2.7 %collective-permute-start.17 = (bf16[32,3584]{1,0:T(8,128)(2,1)S(1)}, bf16[32,3584]{1,0:T(8,128)(2,1)S(1)}, u32[]{:S(2)}, u32[]{:S(2)}) collective-permute-start(bf16[32,3584]{1,0:T(8,128)(2,1)S(1)} %collective-permute-done.5.refs_7_), channel_id=1, source_target_pairs={{0,1},{1,0},{2,3},{3,2},{4,5},{5,4},{6,7},{7,6},{8,9},{9,8},{10,11... | collective-permute-start | bytes 688136 | tf_op jit(solution)/shard_map/ppermute | solution.py:297
  52.5 2.7 %collective-permute-start.18 = (bf16[32,3584]{1,0:T(8,128)(2,1)S(1)}, bf16[32,3584]{1,0:T(8,128)(2,1)S(1)}, u32[]{:S(2)}, u32[]{:S(2)}) collective-permute-start(bf16[32,3584]{1,0:T(8,128)(2,1)S(1)} %collective-permute-done.6.refs_6_), channel_id=1, source_target_pairs={{0,1},{1,0},{2,3},{3,2},{4,5},{5,4},{6,7},{7,6},{8,9},{9,8},{10,11... | collective-permute-start | bytes 688136 | tf_op jit(solution)/shard_map/ppermute | solution.py:297
  53.1 6.8 %collective-permute-start.19 = (bf16[32,3584]{1,0:T(8,128)(2,1)S(1)}, bf16[32,3584]{1,0:T(8,128)(2,1)S(1)}, u32[]{:S(2)}, u32[]{:S(2)}) collective-permute-start(bf16[32,3584]{1,0:T(8,128)(2,1)S(1)} %constant_dynamic-update-slice_fusion.4.refs_5_), channel_id=1, source_target_pairs={{0,1},{1,0},{2,3},{3,2},{4,5},{5,4},{6,7},{7,6},{8,9},{9,8},{10,11... | collective-permute-start | bytes 688136 | tf_op jit(solution)/shard_map/ppermute | solution.py:297
  53.2 6.7 %collective-permute-start.16 = (bf16[128,640]{1,0:T(8,128)(2,1)S(1)}, bf16[128,640]{1,0:T(8,128)(2,1)S(1)}, u32[]{:S(2)}, u32[]{:S(2)}) collective-permute-start(bf16[128,640]{1,0:T(8,128)(2,1)S(1)} %constant_dynamic-update-slice_fusion.refs_1_), channel_id=1, source_target_pairs={{0,2},{1,3},{2,0},{3,1},{4,6},{5,7},{6,4},{7,5},{8,10},{9,11},{10,... | collective-permute-start | bytes 491528 | tf_op jit(solution)/shard_map/ppermute | solution.py:297
  55.0 4.9 %collective-permute-start.20 = (bf16[128,640]{1,0:T(8,128)(2,1)S(1)}, bf16[128,640]{1,0:T(8,128)(2,1)S(1)}, u32[]{:S(2)}, u32[]{:S(2)}) collective-permute-start(bf16[128,640]{1,0:T(8,128)(2,1)S(1)} %constant_dynamic-update-slice_fusion.refs_1_), channel_id=1, source_target_pairs={{0,1},{1,0},{2,3},{3,2},{4,5},{5,4},{6,7},{7,6},{8,9},{9,8},{10,11... | collective-permute-start | bytes 491528 | tf_op jit(solution)/shard_map/ppermute | solution.py:297
  59.9 1.4 %collective-permute-start.21 = (bf16[128,640]{1,0:T(8,128)(2,1)S(1)}, bf16[128,640]{1,0:T(8,128)(2,1)S(1)}, u32[]{:S(2)}, u32[]{:S(2)}) collective-permute-start(bf16[128,640]{1,0:T(8,128)(2,1)S(1)} %collective-permute-done.16.refs_2_), channel_id=1, source_target_pairs={{0,1},{1,0},{2,3},{3,2},{4,5},{5,4},{6,7},{7,6},{8,9},{9,8},{10,11... | collective-permute-start | bytes 491528 | tf_op jit(solution)/shard_map/ppermute | solution.py:297
  61.3 9.9 %slice-start.2 = ((s8[7340032]{0:T(1024)(128)(4,1)}), s8[4194304]{0:T(1024)(128)(4,1)S(1)}, s32[]{:S(2)}) async-start(s8[7340032]{0:T(1024)(128)(4,1)} %bitcast.67), calls=%async_computation.3 | async-start | bytes 8388608
  66.2 5.0 %slice-start.3 = ((s8[7340032]{0:T(1024)(128)(4,1)}), s8[3145728]{0:T(1024)(128)(4,1)S(1)}, s32[]{:S(2)}) async-start(s8[7340032]{0:T(1024)(128)(4,1)} %bitcast.67), calls=%async_computation.4 | async-start | bytes 6291456
  66.2 6.7 %slice-start.4 = ((s8[7340032]{0:T(1024)(128)(4,1)}), s8[4194304]{0:T(1024)(128)(4,1)S(1)}, s32[]{:S(2)}) async-start(s8[7340032]{0:T(1024)(128)(4,1)} %bitcast.69), calls=%async_computation.5 | async-start | bytes 8388608
  71.2 2.0 %slice-start.5 = ((s8[7340032]{0:T(1024)(128)(4,1)}), s8[3145728]{0:T(1024)(128)(4,1)S(1)}, s32[]{:S(2)}) async-start(s8[7340032]{0:T(1024)(128)(4,1)} %bitcast.69), calls=%async_computation.6 | async-start | bytes 6291456
  71.2 12.0 %slice-start = ((s8[7340032]{0:T(1024)(128)(4,1)}), s8[4194304]{0:T(1024)(128)(4,1)S(1)}, s32[]{:S(2)}) async-start(s8[7340032]{0:T(1024)(128)(4,1)} %bitcast.65), calls=%async_computation.1 | async-start | bytes 8388608
  73.2 10.1 %slice-start.1 = ((s8[7340032]{0:T(1024)(128)(4,1)}), s8[3145728]{0:T(1024)(128)(4,1)S(1)}, s32[]{:S(2)}) async-start(s8[7340032]{0:T(1024)(128)(4,1)} %bitcast.65), calls=%async_computation.2 | async-start | bytes 6291456
  74.8 6.2 %collective-permute-start.22 = (bf16[96,3584]{1,0:T(8,128)(2,1)S(1)}, bf16[96,3584]{1,0:T(8,128)(2,1)S(1)}, u32[]{:S(2)}, u32[]{:S(2)}) collective-permute-start(bf16[96,3584]{1,0:T(8,128)(2,1)S(1)} %slice.106), channel_id=1, source_target_pairs={{0,1},{1,0},{2,3},{3,2},{4,5},{5,4},{6,7},{7,6},{8,9},{9,8},{10,11... | collective-permute-start | bytes 2064392 | tf_op jit(solution)/shard_map/ppermute | solution.py:297
  81.1 7.4 %collective-permute-start.24 = (bf16[16,3584]{1,0:T(8,128)(2,1)S(1)}, bf16[16,3584]{1,0:T(8,128)(2,1)S(1)}, u32[]{:S(2)}, u32[]{:S(2)}) collective-permute-start(bf16[16,3584]{1,0:T(8,128)(2,1)S(1)} %get-tuple-element.145), channel_id=1, source_target_pairs={{0,2},{1,3},{4,0},{5,1},{8,4},{9,5},{12,8},{13,9},{14,12},{15,13},... | collective-permute-start | bytes 344072 | tf_op jit(solution)/shard_map/ppermute | solution.py:297
  82.9 5.6 %collective-permute-start.23 = (bf16[16,3584]{1,0:T(8,128)(2,1)S(1)}, bf16[16,3584]{1,0:T(8,128)(2,1)S(1)}, u32[]{:S(2)}, u32[]{:S(2)}) collective-permute-start(bf16[16,3584]{1,0:T(8,128)(2,1)S(1)} %get-tuple-element.146), channel_id=1, source_target_pairs={{0,4},{1,5},{4,8},{5,9},{8,12},{9,13},{12,14},{13,15},{14,10},{15,... | collective-permute-start | bytes 344072 | tf_op jit(solution)/shard_map/ppermute | solution.py:297
  91.1 9.7 %collective-permute-start.25 = (bf16[160,3584]{1,0:T(8,128)(2,1)S(1)}, bf16[160,3584]{1,0:T(8,128)(2,1)S(1)}, u32[]{:S(2)}, u32[]{:S(2)}) collective-permute-start(bf16[160,3584]{1,0:T(8,128)(2,1)S(1)} %slice.109), channel_id=1, source_target_pairs={{0,1},{1,0},{2,3},{3,2},{4,5},{5,4},{6,7},{7,6},{8,9},{9,8},{10,11... | collective-permute-start | bytes 3440648 | tf_op jit(solution)/shard_map/ppermute | solution.py:297
  91.4 8.1 %collective-permute-start.27 = (bf16[32,3584]{1,0:T(8,128)(2,1)S(1)}, bf16[32,3584]{1,0:T(8,128)(2,1)S(1)}, u32[]{:S(2)}, u32[]{:S(2)}) collective-permute-start(bf16[32,3584]{1,0:T(8,128)(2,1)S(1)} %get-tuple-element.143), channel_id=1, source_target_pairs={{0,2},{1,3},{4,0},{5,1},{8,4},{9,5},{12,8},{13,9},{14,12},{15,13},... | collective-permute-start | bytes 688136 | tf_op jit(solution)/shard_map/ppermute | solution.py:297
  93.1 7.7 %collective-permute-start.26 = (bf16[32,3584]{1,0:T(8,128)(2,1)S(1)}, bf16[32,3584]{1,0:T(8,128)(2,1)S(1)}, u32[]{:S(2)}, u32[]{:S(2)}) collective-permute-start(bf16[32,3584]{1,0:T(8,128)(2,1)S(1)} %get-tuple-element.144), channel_id=1, source_target_pairs={{0,4},{1,5},{4,8},{5,9},{8,12},{9,13},{12,14},{13,15},{14,10},{15,... | collective-permute-start | bytes 688136 | tf_op jit(solution)/shard_map/ppermute | solution.py:297
  101.0 7.0 %collective-permute-start.29 = (bf16[32,3584]{1,0:T(8,128)(2,1)S(1)}, bf16[32,3584]{1,0:T(8,128)(2,1)S(1)}, u32[]{:S(2)}, u32[]{:S(2)}) collective-permute-start(bf16[32,3584]{1,0:T(8,128)(2,1)S(1)} %get-tuple-element.141), channel_id=1, source_target_pairs={{0,2},{1,3},{4,0},{5,1},{8,4},{9,5},{12,8},{13,9},{14,12},{15,13},... | collective-permute-start | bytes 688136 | tf_op jit(solution)/shard_map/ppermute | solution.py:297
  102.2 7.1 %collective-permute-start.28 = (bf16[32,3584]{1,0:T(8,128)(2,1)S(1)}, bf16[32,3584]{1,0:T(8,128)(2,1)S(1)}, u32[]{:S(2)}, u32[]{:S(2)}) collective-permute-start(bf16[32,3584]{1,0:T(8,128)(2,1)S(1)} %get-tuple-element.142), channel_id=1, source_target_pairs={{0,4},{1,5},{4,8},{5,9},{8,12},{9,13},{12,14},{13,15},{14,10},{15,... | collective-permute-start | bytes 688136 | tf_op jit(solution)/shard_map/ppermute | solution.py:297
  109.5 6.3 %collective-permute-start.31 = (bf16[32,3584]{1,0:T(8,128)(2,1)S(1)}, bf16[32,3584]{1,0:T(8,128)(2,1)S(1)}, u32[]{:S(2)}, u32[]{:S(2)}) collective-permute-start(bf16[32,3584]{1,0:T(8,128)(2,1)S(1)} %get-tuple-element.139), channel_id=1, source_target_pairs={{0,2},{1,3},{4,0},{5,1},{8,4},{9,5},{12,8},{13,9},{14,12},{15,13},... | collective-permute-start | bytes 688136 | tf_op jit(solution)/shard_map/ppermute | solution.py:297
  111.3 6.0 %collective-permute-start.30 = (bf16[32,3584]{1,0:T(8,128)(2,1)S(1)}, bf16[32,3584]{1,0:T(8,128)(2,1)S(1)}, u32[]{:S(2)}, u32[]{:S(2)}) collective-permute-start(bf16[32,3584]{1,0:T(8,128)(2,1)S(1)} %get-tuple-element.140), channel_id=1, source_target_pairs={{0,4},{1,5},{4,8},{5,9},{8,12},{9,13},{12,14},{13,15},{14,10},{15,... | collective-permute-start | bytes 688136 | tf_op jit(solution)/shard_map/ppermute | solution.py:297
  (1 other events, 1.1 us)

commit v8 on v7

--- a/solution.py
+++ b/solution.py
@@ -131,7 +131,7 @@
     rows, width = resid_blocks[0].shape
     latent = w_out.shape[0]
     total = blocks * rows
-    cols = tile_of(width, 512)
+    cols = tile_of(width, 1024)
     packed = pooled[0].shape[1]
     experts_all = w_router_t.shape[0]
 
@@ -142,7 +142,7 @@
         return pl.BlockSpec((height, cols), lambda i: (0, i))
 
     gathered = sum(a.shape[0] for a in pooled)
-    need = total * (cols * 24 + packed * 2 + 8 * LANES * 4) + gathered * packed * 4 + 4 * latent * cols
+    need = total * (cols * 16 + packed * 2 + 8 * LANES * 4) + gathered * packed * 4 + 4 * latent * cols
     return pl.pallas_call(
         lambda *refs: norm_kernel(first, blocks, rows, latent, width, with_hidden, *refs),
         grid=(width // cols,),
@@ -176,6 +176,24 @@
     )(scalars, *pooled, *resid_blocks, w_out, gain, w_router_t)
 
 
+def lengths_kernel(owner, lengths, device, out):
+    rows = out.shape[0]
+    for j in range(rows):
+        length = lengths[owner[device[0] * rows + j]]
+        out[j : j + 1, :] = jnp.full((1, LANES), length, jnp.int32)
+
+
+def lengths_of(owner, lengths, device_index, rows):
+    scalar = pl.BlockSpec(memory_space=pltpu.SMEM)
+    return pl.pallas_call(
+        lengths_kernel,
+        in_specs=[scalar] * 3,
+        out_shape=jax.ShapeDtypeStruct((rows, LANES), jnp.int32),
+        cost_estimate=pl.CostEstimate(flops=10**10, bytes_accessed=10**8, transcendentals=0),
+        name="lengths",
+    )(owner, lengths, device_index[None])
+
+
 def attention_kernel(context, latent, q, cache, fresh, lengths, routes, packet, keys_a, keys_b, total):
     step = pl.program_id(0)
     rows, kv_width = q.shape[1], cache.shape[1]
@@ -254,7 +272,7 @@
             pltpu.VMEM((steps * rows, keys), jnp.float32),
         ],
         compiler_params=pltpu.CompilerParams(
-            dimension_semantics=("arbitrary",), vmem_limit_bytes=24 << 20
+            dimension_semantics=("arbitrary",), vmem_limit_bytes=(10 << 20) + 10240 * keys
         ),
         cost_estimate=pl.CostEstimate(
             flops=2 * steps * rows * heads * wide * keys,
@@ -312,18 +330,10 @@
     mine = resid.reshape(rows, width)
     held, sib = {0: mine}, {}
     held[-1], held[1] = around(mine, mine)
-    owner, lengths, held[-1], held[1] = hold((owner, lengths, held[-1], held[1]))
+    row_lengths = lengths_of(owner, lengths, device_index, row_count)
+    row_lengths, held[-1], held[1] = hold((row_lengths, held[-1], held[1]))
     held[-2], held[2] = around(held[-1], held[1])
     sib[0] = send(mine, sibling)
-    row_owner = lax.dynamic_slice_in_dim(owner, device_index * row_count, row_count)
-    row_lengths = jnp.sum(
-        jnp.where(
-            row_owner[:, None] == jnp.arange(owner.shape[0], dtype=jnp.int32), lengths[None, :], 0
-        ),
-        axis=1,
-        keepdims=True,
-    )
-    row_lengths = jnp.broadcast_to(row_lengths, (row_count, LANES))
     gain = norm_gain[None, :]
     scalars = jnp.array(
         [

time: 118 us -> 110 us (0.932)
  waiting for transfers between devices: 46.5 us -> 40.2 us
    ppermute x32, waiting for transfers between devices: 46.5 us -> 40.2 us  [send(): return lax.ppermute(a, 'expert', perm)]
    pallas_call x2, Pallas kernels: 10.5 us -> 8.71 us  [normalize(): pl.pallas_call(lambda *refs: norm_kernel(first, blocks, rows, latent, wid...]
    pallas_call x0 -> x1, Pallas kernels: none -> 1.41 us  [lengths_of(): pl.pallas_call(lengths_kernel, in_specs=[scalar] * 3, out_shape=jax.Shape...]
    all_to_all x1, starting transfers between devices: 7.53 us -> 6.29 us  [local(): lax.all_to_all(ordered, 'expert', split_axis=0, concat_axis=0, tiled=True)]
    unnamed x36 -> x34, local copies, waits for them, and re-layouts: 3 us -> 2.64 us
  transfers between devices with their start and end apart: 33 -> 33, of which waited for: 14 -> 14; matrix products, arithmetic and copies ran while one was open for 6% -> 8% of each run, Pallas kernels for 8% -> 9%
where the time goes in v8:
time: 110 us
  waiting for transfers between devices  40.2 us (37%)
  starting transfers between devices  32.3 us (29%)
  matrix products  17 us (15%)
  Pallas kernels  13.8 us (13%)
  local copies, waits for them, and re-layouts  4.94 us (4%)
  other arithmetic  1.36 us (1%)
    ppermute x32, waiting for transfers between devices, send(): return lax.ppermute(a, 'expert', perm)  40.2 us
    ppermute x32, starting transfers between devices, send(): return lax.ppermute(a, 'expert', perm)  26 us
    dot_general x6, matrix products, product(): return jnp.dot(a, w[0], preferred_element_type=f32)  16 us
    pallas_call x2, Pallas kernels, normalize(): pl.pallas_call(lambda *refs: norm_kernel(first, blocks, rows, latent, wid...  8.71 us
    all_to_all x1, starting transfers between devices, local(): lax.all_to_all(ordered, 'expert', split_axis=0, concat_axis=0, tiled=True)  6.29 us
    pallas_call x1, Pallas kernels, attention(): pl.pallas_call(lambda *refs: attention_kernel(context, latent, *refs), gr...  3.65 us
    unnamed x34, local copies, waits for them, and re-layouts  2.64 us
  transfers between devices with their start and end apart: 33, of which 14 were waited for; matrix products, arithmetic and copies ran while one was open for 8% of the time, Pallas kernels for 9%

profile of v8, /device:TPU:0, one launch (start us, length us, event | category | flops | bytes accessed | tf_op | source)
XLA Modules:
  0.0 110.0 jit_solution(3347344479799726714)
XLA Ops:
  0.0 0.5 collective-permute-start.4
  0.5 2.6 %collective-permute-start.1 = (bf16[32,3584]{1,0:T(8,128)(2,1)}, bf16[32,3584]{1,0:T(8,128)(2,1)S(1)}, u32[]{:S(2)}, u32[]{:S(2)}) collective-permute-start(bf16[32,3584]{1,0:T(8,128)(2,1)} %bitcast.60), channel_id=1, source_target_pairs={{0,2},{1,3},{4,0},{5,1},{8,4},{9,5},{12,8},{13,9},{14,12},{15,13},... | collective-permute-start | bytes 688136 | tf_op jit(solution)/shard_map/ppermute | solution.py:315
  3.2 1.0 fusion.30
  4.4 0.8 copy.19
  5.1 6.3 %all-to-all-start = ((bf16[16,2,8,576]{3,2,1,0:T(8,128)(2,1)}), bf16[16,2,8,576]{3,2,1,0:T(8,128)(2,1)S(1)}, u32[]{:S(2)}, u32[]{:S(2)}) async-start(bf16[16,2,8,576]{3,2,1,0:T(8,128)(2,1)} %copy.19), calls=%async_computation | async-start | bytes 655360 | tf_op jit(solution)/shard_map/all_to_all | solution.py:328
  11.5 1.4 %lengths.2.refs_3_ = s32[8,128]{1,0:T(8,128)} custom-call(s32[128]{0:T(128)} %owner.1, s32[128]{0:T(128)} %lengths.3, s32[1]{0:T(128)} %bitcast.4.device), custom_call_target="tpu_custom_call" | custom-call | flops 10000000000 | bytes 100000000 | tf_op jit(solution)/shard_map/lengths/pallas_call | solution.py:188
  12.9 2.0 %collective-permute-start.2 = (bf16[32,3584]{1,0:T(8,128)(2,1)S(1)}, bf16[32,3584]{1,0:T(8,128)(2,1)S(1)}, u32[]{:S(2)}, u32[]{:S(2)}) collective-permute-start(bf16[32,3584]{1,0:T(8,128)(2,1)S(1)} %collective-permute-done.refs_7_), channel_id=1, source_target_pairs={{0,4},{1,5},{4,8},{5,9},{8,12},{9,13},{12,14},{13,15},{14,10},{15,... | collective-permute-start | bytes 688136 | tf_op jit(solution)/shard_map/ppermute | solution.py:315
  15.0 0.7 dynamic-slice_bitcast_fusion.refs_0_
  15.7 0.5 collective-permute-start.8
  16.2 7.0 %collective-permute-done.2.refs_9_ = bf16[32,3584]{1,0:T(8,128)(2,1)S(1)} collective-permute-done((bf16[32,3584]{1,0:T(8,128)(2,1)S(1)}, bf16[32,3584]{1,0:T(8,128)(2,1)S(1)}, u32[]{:S(2)}, u32[]{:S(2)}) %collective-permute-start.2) | collective-permute-done | bytes 229408 | tf_op jit(solution)/shard_map/ppermute | solution.py:315
  23.2 1.5 %collective-permute-done.3.refs_8_ = bf16[32,3584]{1,0:T(8,128)(2,1)S(1)} collective-permute-done((bf16[32,3584]{1,0:T(8,128)(2,1)S(1)}, bf16[32,3584]{1,0:T(8,128)(2,1)S(1)}, u32[]{:S(2)}, u32[]{:S(2)}) %collective-permute-start.3) | collective-permute-done | bytes 229408 | tf_op jit(solution)/shard_map/ppermute | solution.py:315
  24.7 3.2 %collective-permute-start.5 = (bf16[32,3584]{1,0:T(8,128)(2,1)S(1)}, bf16[32,3584]{1,0:T(8,128)(2,1)S(1)}, u32[]{:S(2)}, u32[]{:S(2)}) collective-permute-start(bf16[32,3584]{1,0:T(8,128)(2,1)S(1)} %collective-permute-done.2.refs_9_), channel_id=1, source_target_pairs={{0,4},{1,5},{4,8},{5,9},{8,12},{9,13},{12,14},{13,15},{14,10},{15,... | collective-permute-start | bytes 688136 | tf_op jit(solution)/shard_map/ppermute | solution.py:315
  28.0 1.7 %copy-done.4 = bf16[4,8,36864]{2,1,0:T(8,128)(2,1)S(1)} copy-done((bf16[4,8,36864]{2,1,0:T(8,128)(2,1)S(1)}, bf16[4,8,36864]{2,1,0:T(8,128)(2,1)}, u32[]{:S(2)}) %copy-start.4) | copy-done | bytes 2359320
  29.6 0.7 copy-done.7
  30.3 3.7 %attention.1 = bf16[32,640]{1,0:T(8,128)(2,1)S(1)} custom-call(bf16[4,8,36864]{2,1,0:T(8,128)(2,1)S(1)} %copy-done.4, bf16[256,576]{1,0:T(8,128)(2,1)S(1)} %bitcast.58, bf16[32,576]{1,0:T(8,128)(2,1)S(1)} %bitcast.63, s32[8,128]{1,0:T(8,128)S(1)} %copy-done.7, s32[32,8]{1,0:T(8,128)S(1)} %bitcast.64), custom_call_target="tpu_custom_call" | custom-call | flops 754974720 | bytes 2359296 | tf_op jit(solution)/shard_map/attention/pallas_call | solution.py:262
  34.0 0.8 collective-permute-done.6.refs_6_
  34.8 0.5 collective-permute-start.15
  35.3 1.3 %collective-permute-start.11 = (bf16[32,640]{1,0:T(8,128)(2,1)S(1)}, bf16[32,640]{1,0:T(8,128)(2,1)S(1)}, u32[]{:S(2)}, u32[]{:S(2)}) collective-permute-start(bf16[32,640]{1,0:T(8,128)(2,1)S(1)} %attention.1), channel_id=1, source_target_pairs={{0,4},{1,5},{2,6},{3,7},{4,8},{5,9},{6,10},{7,11},{8,12},{9,13},{1... | collective-permute-start | bytes 122888 | tf_op jit(solution)/shard_map/ppermute | solution.py:315
  36.6 0.6 collective-permute-start.10
  37.3 1.8 %collective-permute-start.13 = (bf16[16,3584]{1,0:T(8,128)(2,1)S(1)}, bf16[16,3584]{1,0:T(8,128)(2,1)S(1)}, u32[]{:S(2)}, u32[]{:S(2)}) collective-permute-start(bf16[16,3584]{1,0:T(8,128)(2,1)S(1)} %slice.81), channel_id=1, source_target_pairs={{0,2},{1,3},{4,0},{5,1},{8,4},{9,5},{12,8},{13,9},{14,12},{15,13},... | collective-permute-start | bytes 344072 | tf_op jit(solution)/shard_map/ppermute | solution.py:315
  39.1 2.1 %collective-permute-done.11 = bf16[32,640]{1,0:T(8,128)(2,1)S(1)} collective-permute-done((bf16[32,640]{1,0:T(8,128)(2,1)S(1)}, bf16[32,640]{1,0:T(8,128)(2,1)S(1)}, u32[]{:S(2)}, u32[]{:S(2)}) %collective-permute-start.11) | collective-permute-done | bytes 40992 | tf_op jit(solution)/shard_map/ppermute | solution.py:315
  41.2 1.3 %collective-permute-done.10 = bf16[32,640]{1,0:T(8,128)(2,1)S(1)} collective-permute-done((bf16[32,640]{1,0:T(8,128)(2,1)S(1)}, bf16[32,640]{1,0:T(8,128)(2,1)S(1)}, u32[]{:S(2)}, u32[]{:S(2)}) %collective-permute-start.10) | collective-permute-done | bytes 40992 | tf_op jit(solution)/shard_map/ppermute | solution.py:315
  42.5 1.7 %collective-permute-start.9 = (bf16[32,640]{1,0:T(8,128)(2,1)S(1)}, bf16[32,640]{1,0:T(8,128)(2,1)S(1)}, u32[]{:S(2)}, u32[]{:S(2)}) collective-permute-start(bf16[32,640]{1,0:T(8,128)(2,1)S(1)} %attention.1), channel_id=1, source_target_pairs={{0,12},{1,13},{2,14},{3,15},{4,0},{5,1},{6,2},{7,3},{8,4},{9,5},{1... | collective-permute-start | bytes 122888 | tf_op jit(solution)/shard_map/ppermute | solution.py:315
  44.2 2.3 %collective-permute-done.9 = bf16[32,640]{1,0:T(8,128)(2,1)S(1)} collective-permute-done((bf16[32,640]{1,0:T(8,128)(2,1)S(1)}, bf16[32,640]{1,0:T(8,128)(2,1)S(1)}, u32[]{:S(2)}, u32[]{:S(2)}) %collective-permute-start.9) | collective-permute-done | bytes 40992 | tf_op jit(solution)/shard_map/ppermute | solution.py:315
  46.5 0.5 collective-permute-start.18
  47.2 1.7 %collective-permute-start.16 = (bf16[128,640]{1,0:T(8,128)(2,1)S(1)}, bf16[128,640]{1,0:T(8,128)(2,1)S(1)}, u32[]{:S(2)}, u32[]{:S(2)}) collective-permute-start(bf16[128,640]{1,0:T(8,128)(2,1)S(1)} %constant_dynamic-update-slice_fusion.refs_1_), channel_id=1, source_target_pairs={{0,2},{1,3},{2,0},{3,1},{4,6},{5,7},{6,4},{7,5},{8,10},{9,11},{10,... | collective-permute-start | bytes 491528 | tf_op jit(solution)/shard_map/ppermute | solution.py:315
  49.1 4.7 %collective-permute-done.16.refs_2_ = bf16[128,640]{1,0:T(8,128)(2,1)S(1)} collective-permute-done((bf16[128,640]{1,0:T(8,128)(2,1)S(1)}, bf16[128,640]{1,0:T(8,128)(2,1)S(1)}, u32[]{:S(2)}, u32[]{:S(2)}) %collective-permute-start.16) | collective-permute-done | bytes 163872 | tf_op jit(solution)/shard_map/ppermute | solution.py:315
  53.8 1.4 %collective-permute-done.21.refs_4_ = bf16[128,640]{1,0:T(8,128)(2,1)S(1)} collective-permute-done((bf16[128,640]{1,0:T(8,128)(2,1)S(1)}, bf16[128,640]{1,0:T(8,128)(2,1)S(1)}, u32[]{:S(2)}, u32[]{:S(2)}) %collective-permute-start.21) | collective-permute-done | bytes 163872 | tf_op jit(solution)/shard_map/ppermute | solution.py:315
  55.2 3.8 %normalize.2 = (bf16[192,3584]{1,0:T(8,128)(2,1)S(1)}, f32[192,128]{1,0:T(8,128)S(1)}, f32[192,128]{1,0:T(8,128)S(1)}) custom-call(s32[17]{0:T(128)S(1)} %dynamic-slice_bitcast_fusion.refs_0_, bf16[128,640]{1,0:T(8,128)(2,1)S(1)} %constant_dynamic-update-slice_fusion.refs_1_, bf16[128,640]{1,0:T(8,128)(2,1)S(1)} %collective-permute-done.16.refs_2_, ...), custom_call_target="tpu_custom_call" | custom-call | flops 704643072 | bytes 6422528 | tf_op jit(solution)/shard_map/normalize/pallas_call | solution.py:146
  59.2 4.9 %fusion.24 = f32[192,1024]{1,0:T(8,128)S(1)} fusion(bf16[192,3584]{1,0:T(8,128)(2,1)S(1)} %get-tuple-element.103, bf16[1,3584,1024]{2,1,0:T(8,128)(2,1)} %param.24, f32[192]{0:T(256)S(1)} %get-tuple-element.146), kind=kOutput, calls=%fused_computation.17 | convolution fusion | flops 1409482752 | bytes 9503488 | tf_op jit(solution)/shard_map/dot_general | solution.py:385
  64.3 1.7 %multiply_convert_fusion.1 = bf16[192,1024]{1,0:T(8,128)(2,1)S(1)} fusion(f32[192,1024]{1,0:T(8,128)S(1)} %fusion.24, f32[192]{0:T(256)S(1)} %get-tuple-element.145, f32[192]{0:T(256)S(1)} %get-tuple-element.146, bf16[192,3584]{1,0:T(8,128)(2,1)S(1)} %get-tuple-element.103, bf16[1,3584,1024]{2,1,0:T(8,128)(2,1)S(1)} %bitcast.69), kind=kOutput, calls=%fused_computation.21 | convolution fusion | flops 1410859008 | bytes 9897472 | tf_op jit(solution)/shard_map/dot_general | solution.py:385
  66.2 1.6 %fusion.15 = bf16[192,3584]{1,0:T(8,128)(2,1)S(1)} fusion(bf16[192,1024]{1,0:T(8,128)(2,1)S(1)} %multiply_convert_fusion.1, bf16[1,1024,3584]{2,1,0:T(8,128)(2,1)S(1)} %bitcast.71), kind=kOutput, calls=%fused_computation.13 | convolution fusion | flops 1409974272 | bytes 9109504 | tf_op jit(solution)/shard_map/dot_general | solution.py:385
  68.0 4.9 %normalize.3 = (bf16[320,3584]{1,0:T(8,128)(2,1)S(1)}, f32[320,128]{1,0:T(8,128)S(1)}, f32[320,128]{1,0:T(8,128)S(1)}, f32[32,3584]{1,0:T(8,128)S(1)}) custom-call(s32[17]{0:T(128)S(1)} %dynamic-slice_bitcast_fusion.refs_0_, bf16[128,640]{1,0:T(8,128)(2,1)S(1)} %constant_dynamic-update-slice_fusion.refs_1_, ...), custom_call_target="tpu_custom_call" | custom-call | flops 1174405120 | bytes 8257536 | tf_op jit(solution)/shard_map/normalize/pallas_call | solution.py:146
  73.3 1.7 %collective-permute-start.24 = (bf16[16,3584]{1,0:T(8,128)(2,1)S(1)}, bf16[16,3584]{1,0:T(8,128)(2,1)S(1)}, u32[]{:S(2)}, u32[]{:S(2)}) collective-permute-start(bf16[16,3584]{1,0:T(8,128)(2,1)S(1)} %get-tuple-element.143), channel_id=1, source_target_pairs={{0,2},{1,3},{4,0},{5,1},{8,4},{9,5},{12,8},{13,9},{14,12},{15,13},... | collective-permute-start | bytes 344072 | tf_op jit(solution)/shard_map/ppermute | solution.py:315
  75.4 2.5 %fusion.18 = f32[320,1024]{1,0:T(8,128)S(1)} fusion(bf16[320,3584]{1,0:T(8,128)(2,1)S(1)} %get-tuple-element.121, bf16[1,3584,1024]{2,1,0:T(8,128)(2,1)S(1)} %bitcast.67, f32[320]{0:T(512)S(1)} %slice_reduce_fusion.1), kind=kOutput, calls=%fused_computation.14 | convolution fusion | flops 2349137920 | bytes 10945792 | tf_op jit(solution)/shard_map/dot_general | solution.py:385
  77.9 2.7 %multiply_convert_fusion = bf16[320,1024]{1,0:T(8,128)(2,1)S(1)} fusion(f32[320,1024]{1,0:T(8,128)S(1)} %fusion.18, f32[320]{0:T(512)S(1)} %slice_reduce_fusion, f32[320]{0:T(512)S(1)} %slice_reduce_fusion.1, bf16[320,3584]{1,0:T(8,128)(2,1)S(1)} %get-tuple-element.121, bf16[1,3584,1024]{2,1,0:T(8,128)(2,1)S(1)} %bitcast.69), kind=kOutput, calls=%fused_computation.16 | convolution fusion | flops 2351431680 | bytes 11602432 | tf_op jit(solution)/shard_map/dot_general | solution.py:385
  80.7 2.6 %fusion.12 = bf16[320,3584]{1,0:T(8,128)(2,1)S(1)} fusion(bf16[320,1024]{1,0:T(8,128)(2,1)S(1)} %multiply_convert_fusion, bf16[1,1024,3584]{2,1,0:T(8,128)(2,1)S(1)} %bitcast.71), kind=kOutput, calls=%fused_computation.12 | convolution fusion | flops 2349957120 | bytes 10289152 | tf_op jit(solution)/shard_map/dot_general | solution.py:385
  83.5 1.7 %collective-permute-start.27 = (bf16[32,3584]{1,0:T(8,128)(2,1)S(1)}, bf16[32,3584]{1,0:T(8,128)(2,1)S(1)}, u32[]{:S(2)}, u32[]{:S(2)}) collective-permute-start(bf16[32,3584]{1,0:T(8,128)(2,1)S(1)} %get-tuple-element.141), channel_id=1, source_target_pairs={{0,2},{1,3},{4,0},{5,1},{8,4},{9,5},{12,8},{13,9},{14,12},{15,13},... | collective-permute-start | bytes 688136 | tf_op jit(solution)/shard_map/ppermute | solution.py:315
  85.6 6.0 %collective-permute-done.27 = bf16[32,3584]{1,0:T(8,128)(2,1)S(1)} collective-permute-done((bf16[32,3584]{1,0:T(8,128)(2,1)S(1)}, bf16[32,3584]{1,0:T(8,128)(2,1)S(1)}, u32[]{:S(2)}, u32[]{:S(2)}) %collective-permute-start.27) | collective-permute-done | bytes 229408 | tf_op jit(solution)/shard_map/ppermute | solution.py:315
  91.6 1.4 %collective-permute-done.26 = bf16[32,3584]{1,0:T(8,128)(2,1)S(1)} collective-permute-done((bf16[32,3584]{1,0:T(8,128)(2,1)S(1)}, bf16[32,3584]{1,0:T(8,128)(2,1)S(1)}, u32[]{:S(2)}, u32[]{:S(2)}) %collective-permute-start.26) | collective-permute-done | bytes 229408 | tf_op jit(solution)/shard_map/ppermute | solution.py:315
  93.1 0.9 collective-permute-start.29
  94.0 1.2 %collective-permute-start.28 = (bf16[32,3584]{1,0:T(8,128)(2,1)S(1)}, bf16[32,3584]{1,0:T(8,128)(2,1)S(1)}, u32[]{:S(2)}, u32[]{:S(2)}) collective-permute-start(bf16[32,3584]{1,0:T(8,128)(2,1)S(1)} %get-tuple-element.140), channel_id=1, source_target_pairs={{0,4},{1,5},{4,8},{5,9},{8,12},{9,13},{12,14},{13,15},{14,10},{15,... | collective-permute-start | bytes 688136 | tf_op jit(solution)/shard_map/ppermute | solution.py:315
  95.2 4.9 %collective-permute-done.29 = bf16[32,3584]{1,0:T(8,128)(2,1)S(1)} collective-permute-done((bf16[32,3584]{1,0:T(8,128)(2,1)S(1)}, bf16[32,3584]{1,0:T(8,128)(2,1)S(1)}, u32[]{:S(2)}, u32[]{:S(2)}) %collective-permute-start.29) | collective-permute-done | bytes 229408 | tf_op jit(solution)/shard_map/ppermute | solution.py:315
  100.1 1.0 collective-permute-done.28
  101.3 1.8 %collective-permute-start.31 = (bf16[32,3584]{1,0:T(8,128)(2,1)S(1)}, bf16[32,3584]{1,0:T(8,128)(2,1)S(1)}, u32[]{:S(2)}, u32[]{:S(2)}) collective-permute-start(bf16[32,3584]{1,0:T(8,128)(2,1)S(1)} %get-tuple-element.137), channel_id=1, source_target_pairs={{0,2},{1,3},{4,0},{5,1},{8,4},{9,5},{12,8},{13,9},{14,12},{15,13},... | collective-permute-start | bytes 688136 | tf_op jit(solution)/shard_map/ppermute | solution.py:315
  103.4 4.2 %collective-permute-done.31 = bf16[32,3584]{1,0:T(8,128)(2,1)S(1)} collective-permute-done((bf16[32,3584]{1,0:T(8,128)(2,1)S(1)}, bf16[32,3584]{1,0:T(8,128)(2,1)S(1)}, u32[]{:S(2)}, u32[]{:S(2)}) %collective-permute-start.31) | collective-permute-done | bytes 229408 | tf_op jit(solution)/shard_map/ppermute | solution.py:315
  107.6 1.6 %collective-permute-done.30 = bf16[32,3584]{1,0:T(8,128)(2,1)S(1)} collective-permute-done((bf16[32,3584]{1,0:T(8,128)(2,1)S(1)}, bf16[32,3584]{1,0:T(8,128)(2,1)S(1)}, u32[]{:S(2)}, u32[]{:S(2)}) %collective-permute-start.30) | collective-permute-done | bytes 229408 | tf_op jit(solution)/shard_map/ppermute | solution.py:315
  109.1 0.8 fusion.35
  (85 shorter events, 3.6 us)
Async XLA Ops:
  0.0 3.2 %copy-start = (bf16[128,2,576]{0,2,1:T(8,128)(2,1)S(1)}, bf16[128,2,576]{0,2,1:T(8,128)(2,1)}, u32[]{:S(2)}) copy-start(bf16[128,2,576]{0,2,1:T(8,128)(2,1)} %param.16) | copy-start | bytes 884740
  0.0 16.2 %collective-permute-start.4 = (bf16[32,3584]{1,0:T(8,128)(2,1)}, bf16[32,3584]{1,0:T(8,128)(2,1)S(1)}, u32[]{:S(2)}, u32[]{:S(2)}) collective-permute-start(bf16[32,3584]{1,0:T(8,128)(2,1)} %bitcast.59), channel_id=1, source_target_pairs={{0,1},{1,0},{2,3},{3,2},{4,5},{5,4},{6,7},{7,6},{8,9},{9,8},{10,11... | collective-permute-start | bytes 688136 | tf_op jit(solution)/shard_map/ppermute | solution.py:315
  0.5 12.4 %collective-permute-start.1 = (bf16[32,3584]{1,0:T(8,128)(2,1)}, bf16[32,3584]{1,0:T(8,128)(2,1)S(1)}, u32[]{:S(2)}, u32[]{:S(2)}) collective-permute-start(bf16[32,3584]{1,0:T(8,128)(2,1)} %bitcast.60), channel_id=1, source_target_pairs={{0,2},{1,3},{4,0},{5,1},{8,4},{9,5},{12,8},{13,9},{14,12},{15,13},... | collective-permute-start | bytes 688136 | tf_op jit(solution)/shard_map/ppermute | solution.py:315
  3.0 9.9 %collective-permute-start = (bf16[32,3584]{1,0:T(8,128)(2,1)}, bf16[32,3584]{1,0:T(8,128)(2,1)S(1)}, u32[]{:S(2)}, u32[]{:S(2)}) collective-permute-start(bf16[32,3584]{1,0:T(8,128)(2,1)} %bitcast.61), channel_id=1, source_target_pairs={{0,4},{1,5},{4,8},{5,9},{8,12},{9,13},{12,14},{13,15},{14,10},{15,... | collective-permute-start | bytes 688136 | tf_op jit(solution)/shard_map/ppermute | solution.py:315
  5.1 19.6 %all-to-all-start = ((bf16[16,2,8,576]{3,2,1,0:T(8,128)(2,1)}), bf16[16,2,8,576]{3,2,1,0:T(8,128)(2,1)S(1)}, u32[]{:S(2)}, u32[]{:S(2)}) async-start(bf16[16,2,8,576]{3,2,1,0:T(8,128)(2,1)} %copy.19), calls=%async_computation | async-start | bytes 655360 | tf_op jit(solution)/shard_map/all_to_all | solution.py:328
  11.4 3.5 %copy-start.8 = (bf16[3584]{0:T(1024)(128)(2,1)S(1)}, bf16[3584]{0:T(1024)(128)(2,1)}, u32[]{:S(2)}) copy-start(bf16[3584]{0:T(1024)(128)(2,1)} %param.22) | copy-start | bytes 21508
  11.4 16.5 %copy-start.5 = (bf16[4,8,576]{2,1,0:T(8,128)(2,1)S(1)}, bf16[4,8,576]{2,1,0:T(8,128)(2,1)}, u32[]{:S(2)}) copy-start(bf16[4,8,576]{2,1,0:T(8,128)(2,1)} %param.15) | copy-start | bytes 110596
  11.5 16.5 %copy-start.6 = (s32[4,8,8]{2,1,0:T(8,128)S(1)}, s32[4,8,8]{2,1,0:T(8,128)}, u32[]{:S(2)}) copy-start(s32[4,8,8]{2,1,0:T(8,128)} %param.20) | copy-start | bytes 3076
  12.9 42.3 %copy-start.2 = (bf16[3584,16]{0,1:T(8,128)(2,1)S(1)}, bf16[3584,16]{0,1:T(8,128)(2,1)}, u32[]{:S(2)}) copy-start(bf16[3584,16]{0,1:T(8,128)(2,1)} %param.23) | copy-start | bytes 344068
  12.9 10.3 %collective-permute-start.2 = (bf16[32,3584]{1,0:T(8,128)(2,1)S(1)}, bf16[32,3584]{1,0:T(8,128)(2,1)S(1)}, u32[]{:S(2)}, u32[]{:S(2)}) collective-permute-start(bf16[32,3584]{1,0:T(8,128)(2,1)S(1)} %collective-permute-done.refs_7_), channel_id=1, source_target_pairs={{0,4},{1,5},{4,8},{5,9},{8,12},{9,13},{12,14},{13,15},{14,10},{15,... | collective-permute-start | bytes 688136 | tf_op jit(solution)/shard_map/ppermute | solution.py:315
  14.9 9.9 %collective-permute-start.3 = (bf16[32,3584]{1,0:T(8,128)(2,1)S(1)}, bf16[32,3584]{1,0:T(8,128)(2,1)S(1)}, u32[]{:S(2)}, u32[]{:S(2)}) collective-permute-start(bf16[32,3584]{1,0:T(8,128)(2,1)S(1)} %collective-permute-done.1.refs_6_), channel_id=1, source_target_pairs={{0,2},{1,3},{4,0},{5,1},{8,4},{9,5},{12,8},{13,9},{14,12},{15,13},... | collective-permute-start | bytes 688136 | tf_op jit(solution)/shard_map/ppermute | solution.py:315
  15.7 18.3 %collective-permute-start.7 = (bf16[32,3584]{1,0:T(8,128)(2,1)S(1)}, bf16[32,3584]{1,0:T(8,128)(2,1)S(1)}, u32[]{:S(2)}, u32[]{:S(2)}) collective-permute-start(bf16[32,3584]{1,0:T(8,128)(2,1)S(1)} %collective-permute-done.refs_7_), channel_id=1, source_target_pairs={{0,1},{1,0},{2,3},{3,2},{4,5},{5,4},{6,7},{7,6},{8,9},{9,8},{10,11... | collective-permute-start | bytes 688136 | tf_op jit(solution)/shard_map/ppermute | solution.py:315
  15.7 18.3 %collective-permute-start.8 = (bf16[32,3584]{1,0:T(8,128)(2,1)S(1)}, bf16[32,3584]{1,0:T(8,128)(2,1)S(1)}, u32[]{:S(2)}, u32[]{:S(2)}) collective-permute-start(bf16[32,3584]{1,0:T(8,128)(2,1)S(1)} %collective-permute-done.1.refs_6_), channel_id=1, source_target_pairs={{0,1},{1,0},{2,3},{3,2},{4,5},{5,4},{6,7},{7,6},{8,9},{9,8},{10,11... | collective-permute-start | bytes 688136 | tf_op jit(solution)/shard_map/ppermute | solution.py:315
  24.7 30.5 %copy-start.1 = (bf16[512,3584]{1,0:T(8,128)(2,1)S(1)}, bf16[512,3584]{1,0:T(8,128)(2,1)}, u32[]{:S(2)}) copy-start(bf16[512,3584]{1,0:T(8,128)(2,1)} %refs_15_.1) | copy-start | bytes 11010052
  24.7 9.3 %collective-permute-start.5 = (bf16[32,3584]{1,0:T(8,128)(2,1)S(1)}, bf16[32,3584]{1,0:T(8,128)(2,1)S(1)}, u32[]{:S(2)}, u32[]{:S(2)}) collective-permute-start(bf16[32,3584]{1,0:T(8,128)(2,1)S(1)} %collective-permute-done.2.refs_9_), channel_id=1, source_target_pairs={{0,4},{1,5},{4,8},{5,9},{8,12},{9,13},{12,14},{13,15},{14,10},{15,... | collective-permute-start | bytes 688136 | tf_op jit(solution)/shard_map/ppermute | solution.py:315
  28.0 6.9 %collective-permute-start.6 = (bf16[32,3584]{1,0:T(8,128)(2,1)S(1)}, bf16[32,3584]{1,0:T(8,128)(2,1)S(1)}, u32[]{:S(2)}, u32[]{:S(2)}) collective-permute-start(bf16[32,3584]{1,0:T(8,128)(2,1)S(1)} %collective-permute-done.3.refs_8_), channel_id=1, source_target_pairs={{0,2},{1,3},{4,0},{5,1},{8,4},{9,5},{12,8},{13,9},{14,12},{15,13},... | collective-permute-start | bytes 688136 | tf_op jit(solution)/shard_map/ppermute | solution.py:315
  28.0 1.7 %copy-start.4 = (bf16[4,8,36864]{2,1,0:T(8,128)(2,1)S(1)}, bf16[4,8,36864]{2,1,0:T(8,128)(2,1)}, u32[]{:S(2)}) copy-start(bf16[4,8,36864]{2,1,0:T(8,128)(2,1)} %refs_0_.1) | copy-start | bytes 7077892
  29.6 0.7 copy-start.7
  34.8 12.2 %collective-permute-start.14 = (bf16[32,3584]{1,0:T(8,128)(2,1)S(1)}, bf16[32,3584]{1,0:T(8,128)(2,1)S(1)}, u32[]{:S(2)}, u32[]{:S(2)}) collective-permute-start(bf16[32,3584]{1,0:T(8,128)(2,1)S(1)} %collective-permute-done.2.refs_9_), channel_id=1, source_target_pairs={{0,1},{1,0},{2,3},{3,2},{4,5},{5,4},{6,7},{7,6},{8,9},{9,8},{10,11... | collective-permute-start | bytes 688136 | tf_op jit(solution)/shard_map/ppermute | solution.py:315
  34.8 12.2 %collective-permute-start.15 = (bf16[32,3584]{1,0:T(8,128)(2,1)S(1)}, bf16[32,3584]{1,0:T(8,128)(2,1)S(1)}, u32[]{:S(2)}, u32[]{:S(2)}) collective-permute-start(bf16[32,3584]{1,0:T(8,128)(2,1)S(1)} %collective-permute-done.3.refs_8_), channel_id=1, source_target_pairs={{0,1},{1,0},{2,3},{3,2},{4,5},{5,4},{6,7},{7,6},{8,9},{9,8},{10,11... | collective-permute-start | bytes 688136 | tf_op jit(solution)/shard_map/ppermute | solution.py:315
  35.3 5.9 %collective-permute-start.11 = (bf16[32,640]{1,0:T(8,128)(2,1)S(1)}, bf16[32,640]{1,0:T(8,128)(2,1)S(1)}, u32[]{:S(2)}, u32[]{:S(2)}) collective-permute-start(bf16[32,640]{1,0:T(8,128)(2,1)S(1)} %attention.1), channel_id=1, source_target_pairs={{0,4},{1,5},{2,6},{3,7},{4,8},{5,9},{6,10},{7,11},{8,12},{9,13},{1... | collective-permute-start | bytes 122888 | tf_op jit(solution)/shard_map/ppermute | solution.py:315
  36.6 5.9 %collective-permute-start.10 = (bf16[32,640]{1,0:T(8,128)(2,1)S(1)}, bf16[32,640]{1,0:T(8,128)(2,1)S(1)}, u32[]{:S(2)}, u32[]{:S(2)}) collective-permute-start(bf16[32,640]{1,0:T(8,128)(2,1)S(1)} %attention.1), channel_id=1, source_target_pairs={{0,8},{1,9},{2,10},{3,11},{4,12},{5,13},{6,14},{7,15},{8,0},{9,1},... | collective-permute-start | bytes 122888 | tf_op jit(solution)/shard_map/ppermute | solution.py:315
  37.3 9.2 %collective-permute-start.13 = (bf16[16,3584]{1,0:T(8,128)(2,1)S(1)}, bf16[16,3584]{1,0:T(8,128)(2,1)S(1)}, u32[]{:S(2)}, u32[]{:S(2)}) collective-permute-start(bf16[16,3584]{1,0:T(8,128)(2,1)S(1)} %slice.81), channel_id=1, source_target_pairs={{0,2},{1,3},{4,0},{5,1},{8,4},{9,5},{12,8},{13,9},{14,12},{15,13},... | collective-permute-start | bytes 344072 | tf_op jit(solution)/shard_map/ppermute | solution.py:315
  41.2 5.8 %collective-permute-start.12 = (bf16[16,3584]{1,0:T(8,128)(2,1)S(1)}, bf16[16,3584]{1,0:T(8,128)(2,1)S(1)}, u32[]{:S(2)}, u32[]{:S(2)}) collective-permute-start(bf16[16,3584]{1,0:T(8,128)(2,1)S(1)} %slice.80), channel_id=1, source_target_pairs={{0,4},{1,5},{4,8},{5,9},{8,12},{9,13},{12,14},{13,15},{14,10},{15,... | collective-permute-start | bytes 344072 | tf_op jit(solution)/shard_map/ppermute | solution.py:315
  42.5 4.0 %collective-permute-start.9 = (bf16[32,640]{1,0:T(8,128)(2,1)S(1)}, bf16[32,640]{1,0:T(8,128)(2,1)S(1)}, u32[]{:S(2)}, u32[]{:S(2)}) collective-permute-start(bf16[32,640]{1,0:T(8,128)(2,1)S(1)} %attention.1), channel_id=1, source_target_pairs={{0,12},{1,13},{2,14},{3,15},{4,0},{5,1},{6,2},{7,3},{8,4},{9,5},{1... | collective-permute-start | bytes 122888 | tf_op jit(solution)/shard_map/ppermute | solution.py:315
  46.5 2.6 %collective-permute-start.17 = (bf16[32,3584]{1,0:T(8,128)(2,1)S(1)}, bf16[32,3584]{1,0:T(8,128)(2,1)S(1)}, u32[]{:S(2)}, u32[]{:S(2)}) collective-permute-start(bf16[32,3584]{1,0:T(8,128)(2,1)S(1)} %collective-permute-done.5.refs_7_), channel_id=1, source_target_pairs={{0,1},{1,0},{2,3},{3,2},{4,5},{5,4},{6,7},{7,6},{8,9},{9,8},{10,11... | collective-permute-start | bytes 688136 | tf_op jit(solution)/shard_map/ppermute | solution.py:315
  46.5 2.6 %collective-permute-start.18 = (bf16[32,3584]{1,0:T(8,128)(2,1)S(1)}, bf16[32,3584]{1,0:T(8,128)(2,1)S(1)}, u32[]{:S(2)}, u32[]{:S(2)}) collective-permute-start(bf16[32,3584]{1,0:T(8,128)(2,1)S(1)} %collective-permute-done.6.refs_6_), channel_id=1, source_target_pairs={{0,1},{1,0},{2,3},{3,2},{4,5},{5,4},{6,7},{7,6},{8,9},{9,8},{10,11... | collective-permute-start | bytes 688136 | tf_op jit(solution)/shard_map/ppermute | solution.py:315
  47.0 6.8 %collective-permute-start.19 = (bf16[32,3584]{1,0:T(8,128)(2,1)S(1)}, bf16[32,3584]{1,0:T(8,128)(2,1)S(1)}, u32[]{:S(2)}, u32[]{:S(2)}) collective-permute-start(bf16[32,3584]{1,0:T(8,128)(2,1)S(1)} %constant_dynamic-update-slice_fusion.4.refs_5_), channel_id=1, source_target_pairs={{0,1},{1,0},{2,3},{3,2},{4,5},{5,4},{6,7},{7,6},{8,9},{9,8},{10,11... | collective-permute-start | bytes 688136 | tf_op jit(solution)/shard_map/ppermute | solution.py:315
  47.2 6.7 %collective-permute-start.16 = (bf16[128,640]{1,0:T(8,128)(2,1)S(1)}, bf16[128,640]{1,0:T(8,128)(2,1)S(1)}, u32[]{:S(2)}, u32[]{:S(2)}) collective-permute-start(bf16[128,640]{1,0:T(8,128)(2,1)S(1)} %constant_dynamic-update-slice_fusion.refs_1_), channel_id=1, source_target_pairs={{0,2},{1,3},{2,0},{3,1},{4,6},{5,7},{6,4},{7,5},{8,10},{9,11},{10,... | collective-permute-start | bytes 491528 | tf_op jit(solution)/shard_map/ppermute | solution.py:315
  48.9 4.9 %collective-permute-start.20 = (bf16[128,640]{1,0:T(8,128)(2,1)S(1)}, bf16[128,640]{1,0:T(8,128)(2,1)S(1)}, u32[]{:S(2)}, u32[]{:S(2)}) collective-permute-start(bf16[128,640]{1,0:T(8,128)(2,1)S(1)} %constant_dynamic-update-slice_fusion.refs_1_), channel_id=1, source_target_pairs={{0,1},{1,0},{2,3},{3,2},{4,5},{5,4},{6,7},{7,6},{8,9},{9,8},{10,11... | collective-permute-start | bytes 491528 | tf_op jit(solution)/shard_map/ppermute | solution.py:315
  53.8 1.4 %collective-permute-start.21 = (bf16[128,640]{1,0:T(8,128)(2,1)S(1)}, bf16[128,640]{1,0:T(8,128)(2,1)S(1)}, u32[]{:S(2)}, u32[]{:S(2)}) collective-permute-start(bf16[128,640]{1,0:T(8,128)(2,1)S(1)} %collective-permute-done.16.refs_2_), channel_id=1, source_target_pairs={{0,1},{1,0},{2,3},{3,2},{4,5},{5,4},{6,7},{7,6},{8,9},{9,8},{10,11... | collective-permute-start | bytes 491528 | tf_op jit(solution)/shard_map/ppermute | solution.py:315
  55.2 9.0 %slice-start.2 = ((s8[7340032]{0:T(1024)(128)(4,1)}), s8[4194304]{0:T(1024)(128)(4,1)S(1)}, s32[]{:S(2)}) async-start(s8[7340032]{0:T(1024)(128)(4,1)} %bitcast.68), calls=%async_computation.3 | async-start | bytes 8388608
  59.2 5.0 %slice-start.3 = ((s8[7340032]{0:T(1024)(128)(4,1)}), s8[3145728]{0:T(1024)(128)(4,1)S(1)}, s32[]{:S(2)}) async-start(s8[7340032]{0:T(1024)(128)(4,1)} %bitcast.68), calls=%async_computation.4 | async-start | bytes 6291456
  59.2 6.8 %slice-start.4 = ((s8[7340032]{0:T(1024)(128)(4,1)}), s8[4194304]{0:T(1024)(128)(4,1)S(1)}, s32[]{:S(2)}) async-start(s8[7340032]{0:T(1024)(128)(4,1)} %bitcast.70), calls=%async_computation.5 | async-start | bytes 8388608
  64.2 2.0 %slice-start.5 = ((s8[7340032]{0:T(1024)(128)(4,1)}), s8[3145728]{0:T(1024)(128)(4,1)S(1)}, s32[]{:S(2)}) async-start(s8[7340032]{0:T(1024)(128)(4,1)} %bitcast.70), calls=%async_computation.6 | async-start | bytes 6291456
  64.2 11.2 %slice-start = ((s8[7340032]{0:T(1024)(128)(4,1)}), s8[4194304]{0:T(1024)(128)(4,1)S(1)}, s32[]{:S(2)}) async-start(s8[7340032]{0:T(1024)(128)(4,1)} %bitcast.66), calls=%async_computation.1 | async-start | bytes 8388608
  66.2 1.9 %copy-start.3 = (bf16[4,8,3584]{2,1,0:T(8,128)(2,1)S(1)}, bf16[4,8,3584]{2,1,0:T(8,128)(2,1)}, u32[]{:S(2)}) copy-start(bf16[4,8,3584]{2,1,0:T(8,128)(2,1)} %param.19) | copy-start | bytes 688132
  66.2 9.2 %slice-start.1 = ((s8[7340032]{0:T(1024)(128)(4,1)}), s8[3145728]{0:T(1024)(128)(4,1)S(1)}, s32[]{:S(2)}) async-start(s8[7340032]{0:T(1024)(128)(4,1)} %bitcast.66), calls=%async_computation.2 | async-start | bytes 6291456
  67.8 5.4 %collective-permute-start.22 = (bf16[96,3584]{1,0:T(8,128)(2,1)S(1)}, bf16[96,3584]{1,0:T(8,128)(2,1)S(1)}, u32[]{:S(2)}, u32[]{:S(2)}) collective-permute-start(bf16[96,3584]{1,0:T(8,128)(2,1)S(1)} %slice.106), channel_id=1, source_target_pairs={{0,1},{1,0},{2,3},{3,2},{4,5},{5,4},{6,7},{7,6},{8,9},{9,8},{10,11... | collective-permute-start | bytes 2064392 | tf_op jit(solution)/shard_map/ppermute | solution.py:315
  73.3 7.4 %collective-permute-start.24 = (bf16[16,3584]{1,0:T(8,128)(2,1)S(1)}, bf16[16,3584]{1,0:T(8,128)(2,1)S(1)}, u32[]{:S(2)}, u32[]{:S(2)}) collective-permute-start(bf16[16,3584]{1,0:T(8,128)(2,1)S(1)} %get-tuple-element.143), channel_id=1, source_target_pairs={{0,2},{1,3},{4,0},{5,1},{8,4},{9,5},{12,8},{13,9},{14,12},{15,13},... | collective-permute-start | bytes 344072 | tf_op jit(solution)/shard_map/ppermute | solution.py:315
  75.0 5.6 %collective-permute-start.23 = (bf16[16,3584]{1,0:T(8,128)(2,1)S(1)}, bf16[16,3584]{1,0:T(8,128)(2,1)S(1)}, u32[]{:S(2)}, u32[]{:S(2)}) collective-permute-start(bf16[16,3584]{1,0:T(8,128)(2,1)S(1)} %get-tuple-element.144), channel_id=1, source_target_pairs={{0,4},{1,5},{4,8},{5,9},{8,12},{9,13},{12,14},{13,15},{14,10},{15,... | collective-permute-start | bytes 344072 | tf_op jit(solution)/shard_map/ppermute | solution.py:315
  83.3 9.7 %collective-permute-start.25 = (bf16[160,3584]{1,0:T(8,128)(2,1)S(1)}, bf16[160,3584]{1,0:T(8,128)(2,1)S(1)}, u32[]{:S(2)}, u32[]{:S(2)}) collective-permute-start(bf16[160,3584]{1,0:T(8,128)(2,1)S(1)} %slice.109), channel_id=1, source_target_pairs={{0,1},{1,0},{2,3},{3,2},{4,5},{5,4},{6,7},{7,6},{8,9},{9,8},{10,11... | collective-permute-start | bytes 3440648 | tf_op jit(solution)/shard_map/ppermute | solution.py:315
  83.5 8.1 %collective-permute-start.27 = (bf16[32,3584]{1,0:T(8,128)(2,1)S(1)}, bf16[32,3584]{1,0:T(8,128)(2,1)S(1)}, u32[]{:S(2)}, u32[]{:S(2)}) collective-permute-start(bf16[32,3584]{1,0:T(8,128)(2,1)S(1)} %get-tuple-element.141), channel_id=1, source_target_pairs={{0,2},{1,3},{4,0},{5,1},{8,4},{9,5},{12,8},{13,9},{14,12},{15,13},... | collective-permute-start | bytes 688136 | tf_op jit(solution)/shard_map/ppermute | solution.py:315
  85.2 7.7 %collective-permute-start.26 = (bf16[32,3584]{1,0:T(8,128)(2,1)S(1)}, bf16[32,3584]{1,0:T(8,128)(2,1)S(1)}, u32[]{:S(2)}, u32[]{:S(2)}) collective-permute-start(bf16[32,3584]{1,0:T(8,128)(2,1)S(1)} %get-tuple-element.142), channel_id=1, source_target_pairs={{0,4},{1,5},{4,8},{5,9},{8,12},{9,13},{12,14},{13,15},{14,10},{15,... | collective-permute-start | bytes 688136 | tf_op jit(solution)/shard_map/ppermute | solution.py:315
  93.1 7.0 %collective-permute-start.29 = (bf16[32,3584]{1,0:T(8,128)(2,1)S(1)}, bf16[32,3584]{1,0:T(8,128)(2,1)S(1)}, u32[]{:S(2)}, u32[]{:S(2)}) collective-permute-start(bf16[32,3584]{1,0:T(8,128)(2,1)S(1)} %get-tuple-element.139), channel_id=1, source_target_pairs={{0,2},{1,3},{4,0},{5,1},{8,4},{9,5},{12,8},{13,9},{14,12},{15,13},... | collective-permute-start | bytes 688136 | tf_op jit(solution)/shard_map/ppermute | solution.py:315
  94.0 7.1 %collective-permute-start.28 = (bf16[32,3584]{1,0:T(8,128)(2,1)S(1)}, bf16[32,3584]{1,0:T(8,128)(2,1)S(1)}, u32[]{:S(2)}, u32[]{:S(2)}) collective-permute-start(bf16[32,3584]{1,0:T(8,128)(2,1)S(1)} %get-tuple-element.140), channel_id=1, source_target_pairs={{0,4},{1,5},{4,8},{5,9},{8,12},{9,13},{12,14},{13,15},{14,10},{15,... | collective-permute-start | bytes 688136 | tf_op jit(solution)/shard_map/ppermute | solution.py:315
  101.3 6.3 %collective-permute-start.31 = (bf16[32,3584]{1,0:T(8,128)(2,1)S(1)}, bf16[32,3584]{1,0:T(8,128)(2,1)S(1)}, u32[]{:S(2)}, u32[]{:S(2)}) collective-permute-start(bf16[32,3584]{1,0:T(8,128)(2,1)S(1)} %get-tuple-element.137), channel_id=1, source_target_pairs={{0,2},{1,3},{4,0},{5,1},{8,4},{9,5},{12,8},{13,9},{14,12},{15,13},... | collective-permute-start | bytes 688136 | tf_op jit(solution)/shard_map/ppermute | solution.py:315
  103.1 6.0 %collective-permute-start.30 = (bf16[32,3584]{1,0:T(8,128)(2,1)S(1)}, bf16[32,3584]{1,0:T(8,128)(2,1)S(1)}, u32[]{:S(2)}, u32[]{:S(2)}) collective-permute-start(bf16[32,3584]{1,0:T(8,128)(2,1)S(1)} %get-tuple-element.138), channel_id=1, source_target_pairs={{0,4},{1,5},{4,8},{5,9},{8,12},{9,13},{12,14},{13,15},{14,10},{15,... | collective-permute-start | bytes 688136 | tf_op jit(solution)/shard_map/ppermute | solution.py:315

commit v9 on v8

--- a/solution.py
+++ b/solution.py
@@ -69,16 +69,16 @@
     return max(t for t in range(LANES, min(size, most) + 1, LANES) if size % t == 0)
 
 
-def norm_kernel(first, blocks, rows, latent, width, with_hidden, *refs):
+def norm_kernel(far, blocks, rows, latent, width, *refs):
     scalars = refs[0]
     pooled = refs[1:5]
     resid = refs[5 : 5 + blocks]
-    w_out, gain, w_router, x, scale, weight = refs[5 + blocks : 11 + blocks]
-    hidden = refs[11 + blocks] if with_hidden else None
-    raw, joined, ssq, logits = refs[-4:]
+    w_out, gain, w_router, x_far, x_near = refs[5 + blocks : 10 + blocks]
+    scale, weight, hidden, raw, joined, ssq, logits = refs[10 + blocks :]
     step = pl.program_id(0)
     cols = w_out.shape[1]
     total = blocks * rows
+    far_rows = far * rows
     experts_all = w_router.shape[0]
     chunk = min(512, total)
 
@@ -89,7 +89,7 @@
             raw[start : start + piece.shape[0], :] = piece[...]
             start += piece.shape[0]
         for b in range(blocks):
-            place = pl.ds(pl.multiple_of(scalars[first + b] * rows, rows), rows)
+            place = pl.ds(pl.multiple_of(scalars[1 + b] * rows, rows), rows)
             joined[b * rows : (b + 1) * rows, :] = raw[place, :]
         ssq[...] = jnp.zeros_like(ssq)
         logits[...] = jnp.zeros_like(logits)
@@ -101,17 +101,23 @@
         for b in range(c // rows, end // rows):
             at = slice(b * rows, (b + 1) * rows)
             h = proj[b * rows - c : (b + 1) * rows - c] + resid[b][...].astype(jnp.float32)
-            if with_hidden and b == 0:
+            if b == far:
                 hidden[...] = h
-            x[at, :] = (h * g).astype(jnp.bfloat16)
+            scaled = (h * g).astype(jnp.bfloat16)
+            if b < far:
+                x_far[at, :] = scaled
+            else:
+                x_near[(b - far) * rows : (b - far + 1) * rows, :] = scaled
             sq = h * h
             part = sq[:, :LANES]
             for k in range(1, cols // LANES):
                 part = part + sq[:, k * LANES : (k + 1) * LANES]
             ssq[at, :] += part
-    logits[...] += lax.dot_general(
-        x[...], w_router[...], (((1,), (1,)), ((), ())), preferred_element_type=jnp.float32
-    )
+    nt = (((1,), (1,)), ((), ()))
+    for x, at in ((x_far, slice(0, far_rows)), (x_near, slice(far_rows, total))):
+        logits[at, :] += lax.dot_general(
+            x[...], w_router[...], nt, preferred_element_type=jnp.float32
+        )
 
     @pl.when(step == pl.num_programs(0) - 1)
     def _():
@@ -126,7 +132,7 @@
         weight[...] = jnp.broadcast_to(gate, weight.shape)
 
 
-def normalize(first, with_hidden, scalars, pooled, w_out, gain, w_router_t, resid_blocks):
+def normalize(far, scalars, pooled, resid_blocks, w_out, gain, w_router_t):
     blocks = len(resid_blocks)
     rows, width = resid_blocks[0].shape
     latent = w_out.shape[0]
@@ -141,25 +147,25 @@
     def tiles(height):
         return pl.BlockSpec((height, cols), lambda i: (0, i))
 
-    gathered = sum(a.shape[0] for a in pooled)
-    need = total * (cols * 16 + packed * 2 + 8 * LANES * 4) + gathered * packed * 4 + 4 * latent * cols
+    need = total * (cols * 16 + packed * 6 + 8 * LANES * 4) + 4 * latent * cols
     return pl.pallas_call(
-        lambda *refs: norm_kernel(first, blocks, rows, latent, width, with_hidden, *refs),
+        lambda *refs: norm_kernel(far, blocks, rows, latent, width, *refs),
         grid=(width // cols,),
         in_specs=[pl.BlockSpec(memory_space=pltpu.SMEM)]
         + [whole(a.shape) for a in pooled]
         + [tiles(rows)] * blocks
         + [tiles(latent), tiles(1), tiles(experts_all)],
         out_shape=[
-            jax.ShapeDtypeStruct((total, width), jnp.bfloat16),
+            jax.ShapeDtypeStruct((far * rows, width), jnp.bfloat16),
+            jax.ShapeDtypeStruct((total - far * rows, width), jnp.bfloat16),
             jax.ShapeDtypeStruct((total, LANES), jnp.float32),
             jax.ShapeDtypeStruct((total, LANES), jnp.float32),
-        ]
-        + [jax.ShapeDtypeStruct((rows, width), jnp.float32)] * with_hidden,
-        out_specs=[tiles(total), whole((total, LANES)), whole((total, LANES))]
-        + [tiles(rows)] * with_hidden,
+            jax.ShapeDtypeStruct((rows, width), jnp.float32),
+        ],
+        out_specs=[tiles(far * rows), tiles(total - far * rows)]
+        + [whole((total, LANES)), whole((total, LANES)), tiles(rows)],
         scratch_shapes=[
-            pltpu.VMEM((gathered, packed), jnp.bfloat16),
+            pltpu.VMEM((total, packed), jnp.bfloat16),
             pltpu.VMEM((total, packed), jnp.bfloat16),
             pltpu.VMEM((total, LANES), jnp.float32),
             pltpu.VMEM((total, experts_all), jnp.float32),
@@ -183,13 +189,16 @@
         out[j : j + 1, :] = jnp.full((1, LANES), length, jnp.int32)
 
 
+LONG = dict(flops=10**10, bytes_accessed=10**8, transcendentals=0)
+
+
 def lengths_of(owner, lengths, device_index, rows):
     scalar = pl.BlockSpec(memory_space=pltpu.SMEM)
     return pl.pallas_call(
         lengths_kernel,
         in_specs=[scalar] * 3,
         out_shape=jax.ShapeDtypeStruct((rows, LANES), jnp.int32),
-        cost_estimate=pl.CostEstimate(flops=10**10, bytes_accessed=10**8, transcendentals=0),
+        cost_estimate=pl.CostEstimate(**LONG),
         name="lengths",
     )(owner, lengths, device_index[None])
 
@@ -258,7 +267,6 @@
     def whole(a):
         return pl.BlockSpec(a.shape, lambda i: (0, 0), pipeline_mode=pl.Buffered(1))
 
-    heads = q_abs.shape[2] // kv_width
     return pl.pallas_call(
         lambda *refs: attention_kernel(context, latent, *refs),
         grid=(steps,),
@@ -274,11 +282,7 @@
         compiler_params=pltpu.CompilerParams(
             dimension_semantics=("arbitrary",), vmem_limit_bytes=(10 << 20) + 10240 * keys
         ),
-        cost_estimate=pl.CostEstimate(
-            flops=2 * steps * rows * heads * wide * keys,
-            bytes_accessed=2 * q_abs.size,
-            transcendentals=steps * rows * heads * keys,
-        ),
+        cost_estimate=pl.CostEstimate(**LONG),
         name="attention",
     )(q_abs, cache, fresh, lengths, routes)
 
@@ -314,10 +318,11 @@
     def send(a, perm):
         return lax.ppermute(a, "expert", perm)
 
-    to_right, to_left = shift_perm(chips, 1), shift_perm(chips, -1)
-
-    def around(to_the_right, to_the_left):
-        return send(to_the_right, to_right), send(to_the_left, to_left)
+    shifts = [(shift_perm(chips, by), shift_perm(chips, -by)) for by in (1, 2)]
+
+    def around(to_the_right, to_the_left, by=1):
+        right, left = shifts[by - 1]
+        return send(to_the_right, right), send(to_the_left, left)
 
     positions, kv_width = latent_cache.shape[1:]
     wanted = (owner[:, None] == jnp.arange(owner.shape[0], dtype=jnp.int32)).astype(jnp.bfloat16)
@@ -330,10 +335,14 @@
     mine = resid.reshape(rows, width)
     held, sib = {0: mine}, {}
     held[-1], held[1] = around(mine, mine)
+    held[-2], held[2] = around(mine, mine, 2)
     row_lengths = lengths_of(owner, lengths, device_index, row_count)
-    row_lengths, held[-1], held[1] = hold((row_lengths, held[-1], held[1]))
-    held[-2], held[2] = around(held[-1], held[1])
-    sib[0] = send(mine, sibling)
+    row_lengths, held = hold((row_lengths, held))
+    for t in range(3, half):
+        held[-t], held[t] = around(held[1 - t], held[t - 1])
+    last = around(held[2 - half][:cut], held[half - 2][cut:], 2)
+    for d in (0, -1, 1, -2, 2):
+        sib[d] = send(held[d], sibling)
     gain = norm_gain[None, :]
     scalars = jnp.array(
         [
@@ -343,12 +352,6 @@
         ],
         jnp.int32,
     )[device_index]
-    owned, row_lengths, gain, scalars, held[-2], held[2], sib[0] = hold(
-        (owned, row_lengths, gain, scalars, held[-2], held[2], sib[0])
-    )
-    for t in range(3, half):
-        held[-t], held[t] = around(held[1 - t], held[t - 1])
-    sib[-1], sib[1] = send(held[-1], sibling), send(held[1], sibling)
     packet = attention(
         q_abs,
         owned.reshape(-1, kv_width),
@@ -358,34 +361,39 @@
         devices * positions,
         w_out.shape[0],
     )
-    packet, held, sib = hold((packet, held, sib))
+    packet, gain, scalars, held, last, sib = hold((packet, gain, scalars, held, last, sib))
 
     high, low = gather_steps(chips)
     along = [send(packet, step_perm(chips, i, 0)) for i in range(1, high)]
-    last = around(held[1 - half][:cut], held[half - 1][cut:])
-    for t in range(2, half - 1):
-        sib[-t], sib[t] = send(held[-t], sibling), send(held[t], sibling)
-    along, last, sib = hold((along, last, sib))
+    along = hold(along)
     along = jnp.concatenate([packet] + along, axis=0)
     across = [send(along, step_perm(chips, 0, i)) for i in range(1, low)]
     held[half] = jnp.concatenate(last, axis=0)
-    for d in (1 - half, half - 1, half):
-        sib[d] = send(held[d], sibling)
+    for d in held:
+        if d not in sib:
+            sib[d] = send(held[d], sibling)
     across, sib = hold((across, sib))
     across = across[0] if low == 2 else jnp.concatenate(across, axis=0)
     gathered = [along, across, send(along, sibling), send(across, sibling)]
 
     f32 = jnp.float32
 
-    def normed(first, dists, with_hidden, gathered):
-        blocks = [a[d] for a in (held, sib) for d in dists]
-        return normalize(first, with_hidden, scalars, gathered, w_out, gain, w_router.T, blocks)
+    x_far, x_near, scale, weight, hidden = normalize(
+        2 * len(far),
+        scalars,
+        gathered,
+        [a[d] for part in (far, near) for a in (held, sib) for d in part],
+        w_out,
+        gain,
+        w_router.T,
+    )
+    far_rows = x_far.shape[0]
 
     def product(a, w):
         return jnp.dot(a, w[0], preferred_element_type=f32)
 
-    def activate(a, b, scale, weight):
-        r, g = scale[:, :1], weight[:, :1]
+    def activate(a, b, at):
+        r, g = scale[at, :1], weight[at, :1]
         return (jax.nn.silu(a * r) * (b * r) * g).astype(jnp.bfloat16)
 
     sums = {}
@@ -398,25 +406,22 @@
             at = slice(i * rows, (i + 1) * rows)
             sums[d] = y[at].astype(f32) + received[at].astype(f32)
 
-    def both(right, left):
-        return around(right.astype(jnp.bfloat16), left.astype(jnp.bfloat16))
-
-    x, scale, weight = normed(1, far, False, gathered)
-    act = hold(activate(product(x, w_gate), product(x, w_up), scale, weight))
+    def both(right, left, by=1):
+        return around(right.astype(jnp.bfloat16), left.astype(jnp.bfloat16), by)
+
+    act = hold(activate(product(x_far, w_gate), product(x_far, w_up), slice(0, far_rows)))
     y, received = swap(far, product(act, w_down).astype(jnp.bfloat16))
-    y, gathered = hold((y, gathered))
-    x, scale, weight, hidden = normed(1 + 2 * len(far), near, True, gathered)
-    x, y, received = hold((x, y, received))
+    gated, y, received = hold((product(x_near, w_gate), y, received))
     add_up(far, y, received)
-    right, left = both(sums[half][:cut], sums[half][cut:])
-    act = activate(product(x, w_gate), product(x, w_up), scale, weight)
-    act, right, left = hold((act, right, left))
-    right = jnp.concatenate([right.astype(f32), jnp.zeros((rows - cut, width), f32)], axis=0)
-    left = jnp.concatenate([jnp.zeros((cut, width), f32), left.astype(f32)], axis=0)
-    right, left = both(sums[half - 1] + right, sums[1 - half] + left)
-    y, received = swap(near, product(act, w_down).astype(jnp.bfloat16))
-    y, received, right, left = hold((y, received, right, left))
+    right, left = both(sums[half - 1], sums[1 - half])
+    right2, left2 = both(sums[half][:cut], sums[half][cut:], 2)
+    act = activate(gated, product(x_near, w_up), slice(far_rows, None))
+    y = product(act, w_down).astype(jnp.bfloat16)
+    y, right, left, right2, left2 = hold((y, right, left, right2, left2))
+    y, received = swap(near, y)
     add_up(near, y, received)
+    right = right.astype(f32) + jnp.pad(right2.astype(f32), ((0, rows - cut), (0, 0)))
+    left = left.astype(f32) + jnp.pad(left2.astype(f32), ((cut, 0), (0, 0)))
     for t in range(half - 2, 0, -1):
         right, left = hold(both(sums[t] + right.astype(f32), sums[-t] + left.astype(f32)))
     mixed = hidden + sums[0] + right.astype(f32) + left.astype(f32)

time: 110 us -> 120 us (1.091)
  matrix products: 17 us -> 25.2 us
  waiting for transfers between devices: 40.2 us -> 34 us
  local copies, waits for them, and re-layouts: 4.94 us -> 9.44 us
  starting transfers between devices: 32.3 us -> 36.1 us
  Pallas kernels: 13.8 us -> 11.5 us
  other arithmetic: 1.36 us -> 3.08 us
    dot_general x6 -> x5, matrix products: 16 us -> 24.2 us  [product(): return jnp.dot(a, w[0], preferred_element_type=f32)]
    ppermute x32, waiting for transfers between devices: 40.2 us -> 34 us  [send(): return lax.ppermute(a, 'expert', perm)]
    ppermute x32, starting transfers between devices: 26 us -> 29.9 us  [send(): return lax.ppermute(a, 'expert', perm)]
    pallas_call x2 -> x1, Pallas kernels: 8.71 us -> 6.43 us  [normalize(): pl.pallas_call(lambda *refs: norm_kernel(far, blocks, rows, latent, width...]
    unnamed x34 -> x40, local copies, waits for them, and re-layouts: 2.64 us -> 4.27 us
    slice x2, local copies, waits for them, and re-layouts: 0.12 us -> 1.53 us  [swap(): return (y, send(y[len(dists) * rows:], sibling))]
  transfers between devices with their start and end apart: 33 -> 33, of which waited for: 14 -> 12; matrix products, arithmetic and copies ran while one was open for 8% -> 17% of each run, Pallas kernels for 9% -> 4%
where the time goes in v9:
time: 120 us
  starting transfers between devices  36.1 us (30%)
  waiting for transfers between devices  34 us (28%)
  matrix products  25.2 us (21%)
  Pallas kernels  11.5 us (10%)
  local copies, waits for them, and re-layouts  9.44 us (8%)
  other arithmetic  3.08 us (3%)
    ppermute x32, waiting for transfers between devices, send(): return lax.ppermute(a, 'expert', perm)  34 us
    ppermute x32, starting transfers between devices, send(): return lax.ppermute(a, 'expert', perm)  29.9 us
    dot_general x5, matrix products, product(): return jnp.dot(a, w[0], preferred_element_type=f32)  24.2 us
    pallas_call x1, Pallas kernels, normalize(): pl.pallas_call(lambda *refs: norm_kernel(far, blocks, rows, latent, width...  6.43 us
    all_to_all x1, starting transfers between devices, local(): lax.all_to_all(ordered, 'expert', split_axis=0, concat_axis=0, tiled=True)  6.21 us
    unnamed x40, local copies, waits for them, and re-layouts  4.27 us
    pallas_call x1, Pallas kernels, attention(): pl.pallas_call(lambda *refs: attention_kernel(context, latent, *refs), gr...  3.67 us
  transfers between devices with their start and end apart: 33, of which 12 were waited for; matrix products, arithmetic and copies ran while one was open for 17% of the time, Pallas kernels for 4%

profile of v9, /device:TPU:0, one launch (start us, length us, event | category | flops | bytes accessed | tf_op | source)
XLA Modules:
  0.0 119.7 jit_solution(2335480463796676759)
XLA Ops:
  0.0 4.0 %collective-permute-start.3 = (bf16[32,3584]{1,0:T(8,128)(2,1)}, bf16[32,3584]{1,0:T(8,128)(2,1)S(1)}, u32[]{:S(2)}, u32[]{:S(2)}) collective-permute-start(bf16[32,3584]{1,0:T(8,128)(2,1)} %bitcast.56), channel_id=1, source_target_pairs={{0,6},{1,7},{4,2},{5,3},{8,0},{9,1},{12,4},{13,5},{14,8},{15,9},{1... | collective-permute-start | bytes 688136 | tf_op jit(solution)/shard_map/ppermute | solution.py:319
  4.0 1.6 %collective-permute-start.2 = (bf16[32,3584]{1,0:T(8,128)(2,1)}, bf16[32,3584]{1,0:T(8,128)(2,1)S(1)}, u32[]{:S(2)}, u32[]{:S(2)}) collective-permute-start(bf16[32,3584]{1,0:T(8,128)(2,1)} %bitcast.57), channel_id=1, source_target_pairs={{0,2},{1,3},{4,0},{5,1},{8,4},{9,5},{12,8},{13,9},{14,12},{15,13},... | collective-permute-start | bytes 688136 | tf_op jit(solution)/shard_map/ppermute | solution.py:319
  6.1 1.0 fusion.27
  7.3 0.7 copy.19
  8.1 6.2 %all-to-all-start = ((bf16[16,2,8,576]{3,2,1,0:T(8,128)(2,1)}), bf16[16,2,8,576]{3,2,1,0:T(8,128)(2,1)S(1)}, u32[]{:S(2)}, u32[]{:S(2)}) async-start(bf16[16,2,8,576]{3,2,1,0:T(8,128)(2,1)} %copy.19), calls=%async_computation | async-start | bytes 655360 | tf_op jit(solution)/shard_map/all_to_all | solution.py:333
  14.3 1.4 %lengths.2.refs_3_ = s32[8,128]{1,0:T(8,128)} custom-call(s32[128]{0:T(128)} %owner.1, s32[128]{0:T(128)} %lengths.3, s32[1]{0:T(128)} %bitcast.6.device), custom_call_target="tpu_custom_call" | custom-call | flops 10000000000 | bytes 100000000 | tf_op jit(solution)/shard_map/lengths/pallas_call | solution.py:197
  15.7 5.0 %collective-permute-done.2.refs_12_ = bf16[32,3584]{1,0:T(8,128)(2,1)S(1)} collective-permute-done((bf16[32,3584]{1,0:T(8,128)(2,1)}, bf16[32,3584]{1,0:T(8,128)(2,1)S(1)}, u32[]{:S(2)}, u32[]{:S(2)}) %collective-permute-start.2) | collective-permute-done | bytes 229408 | tf_op jit(solution)/shard_map/ppermute | solution.py:319
  20.7 3.4 %collective-permute-done.refs_15_ = bf16[32,3584]{1,0:T(8,128)(2,1)S(1)} collective-permute-done((bf16[32,3584]{1,0:T(8,128)(2,1)}, bf16[32,3584]{1,0:T(8,128)(2,1)S(1)}, u32[]{:S(2)}, u32[]{:S(2)}) %collective-permute-start) | collective-permute-done | bytes 229408 | tf_op jit(solution)/shard_map/ppermute | solution.py:319
  24.7 3.0 %collective-permute-start.6 = (bf16[16,3584]{1,0:T(8,128)(2,1)S(1)}, bf16[16,3584]{1,0:T(8,128)(2,1)}, u32[]{:S(2)}, u32[]{:S(2)}) collective-permute-start(bf16[16,3584]{1,0:T(8,128)(2,1)S(1)} %slice.80), channel_id=1, source_target_pairs={{0,8},{1,9},{4,12},{5,13},{8,14},{9,15},{12,10},{13,11},{14,6},{15... | collective-permute-start | bytes 344072 | tf_op jit(solution)/shard_map/ppermute | solution.py:319
  27.6 0.7 dynamic-slice_bitcast_fusion.refs_0_
  28.3 3.9 %collective-permute-done.7 = bf16[16,3584]{1,0:T(8,128)(2,1)} collective-permute-done((bf16[16,3584]{1,0:T(8,128)(2,1)S(1)}, bf16[16,3584]{1,0:T(8,128)(2,1)}, u32[]{:S(2)}, u32[]{:S(2)}) %collective-permute-start.7) | collective-permute-done | bytes 114720 | tf_op jit(solution)/shard_map/ppermute | solution.py:319
  32.2 1.8 %collective-permute-start.4 = (bf16[32,3584]{1,0:T(8,128)(2,1)S(1)}, bf16[32,3584]{1,0:T(8,128)(2,1)S(1)}, u32[]{:S(2)}, u32[]{:S(2)}) collective-permute-start(bf16[32,3584]{1,0:T(8,128)(2,1)S(1)} %collective-permute-done.refs_15_), channel_id=1, source_target_pairs={{0,4},{1,5},{4,8},{5,9},{8,12},{9,13},{12,14},{13,15},{14,10},{15,... | collective-permute-start | bytes 688136 | tf_op jit(solution)/shard_map/ppermute | solution.py:319
  34.1 2.1 %collective-permute-start.5 = (bf16[32,3584]{1,0:T(8,128)(2,1)S(1)}, bf16[32,3584]{1,0:T(8,128)(2,1)S(1)}, u32[]{:S(2)}, u32[]{:S(2)}) collective-permute-start(bf16[32,3584]{1,0:T(8,128)(2,1)S(1)} %collective-permute-done.3.refs_14_), channel_id=1, source_target_pairs={{0,2},{1,3},{4,0},{5,1},{8,4},{9,5},{12,8},{13,9},{14,12},{15,13},... | collective-permute-start | bytes 688136 | tf_op jit(solution)/shard_map/ppermute | solution.py:319
  36.3 1.7 %copy-done.4 = bf16[4,8,36864]{2,1,0:T(8,128)(2,1)S(1)} copy-done((bf16[4,8,36864]{2,1,0:T(8,128)(2,1)S(1)}, bf16[4,8,36864]{2,1,0:T(8,128)(2,1)}, u32[]{:S(2)}) %copy-start.4) | copy-done | bytes 2359320
  38.7 3.7 %attention.1 = bf16[32,640]{1,0:T(8,128)(2,1)S(1)} custom-call(bf16[4,8,36864]{2,1,0:T(8,128)(2,1)S(1)} %copy-done.4, bf16[256,576]{1,0:T(8,128)(2,1)S(1)} %bitcast.55, bf16[32,576]{1,0:T(8,128)(2,1)S(1)} %bitcast.63, s32[8,128]{1,0:T(8,128)S(1)} %copy-done.9, s32[32,8]{1,0:T(8,128)S(1)} %bitcast.64), custom_call_target="tpu_custom_call" | custom-call | flops 10000000000 | bytes 100000000 | tf_op jit(solution)/shard_map/attention/pallas_call | solution.py:270
  42.4 0.7 collective-permute-done.5.refs_6_
  43.1 1.7 %collective-permute-start.15 = (bf16[32,640]{1,0:T(8,128)(2,1)S(1)}, bf16[32,640]{1,0:T(8,128)(2,1)S(1)}, u32[]{:S(2)}, u32[]{:S(2)}) collective-permute-start(bf16[32,640]{1,0:T(8,128)(2,1)S(1)} %attention.1), channel_id=1, source_target_pairs={{0,4},{1,5},{2,6},{3,7},{4,8},{5,9},{6,10},{7,11},{8,12},{9,13},{1... | collective-permute-start | bytes 122888 | tf_op jit(solution)/shard_map/ppermute | solution.py:319
  45.5 2.1 %collective-permute-start.13 = (bf16[32,640]{1,0:T(8,128)(2,1)S(1)}, bf16[32,640]{1,0:T(8,128)(2,1)S(1)}, u32[]{:S(2)}, u32[]{:S(2)}) collective-permute-start(bf16[32,640]{1,0:T(8,128)(2,1)S(1)} %attention.1), channel_id=1, source_target_pairs={{0,12},{1,13},{2,14},{3,15},{4,0},{5,1},{6,2},{7,3},{8,4},{9,5},{1... | collective-permute-start | bytes 122888 | tf_op jit(solution)/shard_map/ppermute | solution.py:319
  47.6 0.9 constant_dynamic-update-slice_fusion.5
  48.5 0.9 constant_dynamic-update-slice_fusion.4.refs_5_
  50.5 1.5 %collective-permute-start.16 = (bf16[128,640]{1,0:T(8,128)(2,1)S(1)}, bf16[128,640]{1,0:T(8,128)(2,1)S(1)}, u32[]{:S(2)}, u32[]{:S(2)}) collective-permute-start(bf16[128,640]{1,0:T(8,128)(2,1)S(1)} %constant_dynamic-update-slice_fusion.refs_1_), channel_id=1, source_target_pairs={{0,2},{1,3},{2,0},{3,1},{4,6},{5,7},{6,4},{7,5},{8,10},{9,11},{10,... | collective-permute-start | bytes 491528 | tf_op jit(solution)/shard_map/ppermute | solution.py:319
  52.1 4.6 %collective-permute-done.16.refs_2_ = bf16[128,640]{1,0:T(8,128)(2,1)S(1)} collective-permute-done((bf16[128,640]{1,0:T(8,128)(2,1)S(1)}, bf16[128,640]{1,0:T(8,128)(2,1)S(1)}, u32[]{:S(2)}, u32[]{:S(2)}) %collective-permute-start.16) | collective-permute-done | bytes 163872 | tf_op jit(solution)/shard_map/ppermute | solution.py:319
  56.8 1.4 %collective-permute-done.21.refs_4_ = bf16[128,640]{1,0:T(8,128)(2,1)S(1)} collective-permute-done((bf16[128,640]{1,0:T(8,128)(2,1)S(1)}, bf16[128,640]{1,0:T(8,128)(2,1)S(1)}, u32[]{:S(2)}, u32[]{:S(2)}) %collective-permute-start.21) | collective-permute-done | bytes 163872 | tf_op jit(solution)/shard_map/ppermute | solution.py:319
  58.2 6.4 %normalize.1 = (bf16[192,3584]{1,0:T(8,128)(2,1)S(1)}, bf16[320,3584]{1,0:T(8,128)(2,1)S(1)}, f32[512,128]{1,0:T(8,128)S(1)}, f32[512,128]{1,0:T(8,128)S(1)}, f32[32,3584]{1,0:T(8,128)S(1)}) custom-call(s32[17]{0:T(128)S(1)} %dynamic-slice_bitcast_fusion.refs_0_, bf16[128,640]{1,0:T(8,128)(2,1)S(1)} %constant_dynamic-update-slice_fusion.refs_1_, ...), custom_call_target="tpu_custom_call" | custom-call | flops 1879048192 | bytes 11010048 | tf_op jit(solution)/shard_map/normalize/pallas_call | solution.py:151
  65.0 5.3 %fusion.21 = f32[192,1024]{1,0:T(8,128)S(1)} fusion(bf16[192,3584]{1,0:T(8,128)(2,1)S(1)} %get-tuple-element.94, bf16[1,3584,1024]{2,1,0:T(8,128)(2,1)} %param.24, f32[192]{0:T(256)S(1)} %get-tuple-element.121), kind=kOutput, calls=%fused_computation.16 | convolution fusion | flops 1409482752 | bytes 9503488 | tf_op jit(solution)/shard_map/dot_general | solution.py:393
  70.4 1.7 %multiply_convert_fusion.1 = bf16[192,1024]{1,0:T(8,128)(2,1)S(1)} fusion(f32[192,1024]{1,0:T(8,128)S(1)} %fusion.21, f32[192]{0:T(256)S(1)} %get-tuple-element.120, f32[192]{0:T(256)S(1)} %get-tuple-element.121, bf16[192,3584]{1,0:T(8,128)(2,1)S(1)} %get-tuple-element.94, bf16[1,3584,1024]{2,1,0:T(8,128)(2,1)S(1)} %bitcast.69), kind=kOutput, calls=%fused_computation.20 | convolution fusion | flops 1410859008 | bytes 9897472 | tf_op jit(solution)/shard_map/dot_general | solution.py:393
  72.1 0.9 slice-done.5
  73.0 1.7 %fusion.15 = bf16[192,3584]{1,0:T(8,128)(2,1)S(1)} fusion(bf16[192,1024]{1,0:T(8,128)(2,1)S(1)} %multiply_convert_fusion.1, bf16[1,1024,3584]{2,1,0:T(8,128)(2,1)S(1)} %bitcast.71), kind=kOutput, calls=%fused_computation.13 | convolution fusion | flops 1409974272 | bytes 9109504 | tf_op jit(solution)/shard_map/dot_general | solution.py:393
  74.9 3.6 %fusion.10 = f32[320,1024]{1,0:T(8,128)} fusion(bf16[320,3584]{1,0:T(8,128)(2,1)S(1)} %get-tuple-element.93, bf16[1,3584,1024]{2,1,0:T(8,128)(2,1)S(1)} %bitcast.67), kind=kOutput, calls=%fused_computation.10 | convolution fusion | flops 2348810240 | bytes 10944512 | tf_op jit(solution)/shard_map/dot_general | solution.py:393
  78.5 0.8 add_convert_fusion.5
  79.4 0.7 fusion.42
  80.1 1.8 %collective-permute-start.26 = (bf16[16,3584]{1,0:T(8,128)(2,1)}, bf16[16,3584]{1,0:T(8,128)(2,1)}, u32[]{:S(2)}, u32[]{:S(2)}) collective-permute-start(bf16[16,3584]{1,0:T(8,128)(2,1)} %get-tuple-element.116), channel_id=1, source_target_pairs={{0,6},{1,7},{4,2},{5,3},{8,0},{9,1},{12,4},{13,5},{14,8},{15,9},{1... | collective-permute-start | bytes 344072 | tf_op jit(solution)/shard_map/ppermute | solution.py:319
  81.9 1.1 collective-permute-start.25
  83.0 1.1 collective-permute-start.24
  84.2 0.9 collective-permute-start.23
  85.0 12.0 %fusion.12 = bf16[320,3584]{1,0:T(8,128)(2,1)} fusion(bf16[1,1024,3584]{2,1,0:T(8,128)(2,1)} %param.26, f32[320,1024]{1,0:T(8,128)} %fusion.10, bf16[320,3584]{1,0:T(8,128)(2,1)S(1)} %copy-done.6, bf16[1,3584,1024]{2,1,0:T(8,128)(2,1)} %param.25, f32[320]{0:T(512)S(1)} %get-tuple-element.118, f32[320]{0:T(512)S(1)} %get-tuple-element.119), kind=kOutput, calls=%fused_computation.12 | convolution fusion | flops 4701716480 | bytes 20580864 | tf_op jit(solution)/shard_map/dot_general | solution.py:393
  97.0 1.5 %slice.96 = bf16[160,3584]{1,0:T(8,128)(2,1)S(1)} slice(bf16[320,3584]{1,0:T(8,128)(2,1)} %fusion.12), slice={[160:320], [0:3584]} | slice | bytes 2293760 | tf_op jit(solution)/shard_map/slice | solution.py:402
  98.6 2.8 %collective-permute-done.27 = bf16[160,3584]{1,0:T(8,128)(2,1)S(1)} collective-permute-done((bf16[160,3584]{1,0:T(8,128)(2,1)S(1)}, bf16[160,3584]{1,0:T(8,128)(2,1)S(1)}, u32[]{:S(2)}, u32[]{:S(2)}) %collective-permute-start.27) | collective-permute-done | bytes 1146912 | tf_op jit(solution)/shard_map/ppermute | solution.py:319
  101.4 1.2 %add_convert_fusion.3 = (bf16[32,3584]{1,0:T(8,128)(2,1)S(1)}, bf16[32,3584]{1,0:T(8,128)(2,1)S(1)}) fusion(bf16[32,3584]{1,0:T(8,128)(2,1)S(1)} %collective-permute-done.24, bf16[160,3584]{1,0:T(8,128)(2,1)S(1)} %collective-permute-done.27, bf16[16,3584]{1,0:T(8,128)(2,1)} %collective-permute-done.26, bf16[320,3584]{1,0:T(8,128)(2,1)S(1)} %copy-done.10, ...), kind=kLoop, calls=%fused_computation.27 | loop fusion | flops 1835008 | bytes 2064384 | tf_op jit(solution)/shard_map/convert_element_type | solution.py:410
  102.6 1.2 collective-permute-start.29
  103.8 0.9 collective-permute-start.28
  104.7 5.6 %collective-permute-done.29 = bf16[32,3584]{1,0:T(8,128)(2,1)S(1)} collective-permute-done((bf16[32,3584]{1,0:T(8,128)(2,1)S(1)}, bf16[32,3584]{1,0:T(8,128)(2,1)S(1)}, u32[]{:S(2)}, u32[]{:S(2)}) %collective-permute-start.29) | collective-permute-done | bytes 229408 | tf_op jit(solution)/shard_map/ppermute | solution.py:319
  110.3 0.9 collective-permute-done.28
  111.4 1.3 %collective-permute-start.31 = (bf16[32,3584]{1,0:T(8,128)(2,1)S(1)}, bf16[32,3584]{1,0:T(8,128)(2,1)S(1)}, u32[]{:S(2)}, u32[]{:S(2)}) collective-permute-start(bf16[32,3584]{1,0:T(8,128)(2,1)S(1)} %get-tuple-element.109), channel_id=1, source_target_pairs={{0,2},{1,3},{4,0},{5,1},{8,4},{9,5},{12,8},{13,9},{14,12},{15,13},... | collective-permute-start | bytes 688136 | tf_op jit(solution)/shard_map/ppermute | solution.py:319
  112.6 0.8 collective-permute-start.30
  113.4 4.5 %collective-permute-done.31 = bf16[32,3584]{1,0:T(8,128)(2,1)S(1)} collective-permute-done((bf16[32,3584]{1,0:T(8,128)(2,1)S(1)}, bf16[32,3584]{1,0:T(8,128)(2,1)S(1)}, u32[]{:S(2)}, u32[]{:S(2)}) %collective-permute-start.31) | collective-permute-done | bytes 229408 | tf_op jit(solution)/shard_map/ppermute | solution.py:319
  117.9 0.9 collective-permute-done.30
  118.8 0.8 fusion.37
  (87 shorter events, 5.0 us)
Async XLA Ops:
  0.0 6.1 %copy-start = (bf16[128,2,576]{0,2,1:T(8,128)(2,1)S(1)}, bf16[128,2,576]{0,2,1:T(8,128)(2,1)}, u32[]{:S(2)}) copy-start(bf16[128,2,576]{0,2,1:T(8,128)(2,1)} %param.16) | copy-start | bytes 884740
  0.0 15.7 %collective-permute-start.3 = (bf16[32,3584]{1,0:T(8,128)(2,1)}, bf16[32,3584]{1,0:T(8,128)(2,1)S(1)}, u32[]{:S(2)}, u32[]{:S(2)}) collective-permute-start(bf16[32,3584]{1,0:T(8,128)(2,1)} %bitcast.56), channel_id=1, source_target_pairs={{0,6},{1,7},{4,2},{5,3},{8,0},{9,1},{12,4},{13,5},{14,8},{15,9},{1... | collective-permute-start | bytes 688136 | tf_op jit(solution)/shard_map/ppermute | solution.py:319
  4.0 16.7 %collective-permute-start.2 = (bf16[32,3584]{1,0:T(8,128)(2,1)}, bf16[32,3584]{1,0:T(8,128)(2,1)S(1)}, u32[]{:S(2)}, u32[]{:S(2)}) collective-permute-start(bf16[32,3584]{1,0:T(8,128)(2,1)} %bitcast.57), channel_id=1, source_target_pairs={{0,2},{1,3},{4,0},{5,1},{8,4},{9,5},{12,8},{13,9},{14,12},{15,13},... | collective-permute-start | bytes 688136 | tf_op jit(solution)/shard_map/ppermute | solution.py:319
  5.6 15.1 %collective-permute-start.1 = (bf16[32,3584]{1,0:T(8,128)(2,1)}, bf16[32,3584]{1,0:T(8,128)(2,1)S(1)}, u32[]{:S(2)}, u32[]{:S(2)}) collective-permute-start(bf16[32,3584]{1,0:T(8,128)(2,1)} %bitcast.58), channel_id=1, source_target_pairs={{0,4},{1,5},{4,8},{5,9},{8,12},{9,13},{12,14},{13,15},{14,10},{15,... | collective-permute-start | bytes 688136 | tf_op jit(solution)/shard_map/ppermute | solution.py:319
  6.0 18.0 %collective-permute-start = (bf16[32,3584]{1,0:T(8,128)(2,1)}, bf16[32,3584]{1,0:T(8,128)(2,1)S(1)}, u32[]{:S(2)}, u32[]{:S(2)}) collective-permute-start(bf16[32,3584]{1,0:T(8,128)(2,1)} %bitcast.59), channel_id=1, source_target_pairs={{0,8},{1,9},{4,12},{5,13},{8,14},{9,15},{12,10},{13,11},{14,6},{15... | collective-permute-start | bytes 688136 | tf_op jit(solution)/shard_map/ppermute | solution.py:319
  8.1 28.3 %all-to-all-start = ((bf16[16,2,8,576]{3,2,1,0:T(8,128)(2,1)}), bf16[16,2,8,576]{3,2,1,0:T(8,128)(2,1)S(1)}, u32[]{:S(2)}, u32[]{:S(2)}) async-start(bf16[16,2,8,576]{3,2,1,0:T(8,128)(2,1)} %copy.19), calls=%async_computation | async-start | bytes 655360 | tf_op jit(solution)/shard_map/all_to_all | solution.py:333
  14.3 9.8 %copy-start.2 = (bf16[4,8,3584]{2,1,0:T(8,128)(2,1)S(1)}, bf16[4,8,3584]{2,1,0:T(8,128)(2,1)}, u32[]{:S(2)}) copy-start(bf16[4,8,3584]{2,1,0:T(8,128)(2,1)} %param.19) | copy-start | bytes 688132
  14.3 13.3 %copy-start.11 = (bf16[3584]{0:T(1024)(128)(2,1)S(1)}, bf16[3584]{0:T(1024)(128)(2,1)}, u32[]{:S(2)}) copy-start(bf16[3584]{0:T(1024)(128)(2,1)} %param.22) | copy-start | bytes 21508
  14.3 22.0 %copy-start.7 = (bf16[4,8,576]{2,1,0:T(8,128)(2,1)S(1)}, bf16[4,8,576]{2,1,0:T(8,128)(2,1)}, u32[]{:S(2)}) copy-start(bf16[4,8,576]{2,1,0:T(8,128)(2,1)} %param.15) | copy-start | bytes 110596
  14.3 22.0 %copy-start.8 = (s32[4,8,8]{2,1,0:T(8,128)S(1)}, s32[4,8,8]{2,1,0:T(8,128)}, u32[]{:S(2)}) copy-start(s32[4,8,8]{2,1,0:T(8,128)} %param.20) | copy-start | bytes 3076
  24.1 10.0 %collective-permute-start.9 = (bf16[32,3584]{1,0:T(8,128)(2,1)S(1)}, bf16[32,3584]{1,0:T(8,128)(2,1)S(1)}, u32[]{:S(2)}, u32[]{:S(2)}) collective-permute-start(bf16[32,3584]{1,0:T(8,128)(2,1)S(1)} %collective-permute-done.1.refs_13_), channel_id=1, source_target_pairs={{0,1},{1,0},{2,3},{3,2},{4,5},{5,4},{6,7},{7,6},{8,9},{9,8},{10,11... | collective-permute-start | bytes 688136 | tf_op jit(solution)/shard_map/ppermute | solution.py:319
  24.1 12.1 %collective-permute-start.10 = (bf16[32,3584]{1,0:T(8,128)(2,1)S(1)}, bf16[32,3584]{1,0:T(8,128)(2,1)S(1)}, u32[]{:S(2)}, u32[]{:S(2)}) collective-permute-start(bf16[32,3584]{1,0:T(8,128)(2,1)S(1)} %bitcast.60), channel_id=1, source_target_pairs={{0,1},{1,0},{2,3},{3,2},{4,5},{5,4},{6,7},{7,6},{8,9},{9,8},{10,11... | collective-permute-start | bytes 688136 | tf_op jit(solution)/shard_map/ppermute | solution.py:319
  24.6 7.6 %collective-permute-start.7 = (bf16[16,3584]{1,0:T(8,128)(2,1)S(1)}, bf16[16,3584]{1,0:T(8,128)(2,1)}, u32[]{:S(2)}, u32[]{:S(2)}) collective-permute-start(bf16[16,3584]{1,0:T(8,128)(2,1)S(1)} %slice.81), channel_id=1, source_target_pairs={{0,6},{1,7},{4,2},{5,3},{8,0},{9,1},{12,4},{13,5},{14,8},{15,9},{1... | collective-permute-start | bytes 344072 | tf_op jit(solution)/shard_map/ppermute | solution.py:319
  24.7 9.4 %collective-permute-start.6 = (bf16[16,3584]{1,0:T(8,128)(2,1)S(1)}, bf16[16,3584]{1,0:T(8,128)(2,1)}, u32[]{:S(2)}, u32[]{:S(2)}) collective-permute-start(bf16[16,3584]{1,0:T(8,128)(2,1)S(1)} %slice.80), channel_id=1, source_target_pairs={{0,8},{1,9},{4,12},{5,13},{8,14},{9,15},{12,10},{13,11},{14,6},{15... | collective-permute-start | bytes 344072 | tf_op jit(solution)/shard_map/ppermute | solution.py:319
  28.3 14.0 %collective-permute-start.8 = (bf16[32,3584]{1,0:T(8,128)(2,1)S(1)}, bf16[32,3584]{1,0:T(8,128)(2,1)S(1)}, u32[]{:S(2)}, u32[]{:S(2)}) collective-permute-start(bf16[32,3584]{1,0:T(8,128)(2,1)S(1)} %collective-permute-done.refs_15_), channel_id=1, source_target_pairs={{0,1},{1,0},{2,3},{3,2},{4,5},{5,4},{6,7},{7,6},{8,9},{9,8},{10,11... | collective-permute-start | bytes 688136 | tf_op jit(solution)/shard_map/ppermute | solution.py:319
  32.2 10.2 %collective-permute-start.4 = (bf16[32,3584]{1,0:T(8,128)(2,1)S(1)}, bf16[32,3584]{1,0:T(8,128)(2,1)S(1)}, u32[]{:S(2)}, u32[]{:S(2)}) collective-permute-start(bf16[32,3584]{1,0:T(8,128)(2,1)S(1)} %collective-permute-done.refs_15_), channel_id=1, source_target_pairs={{0,4},{1,5},{4,8},{5,9},{8,12},{9,13},{12,14},{13,15},{14,10},{15,... | collective-permute-start | bytes 688136 | tf_op jit(solution)/shard_map/ppermute | solution.py:319
  34.0 8.3 %collective-permute-start.12 = (bf16[32,3584]{1,0:T(8,128)(2,1)S(1)}, bf16[32,3584]{1,0:T(8,128)(2,1)S(1)}, u32[]{:S(2)}, u32[]{:S(2)}) collective-permute-start(bf16[32,3584]{1,0:T(8,128)(2,1)S(1)} %collective-permute-done.3.refs_14_), channel_id=1, source_target_pairs={{0,1},{1,0},{2,3},{3,2},{4,5},{5,4},{6,7},{7,6},{8,9},{9,8},{10,11... | collective-permute-start | bytes 688136 | tf_op jit(solution)/shard_map/ppermute | solution.py:319
  34.1 9.0 %collective-permute-start.5 = (bf16[32,3584]{1,0:T(8,128)(2,1)S(1)}, bf16[32,3584]{1,0:T(8,128)(2,1)S(1)}, u32[]{:S(2)}, u32[]{:S(2)}) collective-permute-start(bf16[32,3584]{1,0:T(8,128)(2,1)S(1)} %collective-permute-done.3.refs_14_), channel_id=1, source_target_pairs={{0,2},{1,3},{4,0},{5,1},{8,4},{9,5},{12,8},{13,9},{14,12},{15,13},... | collective-permute-start | bytes 688136 | tf_op jit(solution)/shard_map/ppermute | solution.py:319
  36.1 6.2 %collective-permute-start.11 = (bf16[32,3584]{1,0:T(8,128)(2,1)S(1)}, bf16[32,3584]{1,0:T(8,128)(2,1)S(1)}, u32[]{:S(2)}, u32[]{:S(2)}) collective-permute-start(bf16[32,3584]{1,0:T(8,128)(2,1)S(1)} %collective-permute-done.2.refs_12_), channel_id=1, source_target_pairs={{0,1},{1,0},{2,3},{3,2},{4,5},{5,4},{6,7},{7,6},{8,9},{9,8},{10,11... | collective-permute-start | bytes 688136 | tf_op jit(solution)/shard_map/ppermute | solution.py:319
  38.7 19.5 %copy-start.1 = (bf16[512,3584]{1,0:T(8,128)(2,1)S(1)}, bf16[512,3584]{1,0:T(8,128)(2,1)}, u32[]{:S(2)}) copy-start(bf16[512,3584]{1,0:T(8,128)(2,1)} %refs_21_.1) | copy-start | bytes 11010052
  38.7 19.5 %copy-start.3 = (bf16[3584,16]{0,1:T(8,128)(2,1)S(1)}, bf16[3584,16]{0,1:T(8,128)(2,1)}, u32[]{:S(2)}) copy-start(bf16[3584,16]{0,1:T(8,128)(2,1)} %param.23) | copy-start | bytes 344068
  43.1 6.9 %collective-permute-start.15 = (bf16[32,640]{1,0:T(8,128)(2,1)S(1)}, bf16[32,640]{1,0:T(8,128)(2,1)S(1)}, u32[]{:S(2)}, u32[]{:S(2)}) collective-permute-start(bf16[32,640]{1,0:T(8,128)(2,1)S(1)} %attention.1), channel_id=1, source_target_pairs={{0,4},{1,5},{2,6},{3,7},{4,8},{5,9},{6,10},{7,11},{8,12},{9,13},{1... | collective-permute-start | bytes 122888 | tf_op jit(solution)/shard_map/ppermute | solution.py:319
  44.8 5.6 %collective-permute-start.14 = (bf16[32,640]{1,0:T(8,128)(2,1)S(1)}, bf16[32,640]{1,0:T(8,128)(2,1)S(1)}, u32[]{:S(2)}, u32[]{:S(2)}) collective-permute-start(bf16[32,640]{1,0:T(8,128)(2,1)S(1)} %attention.1), channel_id=1, source_target_pairs={{0,8},{1,9},{2,10},{3,11},{4,12},{5,13},{6,14},{7,15},{8,0},{9,1},... | collective-permute-start | bytes 122888 | tf_op jit(solution)/shard_map/ppermute | solution.py:319
  45.5 5.0 %collective-permute-start.13 = (bf16[32,640]{1,0:T(8,128)(2,1)S(1)}, bf16[32,640]{1,0:T(8,128)(2,1)S(1)}, u32[]{:S(2)}, u32[]{:S(2)}) collective-permute-start(bf16[32,640]{1,0:T(8,128)(2,1)S(1)} %attention.1), channel_id=1, source_target_pairs={{0,12},{1,13},{2,14},{3,15},{4,0},{5,1},{6,2},{7,3},{8,4},{9,5},{1... | collective-permute-start | bytes 122888 | tf_op jit(solution)/shard_map/ppermute | solution.py:319
  49.4 7.3 %collective-permute-start.19 = (bf16[32,3584]{1,0:T(8,128)(2,1)S(1)}, bf16[32,3584]{1,0:T(8,128)(2,1)S(1)}, u32[]{:S(2)}, u32[]{:S(2)}) collective-permute-start(bf16[32,3584]{1,0:T(8,128)(2,1)S(1)} %constant_dynamic-update-slice_fusion.4.refs_5_), channel_id=1, source_target_pairs={{0,1},{1,0},{2,3},{3,2},{4,5},{5,4},{6,7},{7,6},{8,9},{9,8},{10,11... | collective-permute-start | bytes 688136 | tf_op jit(solution)/shard_map/ppermute | solution.py:319
  49.5 7.2 %collective-permute-start.17 = (bf16[32,3584]{1,0:T(8,128)(2,1)S(1)}, bf16[32,3584]{1,0:T(8,128)(2,1)S(1)}, u32[]{:S(2)}, u32[]{:S(2)}) collective-permute-start(bf16[32,3584]{1,0:T(8,128)(2,1)S(1)} %collective-permute-done.4.refs_7_), channel_id=1, source_target_pairs={{0,1},{1,0},{2,3},{3,2},{4,5},{5,4},{6,7},{7,6},{8,9},{9,8},{10,11... | collective-permute-start | bytes 688136 | tf_op jit(solution)/shard_map/ppermute | solution.py:319
  50.0 6.7 %collective-permute-start.18 = (bf16[32,3584]{1,0:T(8,128)(2,1)S(1)}, bf16[32,3584]{1,0:T(8,128)(2,1)S(1)}, u32[]{:S(2)}, u32[]{:S(2)}) collective-permute-start(bf16[32,3584]{1,0:T(8,128)(2,1)S(1)} %collective-permute-done.5.refs_6_), channel_id=1, source_target_pairs={{0,1},{1,0},{2,3},{3,2},{4,5},{5,4},{6,7},{7,6},{8,9},{9,8},{10,11... | collective-permute-start | bytes 688136 | tf_op jit(solution)/shard_map/ppermute | solution.py:319
  50.5 6.2 %collective-permute-start.16 = (bf16[128,640]{1,0:T(8,128)(2,1)S(1)}, bf16[128,640]{1,0:T(8,128)(2,1)S(1)}, u32[]{:S(2)}, u32[]{:S(2)}) collective-permute-start(bf16[128,640]{1,0:T(8,128)(2,1)S(1)} %constant_dynamic-update-slice_fusion.refs_1_), channel_id=1, source_target_pairs={{0,2},{1,3},{2,0},{3,1},{4,6},{5,7},{6,4},{7,5},{8,10},{9,11},{10,... | collective-permute-start | bytes 491528 | tf_op jit(solution)/shard_map/ppermute | solution.py:319
  52.1 4.7 %collective-permute-start.20 = (bf16[128,640]{1,0:T(8,128)(2,1)S(1)}, bf16[128,640]{1,0:T(8,128)(2,1)S(1)}, u32[]{:S(2)}, u32[]{:S(2)}) collective-permute-start(bf16[128,640]{1,0:T(8,128)(2,1)S(1)} %constant_dynamic-update-slice_fusion.refs_1_), channel_id=1, source_target_pairs={{0,1},{1,0},{2,3},{3,2},{4,5},{5,4},{6,7},{7,6},{8,9},{9,8},{10,11... | collective-permute-start | bytes 491528 | tf_op jit(solution)/shard_map/ppermute | solution.py:319
  56.7 1.5 %collective-permute-start.21 = (bf16[128,640]{1,0:T(8,128)(2,1)S(1)}, bf16[128,640]{1,0:T(8,128)(2,1)S(1)}, u32[]{:S(2)}, u32[]{:S(2)}) collective-permute-start(bf16[128,640]{1,0:T(8,128)(2,1)S(1)} %collective-permute-done.16.refs_2_), channel_id=1, source_target_pairs={{0,1},{1,0},{2,3},{3,2},{4,5},{5,4},{6,7},{7,6},{8,9},{9,8},{10,11... | collective-permute-start | bytes 491528 | tf_op jit(solution)/shard_map/ppermute | solution.py:319
  58.2 12.1 %slice-start.2 = ((s8[7340032]{0:T(1024)(128)(4,1)}), s8[4194304]{0:T(1024)(128)(4,1)S(1)}, s32[]{:S(2)}) async-start(s8[7340032]{0:T(1024)(128)(4,1)} %bitcast.68), calls=%async_computation.3 | async-start | bytes 8388608
  64.6 10.3 %copy-start.5 = (bf16[320,3584]{1,0:T(8,128)(2,1)}, bf16[320,3584]{1,0:T(8,128)(2,1)S(1)}, u32[]{:S(2)}) copy-start(bf16[320,3584]{1,0:T(8,128)(2,1)S(1)} %get-tuple-element.93) | copy-start | bytes 6881284
  65.0 5.3 %slice-start.3 = ((s8[7340032]{0:T(1024)(128)(4,1)}), s8[3145728]{0:T(1024)(128)(4,1)S(1)}, s32[]{:S(2)}) async-start(s8[7340032]{0:T(1024)(128)(4,1)} %bitcast.68), calls=%async_computation.4 | async-start | bytes 6291456
  65.0 7.1 %slice-start.4 = ((s8[7340032]{0:T(1024)(128)(4,1)}), s8[4194304]{0:T(1024)(128)(4,1)S(1)}, s32[]{:S(2)}) async-start(s8[7340032]{0:T(1024)(128)(4,1)} %bitcast.70), calls=%async_computation.5 | async-start | bytes 8388608
  65.0 9.9 %slice-start = ((s8[7340032]{0:T(1024)(128)(4,1)}), s8[4194304]{0:T(1024)(128)(4,1)S(1)}, s32[]{:S(2)}) async-start(s8[7340032]{0:T(1024)(128)(4,1)} %bitcast.66), calls=%async_computation.1 | async-start | bytes 8388608
  70.3 4.6 %slice-start.1 = ((s8[7340032]{0:T(1024)(128)(4,1)}), s8[3145728]{0:T(1024)(128)(4,1)S(1)}, s32[]{:S(2)}) async-start(s8[7340032]{0:T(1024)(128)(4,1)} %bitcast.66), calls=%async_computation.2 | async-start | bytes 6291456
  74.7 3.8 %collective-permute-start.22 = (bf16[96,3584]{1,0:T(8,128)(2,1)S(1)}, bf16[96,3584]{1,0:T(8,128)(2,1)S(1)}, u32[]{:S(2)}, u32[]{:S(2)}) collective-permute-start(bf16[96,3584]{1,0:T(8,128)(2,1)S(1)} %slice.106), channel_id=1, source_target_pairs={{0,1},{1,0},{2,3},{3,2},{4,5},{5,4},{6,7},{7,6},{8,9},{9,8},{10,11... | collective-permute-start | bytes 2064392 | tf_op jit(solution)/shard_map/ppermute | solution.py:319
  78.5 6.5 %copy-start.6 = (bf16[320,3584]{1,0:T(8,128)(2,1)S(1)}, bf16[320,3584]{1,0:T(8,128)(2,1)}, u32[]{:S(2)}) copy-start(bf16[320,3584]{1,0:T(8,128)(2,1)} %copy-done.5) | copy-start | bytes 6881284
  80.1 16.9 %collective-permute-start.26 = (bf16[16,3584]{1,0:T(8,128)(2,1)}, bf16[16,3584]{1,0:T(8,128)(2,1)}, u32[]{:S(2)}, u32[]{:S(2)}) collective-permute-start(bf16[16,3584]{1,0:T(8,128)(2,1)} %get-tuple-element.116), channel_id=1, source_target_pairs={{0,6},{1,7},{4,2},{5,3},{8,0},{9,1},{12,4},{13,5},{14,8},{15,9},{1... | collective-permute-start | bytes 344072 | tf_op jit(solution)/shard_map/ppermute | solution.py:319
  81.9 15.1 %collective-permute-start.25 = (bf16[16,3584]{1,0:T(8,128)(2,1)}, bf16[16,3584]{1,0:T(8,128)(2,1)}, u32[]{:S(2)}, u32[]{:S(2)}) collective-permute-start(bf16[16,3584]{1,0:T(8,128)(2,1)} %get-tuple-element.117), channel_id=1, source_target_pairs={{0,8},{1,9},{4,12},{5,13},{8,14},{9,15},{12,10},{13,11},{14,6},{15... | collective-permute-start | bytes 344072 | tf_op jit(solution)/shard_map/ppermute | solution.py:319
  83.0 14.0 %collective-permute-start.24 = (bf16[32,3584]{1,0:T(8,128)(2,1)}, bf16[32,3584]{1,0:T(8,128)(2,1)S(1)}, u32[]{:S(2)}, u32[]{:S(2)}) collective-permute-start(bf16[32,3584]{1,0:T(8,128)(2,1)} %get-tuple-element.114), channel_id=1, source_target_pairs={{0,2},{1,3},{4,0},{5,1},{8,4},{9,5},{12,8},{13,9},{14,12},{15,13},... | collective-permute-start | bytes 688136 | tf_op jit(solution)/shard_map/ppermute | solution.py:319
  84.2 12.9 %collective-permute-start.23 = (bf16[32,3584]{1,0:T(8,128)(2,1)S(1)}, bf16[32,3584]{1,0:T(8,128)(2,1)}, u32[]{:S(2)}, u32[]{:S(2)}) collective-permute-start(bf16[32,3584]{1,0:T(8,128)(2,1)S(1)} %get-tuple-element.115), channel_id=1, source_target_pairs={{0,4},{1,5},{4,8},{5,9},{8,12},{9,13},{12,14},{13,15},{14,10},{15,... | collective-permute-start | bytes 688136 | tf_op jit(solution)/shard_map/ppermute | solution.py:319
  97.0 4.4 %copy-start.10 = (bf16[320,3584]{1,0:T(8,128)(2,1)S(1)}, bf16[320,3584]{1,0:T(8,128)(2,1)}, u32[]{:S(2)}) copy-start(bf16[320,3584]{1,0:T(8,128)(2,1)} %fusion.12) | copy-start | bytes 6881284
  98.5 2.9 %collective-permute-start.27 = (bf16[160,3584]{1,0:T(8,128)(2,1)S(1)}, bf16[160,3584]{1,0:T(8,128)(2,1)S(1)}, u32[]{:S(2)}, u32[]{:S(2)}) collective-permute-start(bf16[160,3584]{1,0:T(8,128)(2,1)S(1)} %slice.96), channel_id=1, source_target_pairs={{0,1},{1,0},{2,3},{3,2},{4,5},{5,4},{6,7},{7,6},{8,9},{9,8},{10,11... | collective-permute-start | bytes 3440648 | tf_op jit(solution)/shard_map/ppermute | solution.py:319
  102.6 7.7 %collective-permute-start.29 = (bf16[32,3584]{1,0:T(8,128)(2,1)S(1)}, bf16[32,3584]{1,0:T(8,128)(2,1)S(1)}, u32[]{:S(2)}, u32[]{:S(2)}) collective-permute-start(bf16[32,3584]{1,0:T(8,128)(2,1)S(1)} %get-tuple-element.111), channel_id=1, source_target_pairs={{0,2},{1,3},{4,0},{5,1},{8,4},{9,5},{12,8},{13,9},{14,12},{15,13},... | collective-permute-start | bytes 688136 | tf_op jit(solution)/shard_map/ppermute | solution.py:319
  103.8 7.4 %collective-permute-start.28 = (bf16[32,3584]{1,0:T(8,128)(2,1)S(1)}, bf16[32,3584]{1,0:T(8,128)(2,1)S(1)}, u32[]{:S(2)}, u32[]{:S(2)}) collective-permute-start(bf16[32,3584]{1,0:T(8,128)(2,1)S(1)} %get-tuple-element.112), channel_id=1, source_target_pairs={{0,4},{1,5},{4,8},{5,9},{8,12},{9,13},{12,14},{13,15},{14,10},{15,... | collective-permute-start | bytes 688136 | tf_op jit(solution)/shard_map/ppermute | solution.py:319
  111.4 6.5 %collective-permute-start.31 = (bf16[32,3584]{1,0:T(8,128)(2,1)S(1)}, bf16[32,3584]{1,0:T(8,128)(2,1)S(1)}, u32[]{:S(2)}, u32[]{:S(2)}) collective-permute-start(bf16[32,3584]{1,0:T(8,128)(2,1)S(1)} %get-tuple-element.109), channel_id=1, source_target_pairs={{0,2},{1,3},{4,0},{5,1},{8,4},{9,5},{12,8},{13,9},{14,12},{15,13},... | collective-permute-start | bytes 688136 | tf_op jit(solution)/shard_map/ppermute | solution.py:319
  112.6 6.2 %collective-permute-start.30 = (bf16[32,3584]{1,0:T(8,128)(2,1)S(1)}, bf16[32,3584]{1,0:T(8,128)(2,1)S(1)}, u32[]{:S(2)}, u32[]{:S(2)}) collective-permute-start(bf16[32,3584]{1,0:T(8,128)(2,1)S(1)} %get-tuple-element.110), channel_id=1, source_target_pairs={{0,4},{1,5},{4,8},{5,9},{8,12},{9,13},{12,14},{13,15},{14,10},{15,... | collective-permute-start | bytes 688136 | tf_op jit(solution)/shard_map/ppermute | solution.py:319
  (3 other events, 5.0 us)

commit v10 on v9

--- a/solution.py
+++ b/solution.py
@@ -147,7 +147,7 @@
     def tiles(height):
         return pl.BlockSpec((height, cols), lambda i: (0, i))
 
-    need = total * (cols * 16 + packed * 6 + 8 * LANES * 4) + 4 * latent * cols
+    need = total * (cols * 14 + packed * 6 + 6 * LANES * 4) + 4 * latent * cols
     return pl.pallas_call(
         lambda *refs: norm_kernel(far, blocks, rows, latent, width, *refs),
         grid=(width // cols,),
@@ -171,36 +171,40 @@
             pltpu.VMEM((total, experts_all), jnp.float32),
         ],
         compiler_params=pltpu.CompilerParams(
-            dimension_semantics=("arbitrary",), vmem_limit_bytes=(int(need) // (1 << 20) + 6) << 20
+            dimension_semantics=("arbitrary",), vmem_limit_bytes=(int(need) // (1 << 20) + 2) << 20
         ),
         cost_estimate=pl.CostEstimate(
-            flops=2 * total * width * latent,
-            bytes_accessed=2 * total * width * 2 + latent * width * 2,
+            flops=8 * total * width * latent,
+            bytes_accessed=6 * total * width * 2 + latent * width * 2,
             transcendentals=total,
         ),
         name="normalize",
     )(scalars, *pooled, *resid_blocks, w_out, gain, w_router_t)
 
 
-def lengths_kernel(owner, lengths, device, out):
-    rows = out.shape[0]
-    for j in range(rows):
-        length = lengths[owner[device[0] * rows + j]]
-        out[j : j + 1, :] = jnp.full((1, LANES), length, jnp.int32)
+def lookup_kernel(owner, lengths, table, device, row_lengths, scalars):
+    for j in range(row_lengths.shape[0]):
+        row_lengths[j] = lengths[owner[device[0] * row_lengths.shape[0] + j]]
+    for j in range(scalars.shape[0]):
+        scalars[j] = table[device[0] * scalars.shape[0] + j]
 
 
 LONG = dict(flops=10**10, bytes_accessed=10**8, transcendentals=0)
 
 
-def lengths_of(owner, lengths, device_index, rows):
+def lookup(owner, lengths, table, device_index, rows):
     scalar = pl.BlockSpec(memory_space=pltpu.SMEM)
     return pl.pallas_call(
-        lengths_kernel,
-        in_specs=[scalar] * 3,
-        out_shape=jax.ShapeDtypeStruct((rows, LANES), jnp.int32),
+        lookup_kernel,
+        in_specs=[scalar] * 4,
+        out_specs=[scalar] * 2,
+        out_shape=[
+            jax.ShapeDtypeStruct((rows,), jnp.int32),
+            jax.ShapeDtypeStruct(table.shape[1:], jnp.int32),
+        ],
         cost_estimate=pl.CostEstimate(**LONG),
-        name="lengths",
-    )(owner, lengths, device_index[None])
+        name="lookup",
+    )(owner, lengths, table.reshape(-1), device_index[None])
 
 
 def attention_kernel(context, latent, q, cache, fresh, lengths, routes, packet, keys_a, keys_b, total):
@@ -222,7 +226,10 @@
     row = lax.broadcasted_iota(jnp.int32, (rows, keys), 0)
     key = lax.broadcasted_iota(jnp.int32, (rows, keys), 1)
     place = key // rows
-    seen = (place < lengths[:, :1]) & (place < context)
+    length = jnp.zeros((rows, keys), jnp.int32)
+    for j in range(rows):
+        length = jnp.where(row == j, lengths[j], length)
+    seen = (place < length) & (place < context)
     seen = seen | ((place >= context) & (place <= context + step))
     bias = jnp.where(seen & (key % rows == row), 0.0, -1e30)
     summed = jnp.zeros((rows, keys), jnp.float32)
@@ -271,7 +278,7 @@
         lambda *refs: attention_kernel(context, latent, *refs),
         grid=(steps,),
         in_specs=[pl.BlockSpec((1, rows, q_abs.shape[2]), lambda i: (i, 0, 0))]
-        + [whole(a) for a in (cache, fresh, lengths, routes)],
+        + [whole(cache), whole(fresh), pl.BlockSpec(memory_space=pltpu.SMEM), whole(routes)],
         out_shape=jax.ShapeDtypeStruct((steps * rows, latent + LANES), jnp.bfloat16),
         out_specs=pl.BlockSpec((steps * rows, latent + LANES), lambda i: (0, 0)),
         scratch_shapes=[
@@ -280,7 +287,7 @@
             pltpu.VMEM((steps * rows, keys), jnp.float32),
         ],
         compiler_params=pltpu.CompilerParams(
-            dimension_semantics=("arbitrary",), vmem_limit_bytes=(10 << 20) + 10240 * keys
+            dimension_semantics=("arbitrary",), vmem_limit_bytes=56 << 20
         ),
         cost_estimate=pl.CostEstimate(**LONG),
         name="attention",
@@ -310,7 +317,6 @@
     sharers = devices // experts_all
     chips = devices // 2
     half = chips // 2
-    cut = rows // 2
     far, near = distances(chips)
     hold = lax.optimization_barrier
     sibling = sibling_perm(chips)
@@ -318,11 +324,14 @@
     def send(a, perm):
         return lax.ppermute(a, "expert", perm)
 
-    shifts = [(shift_perm(chips, by), shift_perm(chips, -by)) for by in (1, 2)]
-
-    def around(to_the_right, to_the_left, by=1):
-        right, left = shifts[by - 1]
-        return send(to_the_right, right), send(to_the_left, left)
+    to_right, to_left = shift_perm(chips, 1), shift_perm(chips, -1)
+    parted = [
+        shift_perm(chips, 2 - 4 * core)[2 * p + core] for p in range(chips) for core in range(2)
+    ]
+    first_core = device_index % 2 == 0
+
+    def around(to_the_right, to_the_left):
+        return send(to_the_right, to_right), send(to_the_left, to_left)
 
     positions, kv_width = latent_cache.shape[1:]
     wanted = (owner[:, None] == jnp.arange(owner.shape[0], dtype=jnp.int32)).astype(jnp.bfloat16)
@@ -335,23 +344,22 @@
     mine = resid.reshape(rows, width)
     held, sib = {0: mine}, {}
     held[-1], held[1] = around(mine, mine)
-    held[-2], held[2] = around(mine, mine, 2)
-    row_lengths = lengths_of(owner, lengths, device_index, row_count)
-    row_lengths, held = hold((row_lengths, held))
+    table = [
+        [device // sharers] + places
+        for chip, places in enumerate(gathered_place(chips))
+        for device in (2 * chip, 2 * chip + 1)
+    ]
+    row_lengths, scalars = lookup(
+        owner, lengths, jnp.array(table, jnp.int32), device_index, row_count
+    )
+    row_lengths, scalars, held = hold((row_lengths, scalars, held))
+    held[-2], held[2] = around(held[-1], held[1])
+    sib[0] = send(mine, sibling)
+    owned, held, sib = hold((owned, held, sib))
     for t in range(3, half):
         held[-t], held[t] = around(held[1 - t], held[t - 1])
-    last = around(held[2 - half][:cut], held[half - 2][cut:], 2)
-    for d in (0, -1, 1, -2, 2):
-        sib[d] = send(held[d], sibling)
+    sib[1], sib[-1] = send(held[1], sibling), send(held[-1], sibling)
     gain = norm_gain[None, :]
-    scalars = jnp.array(
-        [
-            [device // sharers] + places
-            for chip, places in enumerate(gathered_place(chips))
-            for device in (2 * chip, 2 * chip + 1)
-        ],
-        jnp.int32,
-    )[device_index]
     packet = attention(
         q_abs,
         owned.reshape(-1, kv_width),
@@ -361,14 +369,16 @@
         devices * positions,
         w_out.shape[0],
     )
-    packet, gain, scalars, held, last, sib = hold((packet, gain, scalars, held, last, sib))
+    packet, gain, held, sib = hold((packet, gain, held, sib))
 
     high, low = gather_steps(chips)
     along = [send(packet, step_perm(chips, i, 0)) for i in range(1, high)]
-    along = hold(along)
+    onward = send(jnp.where(first_core, held[2 - half], held[half - 2]), parted)
+    sib[2] = send(held[2], sibling)
+    along, onward, sib = hold((along, onward, sib))
+    held[half] = onward
     along = jnp.concatenate([packet] + along, axis=0)
     across = [send(along, step_perm(chips, 0, i)) for i in range(1, low)]
-    held[half] = jnp.concatenate(last, axis=0)
     for d in held:
         if d not in sib:
             sib[d] = send(held[d], sibling)
@@ -406,22 +416,23 @@
             at = slice(i * rows, (i + 1) * rows)
             sums[d] = y[at].astype(f32) + received[at].astype(f32)
 
-    def both(right, left, by=1):
-        return around(right.astype(jnp.bfloat16), left.astype(jnp.bfloat16), by)
+    def both(right, left):
+        return around(right.astype(jnp.bfloat16), left.astype(jnp.bfloat16))
 
     act = hold(activate(product(x_far, w_gate), product(x_far, w_up), slice(0, far_rows)))
     y, received = swap(far, product(act, w_down).astype(jnp.bfloat16))
     gated, y, received = hold((product(x_near, w_gate), y, received))
     add_up(far, y, received)
     right, left = both(sums[half - 1], sums[1 - half])
-    right2, left2 = both(sums[half][:cut], sums[half][cut:], 2)
-    act = activate(gated, product(x_near, w_up), slice(far_rows, None))
+    onward = send(sums[half].astype(jnp.bfloat16), parted)
+    act = hold(activate(gated, product(x_near, w_up), slice(far_rows, None)))
     y = product(act, w_down).astype(jnp.bfloat16)
-    y, right, left, right2, left2 = hold((y, right, left, right2, left2))
+    y, right, left, onward = hold((y, right, left, onward))
     y, received = swap(near, y)
     add_up(near, y, received)
-    right = right.astype(f32) + jnp.pad(right2.astype(f32), ((0, rows - cut), (0, 0)))
-    left = left.astype(f32) + jnp.pad(left2.astype(f32), ((cut, 0), (0, 0)))
+    onward = onward.astype(f32)
+    right = right.astype(f32) + jnp.where(first_core, onward, 0.0)
+    left = left.astype(f32) + jnp.where(first_core, 0.0, onward)
     for t in range(half - 2, 0, -1):
         right, left = hold(both(sums[t] + right.astype(f32), sums[-t] + left.astype(f32)))
     mixed = hidden + sums[0] + right.astype(f32) + left.astype(f32)

time: 120 us -> 115 us (0.958)
  waiting for transfers between devices: 34 us -> 41.8 us
  local copies, waits for them, and re-layouts: 9.44 us -> 2.34 us
  matrix products: 25.2 us -> 20.3 us
  Pallas kernels: 11.5 us -> 13.7 us
  other arithmetic: 3.08 us -> 1.41 us
  starting transfers between devices: 36.1 us -> 34.5 us
    ppermute x32 -> x30, waiting for transfers between devices: 34 us -> 41.8 us  [send(): return lax.ppermute(a, 'expert', perm)]
    dot_general x5 -> x6, matrix products: 24.2 us -> 19.3 us  [product(): return jnp.dot(a, w[0], preferred_element_type=f32)]
    unnamed x40 -> x29, local copies, waits for them, and re-layouts: 4.27 us -> 0.91 us
    pallas_call x1, Pallas kernels: 3.67 us -> 5.95 us  [attention(): pl.pallas_call(lambda *refs: attention_kernel(context, latent, *refs), gr...]
    ppermute x32 -> x30, starting transfers between devices: 29.9 us -> 28.2 us  [send(): return lax.ppermute(a, 'expert', perm)]
    slice x2, local copies, waits for them, and re-layouts: 1.53 us -> 0.12 us  [swap(): return (y, send(y[len(dists) * rows:], sibling))]
  transfers between devices with their start and end apart: 33 -> 31, of which waited for: 12 -> 14; matrix products, arithmetic and copies ran while one was open for 17% -> 7% of each run, Pallas kernels for 4% -> 6%
where the time goes in v10:
time: 115 us; the launch traced here: 114 us
  waiting for transfers between devices  41.8 us (36%)
  starting transfers between devices  34.5 us (30%)
  matrix products  20.3 us (18%)
  Pallas kernels  13.7 us (12%)
  local copies, waits for them, and re-layouts  2.34 us (2%)
  other arithmetic  1.41 us (1%)
    ppermute x30, waiting for transfers between devices, send(): return lax.ppermute(a, 'expert', perm)  41.8 us
    ppermute x30, starting transfers between devices, send(): return lax.ppermute(a, 'expert', perm)  28.2 us
    dot_general x6, matrix products, product(): return jnp.dot(a, w[0], preferred_element_type=f32)  19.3 us
    pallas_call x1, Pallas kernels, normalize(): pl.pallas_call(lambda *refs: norm_kernel(far, blocks, rows, latent, width...  6.43 us
    all_to_all x1, starting transfers between devices, local(): lax.all_to_all(ordered, 'expert', split_axis=0, concat_axis=0, tiled=True)  6.29 us
    pallas_call x1, Pallas kernels, attention(): pl.pallas_call(lambda *refs: attention_kernel(context, latent, *refs), gr...  5.95 us
  transfers between devices with their start and end apart: 31, of which 14 were waited for; matrix products, arithmetic and copies ran while one was open for 7% of the time, Pallas kernels for 6%

profile of v10, /device:TPU:0, one launch (start us, length us, event | category | flops | bytes accessed | tf_op | source)
XLA Modules:
  0.0 114.4 jit_solution(13771499691334010954)
XLA Ops:
  0.0 0.5 collective-permute-start.4
  0.5 2.6 %collective-permute-start.1 = (bf16[32,3584]{1,0:T(8,128)(2,1)}, bf16[32,3584]{1,0:T(8,128)(2,1)S(1)}, u32[]{:S(2)}, u32[]{:S(2)}) collective-permute-start(bf16[32,3584]{1,0:T(8,128)(2,1)} %bitcast.53), channel_id=1, source_target_pairs={{0,2},{1,3},{4,0},{5,1},{8,4},{9,5},{12,8},{13,9},{14,12},{15,13},... | collective-permute-start | bytes 688136 | tf_op jit(solution)/shard_map/ppermute | solution.py:325
  3.2 1.0 fusion.27
  4.4 0.7 copy.19
  5.1 6.3 %all-to-all-start = ((bf16[16,2,8,576]{3,2,1,0:T(8,128)(2,1)}), bf16[16,2,8,576]{3,2,1,0:T(8,128)(2,1)S(1)}, u32[]{:S(2)}, u32[]{:S(2)}) async-start(bf16[16,2,8,576]{3,2,1,0:T(8,128)(2,1)} %copy.19), calls=%async_computation | async-start | bytes 655360 | tf_op jit(solution)/shard_map/all_to_all | solution.py:342
  11.4 1.4 %lookup.1 = (s32[8]{0:T(128)}, s32[17]{0:T(128)}) custom-call(s32[128]{0:T(128)} %owner.1, s32[128]{0:T(128)} %lengths.1, s32[272]{0:T(512)} %constant.36.table, s32[1]{0:T(128)} %bitcast.device), custom_call_target="tpu_custom_call" | custom-call | flops 10000000000 | bytes 100000000 | tf_op jit(solution)/shard_map/lookup/pallas_call | solution.py:197
  12.8 2.0 %collective-permute-start.2 = (bf16[32,3584]{1,0:T(8,128)(2,1)S(1)}, bf16[32,3584]{1,0:T(8,128)(2,1)S(1)}, u32[]{:S(2)}, u32[]{:S(2)}) collective-permute-start(bf16[32,3584]{1,0:T(8,128)(2,1)S(1)} %collective-permute-done.refs_13_), channel_id=1, source_target_pairs={{0,4},{1,5},{4,8},{5,9},{8,12},{9,13},{12,14},{13,15},{14,10},{15,... | collective-permute-start | bytes 688136 | tf_op jit(solution)/shard_map/ppermute | solution.py:325
  14.9 8.3 %collective-permute-done.2.refs_15_ = bf16[32,3584]{1,0:T(8,128)(2,1)S(1)} collective-permute-done((bf16[32,3584]{1,0:T(8,128)(2,1)S(1)}, bf16[32,3584]{1,0:T(8,128)(2,1)S(1)}, u32[]{:S(2)}, u32[]{:S(2)}) %collective-permute-start.2) | collective-permute-done | bytes 229408 | tf_op jit(solution)/shard_map/ppermute | solution.py:325
  23.2 1.5 %collective-permute-done.3.refs_14_ = bf16[32,3584]{1,0:T(8,128)(2,1)S(1)} collective-permute-done((bf16[32,3584]{1,0:T(8,128)(2,1)S(1)}, bf16[32,3584]{1,0:T(8,128)(2,1)S(1)}, u32[]{:S(2)}, u32[]{:S(2)}) %collective-permute-start.3) | collective-permute-done | bytes 229408 | tf_op jit(solution)/shard_map/ppermute | solution.py:325
  24.7 3.2 %collective-permute-start.5 = (bf16[32,3584]{1,0:T(8,128)(2,1)S(1)}, bf16[32,3584]{1,0:T(8,128)(2,1)S(1)}, u32[]{:S(2)}, u32[]{:S(2)}) collective-permute-start(bf16[32,3584]{1,0:T(8,128)(2,1)S(1)} %collective-permute-done.2.refs_15_), channel_id=1, source_target_pairs={{0,4},{1,5},{4,8},{5,9},{8,12},{9,13},{12,14},{13,15},{14,10},{15,... | collective-permute-start | bytes 688136 | tf_op jit(solution)/shard_map/ppermute | solution.py:325
  28.0 0.5 collective-permute-start.8
  28.5 6.0 %attention.1 = bf16[32,640]{1,0:T(8,128)(2,1)} custom-call(bf16[4,8,36864]{2,1,0:T(8,128)(2,1)} %refs_0_.1, bf16[256,576]{1,0:T(8,128)(2,1)} %bitcast.58, bf16[32,576]{1,0:T(8,128)(2,1)} %bitcast.65, s32[8]{0:T(128)} %get-tuple-element.71.refs_3_, s32[32,8]{1,0:T(8,128)} %bitcast.66), custom_call_target="tpu_custom_call" | custom-call | flops 10000000000 | bytes 100000000 | tf_op jit(solution)/shard_map/attention/pallas_call | solution.py:277
  34.5 1.5 %collective-permute-done.6.refs_6_ = bf16[32,3584]{1,0:T(8,128)(2,1)S(1)} collective-permute-done((bf16[32,3584]{1,0:T(8,128)(2,1)S(1)}, bf16[32,3584]{1,0:T(8,128)(2,1)S(1)}, u32[]{:S(2)}, u32[]{:S(2)}) %collective-permute-start.6) | collective-permute-done | bytes 229408 | tf_op jit(solution)/shard_map/ppermute | solution.py:325
  36.0 0.6 collective-permute-start.12
  36.6 0.4 collective-permute-start.13
  37.0 0.8 collective-permute-start.11
  37.8 2.7 %collective-permute-start.10 = (bf16[32,640]{1,0:T(8,128)(2,1)}, bf16[32,640]{1,0:T(8,128)(2,1)S(1)}, u32[]{:S(2)}, u32[]{:S(2)}) collective-permute-start(bf16[32,640]{1,0:T(8,128)(2,1)} %attention.1), channel_id=1, source_target_pairs={{0,8},{1,9},{2,10},{3,11},{4,12},{5,13},{6,14},{7,15},{8,0},{9,1},... | collective-permute-start | bytes 122888 | tf_op jit(solution)/shard_map/ppermute | solution.py:325
  40.5 1.4 %collective-permute-start.9 = (bf16[32,640]{1,0:T(8,128)(2,1)}, bf16[32,640]{1,0:T(8,128)(2,1)S(1)}, u32[]{:S(2)}, u32[]{:S(2)}) collective-permute-start(bf16[32,640]{1,0:T(8,128)(2,1)} %attention.1), channel_id=1, source_target_pairs={{0,12},{1,13},{2,14},{3,15},{4,0},{5,1},{6,2},{7,3},{8,4},{9,5},{1... | collective-permute-start | bytes 122888 | tf_op jit(solution)/shard_map/ppermute | solution.py:325
  41.9 0.8 constant_dynamic-update-slice_fusion.3
  42.7 3.4 %collective-permute-done.11 = bf16[32,640]{1,0:T(8,128)(2,1)S(1)} collective-permute-done((bf16[32,640]{1,0:T(8,128)(2,1)}, bf16[32,640]{1,0:T(8,128)(2,1)S(1)}, u32[]{:S(2)}, u32[]{:S(2)}) %collective-permute-start.11) | collective-permute-done | bytes 40992 | tf_op jit(solution)/shard_map/ppermute | solution.py:325
  46.1 0.5 collective-permute-start.15
  46.7 0.4 collective-permute-start.18
  47.2 2.3 %collective-permute-start.14 = (bf16[128,640]{1,0:T(8,128)(2,1)S(1)}, bf16[128,640]{1,0:T(8,128)(2,1)S(1)}, u32[]{:S(2)}, u32[]{:S(2)}) collective-permute-start(bf16[128,640]{1,0:T(8,128)(2,1)S(1)} %constant_dynamic-update-slice_fusion.refs_1_), channel_id=1, source_target_pairs={{0,2},{1,3},{2,0},{3,1},{4,6},{5,7},{6,4},{7,5},{8,10},{9,11},{10,... | collective-permute-start | bytes 491528 | tf_op jit(solution)/shard_map/ppermute | solution.py:325
  49.7 4.6 %collective-permute-done.14.refs_2_ = bf16[128,640]{1,0:T(8,128)(2,1)S(1)} collective-permute-done((bf16[128,640]{1,0:T(8,128)(2,1)S(1)}, bf16[128,640]{1,0:T(8,128)(2,1)S(1)}, u32[]{:S(2)}, u32[]{:S(2)}) %collective-permute-start.14) | collective-permute-done | bytes 163872 | tf_op jit(solution)/shard_map/ppermute | solution.py:325
  54.3 1.4 %collective-permute-done.20.refs_4_ = bf16[128,640]{1,0:T(8,128)(2,1)S(1)} collective-permute-done((bf16[128,640]{1,0:T(8,128)(2,1)S(1)}, bf16[128,640]{1,0:T(8,128)(2,1)S(1)}, u32[]{:S(2)}, u32[]{:S(2)}) %collective-permute-start.20) | collective-permute-done | bytes 163872 | tf_op jit(solution)/shard_map/ppermute | solution.py:325
  55.7 6.4 %normalize.1 = (bf16[192,3584]{1,0:T(8,128)(2,1)S(1)}, bf16[320,3584]{1,0:T(8,128)(2,1)S(1)}, f32[512,128]{1,0:T(8,128)S(1)}, f32[512,128]{1,0:T(8,128)S(1)}, f32[32,3584]{1,0:T(8,128)S(1)}) custom-call(s32[17]{0:T(128)S(1)} %copy-done.4, bf16[128,640]{1,0:T(8,128)(2,1)S(1)} %constant_dynamic-update-slice_fusion.refs_1_, ...), custom_call_target="tpu_custom_call" | custom-call | flops 7516192768 | bytes 25690112 | tf_op jit(solution)/shard_map/normalize/pallas_call | solution.py:151
  62.5 4.9 %fusion.21 = f32[192,1024]{1,0:T(8,128)S(1)} fusion(bf16[192,3584]{1,0:T(8,128)(2,1)S(1)} %get-tuple-element.109, bf16[1,3584,1024]{2,1,0:T(8,128)(2,1)} %param.24, f32[192]{0:T(256)S(1)} %get-tuple-element.133), kind=kOutput, calls=%fused_computation.16 | convolution fusion | flops 1409482752 | bytes 9503488 | tf_op jit(solution)/shard_map/dot_general | solution.py:403
  67.5 5.1 %multiply_convert_fusion.1 = bf16[192,1024]{1,0:T(8,128)(2,1)S(1)} fusion(f32[192,1024]{1,0:T(8,128)S(1)} %fusion.21, f32[192]{0:T(256)S(1)} %get-tuple-element.132, f32[192]{0:T(256)S(1)} %get-tuple-element.133, bf16[192,3584]{1,0:T(8,128)(2,1)S(1)} %get-tuple-element.109, bf16[1,3584,1024]{2,1,0:T(8,128)(2,1)} %param.25), kind=kOutput, calls=%fused_computation.20 | convolution fusion | flops 1410859008 | bytes 9897472 | tf_op jit(solution)/shard_map/dot_general | solution.py:403
  72.6 1.6 %fusion.15 = bf16[192,3584]{1,0:T(8,128)(2,1)S(1)} fusion(bf16[192,1024]{1,0:T(8,128)(2,1)S(1)} %multiply_convert_fusion.1, bf16[1,1024,3584]{2,1,0:T(8,128)(2,1)S(1)} %bitcast.64), kind=kOutput, calls=%fused_computation.13 | convolution fusion | flops 1409974272 | bytes 9109504 | tf_op jit(solution)/shard_map/dot_general | solution.py:403
  74.5 2.5 %fusion.10 = f32[320,1024]{1,0:T(8,128)S(1)} fusion(bf16[320,3584]{1,0:T(8,128)(2,1)S(1)} %get-tuple-element.108, bf16[1,3584,1024]{2,1,0:T(8,128)(2,1)S(1)} %bitcast.60), kind=kOutput, calls=%fused_computation.10 | convolution fusion | flops 2348810240 | bytes 10944512 | tf_op jit(solution)/shard_map/dot_general | solution.py:403
  77.1 2.7 %multiply_convert_fusion = bf16[320,1024]{1,0:T(8,128)(2,1)S(1)} fusion(f32[320,1024]{1,0:T(8,128)S(1)} %fusion.10, f32[320]{0:T(512)S(1)} %get-tuple-element.130, f32[320]{0:T(512)S(1)} %get-tuple-element.131, bf16[320,3584]{1,0:T(8,128)(2,1)S(1)} %get-tuple-element.108, bf16[1,3584,1024]{2,1,0:T(8,128)(2,1)S(1)} %bitcast.62), kind=kOutput, calls=%fused_computation.15 | convolution fusion | flops 2351759360 | bytes 11602432 | tf_op jit(solution)/shard_map/dot_general | solution.py:403
  79.9 1.9 %collective-permute-start.24 = (bf16[32,3584]{1,0:T(8,128)(2,1)S(1)}, bf16[32,3584]{1,0:T(8,128)(2,1)S(1)}, u32[]{:S(2)}, u32[]{:S(2)}) collective-permute-start(bf16[32,3584]{1,0:T(8,128)(2,1)S(1)} %get-tuple-element.127), channel_id=1, source_target_pairs={{0,8},{1,7},{4,12},{5,3},{8,14},{9,1},{12,10},{13,5},{14,6},{15,9}... | collective-permute-start | bytes 688136 | tf_op jit(solution)/shard_map/ppermute | solution.py:325
  82.0 1.8 %collective-permute-start.22 = (bf16[32,3584]{1,0:T(8,128)(2,1)S(1)}, bf16[32,3584]{1,0:T(8,128)(2,1)S(1)}, u32[]{:S(2)}, u32[]{:S(2)}) collective-permute-start(bf16[32,3584]{1,0:T(8,128)(2,1)S(1)} %get-tuple-element.129), channel_id=1, source_target_pairs={{0,4},{1,5},{4,8},{5,9},{8,12},{9,13},{12,14},{13,15},{14,10},{15,... | collective-permute-start | bytes 688136 | tf_op jit(solution)/shard_map/ppermute | solution.py:325
  83.8 2.5 %fusion.12 = bf16[320,3584]{1,0:T(8,128)(2,1)S(1)} fusion(bf16[320,1024]{1,0:T(8,128)(2,1)S(1)} %multiply_convert_fusion, bf16[1,1024,3584]{2,1,0:T(8,128)(2,1)S(1)} %bitcast.64), kind=kOutput, calls=%fused_computation.12 | convolution fusion | flops 2349957120 | bytes 10289152 | tf_op jit(solution)/shard_map/dot_general | solution.py:403
  86.4 2.9 %collective-permute-done.24 = bf16[32,3584]{1,0:T(8,128)(2,1)S(1)} collective-permute-done((bf16[32,3584]{1,0:T(8,128)(2,1)S(1)}, bf16[32,3584]{1,0:T(8,128)(2,1)S(1)}, u32[]{:S(2)}, u32[]{:S(2)}) %collective-permute-start.24) | collective-permute-done | bytes 229408 | tf_op jit(solution)/shard_map/ppermute | solution.py:325
  89.2 2.7 %collective-permute-done.23 = bf16[32,3584]{1,0:T(8,128)(2,1)S(1)} collective-permute-done((bf16[32,3584]{1,0:T(8,128)(2,1)S(1)}, bf16[32,3584]{1,0:T(8,128)(2,1)S(1)}, u32[]{:S(2)}, u32[]{:S(2)}) %collective-permute-start.23) | collective-permute-done | bytes 229408 | tf_op jit(solution)/shard_map/ppermute | solution.py:325
  92.1 1.5 %collective-permute-start.25 = (bf16[160,3584]{1,0:T(8,128)(2,1)S(1)}, bf16[160,3584]{1,0:T(8,128)(2,1)S(1)}, u32[]{:S(2)}, u32[]{:S(2)}) collective-permute-start(bf16[160,3584]{1,0:T(8,128)(2,1)S(1)} %slice.78), channel_id=1, source_target_pairs={{0,1},{1,0},{2,3},{3,2},{4,5},{5,4},{6,7},{7,6},{8,9},{9,8},{10,11... | collective-permute-start | bytes 3440648 | tf_op jit(solution)/shard_map/ppermute | solution.py:325
  93.6 2.4 %collective-permute-done.25 = bf16[160,3584]{1,0:T(8,128)(2,1)S(1)} collective-permute-done((bf16[160,3584]{1,0:T(8,128)(2,1)S(1)}, bf16[160,3584]{1,0:T(8,128)(2,1)S(1)}, u32[]{:S(2)}, u32[]{:S(2)}) %collective-permute-start.25) | collective-permute-done | bytes 1146912 | tf_op jit(solution)/shard_map/ppermute | solution.py:325
  96.0 0.2 fusion.35
  96.3 1.8 %collective-permute-start.27 = (bf16[32,3584]{1,0:T(8,128)(2,1)S(1)}, bf16[32,3584]{1,0:T(8,128)(2,1)S(1)}, u32[]{:S(2)}, u32[]{:S(2)}) collective-permute-start(bf16[32,3584]{1,0:T(8,128)(2,1)S(1)} %get-tuple-element.123), channel_id=1, source_target_pairs={{0,2},{1,3},{4,0},{5,1},{8,4},{9,5},{12,8},{13,9},{14,12},{15,13},... | collective-permute-start | bytes 688136 | tf_op jit(solution)/shard_map/ppermute | solution.py:325
  98.1 0.3 collective-permute-start.26
  98.4 5.8 %collective-permute-done.27 = bf16[32,3584]{1,0:T(8,128)(2,1)S(1)} collective-permute-done((bf16[32,3584]{1,0:T(8,128)(2,1)S(1)}, bf16[32,3584]{1,0:T(8,128)(2,1)S(1)}, u32[]{:S(2)}, u32[]{:S(2)}) %collective-permute-start.27) | collective-permute-done | bytes 229408 | tf_op jit(solution)/shard_map/ppermute | solution.py:325
  104.2 1.2 %collective-permute-done.26 = bf16[32,3584]{1,0:T(8,128)(2,1)S(1)} collective-permute-done((bf16[32,3584]{1,0:T(8,128)(2,1)S(1)}, bf16[32,3584]{1,0:T(8,128)(2,1)S(1)}, u32[]{:S(2)}, u32[]{:S(2)}) %collective-permute-start.26) | collective-permute-done | bytes 229408 | tf_op jit(solution)/shard_map/ppermute | solution.py:325
  105.6 1.8 %collective-permute-start.29 = (bf16[32,3584]{1,0:T(8,128)(2,1)S(1)}, bf16[32,3584]{1,0:T(8,128)(2,1)S(1)}, u32[]{:S(2)}, u32[]{:S(2)}) collective-permute-start(bf16[32,3584]{1,0:T(8,128)(2,1)S(1)} %get-tuple-element.125), channel_id=1, source_target_pairs={{0,2},{1,3},{4,0},{5,1},{8,4},{9,5},{12,8},{13,9},{14,12},{15,13},... | collective-permute-start | bytes 688136 | tf_op jit(solution)/shard_map/ppermute | solution.py:325
  107.4 0.3 collective-permute-start.28
  107.7 4.5 %collective-permute-done.29 = bf16[32,3584]{1,0:T(8,128)(2,1)S(1)} collective-permute-done((bf16[32,3584]{1,0:T(8,128)(2,1)S(1)}, bf16[32,3584]{1,0:T(8,128)(2,1)S(1)}, u32[]{:S(2)}, u32[]{:S(2)}) %collective-permute-start.29) | collective-permute-done | bytes 229408 | tf_op jit(solution)/shard_map/ppermute | solution.py:325
  112.1 1.4 %collective-permute-done.28 = bf16[32,3584]{1,0:T(8,128)(2,1)S(1)} collective-permute-done((bf16[32,3584]{1,0:T(8,128)(2,1)S(1)}, bf16[32,3584]{1,0:T(8,128)(2,1)S(1)}, u32[]{:S(2)}, u32[]{:S(2)}) %collective-permute-start.28) | collective-permute-done | bytes 229408 | tf_op jit(solution)/shard_map/ppermute | solution.py:325
  113.6 0.8 fusion.38
  (69 shorter events, 2.1 us)
Async XLA Ops:
  0.0 3.2 %copy-start = (bf16[128,2,576]{0,2,1:T(8,128)(2,1)S(1)}, bf16[128,2,576]{0,2,1:T(8,128)(2,1)}, u32[]{:S(2)}) copy-start(bf16[128,2,576]{0,2,1:T(8,128)(2,1)} %param.16) | copy-start | bytes 884740
  0.0 14.9 %collective-permute-start.4 = (bf16[32,3584]{1,0:T(8,128)(2,1)}, bf16[32,3584]{1,0:T(8,128)(2,1)S(1)}, u32[]{:S(2)}, u32[]{:S(2)}) collective-permute-start(bf16[32,3584]{1,0:T(8,128)(2,1)} %bitcast.52), channel_id=1, source_target_pairs={{0,1},{1,0},{2,3},{3,2},{4,5},{5,4},{6,7},{7,6},{8,9},{9,8},{10,11... | collective-permute-start | bytes 688136 | tf_op jit(solution)/shard_map/ppermute | solution.py:325
  0.5 12.3 %collective-permute-start.1 = (bf16[32,3584]{1,0:T(8,128)(2,1)}, bf16[32,3584]{1,0:T(8,128)(2,1)S(1)}, u32[]{:S(2)}, u32[]{:S(2)}) collective-permute-start(bf16[32,3584]{1,0:T(8,128)(2,1)} %bitcast.53), channel_id=1, source_target_pairs={{0,2},{1,3},{4,0},{5,1},{8,4},{9,5},{12,8},{13,9},{14,12},{15,13},... | collective-permute-start | bytes 688136 | tf_op jit(solution)/shard_map/ppermute | solution.py:325
  3.0 9.8 %collective-permute-start = (bf16[32,3584]{1,0:T(8,128)(2,1)}, bf16[32,3584]{1,0:T(8,128)(2,1)S(1)}, u32[]{:S(2)}, u32[]{:S(2)}) collective-permute-start(bf16[32,3584]{1,0:T(8,128)(2,1)} %bitcast.54), channel_id=1, source_target_pairs={{0,4},{1,5},{4,8},{5,9},{8,12},{9,13},{12,14},{13,15},{14,10},{15,... | collective-permute-start | bytes 688136 | tf_op jit(solution)/shard_map/ppermute | solution.py:325
  5.1 19.6 %all-to-all-start = ((bf16[16,2,8,576]{3,2,1,0:T(8,128)(2,1)}), bf16[16,2,8,576]{3,2,1,0:T(8,128)(2,1)S(1)}, u32[]{:S(2)}, u32[]{:S(2)}) async-start(bf16[16,2,8,576]{3,2,1,0:T(8,128)(2,1)} %copy.19), calls=%async_computation | async-start | bytes 655360 | tf_op jit(solution)/shard_map/all_to_all | solution.py:342
  11.4 3.5 %copy-start.6 = (bf16[3584]{0:T(1024)(128)(2,1)S(1)}, bf16[3584]{0:T(1024)(128)(2,1)}, u32[]{:S(2)}) copy-start(bf16[3584]{0:T(1024)(128)(2,1)} %param.22) | copy-start | bytes 21508
  12.8 10.4 %collective-permute-start.2 = (bf16[32,3584]{1,0:T(8,128)(2,1)S(1)}, bf16[32,3584]{1,0:T(8,128)(2,1)S(1)}, u32[]{:S(2)}, u32[]{:S(2)}) collective-permute-start(bf16[32,3584]{1,0:T(8,128)(2,1)S(1)} %collective-permute-done.refs_13_), channel_id=1, source_target_pairs={{0,4},{1,5},{4,8},{5,9},{8,12},{9,13},{12,14},{13,15},{14,10},{15,... | collective-permute-start | bytes 688136 | tf_op jit(solution)/shard_map/ppermute | solution.py:325
  14.8 9.9 %collective-permute-start.3 = (bf16[32,3584]{1,0:T(8,128)(2,1)S(1)}, bf16[32,3584]{1,0:T(8,128)(2,1)S(1)}, u32[]{:S(2)}, u32[]{:S(2)}) collective-permute-start(bf16[32,3584]{1,0:T(8,128)(2,1)S(1)} %collective-permute-done.1.refs_12_), channel_id=1, source_target_pairs={{0,2},{1,3},{4,0},{5,1},{8,4},{9,5},{12,8},{13,9},{14,12},{15,13},... | collective-permute-start | bytes 688136 | tf_op jit(solution)/shard_map/ppermute | solution.py:325
  24.7 3.7 %copy-start.5 = (bf16[16,2,8,576]{3,2,1,0:T(8,128)(2,1)}, bf16[16,2,8,576]{3,2,1,0:T(8,128)(2,1)S(1)}, u32[]{:S(2)}) copy-start(bf16[16,2,8,576]{3,2,1,0:T(8,128)(2,1)S(1)} %all-to-all-done) | copy-start | bytes 884740
  24.7 9.7 %collective-permute-start.5 = (bf16[32,3584]{1,0:T(8,128)(2,1)S(1)}, bf16[32,3584]{1,0:T(8,128)(2,1)S(1)}, u32[]{:S(2)}, u32[]{:S(2)}) collective-permute-start(bf16[32,3584]{1,0:T(8,128)(2,1)S(1)} %collective-permute-done.2.refs_15_), channel_id=1, source_target_pairs={{0,4},{1,5},{4,8},{5,9},{8,12},{9,13},{12,14},{13,15},{14,10},{15,... | collective-permute-start | bytes 688136 | tf_op jit(solution)/shard_map/ppermute | solution.py:325
  28.0 6.5 %collective-permute-start.7 = (bf16[32,3584]{1,0:T(8,128)(2,1)S(1)}, bf16[32,3584]{1,0:T(8,128)(2,1)S(1)}, u32[]{:S(2)}, u32[]{:S(2)}) collective-permute-start(bf16[32,3584]{1,0:T(8,128)(2,1)S(1)} %collective-permute-done.refs_13_), channel_id=1, source_target_pairs={{0,1},{1,0},{2,3},{3,2},{4,5},{5,4},{6,7},{7,6},{8,9},{9,8},{10,11... | collective-permute-start | bytes 688136 | tf_op jit(solution)/shard_map/ppermute | solution.py:325
  28.0 6.5 %collective-permute-start.8 = (bf16[32,3584]{1,0:T(8,128)(2,1)S(1)}, bf16[32,3584]{1,0:T(8,128)(2,1)S(1)}, u32[]{:S(2)}, u32[]{:S(2)}) collective-permute-start(bf16[32,3584]{1,0:T(8,128)(2,1)S(1)} %collective-permute-done.1.refs_12_), channel_id=1, source_target_pairs={{0,1},{1,0},{2,3},{3,2},{4,5},{5,4},{6,7},{7,6},{8,9},{9,8},{10,11... | collective-permute-start | bytes 688136 | tf_op jit(solution)/shard_map/ppermute | solution.py:325
  28.5 7.5 %collective-permute-start.6 = (bf16[32,3584]{1,0:T(8,128)(2,1)S(1)}, bf16[32,3584]{1,0:T(8,128)(2,1)S(1)}, u32[]{:S(2)}, u32[]{:S(2)}) collective-permute-start(bf16[32,3584]{1,0:T(8,128)(2,1)S(1)} %collective-permute-done.3.refs_14_), channel_id=1, source_target_pairs={{0,2},{1,3},{4,0},{5,1},{8,4},{9,5},{12,8},{13,9},{14,12},{15,13},... | collective-permute-start | bytes 688136 | tf_op jit(solution)/shard_map/ppermute | solution.py:325
  28.5 27.2 %copy-start.1 = (bf16[512,3584]{1,0:T(8,128)(2,1)S(1)}, bf16[512,3584]{1,0:T(8,128)(2,1)}, u32[]{:S(2)}) copy-start(bf16[512,3584]{1,0:T(8,128)(2,1)} %refs_21_.1) | copy-start | bytes 11010052
  28.5 27.2 %copy-start.2 = (bf16[4,8,3584]{2,1,0:T(8,128)(2,1)S(1)}, bf16[4,8,3584]{2,1,0:T(8,128)(2,1)}, u32[]{:S(2)}) copy-start(bf16[4,8,3584]{2,1,0:T(8,128)(2,1)} %param.19) | copy-start | bytes 688132
  28.5 27.2 %copy-start.3 = (bf16[3584,16]{0,1:T(8,128)(2,1)S(1)}, bf16[3584,16]{0,1:T(8,128)(2,1)}, u32[]{:S(2)}) copy-start(bf16[3584,16]{0,1:T(8,128)(2,1)} %param.23) | copy-start | bytes 344068
  28.5 27.2 %copy-start.4 = (s32[17]{0:T(128)S(1)}, s32[17]{0:T(128)}, u32[]{:S(2)}) copy-start(s32[17]{0:T(128)} %get-tuple-element.66.refs_0_) | copy-start | bytes 208
  36.0 10.7 %collective-permute-start.12 = (bf16[32,3584]{1,0:T(8,128)(2,1)S(1)}, bf16[32,3584]{1,0:T(8,128)(2,1)S(1)}, u32[]{:S(2)}, u32[]{:S(2)}) collective-permute-start(bf16[32,3584]{1,0:T(8,128)(2,1)S(1)} %broadcast_select_fusion), channel_id=1, source_target_pairs={{0,8},{1,7},{4,12},{5,3},{8,14},{9,1},{12,10},{13,5},{14,6},{15,9}... | collective-permute-start | bytes 688136 | tf_op jit(solution)/shard_map/ppermute | solution.py:325
  36.6 10.1 %collective-permute-start.13 = (bf16[32,3584]{1,0:T(8,128)(2,1)S(1)}, bf16[32,3584]{1,0:T(8,128)(2,1)S(1)}, u32[]{:S(2)}, u32[]{:S(2)}) collective-permute-start(bf16[32,3584]{1,0:T(8,128)(2,1)S(1)} %collective-permute-done.3.refs_14_), channel_id=1, source_target_pairs={{0,1},{1,0},{2,3},{3,2},{4,5},{5,4},{6,7},{7,6},{8,9},{9,8},{10,11... | collective-permute-start | bytes 688136 | tf_op jit(solution)/shard_map/ppermute | solution.py:325
  37.0 9.1 %collective-permute-start.11 = (bf16[32,640]{1,0:T(8,128)(2,1)}, bf16[32,640]{1,0:T(8,128)(2,1)S(1)}, u32[]{:S(2)}, u32[]{:S(2)}) collective-permute-start(bf16[32,640]{1,0:T(8,128)(2,1)} %attention.1), channel_id=1, source_target_pairs={{0,4},{1,5},{2,6},{3,7},{4,8},{5,9},{6,10},{7,11},{8,12},{9,13},{1... | collective-permute-start | bytes 122888 | tf_op jit(solution)/shard_map/ppermute | solution.py:325
  37.8 8.3 %collective-permute-start.10 = (bf16[32,640]{1,0:T(8,128)(2,1)}, bf16[32,640]{1,0:T(8,128)(2,1)S(1)}, u32[]{:S(2)}, u32[]{:S(2)}) collective-permute-start(bf16[32,640]{1,0:T(8,128)(2,1)} %attention.1), channel_id=1, source_target_pairs={{0,8},{1,9},{2,10},{3,11},{4,12},{5,13},{6,14},{7,15},{8,0},{9,1},... | collective-permute-start | bytes 122888 | tf_op jit(solution)/shard_map/ppermute | solution.py:325
  40.5 6.1 %collective-permute-start.9 = (bf16[32,640]{1,0:T(8,128)(2,1)}, bf16[32,640]{1,0:T(8,128)(2,1)S(1)}, u32[]{:S(2)}, u32[]{:S(2)}) collective-permute-start(bf16[32,640]{1,0:T(8,128)(2,1)} %attention.1), channel_id=1, source_target_pairs={{0,12},{1,13},{2,14},{3,15},{4,0},{5,1},{6,2},{7,3},{8,4},{9,5},{1... | collective-permute-start | bytes 122888 | tf_op jit(solution)/shard_map/ppermute | solution.py:325
  46.1 3.6 %collective-permute-start.16 = (bf16[32,3584]{1,0:T(8,128)(2,1)S(1)}, bf16[32,3584]{1,0:T(8,128)(2,1)S(1)}, u32[]{:S(2)}, u32[]{:S(2)}) collective-permute-start(bf16[32,3584]{1,0:T(8,128)(2,1)S(1)} %collective-permute-done.2.refs_15_), channel_id=1, source_target_pairs={{0,1},{1,0},{2,3},{3,2},{4,5},{5,4},{6,7},{7,6},{8,9},{9,8},{10,11... | collective-permute-start | bytes 688136 | tf_op jit(solution)/shard_map/ppermute | solution.py:325
  46.1 3.4 %collective-permute-start.15 = (bf16[32,3584]{1,0:T(8,128)(2,1)S(1)}, bf16[32,3584]{1,0:T(8,128)(2,1)S(1)}, u32[]{:S(2)}, u32[]{:S(2)}) collective-permute-start(bf16[32,3584]{1,0:T(8,128)(2,1)S(1)} %collective-permute-done.5.refs_7_), channel_id=1, source_target_pairs={{0,1},{1,0},{2,3},{3,2},{4,5},{5,4},{6,7},{7,6},{8,9},{9,8},{10,11... | collective-permute-start | bytes 688136 | tf_op jit(solution)/shard_map/ppermute | solution.py:325
  46.6 3.0 %collective-permute-start.17 = (bf16[32,3584]{1,0:T(8,128)(2,1)S(1)}, bf16[32,3584]{1,0:T(8,128)(2,1)S(1)}, u32[]{:S(2)}, u32[]{:S(2)}) collective-permute-start(bf16[32,3584]{1,0:T(8,128)(2,1)S(1)} %collective-permute-done.6.refs_6_), channel_id=1, source_target_pairs={{0,1},{1,0},{2,3},{3,2},{4,5},{5,4},{6,7},{7,6},{8,9},{9,8},{10,11... | collective-permute-start | bytes 688136 | tf_op jit(solution)/shard_map/ppermute | solution.py:325
  46.7 7.6 %collective-permute-start.18 = (bf16[32,3584]{1,0:T(8,128)(2,1)S(1)}, bf16[32,3584]{1,0:T(8,128)(2,1)S(1)}, u32[]{:S(2)}, u32[]{:S(2)}) collective-permute-start(bf16[32,3584]{1,0:T(8,128)(2,1)S(1)} %collective-permute-done.12.refs_5_), channel_id=1, source_target_pairs={{0,1},{1,0},{2,3},{3,2},{4,5},{5,4},{6,7},{7,6},{8,9},{9,8},{10,11... | collective-permute-start | bytes 688136 | tf_op jit(solution)/shard_map/ppermute | solution.py:325
  47.2 7.1 %collective-permute-start.14 = (bf16[128,640]{1,0:T(8,128)(2,1)S(1)}, bf16[128,640]{1,0:T(8,128)(2,1)S(1)}, u32[]{:S(2)}, u32[]{:S(2)}) collective-permute-start(bf16[128,640]{1,0:T(8,128)(2,1)S(1)} %constant_dynamic-update-slice_fusion.refs_1_), channel_id=1, source_target_pairs={{0,2},{1,3},{2,0},{3,1},{4,6},{5,7},{6,4},{7,5},{8,10},{9,11},{10,... | collective-permute-start | bytes 491528 | tf_op jit(solution)/shard_map/ppermute | solution.py:325
  49.5 4.8 %collective-permute-start.19 = (bf16[128,640]{1,0:T(8,128)(2,1)S(1)}, bf16[128,640]{1,0:T(8,128)(2,1)S(1)}, u32[]{:S(2)}, u32[]{:S(2)}) collective-permute-start(bf16[128,640]{1,0:T(8,128)(2,1)S(1)} %constant_dynamic-update-slice_fusion.refs_1_), channel_id=1, source_target_pairs={{0,1},{1,0},{2,3},{3,2},{4,5},{5,4},{6,7},{7,6},{8,9},{9,8},{10,11... | collective-permute-start | bytes 491528 | tf_op jit(solution)/shard_map/ppermute | solution.py:325
  54.3 1.4 %collective-permute-start.20 = (bf16[128,640]{1,0:T(8,128)(2,1)S(1)}, bf16[128,640]{1,0:T(8,128)(2,1)S(1)}, u32[]{:S(2)}, u32[]{:S(2)}) collective-permute-start(bf16[128,640]{1,0:T(8,128)(2,1)S(1)} %collective-permute-done.14.refs_2_), channel_id=1, source_target_pairs={{0,1},{1,0},{2,3},{3,2},{4,5},{5,4},{6,7},{7,6},{8,9},{9,8},{10,11... | collective-permute-start | bytes 491528 | tf_op jit(solution)/shard_map/ppermute | solution.py:325
  62.5 10.1 %slice-start.4 = ((s8[7340032]{0:T(1024)(128)(4,1)}), s8[4194304]{0:T(1024)(128)(4,1)S(1)}, s32[]{:S(2)}) async-start(s8[7340032]{0:T(1024)(128)(4,1)} %bitcast.63), calls=%async_computation.5 | async-start | bytes 8388608
  62.5 12.0 %slice-start = ((s8[7340032]{0:T(1024)(128)(4,1)}), s8[4194304]{0:T(1024)(128)(4,1)S(1)}, s32[]{:S(2)}) async-start(s8[7340032]{0:T(1024)(128)(4,1)} %bitcast.59), calls=%async_computation.1 | async-start | bytes 8388608
  67.5 5.1 %slice-start.5 = ((s8[7340032]{0:T(1024)(128)(4,1)}), s8[3145728]{0:T(1024)(128)(4,1)S(1)}, s32[]{:S(2)}) async-start(s8[7340032]{0:T(1024)(128)(4,1)} %bitcast.63), calls=%async_computation.6 | async-start | bytes 6291456
  67.5 7.0 %slice-start.1 = ((s8[7340032]{0:T(1024)(128)(4,1)}), s8[3145728]{0:T(1024)(128)(4,1)S(1)}, s32[]{:S(2)}) async-start(s8[7340032]{0:T(1024)(128)(4,1)} %bitcast.59), calls=%async_computation.2 | async-start | bytes 6291456
  72.6 4.4 %slice-start.2 = ((s8[7340032]{0:T(1024)(128)(4,1)}), s8[4194304]{0:T(1024)(128)(4,1)S(1)}, s32[]{:S(2)}) async-start(s8[7340032]{0:T(1024)(128)(4,1)} %bitcast.61), calls=%async_computation.3 | async-start | bytes 8388608
  74.3 2.8 %collective-permute-start.21 = (bf16[96,3584]{1,0:T(8,128)(2,1)S(1)}, bf16[96,3584]{1,0:T(8,128)(2,1)S(1)}, u32[]{:S(2)}, u32[]{:S(2)}) collective-permute-start(bf16[96,3584]{1,0:T(8,128)(2,1)S(1)} %slice.88), channel_id=1, source_target_pairs={{0,1},{1,0},{2,3},{3,2},{4,5},{5,4},{6,7},{7,6},{8,9},{9,8},{10,11... | collective-permute-start | bytes 2064392 | tf_op jit(solution)/shard_map/ppermute | solution.py:325
  74.5 2.6 %slice-start.3 = ((s8[7340032]{0:T(1024)(128)(4,1)}), s8[3145728]{0:T(1024)(128)(4,1)S(1)}, s32[]{:S(2)}) async-start(s8[7340032]{0:T(1024)(128)(4,1)} %bitcast.61), calls=%async_computation.4 | async-start | bytes 6291456
  79.9 9.3 %collective-permute-start.24 = (bf16[32,3584]{1,0:T(8,128)(2,1)S(1)}, bf16[32,3584]{1,0:T(8,128)(2,1)S(1)}, u32[]{:S(2)}, u32[]{:S(2)}) collective-permute-start(bf16[32,3584]{1,0:T(8,128)(2,1)S(1)} %get-tuple-element.127), channel_id=1, source_target_pairs={{0,8},{1,7},{4,12},{5,3},{8,14},{9,1},{12,10},{13,5},{14,6},{15,9}... | collective-permute-start | bytes 688136 | tf_op jit(solution)/shard_map/ppermute | solution.py:325
  81.8 10.1 %collective-permute-start.23 = (bf16[32,3584]{1,0:T(8,128)(2,1)S(1)}, bf16[32,3584]{1,0:T(8,128)(2,1)S(1)}, u32[]{:S(2)}, u32[]{:S(2)}) collective-permute-start(bf16[32,3584]{1,0:T(8,128)(2,1)S(1)} %get-tuple-element.128), channel_id=1, source_target_pairs={{0,2},{1,3},{4,0},{5,1},{8,4},{9,5},{12,8},{13,9},{14,12},{15,13},... | collective-permute-start | bytes 688136 | tf_op jit(solution)/shard_map/ppermute | solution.py:325
  82.0 10.0 %collective-permute-start.22 = (bf16[32,3584]{1,0:T(8,128)(2,1)S(1)}, bf16[32,3584]{1,0:T(8,128)(2,1)S(1)}, u32[]{:S(2)}, u32[]{:S(2)}) collective-permute-start(bf16[32,3584]{1,0:T(8,128)(2,1)S(1)} %get-tuple-element.129), channel_id=1, source_target_pairs={{0,4},{1,5},{4,8},{5,9},{8,12},{9,13},{12,14},{13,15},{14,10},{15,... | collective-permute-start | bytes 688136 | tf_op jit(solution)/shard_map/ppermute | solution.py:325
  92.1 4.0 %collective-permute-start.25 = (bf16[160,3584]{1,0:T(8,128)(2,1)S(1)}, bf16[160,3584]{1,0:T(8,128)(2,1)S(1)}, u32[]{:S(2)}, u32[]{:S(2)}) collective-permute-start(bf16[160,3584]{1,0:T(8,128)(2,1)S(1)} %slice.78), channel_id=1, source_target_pairs={{0,1},{1,0},{2,3},{3,2},{4,5},{5,4},{6,7},{7,6},{8,9},{9,8},{10,11... | collective-permute-start | bytes 3440648 | tf_op jit(solution)/shard_map/ppermute | solution.py:325
  96.3 7.9 %collective-permute-start.27 = (bf16[32,3584]{1,0:T(8,128)(2,1)S(1)}, bf16[32,3584]{1,0:T(8,128)(2,1)S(1)}, u32[]{:S(2)}, u32[]{:S(2)}) collective-permute-start(bf16[32,3584]{1,0:T(8,128)(2,1)S(1)} %get-tuple-element.123), channel_id=1, source_target_pairs={{0,2},{1,3},{4,0},{5,1},{8,4},{9,5},{12,8},{13,9},{14,12},{15,13},... | collective-permute-start | bytes 688136 | tf_op jit(solution)/shard_map/ppermute | solution.py:325
  98.1 7.4 %collective-permute-start.26 = (bf16[32,3584]{1,0:T(8,128)(2,1)S(1)}, bf16[32,3584]{1,0:T(8,128)(2,1)S(1)}, u32[]{:S(2)}, u32[]{:S(2)}) collective-permute-start(bf16[32,3584]{1,0:T(8,128)(2,1)S(1)} %get-tuple-element.124), channel_id=1, source_target_pairs={{0,4},{1,5},{4,8},{5,9},{8,12},{9,13},{12,14},{13,15},{14,10},{15,... | collective-permute-start | bytes 688136 | tf_op jit(solution)/shard_map/ppermute | solution.py:325
  105.6 6.5 %collective-permute-start.29 = (bf16[32,3584]{1,0:T(8,128)(2,1)S(1)}, bf16[32,3584]{1,0:T(8,128)(2,1)S(1)}, u32[]{:S(2)}, u32[]{:S(2)}) collective-permute-start(bf16[32,3584]{1,0:T(8,128)(2,1)S(1)} %get-tuple-element.125), channel_id=1, source_target_pairs={{0,2},{1,3},{4,0},{5,1},{8,4},{9,5},{12,8},{13,9},{14,12},{15,13},... | collective-permute-start | bytes 688136 | tf_op jit(solution)/shard_map/ppermute | solution.py:325
  107.4 6.2 %collective-permute-start.28 = (bf16[32,3584]{1,0:T(8,128)(2,1)S(1)}, bf16[32,3584]{1,0:T(8,128)(2,1)S(1)}, u32[]{:S(2)}, u32[]{:S(2)}) collective-permute-start(bf16[32,3584]{1,0:T(8,128)(2,1)S(1)} %get-tuple-element.126), channel_id=1, source_target_pairs={{0,4},{1,5},{4,8},{5,9},{8,12},{9,13},{12,14},{13,15},{14,10},{15,... | collective-permute-start | bytes 688136 | tf_op jit(solution)/shard_map/ppermute | solution.py:325

commit v11 on v8

--- a/solution.py
+++ b/solution.py
@@ -40,10 +40,7 @@
 def step_perm(chips, by_high, by_low):
     high, low = gather_steps(chips)
     return [
-        (
-            2 * (h * low + l) + core,
-            2 * ((h - by_high) % high * low + (l - by_low) % low) + core,
-        )
+        (2 * (h * low + l) + core, 2 * ((h ^ by_high) * low + (l ^ by_low)) + core)
         for h in range(high)
         for l in range(low)
         for core in range(2)
@@ -59,8 +56,8 @@
             for side in (0, chips):
                 for d in part:
                     other = ring[(p + d) % chips]
-                    by_high = (other // low - chip // low) % high
-                    by_low = (other % low - chip % low) % low
+                    by_high = (other // low) ^ (chip // low)
+                    by_low = (other % low) ^ (chip % low)
                     table[chip].append(side + by_low * high + by_high)
     return table
 
@@ -176,22 +173,29 @@
     )(scalars, *pooled, *resid_blocks, w_out, gain, w_router_t)
 
 
-def lengths_kernel(owner, lengths, device, out):
-    rows = out.shape[0]
-    for j in range(rows):
-        length = lengths[owner[device[0] * rows + j]]
-        out[j : j + 1, :] = jnp.full((1, LANES), length, jnp.int32)
-
-
-def lengths_of(owner, lengths, device_index, rows):
+def lookup_kernel(owner, lengths, table, device, row_lengths, scalars):
+    for j in range(row_lengths.shape[0]):
+        row_lengths[j] = lengths[owner[device[0] * row_lengths.shape[0] + j]]
+    for j in range(scalars.shape[0]):
+        scalars[j] = table[device[0] * scalars.shape[0] + j]
+
+
+LONG = dict(flops=10**10, bytes_accessed=10**8, transcendentals=0)
+
+
+def lookup(owner, lengths, table, device_index, rows):
     scalar = pl.BlockSpec(memory_space=pltpu.SMEM)
     return pl.pallas_call(
-        lengths_kernel,
-        in_specs=[scalar] * 3,
-        out_shape=jax.ShapeDtypeStruct((rows, LANES), jnp.int32),
-        cost_estimate=pl.CostEstimate(flops=10**10, bytes_accessed=10**8, transcendentals=0),
-        name="lengths",
-    )(owner, lengths, device_index[None])
+        lookup_kernel,
+        in_specs=[scalar] * 4,
+        out_specs=[scalar] * 2,
+        out_shape=[
+            jax.ShapeDtypeStruct((rows,), jnp.int32),
+            jax.ShapeDtypeStruct(table.shape[1:], jnp.int32),
+        ],
+        cost_estimate=pl.CostEstimate(**LONG),
+        name="lookup",
+    )(owner, lengths, table.reshape(-1), device_index[None])
 
 
 def attention_kernel(context, latent, q, cache, fresh, lengths, routes, packet, keys_a, keys_b, total):
@@ -213,7 +217,10 @@
     row = lax.broadcasted_iota(jnp.int32, (rows, keys), 0)
     key = lax.broadcasted_iota(jnp.int32, (rows, keys), 1)
     place = key // rows
-    seen = (place < lengths[:, :1]) & (place < context)
+    length = jnp.zeros((rows, keys), jnp.int32)
+    for j in range(rows):
+        length = jnp.where(row == j, lengths[j], length)
+    seen = (place < length) & (place < context)
     seen = seen | ((place >= context) & (place <= context + step))
     bias = jnp.where(seen & (key % rows == row), 0.0, -1e30)
     summed = jnp.zeros((rows, keys), jnp.float32)
@@ -258,12 +265,11 @@
     def whole(a):
         return pl.BlockSpec(a.shape, lambda i: (0, 0), pipeline_mode=pl.Buffered(1))
 
-    heads = q_abs.shape[2] // kv_width
     return pl.pallas_call(
         lambda *refs: attention_kernel(context, latent, *refs),
         grid=(steps,),
         in_specs=[pl.BlockSpec((1, rows, q_abs.shape[2]), lambda i: (i, 0, 0))]
-        + [whole(a) for a in (cache, fresh, lengths, routes)],
+        + [whole(cache), whole(fresh), pl.BlockSpec(memory_space=pltpu.SMEM), whole(routes)],
         out_shape=jax.ShapeDtypeStruct((steps * rows, latent + LANES), jnp.bfloat16),
         out_specs=pl.BlockSpec((steps * rows, latent + LANES), lambda i: (0, 0)),
         scratch_shapes=[
@@ -274,11 +280,7 @@
         compiler_params=pltpu.CompilerParams(
             dimension_semantics=("arbitrary",), vmem_limit_bytes=(10 << 20) + 10240 * keys
         ),
-        cost_estimate=pl.CostEstimate(
-            flops=2 * steps * rows * heads * wide * keys,
-            bytes_accessed=2 * q_abs.size,
-            transcendentals=steps * rows * heads * keys,
-        ),
+        cost_estimate=pl.CostEstimate(**LONG),
         name="attention",
     )(q_abs, cache, fresh, lengths, routes)
 
@@ -306,7 +308,6 @@
     sharers = devices // experts_all
     chips = devices // 2
     half = chips // 2
-    cut = rows // 2
     far, near = distances(chips)
     hold = lax.optimization_barrier
     sibling = sibling_perm(chips)
@@ -315,6 +316,10 @@
         return lax.ppermute(a, "expert", perm)
 
     to_right, to_left = shift_perm(chips, 1), shift_perm(chips, -1)
+    parted = lambda hops: [
+        shift_perm(chips, hops - 2 * hops * core)[2 * p + core] for p in range(chips) for core in range(2)
+    ]
+    first_core = device_index % 2 == 0
 
     def around(to_the_right, to_the_left):
         return send(to_the_right, to_right), send(to_the_left, to_left)
@@ -330,25 +335,18 @@
     mine = resid.reshape(rows, width)
     held, sib = {0: mine}, {}
     held[-1], held[1] = around(mine, mine)
-    row_lengths = lengths_of(owner, lengths, device_index, row_count)
-    row_lengths, held[-1], held[1] = hold((row_lengths, held[-1], held[1]))
+    table = [
+        [device // sharers] + places
+        for chip, places in enumerate(gathered_place(chips))
+        for device in (2 * chip, 2 * chip + 1)
+    ]
+    row_lengths, scalars = lookup(
+        owner, lengths, jnp.array(table, jnp.int32), device_index, row_count
+    )
+    row_lengths, scalars, held = hold((row_lengths, scalars, held))
     held[-2], held[2] = around(held[-1], held[1])
     sib[0] = send(mine, sibling)
     gain = norm_gain[None, :]
-    scalars = jnp.array(
-        [
-            [device // sharers] + places
-            for chip, places in enumerate(gathered_place(chips))
-            for device in (2 * chip, 2 * chip + 1)
-        ],
-        jnp.int32,
-    )[device_index]
-    owned, row_lengths, gain, scalars, held[-2], held[2], sib[0] = hold(
-        (owned, row_lengths, gain, scalars, held[-2], held[2], sib[0])
-    )
-    for t in range(3, half):
-        held[-t], held[t] = around(held[1 - t], held[t - 1])
-    sib[-1], sib[1] = send(held[-1], sibling), send(held[1], sibling)
     packet = attention(
         q_abs,
         owned.reshape(-1, kv_width),
@@ -358,22 +356,26 @@
         devices * positions,
         w_out.shape[0],
     )
-    packet, held, sib = hold((packet, held, sib))
+    packet, gain, held, sib = hold((packet, gain, held, sib))
 
     high, low = gather_steps(chips)
     along = [send(packet, step_perm(chips, i, 0)) for i in range(1, high)]
-    last = around(held[1 - half][:cut], held[half - 1][cut:])
-    for t in range(2, half - 1):
-        sib[-t], sib[t] = send(held[-t], sibling), send(held[t], sibling)
-    along, last, sib = hold((along, last, sib))
+    sib[1], sib[-1] = send(held[1], sibling), send(held[-1], sibling)
+    along, sib = hold((along, sib))
     along = jnp.concatenate([packet] + along, axis=0)
     across = [send(along, step_perm(chips, 0, i)) for i in range(1, low)]
-    held[half] = jnp.concatenate(last, axis=0)
-    for d in (1 - half, half - 1, half):
-        sib[d] = send(held[d], sibling)
-    across, sib = hold((across, sib))
+    sib[2], sib[-2] = send(held[2], sibling), send(held[-2], sibling)
+    along_sib = send(along, sibling)
+    across, along_sib, sib = hold((across, along_sib, sib))
     across = across[0] if low == 2 else jnp.concatenate(across, axis=0)
-    gathered = [along, across, send(along, sibling), send(across, sibling)]
+    gathered = [along, across, along_sib, send(across, sibling)]
+
+    gathered, held = hold((gathered, held))
+    for t in range(3, half):
+        held[-t], held[t] = around(held[1 - t], held[t - 1])
+    held[half] = send(jnp.where(first_core, held[2 - half], held[half - 2]), parted(2))
+    for t in range(3, half - 1):
+        sib[t], sib[-t] = send(held[t], sibling), send(held[-t], sibling)
 
     f32 = jnp.float32
 
@@ -401,22 +403,27 @@
     def both(right, left):
         return around(right.astype(jnp.bfloat16), left.astype(jnp.bfloat16))
 
+    x, scale, weight, hidden = normed(1 + 2 * len(far), near, True, gathered)
+    gated, held = hold((product(x, w_gate), held))
+    for d in far:
+        sib[d] = send(held[d], sibling)
+    act, sib = hold((activate(gated, product(x, w_up), scale, weight), sib))
+    y = product(act, w_down).astype(jnp.bfloat16)
+    gathered, y = hold((gathered, y))
+    y_near, received_near = swap(near, y)
     x, scale, weight = normed(1, far, False, gathered)
-    act = hold(activate(product(x, w_gate), product(x, w_up), scale, weight))
+    gated, y_near, received_near = hold((product(x, w_gate), y_near, received_near))
+    add_up(near, y_near, received_near)
+    act = hold(activate(gated, product(x, w_up), scale, weight))
     y, received = swap(far, product(act, w_down).astype(jnp.bfloat16))
-    y, gathered = hold((y, gathered))
-    x, scale, weight, hidden = normed(1 + 2 * len(far), near, True, gathered)
-    x, y, received = hold((x, y, received))
     add_up(far, y, received)
-    right, left = both(sums[half][:cut], sums[half][cut:])
-    act = activate(product(x, w_gate), product(x, w_up), scale, weight)
-    act, right, left = hold((act, right, left))
-    right = jnp.concatenate([right.astype(f32), jnp.zeros((rows - cut, width), f32)], axis=0)
-    left = jnp.concatenate([jnp.zeros((cut, width), f32), left.astype(f32)], axis=0)
-    right, left = both(sums[half - 1] + right, sums[1 - half] + left)
-    y, received = swap(near, product(act, w_down).astype(jnp.bfloat16))
-    y, received, right, left = hold((y, received, right, left))
-    add_up(near, y, received)
+    onward = hold(send(sums[half].astype(jnp.bfloat16), parted(1))).astype(f32)
+    right, left = hold(
+        both(
+            sums[half - 1] + jnp.where(first_core, onward, 0.0),
+            sums[1 - half] + jnp.where(first_core, 0.0, onward),
+        )
+    )
     for t in range(half - 2, 0, -1):
         right, left = hold(both(sums[t] + right.astype(f32), sums[-t] + left.astype(f32)))
     mixed = hidden + sums[0] + right.astype(f32) + left.astype(f32)

time: 110 us -> 110 us (level)
  starting transfers between devices: 32.3 us -> 29.6 us
  local copies, waits for them, and re-layouts: 4.94 us -> 6.37 us
    ppermute x32 -> x30, waiting for transfers between devices: 40.2 us -> 32 us  [send(): return lax.ppermute(a, 'expert', perm)]
    all_to_all x1, waiting for transfers between devices: 0.01 us -> 8.01 us  [local(): lax.all_to_all(ordered, 'expert', split_axis=0, concat_axis=0, tiled=True)]
    ppermute x32 -> x30, starting transfers between devices: 26 us -> 23.1 us  [send(): return lax.ppermute(a, 'expert', perm)]
    unnamed x34 -> x37, local copies, waits for them, and re-layouts: 2.64 us -> 4.86 us
  transfers between devices with their start and end apart: 33 -> 31, of which waited for: 14 -> 16; matrix products, arithmetic and copies ran while one was open for 8% -> 13% of each run, Pallas kernels for 9% -> 13%
where the time goes in v11:
time: 110 us
  waiting for transfers between devices  40 us (36%)
  starting transfers between devices  29.6 us (27%)
  matrix products  16.8 us (15%)
  Pallas kernels  14.4 us (13%)
  local copies, waits for them, and re-layouts  6.37 us (6%)
  other arithmetic  2.36 us (2%)
    ppermute x30, waiting for transfers between devices, send(): return lax.ppermute(a, 'expert', perm)  32 us
    ppermute x30, starting transfers between devices, send(): return lax.ppermute(a, 'expert', perm)  23.1 us
    dot_general x6, matrix products, product(): return jnp.dot(a, w[0], preferred_element_type=f32)  15.8 us
    pallas_call x2, Pallas kernels, normalize(): pl.pallas_call(lambda *refs: norm_kernel(first, blocks, rows, latent, wid...  8.86 us
    all_to_all x1, waiting for transfers between devices, local(): lax.all_to_all(ordered, 'expert', split_axis=0, concat_axis=0, tiled=True)  8.01 us
    all_to_all x1, starting transfers between devices, local(): lax.all_to_all(ordered, 'expert', split_axis=0, concat_axis=0, tiled=True)  6.49 us
    unnamed x37, local copies, waits for them, and re-layouts  4.86 us
    pallas_call x1, Pallas kernels, attention(): pl.pallas_call(lambda *refs: attention_kernel(context, latent, *refs), gr...  4.19 us
  transfers between devices with their start and end apart: 31, of which 16 were waited for; matrix products, arithmetic and copies ran while one was open for 13% of the time, Pallas kernels for 13%

profile of v11, /device:TPU:0, one launch (start us, length us, event | category | flops | bytes accessed | tf_op | source)
XLA Modules:
  0.0 110.0 jit_solution(9600117557649425101)
XLA Ops:
  0.0 3.0 %collective-permute-start = (bf16[32,3584]{1,0:T(8,128)(2,1)}, bf16[32,3584]{1,0:T(8,128)(2,1)S(1)}, u32[]{:S(2)}, u32[]{:S(2)}) collective-permute-start(bf16[32,3584]{1,0:T(8,128)(2,1)} %bitcast.49), channel_id=1, source_target_pairs={{0,4},{1,5},{4,8},{5,9},{8,12},{9,13},{12,14},{13,15},{14,10},{15,... | collective-permute-start | bytes 688136 | tf_op jit(solution)/shard_map/ppermute | solution.py:316
  3.0 1.0 fusion.24
  4.2 0.8 copy.19
  5.0 6.5 %all-to-all-start = ((bf16[16,2,8,576]{3,2,1,0:T(8,128)(2,1)}), bf16[16,2,8,576]{3,2,1,0:T(8,128)(2,1)S(1)}, u32[]{:S(2)}, u32[]{:S(2)}) async-start(bf16[16,2,8,576]{3,2,1,0:T(8,128)(2,1)} %copy.19), calls=%async_computation | async-start | bytes 655360 | tf_op jit(solution)/shard_map/all_to_all | solution.py:333
  11.5 1.4 %lookup.1 = (s32[8]{0:T(128)}, s32[17]{0:T(128)}) custom-call(s32[128]{0:T(128)} %owner.1, s32[128]{0:T(128)} %lengths.1, s32[272]{0:T(512)} %constant.36.table, s32[1]{0:T(128)} %bitcast.device), custom_call_target="tpu_custom_call" | custom-call | flops 10000000000 | bytes 100000000 | tf_op jit(solution)/shard_map/lookup/pallas_call | solution.py:188
  13.0 2.0 %collective-permute-start.2 = (bf16[32,3584]{1,0:T(8,128)(2,1)S(1)}, bf16[32,3584]{1,0:T(8,128)(2,1)S(1)}, u32[]{:S(2)}, u32[]{:S(2)}) collective-permute-start(bf16[32,3584]{1,0:T(8,128)(2,1)S(1)} %collective-permute-done.refs_7_), channel_id=1, source_target_pairs={{0,4},{1,5},{4,8},{5,9},{8,12},{9,13},{12,14},{13,15},{14,10},{15,... | collective-permute-start | bytes 688136 | tf_op jit(solution)/shard_map/ppermute | solution.py:316
  15.0 8.0 %all-to-all-done = bf16[16,2,8,576]{3,2,1,0:T(8,128)(2,1)S(1)} async-done(((bf16[16,2,8,576]{3,2,1,0:T(8,128)(2,1)}), bf16[16,2,8,576]{3,2,1,0:T(8,128)(2,1)S(1)}, u32[]{:S(2)}, u32[]{:S(2)}) %all-to-all-start) | async-done | bytes 294944 | tf_op jit(solution)/shard_map/all_to_all | solution.py:333
  23.1 1.7 %copy-done.6 = bf16[4,8,36864]{2,1,0:T(8,128)(2,1)S(1)} copy-done((bf16[4,8,36864]{2,1,0:T(8,128)(2,1)S(1)}, bf16[4,8,36864]{2,1,0:T(8,128)(2,1)}, u32[]{:S(2)}) %copy-start.6) | copy-done | bytes 2359320
  24.7 0.6 copy-done.9
  25.4 4.2 %attention.1 = bf16[32,640]{1,0:T(8,128)(2,1)S(1)} custom-call(bf16[4,8,36864]{2,1,0:T(8,128)(2,1)S(1)} %copy-done.6, bf16[256,576]{1,0:T(8,128)(2,1)S(1)} %bitcast.48, bf16[32,576]{1,0:T(8,128)(2,1)S(1)} %bitcast.53, s32[8]{0:T(128)S(1)} %copy-done.9, s32[32,8]{1,0:T(8,128)S(1)} %bitcast.54), custom_call_target="tpu_custom_call" | custom-call | flops 10000000000 | bytes 100000000 | tf_op jit(solution)/shard_map/attention/pallas_call | solution.py:268
  29.7 0.5 collective-permute-start.9
  30.2 0.4 collective-permute-start.5
  30.5 0.9 collective-permute-start.6
  31.4 3.1 %collective-permute-start.7 = (bf16[32,640]{1,0:T(8,128)(2,1)S(1)}, bf16[32,640]{1,0:T(8,128)(2,1)S(1)}, u32[]{:S(2)}, u32[]{:S(2)}) collective-permute-start(bf16[32,640]{1,0:T(8,128)(2,1)S(1)} %attention.1), channel_id=1, source_target_pairs={{0,12},{1,13},{2,14},{3,15},{4,8},{5,9},{6,10},{7,11},{8,4},{9,5},... | collective-permute-start | bytes 122888 | tf_op jit(solution)/shard_map/ppermute | solution.py:316
  34.6 2.9 %collective-permute-done.6 = bf16[32,640]{1,0:T(8,128)(2,1)S(1)} collective-permute-done((bf16[32,640]{1,0:T(8,128)(2,1)S(1)}, bf16[32,640]{1,0:T(8,128)(2,1)S(1)}, u32[]{:S(2)}, u32[]{:S(2)}) %collective-permute-start.6) | collective-permute-done | bytes 40992 | tf_op jit(solution)/shard_map/ppermute | solution.py:316
  37.6 1.3 %collective-permute-start.10 = (bf16[128,640]{1,0:T(8,128)(2,1)S(1)}, bf16[128,640]{1,0:T(8,128)(2,1)S(1)}, u32[]{:S(2)}, u32[]{:S(2)}) collective-permute-start(bf16[128,640]{1,0:T(8,128)(2,1)S(1)} %constant_dynamic-update-slice_fusion.refs_1_), channel_id=1, source_target_pairs={{0,2},{1,3},{2,0},{3,1},{4,6},{5,7},{6,4},{7,5},{8,10},{9,11},{10,... | collective-permute-start | bytes 491528 | tf_op jit(solution)/shard_map/ppermute | solution.py:316
  39.0 5.3 %collective-permute-done.10.refs_2_ = bf16[128,640]{1,0:T(8,128)(2,1)S(1)} collective-permute-done((bf16[128,640]{1,0:T(8,128)(2,1)S(1)}, bf16[128,640]{1,0:T(8,128)(2,1)S(1)}, u32[]{:S(2)}, u32[]{:S(2)}) %collective-permute-start.10) | collective-permute-done | bytes 163872 | tf_op jit(solution)/shard_map/ppermute | solution.py:316
  44.3 1.4 %collective-permute-done.14.refs_4_ = bf16[128,640]{1,0:T(8,128)(2,1)S(1)} collective-permute-done((bf16[128,640]{1,0:T(8,128)(2,1)S(1)}, bf16[128,640]{1,0:T(8,128)(2,1)S(1)}, u32[]{:S(2)}, u32[]{:S(2)}) %collective-permute-start.14) | collective-permute-done | bytes 163872 | tf_op jit(solution)/shard_map/ppermute | solution.py:316
  45.7 2.0 %collective-permute-start.16 = (bf16[32,3584]{1,0:T(8,128)(2,1)S(1)}, bf16[32,3584]{1,0:T(8,128)(2,1)S(1)}, u32[]{:S(2)}, u32[]{:S(2)}) collective-permute-start(bf16[32,3584]{1,0:T(8,128)(2,1)S(1)} %collective-permute-done.3.refs_8_), channel_id=1, source_target_pairs={{0,2},{1,3},{4,0},{5,1},{8,4},{9,5},{12,8},{13,9},{14,12},{15,13},... | collective-permute-start | bytes 688136 | tf_op jit(solution)/shard_map/ppermute | solution.py:316
  47.8 2.0 %copy-done.1 = bf16[512,3584]{1,0:T(8,128)(2,1)S(1)} copy-done((bf16[512,3584]{1,0:T(8,128)(2,1)S(1)}, bf16[512,3584]{1,0:T(8,128)(2,1)}, u32[]{:S(2)}) %copy-start.1) | copy-done | bytes 3670040
  49.9 4.9 %normalize.2 = (bf16[320,3584]{1,0:T(8,128)(2,1)S(1)}, f32[320,128]{1,0:T(8,128)S(1)}, f32[320,128]{1,0:T(8,128)S(1)}, f32[32,3584]{1,0:T(8,128)S(1)}) custom-call(s32[17]{0:T(128)S(1)} %copy-done.5, bf16[128,640]{1,0:T(8,128)(2,1)S(1)} %constant_dynamic-update-slice_fusion.refs_1_, bf16[128,640]{1,0:T(8,128)(2,1)S(1)} %collective-permute-done.10.refs_2_, ...), custom_call_target="tpu_custom_call" | custom-call | flops 1174405120 | bytes 8257536 | tf_op jit(solution)/shard_map/normalize/pallas_call | solution.py:143
  54.9 5.8 %fusion.18 = f32[320,1024]{1,0:T(8,128)S(1)} fusion(bf16[320,3584]{1,0:T(8,128)(2,1)S(1)} %get-tuple-element.109, bf16[1,3584,1024]{2,1,0:T(8,128)(2,1)} %param.25, f32[320]{0:T(512)S(1)} %get-tuple-element.144), kind=kOutput, calls=%fused_computation.14 | convolution fusion | flops 2349137920 | bytes 10945792 | tf_op jit(solution)/shard_map/dot_general | solution.py:387
  60.8 2.5 %fusion.10 = f32[320,1024]{1,0:T(8,128)S(1)} fusion(bf16[320,3584]{1,0:T(8,128)(2,1)S(1)} %get-tuple-element.109, bf16[1,3584,1024]{2,1,0:T(8,128)(2,1)S(1)} %bitcast.57), kind=kOutput, calls=%fused_computation.10 | convolution fusion | flops 2348810240 | bytes 10944512 | tf_op jit(solution)/shard_map/dot_general | solution.py:387
  63.4 0.5 collective-permute-start.19
  64.0 0.6 multiply_convert_fusion
  65.5 2.5 %fusion.12 = bf16[320,3584]{1,0:T(8,128)(2,1)S(1)} fusion(bf16[320,1024]{1,0:T(8,128)(2,1)S(1)} %multiply_convert_fusion, bf16[1,1024,3584]{2,1,0:T(8,128)(2,1)S(1)} %bitcast.61), kind=kOutput, calls=%fused_computation.12 | convolution fusion | flops 2349957120 | bytes 10289152 | tf_op jit(solution)/shard_map/dot_general | solution.py:387
  68.4 4.0 %normalize.3 = (bf16[192,3584]{1,0:T(8,128)(2,1)S(1)}, f32[192,128]{1,0:T(8,128)S(1)}, f32[192,128]{1,0:T(8,128)S(1)}) custom-call(s32[17]{0:T(128)S(1)} %copy-done.5, bf16[128,640]{1,0:T(8,128)(2,1)S(1)} %constant_dynamic-update-slice_fusion.refs_1_, bf16[128,640]{1,0:T(8,128)(2,1)S(1)} %collective-permute-done.10.refs_2_, ...), custom_call_target="tpu_custom_call" | custom-call | flops 704643072 | bytes 6422528 | tf_op jit(solution)/shard_map/normalize/pallas_call | solution.py:143
  72.7 1.7 %fusion.8 = f32[192,1024]{1,0:T(8,128)S(1)} fusion(bf16[192,3584]{1,0:T(8,128)(2,1)S(1)} %get-tuple-element.124, bf16[1,3584,1024]{2,1,0:T(8,128)(2,1)S(1)} %bitcast.57), kind=kOutput, calls=%fused_computation.8 | convolution fusion | flops 1409286144 | bytes 9502720 | tf_op jit(solution)/shard_map/dot_general | solution.py:387
  74.4 0.4 slice-done.3
  74.9 1.7 %fusion.21 = f32[192,1024]{1,0:T(8,128)S(1)} fusion(bf16[192,3584]{1,0:T(8,128)(2,1)S(1)} %get-tuple-element.124, bf16[1,3584,1024]{2,1,0:T(8,128)(2,1)S(1)} %bitcast.59, f32[192]{0:T(256)S(1)} %slice_reduce_fusion.3), kind=kOutput, calls=%fused_computation.16 | convolution fusion | flops 1409482752 | bytes 9503488 | tf_op jit(solution)/shard_map/dot_general | solution.py:387
  76.6 0.4 multiply_convert_fusion.1
  76.9 1.6 %fusion.15 = bf16[192,3584]{1,0:T(8,128)(2,1)S(1)} fusion(bf16[192,1024]{1,0:T(8,128)(2,1)S(1)} %multiply_convert_fusion.1, bf16[1,1024,3584]{2,1,0:T(8,128)(2,1)S(1)} %bitcast.61), kind=kOutput, calls=%fused_computation.13 | convolution fusion | flops 1409974272 | bytes 9109504 | tf_op jit(solution)/shard_map/dot_general | solution.py:387
  78.6 0.4 collective-permute-start.22
  79.0 1.8 %collective-permute-done.22 = bf16[96,3584]{1,0:T(8,128)(2,1)S(1)} collective-permute-done((bf16[96,3584]{1,0:T(8,128)(2,1)S(1)}, bf16[96,3584]{1,0:T(8,128)(2,1)S(1)}, u32[]{:S(2)}, u32[]{:S(2)}) %collective-permute-start.22) | collective-permute-done | bytes 688160 | tf_op jit(solution)/shard_map/ppermute | solution.py:316
  80.9 2.1 %collective-permute-start.23 = (bf16[32,3584]{1,0:T(8,128)(2,1)S(1)}, bf16[32,3584]{1,0:T(8,128)(2,1)S(1)}, u32[]{:S(2)}, u32[]{:S(2)}) collective-permute-start(bf16[32,3584]{1,0:T(8,128)(2,1)S(1)} %add_convert_fusion.5), channel_id=1, source_target_pairs={{0,4},{1,3},{4,8},{5,1},{8,12},{9,5},{12,14},{13,9},{14,10},{15,13... | collective-permute-start | bytes 688136 | tf_op jit(solution)/shard_map/ppermute | solution.py:316
  82.9 4.0 %collective-permute-done.23 = bf16[32,3584]{1,0:T(8,128)(2,1)S(1)} collective-permute-done((bf16[32,3584]{1,0:T(8,128)(2,1)S(1)}, bf16[32,3584]{1,0:T(8,128)(2,1)S(1)}, u32[]{:S(2)}, u32[]{:S(2)}) %collective-permute-start.23) | collective-permute-done | bytes 229408 | tf_op jit(solution)/shard_map/ppermute | solution.py:316
  87.1 2.1 %collective-permute-start.24 = (bf16[32,3584]{1,0:T(8,128)(2,1)S(1)}, bf16[32,3584]{1,0:T(8,128)(2,1)S(1)}, u32[]{:S(2)}, u32[]{:S(2)}) collective-permute-start(bf16[32,3584]{1,0:T(8,128)(2,1)S(1)} %get-tuple-element.142), channel_id=1, source_target_pairs={{0,4},{1,5},{4,8},{5,9},{8,12},{9,13},{12,14},{13,15},{14,10},{15,... | collective-permute-start | bytes 688136 | tf_op jit(solution)/shard_map/ppermute | solution.py:316
  89.2 5.3 %collective-permute-done.24 = bf16[32,3584]{1,0:T(8,128)(2,1)S(1)} collective-permute-done((bf16[32,3584]{1,0:T(8,128)(2,1)S(1)}, bf16[32,3584]{1,0:T(8,128)(2,1)S(1)}, u32[]{:S(2)}, u32[]{:S(2)}) %collective-permute-start.24) | collective-permute-done | bytes 229408 | tf_op jit(solution)/shard_map/ppermute | solution.py:316
  94.5 1.5 %collective-permute-done.25 = bf16[32,3584]{1,0:T(8,128)(2,1)S(1)} collective-permute-done((bf16[32,3584]{1,0:T(8,128)(2,1)S(1)}, bf16[32,3584]{1,0:T(8,128)(2,1)S(1)}, u32[]{:S(2)}, u32[]{:S(2)}) %collective-permute-start.25) | collective-permute-done | bytes 229408 | tf_op jit(solution)/shard_map/ppermute | solution.py:316
  96.1 0.4 collective-permute-start.26
  96.5 1.7 %collective-permute-start.27 = (bf16[32,3584]{1,0:T(8,128)(2,1)S(1)}, bf16[32,3584]{1,0:T(8,128)(2,1)S(1)}, u32[]{:S(2)}, u32[]{:S(2)}) collective-permute-start(bf16[32,3584]{1,0:T(8,128)(2,1)S(1)} %get-tuple-element.139), channel_id=1, source_target_pairs={{0,2},{1,3},{4,0},{5,1},{8,4},{9,5},{12,8},{13,9},{14,12},{15,13},... | collective-permute-start | bytes 688136 | tf_op jit(solution)/shard_map/ppermute | solution.py:316
  98.2 4.0 %collective-permute-done.26 = bf16[32,3584]{1,0:T(8,128)(2,1)S(1)} collective-permute-done((bf16[32,3584]{1,0:T(8,128)(2,1)S(1)}, bf16[32,3584]{1,0:T(8,128)(2,1)S(1)}, u32[]{:S(2)}, u32[]{:S(2)}) %collective-permute-start.26) | collective-permute-done | bytes 229408 | tf_op jit(solution)/shard_map/ppermute | solution.py:316
  102.2 0.4 collective-permute-done.27
  102.7 0.4 collective-permute-start.28
  103.1 1.7 %collective-permute-start.29 = (bf16[32,3584]{1,0:T(8,128)(2,1)S(1)}, bf16[32,3584]{1,0:T(8,128)(2,1)S(1)}, u32[]{:S(2)}, u32[]{:S(2)}) collective-permute-start(bf16[32,3584]{1,0:T(8,128)(2,1)S(1)} %get-tuple-element.137), channel_id=1, source_target_pairs={{0,2},{1,3},{4,0},{5,1},{8,4},{9,5},{12,8},{13,9},{14,12},{15,13},... | collective-permute-start | bytes 688136 | tf_op jit(solution)/shard_map/ppermute | solution.py:316
  104.8 4.0 %collective-permute-done.28 = bf16[32,3584]{1,0:T(8,128)(2,1)S(1)} collective-permute-done((bf16[32,3584]{1,0:T(8,128)(2,1)S(1)}, bf16[32,3584]{1,0:T(8,128)(2,1)S(1)}, u32[]{:S(2)}, u32[]{:S(2)}) %collective-permute-start.28) | collective-permute-done | bytes 229408 | tf_op jit(solution)/shard_map/ppermute | solution.py:316
  108.8 0.3 collective-permute-done.29
  109.1 0.8 fusion.29
  (82 shorter events, 3.4 us)
Async XLA Ops:
  0.0 3.0 %copy-start = (bf16[128,2,576]{0,2,1:T(8,128)(2,1)S(1)}, bf16[128,2,576]{0,2,1:T(8,128)(2,1)}, u32[]{:S(2)}) copy-start(bf16[128,2,576]{0,2,1:T(8,128)(2,1)} %param.16) | copy-start | bytes 884740
  0.0 12.9 %collective-permute-start = (bf16[32,3584]{1,0:T(8,128)(2,1)}, bf16[32,3584]{1,0:T(8,128)(2,1)S(1)}, u32[]{:S(2)}, u32[]{:S(2)}) collective-permute-start(bf16[32,3584]{1,0:T(8,128)(2,1)} %bitcast.49), channel_id=1, source_target_pairs={{0,4},{1,5},{4,8},{5,9},{8,12},{9,13},{12,14},{13,15},{14,10},{15,... | collective-permute-start | bytes 688136 | tf_op jit(solution)/shard_map/ppermute | solution.py:316
  3.0 9.9 %collective-permute-start.1 = (bf16[32,3584]{1,0:T(8,128)(2,1)}, bf16[32,3584]{1,0:T(8,128)(2,1)S(1)}, u32[]{:S(2)}, u32[]{:S(2)}) collective-permute-start(bf16[32,3584]{1,0:T(8,128)(2,1)} %bitcast.50), channel_id=1, source_target_pairs={{0,2},{1,3},{4,0},{5,1},{8,4},{9,5},{12,8},{13,9},{14,12},{15,13},... | collective-permute-start | bytes 688136 | tf_op jit(solution)/shard_map/ppermute | solution.py:316
  3.0 26.5 %collective-permute-start.4 = (bf16[32,3584]{1,0:T(8,128)(2,1)}, bf16[32,3584]{1,0:T(8,128)(2,1)S(1)}, u32[]{:S(2)}, u32[]{:S(2)}) collective-permute-start(bf16[32,3584]{1,0:T(8,128)(2,1)} %bitcast.51), channel_id=1, source_target_pairs={{0,1},{1,0},{2,3},{3,2},{4,5},{5,4},{6,7},{7,6},{8,9},{9,8},{10,11... | collective-permute-start | bytes 688136 | tf_op jit(solution)/shard_map/ppermute | solution.py:316
  5.0 18.1 %all-to-all-start = ((bf16[16,2,8,576]{3,2,1,0:T(8,128)(2,1)}), bf16[16,2,8,576]{3,2,1,0:T(8,128)(2,1)S(1)}, u32[]{:S(2)}, u32[]{:S(2)}) async-start(bf16[16,2,8,576]{3,2,1,0:T(8,128)(2,1)} %copy.19), calls=%async_computation | async-start | bytes 655360 | tf_op jit(solution)/shard_map/all_to_all | solution.py:333
  11.5 1.4 %copy-start.10 = (bf16[3584]{0:T(1024)(128)(2,1)S(1)}, bf16[3584]{0:T(1024)(128)(2,1)}, u32[]{:S(2)}) copy-start(bf16[3584]{0:T(1024)(128)(2,1)} %param.22) | copy-start | bytes 21508
  11.5 11.6 %copy-start.7 = (bf16[4,8,576]{2,1,0:T(8,128)(2,1)S(1)}, bf16[4,8,576]{2,1,0:T(8,128)(2,1)}, u32[]{:S(2)}) copy-start(bf16[4,8,576]{2,1,0:T(8,128)(2,1)} %param.15) | copy-start | bytes 110596
  11.5 11.6 %copy-start.8 = (s32[4,8,8]{2,1,0:T(8,128)S(1)}, s32[4,8,8]{2,1,0:T(8,128)}, u32[]{:S(2)}) copy-start(s32[4,8,8]{2,1,0:T(8,128)} %param.20) | copy-start | bytes 3076
  13.0 16.6 %collective-permute-start.2 = (bf16[32,3584]{1,0:T(8,128)(2,1)S(1)}, bf16[32,3584]{1,0:T(8,128)(2,1)S(1)}, u32[]{:S(2)}, u32[]{:S(2)}) collective-permute-start(bf16[32,3584]{1,0:T(8,128)(2,1)S(1)} %collective-permute-done.refs_7_), channel_id=1, source_target_pairs={{0,4},{1,5},{4,8},{5,9},{8,12},{9,13},{12,14},{13,15},{14,10},{15,... | collective-permute-start | bytes 688136 | tf_op jit(solution)/shard_map/ppermute | solution.py:316
  14.9 14.6 %collective-permute-start.3 = (bf16[32,3584]{1,0:T(8,128)(2,1)S(1)}, bf16[32,3584]{1,0:T(8,128)(2,1)S(1)}, u32[]{:S(2)}, u32[]{:S(2)}) collective-permute-start(bf16[32,3584]{1,0:T(8,128)(2,1)S(1)} %collective-permute-done.1.refs_6_), channel_id=1, source_target_pairs={{0,2},{1,3},{4,0},{5,1},{8,4},{9,5},{12,8},{13,9},{14,12},{15,13},... | collective-permute-start | bytes 688136 | tf_op jit(solution)/shard_map/ppermute | solution.py:316
  23.1 1.7 %copy-start.6 = (bf16[4,8,36864]{2,1,0:T(8,128)(2,1)S(1)}, bf16[4,8,36864]{2,1,0:T(8,128)(2,1)}, u32[]{:S(2)}) copy-start(bf16[4,8,36864]{2,1,0:T(8,128)(2,1)} %refs_0_.1) | copy-start | bytes 7077892
  24.7 0.6 copy-start.9
  25.3 22.5 %copy-start.3 = (bf16[3584,16]{0,1:T(8,128)(2,1)S(1)}, bf16[3584,16]{0,1:T(8,128)(2,1)}, u32[]{:S(2)}) copy-start(bf16[3584,16]{0,1:T(8,128)(2,1)} %param.23) | copy-start | bytes 344068
  25.4 22.5 %copy-start.4 = (bf16[4,8,3584]{2,1,0:T(8,128)(2,1)S(1)}, bf16[4,8,3584]{2,1,0:T(8,128)(2,1)}, u32[]{:S(2)}) copy-start(bf16[4,8,3584]{2,1,0:T(8,128)(2,1)} %param.19) | copy-start | bytes 688132
  25.4 22.5 %copy-start.5 = (s32[17]{0:T(128)S(1)}, s32[17]{0:T(128)}, u32[]{:S(2)}) copy-start(s32[17]{0:T(128)} %get-tuple-element.73.refs_0_) | copy-start | bytes 208
  29.6 8.0 %collective-permute-start.8 = (bf16[32,3584]{1,0:T(8,128)(2,1)S(1)}, bf16[32,3584]{1,0:T(8,128)(2,1)S(1)}, u32[]{:S(2)}, u32[]{:S(2)}) collective-permute-start(bf16[32,3584]{1,0:T(8,128)(2,1)S(1)} %collective-permute-done.refs_7_), channel_id=1, source_target_pairs={{0,1},{1,0},{2,3},{3,2},{4,5},{5,4},{6,7},{7,6},{8,9},{9,8},{10,11... | collective-permute-start | bytes 688136 | tf_op jit(solution)/shard_map/ppermute | solution.py:316
  29.7 7.9 %collective-permute-start.9 = (bf16[32,3584]{1,0:T(8,128)(2,1)S(1)}, bf16[32,3584]{1,0:T(8,128)(2,1)S(1)}, u32[]{:S(2)}, u32[]{:S(2)}) collective-permute-start(bf16[32,3584]{1,0:T(8,128)(2,1)S(1)} %collective-permute-done.1.refs_6_), channel_id=1, source_target_pairs={{0,1},{1,0},{2,3},{3,2},{4,5},{5,4},{6,7},{7,6},{8,9},{9,8},{10,11... | collective-permute-start | bytes 688136 | tf_op jit(solution)/shard_map/ppermute | solution.py:316
  30.2 4.4 %collective-permute-start.5 = (bf16[32,640]{1,0:T(8,128)(2,1)S(1)}, bf16[32,640]{1,0:T(8,128)(2,1)S(1)}, u32[]{:S(2)}, u32[]{:S(2)}) collective-permute-start(bf16[32,640]{1,0:T(8,128)(2,1)S(1)} %attention.1), channel_id=1, source_target_pairs={{0,4},{1,5},{2,6},{3,7},{4,0},{5,1},{6,2},{7,3},{8,12},{9,13},{10,... | collective-permute-start | bytes 122888 | tf_op jit(solution)/shard_map/ppermute | solution.py:316
  30.5 7.0 %collective-permute-start.6 = (bf16[32,640]{1,0:T(8,128)(2,1)S(1)}, bf16[32,640]{1,0:T(8,128)(2,1)S(1)}, u32[]{:S(2)}, u32[]{:S(2)}) collective-permute-start(bf16[32,640]{1,0:T(8,128)(2,1)S(1)} %attention.1), channel_id=1, source_target_pairs={{0,8},{1,9},{2,10},{3,11},{4,12},{5,13},{6,14},{7,15},{8,0},{9,1},... | collective-permute-start | bytes 122888 | tf_op jit(solution)/shard_map/ppermute | solution.py:316
  31.4 6.1 %collective-permute-start.7 = (bf16[32,640]{1,0:T(8,128)(2,1)S(1)}, bf16[32,640]{1,0:T(8,128)(2,1)S(1)}, u32[]{:S(2)}, u32[]{:S(2)}) collective-permute-start(bf16[32,640]{1,0:T(8,128)(2,1)S(1)} %attention.1), channel_id=1, source_target_pairs={{0,12},{1,13},{2,14},{3,15},{4,8},{5,9},{6,10},{7,11},{8,4},{9,5},... | collective-permute-start | bytes 122888 | tf_op jit(solution)/shard_map/ppermute | solution.py:316
  34.5 4.3 %collective-permute-start.12 = (bf16[32,3584]{1,0:T(8,128)(2,1)S(1)}, bf16[32,3584]{1,0:T(8,128)(2,1)S(1)}, u32[]{:S(2)}, u32[]{:S(2)}) collective-permute-start(bf16[32,3584]{1,0:T(8,128)(2,1)S(1)} %collective-permute-done.2.refs_9_), channel_id=1, source_target_pairs={{0,1},{1,0},{2,3},{3,2},{4,5},{5,4},{6,7},{7,6},{8,9},{9,8},{10,11... | collective-permute-start | bytes 688136 | tf_op jit(solution)/shard_map/ppermute | solution.py:316
  37.5 1.5 %collective-permute-start.13 = (bf16[32,3584]{1,0:T(8,128)(2,1)S(1)}, bf16[32,3584]{1,0:T(8,128)(2,1)S(1)}, u32[]{:S(2)}, u32[]{:S(2)}) collective-permute-start(bf16[32,3584]{1,0:T(8,128)(2,1)S(1)} %collective-permute-done.3.refs_8_), channel_id=1, source_target_pairs={{0,1},{1,0},{2,3},{3,2},{4,5},{5,4},{6,7},{7,6},{8,9},{9,8},{10,11... | collective-permute-start | bytes 688136 | tf_op jit(solution)/shard_map/ppermute | solution.py:316
  37.6 6.7 %collective-permute-start.10 = (bf16[128,640]{1,0:T(8,128)(2,1)S(1)}, bf16[128,640]{1,0:T(8,128)(2,1)S(1)}, u32[]{:S(2)}, u32[]{:S(2)}) collective-permute-start(bf16[128,640]{1,0:T(8,128)(2,1)S(1)} %constant_dynamic-update-slice_fusion.refs_1_), channel_id=1, source_target_pairs={{0,2},{1,3},{2,0},{3,1},{4,6},{5,7},{6,4},{7,5},{8,10},{9,11},{10,... | collective-permute-start | bytes 491528 | tf_op jit(solution)/shard_map/ppermute | solution.py:316
  38.9 5.4 %collective-permute-start.11 = (bf16[128,640]{1,0:T(8,128)(2,1)S(1)}, bf16[128,640]{1,0:T(8,128)(2,1)S(1)}, u32[]{:S(2)}, u32[]{:S(2)}) collective-permute-start(bf16[128,640]{1,0:T(8,128)(2,1)S(1)} %constant_dynamic-update-slice_fusion.refs_1_), channel_id=1, source_target_pairs={{0,1},{1,0},{2,3},{3,2},{4,5},{5,4},{6,7},{7,6},{8,9},{9,8},{10,11... | collective-permute-start | bytes 491528 | tf_op jit(solution)/shard_map/ppermute | solution.py:316
  44.3 1.4 %collective-permute-start.14 = (bf16[128,640]{1,0:T(8,128)(2,1)S(1)}, bf16[128,640]{1,0:T(8,128)(2,1)S(1)}, u32[]{:S(2)}, u32[]{:S(2)}) collective-permute-start(bf16[128,640]{1,0:T(8,128)(2,1)S(1)} %collective-permute-done.10.refs_2_), channel_id=1, source_target_pairs={{0,1},{1,0},{2,3},{3,2},{4,5},{5,4},{6,7},{7,6},{8,9},{9,8},{10,11... | collective-permute-start | bytes 491528 | tf_op jit(solution)/shard_map/ppermute | solution.py:316
  45.7 17.6 %collective-permute-start.15 = (bf16[32,3584]{1,0:T(8,128)(2,1)S(1)}, bf16[32,3584]{1,0:T(8,128)(2,1)S(1)}, u32[]{:S(2)}, u32[]{:S(2)}) collective-permute-start(bf16[32,3584]{1,0:T(8,128)(2,1)S(1)} %collective-permute-done.2.refs_9_), channel_id=1, source_target_pairs={{0,4},{1,5},{4,8},{5,9},{8,12},{9,13},{12,14},{13,15},{14,10},{15,... | collective-permute-start | bytes 688136 | tf_op jit(solution)/shard_map/ppermute | solution.py:316
  45.7 17.6 %collective-permute-start.16 = (bf16[32,3584]{1,0:T(8,128)(2,1)S(1)}, bf16[32,3584]{1,0:T(8,128)(2,1)S(1)}, u32[]{:S(2)}, u32[]{:S(2)}) collective-permute-start(bf16[32,3584]{1,0:T(8,128)(2,1)S(1)} %collective-permute-done.3.refs_8_), channel_id=1, source_target_pairs={{0,2},{1,3},{4,0},{5,1},{8,4},{9,5},{12,8},{13,9},{14,12},{15,13},... | collective-permute-start | bytes 688136 | tf_op jit(solution)/shard_map/ppermute | solution.py:316
  47.7 15.6 %collective-permute-start.17 = (bf16[32,3584]{1,0:T(8,128)(2,1)S(1)}, bf16[32,3584]{1,0:T(8,128)(2,1)S(1)}, u32[]{:S(2)}, u32[]{:S(2)}) collective-permute-start(bf16[32,3584]{1,0:T(8,128)(2,1)S(1)} %broadcast_select_fusion), channel_id=1, source_target_pairs={{0,8},{1,7},{4,12},{5,3},{8,14},{9,1},{12,10},{13,5},{14,6},{15,9}... | collective-permute-start | bytes 688136 | tf_op jit(solution)/shard_map/ppermute | solution.py:316
  47.8 2.0 %copy-start.1 = (bf16[512,3584]{1,0:T(8,128)(2,1)S(1)}, bf16[512,3584]{1,0:T(8,128)(2,1)}, u32[]{:S(2)}) copy-start(bf16[512,3584]{1,0:T(8,128)(2,1)} %refs_11_.1) | copy-start | bytes 11010052
  49.9 10.8 %slice-start = ((s8[7340032]{0:T(1024)(128)(4,1)}), s8[4194304]{0:T(1024)(128)(4,1)S(1)}, s32[]{:S(2)}) async-start(s8[7340032]{0:T(1024)(128)(4,1)} %bitcast.56), calls=%async_computation.1 | async-start | bytes 8388608
  54.9 5.8 %slice-start.1 = ((s8[7340032]{0:T(1024)(128)(4,1)}), s8[3145728]{0:T(1024)(128)(4,1)S(1)}, s32[]{:S(2)}) async-start(s8[7340032]{0:T(1024)(128)(4,1)} %bitcast.56), calls=%async_computation.2 | async-start | bytes 6291456
  54.9 10.6 %slice-start.4 = ((s8[7340032]{0:T(1024)(128)(4,1)}), s8[4194304]{0:T(1024)(128)(4,1)S(1)}, s32[]{:S(2)}) async-start(s8[7340032]{0:T(1024)(128)(4,1)} %bitcast.60), calls=%async_computation.5 | async-start | bytes 8388608
  60.7 4.8 %slice-start.5 = ((s8[7340032]{0:T(1024)(128)(4,1)}), s8[3145728]{0:T(1024)(128)(4,1)S(1)}, s32[]{:S(2)}) async-start(s8[7340032]{0:T(1024)(128)(4,1)} %bitcast.60), calls=%async_computation.6 | async-start | bytes 6291456
  63.3 1.6 %collective-permute-start.18 = (bf16[32,3584]{1,0:T(8,128)(2,1)S(1)}, bf16[32,3584]{1,0:T(8,128)(2,1)S(1)}, u32[]{:S(2)}, u32[]{:S(2)}) collective-permute-start(bf16[32,3584]{1,0:T(8,128)(2,1)S(1)} %collective-permute-done.15.refs_7_), channel_id=1, source_target_pairs={{0,1},{1,0},{2,3},{3,2},{4,5},{5,4},{6,7},{7,6},{8,9},{9,8},{10,11... | collective-permute-start | bytes 688136 | tf_op jit(solution)/shard_map/ppermute | solution.py:316
  63.4 1.8 %collective-permute-start.19 = (bf16[32,3584]{1,0:T(8,128)(2,1)S(1)}, bf16[32,3584]{1,0:T(8,128)(2,1)S(1)}, u32[]{:S(2)}, u32[]{:S(2)}) collective-permute-start(bf16[32,3584]{1,0:T(8,128)(2,1)S(1)} %collective-permute-done.16.refs_6_), channel_id=1, source_target_pairs={{0,1},{1,0},{2,3},{3,2},{4,5},{5,4},{6,7},{7,6},{8,9},{9,8},{10,11... | collective-permute-start | bytes 688136 | tf_op jit(solution)/shard_map/ppermute | solution.py:316
  63.9 1.6 %collective-permute-start.20 = (bf16[32,3584]{1,0:T(8,128)(2,1)S(1)}, bf16[32,3584]{1,0:T(8,128)(2,1)S(1)}, u32[]{:S(2)}, u32[]{:S(2)}) collective-permute-start(bf16[32,3584]{1,0:T(8,128)(2,1)S(1)} %collective-permute-done.17.refs_5_), channel_id=1, source_target_pairs={{0,1},{1,0},{2,3},{3,2},{4,5},{5,4},{6,7},{7,6},{8,9},{9,8},{10,11... | collective-permute-start | bytes 688136 | tf_op jit(solution)/shard_map/ppermute | solution.py:316
  65.5 2.9 %copy-start.2 = (bf16[512,3584]{1,0:T(8,128)(2,1)S(1)}, bf16[512,3584]{1,0:T(8,128)(2,1)}, u32[]{:S(2)}) copy-start(bf16[512,3584]{1,0:T(8,128)(2,1)} %refs_11_.1) | copy-start | bytes 11010052
  68.2 8.4 %collective-permute-start.21 = (bf16[160,3584]{1,0:T(8,128)(2,1)S(1)}, bf16[160,3584]{1,0:T(8,128)(2,1)S(1)}, u32[]{:S(2)}, u32[]{:S(2)}) collective-permute-start(bf16[160,3584]{1,0:T(8,128)(2,1)S(1)} %slice.68), channel_id=1, source_target_pairs={{0,1},{1,0},{2,3},{3,2},{4,5},{5,4},{6,7},{7,6},{8,9},{9,8},{10,11... | collective-permute-start | bytes 3440648 | tf_op jit(solution)/shard_map/ppermute | solution.py:316
  68.4 6.0 %slice-start.2 = ((s8[7340032]{0:T(1024)(128)(4,1)}), s8[3145728]{0:T(1024)(128)(4,1)S(1)}, s32[]{:S(2)}) async-start(s8[7340032]{0:T(1024)(128)(4,1)} %bitcast.58), calls=%async_computation.3 | async-start | bytes 6291456
  72.7 2.2 %slice-start.3 = ((s8[7340032]{0:T(1024)(128)(4,1)}), s8[4194304]{0:T(1024)(128)(4,1)S(1)}, s32[]{:S(2)}) async-start(s8[7340032]{0:T(1024)(128)(4,1)} %bitcast.58), calls=%async_computation.4 | async-start | bytes 8388608
  78.6 2.2 %collective-permute-start.22 = (bf16[96,3584]{1,0:T(8,128)(2,1)S(1)}, bf16[96,3584]{1,0:T(8,128)(2,1)S(1)}, u32[]{:S(2)}, u32[]{:S(2)}) collective-permute-start(bf16[96,3584]{1,0:T(8,128)(2,1)S(1)} %slice.89), channel_id=1, source_target_pairs={{0,1},{1,0},{2,3},{3,2},{4,5},{5,4},{6,7},{7,6},{8,9},{9,8},{10,11... | collective-permute-start | bytes 2064392 | tf_op jit(solution)/shard_map/ppermute | solution.py:316
  80.9 6.1 %collective-permute-start.23 = (bf16[32,3584]{1,0:T(8,128)(2,1)S(1)}, bf16[32,3584]{1,0:T(8,128)(2,1)S(1)}, u32[]{:S(2)}, u32[]{:S(2)}) collective-permute-start(bf16[32,3584]{1,0:T(8,128)(2,1)S(1)} %add_convert_fusion.5), channel_id=1, source_target_pairs={{0,4},{1,3},{4,8},{5,1},{8,12},{9,5},{12,14},{13,9},{14,10},{15,13... | collective-permute-start | bytes 688136 | tf_op jit(solution)/shard_map/ppermute | solution.py:316
  87.1 7.3 %collective-permute-start.24 = (bf16[32,3584]{1,0:T(8,128)(2,1)S(1)}, bf16[32,3584]{1,0:T(8,128)(2,1)S(1)}, u32[]{:S(2)}, u32[]{:S(2)}) collective-permute-start(bf16[32,3584]{1,0:T(8,128)(2,1)S(1)} %get-tuple-element.142), channel_id=1, source_target_pairs={{0,4},{1,5},{4,8},{5,9},{8,12},{9,13},{12,14},{13,15},{14,10},{15,... | collective-permute-start | bytes 688136 | tf_op jit(solution)/shard_map/ppermute | solution.py:316
  89.2 6.7 %collective-permute-start.25 = (bf16[32,3584]{1,0:T(8,128)(2,1)S(1)}, bf16[32,3584]{1,0:T(8,128)(2,1)S(1)}, u32[]{:S(2)}, u32[]{:S(2)}) collective-permute-start(bf16[32,3584]{1,0:T(8,128)(2,1)S(1)} %get-tuple-element.141), channel_id=1, source_target_pairs={{0,2},{1,3},{4,0},{5,1},{8,4},{9,5},{12,8},{13,9},{14,12},{15,13},... | collective-permute-start | bytes 688136 | tf_op jit(solution)/shard_map/ppermute | solution.py:316
  96.1 6.1 %collective-permute-start.26 = (bf16[32,3584]{1,0:T(8,128)(2,1)S(1)}, bf16[32,3584]{1,0:T(8,128)(2,1)S(1)}, u32[]{:S(2)}, u32[]{:S(2)}) collective-permute-start(bf16[32,3584]{1,0:T(8,128)(2,1)S(1)} %get-tuple-element.140), channel_id=1, source_target_pairs={{0,4},{1,5},{4,8},{5,9},{8,12},{9,13},{12,14},{13,15},{14,10},{15,... | collective-permute-start | bytes 688136 | tf_op jit(solution)/shard_map/ppermute | solution.py:316
  96.5 6.0 %collective-permute-start.27 = (bf16[32,3584]{1,0:T(8,128)(2,1)S(1)}, bf16[32,3584]{1,0:T(8,128)(2,1)S(1)}, u32[]{:S(2)}, u32[]{:S(2)}) collective-permute-start(bf16[32,3584]{1,0:T(8,128)(2,1)S(1)} %get-tuple-element.139), channel_id=1, source_target_pairs={{0,2},{1,3},{4,0},{5,1},{8,4},{9,5},{12,8},{13,9},{14,12},{15,13},... | collective-permute-start | bytes 688136 | tf_op jit(solution)/shard_map/ppermute | solution.py:316
  102.7 6.1 %collective-permute-start.28 = (bf16[32,3584]{1,0:T(8,128)(2,1)S(1)}, bf16[32,3584]{1,0:T(8,128)(2,1)S(1)}, u32[]{:S(2)}, u32[]{:S(2)}) collective-permute-start(bf16[32,3584]{1,0:T(8,128)(2,1)S(1)} %get-tuple-element.138), channel_id=1, source_target_pairs={{0,4},{1,5},{4,8},{5,9},{8,12},{9,13},{12,14},{13,15},{14,10},{15,... | collective-permute-start | bytes 688136 | tf_op jit(solution)/shard_map/ppermute | solution.py:316
  103.1 6.0 %collective-permute-start.29 = (bf16[32,3584]{1,0:T(8,128)(2,1)S(1)}, bf16[32,3584]{1,0:T(8,128)(2,1)S(1)}, u32[]{:S(2)}, u32[]{:S(2)}) collective-permute-start(bf16[32,3584]{1,0:T(8,128)(2,1)S(1)} %get-tuple-element.137), channel_id=1, source_target_pairs={{0,2},{1,3},{4,0},{5,1},{8,4},{9,5},{12,8},{13,9},{14,12},{15,13},... | collective-permute-start | bytes 688136 | tf_op jit(solution)/shard_map/ppermute | solution.py:316

commit v12 on v11

--- a/solution.py
+++ b/solution.py
@@ -180,7 +180,7 @@
         scalars[j] = table[device[0] * scalars.shape[0] + j]
 
 
-LONG = dict(flops=10**10, bytes_accessed=10**8, transcendentals=0)
+LONG = dict(flops=10**9, bytes_accessed=3 * 10**7, transcendentals=0)
 
 
 def lookup(owner, lengths, table, device_index, rows):
@@ -280,7 +280,9 @@
         compiler_params=pltpu.CompilerParams(
             dimension_semantics=("arbitrary",), vmem_limit_bytes=(10 << 20) + 10240 * keys
         ),
-        cost_estimate=pl.CostEstimate(**LONG),
+        cost_estimate=pl.CostEstimate(
+            flops=2 * q_abs.size * keys, bytes_accessed=2 * q_abs.size, transcendentals=0
+        ),
         name="attention",
     )(q_abs, cache, fresh, lengths, routes)
 
@@ -364,18 +366,16 @@
     along, sib = hold((along, sib))
     along = jnp.concatenate([packet] + along, axis=0)
     across = [send(along, step_perm(chips, 0, i)) for i in range(1, low)]
-    sib[2], sib[-2] = send(held[2], sibling), send(held[-2], sibling)
-    along_sib = send(along, sibling)
-    across, along_sib, sib = hold((across, along_sib, sib))
-    across = across[0] if low == 2 else jnp.concatenate(across, axis=0)
-    gathered = [along, across, along_sib, send(across, sibling)]
-
-    gathered, held = hold((gathered, held))
     for t in range(3, half):
         held[-t], held[t] = around(held[1 - t], held[t - 1])
+    sib[2], sib[-2] = send(held[2], sibling), send(held[-2], sibling)
+    across, held, sib = hold((across, held, sib))
+    across = across[0] if low == 2 else jnp.concatenate(across, axis=0)
+    gathered = [along, across, send(along, sibling), send(across, sibling)]
+    for t in range(3, half):
+        sib[t], sib[-t] = send(held[t], sibling), send(held[-t], sibling)
+    gathered, sib = hold((gathered, sib))
     held[half] = send(jnp.where(first_core, held[2 - half], held[half - 2]), parted(2))
-    for t in range(3, half - 1):
-        sib[t], sib[-t] = send(held[t], sibling), send(held[-t], sibling)
 
     f32 = jnp.float32
 
@@ -403,27 +403,25 @@
     def both(right, left):
         return around(right.astype(jnp.bfloat16), left.astype(jnp.bfloat16))
 
-    x, scale, weight, hidden = normed(1 + 2 * len(far), near, True, gathered)
-    gated, held = hold((product(x, w_gate), held))
-    for d in far:
-        sib[d] = send(held[d], sibling)
-    act, sib = hold((activate(gated, product(x, w_up), scale, weight), sib))
-    y = product(act, w_down).astype(jnp.bfloat16)
-    gathered, y = hold((gathered, y))
-    y_near, received_near = swap(near, y)
+    x_near, scale_near, weight_near, hidden = normed(1 + 2 * len(far), near, True, gathered)
+    x_near, held[half] = hold((x_near, held[half]))
+    sib[half] = send(held[half], sibling)
     x, scale, weight = normed(1, far, False, gathered)
-    gated, y_near, received_near = hold((product(x, w_gate), y_near, received_near))
-    add_up(near, y_near, received_near)
-    act = hold(activate(gated, product(x, w_up), scale, weight))
+    act = hold(activate(product(x, w_gate), product(x, w_up), scale, weight))
     y, received = swap(far, product(act, w_down).astype(jnp.bfloat16))
+    gated, y, received = hold((product(x_near, w_gate), y, received))
     add_up(far, y, received)
-    onward = hold(send(sums[half].astype(jnp.bfloat16), parted(1))).astype(f32)
-    right, left = hold(
-        both(
-            sums[half - 1] + jnp.where(first_core, onward, 0.0),
-            sums[1 - half] + jnp.where(first_core, 0.0, onward),
-        )
+    onward = send(sums[half].astype(jnp.bfloat16), parted(1))
+    act = activate(gated, product(x_near, w_up), scale_near, weight_near)
+    act, onward = hold((act, onward))
+    onward = onward.astype(f32)
+    right, left = both(
+        sums[half - 1] + jnp.where(first_core, onward, 0.0),
+        sums[1 - half] + jnp.where(first_core, 0.0, onward),
     )
+    y, received = swap(near, product(act, w_down).astype(jnp.bfloat16))
+    y, received, right, left = hold((y, received, right, left))
+    add_up(near, y, received)
     for t in range(half - 2, 0, -1):
         right, left = hold(both(sums[t] + right.astype(f32), sums[-t] + left.astype(f32)))
     mixed = hidden + sums[0] + right.astype(f32) + left.astype(f32)

time: 110 us -> 117 us (1.064)
  local copies, waits for them, and re-layouts: 6.37 us -> 11.7 us
  waiting for transfers between devices: 40 us -> 43.6 us
  matrix products: 16.8 us -> 13.8 us
  starting transfers between devices: 29.6 us -> 30.8 us
    ppermute x30, waiting for transfers between devices: 32 us -> 43.6 us  [send(): return lax.ppermute(a, 'expert', perm)]
    all_to_all x1, waiting for transfers between devices: 8.01 us -> 0.01 us  [local(): lax.all_to_all(ordered, 'expert', split_axis=0, concat_axis=0, tiled=True)]
    unnamed x37 -> x41, local copies, waits for them, and re-layouts: 4.86 us -> 8.96 us
    dot_general x6, matrix products: 15.8 us -> 12.9 us  [product(): return jnp.dot(a, w[0], preferred_element_type=f32)]
    broadcast_in_dim x1, local copies, waits for them, and re-layouts: 0.01 us -> 1.3 us  [local(): gain = norm_gain[None, :]]
  transfers between devices with their start and end apart: 31 -> 31, of which waited for: 16 -> 17; matrix products, arithmetic and copies ran while one was open for 13% -> 6% of each run, Pallas kernels for 13% -> 9%
where the time goes in v12:
time: 117 us
  waiting for transfers between devices  43.6 us (37%)
  starting transfers between devices  30.8 us (26%)
  Pallas kernels  14.9 us (13%)
  matrix products  13.8 us (12%)
  local copies, waits for them, and re-layouts  11.7 us (10%)
  other arithmetic  1.42 us (1%)
    ppermute x30, waiting for transfers between devices, send(): return lax.ppermute(a, 'expert', perm)  43.6 us
    ppermute x30, starting transfers between devices, send(): return lax.ppermute(a, 'expert', perm)  23.3 us
    dot_general x6, matrix products, product(): return jnp.dot(a, w[0], preferred_element_type=f32)  12.9 us
    pallas_call x2, Pallas kernels, normalize(): pl.pallas_call(lambda *refs: norm_kernel(first, blocks, rows, latent, wid...  9.45 us
    unnamed x41, local copies, waits for them, and re-layouts  8.96 us
    all_to_all x1, starting transfers between devices, local(): lax.all_to_all(ordered, 'expert', split_axis=0, concat_axis=0, tiled=True)  7.52 us
    pallas_call x1, Pallas kernels, attention(): pl.pallas_call(lambda *refs: attention_kernel(context, latent, *refs), gr...  4.2 us
  transfers between devices with their start and end apart: 31, of which 17 were waited for; matrix products, arithmetic and copies ran while one was open for 6% of the time, Pallas kernels for 9%

profile of v12, /device:TPU:0, one launch (start us, length us, event | category | flops | bytes accessed | tf_op | source)
XLA Modules:
  0.0 116.5 jit_solution(16048464059604398851)
XLA Ops:
  0.0 1.0 copy-done
  1.0 1.0 fusion.27
  2.1 0.7 copy.19
  2.9 7.5 %all-to-all-start = ((bf16[16,2,8,576]{3,2,1,0:T(8,128)(2,1)}), bf16[16,2,8,576]{3,2,1,0:T(8,128)(2,1)S(1)}, u32[]{:S(2)}, u32[]{:S(2)}) async-start(bf16[16,2,8,576]{3,2,1,0:T(8,128)(2,1)} %copy.19), calls=%async_computation | async-start | bytes 655360 | tf_op jit(solution)/shard_map/all_to_all | solution.py:335
  10.4 1.9 %collective-permute-start.1 = (bf16[32,3584]{1,0:T(8,128)(2,1)}, bf16[32,3584]{1,0:T(8,128)(2,1)S(1)}, u32[]{:S(2)}, u32[]{:S(2)}) collective-permute-start(bf16[32,3584]{1,0:T(8,128)(2,1)} %bitcast.1.refs_5_), channel_id=1, source_target_pairs={{0,2},{1,3},{4,0},{5,1},{8,4},{9,5},{12,8},{13,9},{14,12},{15,13},... | collective-permute-start | bytes 688136 | tf_op jit(solution)/shard_map/ppermute | solution.py:318
  12.5 1.3 %lookup.1 = (s32[8]{0:T(128)}, s32[17]{0:T(128)}) custom-call(s32[128]{0:T(128)} %owner.1, s32[128]{0:T(128)} %lengths.1, s32[272]{0:T(512)} %constant.36.table, s32[1]{0:T(128)} %bitcast.device), custom_call_target="tpu_custom_call" | custom-call | flops 1000000000 | bytes 30000000 | tf_op jit(solution)/shard_map/lookup/pallas_call | solution.py:188
  13.8 9.9 %collective-permute-done.1.refs_6_ = bf16[32,3584]{1,0:T(8,128)(2,1)S(1)} collective-permute-done((bf16[32,3584]{1,0:T(8,128)(2,1)}, bf16[32,3584]{1,0:T(8,128)(2,1)S(1)}, u32[]{:S(2)}, u32[]{:S(2)}) %collective-permute-start.1) | collective-permute-done | bytes 229408 | tf_op jit(solution)/shard_map/ppermute | solution.py:318
  23.7 0.7 copy-done.5
  24.4 3.2 %collective-permute-start.2 = (bf16[32,3584]{1,0:T(8,128)(2,1)}, bf16[32,3584]{1,0:T(8,128)(2,1)S(1)}, u32[]{:S(2)}, u32[]{:S(2)}) collective-permute-start(bf16[32,3584]{1,0:T(8,128)(2,1)} %collective-permute-done.refs_7_), channel_id=1, source_target_pairs={{0,4},{1,5},{4,8},{5,9},{8,12},{9,13},{12,14},{13,15},{14,10},{15,... | collective-permute-start | bytes 688136 | tf_op jit(solution)/shard_map/ppermute | solution.py:318
  27.6 1.3 %broadcast_in_dim.15.refs_16_.refs_12_ = bf16[1,3584]{1,0:T(2,128)(2,1)} reshape(bf16[3584]{0:T(1024)(128)(2,1)} %param.22) | data formatting | bytes 14336 | tf_op jit(solution)/shard_map/broadcast_in_dim | solution.py:351
  29.0 0.8 copy-done.9
  29.8 0.7 copy-done.10
  31.2 4.2 %attention.1 = bf16[32,640]{1,0:T(8,128)(2,1)S(1)} custom-call(bf16[4,8,36864]{2,1,0:T(8,128)(2,1)S(1)} %copy-done.3, bf16[256,576]{1,0:T(8,128)(2,1)S(1)} %bitcast.52, bf16[32,576]{1,0:T(8,128)(2,1)S(1)} %bitcast.55, s32[8]{0:T(128)S(1)} %copy-done.13, s32[32,8]{1,0:T(8,128)S(1)} %bitcast.56), custom_call_target="tpu_custom_call" | custom-call | flops 679477248 | bytes 2359296 | tf_op jit(solution)/shard_map/attention/pallas_call | solution.py:268
  36.0 0.9 collective-permute-start.7
  36.8 2.6 %collective-permute-start.6 = (bf16[32,640]{1,0:T(8,128)(2,1)S(1)}, bf16[32,640]{1,0:T(8,128)(2,1)S(1)}, u32[]{:S(2)}, u32[]{:S(2)}) collective-permute-start(bf16[32,640]{1,0:T(8,128)(2,1)S(1)} %attention.1), channel_id=1, source_target_pairs={{0,8},{1,9},{2,10},{3,11},{4,12},{5,13},{6,14},{7,15},{8,0},{9,1},... | collective-permute-start | bytes 122888 | tf_op jit(solution)/shard_map/ppermute | solution.py:318
  39.4 0.9 collective-permute-start.5
  40.3 1.8 %collective-permute-done.7 = bf16[32,640]{1,0:T(8,128)(2,1)S(1)} collective-permute-done((bf16[32,640]{1,0:T(8,128)(2,1)S(1)}, bf16[32,640]{1,0:T(8,128)(2,1)S(1)}, u32[]{:S(2)}, u32[]{:S(2)}) %collective-permute-start.7) | collective-permute-done | bytes 40992 | tf_op jit(solution)/shard_map/ppermute | solution.py:318
  42.2 1.5 %collective-permute-done.6 = bf16[32,640]{1,0:T(8,128)(2,1)S(1)} collective-permute-done((bf16[32,640]{1,0:T(8,128)(2,1)S(1)}, bf16[32,640]{1,0:T(8,128)(2,1)S(1)}, u32[]{:S(2)}, u32[]{:S(2)}) %collective-permute-start.6) | collective-permute-done | bytes 40992 | tf_op jit(solution)/shard_map/ppermute | solution.py:318
  44.0 1.8 %collective-permute-start.12 = (bf16[32,3584]{1,0:T(8,128)(2,1)S(1)}, bf16[32,3584]{1,0:T(8,128)(2,1)S(1)}, u32[]{:S(2)}, u32[]{:S(2)}) collective-permute-start(bf16[32,3584]{1,0:T(8,128)(2,1)S(1)} %collective-permute-done.3.refs_8_), channel_id=1, source_target_pairs={{0,2},{1,3},{4,0},{5,1},{8,4},{9,5},{12,8},{13,9},{14,12},{15,13},... | collective-permute-start | bytes 688136 | tf_op jit(solution)/shard_map/ppermute | solution.py:318
  45.8 0.9 collective-permute-start.10
  46.7 5.5 %collective-permute-done.11.refs_7_ = bf16[32,3584]{1,0:T(8,128)(2,1)S(1)} collective-permute-done((bf16[32,3584]{1,0:T(8,128)(2,1)S(1)}, bf16[32,3584]{1,0:T(8,128)(2,1)S(1)}, u32[]{:S(2)}, u32[]{:S(2)}) %collective-permute-start.11) | collective-permute-done | bytes 229408 | tf_op jit(solution)/shard_map/ppermute | solution.py:318
  52.2 2.6 %collective-permute-done.10.refs_2_ = bf16[128,640]{1,0:T(8,128)(2,1)S(1)} collective-permute-done((bf16[128,640]{1,0:T(8,128)(2,1)S(1)}, bf16[128,640]{1,0:T(8,128)(2,1)S(1)}, u32[]{:S(2)}, u32[]{:S(2)}) %collective-permute-start.10) | collective-permute-done | bytes 163872 | tf_op jit(solution)/shard_map/ppermute | solution.py:318
  55.4 0.8 collective-permute-done.16.refs_4_
  56.8 2.0 %copy-done.1 = bf16[512,3584]{1,0:T(8,128)(2,1)S(1)} copy-done((bf16[512,3584]{1,0:T(8,128)(2,1)S(1)}, bf16[512,3584]{1,0:T(8,128)(2,1)}, u32[]{:S(2)}) %copy-start.1) | copy-done | bytes 3670040
  58.8 0.9 copy-done.7
  59.8 0.7 copy-done.8
  60.5 0.7 copy-done.11
  61.2 5.6 %normalize.2 = (bf16[320,3584]{1,0:T(8,128)(2,1)S(1)}, f32[320,128]{1,0:T(8,128)S(1)}, f32[320,128]{1,0:T(8,128)S(1)}, f32[32,3584]{1,0:T(8,128)S(1)}) custom-call(s32[17]{0:T(128)S(1)} %copy-done.11, bf16[128,640]{1,0:T(8,128)(2,1)S(1)} %constant_dynamic-update-slice_fusion.refs_1_, bf16[128,640]{1,0:T(8,128)(2,1)S(1)} %collective-permute-done.10.refs_2_, ...), custom_call_target="tpu_custom_call" | custom-call | flops 1174405120 | bytes 8257536 | tf_op jit(solution)/shard_map/normalize/pallas_call | solution.py:143
  67.3 1.0 collective-permute-done.20.refs_8_
  68.4 3.8 %normalize.3 = (bf16[192,3584]{1,0:T(8,128)(2,1)S(1)}, f32[192,128]{1,0:T(8,128)S(1)}, f32[192,128]{1,0:T(8,128)S(1)}) custom-call(s32[17]{0:T(128)S(1)} %copy-done.12, bf16[128,640]{1,0:T(8,128)(2,1)S(1)} %constant_dynamic-update-slice_fusion.refs_1_, bf16[128,640]{1,0:T(8,128)(2,1)S(1)} %collective-permute-done.10.refs_2_, ...), custom_call_target="tpu_custom_call" | custom-call | flops 704643072 | bytes 6422528 | tf_op jit(solution)/shard_map/normalize/pallas_call | solution.py:143
  72.4 1.7 %fusion.21 = f32[192,1024]{1,0:T(8,128)S(1)} fusion(bf16[192,3584]{1,0:T(8,128)(2,1)S(1)} %get-tuple-element.121, bf16[1,3584,1024]{2,1,0:T(8,128)(2,1)S(1)} %copy-done.14, f32[192]{0:T(256)S(1)} %get-tuple-element.148), kind=kOutput, calls=%fused_computation.16 | convolution fusion | flops 1409482752 | bytes 9503488 | tf_op jit(solution)/shard_map/dot_general | solution.py:387
  74.3 1.8 %multiply_convert_fusion.1 = bf16[192,1024]{1,0:T(8,128)(2,1)S(1)} fusion(f32[192,1024]{1,0:T(8,128)S(1)} %fusion.21, f32[192]{0:T(256)S(1)} %get-tuple-element.147, f32[192]{0:T(256)S(1)} %get-tuple-element.148, bf16[192,3584]{1,0:T(8,128)(2,1)S(1)} %get-tuple-element.121, bf16[1,3584,1024]{2,1,0:T(8,128)(2,1)S(1)} %bitcast.59), kind=kOutput, calls=%fused_computation.20 | convolution fusion | flops 1410859008 | bytes 9897472 | tf_op jit(solution)/shard_map/dot_general | solution.py:387
  76.6 1.6 %fusion.15 = bf16[192,3584]{1,0:T(8,128)(2,1)S(1)} fusion(bf16[192,1024]{1,0:T(8,128)(2,1)S(1)} %multiply_convert_fusion.1, bf16[1,1024,3584]{2,1,0:T(8,128)(2,1)S(1)} %bitcast.61), kind=kOutput, calls=%fused_computation.13 | convolution fusion | flops 1409974272 | bytes 9109504 | tf_op jit(solution)/shard_map/dot_general | solution.py:387
  78.6 2.5 %fusion.10 = f32[320,1024]{1,0:T(8,128)S(1)} fusion(bf16[320,3584]{1,0:T(8,128)(2,1)S(1)} %get-tuple-element.117, bf16[1,3584,1024]{2,1,0:T(8,128)(2,1)S(1)} %copy-done.14), kind=kOutput, calls=%fused_computation.10 | convolution fusion | flops 2348810240 | bytes 10944512 | tf_op jit(solution)/shard_map/dot_general | solution.py:387
  81.2 2.7 %collective-permute-start.22 = (bf16[32,3584]{1,0:T(8,128)(2,1)S(1)}, bf16[32,3584]{1,0:T(8,128)(2,1)S(1)}, u32[]{:S(2)}, u32[]{:S(2)}) collective-permute-start(bf16[32,3584]{1,0:T(8,128)(2,1)S(1)} %add_convert_fusion.5), channel_id=1, source_target_pairs={{0,4},{1,3},{4,8},{5,1},{8,12},{9,5},{12,14},{13,9},{14,10},{15,13... | collective-permute-start | bytes 688136 | tf_op jit(solution)/shard_map/ppermute | solution.py:318
  83.9 2.7 %multiply_convert_fusion = bf16[320,1024]{1,0:T(8,128)(2,1)S(1)} fusion(f32[320,1024]{1,0:T(8,128)S(1)} %fusion.10, f32[320]{0:T(512)S(1)} %get-tuple-element.145, f32[320]{0:T(512)S(1)} %get-tuple-element.146, bf16[320,3584]{1,0:T(8,128)(2,1)S(1)} %get-tuple-element.117, bf16[1,3584,1024]{2,1,0:T(8,128)(2,1)S(1)} %bitcast.59), kind=kOutput, calls=%fused_computation.15 | convolution fusion | flops 2351759360 | bytes 11602432 | tf_op jit(solution)/shard_map/dot_general | solution.py:387
  86.6 1.3 %collective-permute-done.22 = bf16[32,3584]{1,0:T(8,128)(2,1)S(1)} collective-permute-done((bf16[32,3584]{1,0:T(8,128)(2,1)S(1)}, bf16[32,3584]{1,0:T(8,128)(2,1)S(1)}, u32[]{:S(2)}, u32[]{:S(2)}) %collective-permute-start.22) | collective-permute-done | bytes 229408 | tf_op jit(solution)/shard_map/ppermute | solution.py:318
  87.9 2.5 %fusion.12 = bf16[320,3584]{1,0:T(8,128)(2,1)S(1)} fusion(bf16[320,1024]{1,0:T(8,128)(2,1)S(1)} %multiply_convert_fusion, bf16[1,1024,3584]{2,1,0:T(8,128)(2,1)S(1)} %bitcast.61), kind=kOutput, calls=%fused_computation.12 | convolution fusion | flops 2349957120 | bytes 10289152 | tf_op jit(solution)/shard_map/dot_general | solution.py:387
  90.8 2.1 %collective-permute-start.25 = (bf16[32,3584]{1,0:T(8,128)(2,1)S(1)}, bf16[32,3584]{1,0:T(8,128)(2,1)S(1)}, u32[]{:S(2)}, u32[]{:S(2)}) collective-permute-start(bf16[32,3584]{1,0:T(8,128)(2,1)S(1)} %get-tuple-element.143), channel_id=1, source_target_pairs={{0,2},{1,3},{4,0},{5,1},{8,4},{9,5},{12,8},{13,9},{14,12},{15,13},... | collective-permute-start | bytes 688136 | tf_op jit(solution)/shard_map/ppermute | solution.py:318
  93.0 6.2 %collective-permute-done.25 = bf16[32,3584]{1,0:T(8,128)(2,1)S(1)} collective-permute-done((bf16[32,3584]{1,0:T(8,128)(2,1)S(1)}, bf16[32,3584]{1,0:T(8,128)(2,1)S(1)}, u32[]{:S(2)}, u32[]{:S(2)}) %collective-permute-start.25) | collective-permute-done | bytes 229408 | tf_op jit(solution)/shard_map/ppermute | solution.py:318
  99.2 1.5 %collective-permute-done.24 = bf16[32,3584]{1,0:T(8,128)(2,1)S(1)} collective-permute-done((bf16[32,3584]{1,0:T(8,128)(2,1)S(1)}, bf16[32,3584]{1,0:T(8,128)(2,1)S(1)}, u32[]{:S(2)}, u32[]{:S(2)}) %collective-permute-start.24) | collective-permute-done | bytes 229408 | tf_op jit(solution)/shard_map/ppermute | solution.py:318
  101.2 1.7 %collective-permute-start.26 = (bf16[32,3584]{1,0:T(8,128)(2,1)S(1)}, bf16[32,3584]{1,0:T(8,128)(2,1)S(1)}, u32[]{:S(2)}, u32[]{:S(2)}) collective-permute-start(bf16[32,3584]{1,0:T(8,128)(2,1)S(1)} %get-tuple-element.142), channel_id=1, source_target_pairs={{0,4},{1,5},{4,8},{5,9},{8,12},{9,13},{12,14},{13,15},{14,10},{15,... | collective-permute-start | bytes 688136 | tf_op jit(solution)/shard_map/ppermute | solution.py:318
  102.9 4.9 %collective-permute-done.27 = bf16[32,3584]{1,0:T(8,128)(2,1)S(1)} collective-permute-done((bf16[32,3584]{1,0:T(8,128)(2,1)S(1)}, bf16[32,3584]{1,0:T(8,128)(2,1)S(1)}, u32[]{:S(2)}, u32[]{:S(2)}) %collective-permute-start.27) | collective-permute-done | bytes 229408 | tf_op jit(solution)/shard_map/ppermute | solution.py:318
  108.3 1.4 %collective-permute-start.29 = (bf16[32,3584]{1,0:T(8,128)(2,1)S(1)}, bf16[32,3584]{1,0:T(8,128)(2,1)S(1)}, u32[]{:S(2)}, u32[]{:S(2)}) collective-permute-start(bf16[32,3584]{1,0:T(8,128)(2,1)S(1)} %get-tuple-element.139), channel_id=1, source_target_pairs={{0,2},{1,3},{4,0},{5,1},{8,4},{9,5},{12,8},{13,9},{14,12},{15,13},... | collective-permute-start | bytes 688136 | tf_op jit(solution)/shard_map/ppermute | solution.py:318
  109.7 0.7 collective-permute-start.28
  110.4 4.0 %collective-permute-done.29 = bf16[32,3584]{1,0:T(8,128)(2,1)S(1)} collective-permute-done((bf16[32,3584]{1,0:T(8,128)(2,1)S(1)}, bf16[32,3584]{1,0:T(8,128)(2,1)S(1)}, u32[]{:S(2)}, u32[]{:S(2)}) %collective-permute-start.29) | collective-permute-done | bytes 229408 | tf_op jit(solution)/shard_map/ppermute | solution.py:318
  114.4 1.3 %collective-permute-done.28 = bf16[32,3584]{1,0:T(8,128)(2,1)S(1)} collective-permute-done((bf16[32,3584]{1,0:T(8,128)(2,1)S(1)}, bf16[32,3584]{1,0:T(8,128)(2,1)S(1)}, u32[]{:S(2)}, u32[]{:S(2)}) %collective-permute-start.28) | collective-permute-done | bytes 229408 | tf_op jit(solution)/shard_map/ppermute | solution.py:318
  115.7 0.8 fusion.36
  (82 shorter events, 6.6 us)
Async XLA Ops:
  0.0 1.0 copy-start
  2.9 26.1 %copy-start.3 = (bf16[4,8,36864]{2,1,0:T(8,128)(2,1)S(1)}, bf16[4,8,36864]{2,1,0:T(8,128)(2,1)}, u32[]{:S(2)}) copy-start(bf16[4,8,36864]{2,1,0:T(8,128)(2,1)} %refs_0_.1) | copy-start | bytes 7077892
  2.9 26.1 %all-to-all-start = ((bf16[16,2,8,576]{3,2,1,0:T(8,128)(2,1)}), bf16[16,2,8,576]{3,2,1,0:T(8,128)(2,1)S(1)}, u32[]{:S(2)}, u32[]{:S(2)}) async-start(bf16[16,2,8,576]{3,2,1,0:T(8,128)(2,1)} %copy.19), calls=%async_computation | async-start | bytes 655360 | tf_op jit(solution)/shard_map/all_to_all | solution.py:335
  10.4 13.3 %collective-permute-start.1 = (bf16[32,3584]{1,0:T(8,128)(2,1)}, bf16[32,3584]{1,0:T(8,128)(2,1)S(1)}, u32[]{:S(2)}, u32[]{:S(2)}) collective-permute-start(bf16[32,3584]{1,0:T(8,128)(2,1)} %bitcast.1.refs_5_), channel_id=1, source_target_pairs={{0,2},{1,3},{4,0},{5,1},{8,4},{9,5},{12,8},{13,9},{14,12},{15,13},... | collective-permute-start | bytes 688136 | tf_op jit(solution)/shard_map/ppermute | solution.py:318
  12.3 11.4 %collective-permute-start = (bf16[32,3584]{1,0:T(8,128)(2,1)}, bf16[32,3584]{1,0:T(8,128)(2,1)}, u32[]{:S(2)}, u32[]{:S(2)}) collective-permute-start(bf16[32,3584]{1,0:T(8,128)(2,1)} %bitcast.1.refs_5_), channel_id=1, source_target_pairs={{0,4},{1,5},{4,8},{5,9},{8,12},{9,13},{12,14},{13,15},{14,10},{15,... | collective-permute-start | bytes 688136 | tf_op jit(solution)/shard_map/ppermute | solution.py:318
  12.5 22.8 %collective-permute-start.4 = (bf16[32,3584]{1,0:T(8,128)(2,1)}, bf16[32,3584]{1,0:T(8,128)(2,1)}, u32[]{:S(2)}, u32[]{:S(2)}) collective-permute-start(bf16[32,3584]{1,0:T(8,128)(2,1)} %bitcast.1.refs_5_), channel_id=1, source_target_pairs={{0,1},{1,0},{2,3},{3,2},{4,5},{5,4},{6,7},{7,6},{8,9},{9,8},{10,11... | collective-permute-start | bytes 688136 | tf_op jit(solution)/shard_map/ppermute | solution.py:318
  13.8 43.0 %copy-start.4 = (bf16[3584,16]{0,1:T(8,128)(2,1)S(1)}, bf16[3584,16]{0,1:T(8,128)(2,1)}, u32[]{:S(2)}) copy-start(bf16[3584,16]{0,1:T(8,128)(2,1)} %param.23) | copy-start | bytes 344068
  23.7 0.7 copy-start.5
  24.4 10.9 %collective-permute-start.2 = (bf16[32,3584]{1,0:T(8,128)(2,1)}, bf16[32,3584]{1,0:T(8,128)(2,1)S(1)}, u32[]{:S(2)}, u32[]{:S(2)}) collective-permute-start(bf16[32,3584]{1,0:T(8,128)(2,1)} %collective-permute-done.refs_7_), channel_id=1, source_target_pairs={{0,4},{1,5},{4,8},{5,9},{8,12},{9,13},{12,14},{13,15},{14,10},{15,... | collective-permute-start | bytes 688136 | tf_op jit(solution)/shard_map/ppermute | solution.py:318
  27.6 7.7 %collective-permute-start.3 = (bf16[32,3584]{1,0:T(8,128)(2,1)}, bf16[32,3584]{1,0:T(8,128)(2,1)S(1)}, u32[]{:S(2)}, u32[]{:S(2)}) collective-permute-start(bf16[32,3584]{1,0:T(8,128)(2,1)} %copy-done.5), channel_id=1, source_target_pairs={{0,2},{1,3},{4,0},{5,1},{8,4},{9,5},{12,8},{13,9},{14,12},{15,13},... | collective-permute-start | bytes 688136 | tf_op jit(solution)/shard_map/ppermute | solution.py:318
  28.9 6.5 %copy-start.6 = (bf16[32,3584]{1,0:T(8,128)(2,1)S(1)}, bf16[32,3584]{1,0:T(8,128)(2,1)}, u32[]{:S(2)}) copy-start(bf16[32,3584]{1,0:T(8,128)(2,1)} %copy-done.5) | copy-start | bytes 688132
  28.9 0.8 copy-start.9
  29.8 0.7 copy-start.10
  35.4 8.6 %collective-permute-start.8 = (bf16[32,3584]{1,0:T(8,128)(2,1)}, bf16[32,3584]{1,0:T(8,128)(2,1)S(1)}, u32[]{:S(2)}, u32[]{:S(2)}) collective-permute-start(bf16[32,3584]{1,0:T(8,128)(2,1)} %collective-permute-done.refs_7_), channel_id=1, source_target_pairs={{0,1},{1,0},{2,3},{3,2},{4,5},{5,4},{6,7},{7,6},{8,9},{9,8},{10,11... | collective-permute-start | bytes 688136 | tf_op jit(solution)/shard_map/ppermute | solution.py:318
  35.5 10.3 %collective-permute-start.9 = (bf16[32,3584]{1,0:T(8,128)(2,1)S(1)}, bf16[32,3584]{1,0:T(8,128)(2,1)S(1)}, u32[]{:S(2)}, u32[]{:S(2)}) collective-permute-start(bf16[32,3584]{1,0:T(8,128)(2,1)S(1)} %copy-done.6), channel_id=1, source_target_pairs={{0,1},{1,0},{2,3},{3,2},{4,5},{5,4},{6,7},{7,6},{8,9},{9,8},{10,11... | collective-permute-start | bytes 688136 | tf_op jit(solution)/shard_map/ppermute | solution.py:318
  36.0 6.2 %collective-permute-start.7 = (bf16[32,640]{1,0:T(8,128)(2,1)S(1)}, bf16[32,640]{1,0:T(8,128)(2,1)S(1)}, u32[]{:S(2)}, u32[]{:S(2)}) collective-permute-start(bf16[32,640]{1,0:T(8,128)(2,1)S(1)} %attention.1), channel_id=1, source_target_pairs={{0,12},{1,13},{2,14},{3,15},{4,8},{5,9},{6,10},{7,11},{8,4},{9,5},... | collective-permute-start | bytes 122888 | tf_op jit(solution)/shard_map/ppermute | solution.py:318
  36.8 6.8 %collective-permute-start.6 = (bf16[32,640]{1,0:T(8,128)(2,1)S(1)}, bf16[32,640]{1,0:T(8,128)(2,1)S(1)}, u32[]{:S(2)}, u32[]{:S(2)}) collective-permute-start(bf16[32,640]{1,0:T(8,128)(2,1)S(1)} %attention.1), channel_id=1, source_target_pairs={{0,8},{1,9},{2,10},{3,11},{4,12},{5,13},{6,14},{7,15},{8,0},{9,1},... | collective-permute-start | bytes 122888 | tf_op jit(solution)/shard_map/ppermute | solution.py:318
  39.4 4.5 %collective-permute-start.5 = (bf16[32,640]{1,0:T(8,128)(2,1)S(1)}, bf16[32,640]{1,0:T(8,128)(2,1)S(1)}, u32[]{:S(2)}, u32[]{:S(2)}) collective-permute-start(bf16[32,640]{1,0:T(8,128)(2,1)S(1)} %attention.1), channel_id=1, source_target_pairs={{0,4},{1,5},{2,6},{3,7},{4,0},{5,1},{6,2},{7,3},{8,12},{9,13},{10,... | collective-permute-start | bytes 122888 | tf_op jit(solution)/shard_map/ppermute | solution.py:318
  42.2 4.5 %collective-permute-start.13 = (bf16[32,3584]{1,0:T(8,128)(2,1)S(1)}, bf16[32,3584]{1,0:T(8,128)(2,1)S(1)}, u32[]{:S(2)}, u32[]{:S(2)}) collective-permute-start(bf16[32,3584]{1,0:T(8,128)(2,1)S(1)} %collective-permute-done.2.refs_9_), channel_id=1, source_target_pairs={{0,1},{1,0},{2,3},{3,2},{4,5},{5,4},{6,7},{7,6},{8,9},{9,8},{10,11... | collective-permute-start | bytes 688136 | tf_op jit(solution)/shard_map/ppermute | solution.py:318
  43.7 8.5 %collective-permute-start.11 = (bf16[32,3584]{1,0:T(8,128)(2,1)S(1)}, bf16[32,3584]{1,0:T(8,128)(2,1)S(1)}, u32[]{:S(2)}, u32[]{:S(2)}) collective-permute-start(bf16[32,3584]{1,0:T(8,128)(2,1)S(1)} %collective-permute-done.2.refs_9_), channel_id=1, source_target_pairs={{0,4},{1,5},{4,8},{5,9},{8,12},{9,13},{12,14},{13,15},{14,10},{15,... | collective-permute-start | bytes 688136 | tf_op jit(solution)/shard_map/ppermute | solution.py:318
  44.0 8.2 %collective-permute-start.14 = (bf16[32,3584]{1,0:T(8,128)(2,1)S(1)}, bf16[32,3584]{1,0:T(8,128)(2,1)S(1)}, u32[]{:S(2)}, u32[]{:S(2)}) collective-permute-start(bf16[32,3584]{1,0:T(8,128)(2,1)S(1)} %collective-permute-done.3.refs_8_), channel_id=1, source_target_pairs={{0,1},{1,0},{2,3},{3,2},{4,5},{5,4},{6,7},{7,6},{8,9},{9,8},{10,11... | collective-permute-start | bytes 688136 | tf_op jit(solution)/shard_map/ppermute | solution.py:318
  44.0 8.2 %collective-permute-start.12 = (bf16[32,3584]{1,0:T(8,128)(2,1)S(1)}, bf16[32,3584]{1,0:T(8,128)(2,1)S(1)}, u32[]{:S(2)}, u32[]{:S(2)}) collective-permute-start(bf16[32,3584]{1,0:T(8,128)(2,1)S(1)} %collective-permute-done.3.refs_8_), channel_id=1, source_target_pairs={{0,2},{1,3},{4,0},{5,1},{8,4},{9,5},{12,8},{13,9},{14,12},{15,13},... | collective-permute-start | bytes 688136 | tf_op jit(solution)/shard_map/ppermute | solution.py:318
  45.8 8.9 %collective-permute-start.10 = (bf16[128,640]{1,0:T(8,128)(2,1)S(1)}, bf16[128,640]{1,0:T(8,128)(2,1)S(1)}, u32[]{:S(2)}, u32[]{:S(2)}) collective-permute-start(bf16[128,640]{1,0:T(8,128)(2,1)S(1)} %constant_dynamic-update-slice_fusion.refs_1_), channel_id=1, source_target_pairs={{0,2},{1,3},{2,0},{3,1},{4,6},{5,7},{6,4},{7,5},{8,10},{9,11},{10,... | collective-permute-start | bytes 491528 | tf_op jit(solution)/shard_map/ppermute | solution.py:318
  46.7 8.7 %collective-permute-start.15 = (bf16[128,640]{1,0:T(8,128)(2,1)S(1)}, bf16[128,640]{1,0:T(8,128)(2,1)S(1)}, u32[]{:S(2)}, u32[]{:S(2)}) collective-permute-start(bf16[128,640]{1,0:T(8,128)(2,1)S(1)} %constant_dynamic-update-slice_fusion.refs_1_), channel_id=1, source_target_pairs={{0,1},{1,0},{2,3},{3,2},{4,5},{5,4},{6,7},{7,6},{8,9},{9,8},{10,11... | collective-permute-start | bytes 491528 | tf_op jit(solution)/shard_map/ppermute | solution.py:318
  54.7 1.4 %collective-permute-start.16 = (bf16[128,640]{1,0:T(8,128)(2,1)S(1)}, bf16[128,640]{1,0:T(8,128)(2,1)S(1)}, u32[]{:S(2)}, u32[]{:S(2)}) collective-permute-start(bf16[128,640]{1,0:T(8,128)(2,1)S(1)} %collective-permute-done.10.refs_2_), channel_id=1, source_target_pairs={{0,1},{1,0},{2,3},{3,2},{4,5},{5,4},{6,7},{7,6},{8,9},{9,8},{10,11... | collective-permute-start | bytes 491528 | tf_op jit(solution)/shard_map/ppermute | solution.py:318
  54.7 1.7 %collective-permute-start.17 = (bf16[32,3584]{1,0:T(8,128)(2,1)S(1)}, bf16[32,3584]{1,0:T(8,128)(2,1)S(1)}, u32[]{:S(2)}, u32[]{:S(2)}) collective-permute-start(bf16[32,3584]{1,0:T(8,128)(2,1)S(1)} %collective-permute-done.11.refs_7_), channel_id=1, source_target_pairs={{0,1},{1,0},{2,3},{3,2},{4,5},{5,4},{6,7},{7,6},{8,9},{9,8},{10,11... | collective-permute-start | bytes 688136 | tf_op jit(solution)/shard_map/ppermute | solution.py:318
  55.2 1.5 %collective-permute-start.18 = (bf16[32,3584]{1,0:T(8,128)(2,1)S(1)}, bf16[32,3584]{1,0:T(8,128)(2,1)S(1)}, u32[]{:S(2)}, u32[]{:S(2)}) collective-permute-start(bf16[32,3584]{1,0:T(8,128)(2,1)S(1)} %collective-permute-done.12.refs_6_), channel_id=1, source_target_pairs={{0,1},{1,0},{2,3},{3,2},{4,5},{5,4},{6,7},{7,6},{8,9},{9,8},{10,11... | collective-permute-start | bytes 688136 | tf_op jit(solution)/shard_map/ppermute | solution.py:318
  55.3 11.5 %collective-permute-start.19 = (bf16[32,3584]{1,0:T(8,128)(2,1)S(1)}, bf16[32,3584]{1,0:T(8,128)(2,1)S(1)}, u32[]{:S(2)}, u32[]{:S(2)}) collective-permute-start(bf16[32,3584]{1,0:T(8,128)(2,1)S(1)} %broadcast_select_fusion), channel_id=1, source_target_pairs={{0,8},{1,7},{4,12},{5,3},{8,14},{9,1},{12,10},{13,5},{14,6},{15,9}... | collective-permute-start | bytes 688136 | tf_op jit(solution)/shard_map/ppermute | solution.py:318
  56.8 2.0 %copy-start.1 = (bf16[512,3584]{1,0:T(8,128)(2,1)S(1)}, bf16[512,3584]{1,0:T(8,128)(2,1)}, u32[]{:S(2)}) copy-start(bf16[512,3584]{1,0:T(8,128)(2,1)} %refs_11_.1) | copy-start | bytes 11010052
  58.8 0.9 copy-start.7
  59.8 0.7 copy-start.8
  61.2 7.2 %copy-start.2 = (bf16[512,3584]{1,0:T(8,128)(2,1)S(1)}, bf16[512,3584]{1,0:T(8,128)(2,1)}, u32[]{:S(2)}) copy-start(bf16[512,3584]{1,0:T(8,128)(2,1)} %refs_11_.1) | copy-start | bytes 11010052
  61.2 7.2 %copy-start.12 = (s32[17]{0:T(128)S(1)}, s32[17]{0:T(128)}, u32[]{:S(2)}) copy-start(s32[17]{0:T(128)} %get-tuple-element.74.refs_0_) | copy-start | bytes 208
  61.2 11.2 %copy-start.14 = (bf16[1,3584,1024]{2,1,0:T(8,128)(2,1)S(1)}, bf16[1,3584,1024]{2,1,0:T(8,128)(2,1)}, u32[]{:S(2)}) copy-start(bf16[1,3584,1024]{2,1,0:T(8,128)(2,1)} %param.24) | copy-start | bytes 22020100
  66.8 1.6 %collective-permute-start.20 = (bf16[32,3584]{1,0:T(8,128)(2,1)S(1)}, bf16[32,3584]{1,0:T(8,128)(2,1)S(1)}, u32[]{:S(2)}, u32[]{:S(2)}) collective-permute-start(bf16[32,3584]{1,0:T(8,128)(2,1)S(1)} %collective-permute-done.19.refs_5_), channel_id=1, source_target_pairs={{0,1},{1,0},{2,3},{3,2},{4,5},{5,4},{6,7},{7,6},{8,9},{9,8},{10,11... | collective-permute-start | bytes 688136 | tf_op jit(solution)/shard_map/ppermute | solution.py:318
  68.4 5.8 %slice-start = ((s8[7340032]{0:T(1024)(128)(4,1)}), s8[4194304]{0:T(1024)(128)(4,1)S(1)}, s32[]{:S(2)}) async-start(s8[7340032]{0:T(1024)(128)(4,1)} %bitcast.58), calls=%async_computation.1 | async-start | bytes 8388608
  72.4 1.9 %slice-start.1 = ((s8[7340032]{0:T(1024)(128)(4,1)}), s8[3145728]{0:T(1024)(128)(4,1)S(1)}, s32[]{:S(2)}) async-start(s8[7340032]{0:T(1024)(128)(4,1)} %bitcast.58), calls=%async_computation.2 | async-start | bytes 6291456
  72.4 3.7 %slice-start.2 = ((s8[7340032]{0:T(1024)(128)(4,1)}), s8[4194304]{0:T(1024)(128)(4,1)S(1)}, s32[]{:S(2)}) async-start(s8[7340032]{0:T(1024)(128)(4,1)} %bitcast.60), calls=%async_computation.3 | async-start | bytes 8388608
  74.3 2.4 %slice-start.3 = ((s8[7340032]{0:T(1024)(128)(4,1)}), s8[3145728]{0:T(1024)(128)(4,1)S(1)}, s32[]{:S(2)}) async-start(s8[7340032]{0:T(1024)(128)(4,1)} %bitcast.60), calls=%async_computation.4 | async-start | bytes 6291456
  78.3 2.9 %collective-permute-start.21 = (bf16[96,3584]{1,0:T(8,128)(2,1)S(1)}, bf16[96,3584]{1,0:T(8,128)(2,1)S(1)}, u32[]{:S(2)}, u32[]{:S(2)}) collective-permute-start(bf16[96,3584]{1,0:T(8,128)(2,1)S(1)} %slice.88), channel_id=1, source_target_pairs={{0,1},{1,0},{2,3},{3,2},{4,5},{5,4},{6,7},{7,6},{8,9},{9,8},{10,11... | collective-permute-start | bytes 2064392 | tf_op jit(solution)/shard_map/ppermute | solution.py:318
  81.2 6.7 %collective-permute-start.22 = (bf16[32,3584]{1,0:T(8,128)(2,1)S(1)}, bf16[32,3584]{1,0:T(8,128)(2,1)S(1)}, u32[]{:S(2)}, u32[]{:S(2)}) collective-permute-start(bf16[32,3584]{1,0:T(8,128)(2,1)S(1)} %add_convert_fusion.5), channel_id=1, source_target_pairs={{0,4},{1,3},{4,8},{5,1},{8,12},{9,5},{12,14},{13,9},{14,10},{15,13... | collective-permute-start | bytes 688136 | tf_op jit(solution)/shard_map/ppermute | solution.py:318
  90.6 10.1 %collective-permute-start.23 = (bf16[160,3584]{1,0:T(8,128)(2,1)S(1)}, bf16[160,3584]{1,0:T(8,128)(2,1)S(1)}, u32[]{:S(2)}, u32[]{:S(2)}) collective-permute-start(bf16[160,3584]{1,0:T(8,128)(2,1)S(1)} %slice.89), channel_id=1, source_target_pairs={{0,1},{1,0},{2,3},{3,2},{4,5},{5,4},{6,7},{7,6},{8,9},{9,8},{10,11... | collective-permute-start | bytes 3440648 | tf_op jit(solution)/shard_map/ppermute | solution.py:318
  90.8 8.3 %collective-permute-start.25 = (bf16[32,3584]{1,0:T(8,128)(2,1)S(1)}, bf16[32,3584]{1,0:T(8,128)(2,1)S(1)}, u32[]{:S(2)}, u32[]{:S(2)}) collective-permute-start(bf16[32,3584]{1,0:T(8,128)(2,1)S(1)} %get-tuple-element.143), channel_id=1, source_target_pairs={{0,2},{1,3},{4,0},{5,1},{8,4},{9,5},{12,8},{13,9},{14,12},{15,13},... | collective-permute-start | bytes 688136 | tf_op jit(solution)/shard_map/ppermute | solution.py:318
  92.9 7.7 %collective-permute-start.24 = (bf16[32,3584]{1,0:T(8,128)(2,1)S(1)}, bf16[32,3584]{1,0:T(8,128)(2,1)S(1)}, u32[]{:S(2)}, u32[]{:S(2)}) collective-permute-start(bf16[32,3584]{1,0:T(8,128)(2,1)S(1)} %get-tuple-element.144), channel_id=1, source_target_pairs={{0,4},{1,5},{4,8},{5,9},{8,12},{9,13},{12,14},{13,15},{14,10},{15,... | collective-permute-start | bytes 688136 | tf_op jit(solution)/shard_map/ppermute | solution.py:318
  100.8 7.0 %collective-permute-start.27 = (bf16[32,3584]{1,0:T(8,128)(2,1)S(1)}, bf16[32,3584]{1,0:T(8,128)(2,1)S(1)}, u32[]{:S(2)}, u32[]{:S(2)}) collective-permute-start(bf16[32,3584]{1,0:T(8,128)(2,1)S(1)} %get-tuple-element.141), channel_id=1, source_target_pairs={{0,2},{1,3},{4,0},{5,1},{8,4},{9,5},{12,8},{13,9},{14,12},{15,13},... | collective-permute-start | bytes 688136 | tf_op jit(solution)/shard_map/ppermute | solution.py:318
  101.2 6.9 %collective-permute-start.26 = (bf16[32,3584]{1,0:T(8,128)(2,1)S(1)}, bf16[32,3584]{1,0:T(8,128)(2,1)S(1)}, u32[]{:S(2)}, u32[]{:S(2)}) collective-permute-start(bf16[32,3584]{1,0:T(8,128)(2,1)S(1)} %get-tuple-element.142), channel_id=1, source_target_pairs={{0,4},{1,5},{4,8},{5,9},{8,12},{9,13},{12,14},{13,15},{14,10},{15,... | collective-permute-start | bytes 688136 | tf_op jit(solution)/shard_map/ppermute | solution.py:318
  108.3 6.1 %collective-permute-start.29 = (bf16[32,3584]{1,0:T(8,128)(2,1)S(1)}, bf16[32,3584]{1,0:T(8,128)(2,1)S(1)}, u32[]{:S(2)}, u32[]{:S(2)}) collective-permute-start(bf16[32,3584]{1,0:T(8,128)(2,1)S(1)} %get-tuple-element.139), channel_id=1, source_target_pairs={{0,2},{1,3},{4,0},{5,1},{8,4},{9,5},{12,8},{13,9},{14,12},{15,13},... | collective-permute-start | bytes 688136 | tf_op jit(solution)/shard_map/ppermute | solution.py:318
  109.7 6.0 %collective-permute-start.28 = (bf16[32,3584]{1,0:T(8,128)(2,1)S(1)}, bf16[32,3584]{1,0:T(8,128)(2,1)S(1)}, u32[]{:S(2)}, u32[]{:S(2)}) collective-permute-start(bf16[32,3584]{1,0:T(8,128)(2,1)S(1)} %get-tuple-element.140), channel_id=1, source_target_pairs={{0,4},{1,5},{4,8},{5,9},{8,12},{9,13},{12,14},{13,15},{14,10},{15,... | collective-permute-start | bytes 688136 | tf_op jit(solution)/shard_map/ppermute | solution.py:318
  (2 other events, 1.3 us)

commit v13 on v10

--- a/solution.py
+++ b/solution.py
@@ -40,10 +40,7 @@
 def step_perm(chips, by_high, by_low):
     high, low = gather_steps(chips)
     return [
-        (
-            2 * (h * low + l) + core,
-            2 * ((h - by_high) % high * low + (l - by_low) % low) + core,
-        )
+        (2 * (h * low + l) + core, 2 * ((h ^ by_high) * low + (l ^ by_low)) + core)
         for h in range(high)
         for l in range(low)
         for core in range(2)
@@ -59,8 +56,8 @@
             for side in (0, chips):
                 for d in part:
                     other = ring[(p + d) % chips]
-                    by_high = (other // low - chip // low) % high
-                    by_low = (other % low - chip % low) % low
+                    by_high = (other // low) ^ (chip // low)
+                    by_low = (other % low) ^ (chip % low)
                     table[chip].append(side + by_low * high + by_high)
     return table
 
@@ -137,7 +134,7 @@
     rows, width = resid_blocks[0].shape
     latent = w_out.shape[0]
     total = blocks * rows
-    cols = tile_of(width, 1024)
+    cols = tile_of(width, 512)
     packed = pooled[0].shape[1]
     experts_all = w_router_t.shape[0]
 
@@ -147,7 +144,7 @@
     def tiles(height):
         return pl.BlockSpec((height, cols), lambda i: (0, i))
 
-    need = total * (cols * 14 + packed * 6 + 6 * LANES * 4) + 4 * latent * cols
+    need = total * (cols * 24 + packed * 6 + 8 * LANES * 4) + 4 * latent * cols
     return pl.pallas_call(
         lambda *refs: norm_kernel(far, blocks, rows, latent, width, *refs),
         grid=(width // cols,),
@@ -171,11 +168,11 @@
             pltpu.VMEM((total, experts_all), jnp.float32),
         ],
         compiler_params=pltpu.CompilerParams(
-            dimension_semantics=("arbitrary",), vmem_limit_bytes=(int(need) // (1 << 20) + 2) << 20
+            dimension_semantics=("arbitrary",), vmem_limit_bytes=(int(need) // (1 << 20) + 6) << 20
         ),
         cost_estimate=pl.CostEstimate(
-            flops=8 * total * width * latent,
-            bytes_accessed=6 * total * width * 2 + latent * width * 2,
+            flops=2 * total * width * latent,
+            bytes_accessed=2 * total * width * 2 + latent * width * 2,
             transcendentals=total,
         ),
         name="normalize",
@@ -287,9 +284,11 @@
             pltpu.VMEM((steps * rows, keys), jnp.float32),
         ],
         compiler_params=pltpu.CompilerParams(
-            dimension_semantics=("arbitrary",), vmem_limit_bytes=56 << 20
+            dimension_semantics=("arbitrary",), vmem_limit_bytes=(10 << 20) + 10240 * keys
         ),
-        cost_estimate=pl.CostEstimate(**LONG),
+        cost_estimate=pl.CostEstimate(
+            flops=2 * q_abs.size * keys, bytes_accessed=2 * q_abs.size, transcendentals=0
+        ),
         name="attention",
     )(q_abs, cache, fresh, lengths, routes)
 
@@ -319,6 +318,7 @@
     half = chips // 2
     far, near = distances(chips)
     hold = lax.optimization_barrier
+    cut = rows // 2
     sibling = sibling_perm(chips)
 
     def send(a, perm):
@@ -355,9 +355,6 @@
     row_lengths, scalars, held = hold((row_lengths, scalars, held))
     held[-2], held[2] = around(held[-1], held[1])
     sib[0] = send(mine, sibling)
-    owned, held, sib = hold((owned, held, sib))
-    for t in range(3, half):
-        held[-t], held[t] = around(held[1 - t], held[t - 1])
     sib[1], sib[-1] = send(held[1], sibling), send(held[-1], sibling)
     gain = norm_gain[None, :]
     packet = attention(
@@ -373,25 +370,26 @@
 
     high, low = gather_steps(chips)
     along = [send(packet, step_perm(chips, i, 0)) for i in range(1, high)]
-    onward = send(jnp.where(first_core, held[2 - half], held[half - 2]), parted)
-    sib[2] = send(held[2], sibling)
-    along, onward, sib = hold((along, onward, sib))
-    held[half] = onward
+    for t in range(3, half):
+        held[-t], held[t] = around(held[1 - t], held[t - 1])
+    along, held = hold((along, held))
     along = jnp.concatenate([packet] + along, axis=0)
     across = [send(along, step_perm(chips, 0, i)) for i in range(1, low)]
+    held[half] = send(jnp.where(first_core, held[2 - half], held[half - 2]), parted)
+    along_sib = send(along, sibling)
+    sib[2], sib[-2] = send(held[2], sibling), send(held[-2], sibling)
+    across, along_sib, held, sib = hold((across, along_sib, held, sib))
     for d in held:
         if d not in sib:
             sib[d] = send(held[d], sibling)
-    across, sib = hold((across, sib))
     across = across[0] if low == 2 else jnp.concatenate(across, axis=0)
-    gathered = [along, across, send(along, sibling), send(across, sibling)]
 
     f32 = jnp.float32
 
     x_far, x_near, scale, weight, hidden = normalize(
         2 * len(far),
         scalars,
-        gathered,
+        [along, across, along_sib, send(across, sibling)],
         [a[d] for part in (far, near) for a in (held, sib) for d in part],
         w_out,
         gain,
@@ -423,16 +421,15 @@
     y, received = swap(far, product(act, w_down).astype(jnp.bfloat16))
     gated, y, received = hold((product(x_near, w_gate), y, received))
     add_up(far, y, received)
-    right, left = both(sums[half - 1], sums[1 - half])
-    onward = send(sums[half].astype(jnp.bfloat16), parted)
-    act = hold(activate(gated, product(x_near, w_up), slice(far_rows, None)))
-    y = product(act, w_down).astype(jnp.bfloat16)
-    y, right, left, onward = hold((y, right, left, onward))
-    y, received = swap(near, y)
+    right, left = both(sums[half][:cut], sums[half][cut:])
+    act = activate(gated, product(x_near, w_up), slice(far_rows, None))
+    act, right, left = hold((act, right, left))
+    right = jnp.concatenate([right.astype(f32), jnp.zeros((rows - cut, width), f32)], axis=0)
+    left = jnp.concatenate([jnp.zeros((cut, width), f32), left.astype(f32)], axis=0)
+    right, left = both(sums[half - 1] + right, sums[1 - half] + left)
+    y, received = swap(near, product(act, w_down).astype(jnp.bfloat16))
+    y, received, right, left = hold((y, received, right, left))
     add_up(near, y, received)
-    onward = onward.astype(f32)
-    right = right.astype(f32) + jnp.where(first_core, onward, 0.0)
-    left = left.astype(f32) + jnp.where(first_core, 0.0, onward)
     for t in range(half - 2, 0, -1):
         right, left = hold(both(sums[t] + right.astype(f32), sums[-t] + left.astype(f32)))
     mixed = hidden + sums[0] + right.astype(f32) + left.astype(f32)

time: 115 us -> 111 us (0.965)
  local copies, waits for them, and re-layouts: 2.34 us -> 7.31 us
  starting transfers between devices: 34.5 us -> 31.2 us
  matrix products: 20.3 us -> 17.4 us
  waiting for transfers between devices: 41.8 us -> 40.3 us
    ppermute x30 -> x31, waiting for transfers between devices: 41.8 us -> 32.7 us  [send(): return lax.ppermute(a, 'expert', perm)]
    all_to_all x1, waiting for transfers between devices: 0.01 us -> 7.6 us  [local(): lax.all_to_all(ordered, 'expert', split_axis=0, concat_axis=0, tiled=True)]
    unnamed x29 -> x35, local copies, waits for them, and re-layouts: 0.91 us -> 5.86 us
    ppermute x30 -> x31, starting transfers between devices: 28.2 us -> 24.9 us  [send(): return lax.ppermute(a, 'expert', perm)]
    dot_general x6, matrix products: 19.3 us -> 16.4 us  [product(): return jnp.dot(a, w[0], preferred_element_type=f32)]
    pallas_call x1, Pallas kernels: 5.95 us -> 4.19 us  [attention(): pl.pallas_call(lambda *refs: attention_kernel(context, latent, *refs), gr...]
  transfers between devices with their start and end apart: 31 -> 32, of which waited for: 14 -> 13; matrix products, arithmetic and copies ran while one was open for 7% -> 7% of each run, Pallas kernels for 6% -> 5%
where the time goes in v13:
time: 111 us
  waiting for transfers between devices  40.3 us (36%)
  starting transfers between devices  31.2 us (28%)
  matrix products  17.4 us (16%)
  Pallas kernels  13 us (12%)
  local copies, waits for them, and re-layouts  7.31 us (7%)
  other arithmetic  1.37 us (1%)
    ppermute x31, waiting for transfers between devices, send(): return lax.ppermute(a, 'expert', perm)  32.7 us
    ppermute x31, starting transfers between devices, send(): return lax.ppermute(a, 'expert', perm)  24.9 us
    dot_general x6, matrix products, product(): return jnp.dot(a, w[0], preferred_element_type=f32)  16.4 us
    all_to_all x1, waiting for transfers between devices, local(): lax.all_to_all(ordered, 'expert', split_axis=0, concat_axis=0, tiled=True)  7.6 us
    pallas_call x1, Pallas kernels, normalize(): pl.pallas_call(lambda *refs: norm_kernel(far, blocks, rows, latent, width...  7.38 us
    all_to_all x1, starting transfers between devices, local(): lax.all_to_all(ordered, 'expert', split_axis=0, concat_axis=0, tiled=True)  6.29 us
    unnamed x35, local copies, waits for them, and re-layouts  5.86 us
    pallas_call x1, Pallas kernels, attention(): pl.pallas_call(lambda *refs: attention_kernel(context, latent, *refs), gr...  4.19 us
  transfers between devices with their start and end apart: 32, of which 13 were waited for; matrix products, arithmetic and copies ran while one was open for 7% of the time, Pallas kernels for 5%

profile of v13, /device:TPU:0, one launch (start us, length us, event | category | flops | bytes accessed | tf_op | source)
XLA Modules:
  0.0 110.9 jit_solution(2778112128788960067)
XLA Ops:
  0.5 2.6 %collective-permute-start.1 = (bf16[32,3584]{1,0:T(8,128)(2,1)}, bf16[32,3584]{1,0:T(8,128)(2,1)}, u32[]{:S(2)}, u32[]{:S(2)}) collective-permute-start(bf16[32,3584]{1,0:T(8,128)(2,1)} %bitcast.54), channel_id=1, source_target_pairs={{0,2},{1,3},{4,0},{5,1},{8,4},{9,5},{12,8},{13,9},{14,12},{15,13},... | collective-permute-start | bytes 688136 | tf_op jit(solution)/shard_map/ppermute | solution.py:325
  3.2 1.0 fusion.27
  4.4 0.7 copy.19
  5.1 6.3 %all-to-all-start = ((bf16[16,2,8,576]{3,2,1,0:T(8,128)(2,1)}), bf16[16,2,8,576]{3,2,1,0:T(8,128)(2,1)S(1)}, u32[]{:S(2)}, u32[]{:S(2)}) async-start(bf16[16,2,8,576]{3,2,1,0:T(8,128)(2,1)} %copy.19), calls=%async_computation | async-start | bytes 655360 | tf_op jit(solution)/shard_map/all_to_all | solution.py:342
  11.5 1.4 %lookup.1 = (s32[8]{0:T(128)}, s32[17]{0:T(128)}) custom-call(s32[128]{0:T(128)} %owner.1, s32[128]{0:T(128)} %lengths.1, s32[272]{0:T(512)} %constant.41.table, s32[1]{0:T(128)} %bitcast.device), custom_call_target="tpu_custom_call" | custom-call | flops 10000000000 | bytes 100000000 | tf_op jit(solution)/shard_map/lookup/pallas_call | solution.py:194
  13.3 1.7 %collective-permute-start.2 = (bf16[32,3584]{1,0:T(8,128)(2,1)}, bf16[32,3584]{1,0:T(8,128)(2,1)S(1)}, u32[]{:S(2)}, u32[]{:S(2)}) collective-permute-start(bf16[32,3584]{1,0:T(8,128)(2,1)} %collective-permute-done.refs_13_), channel_id=1, source_target_pairs={{0,4},{1,5},{4,8},{5,9},{8,12},{9,13},{12,14},{13,15},{14,10},{15,... | collective-permute-start | bytes 688136 | tf_op jit(solution)/shard_map/ppermute | solution.py:325
  15.4 7.6 %all-to-all-done = bf16[16,2,8,576]{3,2,1,0:T(8,128)(2,1)S(1)} async-done(((bf16[16,2,8,576]{3,2,1,0:T(8,128)(2,1)}), bf16[16,2,8,576]{3,2,1,0:T(8,128)(2,1)S(1)}, u32[]{:S(2)}, u32[]{:S(2)}) %all-to-all-start) | async-done | bytes 294944 | tf_op jit(solution)/shard_map/all_to_all | solution.py:342
  23.0 0.6 copy-done.8
  23.6 4.2 %attention.1 = bf16[32,640]{1,0:T(8,128)(2,1)S(1)} custom-call(bf16[4,8,36864]{2,1,0:T(8,128)(2,1)S(1)} %copy-done.2, bf16[256,576]{1,0:T(8,128)(2,1)S(1)} %bitcast.52, bf16[32,576]{1,0:T(8,128)(2,1)S(1)} %bitcast.58, s32[8]{0:T(128)S(1)} %copy-done.8, s32[32,8]{1,0:T(8,128)S(1)} %bitcast.59), custom_call_target="tpu_custom_call" | custom-call | flops 679477248 | bytes 2359296 | tf_op jit(solution)/shard_map/attention/pallas_call | solution.py:274
  27.9 2.0 %collective-permute-start.11 = (bf16[32,3584]{1,0:T(8,128)(2,1)S(1)}, bf16[32,3584]{1,0:T(8,128)(2,1)S(1)}, u32[]{:S(2)}, u32[]{:S(2)}) collective-permute-start(bf16[32,3584]{1,0:T(8,128)(2,1)S(1)} %collective-permute-done.3.refs_14_), channel_id=1, source_target_pairs={{0,2},{1,3},{4,0},{5,1},{8,4},{9,5},{12,8},{13,9},{14,12},{15,13},... | collective-permute-start | bytes 688136 | tf_op jit(solution)/shard_map/ppermute | solution.py:325
  29.9 0.7 collective-permute-start.9
  30.7 0.8 collective-permute-start.8
  31.5 2.9 %collective-permute-start.7 = (bf16[32,640]{1,0:T(8,128)(2,1)S(1)}, bf16[32,640]{1,0:T(8,128)(2,1)S(1)}, u32[]{:S(2)}, u32[]{:S(2)}) collective-permute-start(bf16[32,640]{1,0:T(8,128)(2,1)S(1)} %attention.1), channel_id=1, source_target_pairs={{0,4},{1,5},{2,6},{3,7},{4,0},{5,1},{6,2},{7,3},{8,12},{9,13},{10,... | collective-permute-start | bytes 122888 | tf_op jit(solution)/shard_map/ppermute | solution.py:325
  34.3 3.7 %collective-permute-done.9 = bf16[32,640]{1,0:T(8,128)(2,1)S(1)} collective-permute-done((bf16[32,640]{1,0:T(8,128)(2,1)S(1)}, bf16[32,640]{1,0:T(8,128)(2,1)S(1)}, u32[]{:S(2)}, u32[]{:S(2)}) %collective-permute-start.9) | collective-permute-done | bytes 40992 | tf_op jit(solution)/shard_map/ppermute | solution.py:325
  38.0 1.2 %collective-permute-done.8 = bf16[32,640]{1,0:T(8,128)(2,1)S(1)} collective-permute-done((bf16[32,640]{1,0:T(8,128)(2,1)S(1)}, bf16[32,640]{1,0:T(8,128)(2,1)S(1)}, u32[]{:S(2)}, u32[]{:S(2)}) %collective-permute-start.8) | collective-permute-done | bytes 40992 | tf_op jit(solution)/shard_map/ppermute | solution.py:325
  39.3 0.5 collective-permute-start.16
  40.4 1.9 %collective-permute-start.12 = (bf16[128,640]{1,0:T(8,128)(2,1)S(1)}, bf16[128,640]{1,0:T(8,128)(2,1)S(1)}, u32[]{:S(2)}, u32[]{:S(2)}) collective-permute-start(bf16[128,640]{1,0:T(8,128)(2,1)S(1)} %constant_dynamic-update-slice_fusion.refs_1_), channel_id=1, source_target_pairs={{0,2},{1,3},{2,0},{3,1},{4,6},{5,7},{6,4},{7,5},{8,10},{9,11},{10,... | collective-permute-start | bytes 491528 | tf_op jit(solution)/shard_map/ppermute | solution.py:325
  42.3 6.9 %collective-permute-done.12.refs_2_ = bf16[128,640]{1,0:T(8,128)(2,1)S(1)} collective-permute-done((bf16[128,640]{1,0:T(8,128)(2,1)S(1)}, bf16[128,640]{1,0:T(8,128)(2,1)S(1)}, u32[]{:S(2)}, u32[]{:S(2)}) %collective-permute-start.12) | collective-permute-done | bytes 163872 | tf_op jit(solution)/shard_map/ppermute | solution.py:325
  49.3 0.5 collective-permute-start.19
  50.3 1.4 %collective-permute-done.17.refs_4_ = bf16[128,640]{1,0:T(8,128)(2,1)S(1)} collective-permute-done((bf16[128,640]{1,0:T(8,128)(2,1)S(1)}, bf16[128,640]{1,0:T(8,128)(2,1)S(1)}, u32[]{:S(2)}, u32[]{:S(2)}) %collective-permute-start.17) | collective-permute-done | bytes 163872 | tf_op jit(solution)/shard_map/ppermute | solution.py:325
  51.7 2.0 %copy-done.1 = bf16[512,3584]{1,0:T(8,128)(2,1)S(1)} copy-done((bf16[512,3584]{1,0:T(8,128)(2,1)S(1)}, bf16[512,3584]{1,0:T(8,128)(2,1)}, u32[]{:S(2)}) %copy-start.1) | copy-done | bytes 3670040
  53.8 0.9 copy-done.3
  54.7 0.9 copy-done.4
  55.6 0.6 copy-done.7
  56.2 7.4 %normalize.1 = (bf16[192,3584]{1,0:T(8,128)(2,1)S(1)}, bf16[320,3584]{1,0:T(8,128)(2,1)S(1)}, f32[512,128]{1,0:T(8,128)S(1)}, f32[512,128]{1,0:T(8,128)S(1)}, f32[32,3584]{1,0:T(8,128)S(1)}) custom-call(s32[17]{0:T(128)S(1)} %copy-done.7, bf16[128,640]{1,0:T(8,128)(2,1)S(1)} %constant_dynamic-update-slice_fusion.refs_1_, ...), custom_call_target="tpu_custom_call" | custom-call | flops 1879048192 | bytes 11010048 | tf_op jit(solution)/shard_map/normalize/pallas_call | solution.py:148
  64.0 4.9 %fusion.21 = f32[192,1024]{1,0:T(8,128)S(1)} fusion(bf16[192,3584]{1,0:T(8,128)(2,1)S(1)} %get-tuple-element.110, bf16[1,3584,1024]{2,1,0:T(8,128)(2,1)} %param.24, f32[192]{0:T(256)S(1)} %get-tuple-element.138), kind=kOutput, calls=%fused_computation.16 | convolution fusion | flops 1409482752 | bytes 9503488 | tf_op jit(solution)/shard_map/dot_general | solution.py:401
  69.0 1.8 %multiply_convert_fusion.1 = bf16[192,1024]{1,0:T(8,128)(2,1)S(1)} fusion(f32[192,1024]{1,0:T(8,128)S(1)} %fusion.21, f32[192]{0:T(256)S(1)} %get-tuple-element.137, f32[192]{0:T(256)S(1)} %get-tuple-element.138, bf16[192,3584]{1,0:T(8,128)(2,1)S(1)} %get-tuple-element.110, bf16[1,3584,1024]{2,1,0:T(8,128)(2,1)S(1)} %bitcast.64), kind=kOutput, calls=%fused_computation.20 | convolution fusion | flops 1410859008 | bytes 9897472 | tf_op jit(solution)/shard_map/dot_general | solution.py:401
  70.9 0.7 slice-done.5
  71.5 1.6 %fusion.15 = bf16[192,3584]{1,0:T(8,128)(2,1)S(1)} fusion(bf16[192,1024]{1,0:T(8,128)(2,1)S(1)} %multiply_convert_fusion.1, bf16[1,1024,3584]{2,1,0:T(8,128)(2,1)S(1)} %bitcast.66), kind=kOutput, calls=%fused_computation.13 | convolution fusion | flops 1409974272 | bytes 9109504 | tf_op jit(solution)/shard_map/dot_general | solution.py:401
  73.5 2.7 %fusion.10 = f32[320,1024]{1,0:T(8,128)S(1)} fusion(bf16[320,3584]{1,0:T(8,128)(2,1)S(1)} %get-tuple-element.109, bf16[1,3584,1024]{2,1,0:T(8,128)(2,1)S(1)} %bitcast.62), kind=kOutput, calls=%fused_computation.10 | convolution fusion | flops 2348810240 | bytes 10944512 | tf_op jit(solution)/shard_map/dot_general | solution.py:401
  76.2 1.5 %collective-permute-start.23 = (bf16[16,3584]{1,0:T(8,128)(2,1)S(1)}, bf16[16,3584]{1,0:T(8,128)(2,1)S(1)}, u32[]{:S(2)}, u32[]{:S(2)}) collective-permute-start(bf16[16,3584]{1,0:T(8,128)(2,1)S(1)} %get-tuple-element.133), channel_id=1, source_target_pairs={{0,2},{1,3},{4,0},{5,1},{8,4},{9,5},{12,8},{13,9},{14,12},{15,13},... | collective-permute-start | bytes 344072 | tf_op jit(solution)/shard_map/ppermute | solution.py:325
  77.7 0.6 collective-permute-start.22
  78.3 2.8 %multiply_convert_fusion = bf16[320,1024]{1,0:T(8,128)(2,1)S(1)} fusion(f32[320,1024]{1,0:T(8,128)S(1)} %fusion.10, f32[320]{0:T(512)S(1)} %get-tuple-element.135, f32[320]{0:T(512)S(1)} %get-tuple-element.136, bf16[320,3584]{1,0:T(8,128)(2,1)S(1)} %get-tuple-element.109, bf16[1,3584,1024]{2,1,0:T(8,128)(2,1)S(1)} %bitcast.64), kind=kOutput, calls=%fused_computation.15 | convolution fusion | flops 2351759360 | bytes 11602432 | tf_op jit(solution)/shard_map/dot_general | solution.py:401
  81.1 0.5 collective-permute-done.23
  81.7 1.1 %collective-permute-done.22 = bf16[16,3584]{1,0:T(8,128)(2,1)S(1)} collective-permute-done((bf16[16,3584]{1,0:T(8,128)(2,1)S(1)}, bf16[16,3584]{1,0:T(8,128)(2,1)S(1)}, u32[]{:S(2)}, u32[]{:S(2)}) %collective-permute-start.22) | collective-permute-done | bytes 114720 | tf_op jit(solution)/shard_map/ppermute | solution.py:325
  82.8 2.5 %fusion.12 = bf16[320,3584]{1,0:T(8,128)(2,1)S(1)} fusion(bf16[320,1024]{1,0:T(8,128)(2,1)S(1)} %multiply_convert_fusion, bf16[1,1024,3584]{2,1,0:T(8,128)(2,1)S(1)} %bitcast.66), kind=kOutput, calls=%fused_computation.12 | convolution fusion | flops 2349957120 | bytes 10289152 | tf_op jit(solution)/shard_map/dot_general | solution.py:401
  85.6 1.3 %collective-permute-start.26 = (bf16[32,3584]{1,0:T(8,128)(2,1)S(1)}, bf16[32,3584]{1,0:T(8,128)(2,1)S(1)}, u32[]{:S(2)}, u32[]{:S(2)}) collective-permute-start(bf16[32,3584]{1,0:T(8,128)(2,1)S(1)} %get-tuple-element.131), channel_id=1, source_target_pairs={{0,2},{1,3},{4,0},{5,1},{8,4},{9,5},{12,8},{13,9},{14,12},{15,13},... | collective-permute-start | bytes 688136 | tf_op jit(solution)/shard_map/ppermute | solution.py:325
  86.9 0.8 collective-permute-start.25
  87.7 6.0 %collective-permute-done.26 = bf16[32,3584]{1,0:T(8,128)(2,1)S(1)} collective-permute-done((bf16[32,3584]{1,0:T(8,128)(2,1)S(1)}, bf16[32,3584]{1,0:T(8,128)(2,1)S(1)}, u32[]{:S(2)}, u32[]{:S(2)}) %collective-permute-start.26) | collective-permute-done | bytes 229408 | tf_op jit(solution)/shard_map/ppermute | solution.py:325
  93.7 1.0 collective-permute-done.25
  94.8 1.8 %collective-permute-start.28 = (bf16[32,3584]{1,0:T(8,128)(2,1)S(1)}, bf16[32,3584]{1,0:T(8,128)(2,1)S(1)}, u32[]{:S(2)}, u32[]{:S(2)}) collective-permute-start(bf16[32,3584]{1,0:T(8,128)(2,1)S(1)} %get-tuple-element.129), channel_id=1, source_target_pairs={{0,2},{1,3},{4,0},{5,1},{8,4},{9,5},{12,8},{13,9},{14,12},{15,13},... | collective-permute-start | bytes 688136 | tf_op jit(solution)/shard_map/ppermute | solution.py:325
  96.9 4.9 %collective-permute-done.28 = bf16[32,3584]{1,0:T(8,128)(2,1)S(1)} collective-permute-done((bf16[32,3584]{1,0:T(8,128)(2,1)S(1)}, bf16[32,3584]{1,0:T(8,128)(2,1)S(1)}, u32[]{:S(2)}, u32[]{:S(2)}) %collective-permute-start.28) | collective-permute-done | bytes 229408 | tf_op jit(solution)/shard_map/ppermute | solution.py:325
  101.8 1.5 %collective-permute-done.27 = bf16[32,3584]{1,0:T(8,128)(2,1)S(1)} collective-permute-done((bf16[32,3584]{1,0:T(8,128)(2,1)S(1)}, bf16[32,3584]{1,0:T(8,128)(2,1)S(1)}, u32[]{:S(2)}, u32[]{:S(2)}) %collective-permute-start.27) | collective-permute-done | bytes 229408 | tf_op jit(solution)/shard_map/ppermute | solution.py:325
  103.4 0.7 collective-permute-start.30
  104.0 1.4 %collective-permute-start.29 = (bf16[32,3584]{1,0:T(8,128)(2,1)S(1)}, bf16[32,3584]{1,0:T(8,128)(2,1)S(1)}, u32[]{:S(2)}, u32[]{:S(2)}) collective-permute-start(bf16[32,3584]{1,0:T(8,128)(2,1)S(1)} %get-tuple-element.128), channel_id=1, source_target_pairs={{0,4},{1,5},{4,8},{5,9},{8,12},{9,13},{12,14},{13,15},{14,10},{15,... | collective-permute-start | bytes 688136 | tf_op jit(solution)/shard_map/ppermute | solution.py:325
  105.5 4.0 %collective-permute-done.30 = bf16[32,3584]{1,0:T(8,128)(2,1)S(1)} collective-permute-done((bf16[32,3584]{1,0:T(8,128)(2,1)S(1)}, bf16[32,3584]{1,0:T(8,128)(2,1)S(1)}, u32[]{:S(2)}, u32[]{:S(2)}) %collective-permute-start.30) | collective-permute-done | bytes 229408 | tf_op jit(solution)/shard_map/ppermute | solution.py:325
  109.5 0.6 collective-permute-done.29
  110.1 0.8 fusion.32
  (79 shorter events, 4.7 us)
Async XLA Ops:
  0.0 3.2 %copy-start = (bf16[128,2,576]{0,2,1:T(8,128)(2,1)S(1)}, bf16[128,2,576]{0,2,1:T(8,128)(2,1)}, u32[]{:S(2)}) copy-start(bf16[128,2,576]{0,2,1:T(8,128)(2,1)} %param.16) | copy-start | bytes 884740
  0.0 27.8 %collective-permute-start.5 = (bf16[32,3584]{1,0:T(8,128)(2,1)}, bf16[32,3584]{1,0:T(8,128)(2,1)}, u32[]{:S(2)}, u32[]{:S(2)}) collective-permute-start(bf16[32,3584]{1,0:T(8,128)(2,1)} %bitcast.53), channel_id=1, source_target_pairs={{0,1},{1,0},{2,3},{3,2},{4,5},{5,4},{6,7},{7,6},{8,9},{9,8},{10,11... | collective-permute-start | bytes 688136 | tf_op jit(solution)/shard_map/ppermute | solution.py:325
  0.5 12.4 %collective-permute-start.1 = (bf16[32,3584]{1,0:T(8,128)(2,1)}, bf16[32,3584]{1,0:T(8,128)(2,1)}, u32[]{:S(2)}, u32[]{:S(2)}) collective-permute-start(bf16[32,3584]{1,0:T(8,128)(2,1)} %bitcast.54), channel_id=1, source_target_pairs={{0,2},{1,3},{4,0},{5,1},{8,4},{9,5},{12,8},{13,9},{14,12},{15,13},... | collective-permute-start | bytes 688136 | tf_op jit(solution)/shard_map/ppermute | solution.py:325
  3.0 9.8 %collective-permute-start = (bf16[32,3584]{1,0:T(8,128)(2,1)}, bf16[32,3584]{1,0:T(8,128)(2,1)}, u32[]{:S(2)}, u32[]{:S(2)}) collective-permute-start(bf16[32,3584]{1,0:T(8,128)(2,1)} %bitcast.55), channel_id=1, source_target_pairs={{0,4},{1,5},{4,8},{5,9},{8,12},{9,13},{12,14},{13,15},{14,10},{15,... | collective-permute-start | bytes 688136 | tf_op jit(solution)/shard_map/ppermute | solution.py:325
  5.1 17.9 %all-to-all-start = ((bf16[16,2,8,576]{3,2,1,0:T(8,128)(2,1)}), bf16[16,2,8,576]{3,2,1,0:T(8,128)(2,1)S(1)}, u32[]{:S(2)}, u32[]{:S(2)}) async-start(bf16[16,2,8,576]{3,2,1,0:T(8,128)(2,1)} %copy.19), calls=%async_computation | async-start | bytes 655360 | tf_op jit(solution)/shard_map/all_to_all | solution.py:342
  11.4 4.0 %copy-start.9 = (bf16[3584]{0:T(1024)(128)(2,1)S(1)}, bf16[3584]{0:T(1024)(128)(2,1)}, u32[]{:S(2)}) copy-start(bf16[3584]{0:T(1024)(128)(2,1)} %param.22) | copy-start | bytes 21508
  11.4 11.6 %copy-start.2 = (bf16[4,8,36864]{2,1,0:T(8,128)(2,1)S(1)}, bf16[4,8,36864]{2,1,0:T(8,128)(2,1)}, u32[]{:S(2)}) copy-start(bf16[4,8,36864]{2,1,0:T(8,128)(2,1)} %refs_0_.1) | copy-start | bytes 7077892
  11.4 11.6 %copy-start.5 = (bf16[4,8,576]{2,1,0:T(8,128)(2,1)S(1)}, bf16[4,8,576]{2,1,0:T(8,128)(2,1)}, u32[]{:S(2)}) copy-start(bf16[4,8,576]{2,1,0:T(8,128)(2,1)} %param.15) | copy-start | bytes 110596
  11.4 11.5 %copy-start.6 = (s32[4,8,8]{2,1,0:T(8,128)S(1)}, s32[4,8,8]{2,1,0:T(8,128)}, u32[]{:S(2)}) copy-start(s32[4,8,8]{2,1,0:T(8,128)} %param.20) | copy-start | bytes 3076
  12.9 14.9 %collective-permute-start.4 = (bf16[32,3584]{1,0:T(8,128)(2,1)}, bf16[32,3584]{1,0:T(8,128)(2,1)}, u32[]{:S(2)}, u32[]{:S(2)}) collective-permute-start(bf16[32,3584]{1,0:T(8,128)(2,1)} %collective-permute-done.refs_13_), channel_id=1, source_target_pairs={{0,1},{1,0},{2,3},{3,2},{4,5},{5,4},{6,7},{7,6},{8,9},{9,8},{10,11... | collective-permute-start | bytes 688136 | tf_op jit(solution)/shard_map/ppermute | solution.py:325
  13.3 14.5 %collective-permute-start.2 = (bf16[32,3584]{1,0:T(8,128)(2,1)}, bf16[32,3584]{1,0:T(8,128)(2,1)S(1)}, u32[]{:S(2)}, u32[]{:S(2)}) collective-permute-start(bf16[32,3584]{1,0:T(8,128)(2,1)} %collective-permute-done.refs_13_), channel_id=1, source_target_pairs={{0,4},{1,5},{4,8},{5,9},{8,12},{9,13},{12,14},{13,15},{14,10},{15,... | collective-permute-start | bytes 688136 | tf_op jit(solution)/shard_map/ppermute | solution.py:325
  15.0 12.8 %collective-permute-start.6 = (bf16[32,3584]{1,0:T(8,128)(2,1)}, bf16[32,3584]{1,0:T(8,128)(2,1)}, u32[]{:S(2)}, u32[]{:S(2)}) collective-permute-start(bf16[32,3584]{1,0:T(8,128)(2,1)} %collective-permute-done.1.refs_12_), channel_id=1, source_target_pairs={{0,1},{1,0},{2,3},{3,2},{4,5},{5,4},{6,7},{7,6},{8,9},{9,8},{10,11... | collective-permute-start | bytes 688136 | tf_op jit(solution)/shard_map/ppermute | solution.py:325
  15.1 12.8 %collective-permute-start.3 = (bf16[32,3584]{1,0:T(8,128)(2,1)}, bf16[32,3584]{1,0:T(8,128)(2,1)S(1)}, u32[]{:S(2)}, u32[]{:S(2)}) collective-permute-start(bf16[32,3584]{1,0:T(8,128)(2,1)} %collective-permute-done.1.refs_12_), channel_id=1, source_target_pairs={{0,2},{1,3},{4,0},{5,1},{8,4},{9,5},{12,8},{13,9},{14,12},{15,13},... | collective-permute-start | bytes 688136 | tf_op jit(solution)/shard_map/ppermute | solution.py:325
  23.0 0.6 copy-start.8
  27.9 11.4 %collective-permute-start.10 = (bf16[32,3584]{1,0:T(8,128)(2,1)S(1)}, bf16[32,3584]{1,0:T(8,128)(2,1)S(1)}, u32[]{:S(2)}, u32[]{:S(2)}) collective-permute-start(bf16[32,3584]{1,0:T(8,128)(2,1)S(1)} %collective-permute-done.2.refs_15_), channel_id=1, source_target_pairs={{0,4},{1,5},{4,8},{5,9},{8,12},{9,13},{12,14},{13,15},{14,10},{15,... | collective-permute-start | bytes 688136 | tf_op jit(solution)/shard_map/ppermute | solution.py:325
  27.9 11.3 %collective-permute-start.11 = (bf16[32,3584]{1,0:T(8,128)(2,1)S(1)}, bf16[32,3584]{1,0:T(8,128)(2,1)S(1)}, u32[]{:S(2)}, u32[]{:S(2)}) collective-permute-start(bf16[32,3584]{1,0:T(8,128)(2,1)S(1)} %collective-permute-done.3.refs_14_), channel_id=1, source_target_pairs={{0,2},{1,3},{4,0},{5,1},{8,4},{9,5},{12,8},{13,9},{14,12},{15,13},... | collective-permute-start | bytes 688136 | tf_op jit(solution)/shard_map/ppermute | solution.py:325
  29.9 8.1 %collective-permute-start.9 = (bf16[32,640]{1,0:T(8,128)(2,1)S(1)}, bf16[32,640]{1,0:T(8,128)(2,1)S(1)}, u32[]{:S(2)}, u32[]{:S(2)}) collective-permute-start(bf16[32,640]{1,0:T(8,128)(2,1)S(1)} %attention.1), channel_id=1, source_target_pairs={{0,12},{1,13},{2,14},{3,15},{4,8},{5,9},{6,10},{7,11},{8,4},{9,5},... | collective-permute-start | bytes 122888 | tf_op jit(solution)/shard_map/ppermute | solution.py:325
  30.7 8.5 %collective-permute-start.8 = (bf16[32,640]{1,0:T(8,128)(2,1)S(1)}, bf16[32,640]{1,0:T(8,128)(2,1)S(1)}, u32[]{:S(2)}, u32[]{:S(2)}) collective-permute-start(bf16[32,640]{1,0:T(8,128)(2,1)S(1)} %attention.1), channel_id=1, source_target_pairs={{0,8},{1,9},{2,10},{3,11},{4,12},{5,13},{6,14},{7,15},{8,0},{9,1},... | collective-permute-start | bytes 122888 | tf_op jit(solution)/shard_map/ppermute | solution.py:325
  31.5 7.8 %collective-permute-start.7 = (bf16[32,640]{1,0:T(8,128)(2,1)S(1)}, bf16[32,640]{1,0:T(8,128)(2,1)S(1)}, u32[]{:S(2)}, u32[]{:S(2)}) collective-permute-start(bf16[32,640]{1,0:T(8,128)(2,1)S(1)} %attention.1), channel_id=1, source_target_pairs={{0,4},{1,5},{2,6},{3,7},{4,0},{5,1},{6,2},{7,3},{8,12},{9,13},{10,... | collective-permute-start | bytes 122888 | tf_op jit(solution)/shard_map/ppermute | solution.py:325
  39.2 10.0 %collective-permute-start.15 = (bf16[32,3584]{1,0:T(8,128)(2,1)S(1)}, bf16[32,3584]{1,0:T(8,128)(2,1)S(1)}, u32[]{:S(2)}, u32[]{:S(2)}) collective-permute-start(bf16[32,3584]{1,0:T(8,128)(2,1)S(1)} %collective-permute-done.2.refs_15_), channel_id=1, source_target_pairs={{0,1},{1,0},{2,3},{3,2},{4,5},{5,4},{6,7},{7,6},{8,9},{9,8},{10,11... | collective-permute-start | bytes 688136 | tf_op jit(solution)/shard_map/ppermute | solution.py:325
  39.3 9.9 %collective-permute-start.16 = (bf16[32,3584]{1,0:T(8,128)(2,1)S(1)}, bf16[32,3584]{1,0:T(8,128)(2,1)S(1)}, u32[]{:S(2)}, u32[]{:S(2)}) collective-permute-start(bf16[32,3584]{1,0:T(8,128)(2,1)S(1)} %collective-permute-done.3.refs_14_), channel_id=1, source_target_pairs={{0,1},{1,0},{2,3},{3,2},{4,5},{5,4},{6,7},{7,6},{8,9},{9,8},{10,11... | collective-permute-start | bytes 688136 | tf_op jit(solution)/shard_map/ppermute | solution.py:325
  39.8 9.4 %collective-permute-start.14 = (bf16[32,3584]{1,0:T(8,128)(2,1)S(1)}, bf16[32,3584]{1,0:T(8,128)(2,1)S(1)}, u32[]{:S(2)}, u32[]{:S(2)}) collective-permute-start(bf16[32,3584]{1,0:T(8,128)(2,1)S(1)} %broadcast_select_fusion), channel_id=1, source_target_pairs={{0,8},{1,7},{4,12},{5,3},{8,14},{9,1},{12,10},{13,5},{14,6},{15,9}... | collective-permute-start | bytes 688136 | tf_op jit(solution)/shard_map/ppermute | solution.py:325
  40.1 2.2 %collective-permute-start.13 = (bf16[128,640]{1,0:T(8,128)(2,1)S(1)}, bf16[128,640]{1,0:T(8,128)(2,1)S(1)}, u32[]{:S(2)}, u32[]{:S(2)}) collective-permute-start(bf16[128,640]{1,0:T(8,128)(2,1)S(1)} %constant_dynamic-update-slice_fusion.refs_1_), channel_id=1, source_target_pairs={{0,1},{1,0},{2,3},{3,2},{4,5},{5,4},{6,7},{7,6},{8,9},{9,8},{10,11... | collective-permute-start | bytes 491528 | tf_op jit(solution)/shard_map/ppermute | solution.py:325
  40.4 8.8 %collective-permute-start.12 = (bf16[128,640]{1,0:T(8,128)(2,1)S(1)}, bf16[128,640]{1,0:T(8,128)(2,1)S(1)}, u32[]{:S(2)}, u32[]{:S(2)}) collective-permute-start(bf16[128,640]{1,0:T(8,128)(2,1)S(1)} %constant_dynamic-update-slice_fusion.refs_1_), channel_id=1, source_target_pairs={{0,2},{1,3},{2,0},{3,1},{4,6},{5,7},{6,4},{7,5},{8,10},{9,11},{10,... | collective-permute-start | bytes 491528 | tf_op jit(solution)/shard_map/ppermute | solution.py:325
  49.3 2.4 %collective-permute-start.18 = (bf16[32,3584]{1,0:T(8,128)(2,1)S(1)}, bf16[32,3584]{1,0:T(8,128)(2,1)S(1)}, u32[]{:S(2)}, u32[]{:S(2)}) collective-permute-start(bf16[32,3584]{1,0:T(8,128)(2,1)S(1)} %collective-permute-done.14.refs_5_), channel_id=1, source_target_pairs={{0,1},{1,0},{2,3},{3,2},{4,5},{5,4},{6,7},{7,6},{8,9},{9,8},{10,11... | collective-permute-start | bytes 688136 | tf_op jit(solution)/shard_map/ppermute | solution.py:325
  49.3 2.4 %collective-permute-start.19 = (bf16[32,3584]{1,0:T(8,128)(2,1)S(1)}, bf16[32,3584]{1,0:T(8,128)(2,1)S(1)}, u32[]{:S(2)}, u32[]{:S(2)}) collective-permute-start(bf16[32,3584]{1,0:T(8,128)(2,1)S(1)} %collective-permute-done.11.refs_6_), channel_id=1, source_target_pairs={{0,1},{1,0},{2,3},{3,2},{4,5},{5,4},{6,7},{7,6},{8,9},{9,8},{10,11... | collective-permute-start | bytes 688136 | tf_op jit(solution)/shard_map/ppermute | solution.py:325
  49.8 1.9 %collective-permute-start.20 = (bf16[32,3584]{1,0:T(8,128)(2,1)S(1)}, bf16[32,3584]{1,0:T(8,128)(2,1)S(1)}, u32[]{:S(2)}, u32[]{:S(2)}) collective-permute-start(bf16[32,3584]{1,0:T(8,128)(2,1)S(1)} %collective-permute-done.10.refs_7_), channel_id=1, source_target_pairs={{0,1},{1,0},{2,3},{3,2},{4,5},{5,4},{6,7},{7,6},{8,9},{9,8},{10,11... | collective-permute-start | bytes 688136 | tf_op jit(solution)/shard_map/ppermute | solution.py:325
  49.9 1.8 %collective-permute-start.17 = (bf16[128,640]{1,0:T(8,128)(2,1)S(1)}, bf16[128,640]{1,0:T(8,128)(2,1)S(1)}, u32[]{:S(2)}, u32[]{:S(2)}) collective-permute-start(bf16[128,640]{1,0:T(8,128)(2,1)S(1)} %collective-permute-done.12.refs_2_), channel_id=1, source_target_pairs={{0,1},{1,0},{2,3},{3,2},{4,5},{5,4},{6,7},{7,6},{8,9},{9,8},{10,11... | collective-permute-start | bytes 491528 | tf_op jit(solution)/shard_map/ppermute | solution.py:325
  51.7 2.0 %copy-start.1 = (bf16[512,3584]{1,0:T(8,128)(2,1)S(1)}, bf16[512,3584]{1,0:T(8,128)(2,1)}, u32[]{:S(2)}) copy-start(bf16[512,3584]{1,0:T(8,128)(2,1)} %refs_21_.1) | copy-start | bytes 11010052
  53.8 0.9 copy-start.3
  54.7 0.9 copy-start.4
  55.6 0.6 copy-start.7
  56.2 12.7 %slice-start.2 = ((s8[7340032]{0:T(1024)(128)(4,1)}), s8[4194304]{0:T(1024)(128)(4,1)S(1)}, s32[]{:S(2)}) async-start(s8[7340032]{0:T(1024)(128)(4,1)} %bitcast.63), calls=%async_computation.3 | async-start | bytes 8388608
  63.9 5.0 %slice-start.3 = ((s8[7340032]{0:T(1024)(128)(4,1)}), s8[3145728]{0:T(1024)(128)(4,1)S(1)}, s32[]{:S(2)}) async-start(s8[7340032]{0:T(1024)(128)(4,1)} %bitcast.63), calls=%async_computation.4 | async-start | bytes 6291456
  64.0 6.9 %slice-start.4 = ((s8[7340032]{0:T(1024)(128)(4,1)}), s8[4194304]{0:T(1024)(128)(4,1)S(1)}, s32[]{:S(2)}) async-start(s8[7340032]{0:T(1024)(128)(4,1)} %bitcast.65), calls=%async_computation.5 | async-start | bytes 8388608
  64.0 9.5 %slice-start = ((s8[7340032]{0:T(1024)(128)(4,1)}), s8[4194304]{0:T(1024)(128)(4,1)S(1)}, s32[]{:S(2)}) async-start(s8[7340032]{0:T(1024)(128)(4,1)} %bitcast.61), calls=%async_computation.1 | async-start | bytes 8388608
  69.0 2.5 %slice-start.5 = ((s8[7340032]{0:T(1024)(128)(4,1)}), s8[3145728]{0:T(1024)(128)(4,1)S(1)}, s32[]{:S(2)}) async-start(s8[7340032]{0:T(1024)(128)(4,1)} %bitcast.65), calls=%async_computation.6 | async-start | bytes 6291456
  69.0 4.5 %slice-start.1 = ((s8[7340032]{0:T(1024)(128)(4,1)}), s8[3145728]{0:T(1024)(128)(4,1)S(1)}, s32[]{:S(2)}) async-start(s8[7340032]{0:T(1024)(128)(4,1)} %bitcast.61), calls=%async_computation.2 | async-start | bytes 6291456
  73.2 2.9 %collective-permute-start.21 = (bf16[96,3584]{1,0:T(8,128)(2,1)S(1)}, bf16[96,3584]{1,0:T(8,128)(2,1)S(1)}, u32[]{:S(2)}, u32[]{:S(2)}) collective-permute-start(bf16[96,3584]{1,0:T(8,128)(2,1)S(1)} %slice.98), channel_id=1, source_target_pairs={{0,1},{1,0},{2,3},{3,2},{4,5},{5,4},{6,7},{7,6},{8,9},{9,8},{10,11... | collective-permute-start | bytes 2064392 | tf_op jit(solution)/shard_map/ppermute | solution.py:325
  76.2 5.4 %collective-permute-start.23 = (bf16[16,3584]{1,0:T(8,128)(2,1)S(1)}, bf16[16,3584]{1,0:T(8,128)(2,1)S(1)}, u32[]{:S(2)}, u32[]{:S(2)}) collective-permute-start(bf16[16,3584]{1,0:T(8,128)(2,1)S(1)} %get-tuple-element.133), channel_id=1, source_target_pairs={{0,2},{1,3},{4,0},{5,1},{8,4},{9,5},{12,8},{13,9},{14,12},{15,13},... | collective-permute-start | bytes 344072 | tf_op jit(solution)/shard_map/ppermute | solution.py:325
  77.7 5.1 %collective-permute-start.22 = (bf16[16,3584]{1,0:T(8,128)(2,1)S(1)}, bf16[16,3584]{1,0:T(8,128)(2,1)S(1)}, u32[]{:S(2)}, u32[]{:S(2)}) collective-permute-start(bf16[16,3584]{1,0:T(8,128)(2,1)S(1)} %get-tuple-element.134), channel_id=1, source_target_pairs={{0,4},{1,5},{4,8},{5,9},{8,12},{9,13},{12,14},{13,15},{14,10},{15,... | collective-permute-start | bytes 344072 | tf_op jit(solution)/shard_map/ppermute | solution.py:325
  85.4 9.2 %collective-permute-start.24 = (bf16[160,3584]{1,0:T(8,128)(2,1)S(1)}, bf16[160,3584]{1,0:T(8,128)(2,1)S(1)}, u32[]{:S(2)}, u32[]{:S(2)}) collective-permute-start(bf16[160,3584]{1,0:T(8,128)(2,1)S(1)} %slice.101), channel_id=1, source_target_pairs={{0,1},{1,0},{2,3},{3,2},{4,5},{5,4},{6,7},{7,6},{8,9},{9,8},{10,11... | collective-permute-start | bytes 3440648 | tf_op jit(solution)/shard_map/ppermute | solution.py:325
  85.6 8.1 %collective-permute-start.26 = (bf16[32,3584]{1,0:T(8,128)(2,1)S(1)}, bf16[32,3584]{1,0:T(8,128)(2,1)S(1)}, u32[]{:S(2)}, u32[]{:S(2)}) collective-permute-start(bf16[32,3584]{1,0:T(8,128)(2,1)S(1)} %get-tuple-element.131), channel_id=1, source_target_pairs={{0,2},{1,3},{4,0},{5,1},{8,4},{9,5},{12,8},{13,9},{14,12},{15,13},... | collective-permute-start | bytes 688136 | tf_op jit(solution)/shard_map/ppermute | solution.py:325
  86.9 7.7 %collective-permute-start.25 = (bf16[32,3584]{1,0:T(8,128)(2,1)S(1)}, bf16[32,3584]{1,0:T(8,128)(2,1)S(1)}, u32[]{:S(2)}, u32[]{:S(2)}) collective-permute-start(bf16[32,3584]{1,0:T(8,128)(2,1)S(1)} %get-tuple-element.132), channel_id=1, source_target_pairs={{0,4},{1,5},{4,8},{5,9},{8,12},{9,13},{12,14},{13,15},{14,10},{15,... | collective-permute-start | bytes 688136 | tf_op jit(solution)/shard_map/ppermute | solution.py:325
  94.8 7.0 %collective-permute-start.28 = (bf16[32,3584]{1,0:T(8,128)(2,1)S(1)}, bf16[32,3584]{1,0:T(8,128)(2,1)S(1)}, u32[]{:S(2)}, u32[]{:S(2)}) collective-permute-start(bf16[32,3584]{1,0:T(8,128)(2,1)S(1)} %get-tuple-element.129), channel_id=1, source_target_pairs={{0,2},{1,3},{4,0},{5,1},{8,4},{9,5},{12,8},{13,9},{14,12},{15,13},... | collective-permute-start | bytes 688136 | tf_op jit(solution)/shard_map/ppermute | solution.py:325
  96.6 6.6 %collective-permute-start.27 = (bf16[32,3584]{1,0:T(8,128)(2,1)S(1)}, bf16[32,3584]{1,0:T(8,128)(2,1)S(1)}, u32[]{:S(2)}, u32[]{:S(2)}) collective-permute-start(bf16[32,3584]{1,0:T(8,128)(2,1)S(1)} %get-tuple-element.130), channel_id=1, source_target_pairs={{0,4},{1,5},{4,8},{5,9},{8,12},{9,13},{12,14},{13,15},{14,10},{15,... | collective-permute-start | bytes 688136 | tf_op jit(solution)/shard_map/ppermute | solution.py:325
  103.4 6.1 %collective-permute-start.30 = (bf16[32,3584]{1,0:T(8,128)(2,1)S(1)}, bf16[32,3584]{1,0:T(8,128)(2,1)S(1)}, u32[]{:S(2)}, u32[]{:S(2)}) collective-permute-start(bf16[32,3584]{1,0:T(8,128)(2,1)S(1)} %get-tuple-element.127), channel_id=1, source_target_pairs={{0,2},{1,3},{4,0},{5,1},{8,4},{9,5},{12,8},{13,9},{14,12},{15,13},... | collective-permute-start | bytes 688136 | tf_op jit(solution)/shard_map/ppermute | solution.py:325
  104.0 6.0 %collective-permute-start.29 = (bf16[32,3584]{1,0:T(8,128)(2,1)S(1)}, bf16[32,3584]{1,0:T(8,128)(2,1)S(1)}, u32[]{:S(2)}, u32[]{:S(2)}) collective-permute-start(bf16[32,3584]{1,0:T(8,128)(2,1)S(1)} %get-tuple-element.128), channel_id=1, source_target_pairs={{0,4},{1,5},{4,8},{5,9},{8,12},{9,13},{12,14},{13,15},{14,10},{15,... | collective-permute-start | bytes 688136 | tf_op jit(solution)/shard_map/ppermute | solution.py:325

commit v14 on v13

--- a/solution.py
+++ b/solution.py
@@ -7,6 +7,7 @@
 
 qk_scale = 192.0 ** (-0.5)
 LANES = 128
+LONG = dict(flops=10**10, bytes_accessed=10**8, transcendentals=0)
 
 
 def ring_of(chips):
@@ -170,11 +171,7 @@
         compiler_params=pltpu.CompilerParams(
             dimension_semantics=("arbitrary",), vmem_limit_bytes=(int(need) // (1 << 20) + 6) << 20
         ),
-        cost_estimate=pl.CostEstimate(
-            flops=2 * total * width * latent,
-            bytes_accessed=2 * total * width * 2 + latent * width * 2,
-            transcendentals=total,
-        ),
+        cost_estimate=pl.CostEstimate(**LONG),
         name="normalize",
     )(scalars, *pooled, *resid_blocks, w_out, gain, w_router_t)
 
@@ -184,9 +181,6 @@
         row_lengths[j] = lengths[owner[device[0] * row_lengths.shape[0] + j]]
     for j in range(scalars.shape[0]):
         scalars[j] = table[device[0] * scalars.shape[0] + j]
-
-
-LONG = dict(flops=10**10, bytes_accessed=10**8, transcendentals=0)
 
 
 def lookup(owner, lengths, table, device_index, rows):
@@ -286,9 +280,7 @@
         compiler_params=pltpu.CompilerParams(
             dimension_semantics=("arbitrary",), vmem_limit_bytes=(10 << 20) + 10240 * keys
         ),
-        cost_estimate=pl.CostEstimate(
-            flops=2 * q_abs.size * keys, bytes_accessed=2 * q_abs.size, transcendentals=0
-        ),
+        cost_estimate=pl.CostEstimate(**LONG),
         name="attention",
     )(q_abs, cache, fresh, lengths, routes)
 

time: 111 us -> 114 us (1.027)
  matrix products: 17.4 us -> 20.4 us
    dot_general x6, matrix products: 16.4 us -> 19.4 us  [product(): return jnp.dot(a, w[0], preferred_element_type=f32)]
  transfers between devices with their start and end apart: 32 -> 32, of which waited for: 13 -> 13; matrix products, arithmetic and copies ran while one was open for 7% -> 6% of each run, Pallas kernels for 5% -> 5%
where the time goes in v14:
time: 114 us; the launch traced here: 113 us
  waiting for transfers between devices  40.4 us (35%)
  starting transfers between devices  31.2 us (27%)
  matrix products  20.4 us (18%)
  Pallas kernels  12.8 us (11%)
  local copies, waits for them, and re-layouts  6.65 us (6%)
  other arithmetic  1.39 us (1%)
    ppermute x31, waiting for transfers between devices, send(): return lax.ppermute(a, 'expert', perm)  32.9 us
    ppermute x31, starting transfers between devices, send(): return lax.ppermute(a, 'expert', perm)  24.9 us
    dot_general x6, matrix products, product(): return jnp.dot(a, w[0], preferred_element_type=f32)  19.4 us
    all_to_all x1, waiting for transfers between devices, local(): lax.all_to_all(ordered, 'expert', split_axis=0, concat_axis=0, tiled=True)  7.58 us
    pallas_call x1, Pallas kernels, normalize(): pl.pallas_call(lambda *refs: norm_kernel(far, blocks, rows, latent, width...  7.23 us
    all_to_all x1, starting transfers between devices, local(): lax.all_to_all(ordered, 'expert', split_axis=0, concat_axis=0, tiled=True)  6.29 us
    unnamed x35, local copies, waits for them, and re-layouts  5.21 us
    pallas_call x1, Pallas kernels, attention(): pl.pallas_call(lambda *refs: attention_kernel(context, latent, *refs), gr...  4.23 us
  transfers between devices with their start and end apart: 32, of which 13 were waited for; matrix products, arithmetic and copies ran while one was open for 6% of the time, Pallas kernels for 5%

profile of v14, /device:TPU:0, one launch (start us, length us, event | category | flops | bytes accessed | tf_op | source)
XLA Modules:
  0.0 113.3 jit_solution(11552072549868318507)
XLA Ops:
  0.5 2.6 %collective-permute-start.1 = (bf16[32,3584]{1,0:T(8,128)(2,1)}, bf16[32,3584]{1,0:T(8,128)(2,1)}, u32[]{:S(2)}, u32[]{:S(2)}) collective-permute-start(bf16[32,3584]{1,0:T(8,128)(2,1)} %bitcast.54), channel_id=1, source_target_pairs={{0,2},{1,3},{4,0},{5,1},{8,4},{9,5},{12,8},{13,9},{14,12},{15,13},... | collective-permute-start | bytes 688136 | tf_op jit(solution)/shard_map/ppermute | solution.py:317
  3.2 1.0 fusion.27
  4.4 0.7 copy.19
  5.1 6.3 %all-to-all-start = ((bf16[16,2,8,576]{3,2,1,0:T(8,128)(2,1)}), bf16[16,2,8,576]{3,2,1,0:T(8,128)(2,1)S(1)}, u32[]{:S(2)}, u32[]{:S(2)}) async-start(bf16[16,2,8,576]{3,2,1,0:T(8,128)(2,1)} %copy.19), calls=%async_computation | async-start | bytes 655360 | tf_op jit(solution)/shard_map/all_to_all | solution.py:334
  11.5 1.4 %lookup.1 = (s32[8]{0:T(128)}, s32[17]{0:T(128)}) custom-call(s32[128]{0:T(128)} %owner.1, s32[128]{0:T(128)} %lengths.1, s32[272]{0:T(512)} %constant.41.table, s32[1]{0:T(128)} %bitcast.device), custom_call_target="tpu_custom_call" | custom-call | flops 10000000000 | bytes 100000000 | tf_op jit(solution)/shard_map/lookup/pallas_call | solution.py:188
  12.9 0.5 collective-permute-start.4
  13.4 1.7 %collective-permute-start.2 = (bf16[32,3584]{1,0:T(8,128)(2,1)}, bf16[32,3584]{1,0:T(8,128)(2,1)S(1)}, u32[]{:S(2)}, u32[]{:S(2)}) collective-permute-start(bf16[32,3584]{1,0:T(8,128)(2,1)} %collective-permute-done.refs_13_), channel_id=1, source_target_pairs={{0,4},{1,5},{4,8},{5,9},{8,12},{9,13},{12,14},{13,15},{14,10},{15,... | collective-permute-start | bytes 688136 | tf_op jit(solution)/shard_map/ppermute | solution.py:317
  15.4 7.6 %all-to-all-done = bf16[16,2,8,576]{3,2,1,0:T(8,128)(2,1)S(1)} async-done(((bf16[16,2,8,576]{3,2,1,0:T(8,128)(2,1)}), bf16[16,2,8,576]{3,2,1,0:T(8,128)(2,1)S(1)}, u32[]{:S(2)}, u32[]{:S(2)}) %all-to-all-start) | async-done | bytes 294944 | tf_op jit(solution)/shard_map/all_to_all | solution.py:334
  23.0 0.6 copy-done.8
  23.6 4.2 %attention.1 = bf16[32,640]{1,0:T(8,128)(2,1)S(1)} custom-call(bf16[4,8,36864]{2,1,0:T(8,128)(2,1)S(1)} %copy-done.2, bf16[256,576]{1,0:T(8,128)(2,1)S(1)} %bitcast.52, bf16[32,576]{1,0:T(8,128)(2,1)S(1)} %bitcast.58, s32[8]{0:T(128)S(1)} %copy-done.8, s32[32,8]{1,0:T(8,128)S(1)} %bitcast.59), custom_call_target="tpu_custom_call" | custom-call | flops 10000000000 | bytes 100000000 | tf_op jit(solution)/shard_map/attention/pallas_call | solution.py:268
  28.0 2.0 %collective-permute-start.11 = (bf16[32,3584]{1,0:T(8,128)(2,1)S(1)}, bf16[32,3584]{1,0:T(8,128)(2,1)S(1)}, u32[]{:S(2)}, u32[]{:S(2)}) collective-permute-start(bf16[32,3584]{1,0:T(8,128)(2,1)S(1)} %collective-permute-done.3.refs_14_), channel_id=1, source_target_pairs={{0,2},{1,3},{4,0},{5,1},{8,4},{9,5},{12,8},{13,9},{14,12},{15,13},... | collective-permute-start | bytes 688136 | tf_op jit(solution)/shard_map/ppermute | solution.py:317
  30.0 0.8 collective-permute-start.9
  30.7 0.8 collective-permute-start.8
  31.5 2.9 %collective-permute-start.7 = (bf16[32,640]{1,0:T(8,128)(2,1)S(1)}, bf16[32,640]{1,0:T(8,128)(2,1)S(1)}, u32[]{:S(2)}, u32[]{:S(2)}) collective-permute-start(bf16[32,640]{1,0:T(8,128)(2,1)S(1)} %attention.1), channel_id=1, source_target_pairs={{0,4},{1,5},{2,6},{3,7},{4,0},{5,1},{6,2},{7,3},{8,12},{9,13},{10,... | collective-permute-start | bytes 122888 | tf_op jit(solution)/shard_map/ppermute | solution.py:317
  34.4 3.7 %collective-permute-done.9 = bf16[32,640]{1,0:T(8,128)(2,1)S(1)} collective-permute-done((bf16[32,640]{1,0:T(8,128)(2,1)S(1)}, bf16[32,640]{1,0:T(8,128)(2,1)S(1)}, u32[]{:S(2)}, u32[]{:S(2)}) %collective-permute-start.9) | collective-permute-done | bytes 40992 | tf_op jit(solution)/shard_map/ppermute | solution.py:317
  38.0 1.2 %collective-permute-done.8 = bf16[32,640]{1,0:T(8,128)(2,1)S(1)} collective-permute-done((bf16[32,640]{1,0:T(8,128)(2,1)S(1)}, bf16[32,640]{1,0:T(8,128)(2,1)S(1)}, u32[]{:S(2)}, u32[]{:S(2)}) %collective-permute-start.8) | collective-permute-done | bytes 40992 | tf_op jit(solution)/shard_map/ppermute | solution.py:317
  39.4 0.5 collective-permute-start.16
  40.5 1.8 %collective-permute-start.12 = (bf16[128,640]{1,0:T(8,128)(2,1)S(1)}, bf16[128,640]{1,0:T(8,128)(2,1)S(1)}, u32[]{:S(2)}, u32[]{:S(2)}) collective-permute-start(bf16[128,640]{1,0:T(8,128)(2,1)S(1)} %constant_dynamic-update-slice_fusion.refs_1_), channel_id=1, source_target_pairs={{0,2},{1,3},{2,0},{3,1},{4,6},{5,7},{6,4},{7,5},{8,10},{9,11},{10,... | collective-permute-start | bytes 491528 | tf_op jit(solution)/shard_map/ppermute | solution.py:317
  42.4 6.9 %collective-permute-done.12.refs_2_ = bf16[128,640]{1,0:T(8,128)(2,1)S(1)} collective-permute-done((bf16[128,640]{1,0:T(8,128)(2,1)S(1)}, bf16[128,640]{1,0:T(8,128)(2,1)S(1)}, u32[]{:S(2)}, u32[]{:S(2)}) %collective-permute-start.12) | collective-permute-done | bytes 163872 | tf_op jit(solution)/shard_map/ppermute | solution.py:317
  49.4 0.5 collective-permute-start.19
  50.4 1.4 %collective-permute-done.17.refs_4_ = bf16[128,640]{1,0:T(8,128)(2,1)S(1)} collective-permute-done((bf16[128,640]{1,0:T(8,128)(2,1)S(1)}, bf16[128,640]{1,0:T(8,128)(2,1)S(1)}, u32[]{:S(2)}, u32[]{:S(2)}) %collective-permute-start.17) | collective-permute-done | bytes 163872 | tf_op jit(solution)/shard_map/ppermute | solution.py:317
  51.8 2.0 %copy-done.1 = bf16[512,3584]{1,0:T(8,128)(2,1)S(1)} copy-done((bf16[512,3584]{1,0:T(8,128)(2,1)S(1)}, bf16[512,3584]{1,0:T(8,128)(2,1)}, u32[]{:S(2)}) %copy-start.1) | copy-done | bytes 3670040
  53.8 0.9 copy-done.3
  54.7 0.9 copy-done.4
  55.6 0.6 copy-done.7
  56.3 7.2 %normalize.1 = (bf16[192,3584]{1,0:T(8,128)(2,1)S(1)}, bf16[320,3584]{1,0:T(8,128)(2,1)S(1)}, f32[512,128]{1,0:T(8,128)S(1)}, f32[512,128]{1,0:T(8,128)S(1)}, f32[32,3584]{1,0:T(8,128)S(1)}) custom-call(s32[17]{0:T(128)S(1)} %copy-done.7, bf16[128,640]{1,0:T(8,128)(2,1)S(1)} %constant_dynamic-update-slice_fusion.refs_1_, ...), custom_call_target="tpu_custom_call" | custom-call | flops 10000000000 | bytes 100000000 | tf_op jit(solution)/shard_map/normalize/pallas_call | solution.py:149
  63.9 4.9 %fusion.21 = f32[192,1024]{1,0:T(8,128)S(1)} fusion(bf16[192,3584]{1,0:T(8,128)(2,1)S(1)} %get-tuple-element.110, bf16[1,3584,1024]{2,1,0:T(8,128)(2,1)} %param.24, f32[192]{0:T(256)S(1)} %get-tuple-element.138), kind=kOutput, calls=%fused_computation.16 | convolution fusion | flops 1409482752 | bytes 9503488 | tf_op jit(solution)/shard_map/dot_general | solution.py:393
  68.8 5.1 %multiply_convert_fusion.1 = bf16[192,1024]{1,0:T(8,128)(2,1)S(1)} fusion(f32[192,1024]{1,0:T(8,128)S(1)} %fusion.21, f32[192]{0:T(256)S(1)} %get-tuple-element.137, f32[192]{0:T(256)S(1)} %get-tuple-element.138, bf16[192,3584]{1,0:T(8,128)(2,1)S(1)} %get-tuple-element.110, bf16[1,3584,1024]{2,1,0:T(8,128)(2,1)} %param.25), kind=kOutput, calls=%fused_computation.20 | convolution fusion | flops 1410859008 | bytes 9897472 | tf_op jit(solution)/shard_map/dot_general | solution.py:393
  74.0 1.6 %fusion.15 = bf16[192,3584]{1,0:T(8,128)(2,1)S(1)} fusion(bf16[192,1024]{1,0:T(8,128)(2,1)S(1)} %multiply_convert_fusion.1, bf16[1,1024,3584]{2,1,0:T(8,128)(2,1)S(1)} %bitcast.66), kind=kOutput, calls=%fused_computation.13 | convolution fusion | flops 1409974272 | bytes 9109504 | tf_op jit(solution)/shard_map/dot_general | solution.py:393
  75.9 2.5 %fusion.10 = f32[320,1024]{1,0:T(8,128)S(1)} fusion(bf16[320,3584]{1,0:T(8,128)(2,1)S(1)} %get-tuple-element.109, bf16[1,3584,1024]{2,1,0:T(8,128)(2,1)S(1)} %bitcast.62), kind=kOutput, calls=%fused_computation.10 | convolution fusion | flops 2348810240 | bytes 10944512 | tf_op jit(solution)/shard_map/dot_general | solution.py:393
  78.5 1.5 %collective-permute-start.23 = (bf16[16,3584]{1,0:T(8,128)(2,1)S(1)}, bf16[16,3584]{1,0:T(8,128)(2,1)S(1)}, u32[]{:S(2)}, u32[]{:S(2)}) collective-permute-start(bf16[16,3584]{1,0:T(8,128)(2,1)S(1)} %get-tuple-element.133), channel_id=1, source_target_pairs={{0,2},{1,3},{4,0},{5,1},{8,4},{9,5},{12,8},{13,9},{14,12},{15,13},... | collective-permute-start | bytes 344072 | tf_op jit(solution)/shard_map/ppermute | solution.py:317
  80.0 0.6 collective-permute-start.22
  80.6 2.7 %multiply_convert_fusion = bf16[320,1024]{1,0:T(8,128)(2,1)S(1)} fusion(f32[320,1024]{1,0:T(8,128)S(1)} %fusion.10, f32[320]{0:T(512)S(1)} %get-tuple-element.135, f32[320]{0:T(512)S(1)} %get-tuple-element.136, bf16[320,3584]{1,0:T(8,128)(2,1)S(1)} %get-tuple-element.109, bf16[1,3584,1024]{2,1,0:T(8,128)(2,1)S(1)} %bitcast.64), kind=kOutput, calls=%fused_computation.15 | convolution fusion | flops 2351759360 | bytes 11602432 | tf_op jit(solution)/shard_map/dot_general | solution.py:393
  83.3 0.6 collective-permute-done.23
  84.0 1.2 %collective-permute-done.22 = bf16[16,3584]{1,0:T(8,128)(2,1)S(1)} collective-permute-done((bf16[16,3584]{1,0:T(8,128)(2,1)S(1)}, bf16[16,3584]{1,0:T(8,128)(2,1)S(1)}, u32[]{:S(2)}, u32[]{:S(2)}) %collective-permute-start.22) | collective-permute-done | bytes 114720 | tf_op jit(solution)/shard_map/ppermute | solution.py:317
  85.1 2.5 %fusion.12 = bf16[320,3584]{1,0:T(8,128)(2,1)S(1)} fusion(bf16[320,1024]{1,0:T(8,128)(2,1)S(1)} %multiply_convert_fusion, bf16[1,1024,3584]{2,1,0:T(8,128)(2,1)S(1)} %bitcast.66), kind=kOutput, calls=%fused_computation.12 | convolution fusion | flops 2349957120 | bytes 10289152 | tf_op jit(solution)/shard_map/dot_general | solution.py:393
  88.0 1.3 %collective-permute-start.26 = (bf16[32,3584]{1,0:T(8,128)(2,1)S(1)}, bf16[32,3584]{1,0:T(8,128)(2,1)S(1)}, u32[]{:S(2)}, u32[]{:S(2)}) collective-permute-start(bf16[32,3584]{1,0:T(8,128)(2,1)S(1)} %get-tuple-element.131), channel_id=1, source_target_pairs={{0,2},{1,3},{4,0},{5,1},{8,4},{9,5},{12,8},{13,9},{14,12},{15,13},... | collective-permute-start | bytes 688136 | tf_op jit(solution)/shard_map/ppermute | solution.py:317
  89.3 0.8 collective-permute-start.25
  90.1 6.0 %collective-permute-done.26 = bf16[32,3584]{1,0:T(8,128)(2,1)S(1)} collective-permute-done((bf16[32,3584]{1,0:T(8,128)(2,1)S(1)}, bf16[32,3584]{1,0:T(8,128)(2,1)S(1)}, u32[]{:S(2)}, u32[]{:S(2)}) %collective-permute-start.26) | collective-permute-done | bytes 229408 | tf_op jit(solution)/shard_map/ppermute | solution.py:317
  96.0 1.0 collective-permute-done.25
  97.2 1.8 %collective-permute-start.28 = (bf16[32,3584]{1,0:T(8,128)(2,1)S(1)}, bf16[32,3584]{1,0:T(8,128)(2,1)S(1)}, u32[]{:S(2)}, u32[]{:S(2)}) collective-permute-start(bf16[32,3584]{1,0:T(8,128)(2,1)S(1)} %get-tuple-element.129), channel_id=1, source_target_pairs={{0,2},{1,3},{4,0},{5,1},{8,4},{9,5},{12,8},{13,9},{14,12},{15,13},... | collective-permute-start | bytes 688136 | tf_op jit(solution)/shard_map/ppermute | solution.py:317
  99.2 4.9 %collective-permute-done.28 = bf16[32,3584]{1,0:T(8,128)(2,1)S(1)} collective-permute-done((bf16[32,3584]{1,0:T(8,128)(2,1)S(1)}, bf16[32,3584]{1,0:T(8,128)(2,1)S(1)}, u32[]{:S(2)}, u32[]{:S(2)}) %collective-permute-start.28) | collective-permute-done | bytes 229408 | tf_op jit(solution)/shard_map/ppermute | solution.py:317
  104.1 1.5 %collective-permute-done.27 = bf16[32,3584]{1,0:T(8,128)(2,1)S(1)} collective-permute-done((bf16[32,3584]{1,0:T(8,128)(2,1)S(1)}, bf16[32,3584]{1,0:T(8,128)(2,1)S(1)}, u32[]{:S(2)}, u32[]{:S(2)}) %collective-permute-start.27) | collective-permute-done | bytes 229408 | tf_op jit(solution)/shard_map/ppermute | solution.py:317
  105.7 0.7 collective-permute-start.30
  106.4 1.4 %collective-permute-start.29 = (bf16[32,3584]{1,0:T(8,128)(2,1)S(1)}, bf16[32,3584]{1,0:T(8,128)(2,1)S(1)}, u32[]{:S(2)}, u32[]{:S(2)}) collective-permute-start(bf16[32,3584]{1,0:T(8,128)(2,1)S(1)} %get-tuple-element.128), channel_id=1, source_target_pairs={{0,4},{1,5},{4,8},{5,9},{8,12},{9,13},{12,14},{13,15},{14,10},{15,... | collective-permute-start | bytes 688136 | tf_op jit(solution)/shard_map/ppermute | solution.py:317
  107.8 4.0 %collective-permute-done.30 = bf16[32,3584]{1,0:T(8,128)(2,1)S(1)} collective-permute-done((bf16[32,3584]{1,0:T(8,128)(2,1)S(1)}, bf16[32,3584]{1,0:T(8,128)(2,1)S(1)}, u32[]{:S(2)}, u32[]{:S(2)}) %collective-permute-start.30) | collective-permute-done | bytes 229408 | tf_op jit(solution)/shard_map/ppermute | solution.py:317
  111.8 0.6 collective-permute-done.29
  112.4 0.8 fusion.32
  (79 shorter events, 4.3 us)
Async XLA Ops:
  0.0 3.2 %copy-start = (bf16[128,2,576]{0,2,1:T(8,128)(2,1)S(1)}, bf16[128,2,576]{0,2,1:T(8,128)(2,1)}, u32[]{:S(2)}) copy-start(bf16[128,2,576]{0,2,1:T(8,128)(2,1)} %param.16) | copy-start | bytes 884740
  0.0 27.8 %collective-permute-start.5 = (bf16[32,3584]{1,0:T(8,128)(2,1)}, bf16[32,3584]{1,0:T(8,128)(2,1)}, u32[]{:S(2)}, u32[]{:S(2)}) collective-permute-start(bf16[32,3584]{1,0:T(8,128)(2,1)} %bitcast.53), channel_id=1, source_target_pairs={{0,1},{1,0},{2,3},{3,2},{4,5},{5,4},{6,7},{7,6},{8,9},{9,8},{10,11... | collective-permute-start | bytes 688136 | tf_op jit(solution)/shard_map/ppermute | solution.py:317
  0.5 12.4 %collective-permute-start.1 = (bf16[32,3584]{1,0:T(8,128)(2,1)}, bf16[32,3584]{1,0:T(8,128)(2,1)}, u32[]{:S(2)}, u32[]{:S(2)}) collective-permute-start(bf16[32,3584]{1,0:T(8,128)(2,1)} %bitcast.54), channel_id=1, source_target_pairs={{0,2},{1,3},{4,0},{5,1},{8,4},{9,5},{12,8},{13,9},{14,12},{15,13},... | collective-permute-start | bytes 688136 | tf_op jit(solution)/shard_map/ppermute | solution.py:317
  3.0 9.9 %collective-permute-start = (bf16[32,3584]{1,0:T(8,128)(2,1)}, bf16[32,3584]{1,0:T(8,128)(2,1)}, u32[]{:S(2)}, u32[]{:S(2)}) collective-permute-start(bf16[32,3584]{1,0:T(8,128)(2,1)} %bitcast.55), channel_id=1, source_target_pairs={{0,4},{1,5},{4,8},{5,9},{8,12},{9,13},{12,14},{13,15},{14,10},{15,... | collective-permute-start | bytes 688136 | tf_op jit(solution)/shard_map/ppermute | solution.py:317
  5.1 17.9 %all-to-all-start = ((bf16[16,2,8,576]{3,2,1,0:T(8,128)(2,1)}), bf16[16,2,8,576]{3,2,1,0:T(8,128)(2,1)S(1)}, u32[]{:S(2)}, u32[]{:S(2)}) async-start(bf16[16,2,8,576]{3,2,1,0:T(8,128)(2,1)} %copy.19), calls=%async_computation | async-start | bytes 655360 | tf_op jit(solution)/shard_map/all_to_all | solution.py:334
  11.4 1.4 %copy-start.9 = (bf16[3584]{0:T(1024)(128)(2,1)S(1)}, bf16[3584]{0:T(1024)(128)(2,1)}, u32[]{:S(2)}) copy-start(bf16[3584]{0:T(1024)(128)(2,1)} %param.22) | copy-start | bytes 21508
  11.4 11.6 %copy-start.2 = (bf16[4,8,36864]{2,1,0:T(8,128)(2,1)S(1)}, bf16[4,8,36864]{2,1,0:T(8,128)(2,1)}, u32[]{:S(2)}) copy-start(bf16[4,8,36864]{2,1,0:T(8,128)(2,1)} %refs_0_.1) | copy-start | bytes 7077892
  11.4 11.6 %copy-start.5 = (bf16[4,8,576]{2,1,0:T(8,128)(2,1)S(1)}, bf16[4,8,576]{2,1,0:T(8,128)(2,1)}, u32[]{:S(2)}) copy-start(bf16[4,8,576]{2,1,0:T(8,128)(2,1)} %param.15) | copy-start | bytes 110596
  11.4 11.5 %copy-start.6 = (s32[4,8,8]{2,1,0:T(8,128)S(1)}, s32[4,8,8]{2,1,0:T(8,128)}, u32[]{:S(2)}) copy-start(s32[4,8,8]{2,1,0:T(8,128)} %param.20) | copy-start | bytes 3076
  12.9 14.9 %collective-permute-start.4 = (bf16[32,3584]{1,0:T(8,128)(2,1)}, bf16[32,3584]{1,0:T(8,128)(2,1)}, u32[]{:S(2)}, u32[]{:S(2)}) collective-permute-start(bf16[32,3584]{1,0:T(8,128)(2,1)} %collective-permute-done.refs_13_), channel_id=1, source_target_pairs={{0,1},{1,0},{2,3},{3,2},{4,5},{5,4},{6,7},{7,6},{8,9},{9,8},{10,11... | collective-permute-start | bytes 688136 | tf_op jit(solution)/shard_map/ppermute | solution.py:317
  13.4 14.5 %collective-permute-start.2 = (bf16[32,3584]{1,0:T(8,128)(2,1)}, bf16[32,3584]{1,0:T(8,128)(2,1)S(1)}, u32[]{:S(2)}, u32[]{:S(2)}) collective-permute-start(bf16[32,3584]{1,0:T(8,128)(2,1)} %collective-permute-done.refs_13_), channel_id=1, source_target_pairs={{0,4},{1,5},{4,8},{5,9},{8,12},{9,13},{12,14},{13,15},{14,10},{15,... | collective-permute-start | bytes 688136 | tf_op jit(solution)/shard_map/ppermute | solution.py:317
  15.1 12.8 %collective-permute-start.6 = (bf16[32,3584]{1,0:T(8,128)(2,1)}, bf16[32,3584]{1,0:T(8,128)(2,1)}, u32[]{:S(2)}, u32[]{:S(2)}) collective-permute-start(bf16[32,3584]{1,0:T(8,128)(2,1)} %collective-permute-done.1.refs_12_), channel_id=1, source_target_pairs={{0,1},{1,0},{2,3},{3,2},{4,5},{5,4},{6,7},{7,6},{8,9},{9,8},{10,11... | collective-permute-start | bytes 688136 | tf_op jit(solution)/shard_map/ppermute | solution.py:317
  15.1 12.8 %collective-permute-start.3 = (bf16[32,3584]{1,0:T(8,128)(2,1)}, bf16[32,3584]{1,0:T(8,128)(2,1)S(1)}, u32[]{:S(2)}, u32[]{:S(2)}) collective-permute-start(bf16[32,3584]{1,0:T(8,128)(2,1)} %collective-permute-done.1.refs_12_), channel_id=1, source_target_pairs={{0,2},{1,3},{4,0},{5,1},{8,4},{9,5},{12,8},{13,9},{14,12},{15,13},... | collective-permute-start | bytes 688136 | tf_op jit(solution)/shard_map/ppermute | solution.py:317
  23.0 0.6 copy-start.8
  27.9 11.4 %collective-permute-start.10 = (bf16[32,3584]{1,0:T(8,128)(2,1)S(1)}, bf16[32,3584]{1,0:T(8,128)(2,1)S(1)}, u32[]{:S(2)}, u32[]{:S(2)}) collective-permute-start(bf16[32,3584]{1,0:T(8,128)(2,1)S(1)} %collective-permute-done.2.refs_15_), channel_id=1, source_target_pairs={{0,4},{1,5},{4,8},{5,9},{8,12},{9,13},{12,14},{13,15},{14,10},{15,... | collective-permute-start | bytes 688136 | tf_op jit(solution)/shard_map/ppermute | solution.py:317
  28.0 11.3 %collective-permute-start.11 = (bf16[32,3584]{1,0:T(8,128)(2,1)S(1)}, bf16[32,3584]{1,0:T(8,128)(2,1)S(1)}, u32[]{:S(2)}, u32[]{:S(2)}) collective-permute-start(bf16[32,3584]{1,0:T(8,128)(2,1)S(1)} %collective-permute-done.3.refs_14_), channel_id=1, source_target_pairs={{0,2},{1,3},{4,0},{5,1},{8,4},{9,5},{12,8},{13,9},{14,12},{15,13},... | collective-permute-start | bytes 688136 | tf_op jit(solution)/shard_map/ppermute | solution.py:317
  30.0 8.1 %collective-permute-start.9 = (bf16[32,640]{1,0:T(8,128)(2,1)S(1)}, bf16[32,640]{1,0:T(8,128)(2,1)S(1)}, u32[]{:S(2)}, u32[]{:S(2)}) collective-permute-start(bf16[32,640]{1,0:T(8,128)(2,1)S(1)} %attention.1), channel_id=1, source_target_pairs={{0,12},{1,13},{2,14},{3,15},{4,8},{5,9},{6,10},{7,11},{8,4},{9,5},... | collective-permute-start | bytes 122888 | tf_op jit(solution)/shard_map/ppermute | solution.py:317
  30.7 8.5 %collective-permute-start.8 = (bf16[32,640]{1,0:T(8,128)(2,1)S(1)}, bf16[32,640]{1,0:T(8,128)(2,1)S(1)}, u32[]{:S(2)}, u32[]{:S(2)}) collective-permute-start(bf16[32,640]{1,0:T(8,128)(2,1)S(1)} %attention.1), channel_id=1, source_target_pairs={{0,8},{1,9},{2,10},{3,11},{4,12},{5,13},{6,14},{7,15},{8,0},{9,1},... | collective-permute-start | bytes 122888 | tf_op jit(solution)/shard_map/ppermute | solution.py:317
  31.5 7.8 %collective-permute-start.7 = (bf16[32,640]{1,0:T(8,128)(2,1)S(1)}, bf16[32,640]{1,0:T(8,128)(2,1)S(1)}, u32[]{:S(2)}, u32[]{:S(2)}) collective-permute-start(bf16[32,640]{1,0:T(8,128)(2,1)S(1)} %attention.1), channel_id=1, source_target_pairs={{0,4},{1,5},{2,6},{3,7},{4,0},{5,1},{6,2},{7,3},{8,12},{9,13},{10,... | collective-permute-start | bytes 122888 | tf_op jit(solution)/shard_map/ppermute | solution.py:317
  39.3 10.0 %collective-permute-start.15 = (bf16[32,3584]{1,0:T(8,128)(2,1)S(1)}, bf16[32,3584]{1,0:T(8,128)(2,1)S(1)}, u32[]{:S(2)}, u32[]{:S(2)}) collective-permute-start(bf16[32,3584]{1,0:T(8,128)(2,1)S(1)} %collective-permute-done.2.refs_15_), channel_id=1, source_target_pairs={{0,1},{1,0},{2,3},{3,2},{4,5},{5,4},{6,7},{7,6},{8,9},{9,8},{10,11... | collective-permute-start | bytes 688136 | tf_op jit(solution)/shard_map/ppermute | solution.py:317
  39.4 9.9 %collective-permute-start.16 = (bf16[32,3584]{1,0:T(8,128)(2,1)S(1)}, bf16[32,3584]{1,0:T(8,128)(2,1)S(1)}, u32[]{:S(2)}, u32[]{:S(2)}) collective-permute-start(bf16[32,3584]{1,0:T(8,128)(2,1)S(1)} %collective-permute-done.3.refs_14_), channel_id=1, source_target_pairs={{0,1},{1,0},{2,3},{3,2},{4,5},{5,4},{6,7},{7,6},{8,9},{9,8},{10,11... | collective-permute-start | bytes 688136 | tf_op jit(solution)/shard_map/ppermute | solution.py:317
  39.9 9.4 %collective-permute-start.14 = (bf16[32,3584]{1,0:T(8,128)(2,1)S(1)}, bf16[32,3584]{1,0:T(8,128)(2,1)S(1)}, u32[]{:S(2)}, u32[]{:S(2)}) collective-permute-start(bf16[32,3584]{1,0:T(8,128)(2,1)S(1)} %broadcast_select_fusion), channel_id=1, source_target_pairs={{0,8},{1,7},{4,12},{5,3},{8,14},{9,1},{12,10},{13,5},{14,6},{15,9}... | collective-permute-start | bytes 688136 | tf_op jit(solution)/shard_map/ppermute | solution.py:317
  40.1 2.2 %collective-permute-start.13 = (bf16[128,640]{1,0:T(8,128)(2,1)S(1)}, bf16[128,640]{1,0:T(8,128)(2,1)S(1)}, u32[]{:S(2)}, u32[]{:S(2)}) collective-permute-start(bf16[128,640]{1,0:T(8,128)(2,1)S(1)} %constant_dynamic-update-slice_fusion.refs_1_), channel_id=1, source_target_pairs={{0,1},{1,0},{2,3},{3,2},{4,5},{5,4},{6,7},{7,6},{8,9},{9,8},{10,11... | collective-permute-start | bytes 491528 | tf_op jit(solution)/shard_map/ppermute | solution.py:317
  40.5 8.7 %collective-permute-start.12 = (bf16[128,640]{1,0:T(8,128)(2,1)S(1)}, bf16[128,640]{1,0:T(8,128)(2,1)S(1)}, u32[]{:S(2)}, u32[]{:S(2)}) collective-permute-start(bf16[128,640]{1,0:T(8,128)(2,1)S(1)} %constant_dynamic-update-slice_fusion.refs_1_), channel_id=1, source_target_pairs={{0,2},{1,3},{2,0},{3,1},{4,6},{5,7},{6,4},{7,5},{8,10},{9,11},{10,... | collective-permute-start | bytes 491528 | tf_op jit(solution)/shard_map/ppermute | solution.py:317
  49.3 2.4 %collective-permute-start.18 = (bf16[32,3584]{1,0:T(8,128)(2,1)S(1)}, bf16[32,3584]{1,0:T(8,128)(2,1)S(1)}, u32[]{:S(2)}, u32[]{:S(2)}) collective-permute-start(bf16[32,3584]{1,0:T(8,128)(2,1)S(1)} %collective-permute-done.14.refs_5_), channel_id=1, source_target_pairs={{0,1},{1,0},{2,3},{3,2},{4,5},{5,4},{6,7},{7,6},{8,9},{9,8},{10,11... | collective-permute-start | bytes 688136 | tf_op jit(solution)/shard_map/ppermute | solution.py:317
  49.4 2.4 %collective-permute-start.19 = (bf16[32,3584]{1,0:T(8,128)(2,1)S(1)}, bf16[32,3584]{1,0:T(8,128)(2,1)S(1)}, u32[]{:S(2)}, u32[]{:S(2)}) collective-permute-start(bf16[32,3584]{1,0:T(8,128)(2,1)S(1)} %collective-permute-done.11.refs_6_), channel_id=1, source_target_pairs={{0,1},{1,0},{2,3},{3,2},{4,5},{5,4},{6,7},{7,6},{8,9},{9,8},{10,11... | collective-permute-start | bytes 688136 | tf_op jit(solution)/shard_map/ppermute | solution.py:317
  49.9 1.9 %collective-permute-start.20 = (bf16[32,3584]{1,0:T(8,128)(2,1)S(1)}, bf16[32,3584]{1,0:T(8,128)(2,1)S(1)}, u32[]{:S(2)}, u32[]{:S(2)}) collective-permute-start(bf16[32,3584]{1,0:T(8,128)(2,1)S(1)} %collective-permute-done.10.refs_7_), channel_id=1, source_target_pairs={{0,1},{1,0},{2,3},{3,2},{4,5},{5,4},{6,7},{7,6},{8,9},{9,8},{10,11... | collective-permute-start | bytes 688136 | tf_op jit(solution)/shard_map/ppermute | solution.py:317
  49.9 1.8 %collective-permute-start.17 = (bf16[128,640]{1,0:T(8,128)(2,1)S(1)}, bf16[128,640]{1,0:T(8,128)(2,1)S(1)}, u32[]{:S(2)}, u32[]{:S(2)}) collective-permute-start(bf16[128,640]{1,0:T(8,128)(2,1)S(1)} %collective-permute-done.12.refs_2_), channel_id=1, source_target_pairs={{0,1},{1,0},{2,3},{3,2},{4,5},{5,4},{6,7},{7,6},{8,9},{9,8},{10,11... | collective-permute-start | bytes 491528 | tf_op jit(solution)/shard_map/ppermute | solution.py:317
  51.8 2.0 %copy-start.1 = (bf16[512,3584]{1,0:T(8,128)(2,1)S(1)}, bf16[512,3584]{1,0:T(8,128)(2,1)}, u32[]{:S(2)}) copy-start(bf16[512,3584]{1,0:T(8,128)(2,1)} %refs_21_.1) | copy-start | bytes 11010052
  53.8 0.9 copy-start.3
  54.7 0.9 copy-start.4
  55.6 0.6 copy-start.7
  63.8 10.1 %slice-start.4 = ((s8[7340032]{0:T(1024)(128)(4,1)}), s8[4194304]{0:T(1024)(128)(4,1)S(1)}, s32[]{:S(2)}) async-start(s8[7340032]{0:T(1024)(128)(4,1)} %bitcast.65), calls=%async_computation.5 | async-start | bytes 8388608
  63.8 12.0 %slice-start = ((s8[7340032]{0:T(1024)(128)(4,1)}), s8[4194304]{0:T(1024)(128)(4,1)S(1)}, s32[]{:S(2)}) async-start(s8[7340032]{0:T(1024)(128)(4,1)} %bitcast.61), calls=%async_computation.1 | async-start | bytes 8388608
  68.8 5.1 %slice-start.5 = ((s8[7340032]{0:T(1024)(128)(4,1)}), s8[3145728]{0:T(1024)(128)(4,1)S(1)}, s32[]{:S(2)}) async-start(s8[7340032]{0:T(1024)(128)(4,1)} %bitcast.65), calls=%async_computation.6 | async-start | bytes 6291456
  68.8 7.1 %slice-start.1 = ((s8[7340032]{0:T(1024)(128)(4,1)}), s8[3145728]{0:T(1024)(128)(4,1)S(1)}, s32[]{:S(2)}) async-start(s8[7340032]{0:T(1024)(128)(4,1)} %bitcast.61), calls=%async_computation.2 | async-start | bytes 6291456
  73.9 6.7 %slice-start.2 = ((s8[7340032]{0:T(1024)(128)(4,1)}), s8[4194304]{0:T(1024)(128)(4,1)S(1)}, s32[]{:S(2)}) async-start(s8[7340032]{0:T(1024)(128)(4,1)} %bitcast.63), calls=%async_computation.3 | async-start | bytes 8388608
  75.6 2.8 %collective-permute-start.21 = (bf16[96,3584]{1,0:T(8,128)(2,1)S(1)}, bf16[96,3584]{1,0:T(8,128)(2,1)S(1)}, u32[]{:S(2)}, u32[]{:S(2)}) collective-permute-start(bf16[96,3584]{1,0:T(8,128)(2,1)S(1)} %slice.98), channel_id=1, source_target_pairs={{0,1},{1,0},{2,3},{3,2},{4,5},{5,4},{6,7},{7,6},{8,9},{9,8},{10,11... | collective-permute-start | bytes 2064392 | tf_op jit(solution)/shard_map/ppermute | solution.py:317
  75.9 4.7 %slice-start.3 = ((s8[7340032]{0:T(1024)(128)(4,1)}), s8[3145728]{0:T(1024)(128)(4,1)S(1)}, s32[]{:S(2)}) async-start(s8[7340032]{0:T(1024)(128)(4,1)} %bitcast.63), calls=%async_computation.4 | async-start | bytes 6291456
  78.5 5.4 %collective-permute-start.23 = (bf16[16,3584]{1,0:T(8,128)(2,1)S(1)}, bf16[16,3584]{1,0:T(8,128)(2,1)S(1)}, u32[]{:S(2)}, u32[]{:S(2)}) collective-permute-start(bf16[16,3584]{1,0:T(8,128)(2,1)S(1)} %get-tuple-element.133), channel_id=1, source_target_pairs={{0,2},{1,3},{4,0},{5,1},{8,4},{9,5},{12,8},{13,9},{14,12},{15,13},... | collective-permute-start | bytes 344072 | tf_op jit(solution)/shard_map/ppermute | solution.py:317
  80.0 5.1 %collective-permute-start.22 = (bf16[16,3584]{1,0:T(8,128)(2,1)S(1)}, bf16[16,3584]{1,0:T(8,128)(2,1)S(1)}, u32[]{:S(2)}, u32[]{:S(2)}) collective-permute-start(bf16[16,3584]{1,0:T(8,128)(2,1)S(1)} %get-tuple-element.134), channel_id=1, source_target_pairs={{0,4},{1,5},{4,8},{5,9},{8,12},{9,13},{12,14},{13,15},{14,10},{15,... | collective-permute-start | bytes 344072 | tf_op jit(solution)/shard_map/ppermute | solution.py:317
  87.8 9.2 %collective-permute-start.24 = (bf16[160,3584]{1,0:T(8,128)(2,1)S(1)}, bf16[160,3584]{1,0:T(8,128)(2,1)S(1)}, u32[]{:S(2)}, u32[]{:S(2)}) collective-permute-start(bf16[160,3584]{1,0:T(8,128)(2,1)S(1)} %slice.101), channel_id=1, source_target_pairs={{0,1},{1,0},{2,3},{3,2},{4,5},{5,4},{6,7},{7,6},{8,9},{9,8},{10,11... | collective-permute-start | bytes 3440648 | tf_op jit(solution)/shard_map/ppermute | solution.py:317
  88.0 8.1 %collective-permute-start.26 = (bf16[32,3584]{1,0:T(8,128)(2,1)S(1)}, bf16[32,3584]{1,0:T(8,128)(2,1)S(1)}, u32[]{:S(2)}, u32[]{:S(2)}) collective-permute-start(bf16[32,3584]{1,0:T(8,128)(2,1)S(1)} %get-tuple-element.131), channel_id=1, source_target_pairs={{0,2},{1,3},{4,0},{5,1},{8,4},{9,5},{12,8},{13,9},{14,12},{15,13},... | collective-permute-start | bytes 688136 | tf_op jit(solution)/shard_map/ppermute | solution.py:317
  89.3 7.7 %collective-permute-start.25 = (bf16[32,3584]{1,0:T(8,128)(2,1)S(1)}, bf16[32,3584]{1,0:T(8,128)(2,1)S(1)}, u32[]{:S(2)}, u32[]{:S(2)}) collective-permute-start(bf16[32,3584]{1,0:T(8,128)(2,1)S(1)} %get-tuple-element.132), channel_id=1, source_target_pairs={{0,4},{1,5},{4,8},{5,9},{8,12},{9,13},{12,14},{13,15},{14,10},{15,... | collective-permute-start | bytes 688136 | tf_op jit(solution)/shard_map/ppermute | solution.py:317
  97.2 7.0 %collective-permute-start.28 = (bf16[32,3584]{1,0:T(8,128)(2,1)S(1)}, bf16[32,3584]{1,0:T(8,128)(2,1)S(1)}, u32[]{:S(2)}, u32[]{:S(2)}) collective-permute-start(bf16[32,3584]{1,0:T(8,128)(2,1)S(1)} %get-tuple-element.129), channel_id=1, source_target_pairs={{0,2},{1,3},{4,0},{5,1},{8,4},{9,5},{12,8},{13,9},{14,12},{15,13},... | collective-permute-start | bytes 688136 | tf_op jit(solution)/shard_map/ppermute | solution.py:317
  99.0 6.6 %collective-permute-start.27 = (bf16[32,3584]{1,0:T(8,128)(2,1)S(1)}, bf16[32,3584]{1,0:T(8,128)(2,1)S(1)}, u32[]{:S(2)}, u32[]{:S(2)}) collective-permute-start(bf16[32,3584]{1,0:T(8,128)(2,1)S(1)} %get-tuple-element.130), channel_id=1, source_target_pairs={{0,4},{1,5},{4,8},{5,9},{8,12},{9,13},{12,14},{13,15},{14,10},{15,... | collective-permute-start | bytes 688136 | tf_op jit(solution)/shard_map/ppermute | solution.py:317
  105.7 6.1 %collective-permute-start.30 = (bf16[32,3584]{1,0:T(8,128)(2,1)S(1)}, bf16[32,3584]{1,0:T(8,128)(2,1)S(1)}, u32[]{:S(2)}, u32[]{:S(2)}) collective-permute-start(bf16[32,3584]{1,0:T(8,128)(2,1)S(1)} %get-tuple-element.127), channel_id=1, source_target_pairs={{0,2},{1,3},{4,0},{5,1},{8,4},{9,5},{12,8},{13,9},{14,12},{15,13},... | collective-permute-start | bytes 688136 | tf_op jit(solution)/shard_map/ppermute | solution.py:317
  106.4 6.0 %collective-permute-start.29 = (bf16[32,3584]{1,0:T(8,128)(2,1)S(1)}, bf16[32,3584]{1,0:T(8,128)(2,1)S(1)}, u32[]{:S(2)}, u32[]{:S(2)}) collective-permute-start(bf16[32,3584]{1,0:T(8,128)(2,1)S(1)} %get-tuple-element.128), channel_id=1, source_target_pairs={{0,4},{1,5},{4,8},{5,9},{8,12},{9,13},{12,14},{13,15},{14,10},{15,... | collective-permute-start | bytes 688136 | tf_op jit(solution)/shard_map/ppermute | solution.py:317

commit v15 on v13

--- a/solution.py
+++ b/solution.py
@@ -318,6 +318,7 @@
     half = chips // 2
     far, near = distances(chips)
     hold = lax.optimization_barrier
+    stay = lambda a: pltpu.with_memory_space_constraint(a, pltpu.HBM)
     cut = rows // 2
     sibling = sibling_perm(chips)
 
@@ -361,7 +362,7 @@
         q_abs,
         owned.reshape(-1, kv_width),
         new_lat.reshape(rows, kv_width),
-        row_lengths,
+        stay(row_lengths),
         routes.reshape(rows, -1),
         devices * positions,
         w_out.shape[0],
@@ -385,15 +386,16 @@
     across = across[0] if low == 2 else jnp.concatenate(across, axis=0)
 
     f32 = jnp.float32
+    held[0] = stay(held[0])
 
     x_far, x_near, scale, weight, hidden = normalize(
         2 * len(far),
-        scalars,
+        stay(scalars),
         [along, across, along_sib, send(across, sibling)],
         [a[d] for part in (far, near) for a in (held, sib) for d in part],
-        w_out,
+        stay(w_out),
         gain,
-        w_router.T,
+        stay(w_router.T),
     )
     far_rows = x_far.shape[0]
 

time: 111 us -> 107 us (0.964)
  local copies, waits for them, and re-layouts: 7.31 us -> 2.44 us
  Pallas kernels: 13 us -> 14.2 us
    unnamed x35 -> x25, local copies, waits for them, and re-layouts: 5.86 us -> 0.99 us
where the time goes in v15:
time: 107 us
  waiting for transfers between devices  40.3 us (38%)
  starting transfers between devices  31.2 us (29%)
  matrix products  17.1 us (16%)
  Pallas kernels  14.2 us (13%)
  local copies, waits for them, and re-layouts  2.44 us (2%)
  other arithmetic  1.37 us (1%)
    ppermute x31, waiting for transfers between devices, send(): return lax.ppermute(a, 'expert', perm)  32.7 us
    ppermute x31, starting transfers between devices, send(): return lax.ppermute(a, 'expert', perm)  24.9 us
    dot_general x6, matrix products, product(): return jnp.dot(a, w[0], preferred_element_type=f32)  16.2 us
    pallas_call x1, Pallas kernels, normalize(): pl.pallas_call(lambda *refs: norm_kernel(far, blocks, rows, latent, width...  8.43 us
    all_to_all x1, waiting for transfers between devices, local(): lax.all_to_all(ordered, 'expert', split_axis=0, concat_axis=0, tiled=True)  7.6 us
    all_to_all x1, starting transfers between devices, local(): lax.all_to_all(ordered, 'expert', split_axis=0, concat_axis=0, tiled=True)  6.29 us
    pallas_call x1, Pallas kernels, attention(): pl.pallas_call(lambda *refs: attention_kernel(context, latent, *refs), gr...  4.33 us
  transfers between devices with their start and end apart: 32, of which 13 were waited for; matrix products, arithmetic and copies ran while one was open for 7% of the time, Pallas kernels for 5%

profile of v15, /device:TPU:0, one launch (start us, length us, event | category | flops | bytes accessed | tf_op | source)
XLA Modules:
  0.0 107.0 jit_solution(5345725651486170855)
XLA Ops:
  0.0 0.5 collective-permute-start.5
  0.5 2.6 %collective-permute-start.1 = (bf16[32,3584]{1,0:T(8,128)(2,1)}, bf16[32,3584]{1,0:T(8,128)(2,1)}, u32[]{:S(2)}, u32[]{:S(2)}) collective-permute-start(bf16[32,3584]{1,0:T(8,128)(2,1)} %bitcast.57), channel_id=1, source_target_pairs={{0,2},{1,3},{4,0},{5,1},{8,4},{9,5},{12,8},{13,9},{14,12},{15,13},... | collective-permute-start | bytes 688136 | tf_op jit(solution)/shard_map/ppermute | solution.py:326
  3.2 1.0 fusion.27
  4.4 0.7 copy.19
  5.1 6.3 %all-to-all-start = ((bf16[16,2,8,576]{3,2,1,0:T(8,128)(2,1)}), bf16[16,2,8,576]{3,2,1,0:T(8,128)(2,1)S(1)}, u32[]{:S(2)}, u32[]{:S(2)}) async-start(bf16[16,2,8,576]{3,2,1,0:T(8,128)(2,1)} %copy.19), calls=%async_computation | async-start | bytes 655360 | tf_op jit(solution)/shard_map/all_to_all | solution.py:343
  11.5 1.4 %lookup.1 = (s32[8]{0:T(128)}, s32[17]{0:T(128)}) custom-call(s32[128]{0:T(128)} %owner.1, s32[128]{0:T(128)} %lengths.1, s32[272]{0:T(512)} %constant.41.table, s32[1]{0:T(128)} %bitcast.device), custom_call_target="tpu_custom_call" | custom-call | flops 10000000000 | bytes 100000000 | tf_op jit(solution)/shard_map/lookup/pallas_call | solution.py:194
  12.9 0.5 collective-permute-start.4
  13.4 1.7 %collective-permute-start.2 = (bf16[32,3584]{1,0:T(8,128)(2,1)}, bf16[32,3584]{1,0:T(8,128)(2,1)S(1)}, u32[]{:S(2)}, u32[]{:S(2)}) collective-permute-start(bf16[32,3584]{1,0:T(8,128)(2,1)} %collective-permute-done.refs_13_), channel_id=1, source_target_pairs={{0,4},{1,5},{4,8},{5,9},{8,12},{9,13},{12,14},{13,15},{14,10},{15,... | collective-permute-start | bytes 688136 | tf_op jit(solution)/shard_map/ppermute | solution.py:326
  15.4 7.6 %all-to-all-done = bf16[16,2,8,576]{3,2,1,0:T(8,128)(2,1)S(1)} async-done(((bf16[16,2,8,576]{3,2,1,0:T(8,128)(2,1)}), bf16[16,2,8,576]{3,2,1,0:T(8,128)(2,1)S(1)}, u32[]{:S(2)}, u32[]{:S(2)}) %all-to-all-start) | async-done | bytes 294944 | tf_op jit(solution)/shard_map/all_to_all | solution.py:343
  23.0 4.3 %attention.1 = bf16[32,640]{1,0:T(8,128)(2,1)S(1)} custom-call(bf16[4,8,36864]{2,1,0:T(8,128)(2,1)S(1)} %copy-done.1, bf16[256,576]{1,0:T(8,128)(2,1)S(1)} %bitcast.52, bf16[32,576]{1,0:T(8,128)(2,1)S(1)} %bitcast.53, s32[8]{0:T(128)} %get-tuple-element.69.refs_3_, s32[32,8]{1,0:T(8,128)S(1)} %bitcast.54), custom_call_target="tpu_custom_call" | custom-call | flops 679477248 | bytes 2359296 | tf_op jit(solution)/shard_map/attention/pallas_call | solution.py:274
  27.4 0.6 collective-permute-start.10
  27.9 1.5 %collective-permute-start.11 = (bf16[32,3584]{1,0:T(8,128)(2,1)S(1)}, bf16[32,3584]{1,0:T(8,128)(2,1)S(1)}, u32[]{:S(2)}, u32[]{:S(2)}) collective-permute-start(bf16[32,3584]{1,0:T(8,128)(2,1)S(1)} %collective-permute-done.3.refs_14_), channel_id=1, source_target_pairs={{0,2},{1,3},{4,0},{5,1},{8,4},{9,5},{12,8},{13,9},{14,12},{15,13},... | collective-permute-start | bytes 688136 | tf_op jit(solution)/shard_map/ppermute | solution.py:326
  29.5 0.8 collective-permute-start.9
  30.2 1.2 %collective-permute-start.8 = (bf16[32,640]{1,0:T(8,128)(2,1)S(1)}, bf16[32,640]{1,0:T(8,128)(2,1)S(1)}, u32[]{:S(2)}, u32[]{:S(2)}) collective-permute-start(bf16[32,640]{1,0:T(8,128)(2,1)S(1)} %attention.1), channel_id=1, source_target_pairs={{0,8},{1,9},{2,10},{3,11},{4,12},{5,13},{6,14},{7,15},{8,0},{9,1},... | collective-permute-start | bytes 122888 | tf_op jit(solution)/shard_map/ppermute | solution.py:326
  31.4 2.4 %collective-permute-start.7 = (bf16[32,640]{1,0:T(8,128)(2,1)S(1)}, bf16[32,640]{1,0:T(8,128)(2,1)S(1)}, u32[]{:S(2)}, u32[]{:S(2)}) collective-permute-start(bf16[32,640]{1,0:T(8,128)(2,1)S(1)} %attention.1), channel_id=1, source_target_pairs={{0,4},{1,5},{2,6},{3,7},{4,0},{5,1},{6,2},{7,3},{8,12},{9,13},{10,... | collective-permute-start | bytes 122888 | tf_op jit(solution)/shard_map/ppermute | solution.py:326
  33.9 3.7 %collective-permute-done.9 = bf16[32,640]{1,0:T(8,128)(2,1)S(1)} collective-permute-done((bf16[32,640]{1,0:T(8,128)(2,1)S(1)}, bf16[32,640]{1,0:T(8,128)(2,1)S(1)}, u32[]{:S(2)}, u32[]{:S(2)}) %collective-permute-start.9) | collective-permute-done | bytes 40992 | tf_op jit(solution)/shard_map/ppermute | solution.py:326
  37.5 1.2 %collective-permute-done.8 = bf16[32,640]{1,0:T(8,128)(2,1)S(1)} collective-permute-done((bf16[32,640]{1,0:T(8,128)(2,1)S(1)}, bf16[32,640]{1,0:T(8,128)(2,1)S(1)}, u32[]{:S(2)}, u32[]{:S(2)}) %collective-permute-start.8) | collective-permute-done | bytes 40992 | tf_op jit(solution)/shard_map/ppermute | solution.py:326
  38.8 0.5 collective-permute-start.16
  39.6 0.5 collective-permute-start.13
  40.1 1.7 %collective-permute-start.12 = (bf16[128,640]{1,0:T(8,128)(2,1)S(1)}, bf16[128,640]{1,0:T(8,128)(2,1)S(1)}, u32[]{:S(2)}, u32[]{:S(2)}) collective-permute-start(bf16[128,640]{1,0:T(8,128)(2,1)S(1)} %constant_dynamic-update-slice_fusion.refs_1_), channel_id=1, source_target_pairs={{0,2},{1,3},{2,0},{3,1},{4,6},{5,7},{6,4},{7,5},{8,10},{9,11},{10,... | collective-permute-start | bytes 491528 | tf_op jit(solution)/shard_map/ppermute | solution.py:326
  41.9 6.9 %collective-permute-done.12.refs_2_ = bf16[128,640]{1,0:T(8,128)(2,1)S(1)} collective-permute-done((bf16[128,640]{1,0:T(8,128)(2,1)S(1)}, bf16[128,640]{1,0:T(8,128)(2,1)S(1)}, u32[]{:S(2)}, u32[]{:S(2)}) %collective-permute-start.12) | collective-permute-done | bytes 163872 | tf_op jit(solution)/shard_map/ppermute | solution.py:326
  48.9 0.5 collective-permute-start.19
  49.4 0.4 collective-permute-start.17
  49.9 1.4 %collective-permute-done.17.refs_4_ = bf16[128,640]{1,0:T(8,128)(2,1)S(1)} collective-permute-done((bf16[128,640]{1,0:T(8,128)(2,1)S(1)}, bf16[128,640]{1,0:T(8,128)(2,1)S(1)}, u32[]{:S(2)}, u32[]{:S(2)}) %collective-permute-start.17) | collective-permute-done | bytes 163872 | tf_op jit(solution)/shard_map/ppermute | solution.py:326
  51.2 8.4 %normalize.1 = (bf16[192,3584]{1,0:T(8,128)(2,1)S(1)}, bf16[320,3584]{1,0:T(8,128)(2,1)S(1)}, f32[512,128]{1,0:T(8,128)S(1)}, f32[512,128]{1,0:T(8,128)S(1)}, f32[32,3584]{1,0:T(8,128)S(1)}) custom-call(s32[17]{0:T(128)} %get-tuple-element.68.refs_0_, bf16[128,640]{1,0:T(8,128)(2,1)S(1)} %constant_dynamic-update-slice_fusion.refs_1_, ...), custom_call_target="tpu_custom_call" | custom-call | flops 1879048192 | bytes 11010048 | tf_op jit(solution)/shard_map/normalize/pallas_call | solution.py:148
  60.1 4.8 %fusion.21 = f32[192,1024]{1,0:T(8,128)S(1)} fusion(bf16[192,3584]{1,0:T(8,128)(2,1)S(1)} %get-tuple-element.110, bf16[1,3584,1024]{2,1,0:T(8,128)(2,1)} %param.24, f32[192]{0:T(256)S(1)} %get-tuple-element.138), kind=kOutput, calls=%fused_computation.16 | convolution fusion | flops 1409482752 | bytes 9503488 | tf_op jit(solution)/shard_map/dot_general | solution.py:403
  64.9 1.7 %multiply_convert_fusion.1 = bf16[192,1024]{1,0:T(8,128)(2,1)S(1)} fusion(f32[192,1024]{1,0:T(8,128)S(1)} %fusion.21, f32[192]{0:T(256)S(1)} %get-tuple-element.137, f32[192]{0:T(256)S(1)} %get-tuple-element.138, bf16[192,3584]{1,0:T(8,128)(2,1)S(1)} %get-tuple-element.110, bf16[1,3584,1024]{2,1,0:T(8,128)(2,1)S(1)} %bitcast.64), kind=kOutput, calls=%fused_computation.20 | convolution fusion | flops 1410859008 | bytes 9897472 | tf_op jit(solution)/shard_map/dot_general | solution.py:403
  66.7 0.9 slice-done.5
  67.6 1.6 %fusion.15 = bf16[192,3584]{1,0:T(8,128)(2,1)S(1)} fusion(bf16[192,1024]{1,0:T(8,128)(2,1)S(1)} %multiply_convert_fusion.1, bf16[1,1024,3584]{2,1,0:T(8,128)(2,1)S(1)} %bitcast.66), kind=kOutput, calls=%fused_computation.13 | convolution fusion | flops 1409974272 | bytes 9109504 | tf_op jit(solution)/shard_map/dot_general | solution.py:403
  69.5 2.7 %fusion.10 = f32[320,1024]{1,0:T(8,128)S(1)} fusion(bf16[320,3584]{1,0:T(8,128)(2,1)S(1)} %get-tuple-element.109, bf16[1,3584,1024]{2,1,0:T(8,128)(2,1)S(1)} %bitcast.62), kind=kOutput, calls=%fused_computation.10 | convolution fusion | flops 2348810240 | bytes 10944512 | tf_op jit(solution)/shard_map/dot_general | solution.py:403
  72.3 1.5 %collective-permute-start.23 = (bf16[16,3584]{1,0:T(8,128)(2,1)S(1)}, bf16[16,3584]{1,0:T(8,128)(2,1)S(1)}, u32[]{:S(2)}, u32[]{:S(2)}) collective-permute-start(bf16[16,3584]{1,0:T(8,128)(2,1)S(1)} %get-tuple-element.133), channel_id=1, source_target_pairs={{0,2},{1,3},{4,0},{5,1},{8,4},{9,5},{12,8},{13,9},{14,12},{15,13},... | collective-permute-start | bytes 344072 | tf_op jit(solution)/shard_map/ppermute | solution.py:326
  73.7 0.6 collective-permute-start.22
  74.3 2.8 %multiply_convert_fusion = bf16[320,1024]{1,0:T(8,128)(2,1)S(1)} fusion(f32[320,1024]{1,0:T(8,128)S(1)} %fusion.10, f32[320]{0:T(512)S(1)} %get-tuple-element.135, f32[320]{0:T(512)S(1)} %get-tuple-element.136, bf16[320,3584]{1,0:T(8,128)(2,1)S(1)} %get-tuple-element.109, bf16[1,3584,1024]{2,1,0:T(8,128)(2,1)S(1)} %bitcast.64), kind=kOutput, calls=%fused_computation.15 | convolution fusion | flops 2351759360 | bytes 11602432 | tf_op jit(solution)/shard_map/dot_general | solution.py:403
  77.2 0.5 collective-permute-done.23
  77.7 1.2 %collective-permute-done.22 = bf16[16,3584]{1,0:T(8,128)(2,1)S(1)} collective-permute-done((bf16[16,3584]{1,0:T(8,128)(2,1)S(1)}, bf16[16,3584]{1,0:T(8,128)(2,1)S(1)}, u32[]{:S(2)}, u32[]{:S(2)}) %collective-permute-start.22) | collective-permute-done | bytes 114720 | tf_op jit(solution)/shard_map/ppermute | solution.py:326
  78.9 2.5 %fusion.12 = bf16[320,3584]{1,0:T(8,128)(2,1)S(1)} fusion(bf16[320,1024]{1,0:T(8,128)(2,1)S(1)} %multiply_convert_fusion, bf16[1,1024,3584]{2,1,0:T(8,128)(2,1)S(1)} %bitcast.66), kind=kOutput, calls=%fused_computation.12 | convolution fusion | flops 2349957120 | bytes 10289152 | tf_op jit(solution)/shard_map/dot_general | solution.py:403
  81.7 1.3 %collective-permute-start.26 = (bf16[32,3584]{1,0:T(8,128)(2,1)S(1)}, bf16[32,3584]{1,0:T(8,128)(2,1)S(1)}, u32[]{:S(2)}, u32[]{:S(2)}) collective-permute-start(bf16[32,3584]{1,0:T(8,128)(2,1)S(1)} %get-tuple-element.131), channel_id=1, source_target_pairs={{0,2},{1,3},{4,0},{5,1},{8,4},{9,5},{12,8},{13,9},{14,12},{15,13},... | collective-permute-start | bytes 688136 | tf_op jit(solution)/shard_map/ppermute | solution.py:326
  83.0 0.8 collective-permute-start.25
  83.8 6.0 %collective-permute-done.26 = bf16[32,3584]{1,0:T(8,128)(2,1)S(1)} collective-permute-done((bf16[32,3584]{1,0:T(8,128)(2,1)S(1)}, bf16[32,3584]{1,0:T(8,128)(2,1)S(1)}, u32[]{:S(2)}, u32[]{:S(2)}) %collective-permute-start.26) | collective-permute-done | bytes 229408 | tf_op jit(solution)/shard_map/ppermute | solution.py:326
  89.8 0.9 collective-permute-done.25
  90.9 1.8 %collective-permute-start.28 = (bf16[32,3584]{1,0:T(8,128)(2,1)S(1)}, bf16[32,3584]{1,0:T(8,128)(2,1)S(1)}, u32[]{:S(2)}, u32[]{:S(2)}) collective-permute-start(bf16[32,3584]{1,0:T(8,128)(2,1)S(1)} %get-tuple-element.129), channel_id=1, source_target_pairs={{0,2},{1,3},{4,0},{5,1},{8,4},{9,5},{12,8},{13,9},{14,12},{15,13},... | collective-permute-start | bytes 688136 | tf_op jit(solution)/shard_map/ppermute | solution.py:326
  92.9 4.9 %collective-permute-done.28 = bf16[32,3584]{1,0:T(8,128)(2,1)S(1)} collective-permute-done((bf16[32,3584]{1,0:T(8,128)(2,1)S(1)}, bf16[32,3584]{1,0:T(8,128)(2,1)S(1)}, u32[]{:S(2)}, u32[]{:S(2)}) %collective-permute-start.28) | collective-permute-done | bytes 229408 | tf_op jit(solution)/shard_map/ppermute | solution.py:326
  97.8 1.5 %collective-permute-done.27 = bf16[32,3584]{1,0:T(8,128)(2,1)S(1)} collective-permute-done((bf16[32,3584]{1,0:T(8,128)(2,1)S(1)}, bf16[32,3584]{1,0:T(8,128)(2,1)S(1)}, u32[]{:S(2)}, u32[]{:S(2)}) %collective-permute-start.27) | collective-permute-done | bytes 229408 | tf_op jit(solution)/shard_map/ppermute | solution.py:326
  99.5 0.7 collective-permute-start.30
  100.1 1.4 %collective-permute-start.29 = (bf16[32,3584]{1,0:T(8,128)(2,1)S(1)}, bf16[32,3584]{1,0:T(8,128)(2,1)S(1)}, u32[]{:S(2)}, u32[]{:S(2)}) collective-permute-start(bf16[32,3584]{1,0:T(8,128)(2,1)S(1)} %get-tuple-element.128), channel_id=1, source_target_pairs={{0,4},{1,5},{4,8},{5,9},{8,12},{9,13},{12,14},{13,15},{14,10},{15,... | collective-permute-start | bytes 688136 | tf_op jit(solution)/shard_map/ppermute | solution.py:326
  101.5 4.0 %collective-permute-done.30 = bf16[32,3584]{1,0:T(8,128)(2,1)S(1)} collective-permute-done((bf16[32,3584]{1,0:T(8,128)(2,1)S(1)}, bf16[32,3584]{1,0:T(8,128)(2,1)S(1)}, u32[]{:S(2)}, u32[]{:S(2)}) %collective-permute-start.30) | collective-permute-done | bytes 229408 | tf_op jit(solution)/shard_map/ppermute | solution.py:326
  105.5 0.6 collective-permute-done.29
  106.1 0.8 fusion.32
  (69 shorter events, 2.9 us)
Async XLA Ops:
  0.0 3.2 %copy-start = (bf16[128,2,576]{0,2,1:T(8,128)(2,1)S(1)}, bf16[128,2,576]{0,2,1:T(8,128)(2,1)}, u32[]{:S(2)}) copy-start(bf16[128,2,576]{0,2,1:T(8,128)(2,1)} %param.16) | copy-start | bytes 884740
  0.0 27.3 %collective-permute-start.5 = (bf16[32,3584]{1,0:T(8,128)(2,1)}, bf16[32,3584]{1,0:T(8,128)(2,1)}, u32[]{:S(2)}, u32[]{:S(2)}) collective-permute-start(bf16[32,3584]{1,0:T(8,128)(2,1)} %bitcast.56), channel_id=1, source_target_pairs={{0,1},{1,0},{2,3},{3,2},{4,5},{5,4},{6,7},{7,6},{8,9},{9,8},{10,11... | collective-permute-start | bytes 688136 | tf_op jit(solution)/shard_map/ppermute | solution.py:326
  0.5 12.4 %collective-permute-start.1 = (bf16[32,3584]{1,0:T(8,128)(2,1)}, bf16[32,3584]{1,0:T(8,128)(2,1)}, u32[]{:S(2)}, u32[]{:S(2)}) collective-permute-start(bf16[32,3584]{1,0:T(8,128)(2,1)} %bitcast.57), channel_id=1, source_target_pairs={{0,2},{1,3},{4,0},{5,1},{8,4},{9,5},{12,8},{13,9},{14,12},{15,13},... | collective-permute-start | bytes 688136 | tf_op jit(solution)/shard_map/ppermute | solution.py:326
  3.0 9.9 %collective-permute-start = (bf16[32,3584]{1,0:T(8,128)(2,1)}, bf16[32,3584]{1,0:T(8,128)(2,1)}, u32[]{:S(2)}, u32[]{:S(2)}) collective-permute-start(bf16[32,3584]{1,0:T(8,128)(2,1)} %bitcast.58), channel_id=1, source_target_pairs={{0,4},{1,5},{4,8},{5,9},{8,12},{9,13},{12,14},{13,15},{14,10},{15,... | collective-permute-start | bytes 688136 | tf_op jit(solution)/shard_map/ppermute | solution.py:326
  5.1 17.9 %all-to-all-start = ((bf16[16,2,8,576]{3,2,1,0:T(8,128)(2,1)}), bf16[16,2,8,576]{3,2,1,0:T(8,128)(2,1)S(1)}, u32[]{:S(2)}, u32[]{:S(2)}) async-start(bf16[16,2,8,576]{3,2,1,0:T(8,128)(2,1)} %copy.19), calls=%async_computation | async-start | bytes 655360 | tf_op jit(solution)/shard_map/all_to_all | solution.py:343
  11.4 4.0 %copy-start.4 = (bf16[3584]{0:T(1024)(128)(2,1)S(1)}, bf16[3584]{0:T(1024)(128)(2,1)}, u32[]{:S(2)}) copy-start(bf16[3584]{0:T(1024)(128)(2,1)} %param.22) | copy-start | bytes 21508
  11.4 11.6 %copy-start.1 = (bf16[4,8,36864]{2,1,0:T(8,128)(2,1)S(1)}, bf16[4,8,36864]{2,1,0:T(8,128)(2,1)}, u32[]{:S(2)}) copy-start(bf16[4,8,36864]{2,1,0:T(8,128)(2,1)} %refs_0_.1) | copy-start | bytes 7077892
  11.4 11.6 %copy-start.2 = (bf16[4,8,576]{2,1,0:T(8,128)(2,1)S(1)}, bf16[4,8,576]{2,1,0:T(8,128)(2,1)}, u32[]{:S(2)}) copy-start(bf16[4,8,576]{2,1,0:T(8,128)(2,1)} %param.15) | copy-start | bytes 110596
  11.5 11.5 %copy-start.3 = (s32[4,8,8]{2,1,0:T(8,128)S(1)}, s32[4,8,8]{2,1,0:T(8,128)}, u32[]{:S(2)}) copy-start(s32[4,8,8]{2,1,0:T(8,128)} %param.20) | copy-start | bytes 3076
  12.9 14.5 %collective-permute-start.4 = (bf16[32,3584]{1,0:T(8,128)(2,1)}, bf16[32,3584]{1,0:T(8,128)(2,1)}, u32[]{:S(2)}, u32[]{:S(2)}) collective-permute-start(bf16[32,3584]{1,0:T(8,128)(2,1)} %collective-permute-done.refs_13_), channel_id=1, source_target_pairs={{0,1},{1,0},{2,3},{3,2},{4,5},{5,4},{6,7},{7,6},{8,9},{9,8},{10,11... | collective-permute-start | bytes 688136 | tf_op jit(solution)/shard_map/ppermute | solution.py:326
  13.4 14.0 %collective-permute-start.2 = (bf16[32,3584]{1,0:T(8,128)(2,1)}, bf16[32,3584]{1,0:T(8,128)(2,1)S(1)}, u32[]{:S(2)}, u32[]{:S(2)}) collective-permute-start(bf16[32,3584]{1,0:T(8,128)(2,1)} %collective-permute-done.refs_13_), channel_id=1, source_target_pairs={{0,4},{1,5},{4,8},{5,9},{8,12},{9,13},{12,14},{13,15},{14,10},{15,... | collective-permute-start | bytes 688136 | tf_op jit(solution)/shard_map/ppermute | solution.py:326
  15.0 12.3 %collective-permute-start.6 = (bf16[32,3584]{1,0:T(8,128)(2,1)}, bf16[32,3584]{1,0:T(8,128)(2,1)}, u32[]{:S(2)}, u32[]{:S(2)}) collective-permute-start(bf16[32,3584]{1,0:T(8,128)(2,1)} %collective-permute-done.1.refs_12_), channel_id=1, source_target_pairs={{0,1},{1,0},{2,3},{3,2},{4,5},{5,4},{6,7},{7,6},{8,9},{9,8},{10,11... | collective-permute-start | bytes 688136 | tf_op jit(solution)/shard_map/ppermute | solution.py:326
  15.1 12.3 %collective-permute-start.3 = (bf16[32,3584]{1,0:T(8,128)(2,1)}, bf16[32,3584]{1,0:T(8,128)(2,1)S(1)}, u32[]{:S(2)}, u32[]{:S(2)}) collective-permute-start(bf16[32,3584]{1,0:T(8,128)(2,1)} %collective-permute-done.1.refs_12_), channel_id=1, source_target_pairs={{0,2},{1,3},{4,0},{5,1},{8,4},{9,5},{12,8},{13,9},{14,12},{15,13},... | collective-permute-start | bytes 688136 | tf_op jit(solution)/shard_map/ppermute | solution.py:326
  27.4 11.4 %collective-permute-start.10 = (bf16[32,3584]{1,0:T(8,128)(2,1)S(1)}, bf16[32,3584]{1,0:T(8,128)(2,1)S(1)}, u32[]{:S(2)}, u32[]{:S(2)}) collective-permute-start(bf16[32,3584]{1,0:T(8,128)(2,1)S(1)} %collective-permute-done.2.refs_15_), channel_id=1, source_target_pairs={{0,4},{1,5},{4,8},{5,9},{8,12},{9,13},{12,14},{13,15},{14,10},{15,... | collective-permute-start | bytes 688136 | tf_op jit(solution)/shard_map/ppermute | solution.py:326
  27.9 10.8 %collective-permute-start.11 = (bf16[32,3584]{1,0:T(8,128)(2,1)S(1)}, bf16[32,3584]{1,0:T(8,128)(2,1)S(1)}, u32[]{:S(2)}, u32[]{:S(2)}) collective-permute-start(bf16[32,3584]{1,0:T(8,128)(2,1)S(1)} %collective-permute-done.3.refs_14_), channel_id=1, source_target_pairs={{0,2},{1,3},{4,0},{5,1},{8,4},{9,5},{12,8},{13,9},{14,12},{15,13},... | collective-permute-start | bytes 688136 | tf_op jit(solution)/shard_map/ppermute | solution.py:326
  29.5 8.1 %collective-permute-start.9 = (bf16[32,640]{1,0:T(8,128)(2,1)S(1)}, bf16[32,640]{1,0:T(8,128)(2,1)S(1)}, u32[]{:S(2)}, u32[]{:S(2)}) collective-permute-start(bf16[32,640]{1,0:T(8,128)(2,1)S(1)} %attention.1), channel_id=1, source_target_pairs={{0,12},{1,13},{2,14},{3,15},{4,8},{5,9},{6,10},{7,11},{8,4},{9,5},... | collective-permute-start | bytes 122888 | tf_op jit(solution)/shard_map/ppermute | solution.py:326
  30.2 8.5 %collective-permute-start.8 = (bf16[32,640]{1,0:T(8,128)(2,1)S(1)}, bf16[32,640]{1,0:T(8,128)(2,1)S(1)}, u32[]{:S(2)}, u32[]{:S(2)}) collective-permute-start(bf16[32,640]{1,0:T(8,128)(2,1)S(1)} %attention.1), channel_id=1, source_target_pairs={{0,8},{1,9},{2,10},{3,11},{4,12},{5,13},{6,14},{7,15},{8,0},{9,1},... | collective-permute-start | bytes 122888 | tf_op jit(solution)/shard_map/ppermute | solution.py:326
  31.4 7.3 %collective-permute-start.7 = (bf16[32,640]{1,0:T(8,128)(2,1)S(1)}, bf16[32,640]{1,0:T(8,128)(2,1)S(1)}, u32[]{:S(2)}, u32[]{:S(2)}) collective-permute-start(bf16[32,640]{1,0:T(8,128)(2,1)S(1)} %attention.1), channel_id=1, source_target_pairs={{0,4},{1,5},{2,6},{3,7},{4,0},{5,1},{6,2},{7,3},{8,12},{9,13},{10,... | collective-permute-start | bytes 122888 | tf_op jit(solution)/shard_map/ppermute | solution.py:326
  38.8 10.0 %collective-permute-start.15 = (bf16[32,3584]{1,0:T(8,128)(2,1)S(1)}, bf16[32,3584]{1,0:T(8,128)(2,1)S(1)}, u32[]{:S(2)}, u32[]{:S(2)}) collective-permute-start(bf16[32,3584]{1,0:T(8,128)(2,1)S(1)} %collective-permute-done.2.refs_15_), channel_id=1, source_target_pairs={{0,1},{1,0},{2,3},{3,2},{4,5},{5,4},{6,7},{7,6},{8,9},{9,8},{10,11... | collective-permute-start | bytes 688136 | tf_op jit(solution)/shard_map/ppermute | solution.py:326
  38.8 9.9 %collective-permute-start.16 = (bf16[32,3584]{1,0:T(8,128)(2,1)S(1)}, bf16[32,3584]{1,0:T(8,128)(2,1)S(1)}, u32[]{:S(2)}, u32[]{:S(2)}) collective-permute-start(bf16[32,3584]{1,0:T(8,128)(2,1)S(1)} %collective-permute-done.3.refs_14_), channel_id=1, source_target_pairs={{0,1},{1,0},{2,3},{3,2},{4,5},{5,4},{6,7},{7,6},{8,9},{9,8},{10,11... | collective-permute-start | bytes 688136 | tf_op jit(solution)/shard_map/ppermute | solution.py:326
  39.4 9.4 %collective-permute-start.14 = (bf16[32,3584]{1,0:T(8,128)(2,1)S(1)}, bf16[32,3584]{1,0:T(8,128)(2,1)S(1)}, u32[]{:S(2)}, u32[]{:S(2)}) collective-permute-start(bf16[32,3584]{1,0:T(8,128)(2,1)S(1)} %broadcast_select_fusion), channel_id=1, source_target_pairs={{0,8},{1,7},{4,12},{5,3},{8,14},{9,1},{12,10},{13,5},{14,6},{15,9}... | collective-permute-start | bytes 688136 | tf_op jit(solution)/shard_map/ppermute | solution.py:326
  39.6 2.2 %collective-permute-start.13 = (bf16[128,640]{1,0:T(8,128)(2,1)S(1)}, bf16[128,640]{1,0:T(8,128)(2,1)S(1)}, u32[]{:S(2)}, u32[]{:S(2)}) collective-permute-start(bf16[128,640]{1,0:T(8,128)(2,1)S(1)} %constant_dynamic-update-slice_fusion.refs_1_), channel_id=1, source_target_pairs={{0,1},{1,0},{2,3},{3,2},{4,5},{5,4},{6,7},{7,6},{8,9},{9,8},{10,11... | collective-permute-start | bytes 491528 | tf_op jit(solution)/shard_map/ppermute | solution.py:326
  40.1 8.6 %collective-permute-start.12 = (bf16[128,640]{1,0:T(8,128)(2,1)S(1)}, bf16[128,640]{1,0:T(8,128)(2,1)S(1)}, u32[]{:S(2)}, u32[]{:S(2)}) collective-permute-start(bf16[128,640]{1,0:T(8,128)(2,1)S(1)} %constant_dynamic-update-slice_fusion.refs_1_), channel_id=1, source_target_pairs={{0,2},{1,3},{2,0},{3,1},{4,6},{5,7},{6,4},{7,5},{8,10},{9,11},{10,... | collective-permute-start | bytes 491528 | tf_op jit(solution)/shard_map/ppermute | solution.py:326
  48.8 2.4 %collective-permute-start.18 = (bf16[32,3584]{1,0:T(8,128)(2,1)S(1)}, bf16[32,3584]{1,0:T(8,128)(2,1)S(1)}, u32[]{:S(2)}, u32[]{:S(2)}) collective-permute-start(bf16[32,3584]{1,0:T(8,128)(2,1)S(1)} %collective-permute-done.14.refs_5_), channel_id=1, source_target_pairs={{0,1},{1,0},{2,3},{3,2},{4,5},{5,4},{6,7},{7,6},{8,9},{9,8},{10,11... | collective-permute-start | bytes 688136 | tf_op jit(solution)/shard_map/ppermute | solution.py:326
  48.9 2.4 %collective-permute-start.19 = (bf16[32,3584]{1,0:T(8,128)(2,1)S(1)}, bf16[32,3584]{1,0:T(8,128)(2,1)S(1)}, u32[]{:S(2)}, u32[]{:S(2)}) collective-permute-start(bf16[32,3584]{1,0:T(8,128)(2,1)S(1)} %collective-permute-done.11.refs_6_), channel_id=1, source_target_pairs={{0,1},{1,0},{2,3},{3,2},{4,5},{5,4},{6,7},{7,6},{8,9},{9,8},{10,11... | collective-permute-start | bytes 688136 | tf_op jit(solution)/shard_map/ppermute | solution.py:326
  49.4 1.9 %collective-permute-start.20 = (bf16[32,3584]{1,0:T(8,128)(2,1)S(1)}, bf16[32,3584]{1,0:T(8,128)(2,1)S(1)}, u32[]{:S(2)}, u32[]{:S(2)}) collective-permute-start(bf16[32,3584]{1,0:T(8,128)(2,1)S(1)} %collective-permute-done.10.refs_7_), channel_id=1, source_target_pairs={{0,1},{1,0},{2,3},{3,2},{4,5},{5,4},{6,7},{7,6},{8,9},{9,8},{10,11... | collective-permute-start | bytes 688136 | tf_op jit(solution)/shard_map/ppermute | solution.py:326
  49.4 1.8 %collective-permute-start.17 = (bf16[128,640]{1,0:T(8,128)(2,1)S(1)}, bf16[128,640]{1,0:T(8,128)(2,1)S(1)}, u32[]{:S(2)}, u32[]{:S(2)}) collective-permute-start(bf16[128,640]{1,0:T(8,128)(2,1)S(1)} %collective-permute-done.12.refs_2_), channel_id=1, source_target_pairs={{0,1},{1,0},{2,3},{3,2},{4,5},{5,4},{6,7},{7,6},{8,9},{9,8},{10,11... | collective-permute-start | bytes 491528 | tf_op jit(solution)/shard_map/ppermute | solution.py:326
  51.2 13.7 %slice-start.2 = ((s8[7340032]{0:T(1024)(128)(4,1)}), s8[4194304]{0:T(1024)(128)(4,1)S(1)}, s32[]{:S(2)}) async-start(s8[7340032]{0:T(1024)(128)(4,1)} %bitcast.63), calls=%async_computation.3 | async-start | bytes 8388608
  60.0 4.9 %slice-start.3 = ((s8[7340032]{0:T(1024)(128)(4,1)}), s8[3145728]{0:T(1024)(128)(4,1)S(1)}, s32[]{:S(2)}) async-start(s8[7340032]{0:T(1024)(128)(4,1)} %bitcast.63), calls=%async_computation.4 | async-start | bytes 6291456
  60.0 6.7 %slice-start.4 = ((s8[7340032]{0:T(1024)(128)(4,1)}), s8[4194304]{0:T(1024)(128)(4,1)S(1)}, s32[]{:S(2)}) async-start(s8[7340032]{0:T(1024)(128)(4,1)} %bitcast.65), calls=%async_computation.5 | async-start | bytes 8388608
  60.0 9.4 %slice-start = ((s8[7340032]{0:T(1024)(128)(4,1)}), s8[4194304]{0:T(1024)(128)(4,1)S(1)}, s32[]{:S(2)}) async-start(s8[7340032]{0:T(1024)(128)(4,1)} %bitcast.61), calls=%async_computation.1 | async-start | bytes 8388608
  64.9 2.7 %slice-start.5 = ((s8[7340032]{0:T(1024)(128)(4,1)}), s8[3145728]{0:T(1024)(128)(4,1)S(1)}, s32[]{:S(2)}) async-start(s8[7340032]{0:T(1024)(128)(4,1)} %bitcast.65), calls=%async_computation.6 | async-start | bytes 6291456
  64.9 4.6 %slice-start.1 = ((s8[7340032]{0:T(1024)(128)(4,1)}), s8[3145728]{0:T(1024)(128)(4,1)S(1)}, s32[]{:S(2)}) async-start(s8[7340032]{0:T(1024)(128)(4,1)} %bitcast.61), calls=%async_computation.2 | async-start | bytes 6291456
  69.2 2.9 %collective-permute-start.21 = (bf16[96,3584]{1,0:T(8,128)(2,1)S(1)}, bf16[96,3584]{1,0:T(8,128)(2,1)S(1)}, u32[]{:S(2)}, u32[]{:S(2)}) collective-permute-start(bf16[96,3584]{1,0:T(8,128)(2,1)S(1)} %slice.98), channel_id=1, source_target_pairs={{0,1},{1,0},{2,3},{3,2},{4,5},{5,4},{6,7},{7,6},{8,9},{9,8},{10,11... | collective-permute-start | bytes 2064392 | tf_op jit(solution)/shard_map/ppermute | solution.py:326
  72.3 5.4 %collective-permute-start.23 = (bf16[16,3584]{1,0:T(8,128)(2,1)S(1)}, bf16[16,3584]{1,0:T(8,128)(2,1)S(1)}, u32[]{:S(2)}, u32[]{:S(2)}) collective-permute-start(bf16[16,3584]{1,0:T(8,128)(2,1)S(1)} %get-tuple-element.133), channel_id=1, source_target_pairs={{0,2},{1,3},{4,0},{5,1},{8,4},{9,5},{12,8},{13,9},{14,12},{15,13},... | collective-permute-start | bytes 344072 | tf_op jit(solution)/shard_map/ppermute | solution.py:326
  73.7 5.1 %collective-permute-start.22 = (bf16[16,3584]{1,0:T(8,128)(2,1)S(1)}, bf16[16,3584]{1,0:T(8,128)(2,1)S(1)}, u32[]{:S(2)}, u32[]{:S(2)}) collective-permute-start(bf16[16,3584]{1,0:T(8,128)(2,1)S(1)} %get-tuple-element.134), channel_id=1, source_target_pairs={{0,4},{1,5},{4,8},{5,9},{8,12},{9,13},{12,14},{13,15},{14,10},{15,... | collective-permute-start | bytes 344072 | tf_op jit(solution)/shard_map/ppermute | solution.py:326
  81.5 9.2 %collective-permute-start.24 = (bf16[160,3584]{1,0:T(8,128)(2,1)S(1)}, bf16[160,3584]{1,0:T(8,128)(2,1)S(1)}, u32[]{:S(2)}, u32[]{:S(2)}) collective-permute-start(bf16[160,3584]{1,0:T(8,128)(2,1)S(1)} %slice.101), channel_id=1, source_target_pairs={{0,1},{1,0},{2,3},{3,2},{4,5},{5,4},{6,7},{7,6},{8,9},{9,8},{10,11... | collective-permute-start | bytes 3440648 | tf_op jit(solution)/shard_map/ppermute | solution.py:326
  81.7 8.1 %collective-permute-start.26 = (bf16[32,3584]{1,0:T(8,128)(2,1)S(1)}, bf16[32,3584]{1,0:T(8,128)(2,1)S(1)}, u32[]{:S(2)}, u32[]{:S(2)}) collective-permute-start(bf16[32,3584]{1,0:T(8,128)(2,1)S(1)} %get-tuple-element.131), channel_id=1, source_target_pairs={{0,2},{1,3},{4,0},{5,1},{8,4},{9,5},{12,8},{13,9},{14,12},{15,13},... | collective-permute-start | bytes 688136 | tf_op jit(solution)/shard_map/ppermute | solution.py:326
  83.0 7.7 %collective-permute-start.25 = (bf16[32,3584]{1,0:T(8,128)(2,1)S(1)}, bf16[32,3584]{1,0:T(8,128)(2,1)S(1)}, u32[]{:S(2)}, u32[]{:S(2)}) collective-permute-start(bf16[32,3584]{1,0:T(8,128)(2,1)S(1)} %get-tuple-element.132), channel_id=1, source_target_pairs={{0,4},{1,5},{4,8},{5,9},{8,12},{9,13},{12,14},{13,15},{14,10},{15,... | collective-permute-start | bytes 688136 | tf_op jit(solution)/shard_map/ppermute | solution.py:326
  90.9 7.0 %collective-permute-start.28 = (bf16[32,3584]{1,0:T(8,128)(2,1)S(1)}, bf16[32,3584]{1,0:T(8,128)(2,1)S(1)}, u32[]{:S(2)}, u32[]{:S(2)}) collective-permute-start(bf16[32,3584]{1,0:T(8,128)(2,1)S(1)} %get-tuple-element.129), channel_id=1, source_target_pairs={{0,2},{1,3},{4,0},{5,1},{8,4},{9,5},{12,8},{13,9},{14,12},{15,13},... | collective-permute-start | bytes 688136 | tf_op jit(solution)/shard_map/ppermute | solution.py:326
  92.7 6.6 %collective-permute-start.27 = (bf16[32,3584]{1,0:T(8,128)(2,1)S(1)}, bf16[32,3584]{1,0:T(8,128)(2,1)S(1)}, u32[]{:S(2)}, u32[]{:S(2)}) collective-permute-start(bf16[32,3584]{1,0:T(8,128)(2,1)S(1)} %get-tuple-element.130), channel_id=1, source_target_pairs={{0,4},{1,5},{4,8},{5,9},{8,12},{9,13},{12,14},{13,15},{14,10},{15,... | collective-permute-start | bytes 688136 | tf_op jit(solution)/shard_map/ppermute | solution.py:326
  99.5 6.1 %collective-permute-start.30 = (bf16[32,3584]{1,0:T(8,128)(2,1)S(1)}, bf16[32,3584]{1,0:T(8,128)(2,1)S(1)}, u32[]{:S(2)}, u32[]{:S(2)}) collective-permute-start(bf16[32,3584]{1,0:T(8,128)(2,1)S(1)} %get-tuple-element.127), channel_id=1, source_target_pairs={{0,2},{1,3},{4,0},{5,1},{8,4},{9,5},{12,8},{13,9},{14,12},{15,13},... | collective-permute-start | bytes 688136 | tf_op jit(solution)/shard_map/ppermute | solution.py:326
  100.1 6.0 %collective-permute-start.29 = (bf16[32,3584]{1,0:T(8,128)(2,1)S(1)}, bf16[32,3584]{1,0:T(8,128)(2,1)S(1)}, u32[]{:S(2)}, u32[]{:S(2)}) collective-permute-start(bf16[32,3584]{1,0:T(8,128)(2,1)S(1)} %get-tuple-element.128), channel_id=1, source_target_pairs={{0,4},{1,5},{4,8},{5,9},{8,12},{9,13},{12,14},{13,15},{14,10},{15,... | collective-permute-start | bytes 688136 | tf_op jit(solution)/shard_map/ppermute | solution.py:326

commit v16 on v15

--- a/solution.py
+++ b/solution.py
@@ -134,7 +134,7 @@
     rows, width = resid_blocks[0].shape
     latent = w_out.shape[0]
     total = blocks * rows
-    cols = tile_of(width, 512)
+    cols = tile_of(width, 1024)
     packed = pooled[0].shape[1]
     experts_all = w_router_t.shape[0]
 
@@ -144,7 +144,7 @@
     def tiles(height):
         return pl.BlockSpec((height, cols), lambda i: (0, i))
 
-    need = total * (cols * 24 + packed * 6 + 8 * LANES * 4) + 4 * latent * cols
+    need = total * (cols * 16 + packed * 6 + 8 * LANES * 4) + 4 * latent * cols
     return pl.pallas_call(
         lambda *refs: norm_kernel(far, blocks, rows, latent, width, *refs),
         grid=(width // cols,),
@@ -172,7 +172,7 @@
         ),
         cost_estimate=pl.CostEstimate(
             flops=2 * total * width * latent,
-            bytes_accessed=2 * total * width * 2 + latent * width * 2,
+            bytes_accessed=4 * total * width * 2 + latent * width * 2,
             transcendentals=total,
         ),
         name="normalize",

time: 107 us -> 106 us (level)
  Pallas kernels: 14.2 us -> 12.8 us
    pallas_call x1, Pallas kernels: 8.43 us -> 7.08 us  [normalize(): pl.pallas_call(lambda *refs: norm_kernel(far, blocks, rows, latent, width...]
where the time goes in v16:
time: 106 us; the launch traced here: 105 us
  waiting for transfers between devices  40.5 us (38%)
  starting transfers between devices  31.2 us (29%)
  matrix products  16.8 us (16%)
  Pallas kernels  12.8 us (12%)
  local copies, waits for them, and re-layouts  2.45 us (2%)
  other arithmetic  1.37 us (1%)
    ppermute x31, waiting for transfers between devices, send(): return lax.ppermute(a, 'expert', perm)  32.9 us
    ppermute x31, starting transfers between devices, send(): return lax.ppermute(a, 'expert', perm)  24.9 us
    dot_general x6, matrix products, product(): return jnp.dot(a, w[0], preferred_element_type=f32)  15.8 us
    all_to_all x1, waiting for transfers between devices, local(): lax.all_to_all(ordered, 'expert', split_axis=0, concat_axis=0, tiled=True)  7.6 us
    pallas_call x1, Pallas kernels, normalize(): pl.pallas_call(lambda *refs: norm_kernel(far, blocks, rows, latent, width...  7.08 us
    all_to_all x1, starting transfers between devices, local(): lax.all_to_all(ordered, 'expert', split_axis=0, concat_axis=0, tiled=True)  6.29 us
    pallas_call x1, Pallas kernels, attention(): pl.pallas_call(lambda *refs: attention_kernel(context, latent, *refs), gr...  4.33 us
  transfers between devices with their start and end apart: 32, of which 13 were waited for; matrix products, arithmetic and copies ran while one was open for 7% of the time, Pallas kernels for 5%

profile of v16, /device:TPU:0, one launch (start us, length us, event | category | flops | bytes accessed | tf_op | source)
XLA Modules:
  0.0 105.5 jit_solution(2294078134082332487)
XLA Ops:
  0.0 0.5 collective-permute-start.5
  0.5 2.6 %collective-permute-start.1 = (bf16[32,3584]{1,0:T(8,128)(2,1)}, bf16[32,3584]{1,0:T(8,128)(2,1)}, u32[]{:S(2)}, u32[]{:S(2)}) collective-permute-start(bf16[32,3584]{1,0:T(8,128)(2,1)} %bitcast.57), channel_id=1, source_target_pairs={{0,2},{1,3},{4,0},{5,1},{8,4},{9,5},{12,8},{13,9},{14,12},{15,13},... | collective-permute-start | bytes 688136 | tf_op jit(solution)/shard_map/ppermute | solution.py:326
  3.2 1.0 fusion.27
  4.4 0.7 copy.19
  5.1 6.3 %all-to-all-start = ((bf16[16,2,8,576]{3,2,1,0:T(8,128)(2,1)}), bf16[16,2,8,576]{3,2,1,0:T(8,128)(2,1)S(1)}, u32[]{:S(2)}, u32[]{:S(2)}) async-start(bf16[16,2,8,576]{3,2,1,0:T(8,128)(2,1)} %copy.19), calls=%async_computation | async-start | bytes 655360 | tf_op jit(solution)/shard_map/all_to_all | solution.py:343
  11.5 1.4 %lookup.1 = (s32[8]{0:T(128)}, s32[17]{0:T(128)}) custom-call(s32[128]{0:T(128)} %owner.1, s32[128]{0:T(128)} %lengths.1, s32[272]{0:T(512)} %constant.41.table, s32[1]{0:T(128)} %bitcast.device), custom_call_target="tpu_custom_call" | custom-call | flops 10000000000 | bytes 100000000 | tf_op jit(solution)/shard_map/lookup/pallas_call | solution.py:194
  12.9 0.5 collective-permute-start.4
  13.4 1.7 %collective-permute-start.2 = (bf16[32,3584]{1,0:T(8,128)(2,1)}, bf16[32,3584]{1,0:T(8,128)(2,1)S(1)}, u32[]{:S(2)}, u32[]{:S(2)}) collective-permute-start(bf16[32,3584]{1,0:T(8,128)(2,1)} %collective-permute-done.refs_13_), channel_id=1, source_target_pairs={{0,4},{1,5},{4,8},{5,9},{8,12},{9,13},{12,14},{13,15},{14,10},{15,... | collective-permute-start | bytes 688136 | tf_op jit(solution)/shard_map/ppermute | solution.py:326
  15.4 7.6 %all-to-all-done = bf16[16,2,8,576]{3,2,1,0:T(8,128)(2,1)S(1)} async-done(((bf16[16,2,8,576]{3,2,1,0:T(8,128)(2,1)}), bf16[16,2,8,576]{3,2,1,0:T(8,128)(2,1)S(1)}, u32[]{:S(2)}, u32[]{:S(2)}) %all-to-all-start) | async-done | bytes 294944 | tf_op jit(solution)/shard_map/all_to_all | solution.py:343
  23.0 4.3 %attention.1 = bf16[32,640]{1,0:T(8,128)(2,1)S(1)} custom-call(bf16[4,8,36864]{2,1,0:T(8,128)(2,1)S(1)} %copy-done.1, bf16[256,576]{1,0:T(8,128)(2,1)S(1)} %bitcast.52, bf16[32,576]{1,0:T(8,128)(2,1)S(1)} %bitcast.53, s32[8]{0:T(128)} %get-tuple-element.69.refs_3_, s32[32,8]{1,0:T(8,128)S(1)} %bitcast.54), custom_call_target="tpu_custom_call" | custom-call | flops 679477248 | bytes 2359296 | tf_op jit(solution)/shard_map/attention/pallas_call | solution.py:274
  27.4 0.6 collective-permute-start.10
  27.9 1.5 %collective-permute-start.11 = (bf16[32,3584]{1,0:T(8,128)(2,1)S(1)}, bf16[32,3584]{1,0:T(8,128)(2,1)S(1)}, u32[]{:S(2)}, u32[]{:S(2)}) collective-permute-start(bf16[32,3584]{1,0:T(8,128)(2,1)S(1)} %collective-permute-done.3.refs_14_), channel_id=1, source_target_pairs={{0,2},{1,3},{4,0},{5,1},{8,4},{9,5},{12,8},{13,9},{14,12},{15,13},... | collective-permute-start | bytes 688136 | tf_op jit(solution)/shard_map/ppermute | solution.py:326
  29.5 0.8 collective-permute-start.9
  30.2 1.2 %collective-permute-start.8 = (bf16[32,640]{1,0:T(8,128)(2,1)S(1)}, bf16[32,640]{1,0:T(8,128)(2,1)S(1)}, u32[]{:S(2)}, u32[]{:S(2)}) collective-permute-start(bf16[32,640]{1,0:T(8,128)(2,1)S(1)} %attention.1), channel_id=1, source_target_pairs={{0,8},{1,9},{2,10},{3,11},{4,12},{5,13},{6,14},{7,15},{8,0},{9,1},... | collective-permute-start | bytes 122888 | tf_op jit(solution)/shard_map/ppermute | solution.py:326
  31.4 2.4 %collective-permute-start.7 = (bf16[32,640]{1,0:T(8,128)(2,1)S(1)}, bf16[32,640]{1,0:T(8,128)(2,1)S(1)}, u32[]{:S(2)}, u32[]{:S(2)}) collective-permute-start(bf16[32,640]{1,0:T(8,128)(2,1)S(1)} %attention.1), channel_id=1, source_target_pairs={{0,4},{1,5},{2,6},{3,7},{4,0},{5,1},{6,2},{7,3},{8,12},{9,13},{10,... | collective-permute-start | bytes 122888 | tf_op jit(solution)/shard_map/ppermute | solution.py:326
  33.9 3.7 %collective-permute-done.9 = bf16[32,640]{1,0:T(8,128)(2,1)S(1)} collective-permute-done((bf16[32,640]{1,0:T(8,128)(2,1)S(1)}, bf16[32,640]{1,0:T(8,128)(2,1)S(1)}, u32[]{:S(2)}, u32[]{:S(2)}) %collective-permute-start.9) | collective-permute-done | bytes 40992 | tf_op jit(solution)/shard_map/ppermute | solution.py:326
  37.5 1.2 %collective-permute-done.8 = bf16[32,640]{1,0:T(8,128)(2,1)S(1)} collective-permute-done((bf16[32,640]{1,0:T(8,128)(2,1)S(1)}, bf16[32,640]{1,0:T(8,128)(2,1)S(1)}, u32[]{:S(2)}, u32[]{:S(2)}) %collective-permute-start.8) | collective-permute-done | bytes 40992 | tf_op jit(solution)/shard_map/ppermute | solution.py:326
  38.8 0.5 collective-permute-start.16
  39.6 0.5 collective-permute-start.13
  40.1 1.7 %collective-permute-start.12 = (bf16[128,640]{1,0:T(8,128)(2,1)S(1)}, bf16[128,640]{1,0:T(8,128)(2,1)S(1)}, u32[]{:S(2)}, u32[]{:S(2)}) collective-permute-start(bf16[128,640]{1,0:T(8,128)(2,1)S(1)} %constant_dynamic-update-slice_fusion.refs_1_), channel_id=1, source_target_pairs={{0,2},{1,3},{2,0},{3,1},{4,6},{5,7},{6,4},{7,5},{8,10},{9,11},{10,... | collective-permute-start | bytes 491528 | tf_op jit(solution)/shard_map/ppermute | solution.py:326
  41.9 6.9 %collective-permute-done.12.refs_2_ = bf16[128,640]{1,0:T(8,128)(2,1)S(1)} collective-permute-done((bf16[128,640]{1,0:T(8,128)(2,1)S(1)}, bf16[128,640]{1,0:T(8,128)(2,1)S(1)}, u32[]{:S(2)}, u32[]{:S(2)}) %collective-permute-start.12) | collective-permute-done | bytes 163872 | tf_op jit(solution)/shard_map/ppermute | solution.py:326
  48.9 0.5 collective-permute-start.19
  49.4 0.4 collective-permute-start.17
  49.9 1.4 %collective-permute-done.17.refs_4_ = bf16[128,640]{1,0:T(8,128)(2,1)S(1)} collective-permute-done((bf16[128,640]{1,0:T(8,128)(2,1)S(1)}, bf16[128,640]{1,0:T(8,128)(2,1)S(1)}, u32[]{:S(2)}, u32[]{:S(2)}) %collective-permute-start.17) | collective-permute-done | bytes 163872 | tf_op jit(solution)/shard_map/ppermute | solution.py:326
  51.2 7.1 %normalize.1 = (bf16[192,3584]{1,0:T(8,128)(2,1)S(1)}, bf16[320,3584]{1,0:T(8,128)(2,1)S(1)}, f32[512,128]{1,0:T(8,128)S(1)}, f32[512,128]{1,0:T(8,128)S(1)}, f32[32,3584]{1,0:T(8,128)S(1)}) custom-call(s32[17]{0:T(128)} %get-tuple-element.68.refs_0_, bf16[128,640]{1,0:T(8,128)(2,1)S(1)} %constant_dynamic-update-slice_fusion.refs_1_, ...), custom_call_target="tpu_custom_call" | custom-call | flops 1879048192 | bytes 18350080 | tf_op jit(solution)/shard_map/normalize/pallas_call | solution.py:148
  58.7 4.8 %fusion.21 = f32[192,1024]{1,0:T(8,128)S(1)} fusion(bf16[192,3584]{1,0:T(8,128)(2,1)S(1)} %get-tuple-element.110, bf16[1,3584,1024]{2,1,0:T(8,128)(2,1)} %param.24, f32[192]{0:T(256)S(1)} %get-tuple-element.138), kind=kOutput, calls=%fused_computation.16 | convolution fusion | flops 1409482752 | bytes 9503488 | tf_op jit(solution)/shard_map/dot_general | solution.py:403
  63.6 1.7 %multiply_convert_fusion.1 = bf16[192,1024]{1,0:T(8,128)(2,1)S(1)} fusion(f32[192,1024]{1,0:T(8,128)S(1)} %fusion.21, f32[192]{0:T(256)S(1)} %get-tuple-element.137, f32[192]{0:T(256)S(1)} %get-tuple-element.138, bf16[192,3584]{1,0:T(8,128)(2,1)S(1)} %get-tuple-element.110, bf16[1,3584,1024]{2,1,0:T(8,128)(2,1)S(1)} %bitcast.64), kind=kOutput, calls=%fused_computation.20 | convolution fusion | flops 1410859008 | bytes 9897472 | tf_op jit(solution)/shard_map/dot_general | solution.py:403
  65.3 0.9 slice-done.5
  66.2 1.6 %fusion.15 = bf16[192,3584]{1,0:T(8,128)(2,1)S(1)} fusion(bf16[192,1024]{1,0:T(8,128)(2,1)S(1)} %multiply_convert_fusion.1, bf16[1,1024,3584]{2,1,0:T(8,128)(2,1)S(1)} %bitcast.66), kind=kOutput, calls=%fused_computation.13 | convolution fusion | flops 1409974272 | bytes 9109504 | tf_op jit(solution)/shard_map/dot_general | solution.py:403
  68.1 2.5 %fusion.10 = f32[320,1024]{1,0:T(8,128)S(1)} fusion(bf16[320,3584]{1,0:T(8,128)(2,1)S(1)} %get-tuple-element.109, bf16[1,3584,1024]{2,1,0:T(8,128)(2,1)S(1)} %bitcast.62), kind=kOutput, calls=%fused_computation.10 | convolution fusion | flops 2348810240 | bytes 10944512 | tf_op jit(solution)/shard_map/dot_general | solution.py:403
  70.8 1.5 %collective-permute-start.23 = (bf16[16,3584]{1,0:T(8,128)(2,1)S(1)}, bf16[16,3584]{1,0:T(8,128)(2,1)S(1)}, u32[]{:S(2)}, u32[]{:S(2)}) collective-permute-start(bf16[16,3584]{1,0:T(8,128)(2,1)S(1)} %get-tuple-element.133), channel_id=1, source_target_pairs={{0,2},{1,3},{4,0},{5,1},{8,4},{9,5},{12,8},{13,9},{14,12},{15,13},... | collective-permute-start | bytes 344072 | tf_op jit(solution)/shard_map/ppermute | solution.py:326
  72.3 0.6 collective-permute-start.22
  72.9 2.7 %multiply_convert_fusion = bf16[320,1024]{1,0:T(8,128)(2,1)S(1)} fusion(f32[320,1024]{1,0:T(8,128)S(1)} %fusion.10, f32[320]{0:T(512)S(1)} %get-tuple-element.135, f32[320]{0:T(512)S(1)} %get-tuple-element.136, bf16[320,3584]{1,0:T(8,128)(2,1)S(1)} %get-tuple-element.109, bf16[1,3584,1024]{2,1,0:T(8,128)(2,1)S(1)} %bitcast.64), kind=kOutput, calls=%fused_computation.15 | convolution fusion | flops 2351759360 | bytes 11602432 | tf_op jit(solution)/shard_map/dot_general | solution.py:403
  75.5 0.7 collective-permute-done.23
  76.2 1.1 %collective-permute-done.22 = bf16[16,3584]{1,0:T(8,128)(2,1)S(1)} collective-permute-done((bf16[16,3584]{1,0:T(8,128)(2,1)S(1)}, bf16[16,3584]{1,0:T(8,128)(2,1)S(1)}, u32[]{:S(2)}, u32[]{:S(2)}) %collective-permute-start.22) | collective-permute-done | bytes 114720 | tf_op jit(solution)/shard_map/ppermute | solution.py:326
  77.4 2.5 %fusion.12 = bf16[320,3584]{1,0:T(8,128)(2,1)S(1)} fusion(bf16[320,1024]{1,0:T(8,128)(2,1)S(1)} %multiply_convert_fusion, bf16[1,1024,3584]{2,1,0:T(8,128)(2,1)S(1)} %bitcast.66), kind=kOutput, calls=%fused_computation.12 | convolution fusion | flops 2349957120 | bytes 10289152 | tf_op jit(solution)/shard_map/dot_general | solution.py:403
  80.2 1.3 %collective-permute-start.26 = (bf16[32,3584]{1,0:T(8,128)(2,1)S(1)}, bf16[32,3584]{1,0:T(8,128)(2,1)S(1)}, u32[]{:S(2)}, u32[]{:S(2)}) collective-permute-start(bf16[32,3584]{1,0:T(8,128)(2,1)S(1)} %get-tuple-element.131), channel_id=1, source_target_pairs={{0,2},{1,3},{4,0},{5,1},{8,4},{9,5},{12,8},{13,9},{14,12},{15,13},... | collective-permute-start | bytes 688136 | tf_op jit(solution)/shard_map/ppermute | solution.py:326
  81.5 0.8 collective-permute-start.25
  82.3 6.0 %collective-permute-done.26 = bf16[32,3584]{1,0:T(8,128)(2,1)S(1)} collective-permute-done((bf16[32,3584]{1,0:T(8,128)(2,1)S(1)}, bf16[32,3584]{1,0:T(8,128)(2,1)S(1)}, u32[]{:S(2)}, u32[]{:S(2)}) %collective-permute-start.26) | collective-permute-done | bytes 229408 | tf_op jit(solution)/shard_map/ppermute | solution.py:326
  88.2 1.0 collective-permute-done.25
  89.4 1.8 %collective-permute-start.28 = (bf16[32,3584]{1,0:T(8,128)(2,1)S(1)}, bf16[32,3584]{1,0:T(8,128)(2,1)S(1)}, u32[]{:S(2)}, u32[]{:S(2)}) collective-permute-start(bf16[32,3584]{1,0:T(8,128)(2,1)S(1)} %get-tuple-element.129), channel_id=1, source_target_pairs={{0,2},{1,3},{4,0},{5,1},{8,4},{9,5},{12,8},{13,9},{14,12},{15,13},... | collective-permute-start | bytes 688136 | tf_op jit(solution)/shard_map/ppermute | solution.py:326
  91.5 4.9 %collective-permute-done.28 = bf16[32,3584]{1,0:T(8,128)(2,1)S(1)} collective-permute-done((bf16[32,3584]{1,0:T(8,128)(2,1)S(1)}, bf16[32,3584]{1,0:T(8,128)(2,1)S(1)}, u32[]{:S(2)}, u32[]{:S(2)}) %collective-permute-start.28) | collective-permute-done | bytes 229408 | tf_op jit(solution)/shard_map/ppermute | solution.py:326
  96.3 1.5 %collective-permute-done.27 = bf16[32,3584]{1,0:T(8,128)(2,1)S(1)} collective-permute-done((bf16[32,3584]{1,0:T(8,128)(2,1)S(1)}, bf16[32,3584]{1,0:T(8,128)(2,1)S(1)}, u32[]{:S(2)}, u32[]{:S(2)}) %collective-permute-start.27) | collective-permute-done | bytes 229408 | tf_op jit(solution)/shard_map/ppermute | solution.py:326
  98.0 0.7 collective-permute-start.30
  98.6 1.4 %collective-permute-start.29 = (bf16[32,3584]{1,0:T(8,128)(2,1)S(1)}, bf16[32,3584]{1,0:T(8,128)(2,1)S(1)}, u32[]{:S(2)}, u32[]{:S(2)}) collective-permute-start(bf16[32,3584]{1,0:T(8,128)(2,1)S(1)} %get-tuple-element.128), channel_id=1, source_target_pairs={{0,4},{1,5},{4,8},{5,9},{8,12},{9,13},{12,14},{13,15},{14,10},{15,... | collective-permute-start | bytes 688136 | tf_op jit(solution)/shard_map/ppermute | solution.py:326
  100.0 4.0 %collective-permute-done.30 = bf16[32,3584]{1,0:T(8,128)(2,1)S(1)} collective-permute-done((bf16[32,3584]{1,0:T(8,128)(2,1)S(1)}, bf16[32,3584]{1,0:T(8,128)(2,1)S(1)}, u32[]{:S(2)}, u32[]{:S(2)}) %collective-permute-start.30) | collective-permute-done | bytes 229408 | tf_op jit(solution)/shard_map/ppermute | solution.py:326
  104.0 0.6 collective-permute-done.29
  104.6 0.8 fusion.32
  (69 shorter events, 2.9 us)
Async XLA Ops:
  0.0 3.2 %copy-start = (bf16[128,2,576]{0,2,1:T(8,128)(2,1)S(1)}, bf16[128,2,576]{0,2,1:T(8,128)(2,1)}, u32[]{:S(2)}) copy-start(bf16[128,2,576]{0,2,1:T(8,128)(2,1)} %param.16) | copy-start | bytes 884740
  0.0 27.3 %collective-permute-start.5 = (bf16[32,3584]{1,0:T(8,128)(2,1)}, bf16[32,3584]{1,0:T(8,128)(2,1)}, u32[]{:S(2)}, u32[]{:S(2)}) collective-permute-start(bf16[32,3584]{1,0:T(8,128)(2,1)} %bitcast.56), channel_id=1, source_target_pairs={{0,1},{1,0},{2,3},{3,2},{4,5},{5,4},{6,7},{7,6},{8,9},{9,8},{10,11... | collective-permute-start | bytes 688136 | tf_op jit(solution)/shard_map/ppermute | solution.py:326
  0.5 12.4 %collective-permute-start.1 = (bf16[32,3584]{1,0:T(8,128)(2,1)}, bf16[32,3584]{1,0:T(8,128)(2,1)}, u32[]{:S(2)}, u32[]{:S(2)}) collective-permute-start(bf16[32,3584]{1,0:T(8,128)(2,1)} %bitcast.57), channel_id=1, source_target_pairs={{0,2},{1,3},{4,0},{5,1},{8,4},{9,5},{12,8},{13,9},{14,12},{15,13},... | collective-permute-start | bytes 688136 | tf_op jit(solution)/shard_map/ppermute | solution.py:326
  3.0 9.9 %collective-permute-start = (bf16[32,3584]{1,0:T(8,128)(2,1)}, bf16[32,3584]{1,0:T(8,128)(2,1)}, u32[]{:S(2)}, u32[]{:S(2)}) collective-permute-start(bf16[32,3584]{1,0:T(8,128)(2,1)} %bitcast.58), channel_id=1, source_target_pairs={{0,4},{1,5},{4,8},{5,9},{8,12},{9,13},{12,14},{13,15},{14,10},{15,... | collective-permute-start | bytes 688136 | tf_op jit(solution)/shard_map/ppermute | solution.py:326
  5.1 17.9 %all-to-all-start = ((bf16[16,2,8,576]{3,2,1,0:T(8,128)(2,1)}), bf16[16,2,8,576]{3,2,1,0:T(8,128)(2,1)S(1)}, u32[]{:S(2)}, u32[]{:S(2)}) async-start(bf16[16,2,8,576]{3,2,1,0:T(8,128)(2,1)} %copy.19), calls=%async_computation | async-start | bytes 655360 | tf_op jit(solution)/shard_map/all_to_all | solution.py:343
  11.4 4.0 %copy-start.4 = (bf16[3584]{0:T(1024)(128)(2,1)S(1)}, bf16[3584]{0:T(1024)(128)(2,1)}, u32[]{:S(2)}) copy-start(bf16[3584]{0:T(1024)(128)(2,1)} %param.22) | copy-start | bytes 21508
  11.4 11.6 %copy-start.1 = (bf16[4,8,36864]{2,1,0:T(8,128)(2,1)S(1)}, bf16[4,8,36864]{2,1,0:T(8,128)(2,1)}, u32[]{:S(2)}) copy-start(bf16[4,8,36864]{2,1,0:T(8,128)(2,1)} %refs_0_.1) | copy-start | bytes 7077892
  11.4 11.6 %copy-start.2 = (bf16[4,8,576]{2,1,0:T(8,128)(2,1)S(1)}, bf16[4,8,576]{2,1,0:T(8,128)(2,1)}, u32[]{:S(2)}) copy-start(bf16[4,8,576]{2,1,0:T(8,128)(2,1)} %param.15) | copy-start | bytes 110596
  11.5 11.5 %copy-start.3 = (s32[4,8,8]{2,1,0:T(8,128)S(1)}, s32[4,8,8]{2,1,0:T(8,128)}, u32[]{:S(2)}) copy-start(s32[4,8,8]{2,1,0:T(8,128)} %param.20) | copy-start | bytes 3076
  12.9 14.5 %collective-permute-start.4 = (bf16[32,3584]{1,0:T(8,128)(2,1)}, bf16[32,3584]{1,0:T(8,128)(2,1)}, u32[]{:S(2)}, u32[]{:S(2)}) collective-permute-start(bf16[32,3584]{1,0:T(8,128)(2,1)} %collective-permute-done.refs_13_), channel_id=1, source_target_pairs={{0,1},{1,0},{2,3},{3,2},{4,5},{5,4},{6,7},{7,6},{8,9},{9,8},{10,11... | collective-permute-start | bytes 688136 | tf_op jit(solution)/shard_map/ppermute | solution.py:326
  13.4 14.0 %collective-permute-start.2 = (bf16[32,3584]{1,0:T(8,128)(2,1)}, bf16[32,3584]{1,0:T(8,128)(2,1)S(1)}, u32[]{:S(2)}, u32[]{:S(2)}) collective-permute-start(bf16[32,3584]{1,0:T(8,128)(2,1)} %collective-permute-done.refs_13_), channel_id=1, source_target_pairs={{0,4},{1,5},{4,8},{5,9},{8,12},{9,13},{12,14},{13,15},{14,10},{15,... | collective-permute-start | bytes 688136 | tf_op jit(solution)/shard_map/ppermute | solution.py:326
  15.0 12.3 %collective-permute-start.6 = (bf16[32,3584]{1,0:T(8,128)(2,1)}, bf16[32,3584]{1,0:T(8,128)(2,1)}, u32[]{:S(2)}, u32[]{:S(2)}) collective-permute-start(bf16[32,3584]{1,0:T(8,128)(2,1)} %collective-permute-done.1.refs_12_), channel_id=1, source_target_pairs={{0,1},{1,0},{2,3},{3,2},{4,5},{5,4},{6,7},{7,6},{8,9},{9,8},{10,11... | collective-permute-start | bytes 688136 | tf_op jit(solution)/shard_map/ppermute | solution.py:326
  15.1 12.3 %collective-permute-start.3 = (bf16[32,3584]{1,0:T(8,128)(2,1)}, bf16[32,3584]{1,0:T(8,128)(2,1)S(1)}, u32[]{:S(2)}, u32[]{:S(2)}) collective-permute-start(bf16[32,3584]{1,0:T(8,128)(2,1)} %collective-permute-done.1.refs_12_), channel_id=1, source_target_pairs={{0,2},{1,3},{4,0},{5,1},{8,4},{9,5},{12,8},{13,9},{14,12},{15,13},... | collective-permute-start | bytes 688136 | tf_op jit(solution)/shard_map/ppermute | solution.py:326
  27.4 11.4 %collective-permute-start.10 = (bf16[32,3584]{1,0:T(8,128)(2,1)S(1)}, bf16[32,3584]{1,0:T(8,128)(2,1)S(1)}, u32[]{:S(2)}, u32[]{:S(2)}) collective-permute-start(bf16[32,3584]{1,0:T(8,128)(2,1)S(1)} %collective-permute-done.2.refs_15_), channel_id=1, source_target_pairs={{0,4},{1,5},{4,8},{5,9},{8,12},{9,13},{12,14},{13,15},{14,10},{15,... | collective-permute-start | bytes 688136 | tf_op jit(solution)/shard_map/ppermute | solution.py:326
  27.9 10.8 %collective-permute-start.11 = (bf16[32,3584]{1,0:T(8,128)(2,1)S(1)}, bf16[32,3584]{1,0:T(8,128)(2,1)S(1)}, u32[]{:S(2)}, u32[]{:S(2)}) collective-permute-start(bf16[32,3584]{1,0:T(8,128)(2,1)S(1)} %collective-permute-done.3.refs_14_), channel_id=1, source_target_pairs={{0,2},{1,3},{4,0},{5,1},{8,4},{9,5},{12,8},{13,9},{14,12},{15,13},... | collective-permute-start | bytes 688136 | tf_op jit(solution)/shard_map/ppermute | solution.py:326
  29.5 8.1 %collective-permute-start.9 = (bf16[32,640]{1,0:T(8,128)(2,1)S(1)}, bf16[32,640]{1,0:T(8,128)(2,1)S(1)}, u32[]{:S(2)}, u32[]{:S(2)}) collective-permute-start(bf16[32,640]{1,0:T(8,128)(2,1)S(1)} %attention.1), channel_id=1, source_target_pairs={{0,12},{1,13},{2,14},{3,15},{4,8},{5,9},{6,10},{7,11},{8,4},{9,5},... | collective-permute-start | bytes 122888 | tf_op jit(solution)/shard_map/ppermute | solution.py:326
  30.2 8.5 %collective-permute-start.8 = (bf16[32,640]{1,0:T(8,128)(2,1)S(1)}, bf16[32,640]{1,0:T(8,128)(2,1)S(1)}, u32[]{:S(2)}, u32[]{:S(2)}) collective-permute-start(bf16[32,640]{1,0:T(8,128)(2,1)S(1)} %attention.1), channel_id=1, source_target_pairs={{0,8},{1,9},{2,10},{3,11},{4,12},{5,13},{6,14},{7,15},{8,0},{9,1},... | collective-permute-start | bytes 122888 | tf_op jit(solution)/shard_map/ppermute | solution.py:326
  31.4 7.3 %collective-permute-start.7 = (bf16[32,640]{1,0:T(8,128)(2,1)S(1)}, bf16[32,640]{1,0:T(8,128)(2,1)S(1)}, u32[]{:S(2)}, u32[]{:S(2)}) collective-permute-start(bf16[32,640]{1,0:T(8,128)(2,1)S(1)} %attention.1), channel_id=1, source_target_pairs={{0,4},{1,5},{2,6},{3,7},{4,0},{5,1},{6,2},{7,3},{8,12},{9,13},{10,... | collective-permute-start | bytes 122888 | tf_op jit(solution)/shard_map/ppermute | solution.py:326
  38.8 10.0 %collective-permute-start.15 = (bf16[32,3584]{1,0:T(8,128)(2,1)S(1)}, bf16[32,3584]{1,0:T(8,128)(2,1)S(1)}, u32[]{:S(2)}, u32[]{:S(2)}) collective-permute-start(bf16[32,3584]{1,0:T(8,128)(2,1)S(1)} %collective-permute-done.2.refs_15_), channel_id=1, source_target_pairs={{0,1},{1,0},{2,3},{3,2},{4,5},{5,4},{6,7},{7,6},{8,9},{9,8},{10,11... | collective-permute-start | bytes 688136 | tf_op jit(solution)/shard_map/ppermute | solution.py:326
  38.8 9.9 %collective-permute-start.16 = (bf16[32,3584]{1,0:T(8,128)(2,1)S(1)}, bf16[32,3584]{1,0:T(8,128)(2,1)S(1)}, u32[]{:S(2)}, u32[]{:S(2)}) collective-permute-start(bf16[32,3584]{1,0:T(8,128)(2,1)S(1)} %collective-permute-done.3.refs_14_), channel_id=1, source_target_pairs={{0,1},{1,0},{2,3},{3,2},{4,5},{5,4},{6,7},{7,6},{8,9},{9,8},{10,11... | collective-permute-start | bytes 688136 | tf_op jit(solution)/shard_map/ppermute | solution.py:326
  39.4 9.4 %collective-permute-start.14 = (bf16[32,3584]{1,0:T(8,128)(2,1)S(1)}, bf16[32,3584]{1,0:T(8,128)(2,1)S(1)}, u32[]{:S(2)}, u32[]{:S(2)}) collective-permute-start(bf16[32,3584]{1,0:T(8,128)(2,1)S(1)} %broadcast_select_fusion), channel_id=1, source_target_pairs={{0,8},{1,7},{4,12},{5,3},{8,14},{9,1},{12,10},{13,5},{14,6},{15,9}... | collective-permute-start | bytes 688136 | tf_op jit(solution)/shard_map/ppermute | solution.py:326
  39.6 2.2 %collective-permute-start.13 = (bf16[128,640]{1,0:T(8,128)(2,1)S(1)}, bf16[128,640]{1,0:T(8,128)(2,1)S(1)}, u32[]{:S(2)}, u32[]{:S(2)}) collective-permute-start(bf16[128,640]{1,0:T(8,128)(2,1)S(1)} %constant_dynamic-update-slice_fusion.refs_1_), channel_id=1, source_target_pairs={{0,1},{1,0},{2,3},{3,2},{4,5},{5,4},{6,7},{7,6},{8,9},{9,8},{10,11... | collective-permute-start | bytes 491528 | tf_op jit(solution)/shard_map/ppermute | solution.py:326
  40.1 8.6 %collective-permute-start.12 = (bf16[128,640]{1,0:T(8,128)(2,1)S(1)}, bf16[128,640]{1,0:T(8,128)(2,1)S(1)}, u32[]{:S(2)}, u32[]{:S(2)}) collective-permute-start(bf16[128,640]{1,0:T(8,128)(2,1)S(1)} %constant_dynamic-update-slice_fusion.refs_1_), channel_id=1, source_target_pairs={{0,2},{1,3},{2,0},{3,1},{4,6},{5,7},{6,4},{7,5},{8,10},{9,11},{10,... | collective-permute-start | bytes 491528 | tf_op jit(solution)/shard_map/ppermute | solution.py:326
  48.8 2.4 %collective-permute-start.18 = (bf16[32,3584]{1,0:T(8,128)(2,1)S(1)}, bf16[32,3584]{1,0:T(8,128)(2,1)S(1)}, u32[]{:S(2)}, u32[]{:S(2)}) collective-permute-start(bf16[32,3584]{1,0:T(8,128)(2,1)S(1)} %collective-permute-done.14.refs_5_), channel_id=1, source_target_pairs={{0,1},{1,0},{2,3},{3,2},{4,5},{5,4},{6,7},{7,6},{8,9},{9,8},{10,11... | collective-permute-start | bytes 688136 | tf_op jit(solution)/shard_map/ppermute | solution.py:326
  48.9 2.4 %collective-permute-start.19 = (bf16[32,3584]{1,0:T(8,128)(2,1)S(1)}, bf16[32,3584]{1,0:T(8,128)(2,1)S(1)}, u32[]{:S(2)}, u32[]{:S(2)}) collective-permute-start(bf16[32,3584]{1,0:T(8,128)(2,1)S(1)} %collective-permute-done.11.refs_6_), channel_id=1, source_target_pairs={{0,1},{1,0},{2,3},{3,2},{4,5},{5,4},{6,7},{7,6},{8,9},{9,8},{10,11... | collective-permute-start | bytes 688136 | tf_op jit(solution)/shard_map/ppermute | solution.py:326
  49.4 1.9 %collective-permute-start.20 = (bf16[32,3584]{1,0:T(8,128)(2,1)S(1)}, bf16[32,3584]{1,0:T(8,128)(2,1)S(1)}, u32[]{:S(2)}, u32[]{:S(2)}) collective-permute-start(bf16[32,3584]{1,0:T(8,128)(2,1)S(1)} %collective-permute-done.10.refs_7_), channel_id=1, source_target_pairs={{0,1},{1,0},{2,3},{3,2},{4,5},{5,4},{6,7},{7,6},{8,9},{9,8},{10,11... | collective-permute-start | bytes 688136 | tf_op jit(solution)/shard_map/ppermute | solution.py:326
  49.4 1.8 %collective-permute-start.17 = (bf16[128,640]{1,0:T(8,128)(2,1)S(1)}, bf16[128,640]{1,0:T(8,128)(2,1)S(1)}, u32[]{:S(2)}, u32[]{:S(2)}) collective-permute-start(bf16[128,640]{1,0:T(8,128)(2,1)S(1)} %collective-permute-done.12.refs_2_), channel_id=1, source_target_pairs={{0,1},{1,0},{2,3},{3,2},{4,5},{5,4},{6,7},{7,6},{8,9},{9,8},{10,11... | collective-permute-start | bytes 491528 | tf_op jit(solution)/shard_map/ppermute | solution.py:326
  51.2 12.3 %slice-start.2 = ((s8[7340032]{0:T(1024)(128)(4,1)}), s8[4194304]{0:T(1024)(128)(4,1)S(1)}, s32[]{:S(2)}) async-start(s8[7340032]{0:T(1024)(128)(4,1)} %bitcast.63), calls=%async_computation.3 | async-start | bytes 8388608
  58.7 4.9 %slice-start.3 = ((s8[7340032]{0:T(1024)(128)(4,1)}), s8[3145728]{0:T(1024)(128)(4,1)S(1)}, s32[]{:S(2)}) async-start(s8[7340032]{0:T(1024)(128)(4,1)} %bitcast.63), calls=%async_computation.4 | async-start | bytes 6291456
  58.7 6.6 %slice-start.4 = ((s8[7340032]{0:T(1024)(128)(4,1)}), s8[4194304]{0:T(1024)(128)(4,1)S(1)}, s32[]{:S(2)}) async-start(s8[7340032]{0:T(1024)(128)(4,1)} %bitcast.65), calls=%async_computation.5 | async-start | bytes 8388608
  58.7 9.4 %slice-start = ((s8[7340032]{0:T(1024)(128)(4,1)}), s8[4194304]{0:T(1024)(128)(4,1)S(1)}, s32[]{:S(2)}) async-start(s8[7340032]{0:T(1024)(128)(4,1)} %bitcast.61), calls=%async_computation.1 | async-start | bytes 8388608
  63.6 2.7 %slice-start.5 = ((s8[7340032]{0:T(1024)(128)(4,1)}), s8[3145728]{0:T(1024)(128)(4,1)S(1)}, s32[]{:S(2)}) async-start(s8[7340032]{0:T(1024)(128)(4,1)} %bitcast.65), calls=%async_computation.6 | async-start | bytes 6291456
  63.6 4.6 %slice-start.1 = ((s8[7340032]{0:T(1024)(128)(4,1)}), s8[3145728]{0:T(1024)(128)(4,1)S(1)}, s32[]{:S(2)}) async-start(s8[7340032]{0:T(1024)(128)(4,1)} %bitcast.61), calls=%async_computation.2 | async-start | bytes 6291456
  67.9 2.8 %collective-permute-start.21 = (bf16[96,3584]{1,0:T(8,128)(2,1)S(1)}, bf16[96,3584]{1,0:T(8,128)(2,1)S(1)}, u32[]{:S(2)}, u32[]{:S(2)}) collective-permute-start(bf16[96,3584]{1,0:T(8,128)(2,1)S(1)} %slice.98), channel_id=1, source_target_pairs={{0,1},{1,0},{2,3},{3,2},{4,5},{5,4},{6,7},{7,6},{8,9},{9,8},{10,11... | collective-permute-start | bytes 2064392 | tf_op jit(solution)/shard_map/ppermute | solution.py:326
  70.8 5.4 %collective-permute-start.23 = (bf16[16,3584]{1,0:T(8,128)(2,1)S(1)}, bf16[16,3584]{1,0:T(8,128)(2,1)S(1)}, u32[]{:S(2)}, u32[]{:S(2)}) collective-permute-start(bf16[16,3584]{1,0:T(8,128)(2,1)S(1)} %get-tuple-element.133), channel_id=1, source_target_pairs={{0,2},{1,3},{4,0},{5,1},{8,4},{9,5},{12,8},{13,9},{14,12},{15,13},... | collective-permute-start | bytes 344072 | tf_op jit(solution)/shard_map/ppermute | solution.py:326
  72.3 5.1 %collective-permute-start.22 = (bf16[16,3584]{1,0:T(8,128)(2,1)S(1)}, bf16[16,3584]{1,0:T(8,128)(2,1)S(1)}, u32[]{:S(2)}, u32[]{:S(2)}) collective-permute-start(bf16[16,3584]{1,0:T(8,128)(2,1)S(1)} %get-tuple-element.134), channel_id=1, source_target_pairs={{0,4},{1,5},{4,8},{5,9},{8,12},{9,13},{12,14},{13,15},{14,10},{15,... | collective-permute-start | bytes 344072 | tf_op jit(solution)/shard_map/ppermute | solution.py:326
  80.0 9.2 %collective-permute-start.24 = (bf16[160,3584]{1,0:T(8,128)(2,1)S(1)}, bf16[160,3584]{1,0:T(8,128)(2,1)S(1)}, u32[]{:S(2)}, u32[]{:S(2)}) collective-permute-start(bf16[160,3584]{1,0:T(8,128)(2,1)S(1)} %slice.101), channel_id=1, source_target_pairs={{0,1},{1,0},{2,3},{3,2},{4,5},{5,4},{6,7},{7,6},{8,9},{9,8},{10,11... | collective-permute-start | bytes 3440648 | tf_op jit(solution)/shard_map/ppermute | solution.py:326
  80.2 8.1 %collective-permute-start.26 = (bf16[32,3584]{1,0:T(8,128)(2,1)S(1)}, bf16[32,3584]{1,0:T(8,128)(2,1)S(1)}, u32[]{:S(2)}, u32[]{:S(2)}) collective-permute-start(bf16[32,3584]{1,0:T(8,128)(2,1)S(1)} %get-tuple-element.131), channel_id=1, source_target_pairs={{0,2},{1,3},{4,0},{5,1},{8,4},{9,5},{12,8},{13,9},{14,12},{15,13},... | collective-permute-start | bytes 688136 | tf_op jit(solution)/shard_map/ppermute | solution.py:326
  81.5 7.7 %collective-permute-start.25 = (bf16[32,3584]{1,0:T(8,128)(2,1)S(1)}, bf16[32,3584]{1,0:T(8,128)(2,1)S(1)}, u32[]{:S(2)}, u32[]{:S(2)}) collective-permute-start(bf16[32,3584]{1,0:T(8,128)(2,1)S(1)} %get-tuple-element.132), channel_id=1, source_target_pairs={{0,4},{1,5},{4,8},{5,9},{8,12},{9,13},{12,14},{13,15},{14,10},{15,... | collective-permute-start | bytes 688136 | tf_op jit(solution)/shard_map/ppermute | solution.py:326
  89.4 7.0 %collective-permute-start.28 = (bf16[32,3584]{1,0:T(8,128)(2,1)S(1)}, bf16[32,3584]{1,0:T(8,128)(2,1)S(1)}, u32[]{:S(2)}, u32[]{:S(2)}) collective-permute-start(bf16[32,3584]{1,0:T(8,128)(2,1)S(1)} %get-tuple-element.129), channel_id=1, source_target_pairs={{0,2},{1,3},{4,0},{5,1},{8,4},{9,5},{12,8},{13,9},{14,12},{15,13},... | collective-permute-start | bytes 688136 | tf_op jit(solution)/shard_map/ppermute | solution.py:326
  91.2 6.6 %collective-permute-start.27 = (bf16[32,3584]{1,0:T(8,128)(2,1)S(1)}, bf16[32,3584]{1,0:T(8,128)(2,1)S(1)}, u32[]{:S(2)}, u32[]{:S(2)}) collective-permute-start(bf16[32,3584]{1,0:T(8,128)(2,1)S(1)} %get-tuple-element.130), channel_id=1, source_target_pairs={{0,4},{1,5},{4,8},{5,9},{8,12},{9,13},{12,14},{13,15},{14,10},{15,... | collective-permute-start | bytes 688136 | tf_op jit(solution)/shard_map/ppermute | solution.py:326
  98.0 6.1 %collective-permute-start.30 = (bf16[32,3584]{1,0:T(8,128)(2,1)S(1)}, bf16[32,3584]{1,0:T(8,128)(2,1)S(1)}, u32[]{:S(2)}, u32[]{:S(2)}) collective-permute-start(bf16[32,3584]{1,0:T(8,128)(2,1)S(1)} %get-tuple-element.127), channel_id=1, source_target_pairs={{0,2},{1,3},{4,0},{5,1},{8,4},{9,5},{12,8},{13,9},{14,12},{15,13},... | collective-permute-start | bytes 688136 | tf_op jit(solution)/shard_map/ppermute | solution.py:326
  98.6 6.0 %collective-permute-start.29 = (bf16[32,3584]{1,0:T(8,128)(2,1)S(1)}, bf16[32,3584]{1,0:T(8,128)(2,1)S(1)}, u32[]{:S(2)}, u32[]{:S(2)}) collective-permute-start(bf16[32,3584]{1,0:T(8,128)(2,1)S(1)} %get-tuple-element.128), channel_id=1, source_target_pairs={{0,4},{1,5},{4,8},{5,9},{8,12},{9,13},{12,14},{13,15},{14,10},{15,... | collective-permute-start | bytes 688136 | tf_op jit(solution)/shard_map/ppermute | solution.py:326

commit v17 on v16

--- a/solution.py
+++ b/solution.py
@@ -375,11 +375,13 @@
         held[-t], held[t] = around(held[1 - t], held[t - 1])
     along, held = hold((along, held))
     along = jnp.concatenate([packet] + along, axis=0)
+    along, w_gate = hold((along, w_gate))
+    w_gate = jnp.where(device_index >= 0, w_gate, jnp.zeros_like(w_gate))
     across = [send(along, step_perm(chips, 0, i)) for i in range(1, low)]
     held[half] = send(jnp.where(first_core, held[2 - half], held[half - 2]), parted)
     along_sib = send(along, sibling)
     sib[2], sib[-2] = send(held[2], sibling), send(held[-2], sibling)
-    across, along_sib, held, sib = hold((across, along_sib, held, sib))
+    across, along_sib, held, sib, w_gate = hold((across, along_sib, held, sib, w_gate))
     for d in held:
         if d not in sib:
             sib[d] = send(held[d], sibling)

time: 106 us -> 103 us (0.972)
  waiting for transfers between devices: 40.5 us -> 36.9 us
  other arithmetic: 1.37 us -> 4.95 us
  matrix products: 16.8 us -> 13.9 us
    ppermute x31, waiting for transfers between devices: 32.9 us -> 29.3 us  [send(): return lax.ppermute(a, 'expert', perm)]
    select_n x0 -> x1, other arithmetic: none -> 3.56 us  [local(): w_gate = jnp.where(device_index >= 0, w_gate, jnp.zeros_like(w_gate))]
    dot_general x6, matrix products: 15.8 us -> 12.9 us  [product(): return jnp.dot(a, w[0], preferred_element_type=f32)]
  transfers between devices with their start and end apart: 32 -> 32, of which waited for: 13 -> 14; matrix products, arithmetic and copies ran while one was open for 7% -> 11% of each run, Pallas kernels for 5% -> 6%
where the time goes in v17:
time: 103 us; the launch traced here: 102 us
  waiting for transfers between devices  36.9 us (36%)
  starting transfers between devices  31.3 us (30%)
  matrix products  13.9 us (13%)
  Pallas kernels  12.8 us (12%)
  other arithmetic  4.95 us (5%)
  local copies, waits for them, and re-layouts  2.16 us (2%)
    ppermute x31, waiting for transfers between devices, send(): return lax.ppermute(a, 'expert', perm)  29.3 us
    ppermute x31, starting transfers between devices, send(): return lax.ppermute(a, 'expert', perm)  25 us
    dot_general x6, matrix products, product(): return jnp.dot(a, w[0], preferred_element_type=f32)  12.9 us
    all_to_all x1, waiting for transfers between devices, local(): lax.all_to_all(ordered, 'expert', split_axis=0, concat_axis=0, tiled=True)  7.6 us
    pallas_call x1, Pallas kernels, normalize(): pl.pallas_call(lambda *refs: norm_kernel(far, blocks, rows, latent, width...  7.08 us
    all_to_all x1, starting transfers between devices, local(): lax.all_to_all(ordered, 'expert', split_axis=0, concat_axis=0, tiled=True)  6.29 us
    pallas_call x1, Pallas kernels, attention(): pl.pallas_call(lambda *refs: attention_kernel(context, latent, *refs), gr...  4.33 us
    select_n x1, other arithmetic, local(): w_gate = jnp.where(device_index >= 0, w_gate, jnp.zeros_like(w_gate))  3.56 us
  transfers between devices with their start and end apart: 32, of which 14 were waited for; matrix products, arithmetic and copies ran while one was open for 11% of the time, Pallas kernels for 6%

profile of v17, /device:TPU:0, one launch (start us, length us, event | category | flops | bytes accessed | tf_op | source)
XLA Modules:
  0.0 102.3 jit_solution(1487843778012217317)
XLA Ops:
  0.0 0.5 collective-permute-start.5
  0.5 2.6 %collective-permute-start.1 = (bf16[32,3584]{1,0:T(8,128)(2,1)}, bf16[32,3584]{1,0:T(8,128)(2,1)}, u32[]{:S(2)}, u32[]{:S(2)}) collective-permute-start(bf16[32,3584]{1,0:T(8,128)(2,1)} %bitcast.57), channel_id=1, source_target_pairs={{0,2},{1,3},{4,0},{5,1},{8,4},{9,5},{12,8},{13,9},{14,12},{15,13},... | collective-permute-start | bytes 688136 | tf_op jit(solution)/shard_map/ppermute | solution.py:326
  3.2 1.0 fusion.27
  4.4 0.8 copy.19
  5.1 6.3 %all-to-all-start = ((bf16[16,2,8,576]{3,2,1,0:T(8,128)(2,1)}), bf16[16,2,8,576]{3,2,1,0:T(8,128)(2,1)S(1)}, u32[]{:S(2)}, u32[]{:S(2)}) async-start(bf16[16,2,8,576]{3,2,1,0:T(8,128)(2,1)} %copy.19), calls=%async_computation | async-start | bytes 655360 | tf_op jit(solution)/shard_map/all_to_all | solution.py:343
  11.5 1.4 %lookup.1 = (s32[8]{0:T(128)}, s32[17]{0:T(128)}) custom-call(s32[128]{0:T(128)} %owner.1, s32[128]{0:T(128)} %lengths.1, s32[272]{0:T(512)} %constant.42.table, s32[1]{0:T(128)} %bitcast.device), custom_call_target="tpu_custom_call" | custom-call | flops 10000000000 | bytes 100000000 | tf_op jit(solution)/shard_map/lookup/pallas_call | solution.py:194
  12.9 0.5 collective-permute-start.4
  13.4 1.7 %collective-permute-start.2 = (bf16[32,3584]{1,0:T(8,128)(2,1)}, bf16[32,3584]{1,0:T(8,128)(2,1)S(1)}, u32[]{:S(2)}, u32[]{:S(2)}) collective-permute-start(bf16[32,3584]{1,0:T(8,128)(2,1)} %collective-permute-done.refs_13_), channel_id=1, source_target_pairs={{0,4},{1,5},{4,8},{5,9},{8,12},{9,13},{12,14},{13,15},{14,10},{15,... | collective-permute-start | bytes 688136 | tf_op jit(solution)/shard_map/ppermute | solution.py:326
  15.4 7.6 %all-to-all-done = bf16[16,2,8,576]{3,2,1,0:T(8,128)(2,1)S(1)} async-done(((bf16[16,2,8,576]{3,2,1,0:T(8,128)(2,1)}), bf16[16,2,8,576]{3,2,1,0:T(8,128)(2,1)S(1)}, u32[]{:S(2)}, u32[]{:S(2)}) %all-to-all-start) | async-done | bytes 294944 | tf_op jit(solution)/shard_map/all_to_all | solution.py:343
  23.0 4.3 %attention.1 = bf16[32,640]{1,0:T(8,128)(2,1)S(1)} custom-call(bf16[4,8,36864]{2,1,0:T(8,128)(2,1)S(1)} %copy-done.1, bf16[256,576]{1,0:T(8,128)(2,1)S(1)} %bitcast.52, bf16[32,576]{1,0:T(8,128)(2,1)S(1)} %bitcast.53, s32[8]{0:T(128)} %get-tuple-element.72.refs_3_, s32[32,8]{1,0:T(8,128)S(1)} %bitcast.54), custom_call_target="tpu_custom_call" | custom-call | flops 679477248 | bytes 2359296 | tf_op jit(solution)/shard_map/attention/pallas_call | solution.py:274
  27.4 0.6 collective-permute-start.10
  28.0 1.5 %collective-permute-start.11 = (bf16[32,3584]{1,0:T(8,128)(2,1)S(1)}, bf16[32,3584]{1,0:T(8,128)(2,1)S(1)}, u32[]{:S(2)}, u32[]{:S(2)}) collective-permute-start(bf16[32,3584]{1,0:T(8,128)(2,1)S(1)} %collective-permute-done.3.refs_14_), channel_id=1, source_target_pairs={{0,2},{1,3},{4,0},{5,1},{8,4},{9,5},{12,8},{13,9},{14,12},{15,13},... | collective-permute-start | bytes 688136 | tf_op jit(solution)/shard_map/ppermute | solution.py:326
  29.5 0.8 collective-permute-start.9
  30.2 1.2 %collective-permute-start.8 = (bf16[32,640]{1,0:T(8,128)(2,1)S(1)}, bf16[32,640]{1,0:T(8,128)(2,1)S(1)}, u32[]{:S(2)}, u32[]{:S(2)}) collective-permute-start(bf16[32,640]{1,0:T(8,128)(2,1)S(1)} %attention.1), channel_id=1, source_target_pairs={{0,8},{1,9},{2,10},{3,11},{4,12},{5,13},{6,14},{7,15},{8,0},{9,1},... | collective-permute-start | bytes 122888 | tf_op jit(solution)/shard_map/ppermute | solution.py:326
  31.5 2.4 %collective-permute-start.7 = (bf16[32,640]{1,0:T(8,128)(2,1)S(1)}, bf16[32,640]{1,0:T(8,128)(2,1)S(1)}, u32[]{:S(2)}, u32[]{:S(2)}) collective-permute-start(bf16[32,640]{1,0:T(8,128)(2,1)S(1)} %attention.1), channel_id=1, source_target_pairs={{0,4},{1,5},{2,6},{3,7},{4,0},{5,1},{6,2},{7,3},{8,12},{9,13},{10,... | collective-permute-start | bytes 122888 | tf_op jit(solution)/shard_map/ppermute | solution.py:326
  33.9 3.7 %collective-permute-done.9 = bf16[32,640]{1,0:T(8,128)(2,1)S(1)} collective-permute-done((bf16[32,640]{1,0:T(8,128)(2,1)S(1)}, bf16[32,640]{1,0:T(8,128)(2,1)S(1)}, u32[]{:S(2)}, u32[]{:S(2)}) %collective-permute-start.9) | collective-permute-done | bytes 40992 | tf_op jit(solution)/shard_map/ppermute | solution.py:326
  37.6 1.2 %collective-permute-done.8 = bf16[32,640]{1,0:T(8,128)(2,1)S(1)} collective-permute-done((bf16[32,640]{1,0:T(8,128)(2,1)S(1)}, bf16[32,640]{1,0:T(8,128)(2,1)S(1)}, u32[]{:S(2)}, u32[]{:S(2)}) %collective-permute-start.8) | collective-permute-done | bytes 40992 | tf_op jit(solution)/shard_map/ppermute | solution.py:326
  38.9 1.3 %collective-permute-start.12 = (bf16[128,640]{1,0:T(8,128)(2,1)S(1)}, bf16[128,640]{1,0:T(8,128)(2,1)S(1)}, u32[]{:S(2)}, u32[]{:S(2)}) collective-permute-start(bf16[128,640]{1,0:T(8,128)(2,1)S(1)} %pad_maximum_fusion.refs_1_), channel_id=1, source_target_pairs={{0,2},{1,3},{2,0},{3,1},{4,6},{5,7},{6,4},{7,5},{8,10},{9,11},{10,... | collective-permute-start | bytes 491528 | tf_op jit(solution)/shard_map/ppermute | solution.py:326
  40.7 1.4 %collective-permute-start.14 = (bf16[32,3584]{1,0:T(8,128)(2,1)S(1)}, bf16[32,3584]{1,0:T(8,128)(2,1)S(1)}, u32[]{:S(2)}, u32[]{:S(2)}) collective-permute-start(bf16[32,3584]{1,0:T(8,128)(2,1)S(1)} %broadcast_select_fusion.1), channel_id=1, source_target_pairs={{0,8},{1,7},{4,12},{5,3},{8,14},{9,1},{12,10},{13,5},{14,6},{15,9}... | collective-permute-start | bytes 688136 | tf_op jit(solution)/shard_map/ppermute | solution.py:326
  42.1 3.6 %broadcast_select_fusion = bf16[1,3584,1024]{2,1,0:T(8,128)(2,1)S(1)} fusion(bf16[1,3584,1024]{2,1,0:T(8,128)(2,1)} %param.24, pred[]{:T(512)S(6)} %ge.3), kind=kLoop, calls=%fused_computation.12 | loop fusion | flops 3670016 | bytes 14680065 | tf_op jit(solution)/shard_map/jit(_where)/select_n | solution.py:379
  45.7 1.0 %collective-permute-done.12.refs_2_ = bf16[128,640]{1,0:T(8,128)(2,1)S(1)} collective-permute-done((bf16[128,640]{1,0:T(8,128)(2,1)S(1)}, bf16[128,640]{1,0:T(8,128)(2,1)S(1)}, u32[]{:S(2)}, u32[]{:S(2)}) %collective-permute-start.12) | collective-permute-done | bytes 163872 | tf_op jit(solution)/shard_map/ppermute | solution.py:326
  46.7 3.2 %collective-permute-done.14.refs_5_ = bf16[32,3584]{1,0:T(8,128)(2,1)S(1)} collective-permute-done((bf16[32,3584]{1,0:T(8,128)(2,1)S(1)}, bf16[32,3584]{1,0:T(8,128)(2,1)S(1)}, u32[]{:S(2)}, u32[]{:S(2)}) %collective-permute-start.14) | collective-permute-done | bytes 229408 | tf_op jit(solution)/shard_map/ppermute | solution.py:326
  49.9 0.5 collective-permute-start.19
  50.9 1.4 %collective-permute-done.17.refs_4_ = bf16[128,640]{1,0:T(8,128)(2,1)S(1)} collective-permute-done((bf16[128,640]{1,0:T(8,128)(2,1)S(1)}, bf16[128,640]{1,0:T(8,128)(2,1)S(1)}, u32[]{:S(2)}, u32[]{:S(2)}) %collective-permute-start.17) | collective-permute-done | bytes 163872 | tf_op jit(solution)/shard_map/ppermute | solution.py:326
  52.3 7.1 %normalize.1 = (bf16[192,3584]{1,0:T(8,128)(2,1)S(1)}, bf16[320,3584]{1,0:T(8,128)(2,1)S(1)}, f32[512,128]{1,0:T(8,128)S(1)}, f32[512,128]{1,0:T(8,128)S(1)}, f32[32,3584]{1,0:T(8,128)S(1)}) custom-call(s32[17]{0:T(128)} %get-tuple-element.71.refs_0_, bf16[128,640]{1,0:T(8,128)(2,1)S(1)} %pad_maximum_fusion.refs_1_, ...), custom_call_target="tpu_custom_call" | custom-call | flops 1879048192 | bytes 18350080 | tf_op jit(solution)/shard_map/normalize/pallas_call | solution.py:148
  59.7 1.7 %fusion.21 = f32[192,1024]{1,0:T(8,128)S(1)} fusion(bf16[192,3584]{1,0:T(8,128)(2,1)S(1)} %get-tuple-element.116, bf16[1,3584,1024]{2,1,0:T(8,128)(2,1)S(1)} %broadcast_select_fusion, f32[192]{0:T(256)S(1)} %get-tuple-element.144), kind=kOutput, calls=%fused_computation.17 | convolution fusion | flops 1409482752 | bytes 9503488 | tf_op jit(solution)/shard_map/dot_general | solution.py:405
  61.6 1.8 %multiply_convert_fusion.1 = bf16[192,1024]{1,0:T(8,128)(2,1)S(1)} fusion(f32[192,1024]{1,0:T(8,128)S(1)} %fusion.21, f32[192]{0:T(256)S(1)} %get-tuple-element.143, f32[192]{0:T(256)S(1)} %get-tuple-element.144, bf16[192,3584]{1,0:T(8,128)(2,1)S(1)} %get-tuple-element.116, bf16[1,3584,1024]{2,1,0:T(8,128)(2,1)S(1)} %bitcast.62), kind=kOutput, calls=%fused_computation.21 | convolution fusion | flops 1410859008 | bytes 9897472 | tf_op jit(solution)/shard_map/dot_general | solution.py:405
  63.5 0.5 slice-done.3
  64.0 1.6 %fusion.15 = bf16[192,3584]{1,0:T(8,128)(2,1)S(1)} fusion(bf16[192,1024]{1,0:T(8,128)(2,1)S(1)} %multiply_convert_fusion.1, bf16[1,1024,3584]{2,1,0:T(8,128)(2,1)S(1)} %bitcast.64), kind=kOutput, calls=%fused_computation.14 | convolution fusion | flops 1409974272 | bytes 9109504 | tf_op jit(solution)/shard_map/dot_general | solution.py:405
  65.9 2.5 %fusion.10 = f32[320,1024]{1,0:T(8,128)S(1)} fusion(bf16[320,3584]{1,0:T(8,128)(2,1)S(1)} %get-tuple-element.114, bf16[1,3584,1024]{2,1,0:T(8,128)(2,1)S(1)} %broadcast_select_fusion), kind=kOutput, calls=%fused_computation.10 | convolution fusion | flops 2348810240 | bytes 10944512 | tf_op jit(solution)/shard_map/dot_general | solution.py:405
  68.5 0.9 collective-permute-start.23
  69.4 1.2 %collective-permute-start.22 = (bf16[16,3584]{1,0:T(8,128)(2,1)S(1)}, bf16[16,3584]{1,0:T(8,128)(2,1)S(1)}, u32[]{:S(2)}, u32[]{:S(2)}) collective-permute-start(bf16[16,3584]{1,0:T(8,128)(2,1)S(1)} %get-tuple-element.140), channel_id=1, source_target_pairs={{0,4},{1,5},{4,8},{5,9},{8,12},{9,13},{12,14},{13,15},{14,10},{15,... | collective-permute-start | bytes 344072 | tf_op jit(solution)/shard_map/ppermute | solution.py:326
  70.6 2.7 %multiply_convert_fusion = bf16[320,1024]{1,0:T(8,128)(2,1)S(1)} fusion(f32[320,1024]{1,0:T(8,128)S(1)} %fusion.10, f32[320]{0:T(512)S(1)} %get-tuple-element.141, f32[320]{0:T(512)S(1)} %get-tuple-element.142, bf16[320,3584]{1,0:T(8,128)(2,1)S(1)} %get-tuple-element.114, bf16[1,3584,1024]{2,1,0:T(8,128)(2,1)S(1)} %bitcast.62), kind=kOutput, calls=%fused_computation.16 | convolution fusion | flops 2351759360 | bytes 11602432 | tf_op jit(solution)/shard_map/dot_general | solution.py:405
  73.3 0.6 collective-permute-done.23
  74.0 0.6 collective-permute-done.22
  74.5 2.5 %fusion.12 = bf16[320,3584]{1,0:T(8,128)(2,1)S(1)} fusion(bf16[320,1024]{1,0:T(8,128)(2,1)S(1)} %multiply_convert_fusion, bf16[1,1024,3584]{2,1,0:T(8,128)(2,1)S(1)} %bitcast.64), kind=kOutput, calls=%fused_computation.13 | convolution fusion | flops 2349957120 | bytes 10289152 | tf_op jit(solution)/shard_map/dot_general | solution.py:405
  77.4 0.6 collective-permute-start.26
  77.9 1.5 %collective-permute-start.25 = (bf16[32,3584]{1,0:T(8,128)(2,1)S(1)}, bf16[32,3584]{1,0:T(8,128)(2,1)S(1)}, u32[]{:S(2)}, u32[]{:S(2)}) collective-permute-start(bf16[32,3584]{1,0:T(8,128)(2,1)S(1)} %get-tuple-element.138), channel_id=1, source_target_pairs={{0,4},{1,5},{4,8},{5,9},{8,12},{9,13},{12,14},{13,15},{14,10},{15,... | collective-permute-start | bytes 688136 | tf_op jit(solution)/shard_map/ppermute | solution.py:326
  79.4 6.0 %collective-permute-done.26 = bf16[32,3584]{1,0:T(8,128)(2,1)S(1)} collective-permute-done((bf16[32,3584]{1,0:T(8,128)(2,1)S(1)}, bf16[32,3584]{1,0:T(8,128)(2,1)S(1)}, u32[]{:S(2)}, u32[]{:S(2)}) %collective-permute-start.26) | collective-permute-done | bytes 229408 | tf_op jit(solution)/shard_map/ppermute | solution.py:326
  85.8 1.1 %collective-permute-start.28 = (bf16[32,3584]{1,0:T(8,128)(2,1)S(1)}, bf16[32,3584]{1,0:T(8,128)(2,1)S(1)}, u32[]{:S(2)}, u32[]{:S(2)}) collective-permute-start(bf16[32,3584]{1,0:T(8,128)(2,1)S(1)} %get-tuple-element.135), channel_id=1, source_target_pairs={{0,2},{1,3},{4,0},{5,1},{8,4},{9,5},{12,8},{13,9},{14,12},{15,13},... | collective-permute-start | bytes 688136 | tf_op jit(solution)/shard_map/ppermute | solution.py:326
  86.9 1.0 collective-permute-start.27
  87.9 5.0 %collective-permute-done.28 = bf16[32,3584]{1,0:T(8,128)(2,1)S(1)} collective-permute-done((bf16[32,3584]{1,0:T(8,128)(2,1)S(1)}, bf16[32,3584]{1,0:T(8,128)(2,1)S(1)}, u32[]{:S(2)}, u32[]{:S(2)}) %collective-permute-start.28) | collective-permute-done | bytes 229408 | tf_op jit(solution)/shard_map/ppermute | solution.py:326
  92.9 1.0 collective-permute-done.27
  94.0 1.5 %collective-permute-start.30 = (bf16[32,3584]{1,0:T(8,128)(2,1)S(1)}, bf16[32,3584]{1,0:T(8,128)(2,1)S(1)}, u32[]{:S(2)}, u32[]{:S(2)}) collective-permute-start(bf16[32,3584]{1,0:T(8,128)(2,1)S(1)} %get-tuple-element.133), channel_id=1, source_target_pairs={{0,2},{1,3},{4,0},{5,1},{8,4},{9,5},{12,8},{13,9},{14,12},{15,13},... | collective-permute-start | bytes 688136 | tf_op jit(solution)/shard_map/ppermute | solution.py:326
  95.5 0.6 collective-permute-start.29
  96.1 4.0 %collective-permute-done.30 = bf16[32,3584]{1,0:T(8,128)(2,1)S(1)} collective-permute-done((bf16[32,3584]{1,0:T(8,128)(2,1)S(1)}, bf16[32,3584]{1,0:T(8,128)(2,1)S(1)}, u32[]{:S(2)}, u32[]{:S(2)}) %collective-permute-start.30) | collective-permute-done | bytes 229408 | tf_op jit(solution)/shard_map/ppermute | solution.py:326
  100.1 1.4 %collective-permute-done.29 = bf16[32,3584]{1,0:T(8,128)(2,1)S(1)} collective-permute-done((bf16[32,3584]{1,0:T(8,128)(2,1)S(1)}, bf16[32,3584]{1,0:T(8,128)(2,1)S(1)}, u32[]{:S(2)}, u32[]{:S(2)}) %collective-permute-start.29) | collective-permute-done | bytes 229408 | tf_op jit(solution)/shard_map/ppermute | solution.py:326
  101.5 0.8 fusion.32
  (62 shorter events, 3.7 us)
Async XLA Ops:
  0.0 3.2 %copy-start = (bf16[128,2,576]{0,2,1:T(8,128)(2,1)S(1)}, bf16[128,2,576]{0,2,1:T(8,128)(2,1)}, u32[]{:S(2)}) copy-start(bf16[128,2,576]{0,2,1:T(8,128)(2,1)} %param.16) | copy-start | bytes 884740
  0.0 27.4 %collective-permute-start.5 = (bf16[32,3584]{1,0:T(8,128)(2,1)}, bf16[32,3584]{1,0:T(8,128)(2,1)}, u32[]{:S(2)}, u32[]{:S(2)}) collective-permute-start(bf16[32,3584]{1,0:T(8,128)(2,1)} %bitcast.56), channel_id=1, source_target_pairs={{0,1},{1,0},{2,3},{3,2},{4,5},{5,4},{6,7},{7,6},{8,9},{9,8},{10,11... | collective-permute-start | bytes 688136 | tf_op jit(solution)/shard_map/ppermute | solution.py:326
  0.5 12.4 %collective-permute-start.1 = (bf16[32,3584]{1,0:T(8,128)(2,1)}, bf16[32,3584]{1,0:T(8,128)(2,1)}, u32[]{:S(2)}, u32[]{:S(2)}) collective-permute-start(bf16[32,3584]{1,0:T(8,128)(2,1)} %bitcast.57), channel_id=1, source_target_pairs={{0,2},{1,3},{4,0},{5,1},{8,4},{9,5},{12,8},{13,9},{14,12},{15,13},... | collective-permute-start | bytes 688136 | tf_op jit(solution)/shard_map/ppermute | solution.py:326
  3.0 9.9 %collective-permute-start = (bf16[32,3584]{1,0:T(8,128)(2,1)}, bf16[32,3584]{1,0:T(8,128)(2,1)}, u32[]{:S(2)}, u32[]{:S(2)}) collective-permute-start(bf16[32,3584]{1,0:T(8,128)(2,1)} %bitcast.58), channel_id=1, source_target_pairs={{0,4},{1,5},{4,8},{5,9},{8,12},{9,13},{12,14},{13,15},{14,10},{15,... | collective-permute-start | bytes 688136 | tf_op jit(solution)/shard_map/ppermute | solution.py:326
  5.1 17.9 %all-to-all-start = ((bf16[16,2,8,576]{3,2,1,0:T(8,128)(2,1)}), bf16[16,2,8,576]{3,2,1,0:T(8,128)(2,1)S(1)}, u32[]{:S(2)}, u32[]{:S(2)}) async-start(bf16[16,2,8,576]{3,2,1,0:T(8,128)(2,1)} %copy.19), calls=%async_computation | async-start | bytes 655360 | tf_op jit(solution)/shard_map/all_to_all | solution.py:343
  11.4 4.0 %copy-start.4 = (bf16[3584]{0:T(1024)(128)(2,1)S(1)}, bf16[3584]{0:T(1024)(128)(2,1)}, u32[]{:S(2)}) copy-start(bf16[3584]{0:T(1024)(128)(2,1)} %param.22) | copy-start | bytes 21508
  11.5 11.6 %copy-start.1 = (bf16[4,8,36864]{2,1,0:T(8,128)(2,1)S(1)}, bf16[4,8,36864]{2,1,0:T(8,128)(2,1)}, u32[]{:S(2)}) copy-start(bf16[4,8,36864]{2,1,0:T(8,128)(2,1)} %refs_0_.1) | copy-start | bytes 7077892
  11.5 11.6 %copy-start.2 = (bf16[4,8,576]{2,1,0:T(8,128)(2,1)S(1)}, bf16[4,8,576]{2,1,0:T(8,128)(2,1)}, u32[]{:S(2)}) copy-start(bf16[4,8,576]{2,1,0:T(8,128)(2,1)} %param.15) | copy-start | bytes 110596
  11.5 11.5 %copy-start.3 = (s32[4,8,8]{2,1,0:T(8,128)S(1)}, s32[4,8,8]{2,1,0:T(8,128)}, u32[]{:S(2)}) copy-start(s32[4,8,8]{2,1,0:T(8,128)} %param.20) | copy-start | bytes 3076
  12.9 14.5 %collective-permute-start.4 = (bf16[32,3584]{1,0:T(8,128)(2,1)}, bf16[32,3584]{1,0:T(8,128)(2,1)}, u32[]{:S(2)}, u32[]{:S(2)}) collective-permute-start(bf16[32,3584]{1,0:T(8,128)(2,1)} %collective-permute-done.refs_13_), channel_id=1, source_target_pairs={{0,1},{1,0},{2,3},{3,2},{4,5},{5,4},{6,7},{7,6},{8,9},{9,8},{10,11... | collective-permute-start | bytes 688136 | tf_op jit(solution)/shard_map/ppermute | solution.py:326
  13.4 14.0 %collective-permute-start.2 = (bf16[32,3584]{1,0:T(8,128)(2,1)}, bf16[32,3584]{1,0:T(8,128)(2,1)S(1)}, u32[]{:S(2)}, u32[]{:S(2)}) collective-permute-start(bf16[32,3584]{1,0:T(8,128)(2,1)} %collective-permute-done.refs_13_), channel_id=1, source_target_pairs={{0,4},{1,5},{4,8},{5,9},{8,12},{9,13},{12,14},{13,15},{14,10},{15,... | collective-permute-start | bytes 688136 | tf_op jit(solution)/shard_map/ppermute | solution.py:326
  15.1 12.3 %collective-permute-start.6 = (bf16[32,3584]{1,0:T(8,128)(2,1)}, bf16[32,3584]{1,0:T(8,128)(2,1)}, u32[]{:S(2)}, u32[]{:S(2)}) collective-permute-start(bf16[32,3584]{1,0:T(8,128)(2,1)} %collective-permute-done.1.refs_12_), channel_id=1, source_target_pairs={{0,1},{1,0},{2,3},{3,2},{4,5},{5,4},{6,7},{7,6},{8,9},{9,8},{10,11... | collective-permute-start | bytes 688136 | tf_op jit(solution)/shard_map/ppermute | solution.py:326
  15.1 12.3 %collective-permute-start.3 = (bf16[32,3584]{1,0:T(8,128)(2,1)}, bf16[32,3584]{1,0:T(8,128)(2,1)S(1)}, u32[]{:S(2)}, u32[]{:S(2)}) collective-permute-start(bf16[32,3584]{1,0:T(8,128)(2,1)} %collective-permute-done.1.refs_12_), channel_id=1, source_target_pairs={{0,2},{1,3},{4,0},{5,1},{8,4},{9,5},{12,8},{13,9},{14,12},{15,13},... | collective-permute-start | bytes 688136 | tf_op jit(solution)/shard_map/ppermute | solution.py:326
  27.4 11.4 %collective-permute-start.10 = (bf16[32,3584]{1,0:T(8,128)(2,1)S(1)}, bf16[32,3584]{1,0:T(8,128)(2,1)S(1)}, u32[]{:S(2)}, u32[]{:S(2)}) collective-permute-start(bf16[32,3584]{1,0:T(8,128)(2,1)S(1)} %collective-permute-done.2.refs_15_), channel_id=1, source_target_pairs={{0,4},{1,5},{4,8},{5,9},{8,12},{9,13},{12,14},{13,15},{14,10},{15,... | collective-permute-start | bytes 688136 | tf_op jit(solution)/shard_map/ppermute | solution.py:326
  28.0 10.8 %collective-permute-start.11 = (bf16[32,3584]{1,0:T(8,128)(2,1)S(1)}, bf16[32,3584]{1,0:T(8,128)(2,1)S(1)}, u32[]{:S(2)}, u32[]{:S(2)}) collective-permute-start(bf16[32,3584]{1,0:T(8,128)(2,1)S(1)} %collective-permute-done.3.refs_14_), channel_id=1, source_target_pairs={{0,2},{1,3},{4,0},{5,1},{8,4},{9,5},{12,8},{13,9},{14,12},{15,13},... | collective-permute-start | bytes 688136 | tf_op jit(solution)/shard_map/ppermute | solution.py:326
  29.5 8.1 %collective-permute-start.9 = (bf16[32,640]{1,0:T(8,128)(2,1)S(1)}, bf16[32,640]{1,0:T(8,128)(2,1)S(1)}, u32[]{:S(2)}, u32[]{:S(2)}) collective-permute-start(bf16[32,640]{1,0:T(8,128)(2,1)S(1)} %attention.1), channel_id=1, source_target_pairs={{0,12},{1,13},{2,14},{3,15},{4,8},{5,9},{6,10},{7,11},{8,4},{9,5},... | collective-permute-start | bytes 122888 | tf_op jit(solution)/shard_map/ppermute | solution.py:326
  30.2 8.5 %collective-permute-start.8 = (bf16[32,640]{1,0:T(8,128)(2,1)S(1)}, bf16[32,640]{1,0:T(8,128)(2,1)S(1)}, u32[]{:S(2)}, u32[]{:S(2)}) collective-permute-start(bf16[32,640]{1,0:T(8,128)(2,1)S(1)} %attention.1), channel_id=1, source_target_pairs={{0,8},{1,9},{2,10},{3,11},{4,12},{5,13},{6,14},{7,15},{8,0},{9,1},... | collective-permute-start | bytes 122888 | tf_op jit(solution)/shard_map/ppermute | solution.py:326
  31.5 7.3 %collective-permute-start.7 = (bf16[32,640]{1,0:T(8,128)(2,1)S(1)}, bf16[32,640]{1,0:T(8,128)(2,1)S(1)}, u32[]{:S(2)}, u32[]{:S(2)}) collective-permute-start(bf16[32,640]{1,0:T(8,128)(2,1)S(1)} %attention.1), channel_id=1, source_target_pairs={{0,4},{1,5},{2,6},{3,7},{4,0},{5,1},{6,2},{7,3},{8,12},{9,13},{10,... | collective-permute-start | bytes 122888 | tf_op jit(solution)/shard_map/ppermute | solution.py:326
  38.8 6.9 %collective-permute-start.13 = (bf16[128,640]{1,0:T(8,128)(2,1)S(1)}, bf16[128,640]{1,0:T(8,128)(2,1)S(1)}, u32[]{:S(2)}, u32[]{:S(2)}) collective-permute-start(bf16[128,640]{1,0:T(8,128)(2,1)S(1)} %pad_maximum_fusion.refs_1_), channel_id=1, source_target_pairs={{0,1},{1,0},{2,3},{3,2},{4,5},{5,4},{6,7},{7,6},{8,9},{9,8},{10,11... | collective-permute-start | bytes 491528 | tf_op jit(solution)/shard_map/ppermute | solution.py:326
  38.9 7.8 %collective-permute-start.12 = (bf16[128,640]{1,0:T(8,128)(2,1)S(1)}, bf16[128,640]{1,0:T(8,128)(2,1)S(1)}, u32[]{:S(2)}, u32[]{:S(2)}) collective-permute-start(bf16[128,640]{1,0:T(8,128)(2,1)S(1)} %pad_maximum_fusion.refs_1_), channel_id=1, source_target_pairs={{0,2},{1,3},{2,0},{3,1},{4,6},{5,7},{6,4},{7,5},{8,10},{9,11},{10,... | collective-permute-start | bytes 491528 | tf_op jit(solution)/shard_map/ppermute | solution.py:326
  40.2 9.7 %collective-permute-start.15 = (bf16[32,3584]{1,0:T(8,128)(2,1)S(1)}, bf16[32,3584]{1,0:T(8,128)(2,1)S(1)}, u32[]{:S(2)}, u32[]{:S(2)}) collective-permute-start(bf16[32,3584]{1,0:T(8,128)(2,1)S(1)} %collective-permute-done.2.refs_15_), channel_id=1, source_target_pairs={{0,1},{1,0},{2,3},{3,2},{4,5},{5,4},{6,7},{7,6},{8,9},{9,8},{10,11... | collective-permute-start | bytes 688136 | tf_op jit(solution)/shard_map/ppermute | solution.py:326
  40.4 9.5 %collective-permute-start.16 = (bf16[32,3584]{1,0:T(8,128)(2,1)S(1)}, bf16[32,3584]{1,0:T(8,128)(2,1)S(1)}, u32[]{:S(2)}, u32[]{:S(2)}) collective-permute-start(bf16[32,3584]{1,0:T(8,128)(2,1)S(1)} %collective-permute-done.3.refs_14_), channel_id=1, source_target_pairs={{0,1},{1,0},{2,3},{3,2},{4,5},{5,4},{6,7},{7,6},{8,9},{9,8},{10,11... | collective-permute-start | bytes 688136 | tf_op jit(solution)/shard_map/ppermute | solution.py:326
  40.7 9.2 %collective-permute-start.14 = (bf16[32,3584]{1,0:T(8,128)(2,1)S(1)}, bf16[32,3584]{1,0:T(8,128)(2,1)S(1)}, u32[]{:S(2)}, u32[]{:S(2)}) collective-permute-start(bf16[32,3584]{1,0:T(8,128)(2,1)S(1)} %broadcast_select_fusion.1), channel_id=1, source_target_pairs={{0,8},{1,7},{4,12},{5,3},{8,14},{9,1},{12,10},{13,5},{14,6},{15,9}... | collective-permute-start | bytes 688136 | tf_op jit(solution)/shard_map/ppermute | solution.py:326
  49.9 2.4 %collective-permute-start.18 = (bf16[32,3584]{1,0:T(8,128)(2,1)S(1)}, bf16[32,3584]{1,0:T(8,128)(2,1)S(1)}, u32[]{:S(2)}, u32[]{:S(2)}) collective-permute-start(bf16[32,3584]{1,0:T(8,128)(2,1)S(1)} %collective-permute-done.14.refs_5_), channel_id=1, source_target_pairs={{0,1},{1,0},{2,3},{3,2},{4,5},{5,4},{6,7},{7,6},{8,9},{9,8},{10,11... | collective-permute-start | bytes 688136 | tf_op jit(solution)/shard_map/ppermute | solution.py:326
  49.9 2.4 %collective-permute-start.19 = (bf16[32,3584]{1,0:T(8,128)(2,1)S(1)}, bf16[32,3584]{1,0:T(8,128)(2,1)S(1)}, u32[]{:S(2)}, u32[]{:S(2)}) collective-permute-start(bf16[32,3584]{1,0:T(8,128)(2,1)S(1)} %collective-permute-done.11.refs_6_), channel_id=1, source_target_pairs={{0,1},{1,0},{2,3},{3,2},{4,5},{5,4},{6,7},{7,6},{8,9},{9,8},{10,11... | collective-permute-start | bytes 688136 | tf_op jit(solution)/shard_map/ppermute | solution.py:326
  50.4 1.9 %collective-permute-start.20 = (bf16[32,3584]{1,0:T(8,128)(2,1)S(1)}, bf16[32,3584]{1,0:T(8,128)(2,1)S(1)}, u32[]{:S(2)}, u32[]{:S(2)}) collective-permute-start(bf16[32,3584]{1,0:T(8,128)(2,1)S(1)} %collective-permute-done.10.refs_7_), channel_id=1, source_target_pairs={{0,1},{1,0},{2,3},{3,2},{4,5},{5,4},{6,7},{7,6},{8,9},{9,8},{10,11... | collective-permute-start | bytes 688136 | tf_op jit(solution)/shard_map/ppermute | solution.py:326
  50.5 1.8 %collective-permute-start.17 = (bf16[128,640]{1,0:T(8,128)(2,1)S(1)}, bf16[128,640]{1,0:T(8,128)(2,1)S(1)}, u32[]{:S(2)}, u32[]{:S(2)}) collective-permute-start(bf16[128,640]{1,0:T(8,128)(2,1)S(1)} %collective-permute-done.12.refs_2_), channel_id=1, source_target_pairs={{0,1},{1,0},{2,3},{3,2},{4,5},{5,4},{6,7},{7,6},{8,9},{9,8},{10,11... | collective-permute-start | bytes 491528 | tf_op jit(solution)/shard_map/ppermute | solution.py:326
  52.3 9.2 %slice-start = ((s8[7340032]{0:T(1024)(128)(4,1)}), s8[4194304]{0:T(1024)(128)(4,1)S(1)}, s32[]{:S(2)}) async-start(s8[7340032]{0:T(1024)(128)(4,1)} %bitcast.61), calls=%async_computation.1 | async-start | bytes 8388608
  59.7 1.9 %slice-start.1 = ((s8[7340032]{0:T(1024)(128)(4,1)}), s8[3145728]{0:T(1024)(128)(4,1)S(1)}, s32[]{:S(2)}) async-start(s8[7340032]{0:T(1024)(128)(4,1)} %bitcast.61), calls=%async_computation.2 | async-start | bytes 6291456
  59.7 3.7 %slice-start.2 = ((s8[7340032]{0:T(1024)(128)(4,1)}), s8[4194304]{0:T(1024)(128)(4,1)S(1)}, s32[]{:S(2)}) async-start(s8[7340032]{0:T(1024)(128)(4,1)} %bitcast.63), calls=%async_computation.3 | async-start | bytes 8388608
  61.6 2.4 %slice-start.3 = ((s8[7340032]{0:T(1024)(128)(4,1)}), s8[3145728]{0:T(1024)(128)(4,1)S(1)}, s32[]{:S(2)}) async-start(s8[7340032]{0:T(1024)(128)(4,1)} %bitcast.63), calls=%async_computation.4 | async-start | bytes 6291456
  65.6 2.8 %collective-permute-start.21 = (bf16[96,3584]{1,0:T(8,128)(2,1)S(1)}, bf16[96,3584]{1,0:T(8,128)(2,1)S(1)}, u32[]{:S(2)}, u32[]{:S(2)}) collective-permute-start(bf16[96,3584]{1,0:T(8,128)(2,1)S(1)} %slice.98), channel_id=1, source_target_pairs={{0,1},{1,0},{2,3},{3,2},{4,5},{5,4},{6,7},{7,6},{8,9},{9,8},{10,11... | collective-permute-start | bytes 2064392 | tf_op jit(solution)/shard_map/ppermute | solution.py:326
  68.5 5.4 %collective-permute-start.23 = (bf16[16,3584]{1,0:T(8,128)(2,1)S(1)}, bf16[16,3584]{1,0:T(8,128)(2,1)S(1)}, u32[]{:S(2)}, u32[]{:S(2)}) collective-permute-start(bf16[16,3584]{1,0:T(8,128)(2,1)S(1)} %get-tuple-element.139), channel_id=1, source_target_pairs={{0,2},{1,3},{4,0},{5,1},{8,4},{9,5},{12,8},{13,9},{14,12},{15,13},... | collective-permute-start | bytes 344072 | tf_op jit(solution)/shard_map/ppermute | solution.py:326
  69.4 5.1 %collective-permute-start.22 = (bf16[16,3584]{1,0:T(8,128)(2,1)S(1)}, bf16[16,3584]{1,0:T(8,128)(2,1)S(1)}, u32[]{:S(2)}, u32[]{:S(2)}) collective-permute-start(bf16[16,3584]{1,0:T(8,128)(2,1)S(1)} %get-tuple-element.140), channel_id=1, source_target_pairs={{0,4},{1,5},{4,8},{5,9},{8,12},{9,13},{12,14},{13,15},{14,10},{15,... | collective-permute-start | bytes 344072 | tf_op jit(solution)/shard_map/ppermute | solution.py:326
  77.1 8.5 %collective-permute-start.24 = (bf16[160,3584]{1,0:T(8,128)(2,1)S(1)}, bf16[160,3584]{1,0:T(8,128)(2,1)S(1)}, u32[]{:S(2)}, u32[]{:S(2)}) collective-permute-start(bf16[160,3584]{1,0:T(8,128)(2,1)S(1)} %slice.101), channel_id=1, source_target_pairs={{0,1},{1,0},{2,3},{3,2},{4,5},{5,4},{6,7},{7,6},{8,9},{9,8},{10,11... | collective-permute-start | bytes 3440648 | tf_op jit(solution)/shard_map/ppermute | solution.py:326
  77.4 8.1 %collective-permute-start.26 = (bf16[32,3584]{1,0:T(8,128)(2,1)S(1)}, bf16[32,3584]{1,0:T(8,128)(2,1)S(1)}, u32[]{:S(2)}, u32[]{:S(2)}) collective-permute-start(bf16[32,3584]{1,0:T(8,128)(2,1)S(1)} %get-tuple-element.137), channel_id=1, source_target_pairs={{0,2},{1,3},{4,0},{5,1},{8,4},{9,5},{12,8},{13,9},{14,12},{15,13},... | collective-permute-start | bytes 688136 | tf_op jit(solution)/shard_map/ppermute | solution.py:326
  77.9 7.7 %collective-permute-start.25 = (bf16[32,3584]{1,0:T(8,128)(2,1)S(1)}, bf16[32,3584]{1,0:T(8,128)(2,1)S(1)}, u32[]{:S(2)}, u32[]{:S(2)}) collective-permute-start(bf16[32,3584]{1,0:T(8,128)(2,1)S(1)} %get-tuple-element.138), channel_id=1, source_target_pairs={{0,4},{1,5},{4,8},{5,9},{8,12},{9,13},{12,14},{13,15},{14,10},{15,... | collective-permute-start | bytes 688136 | tf_op jit(solution)/shard_map/ppermute | solution.py:326
  85.8 7.0 %collective-permute-start.28 = (bf16[32,3584]{1,0:T(8,128)(2,1)S(1)}, bf16[32,3584]{1,0:T(8,128)(2,1)S(1)}, u32[]{:S(2)}, u32[]{:S(2)}) collective-permute-start(bf16[32,3584]{1,0:T(8,128)(2,1)S(1)} %get-tuple-element.135), channel_id=1, source_target_pairs={{0,2},{1,3},{4,0},{5,1},{8,4},{9,5},{12,8},{13,9},{14,12},{15,13},... | collective-permute-start | bytes 688136 | tf_op jit(solution)/shard_map/ppermute | solution.py:326
  86.9 6.9 %collective-permute-start.27 = (bf16[32,3584]{1,0:T(8,128)(2,1)S(1)}, bf16[32,3584]{1,0:T(8,128)(2,1)S(1)}, u32[]{:S(2)}, u32[]{:S(2)}) collective-permute-start(bf16[32,3584]{1,0:T(8,128)(2,1)S(1)} %get-tuple-element.136), channel_id=1, source_target_pairs={{0,4},{1,5},{4,8},{5,9},{8,12},{9,13},{12,14},{13,15},{14,10},{15,... | collective-permute-start | bytes 688136 | tf_op jit(solution)/shard_map/ppermute | solution.py:326
  94.0 6.1 %collective-permute-start.30 = (bf16[32,3584]{1,0:T(8,128)(2,1)S(1)}, bf16[32,3584]{1,0:T(8,128)(2,1)S(1)}, u32[]{:S(2)}, u32[]{:S(2)}) collective-permute-start(bf16[32,3584]{1,0:T(8,128)(2,1)S(1)} %get-tuple-element.133), channel_id=1, source_target_pairs={{0,2},{1,3},{4,0},{5,1},{8,4},{9,5},{12,8},{13,9},{14,12},{15,13},... | collective-permute-start | bytes 688136 | tf_op jit(solution)/shard_map/ppermute | solution.py:326
  95.5 6.0 %collective-permute-start.29 = (bf16[32,3584]{1,0:T(8,128)(2,1)S(1)}, bf16[32,3584]{1,0:T(8,128)(2,1)S(1)}, u32[]{:S(2)}, u32[]{:S(2)}) collective-permute-start(bf16[32,3584]{1,0:T(8,128)(2,1)S(1)} %get-tuple-element.134), channel_id=1, source_target_pairs={{0,4},{1,5},{4,8},{5,9},{8,12},{9,13},{12,14},{13,15},{14,10},{15,... | collective-permute-start | bytes 688136 | tf_op jit(solution)/shard_map/ppermute | solution.py:326

commit v18 on v17

--- a/solution.py
+++ b/solution.py
@@ -327,7 +327,7 @@
 
     to_right, to_left = shift_perm(chips, 1), shift_perm(chips, -1)
     parted = [
-        shift_perm(chips, 2 - 4 * core)[2 * p + core] for p in range(chips) for core in range(2)
+        shift_perm(chips, 1 - 2 * core)[2 * p + core] for p in range(chips) for core in range(2)
     ]
     first_core = device_index % 2 == 0
 
@@ -378,7 +378,7 @@
     along, w_gate = hold((along, w_gate))
     w_gate = jnp.where(device_index >= 0, w_gate, jnp.zeros_like(w_gate))
     across = [send(along, step_perm(chips, 0, i)) for i in range(1, low)]
-    held[half] = send(jnp.where(first_core, held[2 - half], held[half - 2]), parted)
+    held[half] = send(jnp.where(first_core, held[1 - half], held[half - 1]), parted)
     along_sib = send(along, sibling)
     sib[2], sib[-2] = send(held[2], sibling), send(held[-2], sibling)
     across, along_sib, held, sib, w_gate = hold((across, along_sib, held, sib, w_gate))

time: 103 us -> 103 us (level)
  other arithmetic: 4.95 us -> 7.85 us
  waiting for transfers between devices: 36.9 us -> 34.3 us
    select_n x1, other arithmetic: 3.56 us -> 6.46 us  [local(): w_gate = jnp.where(device_index >= 0, w_gate, jnp.zeros_like(w_gate))]
    ppermute x31, waiting for transfers between devices: 29.3 us -> 26.7 us  [send(): return lax.ppermute(a, 'expert', perm)]
    ppermute x31, starting transfers between devices: 25 us -> 24 us  [send(): return lax.ppermute(a, 'expert', perm)]
  transfers between devices with their start and end apart: 32 -> 32, of which waited for: 14 -> 13; matrix products, arithmetic and copies ran while one was open for 11% -> 13% of each run, Pallas kernels for 6% -> 6%
where the time goes in v18:
time: 103 us; the launch traced here: 102 us
  waiting for transfers between devices  34.3 us (33%)
  starting transfers between devices  30.3 us (29%)
  matrix products  13.9 us (13%)
  Pallas kernels  13.5 us (13%)
  other arithmetic  7.85 us (8%)
  local copies, waits for them, and re-layouts  2.17 us (2%)
    ppermute x31, waiting for transfers between devices, send(): return lax.ppermute(a, 'expert', perm)  26.7 us
    ppermute x31, starting transfers between devices, send(): return lax.ppermute(a, 'expert', perm)  24 us
    dot_general x6, matrix products, product(): return jnp.dot(a, w[0], preferred_element_type=f32)  12.9 us
    pallas_call x1, Pallas kernels, normalize(): pl.pallas_call(lambda *refs: norm_kernel(far, blocks, rows, latent, width...  7.74 us
    all_to_all x1, waiting for transfers between devices, local(): lax.all_to_all(ordered, 'expert', split_axis=0, concat_axis=0, tiled=True)  7.6 us
    select_n x1, other arithmetic, local(): w_gate = jnp.where(device_index >= 0, w_gate, jnp.zeros_like(w_gate))  6.46 us
    all_to_all x1, starting transfers between devices, local(): lax.all_to_all(ordered, 'expert', split_axis=0, concat_axis=0, tiled=True)  6.29 us
    pallas_call x1, Pallas kernels, attention(): pl.pallas_call(lambda *refs: attention_kernel(context, latent, *refs), gr...  4.33 us
  transfers between devices with their start and end apart: 32, of which 13 were waited for; matrix products, arithmetic and copies ran while one was open for 13% of the time, Pallas kernels for 6%

profile of v18, /device:TPU:0, one launch (start us, length us, event | category | flops | bytes accessed | tf_op | source)
XLA Modules:
  0.0 102.3 jit_solution(13006667198556537160)
XLA Ops:
  0.0 0.5 collective-permute-start.5
  0.5 2.6 %collective-permute-start.1 = (bf16[32,3584]{1,0:T(8,128)(2,1)}, bf16[32,3584]{1,0:T(8,128)(2,1)S(1)}, u32[]{:S(2)}, u32[]{:S(2)}) collective-permute-start(bf16[32,3584]{1,0:T(8,128)(2,1)} %bitcast.57), channel_id=1, source_target_pairs={{0,2},{1,3},{4,0},{5,1},{8,4},{9,5},{12,8},{13,9},{14,12},{15,13},... | collective-permute-start | bytes 688136 | tf_op jit(solution)/shard_map/ppermute | solution.py:326
  3.2 1.0 fusion.27
  4.4 0.8 copy.19
  5.1 6.3 %all-to-all-start = ((bf16[16,2,8,576]{3,2,1,0:T(8,128)(2,1)}), bf16[16,2,8,576]{3,2,1,0:T(8,128)(2,1)S(1)}, u32[]{:S(2)}, u32[]{:S(2)}) async-start(bf16[16,2,8,576]{3,2,1,0:T(8,128)(2,1)} %copy.19), calls=%async_computation | async-start | bytes 655360 | tf_op jit(solution)/shard_map/all_to_all | solution.py:343
  11.5 1.4 %lookup.1 = (s32[8]{0:T(128)}, s32[17]{0:T(128)}) custom-call(s32[128]{0:T(128)} %owner.1, s32[128]{0:T(128)} %lengths.1, s32[272]{0:T(512)} %constant.42.table, s32[1]{0:T(128)} %bitcast.device), custom_call_target="tpu_custom_call" | custom-call | flops 10000000000 | bytes 100000000 | tf_op jit(solution)/shard_map/lookup/pallas_call | solution.py:194
  12.9 0.5 collective-permute-start.4
  13.4 1.7 %collective-permute-start.2 = (bf16[32,3584]{1,0:T(8,128)(2,1)}, bf16[32,3584]{1,0:T(8,128)(2,1)}, u32[]{:S(2)}, u32[]{:S(2)}) collective-permute-start(bf16[32,3584]{1,0:T(8,128)(2,1)} %collective-permute-done.refs_13_), channel_id=1, source_target_pairs={{0,4},{1,5},{4,8},{5,9},{8,12},{9,13},{12,14},{13,15},{14,10},{15,... | collective-permute-start | bytes 688136 | tf_op jit(solution)/shard_map/ppermute | solution.py:326
  15.4 7.6 %all-to-all-done = bf16[16,2,8,576]{3,2,1,0:T(8,128)(2,1)S(1)} async-done(((bf16[16,2,8,576]{3,2,1,0:T(8,128)(2,1)}), bf16[16,2,8,576]{3,2,1,0:T(8,128)(2,1)S(1)}, u32[]{:S(2)}, u32[]{:S(2)}) %all-to-all-start) | async-done | bytes 294944 | tf_op jit(solution)/shard_map/all_to_all | solution.py:343
  23.0 4.3 %attention.1 = bf16[32,640]{1,0:T(8,128)(2,1)S(1)} custom-call(bf16[4,8,36864]{2,1,0:T(8,128)(2,1)S(1)} %copy-done.1, bf16[256,576]{1,0:T(8,128)(2,1)S(1)} %bitcast.52, bf16[32,576]{1,0:T(8,128)(2,1)S(1)} %bitcast.53, s32[8]{0:T(128)} %get-tuple-element.72.refs_3_, s32[32,8]{1,0:T(8,128)S(1)} %bitcast.54), custom_call_target="tpu_custom_call" | custom-call | flops 679477248 | bytes 2359296 | tf_op jit(solution)/shard_map/attention/pallas_call | solution.py:274
  27.4 0.7 collective-permute-start.10
  28.1 1.4 %collective-permute-start.11 = (bf16[32,3584]{1,0:T(8,128)(2,1)}, bf16[32,3584]{1,0:T(8,128)(2,1)S(1)}, u32[]{:S(2)}, u32[]{:S(2)}) collective-permute-start(bf16[32,3584]{1,0:T(8,128)(2,1)} %collective-permute-done.3.refs_14_), channel_id=1, source_target_pairs={{0,2},{1,3},{4,0},{5,1},{8,4},{9,5},{12,8},{13,9},{14,12},{15,13},... | collective-permute-start | bytes 688136 | tf_op jit(solution)/shard_map/ppermute | solution.py:326
  29.5 0.7 collective-permute-start.9
  30.2 1.3 %collective-permute-start.8 = (bf16[32,640]{1,0:T(8,128)(2,1)S(1)}, bf16[32,640]{1,0:T(8,128)(2,1)S(1)}, u32[]{:S(2)}, u32[]{:S(2)}) collective-permute-start(bf16[32,640]{1,0:T(8,128)(2,1)S(1)} %attention.1), channel_id=1, source_target_pairs={{0,8},{1,9},{2,10},{3,11},{4,12},{5,13},{6,14},{7,15},{8,0},{9,1},... | collective-permute-start | bytes 122888 | tf_op jit(solution)/shard_map/ppermute | solution.py:326
  31.6 2.3 %collective-permute-start.7 = (bf16[32,640]{1,0:T(8,128)(2,1)S(1)}, bf16[32,640]{1,0:T(8,128)(2,1)S(1)}, u32[]{:S(2)}, u32[]{:S(2)}) collective-permute-start(bf16[32,640]{1,0:T(8,128)(2,1)S(1)} %attention.1), channel_id=1, source_target_pairs={{0,4},{1,5},{2,6},{3,7},{4,0},{5,1},{6,2},{7,3},{8,12},{9,13},{10,... | collective-permute-start | bytes 122888 | tf_op jit(solution)/shard_map/ppermute | solution.py:326
  33.9 3.9 %collective-permute-done.9 = bf16[32,640]{1,0:T(8,128)(2,1)S(1)} collective-permute-done((bf16[32,640]{1,0:T(8,128)(2,1)S(1)}, bf16[32,640]{1,0:T(8,128)(2,1)S(1)}, u32[]{:S(2)}, u32[]{:S(2)}) %collective-permute-start.9) | collective-permute-done | bytes 40992 | tf_op jit(solution)/shard_map/ppermute | solution.py:326
  37.8 1.2 %collective-permute-done.8 = bf16[32,640]{1,0:T(8,128)(2,1)S(1)} collective-permute-done((bf16[32,640]{1,0:T(8,128)(2,1)S(1)}, bf16[32,640]{1,0:T(8,128)(2,1)S(1)}, u32[]{:S(2)}, u32[]{:S(2)}) %collective-permute-start.8) | collective-permute-done | bytes 40992 | tf_op jit(solution)/shard_map/ppermute | solution.py:326
  39.1 1.4 %collective-permute-start.12 = (bf16[128,640]{1,0:T(8,128)(2,1)S(1)}, bf16[128,640]{1,0:T(8,128)(2,1)S(1)}, u32[]{:S(2)}, u32[]{:S(2)}) collective-permute-start(bf16[128,640]{1,0:T(8,128)(2,1)S(1)} %pad_maximum_fusion.refs_1_), channel_id=1, source_target_pairs={{0,2},{1,3},{2,0},{3,1},{4,6},{5,7},{6,4},{7,5},{8,10},{9,11},{10,... | collective-permute-start | bytes 491528 | tf_op jit(solution)/shard_map/ppermute | solution.py:326
  40.7 0.4 collective-permute-start.15
  41.2 6.5 %broadcast_select_fusion = bf16[1,3584,1024]{2,1,0:T(8,128)(2,1)} fusion(bf16[1,3584,1024]{2,1,0:T(8,128)(2,1)} %param.24, pred[]{:T(512)S(6)} %ge.3), kind=kLoop, calls=%fused_computation.12 | loop fusion | flops 3670016 | bytes 14680065 | tf_op jit(solution)/shard_map/jit(_where)/select_n | solution.py:379
  47.7 0.5 collective-permute-done.14.refs_5_
  48.2 0.5 collective-permute-start.19
  48.8 0.4 collective-permute-start.17
  49.2 1.4 %collective-permute-done.17.refs_4_ = bf16[128,640]{1,0:T(8,128)(2,1)S(1)} collective-permute-done((bf16[128,640]{1,0:T(8,128)(2,1)S(1)}, bf16[128,640]{1,0:T(8,128)(2,1)S(1)}, u32[]{:S(2)}, u32[]{:S(2)}) %collective-permute-start.17) | collective-permute-done | bytes 163872 | tf_op jit(solution)/shard_map/ppermute | solution.py:326
  50.6 7.7 %normalize.1 = (bf16[192,3584]{1,0:T(8,128)(2,1)S(1)}, bf16[320,3584]{1,0:T(8,128)(2,1)S(1)}, f32[512,128]{1,0:T(8,128)S(1)}, f32[512,128]{1,0:T(8,128)S(1)}, f32[32,3584]{1,0:T(8,128)S(1)}) custom-call(s32[17]{0:T(128)} %get-tuple-element.71.refs_0_, bf16[128,640]{1,0:T(8,128)(2,1)S(1)} %pad_maximum_fusion.refs_1_, ...), custom_call_target="tpu_custom_call" | custom-call | flops 1879048192 | bytes 18350080 | tf_op jit(solution)/shard_map/normalize/pallas_call | solution.py:148
  58.7 1.7 %fusion.21 = f32[192,1024]{1,0:T(8,128)S(1)} fusion(bf16[192,3584]{1,0:T(8,128)(2,1)S(1)} %get-tuple-element.116, bf16[1,3584,1024]{2,1,0:T(8,128)(2,1)S(1)} %copy-done.4, f32[192]{0:T(256)S(1)} %get-tuple-element.144), kind=kOutput, calls=%fused_computation.17 | convolution fusion | flops 1409482752 | bytes 9503488 | tf_op jit(solution)/shard_map/dot_general | solution.py:405
  60.6 1.8 %multiply_convert_fusion.1 = bf16[192,1024]{1,0:T(8,128)(2,1)S(1)} fusion(f32[192,1024]{1,0:T(8,128)S(1)} %fusion.21, f32[192]{0:T(256)S(1)} %get-tuple-element.143, f32[192]{0:T(256)S(1)} %get-tuple-element.144, bf16[192,3584]{1,0:T(8,128)(2,1)S(1)} %get-tuple-element.116, bf16[1,3584,1024]{2,1,0:T(8,128)(2,1)S(1)} %bitcast.62), kind=kOutput, calls=%fused_computation.21 | convolution fusion | flops 1410859008 | bytes 9897472 | tf_op jit(solution)/shard_map/dot_general | solution.py:405
  62.4 0.5 slice-done.3
  62.9 1.6 %fusion.15 = bf16[192,3584]{1,0:T(8,128)(2,1)S(1)} fusion(bf16[192,1024]{1,0:T(8,128)(2,1)S(1)} %multiply_convert_fusion.1, bf16[1,1024,3584]{2,1,0:T(8,128)(2,1)S(1)} %bitcast.64), kind=kOutput, calls=%fused_computation.14 | convolution fusion | flops 1409974272 | bytes 9109504 | tf_op jit(solution)/shard_map/dot_general | solution.py:405
  64.9 2.5 %fusion.10 = f32[320,1024]{1,0:T(8,128)S(1)} fusion(bf16[320,3584]{1,0:T(8,128)(2,1)S(1)} %get-tuple-element.114, bf16[1,3584,1024]{2,1,0:T(8,128)(2,1)S(1)} %copy-done.4), kind=kOutput, calls=%fused_computation.10 | convolution fusion | flops 2348810240 | bytes 10944512 | tf_op jit(solution)/shard_map/dot_general | solution.py:405
  67.5 1.6 %collective-permute-start.23 = (bf16[16,3584]{1,0:T(8,128)(2,1)S(1)}, bf16[16,3584]{1,0:T(8,128)(2,1)S(1)}, u32[]{:S(2)}, u32[]{:S(2)}) collective-permute-start(bf16[16,3584]{1,0:T(8,128)(2,1)S(1)} %get-tuple-element.139), channel_id=1, source_target_pairs={{0,2},{1,3},{4,0},{5,1},{8,4},{9,5},{12,8},{13,9},{14,12},{15,13},... | collective-permute-start | bytes 344072 | tf_op jit(solution)/shard_map/ppermute | solution.py:326
  69.1 0.5 collective-permute-start.22
  69.6 2.7 %multiply_convert_fusion = bf16[320,1024]{1,0:T(8,128)(2,1)S(1)} fusion(f32[320,1024]{1,0:T(8,128)S(1)} %fusion.10, f32[320]{0:T(512)S(1)} %get-tuple-element.141, f32[320]{0:T(512)S(1)} %get-tuple-element.142, bf16[320,3584]{1,0:T(8,128)(2,1)S(1)} %get-tuple-element.114, bf16[1,3584,1024]{2,1,0:T(8,128)(2,1)S(1)} %bitcast.62), kind=kOutput, calls=%fused_computation.16 | convolution fusion | flops 2351759360 | bytes 11602432 | tf_op jit(solution)/shard_map/dot_general | solution.py:405
  72.3 0.6 collective-permute-done.23
  72.9 1.2 %collective-permute-done.22 = bf16[16,3584]{1,0:T(8,128)(2,1)S(1)} collective-permute-done((bf16[16,3584]{1,0:T(8,128)(2,1)S(1)}, bf16[16,3584]{1,0:T(8,128)(2,1)S(1)}, u32[]{:S(2)}, u32[]{:S(2)}) %collective-permute-start.22) | collective-permute-done | bytes 114720 | tf_op jit(solution)/shard_map/ppermute | solution.py:326
  74.2 2.5 %fusion.12 = bf16[320,3584]{1,0:T(8,128)(2,1)S(1)} fusion(bf16[320,1024]{1,0:T(8,128)(2,1)S(1)} %multiply_convert_fusion, bf16[1,1024,3584]{2,1,0:T(8,128)(2,1)S(1)} %bitcast.64), kind=kOutput, calls=%fused_computation.13 | convolution fusion | flops 2349957120 | bytes 10289152 | tf_op jit(solution)/shard_map/dot_general | solution.py:405
  77.0 0.7 collective-permute-start.26
  77.7 1.4 %collective-permute-start.25 = (bf16[32,3584]{1,0:T(8,128)(2,1)S(1)}, bf16[32,3584]{1,0:T(8,128)(2,1)S(1)}, u32[]{:S(2)}, u32[]{:S(2)}) collective-permute-start(bf16[32,3584]{1,0:T(8,128)(2,1)S(1)} %get-tuple-element.138), channel_id=1, source_target_pairs={{0,4},{1,5},{4,8},{5,9},{8,12},{9,13},{12,14},{13,15},{14,10},{15,... | collective-permute-start | bytes 688136 | tf_op jit(solution)/shard_map/ppermute | solution.py:326
  79.1 6.0 %collective-permute-done.26 = bf16[32,3584]{1,0:T(8,128)(2,1)S(1)} collective-permute-done((bf16[32,3584]{1,0:T(8,128)(2,1)S(1)}, bf16[32,3584]{1,0:T(8,128)(2,1)S(1)}, u32[]{:S(2)}, u32[]{:S(2)}) %collective-permute-start.26) | collective-permute-done | bytes 229408 | tf_op jit(solution)/shard_map/ppermute | solution.py:326
  85.1 0.4 collective-permute-done.25
  85.6 1.2 %collective-permute-start.28 = (bf16[32,3584]{1,0:T(8,128)(2,1)S(1)}, bf16[32,3584]{1,0:T(8,128)(2,1)S(1)}, u32[]{:S(2)}, u32[]{:S(2)}) collective-permute-start(bf16[32,3584]{1,0:T(8,128)(2,1)S(1)} %get-tuple-element.135), channel_id=1, source_target_pairs={{0,2},{1,3},{4,0},{5,1},{8,4},{9,5},{12,8},{13,9},{14,12},{15,13},... | collective-permute-start | bytes 688136 | tf_op jit(solution)/shard_map/ppermute | solution.py:326
  86.8 0.8 collective-permute-start.27
  87.7 4.9 %collective-permute-done.28 = bf16[32,3584]{1,0:T(8,128)(2,1)S(1)} collective-permute-done((bf16[32,3584]{1,0:T(8,128)(2,1)S(1)}, bf16[32,3584]{1,0:T(8,128)(2,1)S(1)}, u32[]{:S(2)}, u32[]{:S(2)}) %collective-permute-start.28) | collective-permute-done | bytes 229408 | tf_op jit(solution)/shard_map/ppermute | solution.py:326
  92.6 0.9 collective-permute-done.27
  93.6 1.8 %collective-permute-start.30 = (bf16[32,3584]{1,0:T(8,128)(2,1)S(1)}, bf16[32,3584]{1,0:T(8,128)(2,1)S(1)}, u32[]{:S(2)}, u32[]{:S(2)}) collective-permute-start(bf16[32,3584]{1,0:T(8,128)(2,1)S(1)} %get-tuple-element.133), channel_id=1, source_target_pairs={{0,2},{1,3},{4,0},{5,1},{8,4},{9,5},{12,8},{13,9},{14,12},{15,13},... | collective-permute-start | bytes 688136 | tf_op jit(solution)/shard_map/ppermute | solution.py:326
  95.7 4.0 %collective-permute-done.30 = bf16[32,3584]{1,0:T(8,128)(2,1)S(1)} collective-permute-done((bf16[32,3584]{1,0:T(8,128)(2,1)S(1)}, bf16[32,3584]{1,0:T(8,128)(2,1)S(1)}, u32[]{:S(2)}, u32[]{:S(2)}) %collective-permute-start.30) | collective-permute-done | bytes 229408 | tf_op jit(solution)/shard_map/ppermute | solution.py:326
  99.7 1.7 %collective-permute-done.29 = bf16[32,3584]{1,0:T(8,128)(2,1)S(1)} collective-permute-done((bf16[32,3584]{1,0:T(8,128)(2,1)S(1)}, bf16[32,3584]{1,0:T(8,128)(2,1)S(1)}, u32[]{:S(2)}, u32[]{:S(2)}) %collective-permute-start.29) | collective-permute-done | bytes 229408 | tf_op jit(solution)/shard_map/ppermute | solution.py:326
  101.5 0.8 fusion.32
  (64 shorter events, 3.1 us)
Async XLA Ops:
  0.0 3.2 %copy-start = (bf16[128,2,576]{0,2,1:T(8,128)(2,1)S(1)}, bf16[128,2,576]{0,2,1:T(8,128)(2,1)}, u32[]{:S(2)}) copy-start(bf16[128,2,576]{0,2,1:T(8,128)(2,1)} %param.16) | copy-start | bytes 884740
  0.0 27.4 %collective-permute-start.5 = (bf16[32,3584]{1,0:T(8,128)(2,1)}, bf16[32,3584]{1,0:T(8,128)(2,1)S(1)}, u32[]{:S(2)}, u32[]{:S(2)}) collective-permute-start(bf16[32,3584]{1,0:T(8,128)(2,1)} %bitcast.56), channel_id=1, source_target_pairs={{0,1},{1,0},{2,3},{3,2},{4,5},{5,4},{6,7},{7,6},{8,9},{9,8},{10,11... | collective-permute-start | bytes 688136 | tf_op jit(solution)/shard_map/ppermute | solution.py:326
  0.5 12.4 %collective-permute-start.1 = (bf16[32,3584]{1,0:T(8,128)(2,1)}, bf16[32,3584]{1,0:T(8,128)(2,1)S(1)}, u32[]{:S(2)}, u32[]{:S(2)}) collective-permute-start(bf16[32,3584]{1,0:T(8,128)(2,1)} %bitcast.57), channel_id=1, source_target_pairs={{0,2},{1,3},{4,0},{5,1},{8,4},{9,5},{12,8},{13,9},{14,12},{15,13},... | collective-permute-start | bytes 688136 | tf_op jit(solution)/shard_map/ppermute | solution.py:326
  3.0 9.9 %collective-permute-start = (bf16[32,3584]{1,0:T(8,128)(2,1)}, bf16[32,3584]{1,0:T(8,128)(2,1)}, u32[]{:S(2)}, u32[]{:S(2)}) collective-permute-start(bf16[32,3584]{1,0:T(8,128)(2,1)} %bitcast.58), channel_id=1, source_target_pairs={{0,4},{1,5},{4,8},{5,9},{8,12},{9,13},{12,14},{13,15},{14,10},{15,... | collective-permute-start | bytes 688136 | tf_op jit(solution)/shard_map/ppermute | solution.py:326
  5.1 17.9 %all-to-all-start = ((bf16[16,2,8,576]{3,2,1,0:T(8,128)(2,1)}), bf16[16,2,8,576]{3,2,1,0:T(8,128)(2,1)S(1)}, u32[]{:S(2)}, u32[]{:S(2)}) async-start(bf16[16,2,8,576]{3,2,1,0:T(8,128)(2,1)} %copy.19), calls=%async_computation | async-start | bytes 655360 | tf_op jit(solution)/shard_map/all_to_all | solution.py:343
  11.4 4.0 %copy-start.5 = (bf16[3584]{0:T(1024)(128)(2,1)S(1)}, bf16[3584]{0:T(1024)(128)(2,1)}, u32[]{:S(2)}) copy-start(bf16[3584]{0:T(1024)(128)(2,1)} %param.22) | copy-start | bytes 21508
  11.5 11.6 %copy-start.1 = (bf16[4,8,36864]{2,1,0:T(8,128)(2,1)S(1)}, bf16[4,8,36864]{2,1,0:T(8,128)(2,1)}, u32[]{:S(2)}) copy-start(bf16[4,8,36864]{2,1,0:T(8,128)(2,1)} %refs_0_.1) | copy-start | bytes 7077892
  11.5 11.6 %copy-start.2 = (bf16[4,8,576]{2,1,0:T(8,128)(2,1)S(1)}, bf16[4,8,576]{2,1,0:T(8,128)(2,1)}, u32[]{:S(2)}) copy-start(bf16[4,8,576]{2,1,0:T(8,128)(2,1)} %param.15) | copy-start | bytes 110596
  11.5 11.5 %copy-start.3 = (s32[4,8,8]{2,1,0:T(8,128)S(1)}, s32[4,8,8]{2,1,0:T(8,128)}, u32[]{:S(2)}) copy-start(s32[4,8,8]{2,1,0:T(8,128)} %param.20) | copy-start | bytes 3076
  12.9 14.5 %collective-permute-start.4 = (bf16[32,3584]{1,0:T(8,128)(2,1)}, bf16[32,3584]{1,0:T(8,128)(2,1)}, u32[]{:S(2)}, u32[]{:S(2)}) collective-permute-start(bf16[32,3584]{1,0:T(8,128)(2,1)} %collective-permute-done.refs_13_), channel_id=1, source_target_pairs={{0,1},{1,0},{2,3},{3,2},{4,5},{5,4},{6,7},{7,6},{8,9},{9,8},{10,11... | collective-permute-start | bytes 688136 | tf_op jit(solution)/shard_map/ppermute | solution.py:326
  13.4 14.0 %collective-permute-start.2 = (bf16[32,3584]{1,0:T(8,128)(2,1)}, bf16[32,3584]{1,0:T(8,128)(2,1)}, u32[]{:S(2)}, u32[]{:S(2)}) collective-permute-start(bf16[32,3584]{1,0:T(8,128)(2,1)} %collective-permute-done.refs_13_), channel_id=1, source_target_pairs={{0,4},{1,5},{4,8},{5,9},{8,12},{9,13},{12,14},{13,15},{14,10},{15,... | collective-permute-start | bytes 688136 | tf_op jit(solution)/shard_map/ppermute | solution.py:326
  15.1 12.3 %collective-permute-start.6 = (bf16[32,3584]{1,0:T(8,128)(2,1)S(1)}, bf16[32,3584]{1,0:T(8,128)(2,1)}, u32[]{:S(2)}, u32[]{:S(2)}) collective-permute-start(bf16[32,3584]{1,0:T(8,128)(2,1)S(1)} %collective-permute-done.1.refs_12_), channel_id=1, source_target_pairs={{0,1},{1,0},{2,3},{3,2},{4,5},{5,4},{6,7},{7,6},{8,9},{9,8},{10,11... | collective-permute-start | bytes 688136 | tf_op jit(solution)/shard_map/ppermute | solution.py:326
  15.1 12.3 %collective-permute-start.3 = (bf16[32,3584]{1,0:T(8,128)(2,1)S(1)}, bf16[32,3584]{1,0:T(8,128)(2,1)}, u32[]{:S(2)}, u32[]{:S(2)}) collective-permute-start(bf16[32,3584]{1,0:T(8,128)(2,1)S(1)} %collective-permute-done.1.refs_12_), channel_id=1, source_target_pairs={{0,2},{1,3},{4,0},{5,1},{8,4},{9,5},{12,8},{13,9},{14,12},{15,13},... | collective-permute-start | bytes 688136 | tf_op jit(solution)/shard_map/ppermute | solution.py:326
  27.4 11.6 %collective-permute-start.10 = (bf16[32,3584]{1,0:T(8,128)(2,1)}, bf16[32,3584]{1,0:T(8,128)(2,1)S(1)}, u32[]{:S(2)}, u32[]{:S(2)}) collective-permute-start(bf16[32,3584]{1,0:T(8,128)(2,1)} %collective-permute-done.2.refs_15_), channel_id=1, source_target_pairs={{0,4},{1,5},{4,8},{5,9},{8,12},{9,13},{12,14},{13,15},{14,10},{15,... | collective-permute-start | bytes 688136 | tf_op jit(solution)/shard_map/ppermute | solution.py:326
  28.1 10.9 %collective-permute-start.11 = (bf16[32,3584]{1,0:T(8,128)(2,1)}, bf16[32,3584]{1,0:T(8,128)(2,1)S(1)}, u32[]{:S(2)}, u32[]{:S(2)}) collective-permute-start(bf16[32,3584]{1,0:T(8,128)(2,1)} %collective-permute-done.3.refs_14_), channel_id=1, source_target_pairs={{0,2},{1,3},{4,0},{5,1},{8,4},{9,5},{12,8},{13,9},{14,12},{15,13},... | collective-permute-start | bytes 688136 | tf_op jit(solution)/shard_map/ppermute | solution.py:326
  29.5 8.3 %collective-permute-start.9 = (bf16[32,640]{1,0:T(8,128)(2,1)S(1)}, bf16[32,640]{1,0:T(8,128)(2,1)S(1)}, u32[]{:S(2)}, u32[]{:S(2)}) collective-permute-start(bf16[32,640]{1,0:T(8,128)(2,1)S(1)} %attention.1), channel_id=1, source_target_pairs={{0,12},{1,13},{2,14},{3,15},{4,8},{5,9},{6,10},{7,11},{8,4},{9,5},... | collective-permute-start | bytes 122888 | tf_op jit(solution)/shard_map/ppermute | solution.py:326
  30.2 8.7 %collective-permute-start.8 = (bf16[32,640]{1,0:T(8,128)(2,1)S(1)}, bf16[32,640]{1,0:T(8,128)(2,1)S(1)}, u32[]{:S(2)}, u32[]{:S(2)}) collective-permute-start(bf16[32,640]{1,0:T(8,128)(2,1)S(1)} %attention.1), channel_id=1, source_target_pairs={{0,8},{1,9},{2,10},{3,11},{4,12},{5,13},{6,14},{7,15},{8,0},{9,1},... | collective-permute-start | bytes 122888 | tf_op jit(solution)/shard_map/ppermute | solution.py:326
  31.6 7.4 %collective-permute-start.7 = (bf16[32,640]{1,0:T(8,128)(2,1)S(1)}, bf16[32,640]{1,0:T(8,128)(2,1)S(1)}, u32[]{:S(2)}, u32[]{:S(2)}) collective-permute-start(bf16[32,640]{1,0:T(8,128)(2,1)S(1)} %attention.1), channel_id=1, source_target_pairs={{0,4},{1,5},{2,6},{3,7},{4,0},{5,1},{6,2},{7,3},{8,12},{9,13},{10,... | collective-permute-start | bytes 122888 | tf_op jit(solution)/shard_map/ppermute | solution.py:326
  39.0 8.7 %collective-permute-start.13 = (bf16[128,640]{1,0:T(8,128)(2,1)S(1)}, bf16[128,640]{1,0:T(8,128)(2,1)S(1)}, u32[]{:S(2)}, u32[]{:S(2)}) collective-permute-start(bf16[128,640]{1,0:T(8,128)(2,1)S(1)} %pad_maximum_fusion.refs_1_), channel_id=1, source_target_pairs={{0,1},{1,0},{2,3},{3,2},{4,5},{5,4},{6,7},{7,6},{8,9},{9,8},{10,11... | collective-permute-start | bytes 491528 | tf_op jit(solution)/shard_map/ppermute | solution.py:326
  39.1 8.6 %collective-permute-start.12 = (bf16[128,640]{1,0:T(8,128)(2,1)S(1)}, bf16[128,640]{1,0:T(8,128)(2,1)S(1)}, u32[]{:S(2)}, u32[]{:S(2)}) collective-permute-start(bf16[128,640]{1,0:T(8,128)(2,1)S(1)} %pad_maximum_fusion.refs_1_), channel_id=1, source_target_pairs={{0,2},{1,3},{2,0},{3,1},{4,6},{5,7},{6,4},{7,5},{8,10},{9,11},{10,... | collective-permute-start | bytes 491528 | tf_op jit(solution)/shard_map/ppermute | solution.py:326
  40.5 7.6 %collective-permute-start.14 = (bf16[32,3584]{1,0:T(8,128)(2,1)S(1)}, bf16[32,3584]{1,0:T(8,128)(2,1)S(1)}, u32[]{:S(2)}, u32[]{:S(2)}) collective-permute-start(bf16[32,3584]{1,0:T(8,128)(2,1)S(1)} %broadcast_select_fusion.1), channel_id=1, source_target_pairs={{0,4},{1,3},{4,8},{5,1},{8,12},{9,5},{12,14},{13,9},{14,10},{15,13... | collective-permute-start | bytes 688136 | tf_op jit(solution)/shard_map/ppermute | solution.py:326
  40.7 7.5 %collective-permute-start.15 = (bf16[32,3584]{1,0:T(8,128)(2,1)}, bf16[32,3584]{1,0:T(8,128)(2,1)S(1)}, u32[]{:S(2)}, u32[]{:S(2)}) collective-permute-start(bf16[32,3584]{1,0:T(8,128)(2,1)} %collective-permute-done.2.refs_15_), channel_id=1, source_target_pairs={{0,1},{1,0},{2,3},{3,2},{4,5},{5,4},{6,7},{7,6},{8,9},{9,8},{10,11... | collective-permute-start | bytes 688136 | tf_op jit(solution)/shard_map/ppermute | solution.py:326
  41.2 7.0 %collective-permute-start.16 = (bf16[32,3584]{1,0:T(8,128)(2,1)}, bf16[32,3584]{1,0:T(8,128)(2,1)S(1)}, u32[]{:S(2)}, u32[]{:S(2)}) collective-permute-start(bf16[32,3584]{1,0:T(8,128)(2,1)} %collective-permute-done.3.refs_14_), channel_id=1, source_target_pairs={{0,1},{1,0},{2,3},{3,2},{4,5},{5,4},{6,7},{7,6},{8,9},{9,8},{10,11... | collective-permute-start | bytes 688136 | tf_op jit(solution)/shard_map/ppermute | solution.py:326
  48.2 2.4 %collective-permute-start.18 = (bf16[32,3584]{1,0:T(8,128)(2,1)S(1)}, bf16[32,3584]{1,0:T(8,128)(2,1)S(1)}, u32[]{:S(2)}, u32[]{:S(2)}) collective-permute-start(bf16[32,3584]{1,0:T(8,128)(2,1)S(1)} %collective-permute-done.14.refs_5_), channel_id=1, source_target_pairs={{0,1},{1,0},{2,3},{3,2},{4,5},{5,4},{6,7},{7,6},{8,9},{9,8},{10,11... | collective-permute-start | bytes 688136 | tf_op jit(solution)/shard_map/ppermute | solution.py:326
  48.2 2.3 %collective-permute-start.19 = (bf16[32,3584]{1,0:T(8,128)(2,1)S(1)}, bf16[32,3584]{1,0:T(8,128)(2,1)S(1)}, u32[]{:S(2)}, u32[]{:S(2)}) collective-permute-start(bf16[32,3584]{1,0:T(8,128)(2,1)S(1)} %collective-permute-done.11.refs_6_), channel_id=1, source_target_pairs={{0,1},{1,0},{2,3},{3,2},{4,5},{5,4},{6,7},{7,6},{8,9},{9,8},{10,11... | collective-permute-start | bytes 688136 | tf_op jit(solution)/shard_map/ppermute | solution.py:326
  48.7 1.9 %collective-permute-start.20 = (bf16[32,3584]{1,0:T(8,128)(2,1)S(1)}, bf16[32,3584]{1,0:T(8,128)(2,1)S(1)}, u32[]{:S(2)}, u32[]{:S(2)}) collective-permute-start(bf16[32,3584]{1,0:T(8,128)(2,1)S(1)} %collective-permute-done.10.refs_7_), channel_id=1, source_target_pairs={{0,1},{1,0},{2,3},{3,2},{4,5},{5,4},{6,7},{7,6},{8,9},{9,8},{10,11... | collective-permute-start | bytes 688136 | tf_op jit(solution)/shard_map/ppermute | solution.py:326
  48.8 1.8 %collective-permute-start.17 = (bf16[128,640]{1,0:T(8,128)(2,1)S(1)}, bf16[128,640]{1,0:T(8,128)(2,1)S(1)}, u32[]{:S(2)}, u32[]{:S(2)}) collective-permute-start(bf16[128,640]{1,0:T(8,128)(2,1)S(1)} %collective-permute-done.12.refs_2_), channel_id=1, source_target_pairs={{0,1},{1,0},{2,3},{3,2},{4,5},{5,4},{6,7},{7,6},{8,9},{9,8},{10,11... | collective-permute-start | bytes 491528 | tf_op jit(solution)/shard_map/ppermute | solution.py:326
  50.6 8.1 %copy-start.4 = (bf16[1,3584,1024]{2,1,0:T(8,128)(2,1)S(1)}, bf16[1,3584,1024]{2,1,0:T(8,128)(2,1)}, u32[]{:S(2)}) copy-start(bf16[1,3584,1024]{2,1,0:T(8,128)(2,1)} %broadcast_select_fusion) | copy-start | bytes 22020100
  50.6 9.8 %slice-start = ((s8[7340032]{0:T(1024)(128)(4,1)}), s8[4194304]{0:T(1024)(128)(4,1)S(1)}, s32[]{:S(2)}) async-start(s8[7340032]{0:T(1024)(128)(4,1)} %bitcast.61), calls=%async_computation.1 | async-start | bytes 8388608
  58.7 1.9 %slice-start.1 = ((s8[7340032]{0:T(1024)(128)(4,1)}), s8[3145728]{0:T(1024)(128)(4,1)S(1)}, s32[]{:S(2)}) async-start(s8[7340032]{0:T(1024)(128)(4,1)} %bitcast.61), calls=%async_computation.2 | async-start | bytes 6291456
  58.7 3.7 %slice-start.2 = ((s8[7340032]{0:T(1024)(128)(4,1)}), s8[4194304]{0:T(1024)(128)(4,1)S(1)}, s32[]{:S(2)}) async-start(s8[7340032]{0:T(1024)(128)(4,1)} %bitcast.63), calls=%async_computation.3 | async-start | bytes 8388608
  60.6 2.4 %slice-start.3 = ((s8[7340032]{0:T(1024)(128)(4,1)}), s8[3145728]{0:T(1024)(128)(4,1)S(1)}, s32[]{:S(2)}) async-start(s8[7340032]{0:T(1024)(128)(4,1)} %bitcast.63), calls=%async_computation.4 | async-start | bytes 6291456
  64.6 2.8 %collective-permute-start.21 = (bf16[96,3584]{1,0:T(8,128)(2,1)S(1)}, bf16[96,3584]{1,0:T(8,128)(2,1)S(1)}, u32[]{:S(2)}, u32[]{:S(2)}) collective-permute-start(bf16[96,3584]{1,0:T(8,128)(2,1)S(1)} %slice.98), channel_id=1, source_target_pairs={{0,1},{1,0},{2,3},{3,2},{4,5},{5,4},{6,7},{7,6},{8,9},{9,8},{10,11... | collective-permute-start | bytes 2064392 | tf_op jit(solution)/shard_map/ppermute | solution.py:326
  67.5 5.4 %collective-permute-start.23 = (bf16[16,3584]{1,0:T(8,128)(2,1)S(1)}, bf16[16,3584]{1,0:T(8,128)(2,1)S(1)}, u32[]{:S(2)}, u32[]{:S(2)}) collective-permute-start(bf16[16,3584]{1,0:T(8,128)(2,1)S(1)} %get-tuple-element.139), channel_id=1, source_target_pairs={{0,2},{1,3},{4,0},{5,1},{8,4},{9,5},{12,8},{13,9},{14,12},{15,13},... | collective-permute-start | bytes 344072 | tf_op jit(solution)/shard_map/ppermute | solution.py:326
  69.1 5.1 %collective-permute-start.22 = (bf16[16,3584]{1,0:T(8,128)(2,1)S(1)}, bf16[16,3584]{1,0:T(8,128)(2,1)S(1)}, u32[]{:S(2)}, u32[]{:S(2)}) collective-permute-start(bf16[16,3584]{1,0:T(8,128)(2,1)S(1)} %get-tuple-element.140), channel_id=1, source_target_pairs={{0,4},{1,5},{4,8},{5,9},{8,12},{9,13},{12,14},{13,15},{14,10},{15,... | collective-permute-start | bytes 344072 | tf_op jit(solution)/shard_map/ppermute | solution.py:326
  76.8 8.7 %collective-permute-start.24 = (bf16[160,3584]{1,0:T(8,128)(2,1)S(1)}, bf16[160,3584]{1,0:T(8,128)(2,1)S(1)}, u32[]{:S(2)}, u32[]{:S(2)}) collective-permute-start(bf16[160,3584]{1,0:T(8,128)(2,1)S(1)} %slice.101), channel_id=1, source_target_pairs={{0,1},{1,0},{2,3},{3,2},{4,5},{5,4},{6,7},{7,6},{8,9},{9,8},{10,11... | collective-permute-start | bytes 3440648 | tf_op jit(solution)/shard_map/ppermute | solution.py:326
  77.0 8.1 %collective-permute-start.26 = (bf16[32,3584]{1,0:T(8,128)(2,1)S(1)}, bf16[32,3584]{1,0:T(8,128)(2,1)S(1)}, u32[]{:S(2)}, u32[]{:S(2)}) collective-permute-start(bf16[32,3584]{1,0:T(8,128)(2,1)S(1)} %get-tuple-element.137), channel_id=1, source_target_pairs={{0,2},{1,3},{4,0},{5,1},{8,4},{9,5},{12,8},{13,9},{14,12},{15,13},... | collective-permute-start | bytes 688136 | tf_op jit(solution)/shard_map/ppermute | solution.py:326
  77.7 7.7 %collective-permute-start.25 = (bf16[32,3584]{1,0:T(8,128)(2,1)S(1)}, bf16[32,3584]{1,0:T(8,128)(2,1)S(1)}, u32[]{:S(2)}, u32[]{:S(2)}) collective-permute-start(bf16[32,3584]{1,0:T(8,128)(2,1)S(1)} %get-tuple-element.138), channel_id=1, source_target_pairs={{0,4},{1,5},{4,8},{5,9},{8,12},{9,13},{12,14},{13,15},{14,10},{15,... | collective-permute-start | bytes 688136 | tf_op jit(solution)/shard_map/ppermute | solution.py:326
  85.6 7.0 %collective-permute-start.28 = (bf16[32,3584]{1,0:T(8,128)(2,1)S(1)}, bf16[32,3584]{1,0:T(8,128)(2,1)S(1)}, u32[]{:S(2)}, u32[]{:S(2)}) collective-permute-start(bf16[32,3584]{1,0:T(8,128)(2,1)S(1)} %get-tuple-element.135), channel_id=1, source_target_pairs={{0,2},{1,3},{4,0},{5,1},{8,4},{9,5},{12,8},{13,9},{14,12},{15,13},... | collective-permute-start | bytes 688136 | tf_op jit(solution)/shard_map/ppermute | solution.py:326
  86.8 6.6 %collective-permute-start.27 = (bf16[32,3584]{1,0:T(8,128)(2,1)S(1)}, bf16[32,3584]{1,0:T(8,128)(2,1)S(1)}, u32[]{:S(2)}, u32[]{:S(2)}) collective-permute-start(bf16[32,3584]{1,0:T(8,128)(2,1)S(1)} %get-tuple-element.136), channel_id=1, source_target_pairs={{0,4},{1,5},{4,8},{5,9},{8,12},{9,13},{12,14},{13,15},{14,10},{15,... | collective-permute-start | bytes 688136 | tf_op jit(solution)/shard_map/ppermute | solution.py:326
  93.6 6.1 %collective-permute-start.30 = (bf16[32,3584]{1,0:T(8,128)(2,1)S(1)}, bf16[32,3584]{1,0:T(8,128)(2,1)S(1)}, u32[]{:S(2)}, u32[]{:S(2)}) collective-permute-start(bf16[32,3584]{1,0:T(8,128)(2,1)S(1)} %get-tuple-element.133), channel_id=1, source_target_pairs={{0,2},{1,3},{4,0},{5,1},{8,4},{9,5},{12,8},{13,9},{14,12},{15,13},... | collective-permute-start | bytes 688136 | tf_op jit(solution)/shard_map/ppermute | solution.py:326
  95.4 6.0 %collective-permute-start.29 = (bf16[32,3584]{1,0:T(8,128)(2,1)S(1)}, bf16[32,3584]{1,0:T(8,128)(2,1)S(1)}, u32[]{:S(2)}, u32[]{:S(2)}) collective-permute-start(bf16[32,3584]{1,0:T(8,128)(2,1)S(1)} %get-tuple-element.134), channel_id=1, source_target_pairs={{0,4},{1,5},{4,8},{5,9},{8,12},{9,13},{12,14},{13,15},{14,10},{15,... | collective-permute-start | bytes 688136 | tf_op jit(solution)/shard_map/ppermute | solution.py:326

commit v19 on v18

--- a/solution.py
+++ b/solution.py
@@ -168,7 +168,7 @@
             pltpu.VMEM((total, experts_all), jnp.float32),
         ],
         compiler_params=pltpu.CompilerParams(
-            dimension_semantics=("arbitrary",), vmem_limit_bytes=(int(need) // (1 << 20) + 6) << 20
+            dimension_semantics=("arbitrary",), vmem_limit_bytes=(int(need) // (1 << 20) + 3) << 20
         ),
         cost_estimate=pl.CostEstimate(
             flops=2 * total * width * latent,

time: 103 us -> 103 us (level)
  transfers between devices with their start and end apart: 32 -> 32, of which waited for: 13 -> 13; matrix products, arithmetic and copies ran while one was open for 13% -> 14% of each run, Pallas kernels for 6% -> 6%
where the time goes in v19:
time: 103 us; the launch traced here: 102 us
  waiting for transfers between devices  34.2 us (33%)
  starting transfers between devices  30.3 us (29%)
  matrix products  14.2 us (14%)
  Pallas kernels  13.5 us (13%)
  other arithmetic  7.85 us (8%)
  local copies, waits for them, and re-layouts  2.18 us (2%)
    ppermute x31, waiting for transfers between devices, send(): return lax.ppermute(a, 'expert', perm)  26.6 us
    ppermute x31, starting transfers between devices, send(): return lax.ppermute(a, 'expert', perm)  24 us
    dot_general x6, matrix products, product(): return jnp.dot(a, w[0], preferred_element_type=f32)  13.2 us
    pallas_call x1, Pallas kernels, normalize(): pl.pallas_call(lambda *refs: norm_kernel(far, blocks, rows, latent, width...  7.74 us
    all_to_all x1, waiting for transfers between devices, local(): lax.all_to_all(ordered, 'expert', split_axis=0, concat_axis=0, tiled=True)  7.6 us
    select_n x1, other arithmetic, local(): w_gate = jnp.where(device_index >= 0, w_gate, jnp.zeros_like(w_gate))  6.46 us
    all_to_all x1, starting transfers between devices, local(): lax.all_to_all(ordered, 'expert', split_axis=0, concat_axis=0, tiled=True)  6.29 us
    pallas_call x1, Pallas kernels, attention(): pl.pallas_call(lambda *refs: attention_kernel(context, latent, *refs), gr...  4.33 us
  transfers between devices with their start and end apart: 32, of which 13 were waited for; matrix products, arithmetic and copies ran while one was open for 14% of the time, Pallas kernels for 6%

profile of v19, /device:TPU:0, one launch (start us, length us, event | category | flops | bytes accessed | tf_op | source)
XLA Modules:
  0.0 102.5 jit_solution(2174621928303822880)
XLA Ops:
  0.0 0.5 collective-permute-start.5
  0.5 2.6 %collective-permute-start.1 = (bf16[32,3584]{1,0:T(8,128)(2,1)}, bf16[32,3584]{1,0:T(8,128)(2,1)S(1)}, u32[]{:S(2)}, u32[]{:S(2)}) collective-permute-start(bf16[32,3584]{1,0:T(8,128)(2,1)} %bitcast.57), channel_id=1, source_target_pairs={{0,2},{1,3},{4,0},{5,1},{8,4},{9,5},{12,8},{13,9},{14,12},{15,13},... | collective-permute-start | bytes 688136 | tf_op jit(solution)/shard_map/ppermute | solution.py:326
  3.2 1.0 fusion.27
  4.4 0.8 copy.19
  5.1 6.3 %all-to-all-start = ((bf16[16,2,8,576]{3,2,1,0:T(8,128)(2,1)}), bf16[16,2,8,576]{3,2,1,0:T(8,128)(2,1)S(1)}, u32[]{:S(2)}, u32[]{:S(2)}) async-start(bf16[16,2,8,576]{3,2,1,0:T(8,128)(2,1)} %copy.19), calls=%async_computation | async-start | bytes 655360 | tf_op jit(solution)/shard_map/all_to_all | solution.py:343
  11.5 1.4 %lookup.1 = (s32[8]{0:T(128)}, s32[17]{0:T(128)}) custom-call(s32[128]{0:T(128)} %owner.1, s32[128]{0:T(128)} %lengths.1, s32[272]{0:T(512)} %constant.42.table, s32[1]{0:T(128)} %bitcast.device), custom_call_target="tpu_custom_call" | custom-call | flops 10000000000 | bytes 100000000 | tf_op jit(solution)/shard_map/lookup/pallas_call | solution.py:194
  12.9 0.5 collective-permute-start.4
  13.4 1.7 %collective-permute-start.2 = (bf16[32,3584]{1,0:T(8,128)(2,1)}, bf16[32,3584]{1,0:T(8,128)(2,1)}, u32[]{:S(2)}, u32[]{:S(2)}) collective-permute-start(bf16[32,3584]{1,0:T(8,128)(2,1)} %collective-permute-done.refs_13_), channel_id=1, source_target_pairs={{0,4},{1,5},{4,8},{5,9},{8,12},{9,13},{12,14},{13,15},{14,10},{15,... | collective-permute-start | bytes 688136 | tf_op jit(solution)/shard_map/ppermute | solution.py:326
  15.4 7.6 %all-to-all-done = bf16[16,2,8,576]{3,2,1,0:T(8,128)(2,1)S(1)} async-done(((bf16[16,2,8,576]{3,2,1,0:T(8,128)(2,1)}), bf16[16,2,8,576]{3,2,1,0:T(8,128)(2,1)S(1)}, u32[]{:S(2)}, u32[]{:S(2)}) %all-to-all-start) | async-done | bytes 294944 | tf_op jit(solution)/shard_map/all_to_all | solution.py:343
  23.0 4.3 %attention.1 = bf16[32,640]{1,0:T(8,128)(2,1)S(1)} custom-call(bf16[4,8,36864]{2,1,0:T(8,128)(2,1)S(1)} %copy-done.1, bf16[256,576]{1,0:T(8,128)(2,1)S(1)} %bitcast.52, bf16[32,576]{1,0:T(8,128)(2,1)S(1)} %bitcast.53, s32[8]{0:T(128)} %get-tuple-element.72.refs_3_, s32[32,8]{1,0:T(8,128)S(1)} %bitcast.54), custom_call_target="tpu_custom_call" | custom-call | flops 679477248 | bytes 2359296 | tf_op jit(solution)/shard_map/attention/pallas_call | solution.py:274
  27.4 0.7 collective-permute-start.10
  28.1 1.4 %collective-permute-start.11 = (bf16[32,3584]{1,0:T(8,128)(2,1)}, bf16[32,3584]{1,0:T(8,128)(2,1)S(1)}, u32[]{:S(2)}, u32[]{:S(2)}) collective-permute-start(bf16[32,3584]{1,0:T(8,128)(2,1)} %collective-permute-done.3.refs_14_), channel_id=1, source_target_pairs={{0,2},{1,3},{4,0},{5,1},{8,4},{9,5},{12,8},{13,9},{14,12},{15,13},... | collective-permute-start | bytes 688136 | tf_op jit(solution)/shard_map/ppermute | solution.py:326
  29.5 0.7 collective-permute-start.9
  30.2 1.3 %collective-permute-start.8 = (bf16[32,640]{1,0:T(8,128)(2,1)S(1)}, bf16[32,640]{1,0:T(8,128)(2,1)S(1)}, u32[]{:S(2)}, u32[]{:S(2)}) collective-permute-start(bf16[32,640]{1,0:T(8,128)(2,1)S(1)} %attention.1), channel_id=1, source_target_pairs={{0,8},{1,9},{2,10},{3,11},{4,12},{5,13},{6,14},{7,15},{8,0},{9,1},... | collective-permute-start | bytes 122888 | tf_op jit(solution)/shard_map/ppermute | solution.py:326
  31.6 2.3 %collective-permute-start.7 = (bf16[32,640]{1,0:T(8,128)(2,1)S(1)}, bf16[32,640]{1,0:T(8,128)(2,1)S(1)}, u32[]{:S(2)}, u32[]{:S(2)}) collective-permute-start(bf16[32,640]{1,0:T(8,128)(2,1)S(1)} %attention.1), channel_id=1, source_target_pairs={{0,4},{1,5},{2,6},{3,7},{4,0},{5,1},{6,2},{7,3},{8,12},{9,13},{10,... | collective-permute-start | bytes 122888 | tf_op jit(solution)/shard_map/ppermute | solution.py:326
  33.9 3.9 %collective-permute-done.9 = bf16[32,640]{1,0:T(8,128)(2,1)S(1)} collective-permute-done((bf16[32,640]{1,0:T(8,128)(2,1)S(1)}, bf16[32,640]{1,0:T(8,128)(2,1)S(1)}, u32[]{:S(2)}, u32[]{:S(2)}) %collective-permute-start.9) | collective-permute-done | bytes 40992 | tf_op jit(solution)/shard_map/ppermute | solution.py:326
  37.8 1.2 %collective-permute-done.8 = bf16[32,640]{1,0:T(8,128)(2,1)S(1)} collective-permute-done((bf16[32,640]{1,0:T(8,128)(2,1)S(1)}, bf16[32,640]{1,0:T(8,128)(2,1)S(1)}, u32[]{:S(2)}, u32[]{:S(2)}) %collective-permute-start.8) | collective-permute-done | bytes 40992 | tf_op jit(solution)/shard_map/ppermute | solution.py:326
  39.1 1.4 %collective-permute-start.12 = (bf16[128,640]{1,0:T(8,128)(2,1)S(1)}, bf16[128,640]{1,0:T(8,128)(2,1)S(1)}, u32[]{:S(2)}, u32[]{:S(2)}) collective-permute-start(bf16[128,640]{1,0:T(8,128)(2,1)S(1)} %pad_maximum_fusion.refs_1_), channel_id=1, source_target_pairs={{0,2},{1,3},{2,0},{3,1},{4,6},{5,7},{6,4},{7,5},{8,10},{9,11},{10,... | collective-permute-start | bytes 491528 | tf_op jit(solution)/shard_map/ppermute | solution.py:326
  40.7 0.4 collective-permute-start.15
  41.2 6.5 %broadcast_select_fusion = bf16[1,3584,1024]{2,1,0:T(8,128)(2,1)} fusion(bf16[1,3584,1024]{2,1,0:T(8,128)(2,1)} %param.24, pred[]{:T(512)S(6)} %ge.3), kind=kLoop, calls=%fused_computation.12 | loop fusion | flops 3670016 | bytes 14680065 | tf_op jit(solution)/shard_map/jit(_where)/select_n | solution.py:379
  47.7 0.5 collective-permute-done.14.refs_5_
  48.2 0.5 collective-permute-start.19
  48.8 0.4 collective-permute-start.17
  49.2 1.4 %collective-permute-done.17.refs_4_ = bf16[128,640]{1,0:T(8,128)(2,1)S(1)} collective-permute-done((bf16[128,640]{1,0:T(8,128)(2,1)S(1)}, bf16[128,640]{1,0:T(8,128)(2,1)S(1)}, u32[]{:S(2)}, u32[]{:S(2)}) %collective-permute-start.17) | collective-permute-done | bytes 163872 | tf_op jit(solution)/shard_map/ppermute | solution.py:326
  50.6 7.7 %normalize.1 = (bf16[192,3584]{1,0:T(8,128)(2,1)S(1)}, bf16[320,3584]{1,0:T(8,128)(2,1)S(1)}, f32[512,128]{1,0:T(8,128)S(1)}, f32[512,128]{1,0:T(8,128)S(1)}, f32[32,3584]{1,0:T(8,128)S(1)}) custom-call(s32[17]{0:T(128)} %get-tuple-element.71.refs_0_, bf16[128,640]{1,0:T(8,128)(2,1)S(1)} %pad_maximum_fusion.refs_1_, ...), custom_call_target="tpu_custom_call" | custom-call | flops 1879048192 | bytes 18350080 | tf_op jit(solution)/shard_map/normalize/pallas_call | solution.py:148
  58.7 1.7 %fusion.21 = f32[192,1024]{1,0:T(8,128)S(1)} fusion(bf16[192,3584]{1,0:T(8,128)(2,1)S(1)} %get-tuple-element.116, bf16[1,3584,1024]{2,1,0:T(8,128)(2,1)S(1)} %copy-done.4, f32[192]{0:T(256)S(1)} %get-tuple-element.144), kind=kOutput, calls=%fused_computation.17 | convolution fusion | flops 1409482752 | bytes 9503488 | tf_op jit(solution)/shard_map/dot_general | solution.py:405
  60.6 1.8 %multiply_convert_fusion.1 = bf16[192,1024]{1,0:T(8,128)(2,1)S(1)} fusion(f32[192,1024]{1,0:T(8,128)S(1)} %fusion.21, f32[192]{0:T(256)S(1)} %get-tuple-element.143, f32[192]{0:T(256)S(1)} %get-tuple-element.144, bf16[192,3584]{1,0:T(8,128)(2,1)S(1)} %get-tuple-element.116, bf16[1,3584,1024]{2,1,0:T(8,128)(2,1)S(1)} %bitcast.62), kind=kOutput, calls=%fused_computation.21 | convolution fusion | flops 1410859008 | bytes 9897472 | tf_op jit(solution)/shard_map/dot_general | solution.py:405
  62.4 0.5 slice-done.3
  62.9 1.6 %fusion.15 = bf16[192,3584]{1,0:T(8,128)(2,1)S(1)} fusion(bf16[192,1024]{1,0:T(8,128)(2,1)S(1)} %multiply_convert_fusion.1, bf16[1,1024,3584]{2,1,0:T(8,128)(2,1)S(1)} %bitcast.64), kind=kOutput, calls=%fused_computation.14 | convolution fusion | flops 1409974272 | bytes 9109504 | tf_op jit(solution)/shard_map/dot_general | solution.py:405
  64.9 2.7 %fusion.10 = f32[320,1024]{1,0:T(8,128)S(1)} fusion(bf16[320,3584]{1,0:T(8,128)(2,1)S(1)} %get-tuple-element.114, bf16[1,3584,1024]{2,1,0:T(8,128)(2,1)S(1)} %copy-done.4), kind=kOutput, calls=%fused_computation.10 | convolution fusion | flops 2348810240 | bytes 10944512 | tf_op jit(solution)/shard_map/dot_general | solution.py:405
  67.6 1.6 %collective-permute-start.23 = (bf16[16,3584]{1,0:T(8,128)(2,1)S(1)}, bf16[16,3584]{1,0:T(8,128)(2,1)S(1)}, u32[]{:S(2)}, u32[]{:S(2)}) collective-permute-start(bf16[16,3584]{1,0:T(8,128)(2,1)S(1)} %get-tuple-element.139), channel_id=1, source_target_pairs={{0,2},{1,3},{4,0},{5,1},{8,4},{9,5},{12,8},{13,9},{14,12},{15,13},... | collective-permute-start | bytes 344072 | tf_op jit(solution)/shard_map/ppermute | solution.py:326
  69.2 0.5 collective-permute-start.22
  69.7 2.8 %multiply_convert_fusion = bf16[320,1024]{1,0:T(8,128)(2,1)S(1)} fusion(f32[320,1024]{1,0:T(8,128)S(1)} %fusion.10, f32[320]{0:T(512)S(1)} %get-tuple-element.141, f32[320]{0:T(512)S(1)} %get-tuple-element.142, bf16[320,3584]{1,0:T(8,128)(2,1)S(1)} %get-tuple-element.114, bf16[1,3584,1024]{2,1,0:T(8,128)(2,1)S(1)} %bitcast.62), kind=kOutput, calls=%fused_computation.16 | convolution fusion | flops 2351759360 | bytes 11602432 | tf_op jit(solution)/shard_map/dot_general | solution.py:405
  72.5 0.5 collective-permute-done.23
  73.1 1.2 %collective-permute-done.22 = bf16[16,3584]{1,0:T(8,128)(2,1)S(1)} collective-permute-done((bf16[16,3584]{1,0:T(8,128)(2,1)S(1)}, bf16[16,3584]{1,0:T(8,128)(2,1)S(1)}, u32[]{:S(2)}, u32[]{:S(2)}) %collective-permute-start.22) | collective-permute-done | bytes 114720 | tf_op jit(solution)/shard_map/ppermute | solution.py:326
  74.3 2.6 %fusion.12 = bf16[320,3584]{1,0:T(8,128)(2,1)S(1)} fusion(bf16[320,1024]{1,0:T(8,128)(2,1)S(1)} %multiply_convert_fusion, bf16[1,1024,3584]{2,1,0:T(8,128)(2,1)S(1)} %bitcast.64), kind=kOutput, calls=%fused_computation.13 | convolution fusion | flops 2349957120 | bytes 10289152 | tf_op jit(solution)/shard_map/dot_general | solution.py:405
  77.2 0.7 collective-permute-start.26
  77.9 1.4 %collective-permute-start.25 = (bf16[32,3584]{1,0:T(8,128)(2,1)S(1)}, bf16[32,3584]{1,0:T(8,128)(2,1)S(1)}, u32[]{:S(2)}, u32[]{:S(2)}) collective-permute-start(bf16[32,3584]{1,0:T(8,128)(2,1)S(1)} %get-tuple-element.138), channel_id=1, source_target_pairs={{0,4},{1,5},{4,8},{5,9},{8,12},{9,13},{12,14},{13,15},{14,10},{15,... | collective-permute-start | bytes 688136 | tf_op jit(solution)/shard_map/ppermute | solution.py:326
  79.3 6.0 %collective-permute-done.26 = bf16[32,3584]{1,0:T(8,128)(2,1)S(1)} collective-permute-done((bf16[32,3584]{1,0:T(8,128)(2,1)S(1)}, bf16[32,3584]{1,0:T(8,128)(2,1)S(1)}, u32[]{:S(2)}, u32[]{:S(2)}) %collective-permute-start.26) | collective-permute-done | bytes 229408 | tf_op jit(solution)/shard_map/ppermute | solution.py:326
  85.2 0.4 collective-permute-done.25
  85.8 1.2 %collective-permute-start.28 = (bf16[32,3584]{1,0:T(8,128)(2,1)S(1)}, bf16[32,3584]{1,0:T(8,128)(2,1)S(1)}, u32[]{:S(2)}, u32[]{:S(2)}) collective-permute-start(bf16[32,3584]{1,0:T(8,128)(2,1)S(1)} %get-tuple-element.135), channel_id=1, source_target_pairs={{0,2},{1,3},{4,0},{5,1},{8,4},{9,5},{12,8},{13,9},{14,12},{15,13},... | collective-permute-start | bytes 688136 | tf_op jit(solution)/shard_map/ppermute | solution.py:326
  87.0 0.8 collective-permute-start.27
  87.9 4.9 %collective-permute-done.28 = bf16[32,3584]{1,0:T(8,128)(2,1)S(1)} collective-permute-done((bf16[32,3584]{1,0:T(8,128)(2,1)S(1)}, bf16[32,3584]{1,0:T(8,128)(2,1)S(1)}, u32[]{:S(2)}, u32[]{:S(2)}) %collective-permute-start.28) | collective-permute-done | bytes 229408 | tf_op jit(solution)/shard_map/ppermute | solution.py:326
  92.7 0.9 collective-permute-done.27
  93.8 1.8 %collective-permute-start.30 = (bf16[32,3584]{1,0:T(8,128)(2,1)S(1)}, bf16[32,3584]{1,0:T(8,128)(2,1)S(1)}, u32[]{:S(2)}, u32[]{:S(2)}) collective-permute-start(bf16[32,3584]{1,0:T(8,128)(2,1)S(1)} %get-tuple-element.133), channel_id=1, source_target_pairs={{0,2},{1,3},{4,0},{5,1},{8,4},{9,5},{12,8},{13,9},{14,12},{15,13},... | collective-permute-start | bytes 688136 | tf_op jit(solution)/shard_map/ppermute | solution.py:326
  95.9 4.0 %collective-permute-done.30 = bf16[32,3584]{1,0:T(8,128)(2,1)S(1)} collective-permute-done((bf16[32,3584]{1,0:T(8,128)(2,1)S(1)}, bf16[32,3584]{1,0:T(8,128)(2,1)S(1)}, u32[]{:S(2)}, u32[]{:S(2)}) %collective-permute-start.30) | collective-permute-done | bytes 229408 | tf_op jit(solution)/shard_map/ppermute | solution.py:326
  99.9 1.7 %collective-permute-done.29 = bf16[32,3584]{1,0:T(8,128)(2,1)S(1)} collective-permute-done((bf16[32,3584]{1,0:T(8,128)(2,1)S(1)}, bf16[32,3584]{1,0:T(8,128)(2,1)S(1)}, u32[]{:S(2)}, u32[]{:S(2)}) %collective-permute-start.29) | collective-permute-done | bytes 229408 | tf_op jit(solution)/shard_map/ppermute | solution.py:326
  101.6 0.8 fusion.32
  (64 shorter events, 3.1 us)
Async XLA Ops:
  0.0 3.2 %copy-start = (bf16[128,2,576]{0,2,1:T(8,128)(2,1)S(1)}, bf16[128,2,576]{0,2,1:T(8,128)(2,1)}, u32[]{:S(2)}) copy-start(bf16[128,2,576]{0,2,1:T(8,128)(2,1)} %param.16) | copy-start | bytes 884740
  0.0 27.4 %collective-permute-start.5 = (bf16[32,3584]{1,0:T(8,128)(2,1)}, bf16[32,3584]{1,0:T(8,128)(2,1)S(1)}, u32[]{:S(2)}, u32[]{:S(2)}) collective-permute-start(bf16[32,3584]{1,0:T(8,128)(2,1)} %bitcast.56), channel_id=1, source_target_pairs={{0,1},{1,0},{2,3},{3,2},{4,5},{5,4},{6,7},{7,6},{8,9},{9,8},{10,11... | collective-permute-start | bytes 688136 | tf_op jit(solution)/shard_map/ppermute | solution.py:326
  0.5 12.4 %collective-permute-start.1 = (bf16[32,3584]{1,0:T(8,128)(2,1)}, bf16[32,3584]{1,0:T(8,128)(2,1)S(1)}, u32[]{:S(2)}, u32[]{:S(2)}) collective-permute-start(bf16[32,3584]{1,0:T(8,128)(2,1)} %bitcast.57), channel_id=1, source_target_pairs={{0,2},{1,3},{4,0},{5,1},{8,4},{9,5},{12,8},{13,9},{14,12},{15,13},... | collective-permute-start | bytes 688136 | tf_op jit(solution)/shard_map/ppermute | solution.py:326
  3.0 9.9 %collective-permute-start = (bf16[32,3584]{1,0:T(8,128)(2,1)}, bf16[32,3584]{1,0:T(8,128)(2,1)}, u32[]{:S(2)}, u32[]{:S(2)}) collective-permute-start(bf16[32,3584]{1,0:T(8,128)(2,1)} %bitcast.58), channel_id=1, source_target_pairs={{0,4},{1,5},{4,8},{5,9},{8,12},{9,13},{12,14},{13,15},{14,10},{15,... | collective-permute-start | bytes 688136 | tf_op jit(solution)/shard_map/ppermute | solution.py:326
  5.1 17.9 %all-to-all-start = ((bf16[16,2,8,576]{3,2,1,0:T(8,128)(2,1)}), bf16[16,2,8,576]{3,2,1,0:T(8,128)(2,1)S(1)}, u32[]{:S(2)}, u32[]{:S(2)}) async-start(bf16[16,2,8,576]{3,2,1,0:T(8,128)(2,1)} %copy.19), calls=%async_computation | async-start | bytes 655360 | tf_op jit(solution)/shard_map/all_to_all | solution.py:343
  11.4 4.0 %copy-start.5 = (bf16[3584]{0:T(1024)(128)(2,1)S(1)}, bf16[3584]{0:T(1024)(128)(2,1)}, u32[]{:S(2)}) copy-start(bf16[3584]{0:T(1024)(128)(2,1)} %param.22) | copy-start | bytes 21508
  11.5 11.6 %copy-start.1 = (bf16[4,8,36864]{2,1,0:T(8,128)(2,1)S(1)}, bf16[4,8,36864]{2,1,0:T(8,128)(2,1)}, u32[]{:S(2)}) copy-start(bf16[4,8,36864]{2,1,0:T(8,128)(2,1)} %refs_0_.1) | copy-start | bytes 7077892
  11.5 11.6 %copy-start.2 = (bf16[4,8,576]{2,1,0:T(8,128)(2,1)S(1)}, bf16[4,8,576]{2,1,0:T(8,128)(2,1)}, u32[]{:S(2)}) copy-start(bf16[4,8,576]{2,1,0:T(8,128)(2,1)} %param.15) | copy-start | bytes 110596
  11.5 11.5 %copy-start.3 = (s32[4,8,8]{2,1,0:T(8,128)S(1)}, s32[4,8,8]{2,1,0:T(8,128)}, u32[]{:S(2)}) copy-start(s32[4,8,8]{2,1,0:T(8,128)} %param.20) | copy-start | bytes 3076
  12.9 14.5 %collective-permute-start.4 = (bf16[32,3584]{1,0:T(8,128)(2,1)}, bf16[32,3584]{1,0:T(8,128)(2,1)}, u32[]{:S(2)}, u32[]{:S(2)}) collective-permute-start(bf16[32,3584]{1,0:T(8,128)(2,1)} %collective-permute-done.refs_13_), channel_id=1, source_target_pairs={{0,1},{1,0},{2,3},{3,2},{4,5},{5,4},{6,7},{7,6},{8,9},{9,8},{10,11... | collective-permute-start | bytes 688136 | tf_op jit(solution)/shard_map/ppermute | solution.py:326
  13.4 14.0 %collective-permute-start.2 = (bf16[32,3584]{1,0:T(8,128)(2,1)}, bf16[32,3584]{1,0:T(8,128)(2,1)}, u32[]{:S(2)}, u32[]{:S(2)}) collective-permute-start(bf16[32,3584]{1,0:T(8,128)(2,1)} %collective-permute-done.refs_13_), channel_id=1, source_target_pairs={{0,4},{1,5},{4,8},{5,9},{8,12},{9,13},{12,14},{13,15},{14,10},{15,... | collective-permute-start | bytes 688136 | tf_op jit(solution)/shard_map/ppermute | solution.py:326
  15.1 12.3 %collective-permute-start.6 = (bf16[32,3584]{1,0:T(8,128)(2,1)S(1)}, bf16[32,3584]{1,0:T(8,128)(2,1)}, u32[]{:S(2)}, u32[]{:S(2)}) collective-permute-start(bf16[32,3584]{1,0:T(8,128)(2,1)S(1)} %collective-permute-done.1.refs_12_), channel_id=1, source_target_pairs={{0,1},{1,0},{2,3},{3,2},{4,5},{5,4},{6,7},{7,6},{8,9},{9,8},{10,11... | collective-permute-start | bytes 688136 | tf_op jit(solution)/shard_map/ppermute | solution.py:326
  15.1 12.3 %collective-permute-start.3 = (bf16[32,3584]{1,0:T(8,128)(2,1)S(1)}, bf16[32,3584]{1,0:T(8,128)(2,1)}, u32[]{:S(2)}, u32[]{:S(2)}) collective-permute-start(bf16[32,3584]{1,0:T(8,128)(2,1)S(1)} %collective-permute-done.1.refs_12_), channel_id=1, source_target_pairs={{0,2},{1,3},{4,0},{5,1},{8,4},{9,5},{12,8},{13,9},{14,12},{15,13},... | collective-permute-start | bytes 688136 | tf_op jit(solution)/shard_map/ppermute | solution.py:326
  27.4 11.6 %collective-permute-start.10 = (bf16[32,3584]{1,0:T(8,128)(2,1)}, bf16[32,3584]{1,0:T(8,128)(2,1)S(1)}, u32[]{:S(2)}, u32[]{:S(2)}) collective-permute-start(bf16[32,3584]{1,0:T(8,128)(2,1)} %collective-permute-done.2.refs_15_), channel_id=1, source_target_pairs={{0,4},{1,5},{4,8},{5,9},{8,12},{9,13},{12,14},{13,15},{14,10},{15,... | collective-permute-start | bytes 688136 | tf_op jit(solution)/shard_map/ppermute | solution.py:326
  28.1 10.9 %collective-permute-start.11 = (bf16[32,3584]{1,0:T(8,128)(2,1)}, bf16[32,3584]{1,0:T(8,128)(2,1)S(1)}, u32[]{:S(2)}, u32[]{:S(2)}) collective-permute-start(bf16[32,3584]{1,0:T(8,128)(2,1)} %collective-permute-done.3.refs_14_), channel_id=1, source_target_pairs={{0,2},{1,3},{4,0},{5,1},{8,4},{9,5},{12,8},{13,9},{14,12},{15,13},... | collective-permute-start | bytes 688136 | tf_op jit(solution)/shard_map/ppermute | solution.py:326
  29.5 8.3 %collective-permute-start.9 = (bf16[32,640]{1,0:T(8,128)(2,1)S(1)}, bf16[32,640]{1,0:T(8,128)(2,1)S(1)}, u32[]{:S(2)}, u32[]{:S(2)}) collective-permute-start(bf16[32,640]{1,0:T(8,128)(2,1)S(1)} %attention.1), channel_id=1, source_target_pairs={{0,12},{1,13},{2,14},{3,15},{4,8},{5,9},{6,10},{7,11},{8,4},{9,5},... | collective-permute-start | bytes 122888 | tf_op jit(solution)/shard_map/ppermute | solution.py:326
  30.2 8.7 %collective-permute-start.8 = (bf16[32,640]{1,0:T(8,128)(2,1)S(1)}, bf16[32,640]{1,0:T(8,128)(2,1)S(1)}, u32[]{:S(2)}, u32[]{:S(2)}) collective-permute-start(bf16[32,640]{1,0:T(8,128)(2,1)S(1)} %attention.1), channel_id=1, source_target_pairs={{0,8},{1,9},{2,10},{3,11},{4,12},{5,13},{6,14},{7,15},{8,0},{9,1},... | collective-permute-start | bytes 122888 | tf_op jit(solution)/shard_map/ppermute | solution.py:326
  31.6 7.4 %collective-permute-start.7 = (bf16[32,640]{1,0:T(8,128)(2,1)S(1)}, bf16[32,640]{1,0:T(8,128)(2,1)S(1)}, u32[]{:S(2)}, u32[]{:S(2)}) collective-permute-start(bf16[32,640]{1,0:T(8,128)(2,1)S(1)} %attention.1), channel_id=1, source_target_pairs={{0,4},{1,5},{2,6},{3,7},{4,0},{5,1},{6,2},{7,3},{8,12},{9,13},{10,... | collective-permute-start | bytes 122888 | tf_op jit(solution)/shard_map/ppermute | solution.py:326
  39.0 8.7 %collective-permute-start.13 = (bf16[128,640]{1,0:T(8,128)(2,1)S(1)}, bf16[128,640]{1,0:T(8,128)(2,1)S(1)}, u32[]{:S(2)}, u32[]{:S(2)}) collective-permute-start(bf16[128,640]{1,0:T(8,128)(2,1)S(1)} %pad_maximum_fusion.refs_1_), channel_id=1, source_target_pairs={{0,1},{1,0},{2,3},{3,2},{4,5},{5,4},{6,7},{7,6},{8,9},{9,8},{10,11... | collective-permute-start | bytes 491528 | tf_op jit(solution)/shard_map/ppermute | solution.py:326
  39.1 8.6 %collective-permute-start.12 = (bf16[128,640]{1,0:T(8,128)(2,1)S(1)}, bf16[128,640]{1,0:T(8,128)(2,1)S(1)}, u32[]{:S(2)}, u32[]{:S(2)}) collective-permute-start(bf16[128,640]{1,0:T(8,128)(2,1)S(1)} %pad_maximum_fusion.refs_1_), channel_id=1, source_target_pairs={{0,2},{1,3},{2,0},{3,1},{4,6},{5,7},{6,4},{7,5},{8,10},{9,11},{10,... | collective-permute-start | bytes 491528 | tf_op jit(solution)/shard_map/ppermute | solution.py:326
  40.5 7.6 %collective-permute-start.14 = (bf16[32,3584]{1,0:T(8,128)(2,1)S(1)}, bf16[32,3584]{1,0:T(8,128)(2,1)S(1)}, u32[]{:S(2)}, u32[]{:S(2)}) collective-permute-start(bf16[32,3584]{1,0:T(8,128)(2,1)S(1)} %broadcast_select_fusion.1), channel_id=1, source_target_pairs={{0,4},{1,3},{4,8},{5,1},{8,12},{9,5},{12,14},{13,9},{14,10},{15,13... | collective-permute-start | bytes 688136 | tf_op jit(solution)/shard_map/ppermute | solution.py:326
  40.7 7.5 %collective-permute-start.15 = (bf16[32,3584]{1,0:T(8,128)(2,1)}, bf16[32,3584]{1,0:T(8,128)(2,1)S(1)}, u32[]{:S(2)}, u32[]{:S(2)}) collective-permute-start(bf16[32,3584]{1,0:T(8,128)(2,1)} %collective-permute-done.2.refs_15_), channel_id=1, source_target_pairs={{0,1},{1,0},{2,3},{3,2},{4,5},{5,4},{6,7},{7,6},{8,9},{9,8},{10,11... | collective-permute-start | bytes 688136 | tf_op jit(solution)/shard_map/ppermute | solution.py:326
  41.2 7.0 %collective-permute-start.16 = (bf16[32,3584]{1,0:T(8,128)(2,1)}, bf16[32,3584]{1,0:T(8,128)(2,1)S(1)}, u32[]{:S(2)}, u32[]{:S(2)}) collective-permute-start(bf16[32,3584]{1,0:T(8,128)(2,1)} %collective-permute-done.3.refs_14_), channel_id=1, source_target_pairs={{0,1},{1,0},{2,3},{3,2},{4,5},{5,4},{6,7},{7,6},{8,9},{9,8},{10,11... | collective-permute-start | bytes 688136 | tf_op jit(solution)/shard_map/ppermute | solution.py:326
  48.2 2.4 %collective-permute-start.18 = (bf16[32,3584]{1,0:T(8,128)(2,1)S(1)}, bf16[32,3584]{1,0:T(8,128)(2,1)S(1)}, u32[]{:S(2)}, u32[]{:S(2)}) collective-permute-start(bf16[32,3584]{1,0:T(8,128)(2,1)S(1)} %collective-permute-done.14.refs_5_), channel_id=1, source_target_pairs={{0,1},{1,0},{2,3},{3,2},{4,5},{5,4},{6,7},{7,6},{8,9},{9,8},{10,11... | collective-permute-start | bytes 688136 | tf_op jit(solution)/shard_map/ppermute | solution.py:326
  48.2 2.3 %collective-permute-start.19 = (bf16[32,3584]{1,0:T(8,128)(2,1)S(1)}, bf16[32,3584]{1,0:T(8,128)(2,1)S(1)}, u32[]{:S(2)}, u32[]{:S(2)}) collective-permute-start(bf16[32,3584]{1,0:T(8,128)(2,1)S(1)} %collective-permute-done.11.refs_6_), channel_id=1, source_target_pairs={{0,1},{1,0},{2,3},{3,2},{4,5},{5,4},{6,7},{7,6},{8,9},{9,8},{10,11... | collective-permute-start | bytes 688136 | tf_op jit(solution)/shard_map/ppermute | solution.py:326
  48.7 1.9 %collective-permute-start.20 = (bf16[32,3584]{1,0:T(8,128)(2,1)S(1)}, bf16[32,3584]{1,0:T(8,128)(2,1)S(1)}, u32[]{:S(2)}, u32[]{:S(2)}) collective-permute-start(bf16[32,3584]{1,0:T(8,128)(2,1)S(1)} %collective-permute-done.10.refs_7_), channel_id=1, source_target_pairs={{0,1},{1,0},{2,3},{3,2},{4,5},{5,4},{6,7},{7,6},{8,9},{9,8},{10,11... | collective-permute-start | bytes 688136 | tf_op jit(solution)/shard_map/ppermute | solution.py:326
  48.8 1.8 %collective-permute-start.17 = (bf16[128,640]{1,0:T(8,128)(2,1)S(1)}, bf16[128,640]{1,0:T(8,128)(2,1)S(1)}, u32[]{:S(2)}, u32[]{:S(2)}) collective-permute-start(bf16[128,640]{1,0:T(8,128)(2,1)S(1)} %collective-permute-done.12.refs_2_), channel_id=1, source_target_pairs={{0,1},{1,0},{2,3},{3,2},{4,5},{5,4},{6,7},{7,6},{8,9},{9,8},{10,11... | collective-permute-start | bytes 491528 | tf_op jit(solution)/shard_map/ppermute | solution.py:326
  50.6 8.1 %copy-start.4 = (bf16[1,3584,1024]{2,1,0:T(8,128)(2,1)S(1)}, bf16[1,3584,1024]{2,1,0:T(8,128)(2,1)}, u32[]{:S(2)}) copy-start(bf16[1,3584,1024]{2,1,0:T(8,128)(2,1)} %broadcast_select_fusion) | copy-start | bytes 22020100
  50.6 9.8 %slice-start = ((s8[7340032]{0:T(1024)(128)(4,1)}), s8[4194304]{0:T(1024)(128)(4,1)S(1)}, s32[]{:S(2)}) async-start(s8[7340032]{0:T(1024)(128)(4,1)} %bitcast.61), calls=%async_computation.1 | async-start | bytes 8388608
  58.7 1.9 %slice-start.1 = ((s8[7340032]{0:T(1024)(128)(4,1)}), s8[3145728]{0:T(1024)(128)(4,1)S(1)}, s32[]{:S(2)}) async-start(s8[7340032]{0:T(1024)(128)(4,1)} %bitcast.61), calls=%async_computation.2 | async-start | bytes 6291456
  58.7 3.7 %slice-start.2 = ((s8[7340032]{0:T(1024)(128)(4,1)}), s8[4194304]{0:T(1024)(128)(4,1)S(1)}, s32[]{:S(2)}) async-start(s8[7340032]{0:T(1024)(128)(4,1)} %bitcast.63), calls=%async_computation.3 | async-start | bytes 8388608
  60.6 2.4 %slice-start.3 = ((s8[7340032]{0:T(1024)(128)(4,1)}), s8[3145728]{0:T(1024)(128)(4,1)S(1)}, s32[]{:S(2)}) async-start(s8[7340032]{0:T(1024)(128)(4,1)} %bitcast.63), calls=%async_computation.4 | async-start | bytes 6291456
  64.6 2.9 %collective-permute-start.21 = (bf16[96,3584]{1,0:T(8,128)(2,1)S(1)}, bf16[96,3584]{1,0:T(8,128)(2,1)S(1)}, u32[]{:S(2)}, u32[]{:S(2)}) collective-permute-start(bf16[96,3584]{1,0:T(8,128)(2,1)S(1)} %slice.98), channel_id=1, source_target_pairs={{0,1},{1,0},{2,3},{3,2},{4,5},{5,4},{6,7},{7,6},{8,9},{9,8},{10,11... | collective-permute-start | bytes 2064392 | tf_op jit(solution)/shard_map/ppermute | solution.py:326
  67.6 5.4 %collective-permute-start.23 = (bf16[16,3584]{1,0:T(8,128)(2,1)S(1)}, bf16[16,3584]{1,0:T(8,128)(2,1)S(1)}, u32[]{:S(2)}, u32[]{:S(2)}) collective-permute-start(bf16[16,3584]{1,0:T(8,128)(2,1)S(1)} %get-tuple-element.139), channel_id=1, source_target_pairs={{0,2},{1,3},{4,0},{5,1},{8,4},{9,5},{12,8},{13,9},{14,12},{15,13},... | collective-permute-start | bytes 344072 | tf_op jit(solution)/shard_map/ppermute | solution.py:326
  69.2 5.1 %collective-permute-start.22 = (bf16[16,3584]{1,0:T(8,128)(2,1)S(1)}, bf16[16,3584]{1,0:T(8,128)(2,1)S(1)}, u32[]{:S(2)}, u32[]{:S(2)}) collective-permute-start(bf16[16,3584]{1,0:T(8,128)(2,1)S(1)} %get-tuple-element.140), channel_id=1, source_target_pairs={{0,4},{1,5},{4,8},{5,9},{8,12},{9,13},{12,14},{13,15},{14,10},{15,... | collective-permute-start | bytes 344072 | tf_op jit(solution)/shard_map/ppermute | solution.py:326
  77.0 8.7 %collective-permute-start.24 = (bf16[160,3584]{1,0:T(8,128)(2,1)S(1)}, bf16[160,3584]{1,0:T(8,128)(2,1)S(1)}, u32[]{:S(2)}, u32[]{:S(2)}) collective-permute-start(bf16[160,3584]{1,0:T(8,128)(2,1)S(1)} %slice.101), channel_id=1, source_target_pairs={{0,1},{1,0},{2,3},{3,2},{4,5},{5,4},{6,7},{7,6},{8,9},{9,8},{10,11... | collective-permute-start | bytes 3440648 | tf_op jit(solution)/shard_map/ppermute | solution.py:326
  77.2 8.1 %collective-permute-start.26 = (bf16[32,3584]{1,0:T(8,128)(2,1)S(1)}, bf16[32,3584]{1,0:T(8,128)(2,1)S(1)}, u32[]{:S(2)}, u32[]{:S(2)}) collective-permute-start(bf16[32,3584]{1,0:T(8,128)(2,1)S(1)} %get-tuple-element.137), channel_id=1, source_target_pairs={{0,2},{1,3},{4,0},{5,1},{8,4},{9,5},{12,8},{13,9},{14,12},{15,13},... | collective-permute-start | bytes 688136 | tf_op jit(solution)/shard_map/ppermute | solution.py:326
  77.9 7.7 %collective-permute-start.25 = (bf16[32,3584]{1,0:T(8,128)(2,1)S(1)}, bf16[32,3584]{1,0:T(8,128)(2,1)S(1)}, u32[]{:S(2)}, u32[]{:S(2)}) collective-permute-start(bf16[32,3584]{1,0:T(8,128)(2,1)S(1)} %get-tuple-element.138), channel_id=1, source_target_pairs={{0,4},{1,5},{4,8},{5,9},{8,12},{9,13},{12,14},{13,15},{14,10},{15,... | collective-permute-start | bytes 688136 | tf_op jit(solution)/shard_map/ppermute | solution.py:326
  85.8 7.0 %collective-permute-start.28 = (bf16[32,3584]{1,0:T(8,128)(2,1)S(1)}, bf16[32,3584]{1,0:T(8,128)(2,1)S(1)}, u32[]{:S(2)}, u32[]{:S(2)}) collective-permute-start(bf16[32,3584]{1,0:T(8,128)(2,1)S(1)} %get-tuple-element.135), channel_id=1, source_target_pairs={{0,2},{1,3},{4,0},{5,1},{8,4},{9,5},{12,8},{13,9},{14,12},{15,13},... | collective-permute-start | bytes 688136 | tf_op jit(solution)/shard_map/ppermute | solution.py:326
  87.0 6.6 %collective-permute-start.27 = (bf16[32,3584]{1,0:T(8,128)(2,1)S(1)}, bf16[32,3584]{1,0:T(8,128)(2,1)S(1)}, u32[]{:S(2)}, u32[]{:S(2)}) collective-permute-start(bf16[32,3584]{1,0:T(8,128)(2,1)S(1)} %get-tuple-element.136), channel_id=1, source_target_pairs={{0,4},{1,5},{4,8},{5,9},{8,12},{9,13},{12,14},{13,15},{14,10},{15,... | collective-permute-start | bytes 688136 | tf_op jit(solution)/shard_map/ppermute | solution.py:326
  93.8 6.1 %collective-permute-start.30 = (bf16[32,3584]{1,0:T(8,128)(2,1)S(1)}, bf16[32,3584]{1,0:T(8,128)(2,1)S(1)}, u32[]{:S(2)}, u32[]{:S(2)}) collective-permute-start(bf16[32,3584]{1,0:T(8,128)(2,1)S(1)} %get-tuple-element.133), channel_id=1, source_target_pairs={{0,2},{1,3},{4,0},{5,1},{8,4},{9,5},{12,8},{13,9},{14,12},{15,13},... | collective-permute-start | bytes 688136 | tf_op jit(solution)/shard_map/ppermute | solution.py:326
  95.6 6.0 %collective-permute-start.29 = (bf16[32,3584]{1,0:T(8,128)(2,1)S(1)}, bf16[32,3584]{1,0:T(8,128)(2,1)S(1)}, u32[]{:S(2)}, u32[]{:S(2)}) collective-permute-start(bf16[32,3584]{1,0:T(8,128)(2,1)S(1)} %get-tuple-element.134), channel_id=1, source_target_pairs={{0,4},{1,5},{4,8},{5,9},{8,12},{9,13},{12,14},{13,15},{14,10},{15,... | collective-permute-start | bytes 688136 | tf_op jit(solution)/shard_map/ppermute | solution.py:326
